TPU v7x, 32 devices: a whole 2x2x4 slice. The times are simulated.
32 devices in a mesh: layer: 8 (over z, y), dir: 4 (over x, core).
Axes of the slice: x: 2, y: 2, z: 4, core: 2. Of those that a mesh axis runs over, the one named last changes fastest.
Arguments:
- screens: bfloat16 [3, 512, 4096], P(None, 'dir', 'layer'), may hold values from -6 to 6
- amplitude: float32 [256, 1280], P('layer'), may hold values from 0.5 to 2
- wind: int32 [3, 2], replicated, may hold values from -8 to 8, as said below
- offsets: int32 [4, 3, 2], replicated, may hold values from 0 to 4095, as said below
- ratio: int32 [4, 3, 2], replicated, may hold values from 64 to 192, as said below
Outputs:
- new_screens: bfloat16 [3, 512, 4096], P(None, 'dir', 'layer')
- spots: float32 [4, 512, 2560], P('dir', 'layer')
Inputs may be any that keep to these rules, and one draw needn't show every extreme that they name: wind[l, 0] is layer l's row shift and wind[l, 1] its column shift; no shift is zero; one layer has column shift +8 and a row shift above zero, another has column shift -8 and a row shift below zero. offsets[d, l, 0] is a screen row below 512, offsets[d, l, 1] a screen column below 4096. ratio[d, l] = (num, den) with 64 <= den <= 128 and den <= num <= den + den // 2; some entry is (192, 128) and another (64, 64).
All inputs are finite; a program needn't handle non-finite values.
Results may differ from a plain program's by a relative error of at most 0.009.
Values may be sent and summed in bfloat16 or wider, within the bound.
No kernel may reach another device: no remote copies, remote signals or barrier semaphores. Data moves between devices by JAX's collectives and lax.ppermute only.
A program may use at most 64 MiB of HBM per device.

v0:
```python
import jax
import jax.numpy as jnp
from jax import lax
from jax.sharding import PartitionSpec as P

SUB_PIX = 16
SPOT_PIX = 32
WIND_MAX = 8


def with_halo(shard, sides, width):
    for axis, dim in sides:
        peers, length = (lax.axis_size(axis), shard.shape[dim])
        up = [(i, (i + 1) % peers) for i in range(peers)]
        down = [(j, i) for i, j in up]
        last = lax.slice_in_dim(shard, length - width, length, axis=dim)
        initial = lax.slice_in_dim(shard, 0, width, axis=dim)
        before = lax.ppermute(last, axis, up)
        after = lax.ppermute(initial, axis, down)
        shard = jnp.concatenate([before, shard, after], axis=dim)
    return shard


def spans(anchor, stretch_num, stretch_den, count, length):
    pixel = jnp.arange(count, dtype=jnp.int32)
    stretched = pixel * stretch_num
    base = (anchor + stretched // stretch_den) % length
    upper = (base + 1) % length
    fraction = (stretched % stretch_den).astype(jnp.float32) / stretch_den.astype(jnp.float32)
    return (base, upper, (1.0 - fraction).astype(jnp.bfloat16), fraction.astype(jnp.bfloat16))


def weights_rows(anchor, stretch_num, stretch_den, count, length, width):
    base, upper, low_weight, high_weight = spans(anchor, stretch_num, stretch_den, count, length)
    index = jnp.arange(width, dtype=jnp.int32)
    matrix = jnp.where(
        index[None, :] == base[:, None], low_weight[:, None], jnp.zeros((), jnp.bfloat16)
    )
    return jnp.where(index[None, :] == upper[:, None], high_weight[:, None], matrix)


def weights_cols(anchor, stretch_num, stretch_den, count, length, start, width):
    base, upper, low_weight, high_weight = spans(anchor, stretch_num, stretch_den, count, length)
    index = start + jnp.arange(width, dtype=jnp.int32)
    matrix = jnp.where(
        index[:, None] == base[None, :], low_weight[None, :], jnp.zeros((), jnp.bfloat16)
    )
    return jnp.where(index[:, None] == upper[None, :], high_weight[None, :], matrix)


def dft_tables():
    freq = jnp.arange(SPOT_PIX, dtype=jnp.int32)[:, None] - SPOT_PIX // 2
    pixel = jnp.arange(SUB_PIX, dtype=jnp.int32)[None, :]
    turns = freq * pixel % SPOT_PIX
    angle = turns.astype(jnp.float32) * (2.0 * jnp.pi / SPOT_PIX)
    return (jnp.cos(angle), -jnp.sin(angle))


def imaging(phase, amplitude):
    rows, cols = phase.shape
    sub_rows = rows // SUB_PIX
    sub_cols = cols // SUB_PIX
    real = (amplitude * jnp.cos(phase)).reshape(sub_rows, SUB_PIX, sub_cols, SUB_PIX)
    imag = (amplitude * jnp.sin(phase)).reshape(sub_rows, SUB_PIX, sub_cols, SUB_PIX)
    cos_table, sin_table = dft_tables()
    highest = lax.Precision.HIGHEST
    half_real = jnp.einsum("aibj,kj->aibk", real, cos_table, precision=highest) - jnp.einsum(
        "aibj,kj->aibk", imag, sin_table, precision=highest
    )
    half_imag = jnp.einsum("aibj,kj->aibk", real, sin_table, precision=highest) + jnp.einsum(
        "aibj,kj->aibk", imag, cos_table, precision=highest
    )
    full_real = jnp.einsum("ki,aibl->akbl", cos_table, half_real, precision=highest) - jnp.einsum(
        "ki,aibl->akbl", sin_table, half_imag, precision=highest
    )
    full_imag = jnp.einsum("ki,aibl->akbl", cos_table, half_imag, precision=highest) + jnp.einsum(
        "ki,aibl->akbl", sin_table, half_real, precision=highest
    )
    intensity = full_real * full_real + full_imag * full_imag
    totals = jnp.sum(intensity, axis=(1, 3), keepdims=True)
    normed = intensity * float(SPOT_PIX * SPOT_PIX) / totals
    return normed.reshape(sub_rows * SPOT_PIX, sub_cols * SPOT_PIX)


def per_device(screens, amplitude, wind, offsets, ratio):
    layers, rows_dev, cols_dev = screens.shape
    n_layer = lax.axis_size("layer")
    n_dir = lax.axis_size("dir")
    screen_rows = rows_dev * n_dir
    screen_cols = cols_dev * n_layer
    pupil_rows = amplitude.shape[0] * n_layer
    pupil_cols = amplitude.shape[1]
    direction = lax.axis_index("dir")
    column_start = lax.axis_index("layer") * cols_dev
    widened = with_halo(screens, (("layer", 2), ("dir", 1)), WIND_MAX)
    moved = []
    for level in range(layers):
        corner = (jnp.int32(WIND_MAX) - wind[level, 0], jnp.int32(WIND_MAX) - wind[level, 1])
        moved.append(lax.dynamic_slice(widened[level], corner, (rows_dev, cols_dev)))
    new_screens = jnp.stack(moved)
    piece = lax.all_gather(new_screens, "dir", axis=1, tiled=True)
    sums = []
    for add_level in range(layers):
        weights = weights_rows(
            offsets[direction, add_level, 0],
            ratio[direction, add_level, 0],
            ratio[direction, add_level, 1],
            pupil_rows,
            screen_rows,
            piece.shape[1],
        )
        sums.append(jnp.dot(weights, piece[add_level], preferred_element_type=jnp.float32))
    projected = jnp.stack(sums).astype(jnp.bfloat16)
    col_weights = [
        weights_cols(
            offsets[direction, level, 1],
            ratio[direction, level, 0],
            ratio[direction, level, 1],
            pupil_cols,
            screen_cols,
            column_start,
            cols_dev,
        )
        for level in range(layers)
    ]
    total = jnp.zeros((pupil_rows // n_layer * lax.axis_size("layer"), pupil_cols), jnp.float32)
    for level in range(layers):
        total = total + jnp.dot(
            projected[level], col_weights[level], preferred_element_type=jnp.float32
        )
    phase = lax.psum_scatter(
        total.astype(jnp.bfloat16), "layer", scatter_dimension=0, tiled=True
    ).astype(jnp.float32)
    spots = imaging(phase, amplitude)[None]
    return (new_screens, spots)


def solution(mesh):
    return jax.shard_map(
        per_device,
        mesh=mesh,
        in_specs=(P(None, "dir", "layer"), P("layer", None), P(), P(), P()),
        out_specs=(P(None, "dir", "layer"), P("dir", "layer", None)),
        check_vma=False,
    )
```

profile of v0, /device:TPU:0, one launch (start us, length us, event | category | flops | bytes accessed | tf_op | source)
XLA Modules:
  0.0 161.6 jit_solution(18366804262413313238)
XLA Ops:
  7.2 1.1 fusion.189
  8.3 3.0 %collective-permute-start = (bf16[3,128,8]{2,1,0:T(8,128)(2,1)S(1)}, bf16[3,128,8]{2,1,0:T(8,128)(2,1)S(1)}, u32[]{:S(2)}, u32[]{:S(2)}) collective-permute-start(bf16[3,128,8]{2,1,0:T(8,128)(2,1)S(1)} %get-tuple-element.13), channel_id=1, source_target_pairs={{0,4},{4,8},{8,12},{12,16},{16,20},{20,24},{24,28},{28,0},{1,5},{5... | collective-permute-start | bytes 18440 | tf_op jit(solution)/shard_map/ppermute | solution.py:18
  11.3 3.1 %collective-permute-start.1 = (bf16[3,128,8]{2,1,0:T(8,128)(2,1)S(1)}, bf16[3,128,8]{2,1,0:T(8,128)(2,1)S(1)}, u32[]{:S(2)}, u32[]{:S(2)}) collective-permute-start(bf16[3,128,8]{2,1,0:T(8,128)(2,1)S(1)} %get-tuple-element.14), channel_id=1, source_target_pairs={{4,0},{8,4},{12,8},{16,12},{20,16},{24,20},{28,24},{0,28},{5,1},{9... | collective-permute-start | bytes 18440 | tf_op jit(solution)/shard_map/ppermute | solution.py:19
  14.4 2.8 %collective-permute-done = bf16[3,128,8]{2,1,0:T(8,128)(2,1)S(1)} collective-permute-done((bf16[3,128,8]{2,1,0:T(8,128)(2,1)S(1)}, bf16[3,128,8]{2,1,0:T(8,128)(2,1)S(1)}, u32[]{:S(2)}, u32[]{:S(2)}) %collective-permute-start) | collective-permute-done | bytes 6176 | tf_op jit(solution)/shard_map/ppermute | solution.py:18
  18.1 0.8 pad_maximum_fusion.4
  19.0 1.7 %collective-permute-start.3 = (bf16[3,8,528]{2,1,0:T(8,128)(2,1)S(1)}, bf16[3,8,528]{2,1,0:T(8,128)(2,1)S(1)}, u32[]{:S(2)}, u32[]{:S(2)}) collective-permute-start(bf16[3,8,528]{2,1,0:T(8,128)(2,1)S(1)} %get-tuple-element.9), channel_id=1, source_target_pairs={{1,0},{2,1},{3,2},{0,3},{5,4},{6,5},{7,6},{4,7},{9,8},{10,9},{11,1... | collective-permute-start | bytes 76040 | tf_op jit(solution)/shard_map/ppermute | solution.py:19
  20.7 1.6 fusion.190
  30.5 0.8 pad_maximum_fusion.1
  40.5 1.3 subtract_convert_fusion.5
  41.8 1.4 subtract_convert_fusion.3
  43.2 1.3 fusion.156
  44.5 2.1 %and_select_fusion.9 = (s32[256]{0:T(256)S(1)}, s32[256]{0:T(256)S(1)}) fusion(s32[]{:T(128)} %bitcast.14, s32[]{:T(128)S(6)} %sign.77, s32[]{:T(128)} %bitcast.13, s32[]{:T(128)} %bitcast.12), kind=kLoop, calls=%fused_computation.223 | loop fusion | flops 8448 | bytes 2064 | tf_op jit(solution)/shard_map/jit(remainder)/select_n | solution.py:28
  46.6 3.9 %and_select_fusion.1 = (s32[256]{0:T(256)S(1)}, s32[256]{0:T(256)S(1)}, s32[256]{0:T(256)S(1)}, s32[256]{0:T(256)S(1)}) fusion(s32[]{:T(128)} %bitcast.24, s32[]{:T(128)S(6)} %sign.83, s32[]{:T(128)} %bitcast.23, s32[]{:T(128)} %bitcast.22, s32[]{:T(128)} %bitcast.19, s32[]{:T(128)S(6)} %sign.80, s32[]{:T(128)} %bitcast.18, s32[]{:T(128)} %bitcast.17), kind=kLoop, calls=%fused_computation.215 | loop fusion | flops 16896 | bytes 4128 | tf_op jit(solution)/shard_map/jit(remainder)/select_n | solution.py:28
  52.7 2.0 %add_select_fusion.2 = (s32[1280]{0:T(1024)S(1)}, s32[1280]{0:T(1024)S(1)}) fusion(s32[]{:T(128)} %bitcast.24, s32[]{:T(128)S(6)} %sign.83, s32[]{:T(128)} %bitcast.23, s32[]{:T(128)} %bitcast.26), kind=kLoop, calls=%fused_computation.89 | loop fusion | flops 42240 | bytes 10256 | tf_op jit(solution)/shard_map/jit(remainder)/select_n | solution.py:28
  54.7 2.0 %add_select_fusion.6 = (s32[1280]{0:T(1024)S(1)}, s32[1280]{0:T(1024)S(1)}) fusion(s32[]{:T(128)} %bitcast.19, s32[]{:T(128)S(6)} %sign.80, s32[]{:T(128)} %bitcast.18, s32[]{:T(128)} %bitcast.21), kind=kLoop, calls=%fused_computation.97 | loop fusion | flops 42240 | bytes 10256 | tf_op jit(solution)/shard_map/jit(remainder)/select_n | solution.py:28
  56.7 1.9 %add_select_fusion.10 = (s32[1280]{0:T(1024)S(1)}, s32[1280]{0:T(1024)S(1)}) fusion(s32[]{:T(128)} %bitcast.14, s32[]{:T(128)S(6)} %sign.77, s32[]{:T(128)} %bitcast.13, s32[]{:T(128)} %bitcast.16), kind=kLoop, calls=%fused_computation.105 | loop fusion | flops 42240 | bytes 10256 | tf_op jit(solution)/shard_map/jit(remainder)/select_n | solution.py:28
  58.7 3.3 %fusion.5 = f32[256,1280]{1,0:T(8,128)} fusion(s32[1280]{0:T(1024)S(1)} %get-tuple-element.48, s32[1280]{0:T(1024)S(1)} %get-tuple-element.47, s32[512]{0:T(512)S(1)} %iota_add_fusion, bf16[1280]{0:T(1024)(128)(2,1)S(1)} %get-tuple-element.49, bf16[1280]{0:T(1024)(128)(2,1)S(1)} %get-tuple-element.50, ...), kind=kOutput, calls=%fused_computation.15 | convolution fusion | flops 473038848 | bytes 1855488 | tf_op jit(solution)/shard_map/dot_general | solution.py:128
  62.0 2.4 %convolution_add_fusion.1 = f32[256,1280]{1,0:T(8,128)S(1)} fusion(f32[256,1280]{1,0:T(8,128)} %fusion.5, s32[1280]{0:T(1024)S(1)} %get-tuple-element.52, s32[1280]{0:T(1024)S(1)} %get-tuple-element.51, s32[512]{0:T(512)S(1)} %iota_add_fusion, bf16[1280]{0:T(1024)(128)(2,1)S(1)} %get-tuple-element.53, bf16[1280]{0:T(1024)(128)(2,1)S(1)} %get-tuple-element.54, ...), kind=kOutput, calls=%fused_computation.1 | convolution fusion | flops 473366528 | bytes 3175424 | tf_op jit(solution)/shard_map/dot_general | solution.py:128
  64.5 2.0 %fusion = bf16[256,1280]{1,0:T(8,128)(2,1)} fusion(f32[256,1280]{1,0:T(8,128)S(1)} %convolution_add_fusion.1, s32[1280]{0:T(1024)S(1)} %get-tuple-element.56, s32[1280]{0:T(1024)S(1)} %get-tuple-element.55, s32[512]{0:T(512)S(1)} %iota_add_fusion, bf16[1280]{0:T(1024)(128)(2,1)S(1)} %get-tuple-element.57, bf16[1280]{0:T(1024)(128)(2,1)S(1)} %get-tuple-element.58, ...), kind=kOutput, calls=%fused_computation.8 | convolution fusion | flops 473694208 | bytes 2520064 | tf_op jit(solution)/shard_map/dot_general | solution.py:128
  66.5 62.7 %reduce-scatter.2.cloned.1.call-done = bf16[32,1280]{1,0:T(8,128)(2,1)} async-done(((bf16[256,1280]{1,0:T(8,128)(2,1)}), bf16[32,1280]{1,0:T(8,128)(2,1)}) %reduce-scatter.2.cloned.1.call-update) | async-done | bytes 81936 | tf_op jit(solution)/shard_map/reduce_scatter | solution.py:131
  129.2 1.5 fusion.55
  131.1 3.2 %fusion.99 = f32[2,16,80,32]{2,3,1,0:T(8,128)S(1)} fusion(f32[2,16,80,16]{3,2,1,0:T(8,128)S(1)} %reshape.377, s32[32]{0:T(128)S(1)} %iota_add_fusion.1), kind=kOutput, calls=%fused_computation.137 | convolution fusion | flops 15736320 | bytes 491648 | tf_op jit(solution)/shard_map/aibj,kj->aibk/dot_general | solution.py:70
  134.3 3.2 %fusion.95 = f32[2,16,80,32]{2,3,1,0:T(8,128)S(1)} fusion(f32[2,16,80,16]{3,2,1,0:T(8,128)S(1)} %reshape.377, s32[32]{0:T(128)S(1)} %iota_add_fusion.1), kind=kOutput, calls=%fused_computation.133 | convolution fusion | flops 15735808 | bytes 491648 | tf_op jit(solution)/shard_map/aibj,kj->aibk/dot_general | solution.py:67
  137.9 3.2 %convolution_subtract_fusion.1 = f32[2,16,80,32]{2,3,1,0:T(8,128)S(1)} fusion(f32[2,16,80,32]{2,3,1,0:T(8,128)S(1)} %fusion.95, f32[2,16,80,16]{3,2,1,0:T(8,128)S(1)} %reshape.378, s32[32]{0:T(128)S(1)} %iota_add_fusion.1), kind=kOutput, calls=%fused_computation.26 | convolution fusion | flops 15818240 | bytes 819328 | tf_op jit(solution)/shard_map/aibj,kj->aibk/dot_general | solution.py:67
  141.1 3.3 %convolution_add_fusion.3 = f32[2,16,80,32]{2,3,1,0:T(8,128)S(1)} fusion(f32[2,16,80,32]{2,3,1,0:T(8,128)S(1)} %fusion.99, f32[2,16,80,16]{3,2,1,0:T(8,128)S(1)} %reshape.378, s32[32]{0:T(128)S(1)} %iota_add_fusion.1), kind=kOutput, calls=%fused_computation.25 | convolution fusion | flops 15817728 | bytes 819328 | tf_op jit(solution)/shard_map/aibj,kj->aibk/dot_general | solution.py:70
  144.5 1.3 fusion.30
  145.8 1.3 fusion.34
  147.0 1.3 fusion.4
  148.3 1.5 fusion.191
  149.8 1.2 multiply_divide_fusion
  151.0 1.9 %copy.23 = f32[2,32,80,32]{3,2,1,0:T(8,128)S(1)} copy(f32[2,32,80,32]{2,1,3,0:T(8,128)} %multiply_divide_fusion) | data formatting | bytes 1310720 | tf_op jit(solution)/shard_map/div | solution.py:81
  152.9 1.8 %broadcast_in_dim_reshape.3 = f32[1,64,2560]{2,1,0:T(8,128)} reshape(f32[2,32,80,32]{3,2,1,0:T(8,128)S(1)} %copy.23) | data formatting | bytes 1310720 | tf_op jit(solution)/shard_map/broadcast_in_dim;reshape | solution.py:134
  (32 shorter events, 6.1 us)
Async XLA Ops:
  7.2 22.7 %copy-start = (bf16[3,128,512]{2,1,0:T(8,128)(2,1)S(1)}, bf16[3,128,512]{2,1,0:T(8,128)(2,1)}, u32[]{:S(2)}) copy-start(bf16[3,128,512]{2,1,0:T(8,128)(2,1)} %param.5) | copy-start | bytes 1179652
  7.2 51.5 %all-gather.2.cloned.1.call-start = ((), (), s32[]{:S(2)}) async-start(), calls=%async_computation.1 | async-start | bytes 1966080 | tf_op jit(solution)/shard_map/all_gather | solution.py:101
  8.3 9.0 %collective-permute-start = (bf16[3,128,8]{2,1,0:T(8,128)(2,1)S(1)}, bf16[3,128,8]{2,1,0:T(8,128)(2,1)S(1)}, u32[]{:S(2)}, u32[]{:S(2)}) collective-permute-start(bf16[3,128,8]{2,1,0:T(8,128)(2,1)S(1)} %get-tuple-element.13), channel_id=1, source_target_pairs={{0,4},{4,8},{8,12},{12,16},{16,20},{20,24},{24,28},{28,0},{1,5},{5... | collective-permute-start | bytes 18440 | tf_op jit(solution)/shard_map/ppermute | solution.py:18
  11.3 6.7 %collective-permute-start.1 = (bf16[3,128,8]{2,1,0:T(8,128)(2,1)S(1)}, bf16[3,128,8]{2,1,0:T(8,128)(2,1)S(1)}, u32[]{:S(2)}, u32[]{:S(2)}) collective-permute-start(bf16[3,128,8]{2,1,0:T(8,128)(2,1)S(1)} %get-tuple-element.14), channel_id=1, source_target_pairs={{4,0},{8,4},{12,8},{16,12},{20,16},{24,20},{28,24},{0,28},{5,1},{9... | collective-permute-start | bytes 18440 | tf_op jit(solution)/shard_map/ppermute | solution.py:19
  18.9 10.9 %collective-permute-start.2 = (bf16[3,8,528]{2,1,0:T(8,128)(2,1)S(1)}, bf16[3,8,528]{2,1,0:T(8,128)(2,1)S(1)}, u32[]{:S(2)}, u32[]{:S(2)}) collective-permute-start(bf16[3,8,528]{2,1,0:T(8,128)(2,1)S(1)} %get-tuple-element.8), channel_id=1, source_target_pairs={{0,1},{1,2},{2,3},{3,0},{4,5},{5,6},{6,7},{7,4},{8,9},{9,10},{10,1... | collective-permute-start | bytes 76040 | tf_op jit(solution)/shard_map/ppermute | solution.py:18
  19.0 10.9 %collective-permute-start.3 = (bf16[3,8,528]{2,1,0:T(8,128)(2,1)S(1)}, bf16[3,8,528]{2,1,0:T(8,128)(2,1)S(1)}, u32[]{:S(2)}, u32[]{:S(2)}) collective-permute-start(bf16[3,8,528]{2,1,0:T(8,128)(2,1)S(1)} %get-tuple-element.9), channel_id=1, source_target_pairs={{1,0},{2,1},{3,2},{0,3},{5,4},{6,5},{7,6},{4,7},{9,8},{10,9},{11,1... | collective-permute-start | bytes 76040 | tf_op jit(solution)/shard_map/ppermute | solution.py:19
  30.1 1.3 copy-start.2
  30.1 9.7 %copy-start.3 = (s32[4,3,2]{0,2,1:T(2,128)S(1)}, s32[4,3,2]{0,2,1:T(2,128)}, u32[]{:S(2)}) copy-start(s32[4,3,2]{0,2,1:T(2,128)} %param.8) | copy-start | bytes 292
  31.3 97.9 %reduce-scatter.2.cloned.1.call-start = ((), (), s32[]{:S(2)}) async-start(), calls=%async_computation.2 | async-start | bytes 737280 | tf_op jit(solution)/shard_map/reduce_scatter | solution.py:131
  58.7 3.3 %copy-start.4 = (bf16[3,512,512]{2,1,0:T(8,128)(2,1)S(1)}, bf16[3,512,512]{2,1,0:T(8,128)(2,1)}, u32[]{:S(2)}) copy-start(bf16[3,512,512]{2,1,0:T(8,128)(2,1)} %all-gather.2.cloned.1.call-done) | copy-start | bytes 4718596
  64.4 64.8 %copy-start.1 = (f32[32,1280]{1,0:T(8,128)S(1)}, f32[32,1280]{1,0:T(8,128)}, u32[]{:S(2)}) copy-start(f32[32,1280]{1,0:T(8,128)} %param.6) | copy-start | bytes 491524
Sparse Core Ops, SparseCore 0:
  31.5 20.1 all-gather.1
  66.6 62.5 reduce-scatter.1
where the time goes:
time: 162 us
  waiting for transfers between devices  66.4 us (41%)
  between operations  29.6 us (18%)
  matrix products  25.9 us (16%)
  other arithmetic  22.7 us (14%)
  local copies, waits for them, and re-layouts  9.01 us (6%)
  starting transfers between devices  7.99 us (5%)
    reduce_scatter x1, waiting for transfers between devices, per_device(): lax.psum_scatter(total.astype(jnp.bfloat16), 'layer', scatter_dimension=0...  62.7 us
    select_n x5, other arithmetic, spans(): upper = (base + 1) % length  11.9 us
    dot_general x3, matrix products, per_device(): jnp.dot(projected[level], col_weights[level], preferred_element_type=jnp....  7.72 us
    convert_element_type x5, other arithmetic, spans(): (1.0 - fraction).astype(jnp.bfloat16)  4.93 us
    ppermute x2, starting transfers between devices, with_halo(): after = lax.ppermute(initial, axis, down)  4.84 us
    dot_general x1, matrix products, imaging(): jnp.einsum('aibj,kj->aibk', imag, cos_table, precision=highest)  3.34 us
  transfers between devices with their start and end apart: 6, of which 3 were waited for; matrix products, arithmetic and copies ran while one was open for 13% of the time, Pallas kernels for 0%

commit v1 on v0

v1 whole, which is shorter than its diff:
```python
import functools

import jax
import jax.numpy as jnp
import numpy as np
from jax import lax
from jax.experimental import pallas as pl
from jax.experimental.pallas import tpu as pltpu
from jax.sharding import PartitionSpec as P

SUB_PIX = 16
SPOT_PIX = 32
WIND_MAX = 8
LANES = 128
VMEM_LIMIT = 56 * 1024 * 1024

SMEM_SPEC = pl.BlockSpec(memory_space=pltpu.SMEM)
VMEM_SPEC = pl.BlockSpec(memory_space=pltpu.VMEM)


def params():
    return pltpu.CompilerParams(vmem_limit_bytes=VMEM_LIMIT)


def wrap(value, length):
    value = jnp.where(value < 0, value + length, value)
    return jnp.where(value >= length, value - length, value)


def spans(pixel, anchor, num, den, length):
    stretched = (pixel * num).astype(jnp.float32)
    den = jnp.full(pixel.shape, den, jnp.int32).astype(jnp.float32)
    whole = jnp.floor((stretched + 0.5) / den)
    fraction = (stretched - whole * den) / den
    base = wrap(anchor + whole.astype(jnp.int32), length)
    upper = wrap(base + 1, length)
    return base, upper, 1.0 - fraction, fraction


def weights_kernel(geometry, wind, offsets, ratio, amplitude, ones, rows_out, cols_out, amp_out):
    n_layer, n_dir, rows_dev, cols_dev = geometry
    layers, pupil_rows, screen_rows = rows_out.shape
    pupil_cols = cols_out.shape[2]
    screen_cols = cols_dev * n_layer
    direction = lax.axis_index("dir")
    column = lax.axis_index("layer")
    block = pupil_rows // n_layer
    for level in range(layers):
        num = ratio[level, 0, direction]
        den = ratio[level, 1, direction]
        anchor = wrap(offsets[level, 0, direction] - wind[0, level], screen_rows)
        pixel = lax.broadcasted_iota(jnp.int32, (pupil_rows, LANES), 0) + column * block
        pixel = jnp.where(pixel >= pupil_rows, pixel - pupil_rows, pixel)
        base, upper, low, high = spans(pixel, anchor, num, den, screen_rows)
        lane = lax.broadcasted_iota(jnp.int32, (pupil_rows, LANES), 1)
        for peer in range(n_dir):
            for part in range(rows_dev // LANES):
                index = lane + (jnp.bitwise_xor(direction, peer) * rows_dev + part * LANES)
                weight = jnp.where(index == base, low, 0.0)
                weight = jnp.where(index == upper, high, weight)
                start = peer * rows_dev + part * LANES
                rows_out[level, :, start : start + LANES] = weight.astype(jnp.bfloat16)
        anchor = wrap(offsets[level, 1, direction] - wind[1, level], screen_cols)
        first = lax.broadcasted_iota(jnp.int32, (cols_dev, LANES), 0) + column * cols_dev

        def tile(step, carry):
            start = pl.multiple_of(step * LANES, LANES)
            pixel = lax.broadcasted_iota(jnp.int32, (8, LANES), 1) + start
            base, upper, low, high = spans(pixel, anchor, num, den, screen_cols)
            index = first.reshape(cols_dev // 8, 8, LANES)
            weight = jnp.where(index == base[None], low[None], 0.0)
            weight = jnp.where(index == upper[None], high[None], weight)
            weight = weight.reshape(cols_dev, LANES).astype(jnp.bfloat16)
            cols_out[level, :, pl.ds(start, LANES)] = weight
            return carry

        lax.fori_loop(0, pupil_cols // LANES, tile, 0)
    rows = amplitude.shape[0]
    for step in range(pupil_cols // LANES):
        cut = slice(step * LANES, (step + 1) * LANES)
        amp = amplitude[:, cut]
        energy = (amp * amp).reshape(rows // SUB_PIX, SUB_PIX, LANES).sum(axis=1)
        energy = jnp.broadcast_to(energy[:, None], (rows // SUB_PIX, SUB_PIX, LANES)).reshape(rows, LANES)
        total = jnp.dot(energy, ones[...], precision=lax.Precision.HIGHEST, preferred_element_type=jnp.float32)
        amp_out[:, cut] = amp * lax.rsqrt(total)


def project_kernel(peers, rows_ref, cols_ref, *refs):
    blocks, outs = refs[:peers], refs[peers:]
    layers, pupil_rows, screen_rows = rows_ref.shape
    _, cols_dev, pupil_cols = cols_ref.shape
    size = outs[0].shape[0]
    group = min(pupil_rows, 256)
    per_group = group // size
    for at in range(pupil_rows // group):
        projected = []
        for level in range(layers):
            screen = jnp.concatenate([block[level] for block in blocks], axis=0)
            rows = rows_ref[level, at * group : (at + 1) * group, :]
            part = jnp.dot(rows, screen, preferred_element_type=jnp.float32)
            projected.append(part.astype(jnp.bfloat16))
        projected = jnp.concatenate(projected, axis=1)
        for start in range(0, pupil_cols, 256):
            cols = cols_ref[:, :, start : start + 256].reshape(layers * cols_dev, 256)
            phase = jnp.dot(projected, cols, preferred_element_type=jnp.float32)
            for k in range(per_group):
                piece = phase[k * size : (k + 1) * size].astype(jnp.bfloat16)
                outs[at * per_group + k][:, start : start + 256] = piece


def rows_kernel(wind, own, near, far, moved, right, left):
    layers, rows, cols = own.shape
    odd = lax.rem(lax.axis_index("dir"), 2) == 1
    lane = lax.broadcasted_iota(jnp.int32, (rows, LANES), 1)
    to_right = jnp.zeros((rows, LANES), jnp.float32)
    to_left = jnp.zeros((rows, LANES), jnp.float32)
    for level in range(layers):
        near_last = near[level, rows - 16 :, :].astype(jnp.float32)
        near_first = near[level, :16, :].astype(jnp.float32)
        far_last = far[level, rows - 16 :, :].astype(jnp.float32)
        far_first = far[level, :16, :].astype(jnp.float32)
        before = jnp.where(odd, near_last, far_last)
        after = jnp.where(odd, far_first, near_first)
        wide = jnp.concatenate([before, own[level].astype(jnp.float32), after], axis=0)
        shift = wind[0, level]
        shift = jnp.where(shift < 0, shift + rows + 32, shift)
        wide = pltpu.roll(wide, shift, 0)[16 : 16 + rows]
        moved[level] = wide.astype(jnp.bfloat16)
        mine = (lane >= WIND_MAX * level) & (lane < WIND_MAX * (level + 1))
        last = pltpu.roll(wide[:, cols - LANES :], WIND_MAX * (level + 1), 1)
        to_right = jnp.where(mine, last, to_right)
        initial = wide[:, :LANES]
        if level:
            initial = pltpu.roll(initial, WIND_MAX * level, 1)
        to_left = jnp.where(mine, initial, to_left)
    right[...] = to_right.astype(jnp.bfloat16)
    left[...] = to_left.astype(jnp.bfloat16)


def cols_kernel(wind, moved, from_left, from_right, out):
    layers, rows, cols = moved.shape
    lane = lax.broadcasted_iota(jnp.int32, (rows, LANES), 1)
    before = from_left[...].astype(jnp.float32)
    after = from_right[...].astype(jnp.float32)
    for level in range(layers):
        last = pltpu.roll(before, LANES - WIND_MAX * (level + 1), 1)
        first = pltpu.roll(after, LANES - WIND_MAX * level, 1) if level else after
        extra = jnp.where(lane < WIND_MAX, first, last)
        wide = jnp.concatenate([moved[level].astype(jnp.float32), extra], axis=1)
        shift = wind[1, level]
        shift = jnp.where(shift < 0, shift + cols + LANES, shift)
        out[level] = pltpu.roll(wide, shift, 1)[:, :cols].astype(jnp.bfloat16)


def sin_cos(phase):
    turns = jnp.floor(phase * (1.0 / np.pi) + 0.5)
    rest = phase - turns * 3.140625
    rest = rest - turns * 9.67653589793e-4
    odd = turns - 2.0 * jnp.floor(turns * 0.5)
    sign = 1.0 - 2.0 * odd
    square = rest * rest
    sine = -1.0 / 39916800.0
    for term in (1.0 / 362880.0, -1.0 / 5040.0, 1.0 / 120.0, -1.0 / 6.0, 1.0):
        sine = sine * square + term
    cosine = 1.0 / 479001600.0
    for term in (-1.0 / 3628800.0, 1.0 / 40320.0, -1.0 / 720.0, 1.0 / 24.0, -0.5, 1.0):
        cosine = cosine * square + term
    return sine * rest * sign, cosine * sign


def split(value):
    high = value.astype(jnp.bfloat16)
    low = (value - high.astype(jnp.float32)).astype(jnp.bfloat16)
    return high, low


def imaging_kernel(count, *refs):
    parts = refs[:count]
    amp_ref, cols_high, cols_low, rows_table, out = refs[count:]
    rows, cols = amp_ref.shape
    tiles = cols // LANES
    phase = parts[0][...].astype(jnp.float32)
    for part in parts[1:]:
        phase = phase + part[...].astype(jnp.float32)
    sine, cosine = sin_cos(phase)
    amp = amp_ref[...]
    real, imag = amp * cosine, amp * sine
    field = jnp.concatenate(
        [
            jnp.concatenate(
                [real[:, t * LANES : (t + 1) * LANES], imag[:, t * LANES : (t + 1) * LANES]], axis=1
            )
            for t in range(tiles)
        ],
        axis=0,
    )
    high, low = split(field)
    dot = functools.partial(jnp.dot, preferred_element_type=jnp.float32)
    half = dot(high, cols_high[...]) + (dot(low, cols_high[...]) + dot(high, cols_low[...]))
    wide = 2 * LANES
    out_rows = 2 * rows
    for t in range(tiles):
        mine = half[t * rows : (t + 1) * rows]
        mine = jnp.concatenate([mine[:, :wide], mine[:, wide:]], axis=0)
        high, low = split(mine)
        full = dot(rows_table[...], jnp.concatenate([high, low, high], axis=0))
        real, imag = full[:out_rows], full[out_rows:]
        out[:, t * wide : (t + 1) * wide] = real * real + imag * imag


def tables(rows):
    freq = np.arange(SPOT_PIX)[:, None] - SPOT_PIX // 2
    angle = ((freq * np.arange(SUB_PIX)[None, :]) % SPOT_PIX) * (2.0 * np.pi / SPOT_PIX)
    cos, sin = np.cos(angle), np.sin(angle)

    def blocks(table, count):
        return np.kron(np.eye(count), table)

    per_tile = LANES // SUB_PIX
    col_cos, col_sin = blocks(cos.T, per_tile), blocks(sin.T, per_tile)
    columns = np.block([[col_cos, -col_sin], [col_sin, col_cos]])
    count = rows // SUB_PIX
    row_cos, row_sin = blocks(cos, count), blocks(sin, count)
    lines = np.block([[row_cos, row_sin], [-row_sin, row_cos]])

    def halves(value):
        value = value.astype(np.float32)
        high = value.astype(jnp.bfloat16)
        return high, (value - high.astype(np.float32)).astype(jnp.bfloat16)

    cols_high, cols_low = halves(columns)
    rows_high, rows_low = halves(lines)
    return cols_high, cols_low, np.concatenate([rows_high, rows_high, rows_low], axis=1)


def per_device(screens, amplitude, wind, offsets, ratio):
    layers, rows_dev, cols_dev = screens.shape
    n_layer = lax.axis_size("layer")
    n_dir = lax.axis_size("dir")
    assert n_dir == 4
    rows, pupil_cols = amplitude.shape
    pupil_rows = rows * n_layer
    screen_rows = rows_dev * n_dir
    bf16, f32 = jnp.bfloat16, jnp.float32
    wind = jnp.transpose(wind, (1, 0))
    offsets = jnp.transpose(offsets, (1, 2, 0))
    ratio = jnp.transpose(ratio, (1, 2, 0))

    def swap(value, bit):
        return lax.ppermute(value, "dir", [(i, i ^ bit) for i in range(n_dir)])

    def turn(value, step):
        return lax.ppermute(value, "layer", [(i, (i + step) % n_layer) for i in range(n_layer)])

    across = swap(screens, 2)
    near = swap(screens, 1)
    far = swap(across, 1)

    ones = np.kron(np.eye(LANES // SUB_PIX), np.ones((SUB_PIX, SUB_PIX))).astype(np.float32)
    row_weights, col_weights, amp = pl.pallas_call(
        functools.partial(weights_kernel, (n_layer, n_dir, rows_dev, cols_dev)),
        out_shape=(
            jax.ShapeDtypeStruct((layers, pupil_rows, screen_rows), bf16),
            jax.ShapeDtypeStruct((layers, cols_dev, pupil_cols), bf16),
            jax.ShapeDtypeStruct((rows, pupil_cols), f32),
        ),
        in_specs=[SMEM_SPEC] * 3 + [VMEM_SPEC] * 2,
        out_specs=[VMEM_SPEC] * 3,
        compiler_params=params(),
        cost_estimate=pl.CostEstimate(flops=8_000_000, bytes_accessed=6_000_000, transcendentals=0),
        name="weights",
    )(wind, offsets, ratio, amplitude, jnp.asarray(ones))

    partials = pl.pallas_call(
        functools.partial(project_kernel, n_dir),
        out_shape=[jax.ShapeDtypeStruct((rows, pupil_cols), bf16)] * n_layer,
        in_specs=[VMEM_SPEC] * (2 + n_dir),
        out_specs=[VMEM_SPEC] * n_layer,
        compiler_params=params(),
        cost_estimate=pl.CostEstimate(flops=1_400_000_000, bytes_accessed=6_000_000, transcendentals=0),
        name="project",
    )(row_weights, col_weights, screens, near, across, far)

    received = [partials[0]] + [turn(partials[k], k) for k in range(1, n_layer)]

    moved, right, left = pl.pallas_call(
        rows_kernel,
        out_shape=(
            jax.ShapeDtypeStruct((layers, rows_dev, cols_dev), bf16),
            jax.ShapeDtypeStruct((rows_dev, LANES), bf16),
            jax.ShapeDtypeStruct((rows_dev, LANES), bf16),
        ),
        in_specs=[SMEM_SPEC] + [VMEM_SPEC] * 3,
        out_specs=[VMEM_SPEC] * 3,
        compiler_params=params(),
        cost_estimate=pl.CostEstimate(flops=1_000_000, bytes_accessed=1_600_000, transcendentals=0),
        name="shift_rows",
    )(wind, screens, near, far)
    from_left = turn(right, 1)
    from_right = turn(left, n_layer - 1)
    new_screens = pl.pallas_call(
        cols_kernel,
        out_shape=jax.ShapeDtypeStruct((layers, rows_dev, cols_dev), bf16),
        in_specs=[SMEM_SPEC] + [VMEM_SPEC] * 3,
        out_specs=VMEM_SPEC,
        compiler_params=params(),
        cost_estimate=pl.CostEstimate(flops=1_000_000, bytes_accessed=1_000_000, transcendentals=0),
        name="shift_cols",
    )(wind, moved, from_left, from_right)

    spots = pl.pallas_call(
        functools.partial(imaging_kernel, n_layer),
        out_shape=jax.ShapeDtypeStruct((2 * rows, 2 * pupil_cols), f32),
        in_specs=[VMEM_SPEC] * (n_layer + 4),
        out_specs=VMEM_SPEC,
        compiler_params=params(),
        cost_estimate=pl.CostEstimate(flops=400_000_000, bytes_accessed=2_000_000, transcendentals=0),
        name="imaging",
    )(*received, amp, *[jnp.asarray(table) for table in tables(rows)])
    return (new_screens, spots[None])


def solution(mesh):
    return jax.shard_map(
        per_device,
        mesh=mesh,
        in_specs=(P(None, "dir", "layer"), P("layer", None), P(), P(), P()),
        out_specs=(P(None, "dir", "layer"), P("dir", "layer", None)),
        check_vma=False,
    )
```

time: 162 us -> 56.9 us (0.35)
  waiting for transfers between devices: 66.4 us -> 17.4 us
  between operations: 29.6 us -> 0.76 us
  matrix products: 25.9 us -> 0 us
  other arithmetic: 22.7 us -> 0 us
  Pallas kernels: 0 us -> 18.5 us
  starting transfers between devices: 7.99 us -> 18.6 us
  local copies, waits for them, and re-layouts: 9.01 us -> 1.48 us
    reduce_scatter x1 -> x0, waiting for transfers between devices: 62.7 us -> none  [per_device(): lax.psum_scatter(total.astype(jnp.bfloat16), 'layer', scatter_dimension=0...]
    dot_general x11 -> x0, matrix products: 25.9 us -> none  [the longest x3 7.72 us: per_device(): jnp.dot(projected[level], col_weights[level], preferred_element_type=jnp....]
    pallas_call x0 -> x5, Pallas kernels: none -> 18.5 us  [the longest x1 5.61 us: per_device(): pl.pallas_call(functools.partial(weights_kernel, (n_layer, n_dir, rows_de...]
    ppermute x4 -> x12, waiting for transfers between devices: 3.62 us -> 17.4 us  [the longest x3 9.33 us: swap(): return lax.ppermute(value, 'dir', [(i, i ^ bit) for i in range(n_dir)])]
    select_n x5 -> x0, other arithmetic: 11.9 us -> none  [spans(): upper = (base + 1) % length]
    ppermute x4 -> x12, starting transfers between devices: 7.91 us -> 18.6 us  [the longest x9 15.5 us: turn(): lax.ppermute(value, 'layer', [(i, (i + step) % n_layer) for i in range(n_...]
    convert_element_type x6 -> x0, other arithmetic: 6.22 us -> none  [the longest x5 4.93 us: spans(): (1.0 - fraction).astype(jnp.bfloat16)]
    slice x3 -> x0, local copies, waits for them, and re-layouts: 2.69 us -> none  [the longest x1 1.56 us: per_device(): wind[level, 1]]
  transfers between devices with their start and end apart: 6 -> 12, of which waited for: 3 -> 5; matrix products, arithmetic and copies ran while one was open for 13% -> 0% of each run, Pallas kernels for 0% -> 18%
where the time goes in v1:
time: 56.9 us; the launch traced here: 56.6 us
  starting transfers between devices  18.6 us (33%)
  Pallas kernels  18.5 us (33%)
  waiting for transfers between devices  17.4 us (31%)
  local copies, waits for them, and re-layouts  1.48 us (3%)
  between operations  0.76 us (1%)
    ppermute x9, starting transfers between devices, turn(): lax.ppermute(value, 'layer', [(i, (i + step) % n_layer) for i in range(n_...  15.5 us
    ppermute x3, waiting for transfers between devices, swap(): return lax.ppermute(value, 'dir', [(i, i ^ bit) for i in range(n_dir)])  9.33 us
    ppermute x9, waiting for transfers between devices, turn(): lax.ppermute(value, 'layer', [(i, (i + step) % n_layer) for i in range(n_...  8.03 us
    pallas_call x1, Pallas kernels, per_device(): pl.pallas_call(functools.partial(weights_kernel, (n_layer, n_dir, rows_de...  5.61 us
    pallas_call x1, Pallas kernels, per_device(): pl.pallas_call(functools.partial(project_kernel, n_dir), out_shape=[jax.S...  5.28 us
    pallas_call x1, Pallas kernels, per_device(): pl.pallas_call(functools.partial(imaging_kernel, n_layer), out_shape=jax....  3.09 us
    ppermute x3, starting transfers between devices, swap(): return lax.ppermute(value, 'dir', [(i, i ^ bit) for i in range(n_dir)])  3.01 us
    pallas_call x1, Pallas kernels, per_device(): pl.pallas_call(rows_kernel, out_shape=(jax.ShapeDtypeStruct((layers, rows...  2.35 us
  transfers between devices with their start and end apart: 12, of which 5 were waited for; matrix products, arithmetic and copies ran while one was open for 0% of the time, Pallas kernels for 18%

profile of v1, /device:TPU:0, one launch (start us, length us, event | category | flops | bytes accessed | tf_op | source)
XLA Modules:
  0.0 56.6 jit_solution(7066767920197011990)
XLA Ops:
  0.6 3.0 %collective-permute-start.1 = (bf16[3,128,512]{2,1,0:T(8,128)(2,1)}, bf16[3,128,512]{2,1,0:T(8,128)(2,1)S(1)}, u32[]{:S(2)}, u32[]{:S(2)}) collective-permute-start(bf16[3,128,512]{2,1,0:T(8,128)(2,1)} %refs_0_.1), channel_id=1, source_target_pairs={{0,2},{1,3},{2,0},{3,1},{4,6},{5,7},{6,4},{7,5},{8,10},{9,11},{10,... | collective-permute-start | bytes 1179656 | tf_op jit(solution)/shard_map/ppermute | solution.py:250
  3.6 0.0 collective-permute-start
  3.6 9.3 %collective-permute-done.1.refs_2_ = bf16[3,128,512]{2,1,0:T(8,128)(2,1)S(1)} collective-permute-done((bf16[3,128,512]{2,1,0:T(8,128)(2,1)}, bf16[3,128,512]{2,1,0:T(8,128)(2,1)S(1)}, u32[]{:S(2)}, u32[]{:S(2)}) %collective-permute-start.1) | collective-permute-done | bytes 393248 | tf_op jit(solution)/shard_map/ppermute | solution.py:250
  13.0 0.0 collective-permute-start.2
  13.0 5.6 %weights.1 = (bf16[3,256,512]{2,1,0:T(8,128)(2,1)}, bf16[3,512,1280]{2,1,0:T(8,128)(2,1)}, f32[32,1280]{1,0:T(8,128)}) custom-call(s32[2,3]{1,0:T(2,128)} %bitcast.5, s32[3,2,4]{2,1,0:T(2,128)} %bitcast.8, s32[3,2,4]{2,1,0:T(2,128)} %bitcast.9, f32[32,1280]{1,0:T(8,128)} %amplitude.1, f32[128,128]{1,0:T(8,128)} %constant.8.clone.ones), custom_call_target="tpu_custom_call" | custom-call | flops 8000000 | bytes 6000000 | tf_op jit(solution)/shard_map/weights/pallas_call | solution.py:260
  18.6 0.0 collective-permute-done.near.refs_1_
  18.6 0.0 collective-permute-done.2.far.refs_3_
  18.6 0.0 copy-start.1
  18.6 0.7 %copy-done = bf16[3,128,512]{2,1,0:T(8,128)(2,1)} copy-done((bf16[3,128,512]{2,1,0:T(8,128)(2,1)}, bf16[3,128,512]{2,1,0:T(8,128)(2,1)S(1)}, u32[]{:S(2)}) %copy-start) | copy-done | bytes 393240
  19.3 0.1 copy-done.1
  19.5 5.3 %project.1 = (bf16[32,1280]{1,0:T(8,128)(2,1)}, bf16[32,1280]{1,0:T(8,128)(2,1)}, bf16[32,1280]{1,0:T(8,128)(2,1)}, bf16[32,1280]{1,0:T(8,128)(2,1)}, bf16[32,12...) custom-call(bf16[3,256,512]{2,1,0:T(8,128)(2,1)} %get-tuple-element.19.rows_ref,, ...), custom_call_target="tpu_custom_call" | custom-call | flops 1400000000 | bytes 6000000 | tf_op jit(solution)/shard_map/project/pallas_call | solution.py:274
  24.7 3.9 %collective-permute-start.10 = (bf16[32,1280]{1,0:T(8,128)(2,1)}, bf16[32,1280]{1,0:T(8,128)(2,1)S(1)}, u32[]{:S(2)}, u32[]{:S(2)}) collective-permute-start(bf16[32,1280]{1,0:T(8,128)(2,1)} %get-tuple-element.27), channel_id=1, source_target_pairs={{0,24},{4,28},{8,0},{12,4},{16,8},{20,12},{24,16},{28,20},{1,25},{... | collective-permute-start | bytes 245768 | tf_op jit(solution)/shard_map/ppermute | solution.py:253
  28.6 1.4 %collective-permute-start.11 = (bf16[32,1280]{1,0:T(8,128)(2,1)}, bf16[32,1280]{1,0:T(8,128)(2,1)S(1)}, u32[]{:S(2)}, u32[]{:S(2)}) collective-permute-start(bf16[32,1280]{1,0:T(8,128)(2,1)} %get-tuple-element.28), channel_id=1, source_target_pairs={{0,28},{4,0},{8,4},{12,8},{16,12},{20,16},{24,20},{28,24},{1,29},{... | collective-permute-start | bytes 245768 | tf_op jit(solution)/shard_map/ppermute | solution.py:253
  30.0 2.3 %shift_rows.1 = (bf16[3,128,512]{2,1,0:T(8,128)(2,1)}, bf16[128,128]{1,0:T(8,128)(2,1)}, bf16[128,128]{1,0:T(8,128)(2,1)}) custom-call(s32[2,3]{1,0:T(2,128)} %bitcast.6, bf16[3,128,512]{2,1,0:T(8,128)(2,1)} %refs_0_.1, bf16[3,128,512]{2,1,0:T(8,128)(2,1)} %copy-done, bf16[3,128,512]{2,1,0:T(8,128)(2,1)} %copy-done.1), custom_call_target="tpu_custom_call" | custom-call | flops 1000000 | bytes 1600000 | tf_op jit(solution)/shard_map/shift_rows/pallas_call | solution.py:286
  32.4 0.6 %collective-permute-start.3 = (bf16[128,128]{1,0:T(8,128)(2,1)}, bf16[128,128]{1,0:T(8,128)(2,1)S(1)}, u32[]{:S(2)}, u32[]{:S(2)}) collective-permute-start(bf16[128,128]{1,0:T(8,128)(2,1)} %get-tuple-element.17), channel_id=1, source_target_pairs={{0,4},{4,8},{8,12},{12,16},{16,20},{20,24},{24,28},{28,0},{1,5},{5... | collective-permute-start | bytes 98312 | tf_op jit(solution)/shard_map/ppermute | solution.py:253
  33.0 4.1 %collective-permute-start.4 = (bf16[128,128]{1,0:T(8,128)(2,1)}, bf16[128,128]{1,0:T(8,128)(2,1)S(1)}, u32[]{:S(2)}, u32[]{:S(2)}) collective-permute-start(bf16[128,128]{1,0:T(8,128)(2,1)} %get-tuple-element.18), channel_id=1, source_target_pairs={{0,28},{4,0},{8,4},{12,8},{16,12},{20,16},{24,20},{28,24},{1,29},{... | collective-permute-start | bytes 98312 | tf_op jit(solution)/shard_map/ppermute | solution.py:253
  37.1 0.0 collective-permute-start.5
  37.1 2.1 %collective-permute-done.3.from_left = bf16[128,128]{1,0:T(8,128)(2,1)S(1)} collective-permute-done((bf16[128,128]{1,0:T(8,128)(2,1)}, bf16[128,128]{1,0:T(8,128)(2,1)S(1)}, u32[]{:S(2)}, u32[]{:S(2)}) %collective-permute-start.3) | collective-permute-done | bytes 32800 | tf_op jit(solution)/shard_map/ppermute | solution.py:253
  39.2 0.0 collective-permute-done.4.from_right
  39.2 0.1 collective-permute-start.7
  39.3 0.0 collective-permute-done.10.refs_6_
  39.3 5.5 %collective-permute-start.8 = (bf16[32,1280]{1,0:T(8,128)(2,1)}, bf16[32,1280]{1,0:T(8,128)(2,1)S(1)}, u32[]{:S(2)}, u32[]{:S(2)}) collective-permute-start(bf16[32,1280]{1,0:T(8,128)(2,1)} %get-tuple-element.25), channel_id=1, source_target_pairs={{0,16},{4,20},{8,24},{12,28},{16,0},{20,4},{24,8},{28,12},{1,17},{... | collective-permute-start | bytes 245768 | tf_op jit(solution)/shard_map/ppermute | solution.py:253
  44.8 0.0 collective-permute-done.11.refs_7_
  44.8 0.0 collective-permute-start.9
  44.8 2.2 %shift_cols.1 = bf16[3,128,512]{2,1,0:T(8,128)(2,1)} custom-call(s32[2,3]{1,0:T(2,128)} %bitcast.7, bf16[3,128,512]{2,1,0:T(8,128)(2,1)} %get-tuple-element.16.moved, bf16[128,128]{1,0:T(8,128)(2,1)} %copy-done.10, bf16[128,128]{1,0:T(8,128)(2,1)} %copy-done.11), custom_call_target="tpu_custom_call" | custom-call | flops 1000000 | bytes 1000000 | tf_op jit(solution)/shard_map/shift_cols/pallas_call | solution.py:301
  47.0 0.0 collective-permute-done.5.refs_1_
  47.0 0.0 collective-permute-done.6.refs_2_
  47.0 3.8 %collective-permute-done.7.refs_3_ = bf16[32,1280]{1,0:T(8,128)(2,1)S(1)} collective-permute-done((bf16[32,1280]{1,0:T(8,128)(2,1)}, bf16[32,1280]{1,0:T(8,128)(2,1)S(1)}, u32[]{:S(2)}, u32[]{:S(2)}) %collective-permute-start.7) | collective-permute-done | bytes 81952 | tf_op jit(solution)/shard_map/ppermute | solution.py:253
  50.8 0.7 %collective-permute-done.8.refs_4_ = bf16[32,1280]{1,0:T(8,128)(2,1)S(1)} collective-permute-done((bf16[32,1280]{1,0:T(8,128)(2,1)}, bf16[32,1280]{1,0:T(8,128)(2,1)S(1)}, u32[]{:S(2)}, u32[]{:S(2)}) %collective-permute-start.8) | collective-permute-done | bytes 81952 | tf_op jit(solution)/shard_map/ppermute | solution.py:253
  51.5 1.4 %collective-permute-done.9.refs_5_ = bf16[32,1280]{1,0:T(8,128)(2,1)S(1)} collective-permute-done((bf16[32,1280]{1,0:T(8,128)(2,1)}, bf16[32,1280]{1,0:T(8,128)(2,1)S(1)}, u32[]{:S(2)}, u32[]{:S(2)}) %collective-permute-start.9) | collective-permute-done | bytes 81952 | tf_op jit(solution)/shard_map/ppermute | solution.py:253
  53.0 0.6 %copy-done.9 = bf16[32,1280]{1,0:T(8,128)(2,1)} copy-done((bf16[32,1280]{1,0:T(8,128)(2,1)}, bf16[32,1280]{1,0:T(8,128)(2,1)S(1)}, u32[]{:S(2)}) %copy-start.9) | copy-done | bytes 81944
  53.6 3.1 %imaging.1 = f32[64,2560]{1,0:T(8,128)} custom-call(bf16[32,1280]{1,0:T(8,128)(2,1)} %get-tuple-element.21.refs_0_, bf16[32,1280]{1,0:T(8,128)(2,1)} %copy-done.5, bf16[32,1280]{1,0:T(8,128)(2,1)} %copy-done.6, bf16[32,1280]{1,0:T(8,128)(2,1)} %copy-done.7, bf16[32,1280]{1,0:T(8,128)(2,1)} %copy-done.8, bf16[32,1280]{1,0:T(8,128)(2,1)} %copy-done.9, ...), custom_call_target="tpu_custom_call" | custom-call | flops 400000000 | bytes 2000000 | tf_op jit(solution)/shard_map/imaging/pallas_call | solution.py:311
  (21 shorter events, 0.0 us)
Async XLA Ops:
  0.6 12.3 %collective-permute-start.1 = (bf16[3,128,512]{2,1,0:T(8,128)(2,1)}, bf16[3,128,512]{2,1,0:T(8,128)(2,1)S(1)}, u32[]{:S(2)}, u32[]{:S(2)}) collective-permute-start(bf16[3,128,512]{2,1,0:T(8,128)(2,1)} %refs_0_.1), channel_id=1, source_target_pairs={{0,2},{1,3},{2,0},{3,1},{4,6},{5,7},{6,4},{7,5},{8,10},{9,11},{10,... | collective-permute-start | bytes 1179656 | tf_op jit(solution)/shard_map/ppermute | solution.py:250
  3.6 14.9 %collective-permute-start = (bf16[3,128,512]{2,1,0:T(8,128)(2,1)}, bf16[3,128,512]{2,1,0:T(8,128)(2,1)S(1)}, u32[]{:S(2)}, u32[]{:S(2)}) collective-permute-start(bf16[3,128,512]{2,1,0:T(8,128)(2,1)} %refs_0_.1), channel_id=1, source_target_pairs={{0,1},{1,0},{2,3},{3,2},{4,5},{5,4},{6,7},{7,6},{8,9},{9,8},{10,11... | collective-permute-start | bytes 1179656 | tf_op jit(solution)/shard_map/ppermute | solution.py:250
  13.0 5.6 %copy-start.2 = (bf16[3,128,512]{2,1,0:T(8,128)(2,1)}, bf16[3,128,512]{2,1,0:T(8,128)(2,1)S(1)}, u32[]{:S(2)}) copy-start(bf16[3,128,512]{2,1,0:T(8,128)(2,1)S(1)} %collective-permute-done.1.refs_2_) | copy-start | bytes 1179652
  13.0 5.6 %collective-permute-start.2 = (bf16[3,128,512]{2,1,0:T(8,128)(2,1)S(1)}, bf16[3,128,512]{2,1,0:T(8,128)(2,1)S(1)}, u32[]{:S(2)}, u32[]{:S(2)}) collective-permute-start(bf16[3,128,512]{2,1,0:T(8,128)(2,1)S(1)} %collective-permute-done.1.refs_2_), channel_id=1, source_target_pairs={{0,1},{1,0},{2,3},{3,2},{4,5},{5,4},{6,7},{7,6},{8,9},{9,8},{10,11... | collective-permute-start | bytes 1179656 | tf_op jit(solution)/shard_map/ppermute | solution.py:250
  18.6 0.7 %copy-start = (bf16[3,128,512]{2,1,0:T(8,128)(2,1)}, bf16[3,128,512]{2,1,0:T(8,128)(2,1)S(1)}, u32[]{:S(2)}) copy-start(bf16[3,128,512]{2,1,0:T(8,128)(2,1)S(1)} %collective-permute-done.near.refs_1_) | copy-start | bytes 1179652
  18.6 0.9 %copy-start.1 = (bf16[3,128,512]{2,1,0:T(8,128)(2,1)}, bf16[3,128,512]{2,1,0:T(8,128)(2,1)S(1)}, u32[]{:S(2)}) copy-start(bf16[3,128,512]{2,1,0:T(8,128)(2,1)S(1)} %collective-permute-done.2.far.refs_3_) | copy-start | bytes 1179652
  24.7 14.5 %collective-permute-start.10 = (bf16[32,1280]{1,0:T(8,128)(2,1)}, bf16[32,1280]{1,0:T(8,128)(2,1)S(1)}, u32[]{:S(2)}, u32[]{:S(2)}) collective-permute-start(bf16[32,1280]{1,0:T(8,128)(2,1)} %get-tuple-element.27), channel_id=1, source_target_pairs={{0,24},{4,28},{8,0},{12,4},{16,8},{20,12},{24,16},{28,20},{1,25},{... | collective-permute-start | bytes 245768 | tf_op jit(solution)/shard_map/ppermute | solution.py:253
  28.6 16.2 %collective-permute-start.11 = (bf16[32,1280]{1,0:T(8,128)(2,1)}, bf16[32,1280]{1,0:T(8,128)(2,1)S(1)}, u32[]{:S(2)}, u32[]{:S(2)}) collective-permute-start(bf16[32,1280]{1,0:T(8,128)(2,1)} %get-tuple-element.28), channel_id=1, source_target_pairs={{0,28},{4,0},{8,4},{12,8},{16,12},{20,16},{24,20},{28,24},{1,29},{... | collective-permute-start | bytes 245768 | tf_op jit(solution)/shard_map/ppermute | solution.py:253
  32.4 6.8 %collective-permute-start.3 = (bf16[128,128]{1,0:T(8,128)(2,1)}, bf16[128,128]{1,0:T(8,128)(2,1)S(1)}, u32[]{:S(2)}, u32[]{:S(2)}) collective-permute-start(bf16[128,128]{1,0:T(8,128)(2,1)} %get-tuple-element.17), channel_id=1, source_target_pairs={{0,4},{4,8},{8,12},{12,16},{16,20},{20,24},{24,28},{28,0},{1,5},{5... | collective-permute-start | bytes 98312 | tf_op jit(solution)/shard_map/ppermute | solution.py:253
  33.0 6.2 %collective-permute-start.4 = (bf16[128,128]{1,0:T(8,128)(2,1)}, bf16[128,128]{1,0:T(8,128)(2,1)S(1)}, u32[]{:S(2)}, u32[]{:S(2)}) collective-permute-start(bf16[128,128]{1,0:T(8,128)(2,1)} %get-tuple-element.18), channel_id=1, source_target_pairs={{0,28},{4,0},{8,4},{12,8},{16,12},{20,16},{24,20},{28,24},{1,29},{... | collective-permute-start | bytes 98312 | tf_op jit(solution)/shard_map/ppermute | solution.py:253
  37.1 9.9 %collective-permute-start.5 = (bf16[32,1280]{1,0:T(8,128)(2,1)}, bf16[32,1280]{1,0:T(8,128)(2,1)S(1)}, u32[]{:S(2)}, u32[]{:S(2)}) collective-permute-start(bf16[32,1280]{1,0:T(8,128)(2,1)} %get-tuple-element.22), channel_id=1, source_target_pairs={{0,4},{4,8},{8,12},{12,16},{16,20},{20,24},{24,28},{28,0},{1,5},{5... | collective-permute-start | bytes 245768 | tf_op jit(solution)/shard_map/ppermute | solution.py:253
  39.2 5.6 %copy-start.10 = (bf16[128,128]{1,0:T(8,128)(2,1)}, bf16[128,128]{1,0:T(8,128)(2,1)S(1)}, u32[]{:S(2)}) copy-start(bf16[128,128]{1,0:T(8,128)(2,1)S(1)} %collective-permute-done.3.from_left) | copy-start | bytes 98308
  39.2 7.8 %collective-permute-start.6 = (bf16[32,1280]{1,0:T(8,128)(2,1)}, bf16[32,1280]{1,0:T(8,128)(2,1)S(1)}, u32[]{:S(2)}, u32[]{:S(2)}) collective-permute-start(bf16[32,1280]{1,0:T(8,128)(2,1)} %get-tuple-element.23), channel_id=1, source_target_pairs={{0,8},{4,12},{8,16},{12,20},{16,24},{20,28},{24,0},{28,4},{1,9},{5... | collective-permute-start | bytes 245768 | tf_op jit(solution)/shard_map/ppermute | solution.py:253
  39.2 5.6 %copy-start.11 = (bf16[128,128]{1,0:T(8,128)(2,1)}, bf16[128,128]{1,0:T(8,128)(2,1)S(1)}, u32[]{:S(2)}) copy-start(bf16[128,128]{1,0:T(8,128)(2,1)S(1)} %collective-permute-done.4.from_right) | copy-start | bytes 98308
  39.2 11.6 %collective-permute-start.7 = (bf16[32,1280]{1,0:T(8,128)(2,1)}, bf16[32,1280]{1,0:T(8,128)(2,1)S(1)}, u32[]{:S(2)}, u32[]{:S(2)}) collective-permute-start(bf16[32,1280]{1,0:T(8,128)(2,1)} %get-tuple-element.24), channel_id=1, source_target_pairs={{0,12},{4,16},{8,20},{12,24},{16,28},{20,0},{24,4},{28,8},{1,13},{... | collective-permute-start | bytes 245768 | tf_op jit(solution)/shard_map/ppermute | solution.py:253
  39.3 13.6 %copy-start.3 = (bf16[32,1280]{1,0:T(8,128)(2,1)}, bf16[32,1280]{1,0:T(8,128)(2,1)S(1)}, u32[]{:S(2)}) copy-start(bf16[32,1280]{1,0:T(8,128)(2,1)S(1)} %collective-permute-done.10.refs_6_) | copy-start | bytes 245764
  39.3 12.2 %collective-permute-start.8 = (bf16[32,1280]{1,0:T(8,128)(2,1)}, bf16[32,1280]{1,0:T(8,128)(2,1)S(1)}, u32[]{:S(2)}, u32[]{:S(2)}) collective-permute-start(bf16[32,1280]{1,0:T(8,128)(2,1)} %get-tuple-element.25), channel_id=1, source_target_pairs={{0,16},{4,20},{8,24},{12,28},{16,0},{20,4},{24,8},{28,12},{1,17},{... | collective-permute-start | bytes 245768 | tf_op jit(solution)/shard_map/ppermute | solution.py:253
  44.8 8.2 %copy-start.4 = (bf16[32,1280]{1,0:T(8,128)(2,1)}, bf16[32,1280]{1,0:T(8,128)(2,1)S(1)}, u32[]{:S(2)}) copy-start(bf16[32,1280]{1,0:T(8,128)(2,1)S(1)} %collective-permute-done.11.refs_7_) | copy-start | bytes 245764
  44.8 8.1 %collective-permute-start.9 = (bf16[32,1280]{1,0:T(8,128)(2,1)}, bf16[32,1280]{1,0:T(8,128)(2,1)S(1)}, u32[]{:S(2)}, u32[]{:S(2)}) collective-permute-start(bf16[32,1280]{1,0:T(8,128)(2,1)} %get-tuple-element.26), channel_id=1, source_target_pairs={{0,20},{4,24},{8,28},{12,0},{16,4},{20,8},{24,12},{28,16},{1,21},{... | collective-permute-start | bytes 245768 | tf_op jit(solution)/shard_map/ppermute | solution.py:253
  47.0 6.0 %copy-start.5 = (bf16[32,1280]{1,0:T(8,128)(2,1)}, bf16[32,1280]{1,0:T(8,128)(2,1)S(1)}, u32[]{:S(2)}) copy-start(bf16[32,1280]{1,0:T(8,128)(2,1)S(1)} %collective-permute-done.5.refs_1_) | copy-start | bytes 245764
  47.0 6.0 %copy-start.6 = (bf16[32,1280]{1,0:T(8,128)(2,1)}, bf16[32,1280]{1,0:T(8,128)(2,1)S(1)}, u32[]{:S(2)}) copy-start(bf16[32,1280]{1,0:T(8,128)(2,1)S(1)} %collective-permute-done.6.refs_2_) | copy-start | bytes 245764
  50.8 2.2 %copy-start.7 = (bf16[32,1280]{1,0:T(8,128)(2,1)}, bf16[32,1280]{1,0:T(8,128)(2,1)S(1)}, u32[]{:S(2)}) copy-start(bf16[32,1280]{1,0:T(8,128)(2,1)S(1)} %collective-permute-done.7.refs_3_) | copy-start | bytes 245764
  51.5 1.5 %copy-start.8 = (bf16[32,1280]{1,0:T(8,128)(2,1)}, bf16[32,1280]{1,0:T(8,128)(2,1)S(1)}, u32[]{:S(2)}) copy-start(bf16[32,1280]{1,0:T(8,128)(2,1)S(1)} %collective-permute-done.8.refs_4_) | copy-start | bytes 245764
  52.9 0.6 %copy-start.9 = (bf16[32,1280]{1,0:T(8,128)(2,1)}, bf16[32,1280]{1,0:T(8,128)(2,1)S(1)}, u32[]{:S(2)}) copy-start(bf16[32,1280]{1,0:T(8,128)(2,1)S(1)} %collective-permute-done.9.refs_5_) | copy-start | bytes 245764

commit v2 on v1

--- a/solution.py
+++ b/solution.py
@@ -12,14 +12,31 @@
 SPOT_PIX = 32
 WIND_MAX = 8
 LANES = 128
-VMEM_LIMIT = 56 * 1024 * 1024
 
 SMEM_SPEC = pl.BlockSpec(memory_space=pltpu.SMEM)
 VMEM_SPEC = pl.BlockSpec(memory_space=pltpu.VMEM)
 
 
-def params():
-    return pltpu.CompilerParams(vmem_limit_bytes=VMEM_LIMIT)
+def params(*arrays):
+    held = sum(array.size * array.dtype.itemsize for array in jax.tree.leaves(arrays))
+    return pltpu.CompilerParams(vmem_limit_bytes=held + 8 * 1024 * 1024)
+
+
+def call(kernel, out_shape, operands, flops, name):
+    def spec(array):
+        return SMEM_SPEC if array.dtype == jnp.int32 else VMEM_SPEC
+
+    out_specs = jax.tree.map(lambda _: VMEM_SPEC, out_shape)
+    size = sum(array.size * array.dtype.itemsize for array in jax.tree.leaves((operands, out_shape)))
+    return pl.pallas_call(
+        kernel,
+        out_shape=out_shape,
+        in_specs=[spec(array) for array in operands],
+        out_specs=out_specs,
+        compiler_params=params(operands, out_shape),
+        cost_estimate=pl.CostEstimate(flops=flops, bytes_accessed=size, transcendentals=0),
+        name=name,
+    )(*operands)
 
 
 def wrap(value, length):
@@ -44,13 +61,11 @@
     screen_cols = cols_dev * n_layer
     direction = lax.axis_index("dir")
     column = lax.axis_index("layer")
-    block = pupil_rows // n_layer
     for level in range(layers):
         num = ratio[level, 0, direction]
         den = ratio[level, 1, direction]
         anchor = wrap(offsets[level, 0, direction] - wind[0, level], screen_rows)
-        pixel = lax.broadcasted_iota(jnp.int32, (pupil_rows, LANES), 0) + column * block
-        pixel = jnp.where(pixel >= pupil_rows, pixel - pupil_rows, pixel)
+        pixel = lax.broadcasted_iota(jnp.int32, (pupil_rows, LANES), 0)
         base, upper, low, high = spans(pixel, anchor, num, den, screen_rows)
         lane = lax.broadcasted_iota(jnp.int32, (pupil_rows, LANES), 1)
         for peer in range(n_dir):
@@ -86,10 +101,10 @@
 
 
 def project_kernel(peers, rows_ref, cols_ref, *refs):
-    blocks, outs = refs[:peers], refs[peers:]
+    blocks, out = refs[:peers], refs[peers]
     layers, pupil_rows, screen_rows = rows_ref.shape
     _, cols_dev, pupil_cols = cols_ref.shape
-    size = outs[0].shape[0]
+    size = out.shape[1]
     group = min(pupil_rows, 256)
     per_group = group // size
     for at in range(pupil_rows // group):
@@ -105,7 +120,7 @@
             phase = jnp.dot(projected, cols, preferred_element_type=jnp.float32)
             for k in range(per_group):
                 piece = phase[k * size : (k + 1) * size].astype(jnp.bfloat16)
-                outs[at * per_group + k][:, start : start + 256] = piece
+                out[at * per_group + k, :, start : start + 256] = piece
 
 
 def rows_kernel(wind, own, near, far, moved, right, left):
@@ -174,14 +189,12 @@
     return high, low
 
 
-def imaging_kernel(count, *refs):
-    parts = refs[:count]
-    amp_ref, cols_high, cols_low, rows_table, out = refs[count:]
+def imaging_kernel(parts, amp_ref, cols_high, cols_low, rows_table, out):
     rows, cols = amp_ref.shape
     tiles = cols // LANES
-    phase = parts[0][...].astype(jnp.float32)
-    for part in parts[1:]:
-        phase = phase + part[...].astype(jnp.float32)
+    phase = parts[0].astype(jnp.float32)
+    for k in range(1, parts.shape[0]):
+        phase = phase + parts[k].astype(jnp.float32)
     sine, cosine = sin_cos(phase)
     amp = amp_ref[...]
     real, imag = amp * cosine, amp * sine
@@ -254,69 +267,60 @@
 
     across = swap(screens, 2)
     near = swap(screens, 1)
+
+    def shape(*dims, dtype=bf16):
+        return jax.ShapeDtypeStruct(dims, dtype)
+
+    ones = np.kron(np.eye(LANES // SUB_PIX), np.ones((SUB_PIX, SUB_PIX))).astype(np.float32)
+    row_weights, col_weights, amp = call(
+        functools.partial(weights_kernel, (n_layer, n_dir, rows_dev, cols_dev)),
+        (
+            shape(layers, pupil_rows, screen_rows),
+            shape(layers, cols_dev, pupil_cols),
+            shape(rows, pupil_cols, dtype=f32),
+        ),
+        (wind, offsets, ratio, amplitude, jnp.asarray(ones)),
+        8_000_000,
+        "weights",
+    )
+    across, row_weights, col_weights, amp = lax.optimization_barrier(
+        (across, row_weights, col_weights, amp)
+    )
     far = swap(across, 1)
 
-    ones = np.kron(np.eye(LANES // SUB_PIX), np.ones((SUB_PIX, SUB_PIX))).astype(np.float32)
-    row_weights, col_weights, amp = pl.pallas_call(
-        functools.partial(weights_kernel, (n_layer, n_dir, rows_dev, cols_dev)),
-        out_shape=(
-            jax.ShapeDtypeStruct((layers, pupil_rows, screen_rows), bf16),
-            jax.ShapeDtypeStruct((layers, cols_dev, pupil_cols), bf16),
-            jax.ShapeDtypeStruct((rows, pupil_cols), f32),
-        ),
-        in_specs=[SMEM_SPEC] * 3 + [VMEM_SPEC] * 2,
-        out_specs=[VMEM_SPEC] * 3,
-        compiler_params=params(),
-        cost_estimate=pl.CostEstimate(flops=8_000_000, bytes_accessed=6_000_000, transcendentals=0),
-        name="weights",
-    )(wind, offsets, ratio, amplitude, jnp.asarray(ones))
-
-    partials = pl.pallas_call(
+    partials = call(
         functools.partial(project_kernel, n_dir),
-        out_shape=[jax.ShapeDtypeStruct((rows, pupil_cols), bf16)] * n_layer,
-        in_specs=[VMEM_SPEC] * (2 + n_dir),
-        out_specs=[VMEM_SPEC] * n_layer,
-        compiler_params=params(),
-        cost_estimate=pl.CostEstimate(flops=1_400_000_000, bytes_accessed=6_000_000, transcendentals=0),
-        name="project",
-    )(row_weights, col_weights, screens, near, across, far)
-
-    received = [partials[0]] + [turn(partials[k], k) for k in range(1, n_layer)]
-
-    moved, right, left = pl.pallas_call(
+        shape(n_layer, rows, pupil_cols),
+        (row_weights, col_weights, screens, near, across, far),
+        1_400_000_000,
+        "project",
+    )
+    received = lax.all_to_all(partials, "layer", 0, 0, tiled=True)
+
+    moved, right, left = call(
         rows_kernel,
-        out_shape=(
-            jax.ShapeDtypeStruct((layers, rows_dev, cols_dev), bf16),
-            jax.ShapeDtypeStruct((rows_dev, LANES), bf16),
-            jax.ShapeDtypeStruct((rows_dev, LANES), bf16),
-        ),
-        in_specs=[SMEM_SPEC] + [VMEM_SPEC] * 3,
-        out_specs=[VMEM_SPEC] * 3,
-        compiler_params=params(),
-        cost_estimate=pl.CostEstimate(flops=1_000_000, bytes_accessed=1_600_000, transcendentals=0),
-        name="shift_rows",
-    )(wind, screens, near, far)
+        (shape(layers, rows_dev, cols_dev), shape(rows_dev, LANES), shape(rows_dev, LANES)),
+        (wind, screens, near, far),
+        1_000_000,
+        "shift_rows",
+    )
     from_left = turn(right, 1)
     from_right = turn(left, n_layer - 1)
-    new_screens = pl.pallas_call(
+    new_screens = call(
         cols_kernel,
-        out_shape=jax.ShapeDtypeStruct((layers, rows_dev, cols_dev), bf16),
-        in_specs=[SMEM_SPEC] + [VMEM_SPEC] * 3,
-        out_specs=VMEM_SPEC,
-        compiler_params=params(),
-        cost_estimate=pl.CostEstimate(flops=1_000_000, bytes_accessed=1_000_000, transcendentals=0),
-        name="shift_cols",
-    )(wind, moved, from_left, from_right)
-
-    spots = pl.pallas_call(
-        functools.partial(imaging_kernel, n_layer),
-        out_shape=jax.ShapeDtypeStruct((2 * rows, 2 * pupil_cols), f32),
-        in_specs=[VMEM_SPEC] * (n_layer + 4),
-        out_specs=VMEM_SPEC,
-        compiler_params=params(),
-        cost_estimate=pl.CostEstimate(flops=400_000_000, bytes_accessed=2_000_000, transcendentals=0),
-        name="imaging",
-    )(*received, amp, *[jnp.asarray(table) for table in tables(rows)])
+        shape(layers, rows_dev, cols_dev),
+        (wind, moved, from_left, from_right),
+        1_000_000,
+        "shift_cols",
+    )
+
+    spots = call(
+        imaging_kernel,
+        shape(2 * rows, 2 * pupil_cols, dtype=f32),
+        (received, amp, *[jnp.asarray(table) for table in tables(rows)]),
+        400_000_000,
+        "imaging",
+    )
     return (new_screens, spots[None])
 
 

time: 56.9 us -> 44.7 us (0.79)
  Pallas kernels: 18.5 us -> 10.5 us
  starting transfers between devices: 18.6 us -> 13.9 us
  local copies, waits for them, and re-layouts: 1.48 us -> 4.81 us
  waiting for transfers between devices: 17.4 us -> 14.4 us
    ppermute x9 -> x2, starting transfers between devices: 15.5 us -> 4.83 us  [turn(): lax.ppermute(value, 'layer', [(i, (i + step) % n_layer) for i in range(n_...]
    pallas_call x5, Pallas kernels: 18.5 us -> 10.5 us  [call(): pl.pallas_call(kernel, out_shape=out_shape, in_specs=[spec(array) for arr...]
    all_to_all x0 -> x1, starting transfers between devices: none -> 6.08 us  [per_device(): received = lax.all_to_all(partials, 'layer', 0, 0, tiled=True)]
    ppermute x3, waiting for transfers between devices: 9.33 us -> 3.56 us  [swap(): return lax.ppermute(value, 'dir', [(i, i ^ bit) for i in range(n_dir)])]
    unnamed x24 -> x22, local copies, waits for them, and re-layouts: 1.48 us -> 4.81 us
    ppermute x9 -> x2, waiting for transfers between devices: 8.03 us -> 10.9 us  [turn(): lax.ppermute(value, 'layer', [(i, (i + step) % n_layer) for i in range(n_...]
  transfers between devices with their start and end apart: 12 -> 6, of which waited for: 5 -> 3; matrix products, arithmetic and copies ran while one was open for 0% -> 0% of each run, Pallas kernels for 18% -> 14%
where the time goes in v2:
time: 44.7 us; the launch traced here: 44.4 us
  waiting for transfers between devices  14.4 us (32%)
  starting transfers between devices  13.9 us (31%)
  Pallas kernels  10.5 us (23%)
  local copies, waits for them, and re-layouts  4.81 us (11%)
  between operations  0.69 us (2%)
    ppermute x2, waiting for transfers between devices, turn(): lax.ppermute(value, 'layer', [(i, (i + step) % n_layer) for i in range(n_...  10.9 us
    pallas_call x5, Pallas kernels, call(): pl.pallas_call(kernel, out_shape=out_shape, in_specs=[spec(array) for arr...  10.5 us
    all_to_all x1, starting transfers between devices, per_device(): received = lax.all_to_all(partials, 'layer', 0, 0, tiled=True)  6.08 us
    ppermute x2, starting transfers between devices, turn(): lax.ppermute(value, 'layer', [(i, (i + step) % n_layer) for i in range(n_...  4.83 us
    unnamed x22, local copies, waits for them, and re-layouts  4.81 us
    ppermute x3, waiting for transfers between devices, swap(): return lax.ppermute(value, 'dir', [(i, i ^ bit) for i in range(n_dir)])  3.56 us
    ppermute x3, starting transfers between devices, swap(): return lax.ppermute(value, 'dir', [(i, i ^ bit) for i in range(n_dir)])  3.01 us
  transfers between devices with their start and end apart: 6, of which 3 were waited for; matrix products, arithmetic and copies ran while one was open for 0% of the time, Pallas kernels for 14%

profile of v2, /device:TPU:0, one launch (start us, length us, event | category | flops | bytes accessed | tf_op | source)
XLA Modules:
  0.0 44.4 jit_solution(11943168156591796994)
XLA Ops:
  0.6 3.0 %collective-permute-start.1 = (bf16[3,128,512]{2,1,0:T(8,128)(2,1)}, bf16[3,128,512]{2,1,0:T(8,128)(2,1)S(1)}, u32[]{:S(2)}, u32[]{:S(2)}) collective-permute-start(bf16[3,128,512]{2,1,0:T(8,128)(2,1)} %refs_0_.1), channel_id=1, source_target_pairs={{0,2},{1,3},{2,0},{3,1},{4,6},{5,7},{6,4},{7,5},{8,10},{9,11},{10,... | collective-permute-start | bytes 1179656 | tf_op jit(solution)/shard_map/ppermute | solution.py:263
  3.6 0.0 collective-permute-start
  3.6 0.0 copy-start.4
  3.6 0.9 %copy-done.4 = f32[32,1280]{1,0:T(8,128)S(1)} copy-done((f32[32,1280]{1,0:T(8,128)S(1)}, f32[32,1280]{1,0:T(8,128)}, u32[]{:S(2)}) %copy-start.4) | copy-done | bytes 163864
  4.6 0.0 copy-start.6
  4.6 0.8 %copy-done.6 = f32[128,128]{1,0:T(8,128)S(1)} copy-done((f32[128,128]{1,0:T(8,128)S(1)}, f32[128,128]{1,0:T(8,128)}, u32[]{:S(2)}) %copy-start.6) | copy-done | bytes 65560
  5.4 0.0 copy-start.7
  5.4 0.7 %copy-done.7 = s32[3,2]{0,1:T(2,128)S(1)} copy-done((s32[3,2]{0,1:T(2,128)S(1)}, s32[3,2]{0,1:T(2,128)}, u32[]{:S(2)}) %copy-start.7) | copy-done | bytes 48
  6.1 0.0 copy-start.9
  6.1 0.7 %copy-done.9 = s32[4,3,2]{0,2,1:T(2,128)S(1)} copy-done((s32[4,3,2]{0,2,1:T(2,128)S(1)}, s32[4,3,2]{0,2,1:T(2,128)}, u32[]{:S(2)}) %copy-start.9) | copy-done | bytes 120
  6.8 0.7 %copy-done.10 = s32[4,3,2]{0,2,1:T(2,128)S(1)} copy-done((s32[4,3,2]{0,2,1:T(2,128)S(1)}, s32[4,3,2]{0,2,1:T(2,128)}, u32[]{:S(2)}) %copy-start.10) | copy-done | bytes 120
  7.4 3.7 %weights.1 = (bf16[3,256,512]{2,1,0:T(8,128)(2,1)S(1)}, bf16[3,512,1280]{2,1,0:T(8,128)(2,1)S(1)}, f32[32,1280]{1,0:T(8,128)S(1)}) custom-call(s32[2,3]{1,0:T(2,128)S(1)} %bitcast.4, s32[3,2,4]{2,1,0:T(2,128)S(1)} %bitcast.7, s32[3,2,4]{2,1,0:T(2,128)S(1)} %bitcast.8, f32[32,1280]{1,0:T(8,128)S(1)} %copy-done.4, f32[128,128]{1,0:T(8,128)S(1)} %copy-done.6), custom_call_target="tpu_custom_call" | custom-call | flops 8000000 | bytes 5112024 | tf_op jit(solution)/shard_map/weights/pallas_call | solution.py:31
  11.1 1.8 %collective-permute-done.1.refs_2_ = bf16[3,128,512]{2,1,0:T(8,128)(2,1)S(1)} collective-permute-done((bf16[3,128,512]{2,1,0:T(8,128)(2,1)}, bf16[3,128,512]{2,1,0:T(8,128)(2,1)S(1)}, u32[]{:S(2)}, u32[]{:S(2)}) %collective-permute-start.1) | collective-permute-done | bytes 393248 | tf_op jit(solution)/shard_map/ppermute | solution.py:263
  13.0 0.0 collective-permute-start.2
  13.0 0.0 collective-permute-done.near.refs_1_
  13.0 1.7 %collective-permute-done.2.far.refs_3_ = bf16[3,128,512]{2,1,0:T(8,128)(2,1)S(1)} collective-permute-done((bf16[3,128,512]{2,1,0:T(8,128)(2,1)S(1)}, bf16[3,128,512]{2,1,0:T(8,128)(2,1)S(1)}, u32[]{:S(2)}, u32[]{:S(2)}) %collective-permute-start.2) | collective-permute-done | bytes 393248 | tf_op jit(solution)/shard_map/ppermute | solution.py:263
  14.7 1.0 %copy-done = bf16[3,128,512]{2,1,0:T(8,128)(2,1)S(1)} copy-done((bf16[3,128,512]{2,1,0:T(8,128)(2,1)S(1)}, bf16[3,128,512]{2,1,0:T(8,128)(2,1)}, u32[]{:S(2)}) %copy-start) | copy-done | bytes 393240
  15.7 2.6 %project.1 = bf16[8,32,1280]{2,1,0:T(8,128)(2,1)} custom-call(bf16[3,256,512]{2,1,0:T(8,128)(2,1)S(1)} %get-tuple-element.19.rows_ref, bf16[3,512,1280]{2,1,0:T(8,128)(2,1)S(1)} %get-tuple-element.20.cols_ref, bf16[3,128,512]{2,1,0:T(8,128)(2,1)S(1)} %copy-done, bf16[3,128,512]{2,1,0:T(8,128)(2,1)S(1)} %collective-permute-done.near.refs_1_, ...), custom_call_target="tpu_custom_call" | custom-call | flops 1400000000 | bytes 6946816 | tf_op jit(solution)/shard_map/project/pallas_call | solution.py:31
  18.3 6.1 %all-to-all-start = ((bf16[8,32,1280]{2,1,0:T(8,128)(2,1)}), bf16[8,32,1280]{2,1,0:T(8,128)(2,1)S(1)}, u32[]{:S(2)}, u32[]{:S(2)}) async-start(bf16[8,32,1280]{2,1,0:T(8,128)(2,1)} %project.1), calls=%async_computation | async-start | bytes 1310720 | tf_op jit(solution)/shard_map/all_to_all | solution.py:298
  24.3 0.0 copy-done.8
  24.3 0.0 copy-done.1
  24.4 0.9 %shift_rows.1 = (bf16[3,128,512]{2,1,0:T(8,128)(2,1)S(1)}, bf16[128,128]{1,0:T(8,128)(2,1)S(1)}, bf16[128,128]{1,0:T(8,128)(2,1)S(1)}) custom-call(s32[2,3]{1,0:T(2,128)S(1)} %bitcast.5, bf16[3,128,512]{2,1,0:T(8,128)(2,1)S(1)} %copy-done.1, bf16[3,128,512]{2,1,0:T(8,128)(2,1)S(1)} %collective-permute-done.near.refs_1_, ...), custom_call_target="tpu_custom_call" | custom-call | flops 1000000 | bytes 1638424 | tf_op jit(solution)/shard_map/shift_rows/pallas_call | solution.py:31
  25.2 2.1 %collective-permute-start.3 = (bf16[128,128]{1,0:T(8,128)(2,1)S(1)}, bf16[128,128]{1,0:T(8,128)(2,1)S(1)}, u32[]{:S(2)}, u32[]{:S(2)}) collective-permute-start(bf16[128,128]{1,0:T(8,128)(2,1)S(1)} %get-tuple-element.17), channel_id=1, source_target_pairs={{0,4},{4,8},{8,12},{12,16},{16,20},{20,24},{24,28},{28,0},{1,5},{5... | collective-permute-start | bytes 98312 | tf_op jit(solution)/shard_map/ppermute | solution.py:266
  27.3 2.8 %collective-permute-start.4 = (bf16[128,128]{1,0:T(8,128)(2,1)S(1)}, bf16[128,128]{1,0:T(8,128)(2,1)S(1)}, u32[]{:S(2)}, u32[]{:S(2)}) collective-permute-start(bf16[128,128]{1,0:T(8,128)(2,1)S(1)} %get-tuple-element.18), channel_id=1, source_target_pairs={{0,28},{4,0},{8,4},{12,8},{16,12},{20,16},{24,20},{28,24},{1,29},{... | collective-permute-start | bytes 98312 | tf_op jit(solution)/shard_map/ppermute | solution.py:266
  30.1 10.9 %collective-permute-done.3.from_left = bf16[128,128]{1,0:T(8,128)(2,1)S(1)} collective-permute-done((bf16[128,128]{1,0:T(8,128)(2,1)S(1)}, bf16[128,128]{1,0:T(8,128)(2,1)S(1)}, u32[]{:S(2)}, u32[]{:S(2)}) %collective-permute-start.3) | collective-permute-done | bytes 32800 | tf_op jit(solution)/shard_map/ppermute | solution.py:266
  40.9 0.0 collective-permute-done.4.from_right
  40.9 1.7 %shift_cols.1 = bf16[3,128,512]{2,1,0:T(8,128)(2,1)} custom-call(s32[2,3]{1,0:T(2,128)S(1)} %bitcast.6, bf16[3,128,512]{2,1,0:T(8,128)(2,1)S(1)} %get-tuple-element.16.moved, bf16[128,128]{1,0:T(8,128)(2,1)S(1)} %collective-permute-done.3.from_left, bf16[128,128]{1,0:T(8,128)(2,1)S(1)} %collective-permute-done.4.from_right), custom_call_target="tpu_custom_call" | custom-call | flops 1000000 | bytes 851992 | tf_op jit(solution)/shard_map/shift_cols/pallas_call | solution.py:31
  42.6 0.0 all-to-all-done.parts
  42.6 0.0 copy-done.2
  42.6 0.0 copy-done.3
  42.6 0.0 copy-done.5
  42.6 1.7 %imaging.1 = f32[64,2560]{1,0:T(8,128)} custom-call(bf16[8,32,1280]{2,1,0:T(8,128)(2,1)S(1)} %all-to-all-done.parts, f32[32,1280]{1,0:T(8,128)S(1)} %get-tuple-element.21.amp_ref, bf16[256,512]{1,0:T(8,128)(2,1)S(1)} %copy-done.3, bf16[256,512]{1,0:T(8,128)(2,1)S(1)} %copy-done.2, bf16[128,192]{1,0:T(8,128)(2,1)S(1)} %copy-done.5), custom_call_target="tpu_custom_call" | custom-call | flops 400000000 | bytes 2048000 | tf_op jit(solution)/shard_map/imaging/pallas_call | solution.py:31
  (7 shorter events, 0.0 us)
Async XLA Ops:
  0.6 12.3 %collective-permute-start.1 = (bf16[3,128,512]{2,1,0:T(8,128)(2,1)}, bf16[3,128,512]{2,1,0:T(8,128)(2,1)S(1)}, u32[]{:S(2)}, u32[]{:S(2)}) collective-permute-start(bf16[3,128,512]{2,1,0:T(8,128)(2,1)} %refs_0_.1), channel_id=1, source_target_pairs={{0,2},{1,3},{2,0},{3,1},{4,6},{5,7},{6,4},{7,5},{8,10},{9,11},{10,... | collective-permute-start | bytes 1179656 | tf_op jit(solution)/shard_map/ppermute | solution.py:263
  3.6 9.3 %collective-permute-start = (bf16[3,128,512]{2,1,0:T(8,128)(2,1)}, bf16[3,128,512]{2,1,0:T(8,128)(2,1)S(1)}, u32[]{:S(2)}, u32[]{:S(2)}) collective-permute-start(bf16[3,128,512]{2,1,0:T(8,128)(2,1)} %refs_0_.1), channel_id=1, source_target_pairs={{0,1},{1,0},{2,3},{3,2},{4,5},{5,4},{6,7},{7,6},{8,9},{9,8},{10,11... | collective-permute-start | bytes 1179656 | tf_op jit(solution)/shard_map/ppermute | solution.py:263
  3.6 0.9 %copy-start.4 = (f32[32,1280]{1,0:T(8,128)S(1)}, f32[32,1280]{1,0:T(8,128)}, u32[]{:S(2)}) copy-start(f32[32,1280]{1,0:T(8,128)} %amplitude.1) | copy-start | bytes 491524
  4.6 0.8 %copy-start.6 = (f32[128,128]{1,0:T(8,128)S(1)}, f32[128,128]{1,0:T(8,128)}, u32[]{:S(2)}) copy-start(f32[128,128]{1,0:T(8,128)} %constant.8.clone.ones) | copy-start | bytes 196612
  5.4 0.7 %copy-start.7 = (s32[3,2]{0,1:T(2,128)S(1)}, s32[3,2]{0,1:T(2,128)}, u32[]{:S(2)}) copy-start(s32[3,2]{0,1:T(2,128)} %param.11) | copy-start | bytes 76
  6.1 0.7 %copy-start.9 = (s32[4,3,2]{0,2,1:T(2,128)S(1)}, s32[4,3,2]{0,2,1:T(2,128)}, u32[]{:S(2)}) copy-start(s32[4,3,2]{0,2,1:T(2,128)} %param.12) | copy-start | bytes 292
  6.8 0.7 %copy-start.10 = (s32[4,3,2]{0,2,1:T(2,128)S(1)}, s32[4,3,2]{0,2,1:T(2,128)}, u32[]{:S(2)}) copy-start(s32[4,3,2]{0,2,1:T(2,128)} %param.13) | copy-start | bytes 292
  13.0 11.4 %copy-start.8 = (s32[3,2]{0,1:T(2,128)S(1)}, s32[3,2]{0,1:T(2,128)}, u32[]{:S(2)}) copy-start(s32[3,2]{0,1:T(2,128)} %param.11) | copy-start | bytes 76
  13.0 1.7 %collective-permute-start.2 = (bf16[3,128,512]{2,1,0:T(8,128)(2,1)S(1)}, bf16[3,128,512]{2,1,0:T(8,128)(2,1)S(1)}, u32[]{:S(2)}, u32[]{:S(2)}) collective-permute-start(bf16[3,128,512]{2,1,0:T(8,128)(2,1)S(1)} %collective-permute-done.1.refs_2_), channel_id=1, source_target_pairs={{0,1},{1,0},{2,3},{3,2},{4,5},{5,4},{6,7},{7,6},{8,9},{9,8},{10,11... | collective-permute-start | bytes 1179656 | tf_op jit(solution)/shard_map/ppermute | solution.py:263
  14.7 1.0 %copy-start = (bf16[3,128,512]{2,1,0:T(8,128)(2,1)S(1)}, bf16[3,128,512]{2,1,0:T(8,128)(2,1)}, u32[]{:S(2)}) copy-start(bf16[3,128,512]{2,1,0:T(8,128)(2,1)} %refs_0_.1) | copy-start | bytes 1179652
  15.7 8.7 %copy-start.1 = (bf16[3,128,512]{2,1,0:T(8,128)(2,1)S(1)}, bf16[3,128,512]{2,1,0:T(8,128)(2,1)}, u32[]{:S(2)}) copy-start(bf16[3,128,512]{2,1,0:T(8,128)(2,1)} %refs_0_.1) | copy-start | bytes 1179652
  15.7 26.9 %copy-start.2 = (bf16[256,512]{1,0:T(8,128)(2,1)S(1)}, bf16[256,512]{1,0:T(8,128)(2,1)}, u32[]{:S(2)}) copy-start(bf16[256,512]{1,0:T(8,128)(2,1)} %constant.10.clone.cols_low) | copy-start | bytes 786436
  15.7 26.9 %copy-start.3 = (bf16[256,512]{1,0:T(8,128)(2,1)S(1)}, bf16[256,512]{1,0:T(8,128)(2,1)}, u32[]{:S(2)}) copy-start(bf16[256,512]{1,0:T(8,128)(2,1)} %constant.9.clone.cols_high) | copy-start | bytes 786436
  15.7 26.9 %copy-start.5 = (bf16[128,192]{1,0:T(8,128)(2,1)S(1)}, bf16[128,192]{1,0:T(8,128)(2,1)}, u32[]{:S(2)}) copy-start(bf16[128,192]{1,0:T(8,128)(2,1)} %constant.11.clone.rows_table) | copy-start | bytes 147460
  18.3 24.3 %all-to-all-start = ((bf16[8,32,1280]{2,1,0:T(8,128)(2,1)}), bf16[8,32,1280]{2,1,0:T(8,128)(2,1)S(1)}, u32[]{:S(2)}, u32[]{:S(2)}) async-start(bf16[8,32,1280]{2,1,0:T(8,128)(2,1)} %project.1), calls=%async_computation | async-start | bytes 1310720 | tf_op jit(solution)/shard_map/all_to_all | solution.py:298
  25.2 15.7 %collective-permute-start.3 = (bf16[128,128]{1,0:T(8,128)(2,1)S(1)}, bf16[128,128]{1,0:T(8,128)(2,1)S(1)}, u32[]{:S(2)}, u32[]{:S(2)}) collective-permute-start(bf16[128,128]{1,0:T(8,128)(2,1)S(1)} %get-tuple-element.17), channel_id=1, source_target_pairs={{0,4},{4,8},{8,12},{12,16},{16,20},{20,24},{24,28},{28,0},{1,5},{5... | collective-permute-start | bytes 98312 | tf_op jit(solution)/shard_map/ppermute | solution.py:266
  27.3 13.6 %collective-permute-start.4 = (bf16[128,128]{1,0:T(8,128)(2,1)S(1)}, bf16[128,128]{1,0:T(8,128)(2,1)S(1)}, u32[]{:S(2)}, u32[]{:S(2)}) collective-permute-start(bf16[128,128]{1,0:T(8,128)(2,1)S(1)} %get-tuple-element.18), channel_id=1, source_target_pairs={{0,28},{4,0},{8,4},{12,8},{16,12},{20,16},{24,20},{28,24},{1,29},{... | collective-permute-start | bytes 98312 | tf_op jit(solution)/shard_map/ppermute | solution.py:266

commit v3 on v2

--- a/solution.py
+++ b/solution.py
@@ -54,27 +54,42 @@
     return base, upper, 1.0 - fraction, fraction
 
 
-def weights_kernel(geometry, wind, offsets, ratio, amplitude, ones, rows_out, cols_out, amp_out):
-    n_layer, n_dir, rows_dev, cols_dev = geometry
-    layers, pupil_rows, screen_rows = rows_out.shape
+def early_kernel(n_layer, wind, offsets, ratio, amplitude, ones, own, near, rows_out, cols_out, amp_out, early_out):
+    layers, rows_dev, cols_dev = own.shape
+    pupil_rows = rows_out.shape[1]
+    screen_rows = 4 * rows_dev
     pupil_cols = cols_out.shape[2]
     screen_cols = cols_dev * n_layer
     direction = lax.axis_index("dir")
     column = lax.axis_index("layer")
+    block = pupil_rows // n_layer
+    half = pupil_rows // 2
+    row = lax.broadcasted_iota(jnp.int32, (half, LANES), 0)
+    pair = row // block + column // 2
+    pair = jnp.where(pair >= n_layer // 2, pair - n_layer // 2, pair)
+    parity = lax.rem(column, 2)
+    inside = lax.rem(row, block) + pair * (2 * block)
+    pixel_rows = jnp.concatenate([inside + parity * block, inside + (1 - parity) * block], axis=0)
+    lane = lax.broadcasted_iota(jnp.int32, (pupil_rows, LANES), 1)
     for level in range(layers):
         num = ratio[level, 0, direction]
         den = ratio[level, 1, direction]
         anchor = wrap(offsets[level, 0, direction] - wind[0, level], screen_rows)
-        pixel = lax.broadcasted_iota(jnp.int32, (pupil_rows, LANES), 0)
-        base, upper, low, high = spans(pixel, anchor, num, den, screen_rows)
-        lane = lax.broadcasted_iota(jnp.int32, (pupil_rows, LANES), 1)
-        for peer in range(n_dir):
+        base, upper, low, high = spans(pixel_rows, anchor, num, den, screen_rows)
+
+        def weights_of(peer):
+            parts = []
             for part in range(rows_dev // LANES):
                 index = lane + (jnp.bitwise_xor(direction, peer) * rows_dev + part * LANES)
                 weight = jnp.where(index == base, low, 0.0)
-                weight = jnp.where(index == upper, high, weight)
-                start = peer * rows_dev + part * LANES
-                rows_out[level, :, start : start + LANES] = weight.astype(jnp.bfloat16)
+                parts.append(jnp.where(index == upper, high, weight).astype(jnp.bfloat16))
+            return parts
+
+        mine = jnp.concatenate(weights_of(0) + weights_of(1), axis=1)
+        screen = jnp.concatenate([own[level], near[level]], axis=0)
+        early_out[level] = jnp.dot(mine, screen, preferred_element_type=jnp.float32)
+        rows_out[level] = jnp.concatenate(weights_of(2) + weights_of(3), axis=1)
+
         anchor = wrap(offsets[level, 1, direction] - wind[1, level], screen_cols)
         first = lax.broadcasted_iota(jnp.int32, (cols_dev, LANES), 0) + column * cols_dev
 
@@ -100,27 +115,34 @@
         amp_out[:, cut] = amp * lax.rsqrt(total)
 
 
-def project_kernel(peers, rows_ref, cols_ref, *refs):
-    blocks, out = refs[:peers], refs[peers]
-    layers, pupil_rows, screen_rows = rows_ref.shape
-    _, cols_dev, pupil_cols = cols_ref.shape
-    size = out.shape[1]
-    group = min(pupil_rows, 256)
-    per_group = group // size
-    for at in range(pupil_rows // group):
-        projected = []
-        for level in range(layers):
-            screen = jnp.concatenate([block[level] for block in blocks], axis=0)
-            rows = rows_ref[level, at * group : (at + 1) * group, :]
-            part = jnp.dot(rows, screen, preferred_element_type=jnp.float32)
-            projected.append(part.astype(jnp.bfloat16))
-        projected = jnp.concatenate(projected, axis=1)
-        for start in range(0, pupil_cols, 256):
-            cols = cols_ref[:, :, start : start + 256].reshape(layers * cols_dev, 256)
-            phase = jnp.dot(projected, cols, preferred_element_type=jnp.float32)
-            for k in range(per_group):
-                piece = phase[k * size : (k + 1) * size].astype(jnp.bfloat16)
-                out[at * per_group + k, :, start : start + 256] = piece
+def project_cols(projected, cols_ref, start, stop, kept, sent):
+    layers, cols_dev, _ = cols_ref.shape
+    blocks, size, _ = kept.shape
+    for at in range(start, stop, 256):
+        cols = cols_ref[:, :, at : at + 256].reshape(layers * cols_dev, 256)
+        phase = jnp.dot(projected, cols, preferred_element_type=jnp.float32).astype(jnp.bfloat16)
+        phase = phase.reshape(2, blocks, size, 256)
+        kept[:, :, at - start : at - start + 256] = phase[0]
+        sent[:, :, at - start : at - start + 256] = phase[1]
+
+
+def first_kernel(stop, early, rows_ref, cols_ref, across, far, projected, kept, sent):
+    layers = early.shape[0]
+    width = across.shape[2]
+    for level in range(layers):
+        screen = jnp.concatenate([across[level], far[level]], axis=0)
+        part = early[level] + jnp.dot(rows_ref[level], screen, preferred_element_type=jnp.float32)
+        projected[:, level * width : (level + 1) * width] = part.astype(jnp.bfloat16)
+    project_cols(projected[...], cols_ref, 0, stop, kept, sent)
+
+
+def later_kernel(start, stop, projected, cols_ref, kept, sent):
+    project_cols(projected[...], cols_ref, start, stop, kept, sent)
+
+
+def add_kernel(kept, came, *outs):
+    for k, out in enumerate(outs):
+        out[...] = (kept[k].astype(jnp.float32) + came[k].astype(jnp.float32)).astype(jnp.bfloat16)
 
 
 def rows_kernel(wind, own, near, far, moved, right, left):
@@ -167,6 +189,26 @@
         out[level] = pltpu.roll(wide, shift, 1)[:, :cols].astype(jnp.bfloat16)
 
 
+def image(start, stop, pairs, operands, out_shape):
+    size = sum(array.size * array.dtype.itemsize for array in operands)
+    in_specs = [VMEM_SPEC] * (pairs + 4)
+    aliases = {}
+    if len(operands) > len(in_specs):
+        aliases = {len(in_specs): 0}
+        in_specs = in_specs + [pl.BlockSpec(memory_space=pl.ANY)]
+    return pl.pallas_call(
+        functools.partial(imaging_kernel, pairs, start),
+        out_shape=out_shape,
+        in_specs=in_specs,
+        out_specs=pl.BlockSpec(memory_space=pl.ANY),
+        scratch_shapes=[pltpu.VMEM((out_shape.shape[0], 2 * (stop - start)), jnp.float32), pltpu.SemaphoreType.DMA],
+        input_output_aliases=aliases,
+        compiler_params=params(operands, out_shape),
+        cost_estimate=pl.CostEstimate(flops=200_000_000, bytes_accessed=size, transcendentals=0),
+        name="imaging",
+    )(*operands)
+
+
 def sin_cos(phase):
     turns = jnp.floor(phase * (1.0 / np.pi) + 0.5)
     rest = phase - turns * 3.140625
@@ -189,14 +231,17 @@
     return high, low
 
 
-def imaging_kernel(parts, amp_ref, cols_high, cols_low, rows_table, out):
-    rows, cols = amp_ref.shape
+def imaging_kernel(count, start, *refs):
+    parts = refs[:count]
+    amp_ref, cols_high, cols_low, rows_table = refs[count : count + 4]
+    whole, out, sem = refs[-3:]
+    rows, cols = parts[0].shape
     tiles = cols // LANES
-    phase = parts[0].astype(jnp.float32)
-    for k in range(1, parts.shape[0]):
-        phase = phase + parts[k].astype(jnp.float32)
+    phase = parts[0][...].astype(jnp.float32)
+    for part in parts[1:]:
+        phase = phase + part[...].astype(jnp.float32)
     sine, cosine = sin_cos(phase)
-    amp = amp_ref[...]
+    amp = amp_ref[:, start : start + cols]
     real, imag = amp * cosine, amp * sine
     field = jnp.concatenate(
         [
@@ -219,6 +264,9 @@
         full = dot(rows_table[...], jnp.concatenate([high, low, high], axis=0))
         real, imag = full[:out_rows], full[out_rows:]
         out[:, t * wide : (t + 1) * wide] = real * real + imag * imag
+    copy = pltpu.make_async_copy(out, whole.at[:, 2 * start : 2 * (start + cols)], sem)
+    copy.start()
+    copy.wait()
 
 
 def tables(rows):
@@ -265,37 +313,61 @@
     def turn(value, step):
         return lax.ppermute(value, "layer", [(i, (i + step) % n_layer) for i in range(n_layer)])
 
+    def shape(*dims, dtype=bf16):
+        return jax.ShapeDtypeStruct(dims, dtype)
+
     across = swap(screens, 2)
     near = swap(screens, 1)
-
-    def shape(*dims, dtype=bf16):
-        return jax.ShapeDtypeStruct(dims, dtype)
-
     ones = np.kron(np.eye(LANES // SUB_PIX), np.ones((SUB_PIX, SUB_PIX))).astype(np.float32)
-    row_weights, col_weights, amp = call(
-        functools.partial(weights_kernel, (n_layer, n_dir, rows_dev, cols_dev)),
+    row_weights, col_weights, amp, early = call(
+        functools.partial(early_kernel, n_layer),
         (
-            shape(layers, pupil_rows, screen_rows),
+            shape(layers, pupil_rows, 2 * rows_dev),
             shape(layers, cols_dev, pupil_cols),
             shape(rows, pupil_cols, dtype=f32),
+            shape(layers, pupil_rows, cols_dev, dtype=f32),
         ),
-        (wind, offsets, ratio, amplitude, jnp.asarray(ones)),
-        8_000_000,
-        "weights",
-    )
-    across, row_weights, col_weights, amp = lax.optimization_barrier(
-        (across, row_weights, col_weights, amp)
+        (wind, offsets, ratio, amplitude, jnp.asarray(ones), screens, near),
+        200_000_000,
+        "early",
+    )
+    across, row_weights, col_weights, amp, early = lax.optimization_barrier(
+        (across, row_weights, col_weights, amp, early)
     )
     far = swap(across, 1)
 
-    partials = call(
-        functools.partial(project_kernel, n_dir),
-        shape(n_layer, rows, pupil_cols),
-        (row_weights, col_weights, screens, near, across, far),
-        1_400_000_000,
-        "project",
-    )
-    received = lax.all_to_all(partials, "layer", 0, 0, tiled=True)
+    pairs = n_layer // 2
+    cuts = [0, (pupil_cols * 5 // 8) // 256 * 256, pupil_cols]
+    kept, sent = [None, None], [None, None]
+
+    def halves(piece):
+        return [shape(pairs, rows, cuts[piece + 1] - cuts[piece])] * 2
+
+    projected, kept[0], sent[0] = call(
+        functools.partial(first_kernel, cuts[1]),
+        [shape(pupil_rows, layers * cols_dev)] + halves(0),
+        (early, row_weights, col_weights, across, far),
+        800_000_000,
+        "project_first",
+    )
+    kept[1], sent[1] = call(
+        functools.partial(later_kernel, cuts[1], cuts[2]),
+        halves(1),
+        (projected, col_weights),
+        500_000_000,
+        "project_later",
+    )
+    received = []
+    for piece in range(2):
+        came = lax.ppermute(sent[piece], "layer", [(i, i ^ 1) for i in range(n_layer)])
+        sums = call(
+            add_kernel,
+            [shape(rows, cuts[piece + 1] - cuts[piece])] * pairs,
+            (kept[piece], came),
+            1_000_000,
+            "add_pair",
+        )
+        received.append([sums[0]] + [turn(sums[k], 2 * k) for k in range(1, pairs)])
 
     moved, right, left = call(
         rows_kernel,
@@ -314,13 +386,12 @@
         "shift_cols",
     )
 
-    spots = call(
-        imaging_kernel,
-        shape(2 * rows, 2 * pupil_cols, dtype=f32),
-        (received, amp, *[jnp.asarray(table) for table in tables(rows)]),
-        400_000_000,
-        "imaging",
-    )
+    dft = [jnp.asarray(table) for table in tables(rows)]
+    spots = None
+    for piece in range(2):
+        start, stop = cuts[piece], cuts[piece + 1]
+        operands = [*received[piece], amp, *dft] + ([] if spots is None else [spots])
+        spots = image(start, stop, pairs, operands, shape(2 * rows, 2 * pupil_cols, dtype=f32))
     return (new_screens, spots[None])
 
 

time: 44.7 us -> 46.4 us (1.038)
  starting transfers between devices: 13.9 us -> 19.7 us
  waiting for transfers between devices: 14.4 us -> 9.71 us
  Pallas kernels: 10.5 us -> 11 us
    ppermute x2 -> x8, starting transfers between devices: 4.83 us -> 14.5 us  [turn(): lax.ppermute(value, 'layer', [(i, (i + step) % n_layer) for i in range(n_...]
    ppermute x2 -> x8, waiting for transfers between devices: 10.9 us -> 1.89 us  [turn(): lax.ppermute(value, 'layer', [(i, (i + step) % n_layer) for i in range(n_...]
    all_to_all x1 -> x0, starting transfers between devices: 6.08 us -> none  [per_device(): received = lax.all_to_all(partials, 'layer', 0, 0, tiled=True)]
    ppermute x0 -> x2, waiting for transfers between devices: none -> 5.07 us  [per_device(): lax.ppermute(sent[piece], 'layer', [(i, i ^ 1) for i in range(n_layer)])]
    pallas_call x0 -> x2, Pallas kernels: none -> 2.66 us  [image(): pl.pallas_call(functools.partial(imaging_kernel, pairs, start), out_shape...]
    pallas_call x5 -> x7, Pallas kernels: 10.5 us -> 8.32 us  [call(): pl.pallas_call(kernel, out_shape=out_shape, in_specs=[spec(array) for arr...]
    ppermute x0 -> x2, starting transfers between devices: none -> 2.16 us  [per_device(): lax.ppermute(sent[piece], 'layer', [(i, i ^ 1) for i in range(n_layer)])]
    ppermute x3, waiting for transfers between devices: 3.56 us -> 2.75 us  [swap(): return lax.ppermute(value, 'dir', [(i, i ^ bit) for i in range(n_dir)])]
  transfers between devices with their start and end apart: 6 -> 13, of which waited for: 3 -> 4; matrix products, arithmetic and copies ran while one was open for 0% -> 0% of each run, Pallas kernels for 14% -> 19%
where the time goes in v3:
time: 46.4 us; the launch traced here: 46.1 us
  starting transfers between devices  19.7 us (42%)
  Pallas kernels  11 us (24%)
  waiting for transfers between devices  9.71 us (21%)
  local copies, waits for them, and re-layouts  4.86 us (10%)
  between operations  0.79 us (2%)
    ppermute x8, starting transfers between devices, turn(): lax.ppermute(value, 'layer', [(i, (i + step) % n_layer) for i in range(n_...  14.5 us
    pallas_call x7, Pallas kernels, call(): pl.pallas_call(kernel, out_shape=out_shape, in_specs=[spec(array) for arr...  8.32 us
    ppermute x2, waiting for transfers between devices, per_device(): lax.ppermute(sent[piece], 'layer', [(i, i ^ 1) for i in range(n_layer)])  5.07 us
    unnamed x22, local copies, waits for them, and re-layouts  4.86 us
    ppermute x3, starting transfers between devices, swap(): return lax.ppermute(value, 'dir', [(i, i ^ bit) for i in range(n_dir)])  3.09 us
    ppermute x3, waiting for transfers between devices, swap(): return lax.ppermute(value, 'dir', [(i, i ^ bit) for i in range(n_dir)])  2.75 us
    pallas_call x2, Pallas kernels, image(): pl.pallas_call(functools.partial(imaging_kernel, pairs, start), out_shape...  2.66 us
    ppermute x2, starting transfers between devices, per_device(): lax.ppermute(sent[piece], 'layer', [(i, i ^ 1) for i in range(n_layer)])  2.16 us
  transfers between devices with their start and end apart: 13, of which 4 were waited for; matrix products, arithmetic and copies ran while one was open for 0% of the time, Pallas kernels for 19%

profile of v3, /device:TPU:0, one launch (start us, length us, event | category | flops | bytes accessed | tf_op | source)
XLA Modules:
  0.0 46.1 jit_solution(4568159782732546367)
XLA Ops:
  0.6 0.5 %collective-permute-start = (bf16[3,128,512]{2,1,0:T(8,128)(2,1)}, bf16[3,128,512]{2,1,0:T(8,128)(2,1)S(1)}, u32[]{:S(2)}, u32[]{:S(2)}) collective-permute-start(bf16[3,128,512]{2,1,0:T(8,128)(2,1)} %own.3), channel_id=1, source_target_pairs={{0,1},{1,0},{2,3},{3,2},{4,5},{5,4},{6,7},{7,6},{8,9},{9,8},{10,11... | collective-permute-start | bytes 1179656 | tf_op jit(solution)/shard_map/ppermute | solution.py:311
  1.1 2.6 %collective-permute-start.1 = (bf16[3,128,512]{2,1,0:T(8,128)(2,1)}, bf16[3,128,512]{2,1,0:T(8,128)(2,1)S(1)}, u32[]{:S(2)}, u32[]{:S(2)}) collective-permute-start(bf16[3,128,512]{2,1,0:T(8,128)(2,1)} %own.3), channel_id=1, source_target_pairs={{0,2},{1,3},{2,0},{3,1},{4,6},{5,7},{6,4},{7,5},{8,10},{9,11},{10,... | collective-permute-start | bytes 1179656 | tf_op jit(solution)/shard_map/ppermute | solution.py:311
  3.7 1.0 %copy-done = bf16[3,128,512]{2,1,0:T(8,128)(2,1)S(1)} copy-done((bf16[3,128,512]{2,1,0:T(8,128)(2,1)S(1)}, bf16[3,128,512]{2,1,0:T(8,128)(2,1)}, u32[]{:S(2)}) %copy-start) | copy-done | bytes 393240
  4.7 0.9 %copy-done.5 = f32[32,1280]{1,0:T(8,128)S(1)} copy-done((f32[32,1280]{1,0:T(8,128)S(1)}, f32[32,1280]{1,0:T(8,128)}, u32[]{:S(2)}) %copy-start.5) | copy-done | bytes 163864
  5.7 0.8 %copy-done.6 = f32[128,128]{1,0:T(8,128)S(1)} copy-done((f32[128,128]{1,0:T(8,128)S(1)}, f32[128,128]{1,0:T(8,128)}, u32[]{:S(2)}) %copy-start.6) | copy-done | bytes 65560
  6.5 0.7 %copy-done.7 = s32[3,2]{0,1:T(2,128)S(1)} copy-done((s32[3,2]{0,1:T(2,128)S(1)}, s32[3,2]{0,1:T(2,128)}, u32[]{:S(2)}) %copy-start.7) | copy-done | bytes 48
  7.2 0.7 %copy-done.9 = s32[4,3,2]{0,2,1:T(2,128)S(1)} copy-done((s32[4,3,2]{0,2,1:T(2,128)S(1)}, s32[4,3,2]{0,2,1:T(2,128)}, u32[]{:S(2)}) %copy-start.9) | copy-done | bytes 120
  7.9 0.7 %copy-done.10 = s32[4,3,2]{0,2,1:T(2,128)S(1)} copy-done((s32[4,3,2]{0,2,1:T(2,128)S(1)}, s32[4,3,2]{0,2,1:T(2,128)}, u32[]{:S(2)}) %copy-start.10) | copy-done | bytes 120
  8.6 4.0 %early.1 = (bf16[3,256,256]{2,1,0:T(8,128)(2,1)S(1)}, bf16[3,512,1280]{2,1,0:T(8,128)(2,1)S(1)}, f32[32,1280]{1,0:T(8,128)S(1)}, f32[3,256,512]{2,1,0:T(8,128)S(1)}) custom-call(s32[2,3]{1,0:T(2,128)S(1)} %bitcast.4, s32[3,2,4]{2,1,0:T(2,128)S(1)} %bitcast.7, s32[3,2,4]{2,1,0:T(2,128)S(1)} %bitcast.8, f32[32,1280]{1,0:T(8,128)S(1)} %copy-done.5, ...), custom_call_target="tpu_custom_call" | custom-call | flops 200000000 | bytes 7078104 | tf_op jit(solution)/shard_map/early/pallas_call | solution.py:31
  12.6 1.0 %collective-permute-done.1.across = bf16[3,128,512]{2,1,0:T(8,128)(2,1)S(1)} collective-permute-done((bf16[3,128,512]{2,1,0:T(8,128)(2,1)}, bf16[3,128,512]{2,1,0:T(8,128)(2,1)S(1)}, u32[]{:S(2)}, u32[]{:S(2)}) %collective-permute-start.1) | collective-permute-done | bytes 393248 | tf_op jit(solution)/shard_map/ppermute | solution.py:311
  13.6 1.7 %collective-permute-done.2.far = bf16[3,128,512]{2,1,0:T(8,128)(2,1)S(1)} collective-permute-done((bf16[3,128,512]{2,1,0:T(8,128)(2,1)S(1)}, bf16[3,128,512]{2,1,0:T(8,128)(2,1)S(1)}, u32[]{:S(2)}, u32[]{:S(2)}) %collective-permute-start.2) | collective-permute-done | bytes 393248 | tf_op jit(solution)/shard_map/ppermute | solution.py:311
  15.4 1.1 %project_first.1 = (bf16[256,1536]{1,0:T(8,128)(2,1)S(1)}, bf16[4,32,768]{2,1,0:T(8,128)(2,1)S(1)}, bf16[4,32,768]{2,1,0:T(8,128)(2,1)S(1)}) custom-call(f32[3,256,512]{2,1,0:T(8,128)S(1)} %get-tuple-element.35.early, bf16[3,256,256]{2,1,0:T(8,128)(2,1)S(1)} %get-tuple-element.36.rows_ref, bf16[3,512,1280]{2,1,0:T(8,128)(2,1)S(1)} %get-tuple-element.37.cols_ref, ...), custom_call_target="tpu_custom_call" | custom-call | flops 800000000 | bytes 7864320 | tf_op jit(solution)/shard_map/project_first/pallas_call | solution.py:31
  16.4 0.0 copy-start.1
  16.5 0.0 copy-start.8
  16.5 0.0 copy-start.2
  16.5 0.0 copy-start.3
  16.5 0.0 copy-start.4
  16.5 1.9 %collective-permute-start.9 = (bf16[4,32,768]{2,1,0:T(8,128)(2,1)S(1)}, bf16[4,32,768]{2,1,0:T(8,128)(2,1)S(1)}, u32[]{:S(2)}, u32[]{:S(2)}) collective-permute-start(bf16[4,32,768]{2,1,0:T(8,128)(2,1)S(1)} %get-tuple-element.47), channel_id=1, source_target_pairs={{0,4},{4,0},{8,12},{12,8},{16,20},{20,16},{24,28},{28,24},{1,5},{5... | collective-permute-start | bytes 589832 | tf_op jit(solution)/shard_map/ppermute | solution.py:362
  18.4 0.6 %project_later.1 = (bf16[4,32,512]{2,1,0:T(8,128)(2,1)S(1)}, bf16[4,32,512]{2,1,0:T(8,128)(2,1)S(1)}) custom-call(bf16[256,1536]{1,0:T(8,128)(2,1)S(1)} %get-tuple-element.38.projected, bf16[3,512,1280]{2,1,0:T(8,128)(2,1)S(1)} %get-tuple-element.37.cols_ref), custom_call_target="tpu_custom_call" | custom-call | flops 500000000 | bytes 4980736 | tf_op jit(solution)/shard_map/project_later/pallas_call | solution.py:31
  18.9 0.3 collective-permute-start.5
  19.2 5.1 %collective-permute-done.9.came = bf16[4,32,768]{2,1,0:T(8,128)(2,1)S(1)} collective-permute-done((bf16[4,32,768]{2,1,0:T(8,128)(2,1)S(1)}, bf16[4,32,768]{2,1,0:T(8,128)(2,1)S(1)}, u32[]{:S(2)}, u32[]{:S(2)}) %collective-permute-start.9) | collective-permute-done | bytes 196640 | tf_op jit(solution)/shard_map/ppermute | solution.py:362
  24.4 1.9 %collective-permute-start.10 = (bf16[32,768]{1,0:T(8,128)(2,1)S(1)}, bf16[32,768]{1,0:T(8,128)(2,1)S(1)}, u32[]{:S(2)}, u32[]{:S(2)}) collective-permute-start(bf16[32,768]{1,0:T(8,128)(2,1)S(1)} %get-tuple-element.49), channel_id=1, source_target_pairs={{0,8},{4,12},{8,16},{12,20},{16,24},{20,28},{24,0},{28,4},{1,9},{5... | collective-permute-start | bytes 147464 | tf_op jit(solution)/shard_map/ppermute | solution.py:314
  26.3 2.6 %collective-permute-start.11 = (bf16[32,768]{1,0:T(8,128)(2,1)S(1)}, bf16[32,768]{1,0:T(8,128)(2,1)S(1)}, u32[]{:S(2)}, u32[]{:S(2)}) collective-permute-start(bf16[32,768]{1,0:T(8,128)(2,1)S(1)} %get-tuple-element.50), channel_id=1, source_target_pairs={{0,16},{4,20},{8,24},{12,28},{16,0},{20,4},{24,8},{28,12},{1,17},{... | collective-permute-start | bytes 147464 | tf_op jit(solution)/shard_map/ppermute | solution.py:314
  28.9 1.3 %collective-permute-start.12 = (bf16[32,768]{1,0:T(8,128)(2,1)S(1)}, bf16[32,768]{1,0:T(8,128)(2,1)S(1)}, u32[]{:S(2)}, u32[]{:S(2)}) collective-permute-start(bf16[32,768]{1,0:T(8,128)(2,1)S(1)} %get-tuple-element.51), channel_id=1, source_target_pairs={{0,24},{4,28},{8,0},{12,4},{16,8},{20,12},{24,16},{28,20},{1,25},{... | collective-permute-start | bytes 147464 | tf_op jit(solution)/shard_map/ppermute | solution.py:314
  30.2 0.9 %shift_rows.1 = (bf16[3,128,512]{2,1,0:T(8,128)(2,1)S(1)}, bf16[128,128]{1,0:T(8,128)(2,1)S(1)}, bf16[128,128]{1,0:T(8,128)(2,1)S(1)}) custom-call(s32[2,3]{1,0:T(2,128)S(1)} %bitcast.5, bf16[3,128,512]{2,1,0:T(8,128)(2,1)S(1)} %copy-done.1, bf16[3,128,512]{2,1,0:T(8,128)(2,1)S(1)} %collective-permute-done.near, ...), custom_call_target="tpu_custom_call" | custom-call | flops 1000000 | bytes 1638424 | tf_op jit(solution)/shard_map/shift_rows/pallas_call | solution.py:31
  31.1 1.6 %collective-permute-start.3 = (bf16[128,128]{1,0:T(8,128)(2,1)S(1)}, bf16[128,128]{1,0:T(8,128)(2,1)S(1)}, u32[]{:S(2)}, u32[]{:S(2)}) collective-permute-start(bf16[128,128]{1,0:T(8,128)(2,1)S(1)} %get-tuple-element.33), channel_id=1, source_target_pairs={{0,4},{4,8},{8,12},{12,16},{16,20},{20,24},{24,28},{28,0},{1,5},{5... | collective-permute-start | bytes 98312 | tf_op jit(solution)/shard_map/ppermute | solution.py:314
  32.7 3.2 %collective-permute-start.4 = (bf16[128,128]{1,0:T(8,128)(2,1)S(1)}, bf16[128,128]{1,0:T(8,128)(2,1)S(1)}, u32[]{:S(2)}, u32[]{:S(2)}) collective-permute-start(bf16[128,128]{1,0:T(8,128)(2,1)S(1)} %get-tuple-element.34), channel_id=1, source_target_pairs={{0,28},{4,0},{8,4},{12,8},{16,12},{20,16},{24,20},{28,24},{1,29},{... | collective-permute-start | bytes 98312 | tf_op jit(solution)/shard_map/ppermute | solution.py:314
  35.9 1.9 %collective-permute-done.3.from_left = bf16[128,128]{1,0:T(8,128)(2,1)S(1)} collective-permute-done((bf16[128,128]{1,0:T(8,128)(2,1)S(1)}, bf16[128,128]{1,0:T(8,128)(2,1)S(1)}, u32[]{:S(2)}, u32[]{:S(2)}) %collective-permute-start.3) | collective-permute-done | bytes 32800 | tf_op jit(solution)/shard_map/ppermute | solution.py:314
  37.8 3.9 %collective-permute-start.8 = (bf16[32,512]{1,0:T(8,128)(2,1)S(1)}, bf16[32,512]{1,0:T(8,128)(2,1)S(1)}, u32[]{:S(2)}, u32[]{:S(2)}) collective-permute-start(bf16[32,512]{1,0:T(8,128)(2,1)S(1)} %get-tuple-element.44), channel_id=1, source_target_pairs={{0,24},{4,28},{8,0},{12,4},{16,8},{20,12},{24,16},{28,20},{1,25},{... | collective-permute-start | bytes 98312 | tf_op jit(solution)/shard_map/ppermute | solution.py:314
  41.7 1.7 %shift_cols.1 = bf16[3,128,512]{2,1,0:T(8,128)(2,1)} custom-call(s32[2,3]{1,0:T(2,128)S(1)} %bitcast.6, bf16[3,128,512]{2,1,0:T(8,128)(2,1)S(1)} %get-tuple-element.32.moved, bf16[128,128]{1,0:T(8,128)(2,1)S(1)} %collective-permute-done.3.from_left, bf16[128,128]{1,0:T(8,128)(2,1)S(1)} %collective-permute-done.4.from_right), custom_call_target="tpu_custom_call" | custom-call | flops 1000000 | bytes 851992 | tf_op jit(solution)/shard_map/shift_cols/pallas_call | solution.py:31
  43.4 1.4 %imaging.2.refs_8_ = f32[64,2560]{1,0:T(8,128)} custom-call(bf16[32,768]{1,0:T(8,128)(2,1)S(1)} %get-tuple-element.48.refs_0_, bf16[32,768]{1,0:T(8,128)(2,1)S(1)} %collective-permute-done.10.refs_1_, bf16[32,768]{1,0:T(8,128)(2,1)S(1)} %collective-permute-done.11.refs_2_, bf16[32,768]{1,0:T(8,128)(2,1)S(1)} %collective-permute-done.12.refs_3_, ...), custom_call_target="tpu_custom_call" | custom-call | flops 200000000 | bytes 933888 | tf_op jit(solution)/shard_map/imaging/pallas_call | solution.py:199
  44.8 1.3 %imaging.3 = f32[64,2560]{1,0:T(8,128)} custom-call(bf16[32,512]{1,0:T(8,128)(2,1)S(1)} %get-tuple-element.41.refs_0_, bf16[32,512]{1,0:T(8,128)(2,1)S(1)} %collective-permute-done.6.refs_1_, bf16[32,512]{1,0:T(8,128)(2,1)S(1)} %collective-permute-done.7.refs_2_, bf16[32,512]{1,0:T(8,128)(2,1)S(1)} %collective-permute-done.8.refs_3_, ...), custom_call_target="tpu_custom_call", output_to_operand_aliasing={{}: (8, {})} | custom-call | flops 200000000 | bytes 1523712 | tf_op jit(solution)/shard_map/imaging/pallas_call | solution.py:199
  (25 shorter events, 0.1 us)
Async XLA Ops:
  0.6 3.1 %collective-permute-start = (bf16[3,128,512]{2,1,0:T(8,128)(2,1)}, bf16[3,128,512]{2,1,0:T(8,128)(2,1)S(1)}, u32[]{:S(2)}, u32[]{:S(2)}) collective-permute-start(bf16[3,128,512]{2,1,0:T(8,128)(2,1)} %own.3), channel_id=1, source_target_pairs={{0,1},{1,0},{2,3},{3,2},{4,5},{5,4},{6,7},{7,6},{8,9},{9,8},{10,11... | collective-permute-start | bytes 1179656 | tf_op jit(solution)/shard_map/ppermute | solution.py:311
  1.1 12.5 %collective-permute-start.1 = (bf16[3,128,512]{2,1,0:T(8,128)(2,1)}, bf16[3,128,512]{2,1,0:T(8,128)(2,1)S(1)}, u32[]{:S(2)}, u32[]{:S(2)}) collective-permute-start(bf16[3,128,512]{2,1,0:T(8,128)(2,1)} %own.3), channel_id=1, source_target_pairs={{0,2},{1,3},{2,0},{3,1},{4,6},{5,7},{6,4},{7,5},{8,10},{9,11},{10,... | collective-permute-start | bytes 1179656 | tf_op jit(solution)/shard_map/ppermute | solution.py:311
  3.7 1.0 %copy-start = (bf16[3,128,512]{2,1,0:T(8,128)(2,1)S(1)}, bf16[3,128,512]{2,1,0:T(8,128)(2,1)}, u32[]{:S(2)}) copy-start(bf16[3,128,512]{2,1,0:T(8,128)(2,1)} %own.3) | copy-start | bytes 1179652
  4.7 0.9 %copy-start.5 = (f32[32,1280]{1,0:T(8,128)S(1)}, f32[32,1280]{1,0:T(8,128)}, u32[]{:S(2)}) copy-start(f32[32,1280]{1,0:T(8,128)} %amplitude.1) | copy-start | bytes 491524
  5.7 0.8 %copy-start.6 = (f32[128,128]{1,0:T(8,128)S(1)}, f32[128,128]{1,0:T(8,128)}, u32[]{:S(2)}) copy-start(f32[128,128]{1,0:T(8,128)} %constant.8.clone.ones) | copy-start | bytes 196612
  6.5 0.7 %copy-start.7 = (s32[3,2]{0,1:T(2,128)S(1)}, s32[3,2]{0,1:T(2,128)}, u32[]{:S(2)}) copy-start(s32[3,2]{0,1:T(2,128)} %param.11) | copy-start | bytes 76
  7.2 0.7 %copy-start.9 = (s32[4,3,2]{0,2,1:T(2,128)S(1)}, s32[4,3,2]{0,2,1:T(2,128)}, u32[]{:S(2)}) copy-start(s32[4,3,2]{0,2,1:T(2,128)} %param.12) | copy-start | bytes 292
  7.9 0.7 %copy-start.10 = (s32[4,3,2]{0,2,1:T(2,128)S(1)}, s32[4,3,2]{0,2,1:T(2,128)}, u32[]{:S(2)}) copy-start(s32[4,3,2]{0,2,1:T(2,128)} %param.13) | copy-start | bytes 292
  13.6 1.7 %collective-permute-start.2 = (bf16[3,128,512]{2,1,0:T(8,128)(2,1)S(1)}, bf16[3,128,512]{2,1,0:T(8,128)(2,1)S(1)}, u32[]{:S(2)}, u32[]{:S(2)}) collective-permute-start(bf16[3,128,512]{2,1,0:T(8,128)(2,1)S(1)} %collective-permute-done.1.across), channel_id=1, source_target_pairs={{0,1},{1,0},{2,3},{3,2},{4,5},{5,4},{6,7},{7,6},{8,9},{9,8},{10,11... | collective-permute-start | bytes 1179656 | tf_op jit(solution)/shard_map/ppermute | solution.py:311
  16.4 13.8 %copy-start.1 = (bf16[3,128,512]{2,1,0:T(8,128)(2,1)S(1)}, bf16[3,128,512]{2,1,0:T(8,128)(2,1)}, u32[]{:S(2)}) copy-start(bf16[3,128,512]{2,1,0:T(8,128)(2,1)} %own.3) | copy-start | bytes 1179652
  16.5 13.8 %copy-start.8 = (s32[3,2]{0,1:T(2,128)S(1)}, s32[3,2]{0,1:T(2,128)}, u32[]{:S(2)}) copy-start(s32[3,2]{0,1:T(2,128)} %param.11) | copy-start | bytes 76
  16.5 26.9 %copy-start.2 = (bf16[256,512]{1,0:T(8,128)(2,1)S(1)}, bf16[256,512]{1,0:T(8,128)(2,1)}, u32[]{:S(2)}) copy-start(bf16[256,512]{1,0:T(8,128)(2,1)} %constant.10.clone.refs_6_) | copy-start | bytes 786436
  16.5 26.9 %copy-start.3 = (bf16[256,512]{1,0:T(8,128)(2,1)S(1)}, bf16[256,512]{1,0:T(8,128)(2,1)}, u32[]{:S(2)}) copy-start(bf16[256,512]{1,0:T(8,128)(2,1)} %constant.9.clone.refs_5_) | copy-start | bytes 786436
  16.5 26.9 %copy-start.4 = (bf16[128,192]{1,0:T(8,128)(2,1)S(1)}, bf16[128,192]{1,0:T(8,128)(2,1)}, u32[]{:S(2)}) copy-start(bf16[128,192]{1,0:T(8,128)(2,1)} %constant.11.clone.refs_7_) | copy-start | bytes 147460
  16.5 7.8 %collective-permute-start.9 = (bf16[4,32,768]{2,1,0:T(8,128)(2,1)S(1)}, bf16[4,32,768]{2,1,0:T(8,128)(2,1)S(1)}, u32[]{:S(2)}, u32[]{:S(2)}) collective-permute-start(bf16[4,32,768]{2,1,0:T(8,128)(2,1)S(1)} %get-tuple-element.47), channel_id=1, source_target_pairs={{0,4},{4,0},{8,12},{12,8},{16,20},{20,16},{24,28},{28,24},{1,5},{5... | collective-permute-start | bytes 589832 | tf_op jit(solution)/shard_map/ppermute | solution.py:362
  18.9 13.7 %collective-permute-start.5 = (bf16[4,32,512]{2,1,0:T(8,128)(2,1)S(1)}, bf16[4,32,512]{2,1,0:T(8,128)(2,1)S(1)}, u32[]{:S(2)}, u32[]{:S(2)}) collective-permute-start(bf16[4,32,512]{2,1,0:T(8,128)(2,1)S(1)} %get-tuple-element.40), channel_id=1, source_target_pairs={{0,4},{4,0},{8,12},{12,8},{16,20},{20,16},{24,28},{28,24},{1,5},{5... | collective-permute-start | bytes 393224 | tf_op jit(solution)/shard_map/ppermute | solution.py:362
  24.4 13.4 %collective-permute-start.10 = (bf16[32,768]{1,0:T(8,128)(2,1)S(1)}, bf16[32,768]{1,0:T(8,128)(2,1)S(1)}, u32[]{:S(2)}, u32[]{:S(2)}) collective-permute-start(bf16[32,768]{1,0:T(8,128)(2,1)S(1)} %get-tuple-element.49), channel_id=1, source_target_pairs={{0,8},{4,12},{8,16},{12,20},{16,24},{20,28},{24,0},{28,4},{1,9},{5... | collective-permute-start | bytes 147464 | tf_op jit(solution)/shard_map/ppermute | solution.py:314
  26.3 17.1 %collective-permute-start.11 = (bf16[32,768]{1,0:T(8,128)(2,1)S(1)}, bf16[32,768]{1,0:T(8,128)(2,1)S(1)}, u32[]{:S(2)}, u32[]{:S(2)}) collective-permute-start(bf16[32,768]{1,0:T(8,128)(2,1)S(1)} %get-tuple-element.50), channel_id=1, source_target_pairs={{0,16},{4,20},{8,24},{12,28},{16,0},{20,4},{24,8},{28,12},{1,17},{... | collective-permute-start | bytes 147464 | tf_op jit(solution)/shard_map/ppermute | solution.py:314
  28.9 14.5 %collective-permute-start.12 = (bf16[32,768]{1,0:T(8,128)(2,1)S(1)}, bf16[32,768]{1,0:T(8,128)(2,1)S(1)}, u32[]{:S(2)}, u32[]{:S(2)}) collective-permute-start(bf16[32,768]{1,0:T(8,128)(2,1)S(1)} %get-tuple-element.51), channel_id=1, source_target_pairs={{0,24},{4,28},{8,0},{12,4},{16,8},{20,12},{24,16},{28,20},{1,25},{... | collective-permute-start | bytes 147464 | tf_op jit(solution)/shard_map/ppermute | solution.py:314
  31.1 6.7 %collective-permute-start.3 = (bf16[128,128]{1,0:T(8,128)(2,1)S(1)}, bf16[128,128]{1,0:T(8,128)(2,1)S(1)}, u32[]{:S(2)}, u32[]{:S(2)}) collective-permute-start(bf16[128,128]{1,0:T(8,128)(2,1)S(1)} %get-tuple-element.33), channel_id=1, source_target_pairs={{0,4},{4,8},{8,12},{12,16},{16,20},{20,24},{24,28},{28,0},{1,5},{5... | collective-permute-start | bytes 98312 | tf_op jit(solution)/shard_map/ppermute | solution.py:314
  32.7 5.1 %collective-permute-start.4 = (bf16[128,128]{1,0:T(8,128)(2,1)S(1)}, bf16[128,128]{1,0:T(8,128)(2,1)S(1)}, u32[]{:S(2)}, u32[]{:S(2)}) collective-permute-start(bf16[128,128]{1,0:T(8,128)(2,1)S(1)} %get-tuple-element.34), channel_id=1, source_target_pairs={{0,28},{4,0},{8,4},{12,8},{16,12},{20,16},{24,20},{28,24},{1,29},{... | collective-permute-start | bytes 98312 | tf_op jit(solution)/shard_map/ppermute | solution.py:314
  37.8 7.0 %collective-permute-start.6 = (bf16[32,512]{1,0:T(8,128)(2,1)S(1)}, bf16[32,512]{1,0:T(8,128)(2,1)S(1)}, u32[]{:S(2)}, u32[]{:S(2)}) collective-permute-start(bf16[32,512]{1,0:T(8,128)(2,1)S(1)} %get-tuple-element.42), channel_id=1, source_target_pairs={{0,8},{4,12},{8,16},{12,20},{16,24},{20,28},{24,0},{28,4},{1,9},{5... | collective-permute-start | bytes 98312 | tf_op jit(solution)/shard_map/ppermute | solution.py:314
  37.8 7.0 %collective-permute-start.7 = (bf16[32,512]{1,0:T(8,128)(2,1)S(1)}, bf16[32,512]{1,0:T(8,128)(2,1)S(1)}, u32[]{:S(2)}, u32[]{:S(2)}) collective-permute-start(bf16[32,512]{1,0:T(8,128)(2,1)S(1)} %get-tuple-element.43), channel_id=1, source_target_pairs={{0,16},{4,20},{8,24},{12,28},{16,0},{20,4},{24,8},{28,12},{1,17},{... | collective-permute-start | bytes 98312 | tf_op jit(solution)/shard_map/ppermute | solution.py:314
  37.8 7.0 %collective-permute-start.8 = (bf16[32,512]{1,0:T(8,128)(2,1)S(1)}, bf16[32,512]{1,0:T(8,128)(2,1)S(1)}, u32[]{:S(2)}, u32[]{:S(2)}) collective-permute-start(bf16[32,512]{1,0:T(8,128)(2,1)S(1)} %get-tuple-element.44), channel_id=1, source_target_pairs={{0,24},{4,28},{8,0},{12,4},{16,8},{20,12},{24,16},{28,20},{1,25},{... | collective-permute-start | bytes 98312 | tf_op jit(solution)/shard_map/ppermute | solution.py:314

commit v4 on v3

--- a/solution.py
+++ b/solution.py
@@ -12,8 +12,9 @@
 SPOT_PIX = 32
 WIND_MAX = 8
 LANES = 128
-
-SMEM_SPEC = pl.BlockSpec(memory_space=pltpu.SMEM)
+STRIP = 32
+
+HBM_SPEC = pl.BlockSpec(memory_space=pltpu.HBM)
 VMEM_SPEC = pl.BlockSpec(memory_space=pltpu.VMEM)
 
 
@@ -22,21 +23,34 @@
     return pltpu.CompilerParams(vmem_limit_bytes=held + 8 * 1024 * 1024)
 
 
-def call(kernel, out_shape, operands, flops, name):
-    def spec(array):
-        return SMEM_SPEC if array.dtype == jnp.int32 else VMEM_SPEC
+def call(kernel, out_shape, operands, flops, name, in_hbm=(), scratch=()):
+    def spec(k, array):
+        return HBM_SPEC if array.dtype == jnp.int32 or k in in_hbm else VMEM_SPEC
 
     out_specs = jax.tree.map(lambda _: VMEM_SPEC, out_shape)
     size = sum(array.size * array.dtype.itemsize for array in jax.tree.leaves((operands, out_shape)))
+    in_specs = [spec(k, array) for k, array in enumerate(operands)]
+    operands = [
+        pltpu.with_memory_space_constraint(array, pltpu.HBM) if space is HBM_SPEC else array
+        for array, space in zip(operands, in_specs)
+    ]
     return pl.pallas_call(
         kernel,
         out_shape=out_shape,
-        in_specs=[spec(array) for array in operands],
+        in_specs=in_specs,
         out_specs=out_specs,
+        scratch_shapes=list(scratch),
         compiler_params=params(operands, out_shape),
         cost_estimate=pl.CostEstimate(flops=flops, bytes_accessed=size, transcendentals=0),
         name=name,
     )(*operands)
+
+
+def fetch(*pairs):
+    copies = [pltpu.make_async_copy(source, target, sem) for source, target, sem in pairs]
+    for copy in copies:
+        copy.start()
+    return copies
 
 
 def wrap(value, length):
@@ -54,7 +68,16 @@
     return base, upper, 1.0 - fraction, fraction
 
 
-def early_kernel(n_layer, wind, offsets, ratio, amplitude, ones, own, near, rows_out, cols_out, amp_out, early_out):
+def early_kernel(n_layer, wind_hbm, offsets_hbm, ratio_hbm, own_hbm, near, rows_out, cols_out, early_out, own, *scratch):
+    wind, offsets, ratio, sems = scratch
+    loads = fetch(
+        (wind_hbm, wind, sems.at[0]),
+        (offsets_hbm, offsets, sems.at[1]),
+        (ratio_hbm, ratio, sems.at[2]),
+        (own_hbm, own, sems.at[3]),
+    )
+    for load in loads:
+        load.wait()
     layers, rows_dev, cols_dev = own.shape
     pupil_rows = rows_out.shape[1]
     screen_rows = 4 * rows_dev
@@ -105,7 +128,10 @@
             return carry
 
         lax.fori_loop(0, pupil_cols // LANES, tile, 0)
-    rows = amplitude.shape[0]
+
+
+def optics_kernel(amplitude, ones, columns, lines, amp_out, high_out, low_out, lines_out):
+    rows, pupil_cols = amplitude.shape
     for step in range(pupil_cols // LANES):
         cut = slice(step * LANES, (step + 1) * LANES)
         amp = amplitude[:, cut]
@@ -113,80 +139,96 @@
         energy = jnp.broadcast_to(energy[:, None], (rows // SUB_PIX, SUB_PIX, LANES)).reshape(rows, LANES)
         total = jnp.dot(energy, ones[...], precision=lax.Precision.HIGHEST, preferred_element_type=jnp.float32)
         amp_out[:, cut] = amp * lax.rsqrt(total)
+    high_out[...], low_out[...] = split(columns[...])
+    high, low = split(lines[...])
+    lines_out[...] = jnp.concatenate([high, high, low], axis=1)
 
 
 def project_cols(projected, cols_ref, start, stop, kept, sent):
     layers, cols_dev, _ = cols_ref.shape
-    blocks, size, _ = kept.shape
+    half = kept.shape[0]
     for at in range(start, stop, 256):
         cols = cols_ref[:, :, at : at + 256].reshape(layers * cols_dev, 256)
         phase = jnp.dot(projected, cols, preferred_element_type=jnp.float32).astype(jnp.bfloat16)
-        phase = phase.reshape(2, blocks, size, 256)
-        kept[:, :, at - start : at - start + 256] = phase[0]
-        sent[:, :, at - start : at - start + 256] = phase[1]
-
-
-def first_kernel(stop, early, rows_ref, cols_ref, across, far, projected, kept, sent):
-    layers = early.shape[0]
-    width = across.shape[2]
+        kept[:, at - start : at - start + 256] = phase[:half]
+        sent[:, at - start : at - start + 256] = phase[half:]
+
+
+def shifted_rows(wind, own, near, far, level, start, stop):
+    odd = lax.rem(lax.axis_index("dir"), 2) == 1
+    rows = own.shape[1]
+    near_last = near[level, rows - 16 :, start:stop].astype(jnp.float32)
+    near_first = near[level, :16, start:stop].astype(jnp.float32)
+    far_last = far[level, rows - 16 :, start:stop].astype(jnp.float32)
+    far_first = far[level, :16, start:stop].astype(jnp.float32)
+    before = jnp.where(odd, near_last, far_last)
+    after = jnp.where(odd, far_first, near_first)
+    wide = jnp.concatenate([before, own[level, :, start:stop].astype(jnp.float32), after], axis=0)
+    shift = wind[0, level]
+    shift = jnp.where(shift < 0, shift + rows + 32, shift)
+    return pltpu.roll(wide, shift, 0)[16 : 16 + rows]
+
+
+def first_kernel(stop, wind_hbm, early, rows_ref, cols_ref, own, near, across, far, projected, kept, sent, wind, sem):
+    load = fetch((wind_hbm, wind, sem))[0]
+    layers, rows, width = own.shape
     for level in range(layers):
         screen = jnp.concatenate([across[level], far[level]], axis=0)
         part = early[level] + jnp.dot(rows_ref[level], screen, preferred_element_type=jnp.float32)
         projected[:, level * width : (level + 1) * width] = part.astype(jnp.bfloat16)
     project_cols(projected[...], cols_ref, 0, stop, kept, sent)
+    load.wait()
+    lane = lax.broadcasted_iota(jnp.int32, (rows, LANES), 1)
+    strips = jnp.zeros((rows, LANES), jnp.float32)
+    for level in range(layers):
+        at = WIND_MAX * level
+        last = shifted_rows(wind, own, near, far, level, width - LANES, width)
+        last = pltpu.roll(last, WIND_MAX + at, 1)
+        strips = jnp.where((lane >= at) & (lane < at + WIND_MAX), last, strips)
+        at = STRIP + WIND_MAX * level
+        initial = pltpu.roll(shifted_rows(wind, own, near, far, level, 0, LANES), at, 1)
+        strips = jnp.where((lane >= at) & (lane < at + WIND_MAX), initial, strips)
+    strips = strips.T
+    sent[: 2 * STRIP, stop:] = strips[: 2 * STRIP].astype(jnp.bfloat16)
+    sent[2 * STRIP :, stop:] = jnp.zeros((sent.shape[0] - 2 * STRIP, rows), jnp.bfloat16)
 
 
 def later_kernel(start, stop, projected, cols_ref, kept, sent):
     project_cols(projected[...], cols_ref, start, stop, kept, sent)
 
 
-def add_kernel(kept, came, *outs):
+def add_kernel(width, kept, came, *outs):
+    rows = outs[0].shape[0]
     for k, out in enumerate(outs):
-        out[...] = (kept[k].astype(jnp.float32) + came[k].astype(jnp.float32)).astype(jnp.bfloat16)
-
-
-def rows_kernel(wind, own, near, far, moved, right, left):
+        cut = slice(k * rows, (k + 1) * rows)
+        total = kept[cut].astype(jnp.float32) + came[cut, :width].astype(jnp.float32)
+        out[:, :width] = total.astype(jnp.bfloat16)
+        if out.shape[1] > width:
+            out[:, width:] = came[:STRIP, width:] if k == 1 else came[STRIP : 2 * STRIP, width:]
+
+
+def shift_kernel(wind_hbm, own, near, far, partner, below, above, out, wind, sem):
+    load = fetch((wind_hbm, wind, sem))[0]
     layers, rows, cols = own.shape
-    odd = lax.rem(lax.axis_index("dir"), 2) == 1
+    second = lax.rem(lax.axis_index("layer"), 2) == 1
+    at = partner.shape[1] - rows
+    partner_last = partner[:STRIP, at:].astype(jnp.float32)
+    partner_first = partner[STRIP : 2 * STRIP, at:].astype(jnp.float32)
+    at = below.shape[1] - rows
+    left = jnp.where(second, partner_last, below[:, at:].astype(jnp.float32))
+    right = jnp.where(second, above[:, at:].astype(jnp.float32), partner_first)
+    strips = jnp.concatenate([left, right, jnp.zeros((LANES - 2 * STRIP, rows), jnp.float32)], axis=0).T
     lane = lax.broadcasted_iota(jnp.int32, (rows, LANES), 1)
-    to_right = jnp.zeros((rows, LANES), jnp.float32)
-    to_left = jnp.zeros((rows, LANES), jnp.float32)
+    load.wait()
     for level in range(layers):
-        near_last = near[level, rows - 16 :, :].astype(jnp.float32)
-        near_first = near[level, :16, :].astype(jnp.float32)
-        far_last = far[level, rows - 16 :, :].astype(jnp.float32)
-        far_first = far[level, :16, :].astype(jnp.float32)
-        before = jnp.where(odd, near_last, far_last)
-        after = jnp.where(odd, far_first, near_first)
-        wide = jnp.concatenate([before, own[level].astype(jnp.float32), after], axis=0)
-        shift = wind[0, level]
-        shift = jnp.where(shift < 0, shift + rows + 32, shift)
-        wide = pltpu.roll(wide, shift, 0)[16 : 16 + rows]
-        moved[level] = wide.astype(jnp.bfloat16)
-        mine = (lane >= WIND_MAX * level) & (lane < WIND_MAX * (level + 1))
-        last = pltpu.roll(wide[:, cols - LANES :], WIND_MAX * (level + 1), 1)
-        to_right = jnp.where(mine, last, to_right)
-        initial = wide[:, :LANES]
-        if level:
-            initial = pltpu.roll(initial, WIND_MAX * level, 1)
-        to_left = jnp.where(mine, initial, to_left)
-    right[...] = to_right.astype(jnp.bfloat16)
-    left[...] = to_left.astype(jnp.bfloat16)
-
-
-def cols_kernel(wind, moved, from_left, from_right, out):
-    layers, rows, cols = moved.shape
-    lane = lax.broadcasted_iota(jnp.int32, (rows, LANES), 1)
-    before = from_left[...].astype(jnp.float32)
-    after = from_right[...].astype(jnp.float32)
-    for level in range(layers):
-        last = pltpu.roll(before, LANES - WIND_MAX * (level + 1), 1)
-        first = pltpu.roll(after, LANES - WIND_MAX * level, 1) if level else after
+        last = pltpu.roll(strips, LANES - WIND_MAX * (level + 1), 1)
+        first = pltpu.roll(strips, LANES - STRIP - WIND_MAX * level, 1)
         extra = jnp.where(lane < WIND_MAX, first, last)
-        wide = jnp.concatenate([moved[level].astype(jnp.float32), extra], axis=1)
+        moved = shifted_rows(wind, own, near, far, level, 0, cols)
         shift = wind[1, level]
         shift = jnp.where(shift < 0, shift + cols + LANES, shift)
-        out[level] = pltpu.roll(wide, shift, 1)[:, :cols].astype(jnp.bfloat16)
+        wide = pltpu.roll(jnp.concatenate([moved, extra], axis=1), shift, 1)
+        out[level] = wide[:, :cols].astype(jnp.bfloat16)
 
 
 def image(start, stop, pairs, operands, out_shape):
@@ -195,12 +237,12 @@
     aliases = {}
     if len(operands) > len(in_specs):
         aliases = {len(in_specs): 0}
-        in_specs = in_specs + [pl.BlockSpec(memory_space=pl.ANY)]
+        in_specs = in_specs + [HBM_SPEC]
     return pl.pallas_call(
         functools.partial(imaging_kernel, pairs, start),
-        out_shape=out_shape,
+        out_shape=jax.ShapeDtypeStruct(out_shape.shape, out_shape.dtype),
         in_specs=in_specs,
-        out_specs=pl.BlockSpec(memory_space=pl.ANY),
+        out_specs=HBM_SPEC,
         scratch_shapes=[pltpu.VMEM((out_shape.shape[0], 2 * (stop - start)), jnp.float32), pltpu.SemaphoreType.DMA],
         input_output_aliases=aliases,
         compiler_params=params(operands, out_shape),
@@ -239,7 +281,7 @@
     tiles = cols // LANES
     phase = parts[0][...].astype(jnp.float32)
     for part in parts[1:]:
-        phase = phase + part[...].astype(jnp.float32)
+        phase = phase + part[:, :cols].astype(jnp.float32)
     sine, cosine = sin_cos(phase)
     amp = amp_ref[:, start : start + cols]
     real, imag = amp * cosine, amp * sine
@@ -284,14 +326,7 @@
     row_cos, row_sin = blocks(cos, count), blocks(sin, count)
     lines = np.block([[row_cos, row_sin], [-row_sin, row_cos]])
 
-    def halves(value):
-        value = value.astype(np.float32)
-        high = value.astype(jnp.bfloat16)
-        return high, (value - high.astype(np.float32)).astype(jnp.bfloat16)
-
-    cols_high, cols_low = halves(columns)
-    rows_high, rows_low = halves(lines)
-    return cols_high, cols_low, np.concatenate([rows_high, rows_high, rows_low], axis=1)
+    return columns.astype(np.float32), lines.astype(np.float32)
 
 
 def per_device(screens, amplitude, wind, offsets, ratio):
@@ -318,80 +353,90 @@
 
     across = swap(screens, 2)
     near = swap(screens, 1)
-    ones = np.kron(np.eye(LANES // SUB_PIX), np.ones((SUB_PIX, SUB_PIX))).astype(np.float32)
-    row_weights, col_weights, amp, early = call(
+    smem, sem = pltpu.SMEM, pltpu.SemaphoreType.DMA
+    row_weights, col_weights, early, own = call(
         functools.partial(early_kernel, n_layer),
         (
             shape(layers, pupil_rows, 2 * rows_dev),
             shape(layers, cols_dev, pupil_cols),
-            shape(rows, pupil_cols, dtype=f32),
             shape(layers, pupil_rows, cols_dev, dtype=f32),
+            shape(layers, rows_dev, cols_dev),
         ),
-        (wind, offsets, ratio, amplitude, jnp.asarray(ones), screens, near),
+        (wind, offsets, ratio, screens, near),
         200_000_000,
         "early",
-    )
-    across, row_weights, col_weights, amp, early = lax.optimization_barrier(
-        (across, row_weights, col_weights, amp, early)
+        in_hbm=(3,),
+        scratch=[smem(array.shape, jnp.int32) for array in (wind, offsets, ratio)] + [sem((4,))],
+    )
+    across, row_weights, col_weights, early, own = lax.optimization_barrier(
+        (across, row_weights, col_weights, early, own)
     )
     far = swap(across, 1)
 
     pairs = n_layer // 2
     cuts = [0, (pupil_cols * 5 // 8) // 256 * 256, pupil_cols]
     kept, sent = [None, None], [None, None]
-
-    def halves(piece):
-        return [shape(pairs, rows, cuts[piece + 1] - cuts[piece])] * 2
+    widths = [stop - start for start, stop in zip(cuts, cuts[1:])]
+    half = pairs * rows
+    assert half >= 2 * STRIP and rows == STRIP and pairs > 2
+    wind_scratch = [smem(wind.shape, jnp.int32), sem]
 
     projected, kept[0], sent[0] = call(
         functools.partial(first_kernel, cuts[1]),
-        [shape(pupil_rows, layers * cols_dev)] + halves(0),
-        (early, row_weights, col_weights, across, far),
+        [shape(pupil_rows, layers * cols_dev), shape(half, widths[0]), shape(half, widths[0] + rows_dev)],
+        (wind, early, row_weights, col_weights, own, near, across, far),
         800_000_000,
         "project_first",
+        scratch=wind_scratch,
     )
     kept[1], sent[1] = call(
         functools.partial(later_kernel, cuts[1], cuts[2]),
-        halves(1),
+        [shape(half, widths[1])] * 2,
         (projected, col_weights),
         500_000_000,
         "project_later",
     )
+    came = [lax.ppermute(part, "layer", [(i, i ^ 1) for i in range(n_layer)]) for part in sent]
+
+    amplitude, kept[1] = lax.optimization_barrier((amplitude, kept[1]))
+    ones = np.kron(np.eye(LANES // SUB_PIX), np.ones((SUB_PIX, SUB_PIX))).astype(np.float32)
+    columns, lines = tables(rows)
+    optics = call(
+        optics_kernel,
+        (
+            shape(rows, pupil_cols, dtype=f32),
+            shape(*columns.shape),
+            shape(*columns.shape),
+            shape(lines.shape[0], 3 * lines.shape[1]),
+        ),
+        (amplitude, jnp.asarray(ones), jnp.asarray(columns), jnp.asarray(lines)),
+        30_000_000,
+        "optics",
+    )
+    kept[0], *optics = lax.optimization_barrier((kept[0], *optics))
+
     received = []
     for piece in range(2):
-        came = lax.ppermute(sent[piece], "layer", [(i, i ^ 1) for i in range(n_layer)])
+        extra = [rows_dev if piece == 0 and k in (1, pairs - 1) else 0 for k in range(pairs)]
         sums = call(
-            add_kernel,
-            [shape(rows, cuts[piece + 1] - cuts[piece])] * pairs,
-            (kept[piece], came),
+            functools.partial(add_kernel, widths[piece]),
+            [shape(rows, widths[piece] + more) for more in extra],
+            (kept[piece], came[piece]),
             1_000_000,
             "add_pair",
         )
         received.append([sums[0]] + [turn(sums[k], 2 * k) for k in range(1, pairs)])
 
-    moved, right, left = call(
-        rows_kernel,
-        (shape(layers, rows_dev, cols_dev), shape(rows_dev, LANES), shape(rows_dev, LANES)),
-        (wind, screens, near, far),
+    spots = image(cuts[0], cuts[1], pairs, [*received[0], *optics], shape(2 * rows, 2 * pupil_cols, dtype=f32))
+    new_screens = call(
+        shift_kernel,
+        shape(layers, rows_dev, cols_dev),
+        (wind, own, near, far, came[0], received[0][1], received[0][pairs - 1]),
         1_000_000,
-        "shift_rows",
-    )
-    from_left = turn(right, 1)
-    from_right = turn(left, n_layer - 1)
-    new_screens = call(
-        cols_kernel,
-        shape(layers, rows_dev, cols_dev),
-        (wind, moved, from_left, from_right),
-        1_000_000,
-        "shift_cols",
-    )
-
-    dft = [jnp.asarray(table) for table in tables(rows)]
-    spots = None
-    for piece in range(2):
-        start, stop = cuts[piece], cuts[piece + 1]
-        operands = [*received[piece], amp, *dft] + ([] if spots is None else [spots])
-        spots = image(start, stop, pairs, operands, shape(2 * rows, 2 * pupil_cols, dtype=f32))
+        "shift",
+        scratch=wind_scratch,
+    )
+    spots = image(cuts[1], cuts[2], pairs, [*received[1], *optics, spots], spots)
     return (new_screens, spots[None])
 
 

time: 46.4 us -> 40.2 us (0.87)
  local copies, waits for them, and re-layouts: 4.86 us -> 0.03 us
  starting transfers between devices: 19.7 us -> 15.1 us
  waiting for transfers between devices: 9.71 us -> 12.9 us
    ppermute x3, waiting for transfers between devices: 2.75 us -> 7.78 us  [swap(): return lax.ppermute(value, 'dir', [(i, i ^ bit) for i in range(n_dir)])]
    unnamed x22 -> x8, local copies, waits for them, and re-layouts: 4.86 us -> 0.03 us
    ppermute x8 -> x6, starting transfers between devices: 14.5 us -> 9.89 us  [turn(): lax.ppermute(value, 'layer', [(i, (i + step) % n_layer) for i in range(n_...]
    ppermute x8 -> x6, waiting for transfers between devices: 1.89 us -> 0.02 us  [turn(): lax.ppermute(value, 'layer', [(i, (i + step) % n_layer) for i in range(n_...]
  transfers between devices with their start and end apart: 13 -> 11, of which waited for: 4 -> 3; matrix products, arithmetic and copies ran while one was open for 0% -> 0% of each run, Pallas kernels for 19% -> 21%
where the time goes in v4:
time: 40.2 us; the launch traced here: 40.1 us
  starting transfers between devices  15.1 us (38%)
  waiting for transfers between devices  12.9 us (32%)
  Pallas kernels  11.3 us (28%)
  between operations  0.76 us (2%)
    ppermute x6, starting transfers between devices, turn(): lax.ppermute(value, 'layer', [(i, (i + step) % n_layer) for i in range(n_...  9.89 us
    pallas_call x7, Pallas kernels, call(): pl.pallas_call(kernel, out_shape=out_shape, in_specs=in_specs, out_specs=...  8.59 us
    ppermute x3, waiting for transfers between devices, swap(): return lax.ppermute(value, 'dir', [(i, i ^ bit) for i in range(n_dir)])  7.78 us
    ppermute x2, waiting for transfers between devices, per_device(): lax.ppermute(part, 'layer', [(i, i ^ 1) for i in range(n_layer)])  5.08 us
    ppermute x3, starting transfers between devices, swap(): return lax.ppermute(value, 'dir', [(i, i ^ bit) for i in range(n_dir)])  3.08 us
    pallas_call x2, Pallas kernels, image(): pl.pallas_call(functools.partial(imaging_kernel, pairs, start), out_shape...  2.66 us
    ppermute x2, starting transfers between devices, per_device(): lax.ppermute(part, 'layer', [(i, i ^ 1) for i in range(n_layer)])  2.16 us
  transfers between devices with their start and end apart: 11, of which 3 were waited for; matrix products, arithmetic and copies ran while one was open for 0% of the time, Pallas kernels for 21%

profile of v4, /device:TPU:0, one launch (start us, length us, event | category | flops | bytes accessed | tf_op | source)
XLA Modules:
  0.0 40.1 jit_solution(16562135552480517581)
XLA Ops:
  0.6 0.5 %collective-permute-start.1 = (bf16[3,128,512]{2,1,0:T(8,128)(2,1)}, bf16[3,128,512]{2,1,0:T(8,128)(2,1)S(1)}, u32[]{:S(2)}, u32[]{:S(2)}) collective-permute-start(bf16[3,128,512]{2,1,0:T(8,128)(2,1)} %own_hbm.1), channel_id=1, source_target_pairs={{0,1},{1,0},{2,3},{3,2},{4,5},{5,4},{6,7},{7,6},{8,9},{9,8},{10,11... | collective-permute-start | bytes 1179656 | tf_op jit(solution)/shard_map/ppermute | solution.py:346
  1.1 2.6 %collective-permute-start = (bf16[3,128,512]{2,1,0:T(8,128)(2,1)}, bf16[3,128,512]{2,1,0:T(8,128)(2,1)S(1)}, u32[]{:S(2)}, u32[]{:S(2)}) collective-permute-start(bf16[3,128,512]{2,1,0:T(8,128)(2,1)} %own_hbm.1), channel_id=1, source_target_pairs={{0,2},{1,3},{2,0},{3,1},{4,6},{5,7},{6,4},{7,5},{8,10},{9,11},{10,... | collective-permute-start | bytes 1179656 | tf_op jit(solution)/shard_map/ppermute | solution.py:346
  3.7 0.0 collective-permute-done.1.near
  3.7 3.8 %early.1 = (bf16[3,256,256]{2,1,0:T(8,128)(2,1)S(1)}, bf16[3,512,1280]{2,1,0:T(8,128)(2,1)S(1)}, f32[3,256,512]{2,1,0:T(8,128)S(1)}, bf16[3,128,512]{2,1,0:T(8,128)(2,1)S(1)}) custom-call(s32[2,3]{1,0:T(2,128)} %bitcast.5, s32[3,2,4]{2,1,0:T(2,128)} %bitcast.8, s32[3,2,4]{2,1,0:T(2,128)} %bitcast.9, bf16[3,128,512]{2,1,0:T(8,128)(2,1)} %own_hbm.1, ...), custom_call_target="tpu_custom_call" | custom-call | flops 200000000 | bytes 7078104 | tf_op jit(solution)/shard_map/early/pallas_call | solution.py:37
  7.6 6.1 %collective-permute-done.across = bf16[3,128,512]{2,1,0:T(8,128)(2,1)S(1)} collective-permute-done((bf16[3,128,512]{2,1,0:T(8,128)(2,1)}, bf16[3,128,512]{2,1,0:T(8,128)(2,1)S(1)}, u32[]{:S(2)}, u32[]{:S(2)}) %collective-permute-start) | collective-permute-done | bytes 393248 | tf_op jit(solution)/shard_map/ppermute | solution.py:346
  13.6 0.0 collective-permute-start.2
  13.6 1.7 %collective-permute-done.2.far = bf16[3,128,512]{2,1,0:T(8,128)(2,1)S(1)} collective-permute-done((bf16[3,128,512]{2,1,0:T(8,128)(2,1)S(1)}, bf16[3,128,512]{2,1,0:T(8,128)(2,1)S(1)}, u32[]{:S(2)}, u32[]{:S(2)}) %collective-permute-start.2) | collective-permute-done | bytes 393248 | tf_op jit(solution)/shard_map/ppermute | solution.py:346
  15.4 1.4 %project_first.1 = (bf16[256,1536]{1,0:T(8,128)(2,1)S(1)}, bf16[128,768]{1,0:T(8,128)(2,1)S(1)}, bf16[128,896]{1,0:T(8,128)(2,1)S(1)}) custom-call(s32[2,3]{1,0:T(2,128)} %bitcast.6, f32[3,256,512]{2,1,0:T(8,128)S(1)} %get-tuple-element.41.early, bf16[3,256,256]{2,1,0:T(8,128)(2,1)S(1)} %get-tuple-element.42.rows_ref, ...), custom_call_target="tpu_custom_call" | custom-call | flops 800000000 | bytes 8683544 | tf_op jit(solution)/shard_map/project_first/pallas_call | solution.py:37
  16.8 0.0 copy-start
  16.8 0.0 copy-start.1
  16.8 0.0 copy-start.2
  16.8 0.0 copy-start.3
  16.8 1.9 %collective-permute-start.3 = (bf16[128,896]{1,0:T(8,128)(2,1)S(1)}, bf16[128,896]{1,0:T(8,128)(2,1)S(1)}, u32[]{:S(2)}, u32[]{:S(2)}) collective-permute-start(bf16[128,896]{1,0:T(8,128)(2,1)S(1)} %get-tuple-element.44), channel_id=1, source_target_pairs={{0,4},{4,0},{8,12},{12,8},{16,20},{20,16},{24,28},{28,24},{1,5},{5... | collective-permute-start | bytes 688136 | tf_op jit(solution)/shard_map/ppermute | solution.py:399
  18.7 0.6 %project_later.1 = (bf16[128,512]{1,0:T(8,128)(2,1)S(1)}, bf16[128,512]{1,0:T(8,128)(2,1)S(1)}) custom-call(bf16[256,1536]{1,0:T(8,128)(2,1)S(1)} %get-tuple-element.46.projected, bf16[3,512,1280]{2,1,0:T(8,128)(2,1)S(1)} %get-tuple-element.43.cols_ref), custom_call_target="tpu_custom_call" | custom-call | flops 500000000 | bytes 4980736 | tf_op jit(solution)/shard_map/project_later/pallas_call | solution.py:37
  19.3 0.3 collective-permute-start.6
  19.6 0.7 %optics.1 = (f32[32,1280]{1,0:T(8,128)S(1)}, bf16[256,512]{1,0:T(8,128)(2,1)S(1)}, bf16[256,512]{1,0:T(8,128)(2,1)S(1)}, bf16[128,192]{1,0:T(8,128)(2,1)S(1)}) custom-call(f32[32,1280]{1,0:T(8,128)S(1)} %copy-done.1, f32[128,128]{1,0:T(8,128)S(1)} %copy-done.3, f32[256,512]{1,0:T(8,128)S(1)} %copy-done, f32[128,64]{1,0:T(8,128)S(1)} %copy-done.2), custom_call_target="tpu_custom_call" | custom-call | flops 30000000 | bytes 1523712 | tf_op jit(solution)/shard_map/optics/pallas_call | solution.py:37
  20.3 5.1 %collective-permute-done.3.came.partner = bf16[128,896]{1,0:T(8,128)(2,1)S(1)} collective-permute-done((bf16[128,896]{1,0:T(8,128)(2,1)S(1)}, bf16[128,896]{1,0:T(8,128)(2,1)S(1)}, u32[]{:S(2)}, u32[]{:S(2)}) %collective-permute-start.3) | collective-permute-done | bytes 229408 | tf_op jit(solution)/shard_map/ppermute | solution.py:399
  25.4 1.9 %collective-permute-start.4 = (bf16[32,896]{1,0:T(8,128)(2,1)S(1)}, bf16[32,896]{1,0:T(8,128)(2,1)S(1)}, u32[]{:S(2)}, u32[]{:S(2)}) collective-permute-start(bf16[32,896]{1,0:T(8,128)(2,1)S(1)} %get-tuple-element.54), channel_id=1, source_target_pairs={{0,8},{4,12},{8,16},{12,20},{16,24},{20,28},{24,0},{28,4},{1,9},{5... | collective-permute-start | bytes 172040 | tf_op jit(solution)/shard_map/ppermute | solution.py:349
  27.3 2.1 %collective-permute-start.5 = (bf16[32,896]{1,0:T(8,128)(2,1)S(1)}, bf16[32,896]{1,0:T(8,128)(2,1)S(1)}, u32[]{:S(2)}, u32[]{:S(2)}) collective-permute-start(bf16[32,896]{1,0:T(8,128)(2,1)S(1)} %get-tuple-element.55), channel_id=1, source_target_pairs={{0,24},{4,28},{8,0},{12,4},{16,8},{20,12},{24,16},{28,20},{1,25},{... | collective-permute-start | bytes 172040 | tf_op jit(solution)/shard_map/ppermute | solution.py:349
  29.4 0.9 %collective-permute-start.10 = (bf16[32,768]{1,0:T(8,128)(2,1)S(1)}, bf16[32,768]{1,0:T(8,128)(2,1)S(1)}, u32[]{:S(2)}, u32[]{:S(2)}) collective-permute-start(bf16[32,768]{1,0:T(8,128)(2,1)S(1)} %get-tuple-element.67), channel_id=1, source_target_pairs={{0,16},{4,20},{8,24},{12,28},{16,0},{20,4},{24,8},{28,12},{1,17},{... | collective-permute-start | bytes 147464 | tf_op jit(solution)/shard_map/ppermute | solution.py:349
  30.3 0.0 collective-permute-done.6.came
  30.4 1.6 %collective-permute-start.7 = (bf16[32,512]{1,0:T(8,128)(2,1)S(1)}, bf16[32,512]{1,0:T(8,128)(2,1)S(1)}, u32[]{:S(2)}, u32[]{:S(2)}) collective-permute-start(bf16[32,512]{1,0:T(8,128)(2,1)S(1)} %get-tuple-element.59), channel_id=1, source_target_pairs={{0,8},{4,12},{8,16},{12,20},{16,24},{20,28},{24,0},{28,4},{1,9},{5... | collective-permute-start | bytes 98312 | tf_op jit(solution)/shard_map/ppermute | solution.py:349
  32.0 0.5 %collective-permute-start.8 = (bf16[32,512]{1,0:T(8,128)(2,1)S(1)}, bf16[32,512]{1,0:T(8,128)(2,1)S(1)}, u32[]{:S(2)}, u32[]{:S(2)}) collective-permute-start(bf16[32,512]{1,0:T(8,128)(2,1)S(1)} %get-tuple-element.60), channel_id=1, source_target_pairs={{0,16},{4,20},{8,24},{12,28},{16,0},{20,4},{24,8},{28,12},{1,17},{... | collective-permute-start | bytes 98312 | tf_op jit(solution)/shard_map/ppermute | solution.py:349
  32.5 0.0 collective-permute-done.4.below.refs_1_
  32.5 2.8 %collective-permute-start.9 = (bf16[32,512]{1,0:T(8,128)(2,1)S(1)}, bf16[32,512]{1,0:T(8,128)(2,1)S(1)}, u32[]{:S(2)}, u32[]{:S(2)}) collective-permute-start(bf16[32,512]{1,0:T(8,128)(2,1)S(1)} %get-tuple-element.61), channel_id=1, source_target_pairs={{0,24},{4,28},{8,0},{12,4},{16,8},{20,12},{24,16},{28,20},{1,25},{... | collective-permute-start | bytes 98312 | tf_op jit(solution)/shard_map/ppermute | solution.py:349
  35.3 0.0 collective-permute-done.5.above.refs_3_
  35.3 2.0 %shift.1 = bf16[3,128,512]{2,1,0:T(8,128)(2,1)} custom-call(s32[2,3]{1,0:T(2,128)} %bitcast.7, bf16[3,128,512]{2,1,0:T(8,128)(2,1)S(1)} %get-tuple-element.39.own, bf16[3,128,512]{2,1,0:T(8,128)(2,1)S(1)} %collective-permute-done.1.near, bf16[3,128,512]{2,1,0:T(8,128)(2,1)S(1)} %collective-permute-done.2.far, ...), custom_call_target="tpu_custom_call" | custom-call | flops 1000000 | bytes 1916952 | tf_op jit(solution)/shard_map/shift/pallas_call | solution.py:37
  37.3 0.0 collective-permute-done.10.refs_2_
  37.4 1.4 %imaging.2.refs_8_ = f32[64,2560]{1,0:T(8,128)} custom-call(bf16[32,768]{1,0:T(8,128)(2,1)S(1)} %get-tuple-element.66.refs_0_, bf16[32,896]{1,0:T(8,128)(2,1)S(1)} %collective-permute-done.4.below.refs_1_, bf16[32,768]{1,0:T(8,128)(2,1)S(1)} %collective-permute-done.10.refs_2_, bf16[32,896]{1,0:T(8,128)(2,1)S(1)} %collective-permute-done.5.above.refs_3_, ...), custom_call_target="tpu_custom_call" | custom-call | flops 200000000 | bytes 950272 | tf_op jit(solution)/shard_map/imaging/pallas_call | solution.py:241
  38.8 0.0 collective-permute-done.7.refs_1_
  38.8 0.0 collective-permute-done.9.refs_3_
  38.8 1.3 %imaging.3 = f32[64,2560]{1,0:T(8,128)} custom-call(bf16[32,512]{1,0:T(8,128)(2,1)S(1)} %get-tuple-element.58.refs_0_, bf16[32,512]{1,0:T(8,128)(2,1)S(1)} %collective-permute-done.7.refs_1_, bf16[32,512]{1,0:T(8,128)(2,1)S(1)} %collective-permute-done.8.refs_2_, bf16[32,512]{1,0:T(8,128)(2,1)S(1)} %collective-permute-done.9.refs_3_, ...), custom_call_target="tpu_custom_call", output_to_operand_aliasing={{}: (8, {})} | custom-call | flops 200000000 | bytes 1523712 | tf_op jit(solution)/shard_map/imaging/pallas_call | solution.py:241
  (7 shorter events, 0.1 us)
Async XLA Ops:
  0.6 3.1 %collective-permute-start.1 = (bf16[3,128,512]{2,1,0:T(8,128)(2,1)}, bf16[3,128,512]{2,1,0:T(8,128)(2,1)S(1)}, u32[]{:S(2)}, u32[]{:S(2)}) collective-permute-start(bf16[3,128,512]{2,1,0:T(8,128)(2,1)} %own_hbm.1), channel_id=1, source_target_pairs={{0,1},{1,0},{2,3},{3,2},{4,5},{5,4},{6,7},{7,6},{8,9},{9,8},{10,11... | collective-permute-start | bytes 1179656 | tf_op jit(solution)/shard_map/ppermute | solution.py:346
  1.1 12.5 %collective-permute-start = (bf16[3,128,512]{2,1,0:T(8,128)(2,1)}, bf16[3,128,512]{2,1,0:T(8,128)(2,1)S(1)}, u32[]{:S(2)}, u32[]{:S(2)}) collective-permute-start(bf16[3,128,512]{2,1,0:T(8,128)(2,1)} %own_hbm.1), channel_id=1, source_target_pairs={{0,2},{1,3},{2,0},{3,1},{4,6},{5,7},{6,4},{7,5},{8,10},{9,11},{10,... | collective-permute-start | bytes 1179656 | tf_op jit(solution)/shard_map/ppermute | solution.py:346
  13.6 1.7 %collective-permute-start.2 = (bf16[3,128,512]{2,1,0:T(8,128)(2,1)S(1)}, bf16[3,128,512]{2,1,0:T(8,128)(2,1)S(1)}, u32[]{:S(2)}, u32[]{:S(2)}) collective-permute-start(bf16[3,128,512]{2,1,0:T(8,128)(2,1)S(1)} %collective-permute-done.across), channel_id=1, source_target_pairs={{0,1},{1,0},{2,3},{3,2},{4,5},{5,4},{6,7},{7,6},{8,9},{9,8},{10,11... | collective-permute-start | bytes 1179656 | tf_op jit(solution)/shard_map/ppermute | solution.py:346
  16.8 2.8 %copy-start = (f32[256,512]{1,0:T(8,128)S(1)}, f32[256,512]{1,0:T(8,128)}, u32[]{:S(2)}) copy-start(f32[256,512]{1,0:T(8,128)} %constant.7.clone.columns) | copy-start | bytes 1572868
  16.8 2.8 %copy-start.1 = (f32[32,1280]{1,0:T(8,128)S(1)}, f32[32,1280]{1,0:T(8,128)}, u32[]{:S(2)}) copy-start(f32[32,1280]{1,0:T(8,128)} %amplitude) | copy-start | bytes 491524
  16.8 2.8 %copy-start.2 = (f32[128,64]{1,0:T(8,128)S(1)}, f32[128,64]{1,0:T(8,128)}, u32[]{:S(2)}) copy-start(f32[128,64]{1,0:T(8,128)} %constant.8.clone.lines) | copy-start | bytes 98308
  16.8 2.8 %copy-start.3 = (f32[128,128]{1,0:T(8,128)S(1)}, f32[128,128]{1,0:T(8,128)}, u32[]{:S(2)}) copy-start(f32[128,128]{1,0:T(8,128)} %constant.6.clone.ones) | copy-start | bytes 196612
  16.8 8.5 %collective-permute-start.3 = (bf16[128,896]{1,0:T(8,128)(2,1)S(1)}, bf16[128,896]{1,0:T(8,128)(2,1)S(1)}, u32[]{:S(2)}, u32[]{:S(2)}) collective-permute-start(bf16[128,896]{1,0:T(8,128)(2,1)S(1)} %get-tuple-element.44), channel_id=1, source_target_pairs={{0,4},{4,0},{8,12},{12,8},{16,20},{20,16},{24,28},{28,24},{1,5},{5... | collective-permute-start | bytes 688136 | tf_op jit(solution)/shard_map/ppermute | solution.py:399
  19.3 11.1 %collective-permute-start.6 = (bf16[128,512]{1,0:T(8,128)(2,1)S(1)}, bf16[128,512]{1,0:T(8,128)(2,1)S(1)}, u32[]{:S(2)}, u32[]{:S(2)}) collective-permute-start(bf16[128,512]{1,0:T(8,128)(2,1)S(1)} %get-tuple-element.57), channel_id=1, source_target_pairs={{0,4},{4,0},{8,12},{12,8},{16,20},{20,16},{24,28},{28,24},{1,5},{5... | collective-permute-start | bytes 393224 | tf_op jit(solution)/shard_map/ppermute | solution.py:399
  25.4 7.1 %collective-permute-start.4 = (bf16[32,896]{1,0:T(8,128)(2,1)S(1)}, bf16[32,896]{1,0:T(8,128)(2,1)S(1)}, u32[]{:S(2)}, u32[]{:S(2)}) collective-permute-start(bf16[32,896]{1,0:T(8,128)(2,1)S(1)} %get-tuple-element.54), channel_id=1, source_target_pairs={{0,8},{4,12},{8,16},{12,20},{16,24},{20,28},{24,0},{28,4},{1,9},{5... | collective-permute-start | bytes 172040 | tf_op jit(solution)/shard_map/ppermute | solution.py:349
  27.3 8.0 %collective-permute-start.5 = (bf16[32,896]{1,0:T(8,128)(2,1)S(1)}, bf16[32,896]{1,0:T(8,128)(2,1)S(1)}, u32[]{:S(2)}, u32[]{:S(2)}) collective-permute-start(bf16[32,896]{1,0:T(8,128)(2,1)S(1)} %get-tuple-element.55), channel_id=1, source_target_pairs={{0,24},{4,28},{8,0},{12,4},{16,8},{20,12},{24,16},{28,20},{1,25},{... | collective-permute-start | bytes 172040 | tf_op jit(solution)/shard_map/ppermute | solution.py:349
  29.4 8.0 %collective-permute-start.10 = (bf16[32,768]{1,0:T(8,128)(2,1)S(1)}, bf16[32,768]{1,0:T(8,128)(2,1)S(1)}, u32[]{:S(2)}, u32[]{:S(2)}) collective-permute-start(bf16[32,768]{1,0:T(8,128)(2,1)S(1)} %get-tuple-element.67), channel_id=1, source_target_pairs={{0,16},{4,20},{8,24},{12,28},{16,0},{20,4},{24,8},{28,12},{1,17},{... | collective-permute-start | bytes 147464 | tf_op jit(solution)/shard_map/ppermute | solution.py:349
  30.4 8.4 %collective-permute-start.7 = (bf16[32,512]{1,0:T(8,128)(2,1)S(1)}, bf16[32,512]{1,0:T(8,128)(2,1)S(1)}, u32[]{:S(2)}, u32[]{:S(2)}) collective-permute-start(bf16[32,512]{1,0:T(8,128)(2,1)S(1)} %get-tuple-element.59), channel_id=1, source_target_pairs={{0,8},{4,12},{8,16},{12,20},{16,24},{20,28},{24,0},{28,4},{1,9},{5... | collective-permute-start | bytes 98312 | tf_op jit(solution)/shard_map/ppermute | solution.py:349
  32.0 6.8 %collective-permute-start.8 = (bf16[32,512]{1,0:T(8,128)(2,1)S(1)}, bf16[32,512]{1,0:T(8,128)(2,1)S(1)}, u32[]{:S(2)}, u32[]{:S(2)}) collective-permute-start(bf16[32,512]{1,0:T(8,128)(2,1)S(1)} %get-tuple-element.60), channel_id=1, source_target_pairs={{0,16},{4,20},{8,24},{12,28},{16,0},{20,4},{24,8},{28,12},{1,17},{... | collective-permute-start | bytes 98312 | tf_op jit(solution)/shard_map/ppermute | solution.py:349
  32.5 6.3 %collective-permute-start.9 = (bf16[32,512]{1,0:T(8,128)(2,1)S(1)}, bf16[32,512]{1,0:T(8,128)(2,1)S(1)}, u32[]{:S(2)}, u32[]{:S(2)}) collective-permute-start(bf16[32,512]{1,0:T(8,128)(2,1)S(1)} %get-tuple-element.61), channel_id=1, source_target_pairs={{0,24},{4,28},{8,0},{12,4},{16,8},{20,12},{24,16},{28,20},{1,25},{... | collective-permute-start | bytes 98312 | tf_op jit(solution)/shard_map/ppermute | solution.py:349

commit v5 on v4

v5 whole, which is shorter than its diff:
```python
import functools

import jax
import jax.numpy as jnp
import numpy as np
from jax import lax
from jax.experimental import pallas as pl
from jax.experimental.pallas import tpu as pltpu
from jax.sharding import PartitionSpec as P

SUB_PIX = 16
SPOT_PIX = 32
WIND_MAX = 8
LANES = 128
STRIP = 32

HBM_SPEC = pl.BlockSpec(memory_space=pltpu.HBM)
VMEM_SPEC = pl.BlockSpec(memory_space=pltpu.VMEM)


def params(*arrays):
    held = sum(array.size * array.dtype.itemsize for array in jax.tree.leaves(arrays))
    return pltpu.CompilerParams(vmem_limit_bytes=held + 8 * 1024 * 1024)


def call(kernel, out_shape, operands, flops, name, in_hbm=(), scratch=()):
    def spec(k, array):
        return HBM_SPEC if array.dtype == jnp.int32 or k in in_hbm else VMEM_SPEC

    out_specs = jax.tree.map(lambda _: VMEM_SPEC, out_shape)
    size = sum(array.size * array.dtype.itemsize for array in jax.tree.leaves((operands, out_shape)))
    in_specs = [spec(k, array) for k, array in enumerate(operands)]
    operands = [
        pltpu.with_memory_space_constraint(array, pltpu.HBM) if space is HBM_SPEC else array
        for array, space in zip(operands, in_specs)
    ]
    return pl.pallas_call(
        kernel,
        out_shape=out_shape,
        in_specs=in_specs,
        out_specs=out_specs,
        scratch_shapes=list(scratch),
        compiler_params=params(operands, out_shape),
        cost_estimate=pl.CostEstimate(flops=flops, bytes_accessed=size, transcendentals=0),
        name=name,
    )(*operands)


def fetch(*pairs):
    copies = [pltpu.make_async_copy(source, target, sem) for source, target, sem in pairs]
    for copy in copies:
        copy.start()
    return copies


def wrap(value, length):
    value = jnp.where(value < 0, value + length, value)
    return jnp.where(value >= length, value - length, value)


def spans(pixel, anchor, num, den, length):
    stretched = (pixel * num).astype(jnp.float32)
    den = jnp.full(pixel.shape, den, jnp.int32).astype(jnp.float32)
    whole = jnp.floor((stretched + 0.5) / den)
    fraction = (stretched - whole * den) / den
    base = wrap(anchor + whole.astype(jnp.int32), length)
    upper = wrap(base + 1, length)
    return base, upper, 1.0 - fraction, fraction


def weights_kernel(n_layer, wind_hbm, offsets_hbm, ratio_hbm, own_hbm, rows_out, mine_out, other_out, own, *scratch):
    wind, offsets, ratio, sems = scratch
    loads = fetch(
        (wind_hbm, wind, sems.at[0]),
        (offsets_hbm, offsets, sems.at[1]),
        (ratio_hbm, ratio, sems.at[2]),
        (own_hbm, own, sems.at[3]),
    )
    for load in loads[:3]:
        load.wait()
    layers, rows_dev, cols_dev = own.shape
    half = rows_out.shape[1]
    screen_rows = 4 * rows_dev
    pupil_cols = mine_out.shape[2]
    screen_cols = cols_dev * n_layer
    direction = lax.axis_index("dir")
    column = lax.axis_index("layer")
    pairs = n_layer // 2
    block = half // pairs
    row = lax.broadcasted_iota(jnp.int32, (half, LANES), 0)
    pair = row // block + column // 2
    pair = jnp.where(pair >= pairs, pair - pairs, pair)
    pixel_rows = lax.rem(row, block) + (2 * pair + lax.rem(column, 2)) * block
    lane = lax.broadcasted_iota(jnp.int32, (half, LANES), 1)
    for level in range(layers):
        num = ratio[level, 0, direction]
        den = ratio[level, 1, direction]
        anchor = wrap(offsets[level, 0, direction] - wind[0, level], screen_rows)
        base, upper, low, high = spans(pixel_rows, anchor, num, den, screen_rows)
        for peer in range(4):
            for part in range(rows_dev // LANES):
                index = lane + (jnp.bitwise_xor(direction, peer) * rows_dev + part * LANES)
                weight = jnp.where(index == base, low, 0.0)
                weight = jnp.where(index == upper, high, weight)
                start = peer * rows_dev + part * LANES
                rows_out[level, :, start : start + LANES] = weight.astype(jnp.bfloat16)

        anchor = wrap(offsets[level, 1, direction] - wind[1, level], screen_cols)
        sub = lax.broadcasted_iota(jnp.int32, (cols_dev, LANES), 0).reshape(cols_dev // 8, 8, LANES)

        def tile(step, carry):
            start = pl.multiple_of(step * LANES, LANES)
            pixel = lax.broadcasted_iota(jnp.int32, (8, LANES), 1) + start
            base, upper, low, high = spans(pixel, anchor, num, den, screen_cols)
            for out, first in ((mine_out, column), (other_out, jnp.bitwise_xor(column, 1))):
                shift = first * cols_dev
                weight = jnp.where(sub == (base - shift)[None], low[None], 0.0)
                weight = jnp.where(sub == (upper - shift)[None], high[None], weight)
                out[level, :, pl.ds(start, LANES)] = weight.reshape(cols_dev, LANES).astype(jnp.bfloat16)
            return carry

        lax.fori_loop(0, pupil_cols // LANES, tile, 0)
    loads[3].wait()


def optics_kernel(amplitude, ones, columns, lines, amp_out, high_out, low_out, lines_out):
    rows, pupil_cols = amplitude.shape
    for step in range(pupil_cols // LANES):
        cut = slice(step * LANES, (step + 1) * LANES)
        amp = amplitude[:, cut]
        energy = (amp * amp).reshape(rows // SUB_PIX, SUB_PIX, LANES).sum(axis=1)
        energy = jnp.broadcast_to(energy[:, None], (rows // SUB_PIX, SUB_PIX, LANES)).reshape(rows, LANES)
        total = jnp.dot(energy, ones[...], precision=lax.Precision.HIGHEST, preferred_element_type=jnp.float32)
        amp_out[:, cut] = amp * lax.rsqrt(total)
    high_out[...], low_out[...] = split(columns[...])
    high, low = split(lines[...])
    lines_out[...] = jnp.concatenate([high, high, low], axis=1)


def stack(*blocks):
    return jnp.concatenate(blocks, axis=0)


def dot(left, right):
    return jnp.dot(left, right, preferred_element_type=jnp.float32)


def middle_kernel(rows_ref, cols_ref, own, near, across, far, beside, beside_near, phase, partial):
    layers, rows, _ = own.shape
    projected = []
    for level in range(layers):
        screen = stack(own[level], near[level], across[level], far[level])
        projected.append(dot(rows_ref[level], screen).astype(jnp.bfloat16))
        screen = stack(beside[level], beside_near[level])
        partial[level] = dot(rows_ref[level, :, : 2 * rows], screen)
    projected = jnp.concatenate(projected, axis=1)
    for at in range(0, phase.shape[1], 256):
        cols = cols_ref[:, :, at : at + 256].reshape(projected.shape[1], 256)
        phase[:, at : at + 256] = dot(projected, cols)


def shifted_rows(shift, own, near, far, start, stop):
    odd = lax.rem(lax.axis_index("dir"), 2) == 1
    own, near, far = [block[:, start:stop].astype(jnp.float32) for block in (own, near, far)]
    rows = own.shape[0]
    near_last, near_first = near[rows - 16 :], near[:16]
    far_last, far_first = far[rows - 16 :], far[:16]
    before = jnp.where(odd, near_last, far_last)
    after = jnp.where(odd, far_first, near_first)
    wide = jnp.concatenate([before, own, after], axis=0)
    shift = jnp.where(shift < 0, shift + rows + 32, shift)
    return pltpu.roll(wide, shift, 0)[16 : 16 + rows]


def edge_strips(wind, own, near, far):
    layers, rows, width = own.shape
    lane = lax.broadcasted_iota(jnp.int32, (rows, LANES), 1)
    strips = jnp.zeros((rows, LANES), jnp.float32)
    for level in range(layers):
        blocks = wind[0, level], own[level], near[level], far[level]
        at = WIND_MAX * level
        last = pltpu.roll(shifted_rows(*blocks, width - LANES, width), WIND_MAX + at, 1)
        strips = jnp.where((lane >= at) & (lane < at + WIND_MAX), last, strips)
        at = STRIP + WIND_MAX * level
        initial = pltpu.roll(shifted_rows(*blocks, 0, LANES), at, 1)
        strips = jnp.where((lane >= at) & (lane < at + WIND_MAX), initial, strips)
    return strips


def last_kernel(wind_hbm, rows_ref, cols_ref, phase, partial, beside, beside_near, cross0, cross1, far0, far1, *refs):
    outs, (strips_out, wind, sem) = refs[:-3], refs[-3:]
    load = fetch((wind_hbm, wind, sem))[0]
    layers, _, width = partial.shape
    rows = beside.shape[1]
    projected = []
    for level in range(layers):
        screen = stack(cross0[level], cross1[level], far0[level], far1[level])
        part = partial[level] + dot(rows_ref[level, :, 2 * rows :], screen)
        projected.append(part.astype(jnp.bfloat16))
    projected = jnp.concatenate(projected, axis=1)
    size, pupil_cols = outs[0].shape
    for at in range(0, pupil_cols, 256):
        cols = cols_ref[:, :, at : at + 256].reshape(projected.shape[1], 256)
        total = (phase[:, at : at + 256] + dot(projected, cols)).astype(jnp.bfloat16)
        for k, out in enumerate(outs):
            out[:, at : at + 256] = total[k * size : (k + 1) * size]
    load.wait()
    far = [stack(far0[level], far1[level]) for level in range(layers)]
    strips = edge_strips(wind, beside, beside_near, far)
    strips_out[...] = strips
    strips = strips.T.astype(jnp.bfloat16)
    outs[1][:, pupil_cols:] = strips[:STRIP]
    outs[-1][:, pupil_cols:] = strips[STRIP : 2 * STRIP]


def shift_kernel(wind_hbm, own, near, far, partner, below, above, out, wind, sem):
    load = fetch((wind_hbm, wind, sem))[0]
    layers, rows, cols = own.shape
    second = lax.rem(lax.axis_index("layer"), 2) == 1
    at = below.shape[1] - rows
    others = stack(below[:, at:], above[:, at:], jnp.zeros((LANES - 2 * STRIP, rows), jnp.bfloat16))
    others = others.astype(jnp.float32).T
    lane = lax.broadcasted_iota(jnp.int32, (rows, LANES), 1)
    strips = jnp.where((lane < STRIP) == second, partner[...], others)
    load.wait()
    for level in range(layers):
        last = pltpu.roll(strips, LANES - WIND_MAX * (level + 1), 1)
        first = pltpu.roll(strips, LANES - STRIP - WIND_MAX * level, 1)
        extra = jnp.where(lane < WIND_MAX, first, last)
        moved = shifted_rows(wind[0, level], own[level], near[level], far[level], 0, cols)
        shift = wind[1, level]
        shift = jnp.where(shift < 0, shift + cols + LANES, shift)
        wide = pltpu.roll(jnp.concatenate([moved, extra], axis=1), shift, 1)
        out[level] = wide[:, :cols].astype(jnp.bfloat16)


def sin_cos(phase):
    turns = jnp.floor(phase * (1.0 / np.pi) + 0.5)
    rest = phase - turns * 3.140625
    rest = rest - turns * 9.67653589793e-4
    odd = turns - 2.0 * jnp.floor(turns * 0.5)
    sign = 1.0 - 2.0 * odd
    square = rest * rest
    sine = -1.0 / 39916800.0
    for term in (1.0 / 362880.0, -1.0 / 5040.0, 1.0 / 120.0, -1.0 / 6.0, 1.0):
        sine = sine * square + term
    cosine = 1.0 / 479001600.0
    for term in (-1.0 / 3628800.0, 1.0 / 40320.0, -1.0 / 720.0, 1.0 / 24.0, -0.5, 1.0):
        cosine = cosine * square + term
    return sine * rest * sign, cosine * sign


def split(value):
    high = value.astype(jnp.bfloat16)
    low = (value - high.astype(jnp.float32)).astype(jnp.bfloat16)
    return high, low


def imaging_kernel(count, *refs):
    parts = refs[:count]
    amp_ref, cols_high, cols_low, rows_table, out = refs[count:]
    rows, cols = amp_ref.shape
    tiles = cols // LANES
    phase = parts[0][:, :cols].astype(jnp.float32)
    for part in parts[1:]:
        phase = phase + part[:, :cols].astype(jnp.float32)
    sine, cosine = sin_cos(phase)
    amp = amp_ref[...]
    real, imag = amp * cosine, amp * sine
    field = jnp.concatenate(
        [
            jnp.concatenate(
                [real[:, t * LANES : (t + 1) * LANES], imag[:, t * LANES : (t + 1) * LANES]], axis=1
            )
            for t in range(tiles)
        ],
        axis=0,
    )
    high, low = split(field)
    half = dot(high, cols_high[...]) + (dot(low, cols_high[...]) + dot(high, cols_low[...]))
    wide = 2 * LANES
    out_rows = 2 * rows
    for t in range(tiles):
        mine = half[t * rows : (t + 1) * rows]
        mine = jnp.concatenate([mine[:, :wide], mine[:, wide:]], axis=0)
        high, low = split(mine)
        full = dot(rows_table[...], jnp.concatenate([high, low, high], axis=0))
        real, imag = full[:out_rows], full[out_rows:]
        out[:, t * wide : (t + 1) * wide] = real * real + imag * imag


def tables(rows):
    freq = np.arange(SPOT_PIX)[:, None] - SPOT_PIX // 2
    angle = ((freq * np.arange(SUB_PIX)[None, :]) % SPOT_PIX) * (2.0 * np.pi / SPOT_PIX)
    cos, sin = np.cos(angle), np.sin(angle)

    def blocks(table, count):
        return np.kron(np.eye(count), table)

    per_tile = LANES // SUB_PIX
    col_cos, col_sin = blocks(cos.T, per_tile), blocks(sin.T, per_tile)
    columns = np.block([[col_cos, -col_sin], [col_sin, col_cos]])
    count = rows // SUB_PIX
    row_cos, row_sin = blocks(cos, count), blocks(sin, count)
    lines = np.block([[row_cos, row_sin], [-row_sin, row_cos]])

    return columns.astype(np.float32), lines.astype(np.float32)


def per_device(screens, amplitude, wind, offsets, ratio):
    layers, rows_dev, cols_dev = screens.shape
    n_layer = lax.axis_size("layer")
    n_dir = lax.axis_size("dir")
    assert n_dir == 4
    rows, pupil_cols = amplitude.shape
    pairs = n_layer // 2
    half = pairs * rows
    assert rows == STRIP and pairs > 2
    bf16, f32 = jnp.bfloat16, jnp.float32
    wind = jnp.transpose(wind, (1, 0))
    offsets = jnp.transpose(offsets, (1, 2, 0))
    ratio = jnp.transpose(ratio, (1, 2, 0))
    smem, sem = pltpu.SMEM, pltpu.SemaphoreType.DMA

    def shape(*dims, dtype=bf16):
        return jax.ShapeDtypeStruct(dims, dtype)

    def swap(value, bit):
        return lax.ppermute(value, "dir", [(i, i ^ bit) for i in range(n_dir)])

    def partner(value):
        return lax.ppermute(value, "layer", [(i, i ^ 1) for i in range(n_layer)])

    def turn(value, step):
        return lax.ppermute(value, "layer", [(i, (i + step) % n_layer) for i in range(n_layer)])

    across = swap(screens, 2)
    beside = partner(screens)
    near = swap(screens, 1)
    row_weights, mine, other, own = call(
        functools.partial(weights_kernel, n_layer),
        (
            shape(layers, half, 4 * rows_dev),
            shape(layers, cols_dev, pupil_cols),
            shape(layers, cols_dev, pupil_cols),
            shape(layers, rows_dev, cols_dev),
        ),
        (wind, offsets, ratio, screens),
        100_000_000,
        "weights",
        in_hbm=(3,),
        scratch=[smem(array.shape, jnp.int32) for array in (wind, offsets, ratio)] + [sem((4,))],
    )
    across, beside, near, row_weights, mine, other, own = lax.optimization_barrier(
        (across, beside, near, row_weights, mine, other, own)
    )
    cut = rows_dev // 2
    upper, lower, across, beside = lax.optimization_barrier((beside[:, :cut], across[:, cut:], across, beside))
    cross0 = swap(upper, 2)
    cross1 = partner(lower)
    far = swap(across, 1)
    beside_near = swap(beside, 1)
    phase, partial = call(
        middle_kernel,
        (shape(half, pupil_cols, dtype=f32), shape(layers, half, cols_dev, dtype=f32)),
        (row_weights, mine, own, near, across, far, beside, beside_near),
        700_000_000,
        "middle",
    )

    ones = np.kron(np.eye(LANES // SUB_PIX), np.ones((SUB_PIX, SUB_PIX))).astype(np.float32)
    columns, lines = tables(rows)
    amplitude, far = lax.optimization_barrier((amplitude, far))
    optics = call(
        optics_kernel,
        (
            shape(rows, pupil_cols, dtype=f32),
            shape(*columns.shape),
            shape(*columns.shape),
            shape(lines.shape[0], 3 * lines.shape[1]),
        ),
        (amplitude, jnp.asarray(ones), jnp.asarray(columns), jnp.asarray(lines)),
        30_000_000,
        "optics",
    )
    cross0, cross1, phase, partial, *optics = lax.optimization_barrier((cross0, cross1, phase, partial, *optics))
    far0 = swap(cross0, 1)
    far1 = swap(cross1, 1)

    wind_scratch = [smem(wind.shape, jnp.int32), sem]
    extra = [rows_dev if k in (1, pairs - 1) else 0 for k in range(pairs)]
    *sums, strips = call(
        last_kernel,
        [shape(rows, pupil_cols + more) for more in extra] + [shape(rows_dev, LANES, dtype=f32)],
        (wind, row_weights, other, phase, partial, beside, beside_near, cross0, cross1, far0, far1),
        700_000_000,
        "last",
        scratch=wind_scratch,
    )
    received = [sums[0]] + [turn(sums[k], 2 * k) for k in range(1, pairs)]
    new_screens = call(
        shift_kernel,
        shape(layers, rows_dev, cols_dev),
        (wind, own, near, far, strips, received[1], received[pairs - 1]),
        1_000_000,
        "shift",
        scratch=wind_scratch,
    )
    spots = call(
        functools.partial(imaging_kernel, pairs),
        shape(2 * rows, 2 * pupil_cols, dtype=f32),
        (*received, *optics),
        400_000_000,
        "imaging",
    )
    return (new_screens, spots[None])


def solution(mesh):
    return jax.shard_map(
        per_device,
        mesh=mesh,
        in_specs=(P(None, "dir", "layer"), P("layer", None), P(), P(), P()),
        out_specs=(P(None, "dir", "layer"), P("dir", "layer", None)),
        check_vma=False,
    )
```

time: 40.2 us -> 40.2 us (level)
  local copies, waits for them, and re-layouts: 0.03 us -> 3.66 us
  starting transfers between devices: 15.1 us -> 12.3 us
  waiting for transfers between devices: 12.9 us -> 11.5 us
  Pallas kernels: 11.3 us -> 11.8 us
    ppermute x6 -> x3, waiting for transfers between devices: 0.02 us -> 5.44 us  [turn(): lax.ppermute(value, 'layer', [(i, (i + step) % n_layer) for i in range(n_...]
    ppermute x6 -> x3, starting transfers between devices: 9.89 us -> 4.67 us  [turn(): lax.ppermute(value, 'layer', [(i, (i + step) % n_layer) for i in range(n_...]
    ppermute x3 -> x7, waiting for transfers between devices: 7.78 us -> 2.68 us  [swap(): return lax.ppermute(value, 'dir', [(i, i ^ bit) for i in range(n_dir)])]
    unnamed x8, local copies, waits for them, and re-layouts: 0.03 us -> 3.64 us
    pallas_call x7 -> x6, Pallas kernels: 8.59 us -> 11.8 us  [call(): pl.pallas_call(kernel, out_shape=out_shape, in_specs=in_specs, out_specs=...]
    pallas_call x2 -> x0, Pallas kernels: 2.66 us -> none  [image(): pl.pallas_call(functools.partial(imaging_kernel, pairs, start), out_shape...]
    ppermute x2, waiting for transfers between devices: 5.08 us -> 3.36 us  [partner(): return lax.ppermute(value, 'layer', [(i, i ^ 1) for i in range(n_layer)])]
    ppermute x2, starting transfers between devices: 2.16 us -> 3.54 us  [partner(): return lax.ppermute(value, 'layer', [(i, i ^ 1) for i in range(n_layer)])]
  transfers between devices with their start and end apart: 11 -> 12, of which waited for: 3 -> 8; matrix products, arithmetic and copies ran while one was open for 0% -> 0% of each run, Pallas kernels for 21% -> 22%
where the time goes in v5:
time: 40.2 us; the launch traced here: 39.9 us
  starting transfers between devices  12.3 us (31%)
  Pallas kernels  11.8 us (29%)
  waiting for transfers between devices  11.5 us (29%)
  local copies, waits for them, and re-layouts  3.66 us (9%)
  between operations  0.72 us (2%)
    pallas_call x6, Pallas kernels, call(): pl.pallas_call(kernel, out_shape=out_shape, in_specs=in_specs, out_specs=...  11.8 us
    ppermute x3, waiting for transfers between devices, turn(): lax.ppermute(value, 'layer', [(i, (i + step) % n_layer) for i in range(n_...  5.44 us
    ppermute x3, starting transfers between devices, turn(): lax.ppermute(value, 'layer', [(i, (i + step) % n_layer) for i in range(n_...  4.67 us
    ppermute x7, starting transfers between devices, swap(): return lax.ppermute(value, 'dir', [(i, i ^ bit) for i in range(n_dir)])  4.06 us
    unnamed x8, local copies, waits for them, and re-layouts  3.64 us
    ppermute x2, starting transfers between devices, partner(): return lax.ppermute(value, 'layer', [(i, i ^ 1) for i in range(n_layer)])  3.54 us
    ppermute x2, waiting for transfers between devices, partner(): return lax.ppermute(value, 'layer', [(i, i ^ 1) for i in range(n_layer)])  3.36 us
    ppermute x7, waiting for transfers between devices, swap(): return lax.ppermute(value, 'dir', [(i, i ^ bit) for i in range(n_dir)])  2.68 us
  transfers between devices with their start and end apart: 12, of which 8 were waited for; matrix products, arithmetic and copies ran while one was open for 0% of the time, Pallas kernels for 22%

profile of v5, /device:TPU:0, one launch (start us, length us, event | category | flops | bytes accessed | tf_op | source)
XLA Modules:
  0.0 39.9 jit_solution(17934761043503533168)
XLA Ops:
  0.6 3.0 %collective-permute-start.1 = (bf16[3,128,512]{2,1,0:T(8,128)(2,1)}, bf16[3,128,512]{2,1,0:T(8,128)(2,1)S(1)}, u32[]{:S(2)}, u32[]{:S(2)}) collective-permute-start(bf16[3,128,512]{2,1,0:T(8,128)(2,1)} %own_hbm.1), channel_id=1, source_target_pairs={{0,4},{4,0},{8,12},{12,8},{16,20},{20,16},{24,28},{28,24},{1,5},{5... | collective-permute-start | bytes 1179656 | tf_op jit(solution)/shard_map/ppermute | solution.py:332
  3.7 1.5 %collective-permute-start = (bf16[3,128,512]{2,1,0:T(8,128)(2,1)}, bf16[3,128,512]{2,1,0:T(8,128)(2,1)S(1)}, u32[]{:S(2)}, u32[]{:S(2)}) collective-permute-start(bf16[3,128,512]{2,1,0:T(8,128)(2,1)} %own_hbm.1), channel_id=1, source_target_pairs={{0,2},{1,3},{2,0},{3,1},{4,6},{5,7},{6,4},{7,5},{8,10},{9,11},{10,... | collective-permute-start | bytes 1179656 | tf_op jit(solution)/shard_map/ppermute | solution.py:329
  5.2 0.0 collective-permute-start.2
  5.2 5.1 %weights.1 = (bf16[3,128,512]{2,1,0:T(8,128)(2,1)S(1)}, bf16[3,512,1280]{2,1,0:T(8,128)(2,1)S(1)}, bf16[3,512,1280]{2,1,0:T(8,128)(2,1)S(1)}, bf16[3,128,512]{2,1,0:T(8,128)(2,1)S(1)}) custom-call(s32[2,3]{1,0:T(2,128)} %bitcast.5, s32[3,2,4]{2,1,0:T(2,128)} %bitcast.8, s32[3,2,4]{2,1,0:T(2,128)} %bitcast.9, bf16[3,128,512]{2,1,0:T(8,128)(2,1)} %own_hbm.1), custom_call_target="tpu_custom_call" | custom-call | flops 100000000 | bytes 9044184 | tf_op jit(solution)/shard_map/weights/pallas_call | solution.py:37
  10.3 2.7 %collective-permute-done.1.beside = bf16[3,128,512]{2,1,0:T(8,128)(2,1)S(1)} collective-permute-done((bf16[3,128,512]{2,1,0:T(8,128)(2,1)}, bf16[3,128,512]{2,1,0:T(8,128)(2,1)S(1)}, u32[]{:S(2)}, u32[]{:S(2)}) %collective-permute-start.1) | collective-permute-done | bytes 393248 | tf_op jit(solution)/shard_map/ppermute | solution.py:332
  13.0 1.5 %collective-permute-done.across = bf16[3,128,512]{2,1,0:T(8,128)(2,1)S(1)} collective-permute-done((bf16[3,128,512]{2,1,0:T(8,128)(2,1)}, bf16[3,128,512]{2,1,0:T(8,128)(2,1)S(1)}, u32[]{:S(2)}, u32[]{:S(2)}) %collective-permute-start) | collective-permute-done | bytes 393248 | tf_op jit(solution)/shard_map/ppermute | solution.py:329
  14.4 0.0 collective-permute-done.2.near
  14.5 0.1 collective-permute-start.3
  14.6 0.5 %collective-permute-start.6 = (bf16[3,128,512]{2,1,0:T(8,128)(2,1)S(1)}, bf16[3,128,512]{2,1,0:T(8,128)(2,1)S(1)}, u32[]{:S(2)}, u32[]{:S(2)}) collective-permute-start(bf16[3,128,512]{2,1,0:T(8,128)(2,1)S(1)} %collective-permute-done.1.beside), channel_id=1, source_target_pairs={{0,1},{1,0},{2,3},{3,2},{4,5},{5,4},{6,7},{7,6},{8,9},{9,8},{10,11... | collective-permute-start | bytes 1179656 | tf_op jit(solution)/shard_map/ppermute | solution.py:329
  15.1 1.5 %collective-permute-start.4 = (bf16[3,64,512]{2,1,0:T(8,128)(2,1)S(1)}, bf16[3,64,512]{2,1,0:T(8,128)(2,1)S(1)}, u32[]{:S(2)}, u32[]{:S(2)}) collective-permute-start(bf16[3,64,512]{2,1,0:T(8,128)(2,1)S(1)} %slice.6), channel_id=1, source_target_pairs={{0,2},{1,3},{2,0},{3,1},{4,6},{5,7},{6,4},{7,5},{8,10},{9,11},{10,... | collective-permute-start | bytes 589832 | tf_op jit(solution)/shard_map/ppermute | solution.py:329
  16.6 0.5 %collective-permute-start.5 = (bf16[3,64,512]{2,1,0:T(8,128)(2,1)S(1)}, bf16[3,64,512]{2,1,0:T(8,128)(2,1)S(1)}, u32[]{:S(2)}, u32[]{:S(2)}) collective-permute-start(bf16[3,64,512]{2,1,0:T(8,128)(2,1)S(1)} %slice.7), channel_id=1, source_target_pairs={{0,4},{4,0},{8,12},{12,8},{16,20},{20,16},{24,28},{28,24},{1,5},{5... | collective-permute-start | bytes 589832 | tf_op jit(solution)/shard_map/ppermute | solution.py:332
  17.1 0.0 collective-permute-done.3.far
  17.1 1.0 %copy-done = f32[256,512]{1,0:T(8,128)S(1)} copy-done((f32[256,512]{1,0:T(8,128)S(1)}, f32[256,512]{1,0:T(8,128)}, u32[]{:S(2)}) %copy-start) | copy-done | bytes 524312
  18.1 0.9 %copy-done.1 = f32[32,1280]{1,0:T(8,128)S(1)} copy-done((f32[32,1280]{1,0:T(8,128)S(1)}, f32[32,1280]{1,0:T(8,128)}, u32[]{:S(2)}) %copy-start.1) | copy-done | bytes 163864
  19.0 0.8 %copy-done.2 = f32[128,64]{1,0:T(8,128)S(1)} copy-done((f32[128,64]{1,0:T(8,128)S(1)}, f32[128,64]{1,0:T(8,128)}, u32[]{:S(2)}) %copy-start.2) | copy-done | bytes 32792
  19.9 0.8 %copy-done.3 = f32[128,128]{1,0:T(8,128)S(1)} copy-done((f32[128,128]{1,0:T(8,128)S(1)}, f32[128,128]{1,0:T(8,128)}, u32[]{:S(2)}) %copy-start.3) | copy-done | bytes 65560
  20.7 0.7 %optics.1 = (f32[32,1280]{1,0:T(8,128)S(1)}, bf16[256,512]{1,0:T(8,128)(2,1)S(1)}, bf16[256,512]{1,0:T(8,128)(2,1)S(1)}, bf16[128,192]{1,0:T(8,128)(2,1)S(1)}) custom-call(f32[32,1280]{1,0:T(8,128)S(1)} %copy-done.1, f32[128,128]{1,0:T(8,128)S(1)} %copy-done.3, f32[256,512]{1,0:T(8,128)S(1)} %copy-done, f32[128,64]{1,0:T(8,128)S(1)} %copy-done.2), custom_call_target="tpu_custom_call" | custom-call | flops 30000000 | bytes 1523712 | tf_op jit(solution)/shard_map/optics/pallas_call | solution.py:37
  21.4 0.0 collective-permute-done.6.beside_near
  21.4 1.1 %middle.1 = (f32[128,1280]{1,0:T(8,128)S(1)}, f32[3,128,512]{2,1,0:T(8,128)S(1)}) custom-call(bf16[3,128,512]{2,1,0:T(8,128)(2,1)S(1)} %get-tuple-element.48.rows_ref, bf16[3,512,1280]{2,1,0:T(8,128)(2,1)S(1)} %get-tuple-element.52.cols_ref, bf16[3,128,512]{2,1,0:T(8,128)(2,1)S(1)} %get-tuple-element.42.own, ...), custom_call_target="tpu_custom_call" | custom-call | flops 700000000 | bytes 8126464 | tf_op jit(solution)/shard_map/middle/pallas_call | solution.py:37
  22.5 0.7 %collective-permute-done.5.cross1 = bf16[3,64,512]{2,1,0:T(8,128)(2,1)S(1)} collective-permute-done((bf16[3,64,512]{2,1,0:T(8,128)(2,1)S(1)}, bf16[3,64,512]{2,1,0:T(8,128)(2,1)S(1)}, u32[]{:S(2)}, u32[]{:S(2)}) %collective-permute-start.5) | collective-permute-done | bytes 196640 | tf_op jit(solution)/shard_map/ppermute | solution.py:332
  23.2 0.5 %collective-permute-start.8 = (bf16[3,64,512]{2,1,0:T(8,128)(2,1)S(1)}, bf16[3,64,512]{2,1,0:T(8,128)(2,1)S(1)}, u32[]{:S(2)}, u32[]{:S(2)}) collective-permute-start(bf16[3,64,512]{2,1,0:T(8,128)(2,1)S(1)} %collective-permute-done.5.cross1), channel_id=1, source_target_pairs={{0,1},{1,0},{2,3},{3,2},{4,5},{5,4},{6,7},{7,6},{8,9},{9,8},{10,11... | collective-permute-start | bytes 589832 | tf_op jit(solution)/shard_map/ppermute | solution.py:329
  23.7 0.9 %collective-permute-done.7.far0 = bf16[3,64,512]{2,1,0:T(8,128)(2,1)S(1)} collective-permute-done((bf16[3,64,512]{2,1,0:T(8,128)(2,1)S(1)}, bf16[3,64,512]{2,1,0:T(8,128)(2,1)S(1)}, u32[]{:S(2)}, u32[]{:S(2)}) %collective-permute-start.7) | collective-permute-done | bytes 196640 | tf_op jit(solution)/shard_map/ppermute | solution.py:329
  24.6 0.3 collective-permute-done.8.far1
  24.9 1.2 %last.1 = (bf16[32,1280]{1,0:T(8,128)(2,1)S(1)}, bf16[32,1408]{1,0:T(8,128)(2,1)S(1)}, bf16[32,1280]{1,0:T(8,128)(2,1)S(1)}, bf16[32,1408]{1,0:T(8,128)(2,1)S(1)}, f32[128,128]{1,0:T(8,128)S(1)}) custom-call(s32[2,3]{1,0:T(2,128)} %bitcast.6, bf16[3,128,512]{2,1,0:T(8,128)(2,1)S(1)} %get-tuple-element.48.rows_ref, ...), custom_call_target="tpu_custom_call" | custom-call | flops 700000000 | bytes 7749656 | tf_op jit(solution)/shard_map/last/pallas_call | solution.py:37
  26.1 1.6 %collective-permute-start.9 = (bf16[32,1408]{1,0:T(8,128)(2,1)S(1)}, bf16[32,1408]{1,0:T(8,128)(2,1)S(1)}, u32[]{:S(2)}, u32[]{:S(2)}) collective-permute-start(bf16[32,1408]{1,0:T(8,128)(2,1)S(1)} %get-tuple-element.66), channel_id=1, source_target_pairs={{0,8},{4,12},{8,16},{12,20},{16,24},{20,28},{24,0},{28,4},{1,9},{5... | collective-permute-start | bytes 270344 | tf_op jit(solution)/shard_map/ppermute | solution.py:335
  27.7 2.2 %collective-permute-start.10 = (bf16[32,1408]{1,0:T(8,128)(2,1)S(1)}, bf16[32,1408]{1,0:T(8,128)(2,1)S(1)}, u32[]{:S(2)}, u32[]{:S(2)}) collective-permute-start(bf16[32,1408]{1,0:T(8,128)(2,1)S(1)} %get-tuple-element.67), channel_id=1, source_target_pairs={{0,24},{4,28},{8,0},{12,4},{16,8},{20,12},{24,16},{28,20},{1,25},{... | collective-permute-start | bytes 270344 | tf_op jit(solution)/shard_map/ppermute | solution.py:335
  30.0 0.8 %collective-permute-start.11 = (bf16[32,1280]{1,0:T(8,128)(2,1)S(1)}, bf16[32,1280]{1,0:T(8,128)(2,1)S(1)}, u32[]{:S(2)}, u32[]{:S(2)}) collective-permute-start(bf16[32,1280]{1,0:T(8,128)(2,1)S(1)} %get-tuple-element.69), channel_id=1, source_target_pairs={{0,16},{4,20},{8,24},{12,28},{16,0},{20,4},{24,8},{28,12},{1,17},{... | collective-permute-start | bytes 245768 | tf_op jit(solution)/shard_map/ppermute | solution.py:335
  30.8 2.5 %collective-permute-done.9.below.refs_1_ = bf16[32,1408]{1,0:T(8,128)(2,1)S(1)} collective-permute-done((bf16[32,1408]{1,0:T(8,128)(2,1)S(1)}, bf16[32,1408]{1,0:T(8,128)(2,1)S(1)}, u32[]{:S(2)}, u32[]{:S(2)}) %collective-permute-start.9) | collective-permute-done | bytes 90144 | tf_op jit(solution)/shard_map/ppermute | solution.py:335
  33.3 0.9 %collective-permute-done.10.above.refs_3_ = bf16[32,1408]{1,0:T(8,128)(2,1)S(1)} collective-permute-done((bf16[32,1408]{1,0:T(8,128)(2,1)S(1)}, bf16[32,1408]{1,0:T(8,128)(2,1)S(1)}, u32[]{:S(2)}, u32[]{:S(2)}) %collective-permute-start.10) | collective-permute-done | bytes 90144 | tf_op jit(solution)/shard_map/ppermute | solution.py:335
  34.1 2.0 %shift.1 = bf16[3,128,512]{2,1,0:T(8,128)(2,1)} custom-call(s32[2,3]{1,0:T(2,128)} %bitcast.7, bf16[3,128,512]{2,1,0:T(8,128)(2,1)S(1)} %get-tuple-element.42.own, bf16[3,128,512]{2,1,0:T(8,128)(2,1)S(1)} %collective-permute-done.2.near, bf16[3,128,512]{2,1,0:T(8,128)(2,1)S(1)} %collective-permute-done.3.far, f32[128,128]{1,0:T(8,128)S(1)} %get-tuple-element.65.partner, ...), custom_call_target="tpu_custom_call" | custom-call | flops 1000000 | bytes 1818648 | tf_op jit(solution)/shard_map/shift/pallas_call | solution.py:37
  36.1 2.1 %collective-permute-done.11.refs_2_ = bf16[32,1280]{1,0:T(8,128)(2,1)S(1)} collective-permute-done((bf16[32,1280]{1,0:T(8,128)(2,1)S(1)}, bf16[32,1280]{1,0:T(8,128)(2,1)S(1)}, u32[]{:S(2)}, u32[]{:S(2)}) %collective-permute-start.11) | collective-permute-done | bytes 81952 | tf_op jit(solution)/shard_map/ppermute | solution.py:335
  38.2 1.7 %imaging.1 = f32[64,2560]{1,0:T(8,128)} custom-call(bf16[32,1280]{1,0:T(8,128)(2,1)S(1)} %get-tuple-element.68.refs_0_, bf16[32,1408]{1,0:T(8,128)(2,1)S(1)} %collective-permute-done.9.below.refs_1_, bf16[32,1280]{1,0:T(8,128)(2,1)S(1)} %collective-permute-done.11.refs_2_, bf16[32,1408]{1,0:T(8,128)(2,1)S(1)} %collective-permute-done.10.above.refs_3_, ...), custom_call_target="tpu_custom_call" | custom-call | flops 400000000 | bytes 1736704 | tf_op jit(solution)/shard_map/imaging/pallas_call | solution.py:37
  (8 shorter events, 0.0 us)
Async XLA Ops:
  0.6 12.4 %collective-permute-start.1 = (bf16[3,128,512]{2,1,0:T(8,128)(2,1)}, bf16[3,128,512]{2,1,0:T(8,128)(2,1)S(1)}, u32[]{:S(2)}, u32[]{:S(2)}) collective-permute-start(bf16[3,128,512]{2,1,0:T(8,128)(2,1)} %own_hbm.1), channel_id=1, source_target_pairs={{0,4},{4,0},{8,12},{12,8},{16,20},{20,16},{24,28},{28,24},{1,5},{5... | collective-permute-start | bytes 1179656 | tf_op jit(solution)/shard_map/ppermute | solution.py:332
  3.7 10.8 %collective-permute-start = (bf16[3,128,512]{2,1,0:T(8,128)(2,1)}, bf16[3,128,512]{2,1,0:T(8,128)(2,1)S(1)}, u32[]{:S(2)}, u32[]{:S(2)}) collective-permute-start(bf16[3,128,512]{2,1,0:T(8,128)(2,1)} %own_hbm.1), channel_id=1, source_target_pairs={{0,2},{1,3},{2,0},{3,1},{4,6},{5,7},{6,4},{7,5},{8,10},{9,11},{10,... | collective-permute-start | bytes 1179656 | tf_op jit(solution)/shard_map/ppermute | solution.py:329
  5.2 9.3 %collective-permute-start.2 = (bf16[3,128,512]{2,1,0:T(8,128)(2,1)}, bf16[3,128,512]{2,1,0:T(8,128)(2,1)S(1)}, u32[]{:S(2)}, u32[]{:S(2)}) collective-permute-start(bf16[3,128,512]{2,1,0:T(8,128)(2,1)} %own_hbm.1), channel_id=1, source_target_pairs={{0,1},{1,0},{2,3},{3,2},{4,5},{5,4},{6,7},{7,6},{8,9},{9,8},{10,11... | collective-permute-start | bytes 1179656 | tf_op jit(solution)/shard_map/ppermute | solution.py:329
  14.5 2.6 %collective-permute-start.3 = (bf16[3,128,512]{2,1,0:T(8,128)(2,1)S(1)}, bf16[3,128,512]{2,1,0:T(8,128)(2,1)S(1)}, u32[]{:S(2)}, u32[]{:S(2)}) collective-permute-start(bf16[3,128,512]{2,1,0:T(8,128)(2,1)S(1)} %collective-permute-done.across), channel_id=1, source_target_pairs={{0,1},{1,0},{2,3},{3,2},{4,5},{5,4},{6,7},{7,6},{8,9},{9,8},{10,11... | collective-permute-start | bytes 1179656 | tf_op jit(solution)/shard_map/ppermute | solution.py:329
  14.6 6.8 %collective-permute-start.6 = (bf16[3,128,512]{2,1,0:T(8,128)(2,1)S(1)}, bf16[3,128,512]{2,1,0:T(8,128)(2,1)S(1)}, u32[]{:S(2)}, u32[]{:S(2)}) collective-permute-start(bf16[3,128,512]{2,1,0:T(8,128)(2,1)S(1)} %collective-permute-done.1.beside), channel_id=1, source_target_pairs={{0,1},{1,0},{2,3},{3,2},{4,5},{5,4},{6,7},{7,6},{8,9},{9,8},{10,11... | collective-permute-start | bytes 1179656 | tf_op jit(solution)/shard_map/ppermute | solution.py:329
  15.1 7.4 %collective-permute-start.4 = (bf16[3,64,512]{2,1,0:T(8,128)(2,1)S(1)}, bf16[3,64,512]{2,1,0:T(8,128)(2,1)S(1)}, u32[]{:S(2)}, u32[]{:S(2)}) collective-permute-start(bf16[3,64,512]{2,1,0:T(8,128)(2,1)S(1)} %slice.6), channel_id=1, source_target_pairs={{0,2},{1,3},{2,0},{3,1},{4,6},{5,7},{6,4},{7,5},{8,10},{9,11},{10,... | collective-permute-start | bytes 589832 | tf_op jit(solution)/shard_map/ppermute | solution.py:329
  16.6 6.6 %collective-permute-start.5 = (bf16[3,64,512]{2,1,0:T(8,128)(2,1)S(1)}, bf16[3,64,512]{2,1,0:T(8,128)(2,1)S(1)}, u32[]{:S(2)}, u32[]{:S(2)}) collective-permute-start(bf16[3,64,512]{2,1,0:T(8,128)(2,1)S(1)} %slice.7), channel_id=1, source_target_pairs={{0,4},{4,0},{8,12},{12,8},{16,20},{20,16},{24,28},{28,24},{1,5},{5... | collective-permute-start | bytes 589832 | tf_op jit(solution)/shard_map/ppermute | solution.py:332
  17.1 1.0 %copy-start = (f32[256,512]{1,0:T(8,128)S(1)}, f32[256,512]{1,0:T(8,128)}, u32[]{:S(2)}) copy-start(f32[256,512]{1,0:T(8,128)} %constant.7.clone.columns) | copy-start | bytes 1572868
  18.1 0.9 %copy-start.1 = (f32[32,1280]{1,0:T(8,128)S(1)}, f32[32,1280]{1,0:T(8,128)}, u32[]{:S(2)}) copy-start(f32[32,1280]{1,0:T(8,128)} %amplitude) | copy-start | bytes 491524
  19.0 0.8 %copy-start.2 = (f32[128,64]{1,0:T(8,128)S(1)}, f32[128,64]{1,0:T(8,128)}, u32[]{:S(2)}) copy-start(f32[128,64]{1,0:T(8,128)} %constant.8.clone.lines) | copy-start | bytes 98308
  19.9 0.8 %copy-start.3 = (f32[128,128]{1,0:T(8,128)S(1)}, f32[128,128]{1,0:T(8,128)}, u32[]{:S(2)}) copy-start(f32[128,128]{1,0:T(8,128)} %constant.6.clone.ones) | copy-start | bytes 196612
  23.2 1.4 %collective-permute-start.7 = (bf16[3,64,512]{2,1,0:T(8,128)(2,1)S(1)}, bf16[3,64,512]{2,1,0:T(8,128)(2,1)S(1)}, u32[]{:S(2)}, u32[]{:S(2)}) collective-permute-start(bf16[3,64,512]{2,1,0:T(8,128)(2,1)S(1)} %collective-permute-done.4.cross0), channel_id=1, source_target_pairs={{0,1},{1,0},{2,3},{3,2},{4,5},{5,4},{6,7},{7,6},{8,9},{9,8},{10,11... | collective-permute-start | bytes 589832 | tf_op jit(solution)/shard_map/ppermute | solution.py:329
  23.2 1.7 %collective-permute-start.8 = (bf16[3,64,512]{2,1,0:T(8,128)(2,1)S(1)}, bf16[3,64,512]{2,1,0:T(8,128)(2,1)S(1)}, u32[]{:S(2)}, u32[]{:S(2)}) collective-permute-start(bf16[3,64,512]{2,1,0:T(8,128)(2,1)S(1)} %collective-permute-done.5.cross1), channel_id=1, source_target_pairs={{0,1},{1,0},{2,3},{3,2},{4,5},{5,4},{6,7},{7,6},{8,9},{9,8},{10,11... | collective-permute-start | bytes 589832 | tf_op jit(solution)/shard_map/ppermute | solution.py:329
  26.1 7.2 %collective-permute-start.9 = (bf16[32,1408]{1,0:T(8,128)(2,1)S(1)}, bf16[32,1408]{1,0:T(8,128)(2,1)S(1)}, u32[]{:S(2)}, u32[]{:S(2)}) collective-permute-start(bf16[32,1408]{1,0:T(8,128)(2,1)S(1)} %get-tuple-element.66), channel_id=1, source_target_pairs={{0,8},{4,12},{8,16},{12,20},{16,24},{20,28},{24,0},{28,4},{1,9},{5... | collective-permute-start | bytes 270344 | tf_op jit(solution)/shard_map/ppermute | solution.py:335
  27.7 6.4 %collective-permute-start.10 = (bf16[32,1408]{1,0:T(8,128)(2,1)S(1)}, bf16[32,1408]{1,0:T(8,128)(2,1)S(1)}, u32[]{:S(2)}, u32[]{:S(2)}) collective-permute-start(bf16[32,1408]{1,0:T(8,128)(2,1)S(1)} %get-tuple-element.67), channel_id=1, source_target_pairs={{0,24},{4,28},{8,0},{12,4},{16,8},{20,12},{24,16},{28,20},{1,25},{... | collective-permute-start | bytes 270344 | tf_op jit(solution)/shard_map/ppermute | solution.py:335
  30.0 8.2 %collective-permute-start.11 = (bf16[32,1280]{1,0:T(8,128)(2,1)S(1)}, bf16[32,1280]{1,0:T(8,128)(2,1)S(1)}, u32[]{:S(2)}, u32[]{:S(2)}) collective-permute-start(bf16[32,1280]{1,0:T(8,128)(2,1)S(1)} %get-tuple-element.69), channel_id=1, source_target_pairs={{0,16},{4,20},{8,24},{12,28},{16,0},{20,4},{24,8},{28,12},{1,17},{... | collective-permute-start | bytes 245768 | tf_op jit(solution)/shard_map/ppermute | solution.py:335

commit v6 on v5

v6 whole, which is shorter than its diff:
```python
import functools

import jax
import jax.numpy as jnp
import numpy as np
from jax import lax
from jax.experimental import pallas as pl
from jax.experimental.pallas import tpu as pltpu
from jax.sharding import PartitionSpec as P

SUB_PIX = 16
SPOT_PIX = 32
WIND_MAX = 8
LANES = 128
STRIP = 32

HBM_SPEC = pl.BlockSpec(memory_space=pltpu.HBM)
VMEM_SPEC = pl.BlockSpec(memory_space=pltpu.VMEM)


def params(*arrays):
    held = sum(array.size * array.dtype.itemsize for array in jax.tree.leaves(arrays))
    return pltpu.CompilerParams(vmem_limit_bytes=held + 8 * 1024 * 1024)


def call(kernel, out_shape, operands, flops, name, in_hbm=(), scratch=(), brief=False):
    def spec(k, array):
        scalars = array.dtype == jnp.int32 and array.size < LANES
        return HBM_SPEC if scalars or k in in_hbm else VMEM_SPEC

    out_specs = jax.tree.map(lambda _: VMEM_SPEC, out_shape)
    size = sum(array.size * array.dtype.itemsize for array in jax.tree.leaves((operands, out_shape)))
    if brief:
        flops = size = 0
    in_specs = [spec(k, array) for k, array in enumerate(operands)]
    operands = [
        pltpu.with_memory_space_constraint(array, pltpu.HBM) if space is HBM_SPEC else array
        for array, space in zip(operands, in_specs)
    ]
    return pl.pallas_call(
        kernel,
        out_shape=out_shape,
        in_specs=in_specs,
        out_specs=out_specs,
        scratch_shapes=list(scratch),
        compiler_params=params(operands, out_shape),
        cost_estimate=pl.CostEstimate(flops=flops, bytes_accessed=size, transcendentals=0),
        name=name,
    )(*operands)


def fetch(*pairs):
    copies = [pltpu.make_async_copy(source, target, sem) for source, target, sem in pairs]
    for copy in copies:
        copy.start()
    return copies


def wrap(value, length):
    value = jnp.where(value < 0, value + length, value)
    return jnp.where(value >= length, value - length, value)


def stack(*blocks):
    return jnp.concatenate(blocks, axis=0)


def beside(*blocks):
    return jnp.concatenate(blocks, axis=1)


def dot(left, right):
    return jnp.dot(left, right, preferred_element_type=jnp.float32)


def spans(pixel, anchor, num, den, length):
    stretched = (pixel * num).astype(jnp.float32)
    den = (jnp.zeros_like(pixel) + den).astype(jnp.float32)
    whole = jnp.floor((stretched + 0.5) / den)
    fraction = (stretched - whole * den) / den
    base = wrap(anchor + whole.astype(jnp.int32), length)
    upper = wrap(base + 1, length)
    return base, upper, 1.0 - fraction, fraction


def split_kernel(screens, *refs):
    own, outs, sems = refs[0], refs[1:-1], refs[-1]
    width = outs[0].shape[2]
    core = lax.rem(lax.axis_index("dir"), 2)
    pairs = []
    for k, out in enumerate(outs):
        half = core if k < 2 else 1 - core
        start = pl.multiple_of((2 * half + k % 2) * width, LANES)
        pairs.append((screens.at[:, :, pl.ds(start, width)], out, sems.at[k]))
    pairs.append((screens, own, sems.at[len(outs)]))
    for load in fetch(*pairs):
        load.wait()


def weights_kernel(geometry, wind_hbm, offsets_hbm, ratio_hbm, rows_out, base_out, upper_out, low_out, high_out, *scratch):
    n_layer, rows_dev, screen_cols = geometry
    wind, offsets, ratio, sems = scratch
    loads = fetch(
        (wind_hbm, wind, sems.at[0]),
        (offsets_hbm, offsets, sems.at[1]),
        (ratio_hbm, ratio, sems.at[2]),
    )
    _, layers, pupil_rows, screen_rows = rows_out.shape
    half = pupil_rows // 2
    direction = lax.axis_index("dir")
    column = lax.axis_index("layer")
    block = pupil_rows // n_layer
    row = lax.broadcasted_iota(jnp.int32, (half, LANES), 0)
    pair = jnp.bitwise_xor(row // block, column // 2)
    parity = lax.rem(column, 2)
    inside = lax.rem(row, block) + pair * (2 * block)
    pixel_rows = stack(inside + parity * block, inside + (1 - parity) * block)
    lane = lax.broadcasted_iota(jnp.int32, (pupil_rows, LANES), 1)
    for load in loads:
        load.wait()
    for side in range(2):
        target = jnp.bitwise_xor(direction, side)
        for level in range(layers):
            anchor = wrap(offsets[level, 0, target] - wind[0, level], screen_rows)
            num, den = ratio[level, 0, target], ratio[level, 1, target]
            base, upper, low, high = spans(pixel_rows, anchor, num, den, screen_rows)
            for peer in range(4):
                for part in range(rows_dev // LANES):
                    index = lane + (jnp.bitwise_xor(direction, peer) * rows_dev + part * LANES)
                    weight = jnp.where(index == base, low, 0.0)
                    weight = jnp.where(index == upper, high, weight)
                    start = peer * rows_dev + part * LANES
                    rows_out[side, level, :, start : start + LANES] = weight.astype(jnp.bfloat16)
    sub = lax.broadcasted_iota(jnp.int32, (8, LANES), 0)
    anchor, num, den = jnp.zeros_like(sub), jnp.zeros_like(sub), jnp.ones_like(sub)
    for level in range(layers):
        start = wrap(offsets[level, 1, direction] - wind[1, level], screen_cols)
        anchor = jnp.where(sub == level, start, anchor)
        num = jnp.where(sub == level, ratio[level, 0, direction], num)
        den = jnp.where(sub == level, ratio[level, 1, direction], den)
    for at in range(0, base_out.shape[1], LANES):
        pixel = lax.broadcasted_iota(jnp.int32, (8, LANES), 1) + at
        values = spans(pixel, anchor, num, den, screen_cols)
        for out, value in zip((base_out, upper_out, low_out, high_out), values):
            out[:, at : at + LANES] = value


def column_weights(base_ref, upper_ref, low_ref, high_ref, first, out):
    layers, cols_dev, pupil_cols = out.shape
    half = cols_dev // 2
    core = lax.rem(lax.axis_index("dir"), 2)
    sub = lax.broadcasted_iota(jnp.int32, (half, LANES), 0).reshape(half // 8, 8, LANES)
    for level in range(layers):

        def tile(step, carry):
            start = pl.multiple_of(step * LANES, LANES)
            cut = (slice(level, level + 1), pl.ds(start, LANES))
            base, upper, low, high = [
                jnp.broadcast_to(ref[cut], (8, LANES)) for ref in (base_ref, upper_ref, low_ref, high_ref)
            ]
            for side in range(2):
                shift = first + jnp.bitwise_xor(core, side) * half
                weight = jnp.where(sub == (base - shift)[None], low[None], 0.0)
                weight = jnp.where(sub == (upper - shift)[None], high[None], weight)
                weight = weight.reshape(half, LANES).astype(jnp.bfloat16)
                out[level, side * half : (side + 1) * half, pl.ds(start, LANES)] = weight
            return carry

        lax.fori_loop(0, pupil_cols // LANES, tile, 0)


def columns_kernel(*refs):
    tables, out = refs[:4], refs[-1]
    column_weights(*tables, lax.axis_index("layer") * out.shape[1], out)


def project_rows(chunk, rows_ref, keep, near, across, diagonal, level):
    width = keep.shape[2]
    core = lax.rem(lax.axis_index("dir"), 2)
    start = pl.multiple_of((2 * core + chunk) * width, LANES)
    screen = stack(keep[level], near[level, :, pl.ds(start, width)], across[level], diagonal[level])
    rows = stack(rows_ref[0, level], rows_ref[1, level])
    return dot(rows, screen).astype(jnp.bfloat16)


def first_rows_kernel(rows_ref, keep, near, across, diagonal, mine, sibling, other, sibling_other):
    layers, half, _ = mine.shape
    for level in range(layers):
        part = project_rows(0, rows_ref, keep, near, across, diagonal, level)
        for k, out in enumerate((mine, other, sibling, sibling_other)):
            out[level] = part[k * half : (k + 1) * half]


def later_rows_kernel(rows_ref, keep, near, across, diagonal, across0, sibling0, mine, other, sibling_other, give):
    layers, half, width = mine.shape
    rows = across.shape[1]
    for level in range(layers):
        part = project_rows(1, rows_ref, keep, near, across, diagonal, level)
        mine[level] = part[:half]
        other[level] = part[half : 2 * half]
        sibling_other[level] = part[3 * half :]
        give[level, :half, :width] = sibling0[level]
        give[level, :half, width:] = part[2 * half : 3 * half]
        for k, block in enumerate((across0, across)):
            cut = slice(k * width, (k + 1) * width)
            give[level, half : half + 16, cut] = block[level, :16]
            give[level, half + 16 :, cut] = block[level, rows - 16 :]


def project(parts, cols_refs, at):
    cols = stack(*[ref[level, start:stop, at : at + 256] for ref, level, start, stop in cols_refs])
    return dot(beside(*parts), cols)


def phase_kernel(*refs):
    tables, refs = refs[:4], refs[4:]
    cols_ref, mine0, mine1, came, sibling_came, phase, cols_out = refs
    first = jnp.bitwise_xor(lax.axis_index("layer"), 1) * cols_out.shape[1]
    column_weights(*tables, first, cols_out)
    layers, _, width = mine0.shape
    parts, cuts = [], []
    for level in range(layers):
        parts += [mine0[level], mine1[level], came[level], sibling_came[level]]
        cuts += [(cols_ref, level, 0, 2 * width)]
        cuts += [(cols_out, level, 0, width), (cols_out, level, 2 * width, 3 * width)]
    for at in range(0, phase.shape[1], 256):
        phase[:, at : at + 256] = project(parts, cuts, at)


def last_kernel(mine_ref, cols_ref, phase, taken, came, sibling_came, *outs):
    layers, half, width = came.shape
    size, pupil_cols = outs[0].shape
    parts, cuts = [], []
    for level in range(layers):
        parts += [taken[level, :half], came[level], sibling_came[level]]
        cuts += [(mine_ref, level, 2 * width, 4 * width)]
        cuts += [(cols_ref, level, width, 2 * width), (cols_ref, level, 3 * width, 4 * width)]
    for at in range(0, pupil_cols, 256):
        total = (phase[:, at : at + 256] + project(parts, cuts, at)).astype(jnp.bfloat16)
        for k, out in enumerate(outs):
            out[:, at : at + 256] = total[k * size : (k + 1) * size]


def shifted_rows(shift, own, near, edges):
    odd = lax.rem(lax.axis_index("dir"), 2) == 1
    own, near, edges = [block.astype(jnp.float32) for block in (own, near, edges)]
    rows = own.shape[0]
    before = jnp.where(odd, near[rows - 16 :], edges[16:])
    after = jnp.where(odd, edges[:16], near[:16])
    shift = jnp.where(shift < 0, shift + rows + 32, shift)
    return pltpu.roll(stack(before, own, after), shift, 0)[16 : 16 + rows]


def strips_kernel(wind_hbm, own, near, diagonal0, diagonal1, taken, right, left, edges, wind, sem):
    load = fetch((wind_hbm, wind, sem))[0]
    layers, rows, width = own.shape
    odd = lax.rem(lax.axis_index("dir"), 2) == 1
    half = taken.shape[1] - 32
    lane = lax.broadcasted_iota(jnp.int32, (rows, LANES), 1)
    strips = jnp.zeros((rows, LANES), jnp.float32)
    for level in range(layers):
        chunks = [stack(part[level, :16], part[level, rows - 16 :]) for part in (diagonal0, diagonal1)]
        here = beside(*chunks).astype(jnp.float32)
        there = taken[level, half:].astype(jnp.float32)
        both = beside(jnp.where(odd, there, here), jnp.where(odd, here, there))
        edges[level] = both.astype(jnp.bfloat16)
    load.wait()
    for level in range(layers):
        shift = wind[0, level]
        at = WIND_MAX * level
        cut = slice(width - LANES, width)
        last = shifted_rows(shift, own[level, :, cut], near[level, :, cut], edges[level, :, cut])
        strips = jnp.where((lane >= at) & (lane < at + WIND_MAX), pltpu.roll(last, WIND_MAX + at, 1), strips)
        at = STRIP + WIND_MAX * level
        cut = slice(0, LANES)
        initial = shifted_rows(shift, own[level, :, cut], near[level, :, cut], edges[level, :, cut])
        strips = jnp.where((lane >= at) & (lane < at + WIND_MAX), pltpu.roll(initial, at, 1), strips)
    strips = strips.T.astype(jnp.bfloat16)
    right[...] = strips[:STRIP]
    left[...] = strips[STRIP : 2 * STRIP]


def shift_kernel(wind_hbm, own, near, edges, from_left, from_right, out, wind, sem):
    load = fetch((wind_hbm, wind, sem))[0]
    layers, rows, cols = own.shape
    strips = stack(from_left[...], from_right[...], jnp.zeros((LANES - 2 * STRIP, rows), jnp.bfloat16))
    strips = strips.astype(jnp.float32).T
    lane = lax.broadcasted_iota(jnp.int32, (rows, LANES), 1)
    load.wait()
    for level in range(layers):
        last = pltpu.roll(strips, LANES - WIND_MAX * (level + 1), 1)
        first = pltpu.roll(strips, LANES - STRIP - WIND_MAX * level, 1)
        extra = jnp.where(lane < WIND_MAX, first, last)
        moved = shifted_rows(wind[0, level], own[level], near[level], edges[level])
        shift = wind[1, level]
        shift = jnp.where(shift < 0, shift + cols + LANES, shift)
        out[level] = pltpu.roll(beside(moved, extra), shift, 1)[:, :cols].astype(jnp.bfloat16)


def optics_kernel(*refs):
    sources, refs = refs[:4], refs[4:]
    amp_out, high_out, low_out, lines_out, amplitude, ones, columns, lines, sems = refs
    targets = amplitude, ones, columns, lines
    loads = fetch(*[(source, target, sems.at[k]) for k, (source, target) in enumerate(zip(sources, targets))])
    for load in loads:
        load.wait()
    rows, pupil_cols = amplitude.shape
    for step in range(pupil_cols // LANES):
        cut = slice(step * LANES, (step + 1) * LANES)
        amp = amplitude[:, cut]
        energy = (amp * amp).reshape(rows // SUB_PIX, SUB_PIX, LANES).sum(axis=1)
        energy = jnp.broadcast_to(energy[:, None], (rows // SUB_PIX, SUB_PIX, LANES)).reshape(rows, LANES)
        total = jnp.dot(energy, ones[...], precision=lax.Precision.HIGHEST, preferred_element_type=jnp.float32)
        amp_out[:, cut] = amp * lax.rsqrt(total)
    high_out[...], low_out[...] = split(columns[...])
    high, low = split(lines[...])
    lines_out[...] = jnp.concatenate([high, high, low], axis=1)


def sin_cos(phase):
    turns = jnp.floor(phase * (1.0 / np.pi) + 0.5)
    rest = phase - turns * 3.140625
    rest = rest - turns * 9.67653589793e-4
    odd = turns - 2.0 * jnp.floor(turns * 0.5)
    sign = 1.0 - 2.0 * odd
    square = rest * rest
    sine = -1.0 / 39916800.0
    for term in (1.0 / 362880.0, -1.0 / 5040.0, 1.0 / 120.0, -1.0 / 6.0, 1.0):
        sine = sine * square + term
    cosine = 1.0 / 479001600.0
    for term in (-1.0 / 3628800.0, 1.0 / 40320.0, -1.0 / 720.0, 1.0 / 24.0, -0.5, 1.0):
        cosine = cosine * square + term
    return sine * rest * sign, cosine * sign


def split(value):
    high = value.astype(jnp.bfloat16)
    low = (value - high.astype(jnp.float32)).astype(jnp.bfloat16)
    return high, low


def imaging_kernel(count, *refs):
    parts = refs[:count]
    amp_ref, cols_high, cols_low, rows_table, out = refs[count:]
    rows, cols = amp_ref.shape
    tiles = cols // LANES
    phase = parts[0][...].astype(jnp.float32)
    for part in parts[1:]:
        phase = phase + part[...].astype(jnp.float32)
    sine, cosine = sin_cos(phase)
    amp = amp_ref[...]
    real, imag = amp * cosine, amp * sine
    field = jnp.concatenate(
        [
            jnp.concatenate(
                [real[:, t * LANES : (t + 1) * LANES], imag[:, t * LANES : (t + 1) * LANES]], axis=1
            )
            for t in range(tiles)
        ],
        axis=0,
    )
    high, low = split(field)
    half = dot(high, cols_high[...]) + (dot(low, cols_high[...]) + dot(high, cols_low[...]))
    wide = 2 * LANES
    out_rows = 2 * rows
    for t in range(tiles):
        mine = half[t * rows : (t + 1) * rows]
        mine = jnp.concatenate([mine[:, :wide], mine[:, wide:]], axis=0)
        high, low = split(mine)
        full = dot(rows_table[...], jnp.concatenate([high, low, high], axis=0))
        real, imag = full[:out_rows], full[out_rows:]
        out[:, t * wide : (t + 1) * wide] = real * real + imag * imag


def tables_of(rows):
    freq = np.arange(SPOT_PIX)[:, None] - SPOT_PIX // 2
    angle = ((freq * np.arange(SUB_PIX)[None, :]) % SPOT_PIX) * (2.0 * np.pi / SPOT_PIX)
    cos, sin = np.cos(angle), np.sin(angle)

    def blocks(table, count):
        return np.kron(np.eye(count), table)

    per_tile = LANES // SUB_PIX
    col_cos, col_sin = blocks(cos.T, per_tile), blocks(sin.T, per_tile)
    columns = np.block([[col_cos, -col_sin], [col_sin, col_cos]])
    count = rows // SUB_PIX
    row_cos, row_sin = blocks(cos, count), blocks(sin, count)
    lines = np.block([[row_cos, row_sin], [-row_sin, row_cos]])

    return columns.astype(np.float32), lines.astype(np.float32)


def per_device(screens, amplitude, wind, offsets, ratio):
    layers, rows_dev, cols_dev = screens.shape
    n_layer = lax.axis_size("layer")
    n_dir = lax.axis_size("dir")
    rows, pupil_cols = amplitude.shape
    pairs = n_layer // 2
    half = pairs * rows
    pupil_rows = 2 * half
    assert n_dir == 4 and rows == STRIP and pairs > 2
    bf16, f32 = jnp.bfloat16, jnp.float32
    wind = jnp.transpose(wind, (1, 0))
    offsets = jnp.transpose(offsets, (1, 2, 0))
    ratio = jnp.transpose(ratio, (1, 2, 0))
    smem, sem = pltpu.SMEM, pltpu.SemaphoreType.DMA
    wind_scratch = [smem(wind.shape, jnp.int32), sem]

    def shape(*dims, dtype=bf16):
        return jax.ShapeDtypeStruct(dims, dtype)

    def swap(value, bits):
        return lax.ppermute(value, "dir", [(i, i ^ bits) for i in range(n_dir)])

    def partner(value, bits=0):
        count = n_layer * n_dir
        return lax.ppermute(value, ("layer", "dir"), [(i, i ^ n_dir ^ bits) for i in range(count)])

    def turn(value, step):
        return lax.ppermute(value, "layer", [(i, (i + step) % n_layer) for i in range(n_layer)])

    width = cols_dev // 4
    chunk = shape(layers, rows_dev, width)
    own, keep0, keep1, give0, give1 = call(
        split_kernel,
        [shape(*screens.shape)] + [chunk] * 4,
        (screens,),
        0,
        "split",
        in_hbm=(0,),
        scratch=[sem((5,))],
        brief=True,
    )
    across0 = swap(keep0, 2)
    diagonal0 = swap(give0, 3)
    across1 = swap(keep1, 2)
    diagonal1 = swap(give1, 3)
    near = swap(own, 1)
    row_weights, *tables = call(
        functools.partial(weights_kernel, (n_layer, rows_dev, cols_dev * n_layer)),
        [shape(2, layers, pupil_rows, 4 * rows_dev)]
        + [shape(8, pupil_cols, dtype=dtype) for dtype in (jnp.int32, jnp.int32, f32, f32)],
        (wind, offsets, ratio),
        0,
        "weights",
        scratch=[smem(array.shape, jnp.int32) for array in (wind, offsets, ratio)] + [sem((3,))],
        brief=True,
    )
    tables = tuple(tables)
    across0, diagonal0, row_weights, tables = lax.optimization_barrier((across0, diagonal0, row_weights, tables))

    projected = shape(layers, half, width)
    mine0, sibling0, other0, sibling_other0 = call(
        first_rows_kernel,
        [projected] * 4,
        (row_weights, keep0, near, across0, diagonal0),
        0,
        "rows_first",
        brief=True,
    )
    came0 = partner(other0)
    sibling_came0 = partner(sibling_other0, 1)

    tables, mine0 = lax.optimization_barrier((tables, mine0))
    cols = call(
        columns_kernel, shape(layers, cols_dev, pupil_cols), tables, 0, "columns", brief=True
    )
    cols, sibling0 = lax.optimization_barrier((cols, sibling0))
    mine1, other1, sibling_other1, give = call(
        later_rows_kernel,
        [projected] * 3 + [shape(layers, half + 32, 2 * width)],
        (row_weights, keep1, near, across1, diagonal1, across0, sibling0),
        0,
        "rows_later",
        brief=True,
    )
    came1 = partner(other1)
    sibling_came1 = partner(sibling_other1, 1)
    taken = swap(give, 1)

    phase, others = call(
        phase_kernel,
        (shape(half, pupil_cols, dtype=f32), shape(layers, cols_dev, pupil_cols)),
        (*tables, cols, mine0, mine1, came0, sibling_came0),
        10_000_000_000,
        "phase",
    )
    taken, phase = lax.optimization_barrier((taken, phase))
    right, left, edges = call(
        strips_kernel,
        [shape(STRIP, rows_dev)] * 2 + [shape(layers, 32, cols_dev)],
        (wind, own, near, diagonal0, diagonal1, taken),
        0,
        "strips",
        scratch=wind_scratch,
        brief=True,
    )
    from_left = turn(right, 1)
    from_right = turn(left, n_layer - 1)
    came1, from_left, from_right = lax.optimization_barrier((came1, from_left, from_right))
    sums = call(
        last_kernel,
        [shape(rows, pupil_cols)] * pairs,
        (cols, others, phase, taken, came1, sibling_came1),
        300_000_000,
        "last",
    )
    received = [sums[0]] + [
        lax.ppermute(sums[k], "layer", [(i, i ^ (2 * k)) for i in range(n_layer)])
        for k in sorted(range(1, pairs), key=lambda k: -(k & -k))
    ]

    ones = np.kron(np.eye(LANES // SUB_PIX), np.ones((SUB_PIX, SUB_PIX))).astype(np.float32)
    columns, lines = tables_of(rows)
    amplitude, edges, first = lax.optimization_barrier((amplitude, edges, sums[0]))
    received[0] = first
    optics_in = (amplitude, jnp.asarray(ones), jnp.asarray(columns), jnp.asarray(lines))
    optics = call(
        optics_kernel,
        (
            shape(rows, pupil_cols, dtype=f32),
            shape(*columns.shape),
            shape(*columns.shape),
            shape(lines.shape[0], 3 * lines.shape[1]),
        ),
        optics_in,
        30_000_000,
        "optics",
        in_hbm=range(4),
        scratch=[pltpu.VMEM(array.shape, f32) for array in optics_in] + [sem((4,))],
    )
    new_screens = call(
        shift_kernel,
        shape(layers, rows_dev, cols_dev),
        (wind, own, near, edges, from_left, from_right),
        1_000_000,
        "shift",
        scratch=wind_scratch,
    )
    spots = call(
        functools.partial(imaging_kernel, pairs),
        shape(2 * rows, 2 * pupil_cols, dtype=f32),
        (*received, *optics),
        400_000_000,
        "imaging",
    )
    return (new_screens, spots[None])


def solution(mesh):
    return jax.shard_map(
        per_device,
        mesh=mesh,
        in_specs=(P(None, "dir", "layer"), P("layer", None), P(), P(), P()),
        out_specs=(P(None, "dir", "layer"), P("dir", "layer", None)),
        check_vma=False,
    )
```

time: 40.2 us -> 39.9 us (level)
  waiting for transfers between devices: 11.5 us -> 4.37 us
  starting transfers between devices: 12.3 us -> 18.7 us
  local copies, waits for them, and re-layouts: 3.66 us -> 0 us
  Pallas kernels: 11.8 us -> 15.4 us
    ppermute x9 -> x13, starting transfers between devices: 7.6 us -> 14 us  [the longest x6 5.52 us: swap(): return lax.ppermute(value, 'dir', [(i, i ^ bits) for i in range(n_dir)])]
    ppermute x3 -> x2, waiting for transfers between devices: 5.44 us -> 1.62 us  [turn(): lax.ppermute(value, 'layer', [(i, (i + step) % n_layer) for i in range(n_...]
    unnamed x8 -> x0, local copies, waits for them, and re-layouts: 3.64 us -> none
    pallas_call x6 -> x11, Pallas kernels: 11.8 us -> 15.4 us  [call(): pl.pallas_call(kernel, out_shape=out_shape, in_specs=in_specs, out_specs=...]
    ppermute x9 -> x13, waiting for transfers between devices: 6.04 us -> 2.74 us  [the longest x6 1.61 us: swap(): return lax.ppermute(value, 'dir', [(i, i ^ bits) for i in range(n_dir)])]
    ppermute x3 -> x2, starting transfers between devices: 4.67 us -> 4.78 us  [turn(): lax.ppermute(value, 'layer', [(i, (i + step) % n_layer) for i in range(n_...]
  transfers between devices with their start and end apart: 12 -> 15, of which waited for: 8 -> 4; matrix products, arithmetic and copies ran while one was open for 0% -> 0% of each run, Pallas kernels for 22% -> 30%
where the time goes in v6:
time: 39.9 us; the launch traced here: 39.3 us
  starting transfers between devices  18.7 us (47%)
  Pallas kernels  15.4 us (39%)
  waiting for transfers between devices  4.37 us (11%)
  between operations  0.76 us (2%)
    pallas_call x11, Pallas kernels, call(): pl.pallas_call(kernel, out_shape=out_shape, in_specs=in_specs, out_specs=...  15.4 us
    ppermute x6, starting transfers between devices, swap(): return lax.ppermute(value, 'dir', [(i, i ^ bits) for i in range(n_dir)])  5.52 us
    ppermute x2, starting transfers between devices, turn(): lax.ppermute(value, 'layer', [(i, (i + step) % n_layer) for i in range(n_...  4.78 us
    ppermute x3, starting transfers between devices, per_device(): lax.ppermute(sums[k], 'layer', [(i, i ^ 2 * k) for i in range(n_layer)])  4.45 us
    ppermute x4, starting transfers between devices, partner(): lax.ppermute(value, ('layer', 'dir'), [(i, i ^ n_dir ^ bits) for i in ran...  3.99 us
    ppermute x2, waiting for transfers between devices, turn(): lax.ppermute(value, 'layer', [(i, (i + step) % n_layer) for i in range(n_...  1.62 us
    ppermute x6, waiting for transfers between devices, swap(): return lax.ppermute(value, 'dir', [(i, i ^ bits) for i in range(n_dir)])  1.61 us
  transfers between devices with their start and end apart: 15, of which 4 were waited for; matrix products, arithmetic and copies ran while one was open for 0% of the time, Pallas kernels for 30%

profile of v6, /device:TPU:0, one launch (start us, length us, event | category | flops | bytes accessed | tf_op | source)
XLA Modules:
  0.0 39.3 jit_solution(1719061708020669677)
XLA Ops:
  0.6 1.3 %split.1 = (bf16[3,128,512]{2,1,0:T(8,128)(2,1)S(1)}, bf16[3,128,128]{2,1,0:T(8,128)(2,1)S(1)}, bf16[3,128,128]{2,1,0:T(8,128)(2,1)S(1)}, bf16[3,128,128]{2,1,0:T(8,128)(2,1)S(1)}, bf16[3,128,128]{2,1,0:T(8,128)(2,1)S(1)}) custom-call(bf16[3,128,512]{2,1,0:T(8,128)(2,1)} %screens.1), custom_call_target="tpu_custom_call" | custom-call | tf_op jit(solution)/shard_map/split/pallas_call | solution.py:40
  1.9 0.5 %collective-permute-start = (bf16[3,128,512]{2,1,0:T(8,128)(2,1)S(1)}, bf16[3,128,512]{2,1,0:T(8,128)(2,1)S(1)}, u32[]{:S(2)}, u32[]{:S(2)}) collective-permute-start(bf16[3,128,512]{2,1,0:T(8,128)(2,1)S(1)} %get-tuple-element.55.own), channel_id=1, source_target_pairs={{0,1},{1,0},{2,3},{3,2},{4,5},{5,4},{6,7},{7,6},{8,9},{9,8},{10,11... | collective-permute-start | bytes 1179656 | tf_op jit(solution)/shard_map/ppermute | solution.py:413
  2.4 2.6 %collective-permute-start.2 = (bf16[3,128,128]{2,1,0:T(8,128)(2,1)S(1)}, bf16[3,128,128]{2,1,0:T(8,128)(2,1)S(1)}, u32[]{:S(2)}, u32[]{:S(2)}) collective-permute-start(bf16[3,128,128]{2,1,0:T(8,128)(2,1)S(1)} %get-tuple-element.57), channel_id=1, source_target_pairs={{0,3},{1,2},{2,1},{3,0},{4,7},{5,6},{6,5},{7,4},{8,11},{9,10},{10,... | collective-permute-start | bytes 294920 | tf_op jit(solution)/shard_map/ppermute | solution.py:413
  5.0 0.0 collective-permute-start.1
  5.1 1.4 %collective-permute-start.3 = (bf16[3,128,128]{2,1,0:T(8,128)(2,1)S(1)}, bf16[3,128,128]{2,1,0:T(8,128)(2,1)S(1)}, u32[]{:S(2)}, u32[]{:S(2)}) collective-permute-start(bf16[3,128,128]{2,1,0:T(8,128)(2,1)S(1)} %get-tuple-element.64), channel_id=1, source_target_pairs={{0,3},{1,2},{2,1},{3,0},{4,7},{5,6},{6,5},{7,4},{8,11},{9,10},{10,... | collective-permute-start | bytes 294920 | tf_op jit(solution)/shard_map/ppermute | solution.py:413
  6.4 0.6 %collective-permute-start.4 = (bf16[3,128,128]{2,1,0:T(8,128)(2,1)S(1)}, bf16[3,128,128]{2,1,0:T(8,128)(2,1)S(1)}, u32[]{:S(2)}, u32[]{:S(2)}) collective-permute-start(bf16[3,128,128]{2,1,0:T(8,128)(2,1)S(1)} %get-tuple-element.66.keep), channel_id=1, source_target_pairs={{0,2},{1,3},{2,0},{3,1},{4,6},{5,7},{6,4},{7,5},{8,10},{9,11},{10,... | collective-permute-start | bytes 294920 | tf_op jit(solution)/shard_map/ppermute | solution.py:413
  7.1 2.0 %weights.1 = (bf16[2,3,256,512]{3,2,1,0:T(8,128)(2,1)S(1)}, s32[8,1280]{1,0:T(8,128)S(1)}, s32[8,1280]{1,0:T(8,128)S(1)}, f32[8,1280]{1,0:T(8,128)S(1)}, f32[8,1280]{1,0:T(8,128)S(1)}) custom-call(s32[2,3]{1,0:T(2,128)} %bitcast.5, s32[3,2,4]{2,1,0:T(2,128)} %bitcast.8, s32[3,2,4]{2,1,0:T(2,128)} %bitcast.9), custom_call_target="tpu_custom_call" | custom-call | tf_op jit(solution)/shard_map/weights/pallas_call | solution.py:40
  9.1 1.6 %collective-permute-done.1.across.across0 = bf16[3,128,128]{2,1,0:T(8,128)(2,1)S(1)} collective-permute-done((bf16[3,128,128]{2,1,0:T(8,128)(2,1)S(1)}, bf16[3,128,128]{2,1,0:T(8,128)(2,1)S(1)}, u32[]{:S(2)}, u32[]{:S(2)}) %collective-permute-start.1) | collective-permute-done | bytes 98336 | tf_op jit(solution)/shard_map/ppermute | solution.py:413
  10.7 0.0 collective-permute-done.near
  10.7 0.6 %rows_first.1 = (bf16[3,128,128]{2,1,0:T(8,128)(2,1)S(1)}, bf16[3,128,128]{2,1,0:T(8,128)(2,1)S(1)}, bf16[3,128,128]{2,1,0:T(8,128)(2,1)S(1)}, bf16[3,128,128]{2,1,0:T(8,128)(2,1)S(1)}) custom-call(bf16[2,3,256,512]{3,2,1,0:T(8,128)(2,1)S(1)} %get-tuple-element.65.rows_ref, bf16[3,128,128]{2,1,0:T(8,128)(2,1)S(1)} %get-tuple-element.56.keep, ...), custom_call_target="tpu_custom_call" | custom-call | tf_op jit(solution)/shard_map/rows_first/pallas_call | solution.py:40
  11.3 2.1 %collective-permute-start.6 = (bf16[3,128,128]{2,1,0:T(8,128)(2,1)S(1)}, bf16[3,128,128]{2,1,0:T(8,128)(2,1)S(1)}, u32[]{:S(2)}, u32[]{:S(2)}) collective-permute-start(bf16[3,128,128]{2,1,0:T(8,128)(2,1)S(1)} %get-tuple-element.83), channel_id=1, source_target_pairs={{0,4},{1,5},{2,6},{3,7},{4,0},{5,1},{6,2},{7,3},{8,12},{9,13},{10,... | collective-permute-start | bytes 294920 | tf_op jit(solution)/shard_map/ppermute | solution.py:417
  13.4 1.5 %columns.1.refs_4_.mine_ref = bf16[3,512,1280]{2,1,0:T(8,128)(2,1)S(1)} custom-call(s32[8,1280]{1,0:T(8,128)S(1)} %get-tuple-element.73.refs_0_, s32[8,1280]{1,0:T(8,128)S(1)} %get-tuple-element.74.refs_1_, f32[8,1280]{1,0:T(8,128)S(1)} %get-tuple-element.75.refs_2_, f32[8,1280]{1,0:T(8,128)S(1)} %get-tuple-element.76.refs_3_), custom_call_target="tpu_custom_call" | custom-call | tf_op jit(solution)/shard_map/columns/pallas_call | solution.py:40
  14.9 0.0 collective-permute-done.3.diagonal.diagonal1
  14.9 0.6 %rows_later.1 = (bf16[3,128,128]{2,1,0:T(8,128)(2,1)S(1)}, bf16[3,128,128]{2,1,0:T(8,128)(2,1)S(1)}, bf16[3,128,128]{2,1,0:T(8,128)(2,1)S(1)}, bf16[3,160,256]{2,1,0:T(8,128)(2,1)S(1)}) custom-call(bf16[2,3,256,512]{3,2,1,0:T(8,128)(2,1)S(1)} %get-tuple-element.65.rows_ref, bf16[3,128,128]{2,1,0:T(8,128)(2,1)S(1)} %get-tuple-element.66.keep, ...), custom_call_target="tpu_custom_call" | custom-call | tf_op jit(solution)/shard_map/rows_later/pallas_call | solution.py:40
  15.5 1.6 %collective-permute-start.8 = (bf16[3,128,128]{2,1,0:T(8,128)(2,1)S(1)}, bf16[3,128,128]{2,1,0:T(8,128)(2,1)S(1)}, u32[]{:S(2)}, u32[]{:S(2)}) collective-permute-start(bf16[3,128,128]{2,1,0:T(8,128)(2,1)S(1)} %get-tuple-element.90), channel_id=1, source_target_pairs={{0,4},{1,5},{2,6},{3,7},{4,0},{5,1},{6,2},{7,3},{8,12},{9,13},{10,... | collective-permute-start | bytes 294920 | tf_op jit(solution)/shard_map/ppermute | solution.py:417
  17.1 0.3 collective-permute-start.11
  17.4 0.3 collective-permute-start.5
  17.7 0.4 %collective-permute-done.7.refs_8_ = bf16[3,128,128]{2,1,0:T(8,128)(2,1)S(1)} collective-permute-done((bf16[3,128,128]{2,1,0:T(8,128)(2,1)S(1)}, bf16[3,128,128]{2,1,0:T(8,128)(2,1)S(1)}, u32[]{:S(2)}, u32[]{:S(2)}) %collective-permute-start.7) | collective-permute-done | bytes 98336 | tf_op jit(solution)/shard_map/ppermute | solution.py:417
  18.1 2.2 %phase.1 = (f32[128,1280]{1,0:T(8,128)S(1)}, bf16[3,512,1280]{2,1,0:T(8,128)(2,1)S(1)}) custom-call(s32[8,1280]{1,0:T(8,128)S(1)} %get-tuple-element.73.refs_0_, s32[8,1280]{1,0:T(8,128)S(1)} %get-tuple-element.74.refs_1_, f32[8,1280]{1,0:T(8,128)S(1)} %get-tuple-element.75.refs_2_, f32[8,1280]{1,0:T(8,128)S(1)} %get-tuple-element.76.refs_3_, ...), custom_call_target="tpu_custom_call" | custom-call | flops 10000000000 | bytes 9076736 | tf_op jit(solution)/shard_map/phase/pallas_call | solution.py:40
  20.3 0.0 collective-permute-done.5.taken
  20.3 1.0 %strips.1 = (bf16[32,128]{1,0:T(8,128)(2,1)S(1)}, bf16[32,128]{1,0:T(8,128)(2,1)S(1)}, bf16[3,32,512]{2,1,0:T(8,128)(2,1)S(1)}) custom-call(s32[2,3]{1,0:T(2,128)} %bitcast.6, bf16[3,128,512]{2,1,0:T(8,128)(2,1)S(1)} %get-tuple-element.55.own, bf16[3,128,512]{2,1,0:T(8,128)(2,1)S(1)} %collective-permute-done.near, ...), custom_call_target="tpu_custom_call" | custom-call | tf_op jit(solution)/shard_map/strips/pallas_call | solution.py:40
  21.3 1.1 %collective-permute-start.9 = (bf16[32,128]{1,0:T(8,128)(2,1)S(1)}, bf16[32,128]{1,0:T(8,128)(2,1)S(1)}, u32[]{:S(2)}, u32[]{:S(2)}) collective-permute-start(bf16[32,128]{1,0:T(8,128)(2,1)S(1)} %get-tuple-element.91), channel_id=1, source_target_pairs={{0,4},{4,8},{8,12},{12,16},{16,20},{20,24},{24,28},{28,0},{1,5},{5... | collective-permute-start | bytes 24584 | tf_op jit(solution)/shard_map/ppermute | solution.py:420
  22.4 3.6 %collective-permute-start.10 = (bf16[32,128]{1,0:T(8,128)(2,1)S(1)}, bf16[32,128]{1,0:T(8,128)(2,1)S(1)}, u32[]{:S(2)}, u32[]{:S(2)}) collective-permute-start(bf16[32,128]{1,0:T(8,128)(2,1)S(1)} %get-tuple-element.92), channel_id=1, source_target_pairs={{0,28},{4,0},{8,4},{12,8},{16,12},{20,16},{24,20},{28,24},{1,29},{... | collective-permute-start | bytes 24584 | tf_op jit(solution)/shard_map/ppermute | solution.py:420
  26.1 1.6 %collective-permute-done.9.from_left = bf16[32,128]{1,0:T(8,128)(2,1)S(1)} collective-permute-done((bf16[32,128]{1,0:T(8,128)(2,1)S(1)}, bf16[32,128]{1,0:T(8,128)(2,1)S(1)}, u32[]{:S(2)}, u32[]{:S(2)}) %collective-permute-start.9) | collective-permute-done | bytes 8224 | tf_op jit(solution)/shard_map/ppermute | solution.py:420
  27.7 0.7 %last.1 = (bf16[32,1280]{1,0:T(8,128)(2,1)S(1)}, bf16[32,1280]{1,0:T(8,128)(2,1)S(1)}, bf16[32,1280]{1,0:T(8,128)(2,1)S(1)}, bf16[32,1280]{1,0:T(8,128)(2,1)S(1)}) custom-call(bf16[3,512,1280]{2,1,0:T(8,128)(2,1)S(1)} %columns.1.refs_4_.mine_ref, bf16[3,512,1280]{2,1,0:T(8,128)(2,1)S(1)} %get-tuple-element.88.cols_ref, ...), custom_call_target="tpu_custom_call" | custom-call | flops 300000000 | bytes 9289728 | tf_op jit(solution)/shard_map/last/pallas_call | solution.py:40
  28.4 1.3 %collective-permute-start.12 = (bf16[32,1280]{1,0:T(8,128)(2,1)S(1)}, bf16[32,1280]{1,0:T(8,128)(2,1)S(1)}, u32[]{:S(2)}, u32[]{:S(2)}) collective-permute-start(bf16[32,1280]{1,0:T(8,128)(2,1)S(1)} %get-tuple-element.100), channel_id=1, source_target_pairs={{0,16},{4,20},{8,24},{12,28},{16,0},{20,4},{24,8},{28,12},{1,17},{... | collective-permute-start | bytes 245768 | tf_op jit(solution)/shard_map/ppermute | solution.py:509
  29.8 1.5 %collective-permute-start.13 = (bf16[32,1280]{1,0:T(8,128)(2,1)S(1)}, bf16[32,1280]{1,0:T(8,128)(2,1)S(1)}, u32[]{:S(2)}, u32[]{:S(2)}) collective-permute-start(bf16[32,1280]{1,0:T(8,128)(2,1)S(1)} %get-tuple-element.101), channel_id=1, source_target_pairs={{0,8},{4,12},{8,0},{12,4},{16,24},{20,28},{24,16},{28,20},{1,9},{5... | collective-permute-start | bytes 245768 | tf_op jit(solution)/shard_map/ppermute | solution.py:509
  31.2 1.6 %collective-permute-start.14 = (bf16[32,1280]{1,0:T(8,128)(2,1)S(1)}, bf16[32,1280]{1,0:T(8,128)(2,1)S(1)}, u32[]{:S(2)}, u32[]{:S(2)}) collective-permute-start(bf16[32,1280]{1,0:T(8,128)(2,1)S(1)} %get-tuple-element.102), channel_id=1, source_target_pairs={{0,24},{4,28},{8,16},{12,20},{16,8},{20,12},{24,0},{28,4},{1,25},{... | collective-permute-start | bytes 245768 | tf_op jit(solution)/shard_map/ppermute | solution.py:509
  32.9 2.0 %shift.1 = bf16[3,128,512]{2,1,0:T(8,128)(2,1)} custom-call(s32[2,3]{1,0:T(2,128)} %bitcast.7, bf16[3,128,512]{2,1,0:T(8,128)(2,1)S(1)} %get-tuple-element.55.own, bf16[3,128,512]{2,1,0:T(8,128)(2,1)S(1)} %collective-permute-done.near, bf16[3,32,512]{2,1,0:T(8,128)(2,1)S(1)} %get-tuple-element.96.edges, ...), custom_call_target="tpu_custom_call" | custom-call | flops 1000000 | bytes 1294360 | tf_op jit(solution)/shard_map/shift/pallas_call | solution.py:40
  34.9 2.0 %optics.1 = (f32[32,1280]{1,0:T(8,128)S(1)}, bf16[256,512]{1,0:T(8,128)(2,1)S(1)}, bf16[256,512]{1,0:T(8,128)(2,1)S(1)}, bf16[128,192]{1,0:T(8,128)(2,1)S(1)}) custom-call(f32[32,1280]{1,0:T(8,128)} %refs_0_, f32[128,128]{1,0:T(8,128)} %constant.6.clone.refs_1_, f32[256,512]{1,0:T(8,128)} %constant.7.clone.refs_2_, f32[128,64]{1,0:T(8,128)} %constant.8.clone.refs_3_), custom_call_target="tpu_custom_call" | custom-call | flops 30000000 | bytes 1523712 | tf_op jit(solution)/shard_map/optics/pallas_call | solution.py:40
  36.9 0.7 %collective-permute-done.14.refs_3_ = bf16[32,1280]{1,0:T(8,128)(2,1)S(1)} collective-permute-done((bf16[32,1280]{1,0:T(8,128)(2,1)S(1)}, bf16[32,1280]{1,0:T(8,128)(2,1)S(1)}, u32[]{:S(2)}, u32[]{:S(2)}) %collective-permute-start.14) | collective-permute-done | bytes 81952 | tf_op jit(solution)/shard_map/ppermute | solution.py:509
  37.6 1.7 %imaging.1 = f32[64,2560]{1,0:T(8,128)} custom-call(bf16[32,1280]{1,0:T(8,128)(2,1)S(1)} %get-tuple-element.99.refs_0_, bf16[32,1280]{1,0:T(8,128)(2,1)S(1)} %collective-permute-done.12.refs_1_, bf16[32,1280]{1,0:T(8,128)(2,1)S(1)} %collective-permute-done.13.refs_2_, bf16[32,1280]{1,0:T(8,128)(2,1)S(1)} %collective-permute-done.14.refs_3_, ...), custom_call_target="tpu_custom_call" | custom-call | flops 400000000 | bytes 1720320 | tf_op jit(solution)/shard_map/imaging/pallas_call | solution.py:40
  (9 shorter events, 0.0 us)
Async XLA Ops:
  1.9 8.8 %collective-permute-start = (bf16[3,128,512]{2,1,0:T(8,128)(2,1)S(1)}, bf16[3,128,512]{2,1,0:T(8,128)(2,1)S(1)}, u32[]{:S(2)}, u32[]{:S(2)}) collective-permute-start(bf16[3,128,512]{2,1,0:T(8,128)(2,1)S(1)} %get-tuple-element.55.own), channel_id=1, source_target_pairs={{0,1},{1,0},{2,3},{3,2},{4,5},{5,4},{6,7},{7,6},{8,9},{9,8},{10,11... | collective-permute-start | bytes 1179656 | tf_op jit(solution)/shard_map/ppermute | solution.py:413
  2.4 6.7 %collective-permute-start.2 = (bf16[3,128,128]{2,1,0:T(8,128)(2,1)S(1)}, bf16[3,128,128]{2,1,0:T(8,128)(2,1)S(1)}, u32[]{:S(2)}, u32[]{:S(2)}) collective-permute-start(bf16[3,128,128]{2,1,0:T(8,128)(2,1)S(1)} %get-tuple-element.57), channel_id=1, source_target_pairs={{0,3},{1,2},{2,1},{3,0},{4,7},{5,6},{6,5},{7,4},{8,11},{9,10},{10,... | collective-permute-start | bytes 294920 | tf_op jit(solution)/shard_map/ppermute | solution.py:413
  5.0 5.7 %collective-permute-start.1 = (bf16[3,128,128]{2,1,0:T(8,128)(2,1)S(1)}, bf16[3,128,128]{2,1,0:T(8,128)(2,1)S(1)}, u32[]{:S(2)}, u32[]{:S(2)}) collective-permute-start(bf16[3,128,128]{2,1,0:T(8,128)(2,1)S(1)} %get-tuple-element.56.keep), channel_id=1, source_target_pairs={{0,2},{1,3},{2,0},{3,1},{4,6},{5,7},{6,4},{7,5},{8,10},{9,11},{10,... | collective-permute-start | bytes 294920 | tf_op jit(solution)/shard_map/ppermute | solution.py:413
  5.1 9.8 %collective-permute-start.3 = (bf16[3,128,128]{2,1,0:T(8,128)(2,1)S(1)}, bf16[3,128,128]{2,1,0:T(8,128)(2,1)S(1)}, u32[]{:S(2)}, u32[]{:S(2)}) collective-permute-start(bf16[3,128,128]{2,1,0:T(8,128)(2,1)S(1)} %get-tuple-element.64), channel_id=1, source_target_pairs={{0,3},{1,2},{2,1},{3,0},{4,7},{5,6},{6,5},{7,4},{8,11},{9,10},{10,... | collective-permute-start | bytes 294920 | tf_op jit(solution)/shard_map/ppermute | solution.py:413
  6.4 8.5 %collective-permute-start.4 = (bf16[3,128,128]{2,1,0:T(8,128)(2,1)S(1)}, bf16[3,128,128]{2,1,0:T(8,128)(2,1)S(1)}, u32[]{:S(2)}, u32[]{:S(2)}) collective-permute-start(bf16[3,128,128]{2,1,0:T(8,128)(2,1)S(1)} %get-tuple-element.66.keep), channel_id=1, source_target_pairs={{0,2},{1,3},{2,0},{3,1},{4,6},{5,7},{6,4},{7,5},{8,10},{9,11},{10,... | collective-permute-start | bytes 294920 | tf_op jit(solution)/shard_map/ppermute | solution.py:413
  11.3 6.4 %collective-permute-start.6 = (bf16[3,128,128]{2,1,0:T(8,128)(2,1)S(1)}, bf16[3,128,128]{2,1,0:T(8,128)(2,1)S(1)}, u32[]{:S(2)}, u32[]{:S(2)}) collective-permute-start(bf16[3,128,128]{2,1,0:T(8,128)(2,1)S(1)} %get-tuple-element.83), channel_id=1, source_target_pairs={{0,4},{1,5},{2,6},{3,7},{4,0},{5,1},{6,2},{7,3},{8,12},{9,13},{10,... | collective-permute-start | bytes 294920 | tf_op jit(solution)/shard_map/ppermute | solution.py:417
  13.4 4.7 %collective-permute-start.7 = (bf16[3,128,128]{2,1,0:T(8,128)(2,1)S(1)}, bf16[3,128,128]{2,1,0:T(8,128)(2,1)S(1)}, u32[]{:S(2)}, u32[]{:S(2)}) collective-permute-start(bf16[3,128,128]{2,1,0:T(8,128)(2,1)S(1)} %get-tuple-element.84), channel_id=1, source_target_pairs={{0,5},{1,4},{2,7},{3,6},{4,1},{5,0},{6,3},{7,2},{8,13},{9,12},{10,... | collective-permute-start | bytes 294920 | tf_op jit(solution)/shard_map/ppermute | solution.py:417
  15.5 10.6 %collective-permute-start.8 = (bf16[3,128,128]{2,1,0:T(8,128)(2,1)S(1)}, bf16[3,128,128]{2,1,0:T(8,128)(2,1)S(1)}, u32[]{:S(2)}, u32[]{:S(2)}) collective-permute-start(bf16[3,128,128]{2,1,0:T(8,128)(2,1)S(1)} %get-tuple-element.90), channel_id=1, source_target_pairs={{0,4},{1,5},{2,6},{3,7},{4,0},{5,1},{6,2},{7,3},{8,12},{9,13},{10,... | collective-permute-start | bytes 294920 | tf_op jit(solution)/shard_map/ppermute | solution.py:417
  17.1 10.6 %collective-permute-start.11 = (bf16[3,128,128]{2,1,0:T(8,128)(2,1)S(1)}, bf16[3,128,128]{2,1,0:T(8,128)(2,1)S(1)}, u32[]{:S(2)}, u32[]{:S(2)}) collective-permute-start(bf16[3,128,128]{2,1,0:T(8,128)(2,1)S(1)} %get-tuple-element.94), channel_id=1, source_target_pairs={{0,5},{1,4},{2,7},{3,6},{4,1},{5,0},{6,3},{7,2},{8,13},{9,12},{10,... | collective-permute-start | bytes 294920 | tf_op jit(solution)/shard_map/ppermute | solution.py:417
  17.4 2.9 %collective-permute-start.5 = (bf16[3,160,256]{2,1,0:T(8,128)(2,1)S(1)}, bf16[3,160,256]{2,1,0:T(8,128)(2,1)S(1)}, u32[]{:S(2)}, u32[]{:S(2)}) collective-permute-start(bf16[3,160,256]{2,1,0:T(8,128)(2,1)S(1)} %get-tuple-element.79), channel_id=1, source_target_pairs={{0,1},{1,0},{2,3},{3,2},{4,5},{5,4},{6,7},{7,6},{8,9},{9,8},{10,11... | collective-permute-start | bytes 737288 | tf_op jit(solution)/shard_map/ppermute | solution.py:413
  21.3 6.4 %collective-permute-start.9 = (bf16[32,128]{1,0:T(8,128)(2,1)S(1)}, bf16[32,128]{1,0:T(8,128)(2,1)S(1)}, u32[]{:S(2)}, u32[]{:S(2)}) collective-permute-start(bf16[32,128]{1,0:T(8,128)(2,1)S(1)} %get-tuple-element.91), channel_id=1, source_target_pairs={{0,4},{4,8},{8,12},{12,16},{16,20},{20,24},{24,28},{28,0},{1,5},{5... | collective-permute-start | bytes 24584 | tf_op jit(solution)/shard_map/ppermute | solution.py:420
  22.4 5.3 %collective-permute-start.10 = (bf16[32,128]{1,0:T(8,128)(2,1)S(1)}, bf16[32,128]{1,0:T(8,128)(2,1)S(1)}, u32[]{:S(2)}, u32[]{:S(2)}) collective-permute-start(bf16[32,128]{1,0:T(8,128)(2,1)S(1)} %get-tuple-element.92), channel_id=1, source_target_pairs={{0,28},{4,0},{8,4},{12,8},{16,12},{20,16},{24,20},{28,24},{1,29},{... | collective-permute-start | bytes 24584 | tf_op jit(solution)/shard_map/ppermute | solution.py:420
  28.4 8.4 %collective-permute-start.12 = (bf16[32,1280]{1,0:T(8,128)(2,1)S(1)}, bf16[32,1280]{1,0:T(8,128)(2,1)S(1)}, u32[]{:S(2)}, u32[]{:S(2)}) collective-permute-start(bf16[32,1280]{1,0:T(8,128)(2,1)S(1)} %get-tuple-element.100), channel_id=1, source_target_pairs={{0,16},{4,20},{8,24},{12,28},{16,0},{20,4},{24,8},{28,12},{1,17},{... | collective-permute-start | bytes 245768 | tf_op jit(solution)/shard_map/ppermute | solution.py:509
  29.8 7.1 %collective-permute-start.13 = (bf16[32,1280]{1,0:T(8,128)(2,1)S(1)}, bf16[32,1280]{1,0:T(8,128)(2,1)S(1)}, u32[]{:S(2)}, u32[]{:S(2)}) collective-permute-start(bf16[32,1280]{1,0:T(8,128)(2,1)S(1)} %get-tuple-element.101), channel_id=1, source_target_pairs={{0,8},{4,12},{8,0},{12,4},{16,24},{20,28},{24,16},{28,20},{1,9},{5... | collective-permute-start | bytes 245768 | tf_op jit(solution)/shard_map/ppermute | solution.py:509
  31.2 6.3 %collective-permute-start.14 = (bf16[32,1280]{1,0:T(8,128)(2,1)S(1)}, bf16[32,1280]{1,0:T(8,128)(2,1)S(1)}, u32[]{:S(2)}, u32[]{:S(2)}) collective-permute-start(bf16[32,1280]{1,0:T(8,128)(2,1)S(1)} %get-tuple-element.102), channel_id=1, source_target_pairs={{0,24},{4,28},{8,16},{12,20},{16,8},{20,12},{24,0},{28,4},{1,25},{... | collective-permute-start | bytes 245768 | tf_op jit(solution)/shard_map/ppermute | solution.py:509

commit v7 on v6

--- a/solution.py
+++ b/solution.py
@@ -23,12 +23,14 @@
     return pltpu.CompilerParams(vmem_limit_bytes=held + 8 * 1024 * 1024)
 
 
-def call(kernel, out_shape, operands, flops, name, in_hbm=(), scratch=(), brief=False):
+def call(kernel, out_shape, operands, flops, name, in_hbm=(), out_hbm=(), aliases=None, scratch=(), brief=False):
     def spec(k, array):
         scalars = array.dtype == jnp.int32 and array.size < LANES
         return HBM_SPEC if scalars or k in in_hbm else VMEM_SPEC
 
-    out_specs = jax.tree.map(lambda _: VMEM_SPEC, out_shape)
+    count = len(jax.tree.leaves(out_shape))
+    out_specs = [HBM_SPEC if k in out_hbm else VMEM_SPEC for k in range(count)]
+    out_specs = jax.tree.unflatten(jax.tree.structure(out_shape), out_specs)
     size = sum(array.size * array.dtype.itemsize for array in jax.tree.leaves((operands, out_shape)))
     if brief:
         flops = size = 0
@@ -43,6 +45,7 @@
         in_specs=in_specs,
         out_specs=out_specs,
         scratch_shapes=list(scratch),
+        input_output_aliases=aliases or {},
         compiler_params=params(operands, out_shape),
         cost_estimate=pl.CostEstimate(flops=flops, bytes_accessed=size, transcendentals=0),
         name=name,
@@ -111,7 +114,8 @@
     column = lax.axis_index("layer")
     block = pupil_rows // n_layer
     row = lax.broadcasted_iota(jnp.int32, (half, LANES), 0)
-    pair = jnp.bitwise_xor(row // block, column // 2)
+    pair = row // block + column // 2
+    pair = jnp.where(pair >= n_layer // 2, pair - n_layer // 2, pair)
     parity = lax.rem(column, 2)
     inside = lax.rem(row, block) + pair * (2 * block)
     pixel_rows = stack(inside + parity * block, inside + (1 - parity) * block)
@@ -191,20 +195,60 @@
             out[level] = part[k * half : (k + 1) * half]
 
 
-def later_rows_kernel(rows_ref, keep, near, across, diagonal, across0, sibling0, mine, other, sibling_other, give):
+def outer_strip(wind, odd, own, near, far):
+    rows = own[0].shape[0]
+    core = lax.rem(lax.axis_index("dir"), 2)
+    lane = lax.broadcasted_iota(jnp.int32, (rows, LANES), 1)
+    strip = jnp.zeros((rows, LANES), jnp.float32)
+    for level in range(len(own)):
+        edges = stack(far[level][:16], far[level][rows - 16 :])
+        moved = shifted_rows(wind[0, level], odd, own[level], near[level], edges)
+        at = WIND_MAX * level
+        moved = pltpu.roll(moved, at + WIND_MAX * core, 1)
+        strip = jnp.where((lane >= at) & (lane < at + WIND_MAX), moved, strip)
+    return strip.T[:STRIP].astype(jnp.bfloat16)
+
+
+def put_strip(out, at, strip):
+    for k in range(strip.shape[1] // LANES):
+        out[at + k * STRIP : at + (k + 1) * STRIP, :] = strip[:, k * LANES : (k + 1) * LANES]
+
+
+def get_strip(ref, at):
+    return beside(*[ref[start : start + STRIP, :] for start in range(at, ref.shape[0], STRIP)])
+
+
+def later_rows_kernel(wind_hbm, rows_ref, *refs):
+    chunks, (near, sibling0), (mine, other, sibling_other, give, wind, sem) = refs[:6], refs[6:8], refs[8:]
+    load = fetch((wind_hbm, wind, sem))[0]
+    keep0, across0, diagonal0, keep, across, diagonal = chunks
     layers, half, width = mine.shape
-    rows = across.shape[1]
+    rows, cols = near.shape[1:]
     for level in range(layers):
         part = project_rows(1, rows_ref, keep, near, across, diagonal, level)
         mine[level] = part[:half]
-        other[level] = part[half : 2 * half]
-        sibling_other[level] = part[3 * half :]
+        other[level * half : (level + 1) * half] = part[half : 2 * half]
+        sibling_other[level * half : (level + 1) * half] = part[3 * half :]
         give[level, :half, :width] = sibling0[level]
         give[level, :half, width:] = part[2 * half : 3 * half]
         for k, block in enumerate((across0, across)):
             cut = slice(k * width, (k + 1) * width)
             give[level, half : half + 16, cut] = block[level, :16]
             give[level, half + 16 :, cut] = block[level, rows - 16 :]
+    core = lax.rem(lax.axis_index("dir"), 2)
+    start = pl.multiple_of(core * (cols - LANES), LANES)
+
+    def outer(first, second):
+        return [
+            jnp.where(core == 1, second[level].astype(jnp.float32), first[level].astype(jnp.float32))
+            for level in range(layers)
+        ]
+
+    own, far, sibling_far = outer(keep0, keep), outer(diagonal0, diagonal), outer(across0, across)
+    beyond = [near[level, :, pl.ds(start, LANES)] for level in range(layers)]
+    load.wait()
+    put_strip(other, layers * half, outer_strip(wind, core == 1, own, beyond, far))
+    put_strip(sibling_other, layers * half, outer_strip(wind, core == 0, beyond, own, sibling_far))
 
 
 def project(parts, cols_refs, at):
@@ -228,21 +272,33 @@
 
 
 def last_kernel(mine_ref, cols_ref, phase, taken, came, sibling_came, *outs):
-    layers, half, width = came.shape
+    *outs, partner_strips = outs
+    layers, _, width = taken.shape
+    width = width // 2
     size, pupil_cols = outs[0].shape
+    half = size * len(outs)
     parts, cuts = [], []
     for level in range(layers):
-        parts += [taken[level, :half], came[level], sibling_came[level]]
+        cut = slice(level * half, (level + 1) * half)
+        parts += [taken[level, :half], came[cut], sibling_came[cut]]
         cuts += [(mine_ref, level, 2 * width, 4 * width)]
         cuts += [(cols_ref, level, width, 2 * width), (cols_ref, level, 3 * width, 4 * width)]
     for at in range(0, pupil_cols, 256):
         total = (phase[:, at : at + 256] + project(parts, cuts, at)).astype(jnp.bfloat16)
         for k, out in enumerate(outs):
             out[:, at : at + 256] = total[k * size : (k + 1) * size]
-
-
-def shifted_rows(shift, own, near, edges):
     odd = lax.rem(lax.axis_index("dir"), 2) == 1
+    here = get_strip(came, layers * half).astype(jnp.float32)
+    there = get_strip(sibling_came, layers * half).astype(jnp.float32)
+    last = jnp.where(odd, here, there).astype(jnp.bfloat16)
+    first = jnp.where(odd, there, here).astype(jnp.bfloat16)
+    outs[1][:, pupil_cols:] = last
+    outs[-1][:, pupil_cols:] = first
+    partner_strips[:STRIP] = last
+    partner_strips[STRIP:] = first
+
+
+def shifted_rows(shift, odd, own, near, edges):
     own, near, edges = [block.astype(jnp.float32) for block in (own, near, edges)]
     rows = own.shape[0]
     before = jnp.where(odd, near[rows - 16 :], edges[16:])
@@ -251,50 +307,46 @@
     return pltpu.roll(stack(before, own, after), shift, 0)[16 : 16 + rows]
 
 
-def strips_kernel(wind_hbm, own, near, diagonal0, diagonal1, taken, right, left, edges, wind, sem):
+def shift_kernel(wind_hbm, own, near, diagonal0, diagonal1, taken, whole, ends, wind, sem, out):
     load = fetch((wind_hbm, wind, sem))[0]
-    layers, rows, width = own.shape
+    layers, rows, cols = own.shape
     odd = lax.rem(lax.axis_index("dir"), 2) == 1
     half = taken.shape[1] - 32
-    lane = lax.broadcasted_iota(jnp.int32, (rows, LANES), 1)
-    strips = jnp.zeros((rows, LANES), jnp.float32)
+    load.wait()
     for level in range(layers):
         chunks = [stack(part[level, :16], part[level, rows - 16 :]) for part in (diagonal0, diagonal1)]
         here = beside(*chunks).astype(jnp.float32)
         there = taken[level, half:].astype(jnp.float32)
-        both = beside(jnp.where(odd, there, here), jnp.where(odd, here, there))
-        edges[level] = both.astype(jnp.bfloat16)
-    load.wait()
-    for level in range(layers):
-        shift = wind[0, level]
-        at = WIND_MAX * level
-        cut = slice(width - LANES, width)
-        last = shifted_rows(shift, own[level, :, cut], near[level, :, cut], edges[level, :, cut])
-        strips = jnp.where((lane >= at) & (lane < at + WIND_MAX), pltpu.roll(last, WIND_MAX + at, 1), strips)
-        at = STRIP + WIND_MAX * level
-        cut = slice(0, LANES)
-        initial = shifted_rows(shift, own[level, :, cut], near[level, :, cut], edges[level, :, cut])
-        strips = jnp.where((lane >= at) & (lane < at + WIND_MAX), pltpu.roll(initial, at, 1), strips)
-    strips = strips.T.astype(jnp.bfloat16)
-    right[...] = strips[:STRIP]
-    left[...] = strips[STRIP : 2 * STRIP]
-
-
-def shift_kernel(wind_hbm, own, near, edges, from_left, from_right, out, wind, sem):
-    load = fetch((wind_hbm, wind, sem))[0]
-    layers, rows, cols = own.shape
-    strips = stack(from_left[...], from_right[...], jnp.zeros((LANES - 2 * STRIP, rows), jnp.bfloat16))
+        edges = beside(jnp.where(odd, there, here), jnp.where(odd, here, there))
+        moved = shifted_rows(wind[0, level], odd, own[level], near[level], edges)
+        shift = wind[1, level]
+        moved = pltpu.roll(moved, jnp.where(shift < 0, shift + cols, shift), 1).astype(jnp.bfloat16)
+        out[level] = moved
+        ends[0, level] = moved[:, :LANES]
+        ends[1, level] = moved[:, cols - LANES :]
+    copy = pltpu.make_async_copy(out, whole, sem)
+    copy.start()
+    copy.wait()
+
+
+def patch_ends(wind, ends, partner_strips, below, above, out):
+    _, layers, rows, _ = ends.shape
+    second = lax.rem(lax.axis_index("layer"), 2) == 1
+    at = below.shape[1] - rows
+    strips = stack(partner_strips[:STRIP], below[:, at:], partner_strips[STRIP:], above[:, at:])
     strips = strips.astype(jnp.float32).T
     lane = lax.broadcasted_iota(jnp.int32, (rows, LANES), 1)
-    load.wait()
-    for level in range(layers):
-        last = pltpu.roll(strips, LANES - WIND_MAX * (level + 1), 1)
-        first = pltpu.roll(strips, LANES - STRIP - WIND_MAX * level, 1)
-        extra = jnp.where(lane < WIND_MAX, first, last)
-        moved = shifted_rows(wind[0, level], own[level], near[level], edges[level])
+    left = jnp.where(second, 0, STRIP)
+    right = jnp.where(second, 3 * STRIP, 2 * STRIP)
+    for level in range(layers):
         shift = wind[1, level]
-        shift = jnp.where(shift < 0, shift + cols + LANES, shift)
-        out[level] = pltpu.roll(beside(moved, extra), shift, 1)[:, :cols].astype(jnp.bfloat16)
+        at = WIND_MAX * (level + 1)
+        value = pltpu.roll(strips, lax.rem(2 * LANES - at - left + shift, LANES), 1)
+        out[0, level] = jnp.where(lane < shift, value, ends[0, level].astype(jnp.float32)).astype(jnp.bfloat16)
+        at = WIND_MAX * level
+        value = pltpu.roll(strips, lax.rem(2 * LANES - at - right + shift, LANES), 1)
+        kept = ends[1, level].astype(jnp.float32)
+        out[1, level] = jnp.where(lane >= LANES + shift, value, kept).astype(jnp.bfloat16)
 
 
 def optics_kernel(*refs):
@@ -339,14 +391,15 @@
     return high, low
 
 
-def imaging_kernel(count, *refs):
-    parts = refs[:count]
-    amp_ref, cols_high, cols_low, rows_table, out = refs[count:]
+def imaging_kernel(count, wind_hbm, *refs):
+    parts, refs = refs[:count], refs[count:]
+    amp_ref, cols_high, cols_low, rows_table, ends, partner_strips, _, out, screens, wind, patched, sems = refs
+    load = fetch((wind_hbm, wind, sems.at[0]))[0]
     rows, cols = amp_ref.shape
     tiles = cols // LANES
-    phase = parts[0][...].astype(jnp.float32)
+    phase = parts[0][:, :cols].astype(jnp.float32)
     for part in parts[1:]:
-        phase = phase + part[...].astype(jnp.float32)
+        phase = phase + part[:, :cols].astype(jnp.float32)
     sine, cosine = sin_cos(phase)
     amp = amp_ref[...]
     real, imag = amp * cosine, amp * sine
@@ -361,6 +414,13 @@
     )
     high, low = split(field)
     half = dot(high, cols_high[...]) + (dot(low, cols_high[...]) + dot(high, cols_low[...]))
+    load.wait()
+    patch_ends(wind, ends, partner_strips, parts[1], parts[-1], patched)
+    width = screens.shape[2]
+    copies = fetch(
+        (patched.at[0], screens.at[:, :, :LANES], sems.at[1]),
+        (patched.at[1], screens.at[:, :, width - LANES :], sems.at[2]),
+    )
     wide = 2 * LANES
     out_rows = 2 * rows
     for t in range(tiles):
@@ -370,6 +430,8 @@
         full = dot(rows_table[...], jnp.concatenate([high, low, high], axis=0))
         real, imag = full[:out_rows], full[out_rows:]
         out[:, t * wide : (t + 1) * wide] = real * real + imag * imag
+    for copy in copies:
+        copy.wait()
 
 
 def tables_of(rows):
@@ -466,12 +528,14 @@
         columns_kernel, shape(layers, cols_dev, pupil_cols), tables, 0, "columns", brief=True
     )
     cols, sibling0 = lax.optimization_barrier((cols, sibling0))
+    message = shape(layers * half + STRIP * rows_dev // LANES, width)
     mine1, other1, sibling_other1, give = call(
         later_rows_kernel,
-        [projected] * 3 + [shape(layers, half + 32, 2 * width)],
-        (row_weights, keep1, near, across1, diagonal1, across0, sibling0),
+        [projected, message, message, shape(layers, half + 32, 2 * width)],
+        (wind, row_weights, keep0, across0, diagonal0, keep1, across1, diagonal1, near, sibling0),
         0,
         "rows_later",
+        scratch=wind_scratch,
         brief=True,
     )
     came1 = partner(other1)
@@ -485,35 +549,10 @@
         10_000_000_000,
         "phase",
     )
-    taken, phase = lax.optimization_barrier((taken, phase))
-    right, left, edges = call(
-        strips_kernel,
-        [shape(STRIP, rows_dev)] * 2 + [shape(layers, 32, cols_dev)],
-        (wind, own, near, diagonal0, diagonal1, taken),
-        0,
-        "strips",
-        scratch=wind_scratch,
-        brief=True,
-    )
-    from_left = turn(right, 1)
-    from_right = turn(left, n_layer - 1)
-    came1, from_left, from_right = lax.optimization_barrier((came1, from_left, from_right))
-    sums = call(
-        last_kernel,
-        [shape(rows, pupil_cols)] * pairs,
-        (cols, others, phase, taken, came1, sibling_came1),
-        300_000_000,
-        "last",
-    )
-    received = [sums[0]] + [
-        lax.ppermute(sums[k], "layer", [(i, i ^ (2 * k)) for i in range(n_layer)])
-        for k in sorted(range(1, pairs), key=lambda k: -(k & -k))
-    ]
 
     ones = np.kron(np.eye(LANES // SUB_PIX), np.ones((SUB_PIX, SUB_PIX))).astype(np.float32)
     columns, lines = tables_of(rows)
-    amplitude, edges, first = lax.optimization_barrier((amplitude, edges, sums[0]))
-    received[0] = first
+    amplitude, phase = lax.optimization_barrier((amplitude, phase))
     optics_in = (amplitude, jnp.asarray(ones), jnp.asarray(columns), jnp.asarray(lines))
     optics = call(
         optics_kernel,
@@ -529,20 +568,39 @@
         in_hbm=range(4),
         scratch=[pltpu.VMEM(array.shape, f32) for array in optics_in] + [sem((4,))],
     )
-    new_screens = call(
+    phase, optics = lax.optimization_barrier((phase, optics))
+    extra = [rows_dev if k in (1, pairs - 1) else 0 for k in range(pairs)]
+    *sums, strips = call(
+        last_kernel,
+        [shape(rows, pupil_cols + more) for more in extra] + [shape(2 * STRIP, rows_dev)],
+        (cols, others, phase, taken, came1, sibling_came1),
+        300_000_000,
+        "last",
+    )
+    received = [sums[0]] + [None] * (pairs - 1)
+    for k in sorted(range(1, pairs), key=lambda k: -min(k, pairs - k)):
+        received[k] = turn(sums[k], 2 * k)
+
+    diagonal0, strips = lax.optimization_barrier((diagonal0, strips))
+    shifted, ends = call(
         shift_kernel,
-        shape(layers, rows_dev, cols_dev),
-        (wind, own, near, edges, from_left, from_right),
+        [shape(layers, rows_dev, cols_dev), shape(2, layers, rows_dev, LANES)],
+        (wind, own, near, diagonal0, diagonal1, taken),
         1_000_000,
         "shift",
-        scratch=wind_scratch,
-    )
-    spots = call(
+        scratch=wind_scratch + [pltpu.VMEM(own.shape, bf16)],
+        out_hbm=(0,),
+    )
+    spots, new_screens = call(
         functools.partial(imaging_kernel, pairs),
-        shape(2 * rows, 2 * pupil_cols, dtype=f32),
-        (*received, *optics),
+        [shape(2 * rows, 2 * pupil_cols, dtype=f32), shape(layers, rows_dev, cols_dev)],
+        (wind, *received, *optics, ends, strips, shifted),
         400_000_000,
         "imaging",
+        in_hbm=(pairs + 7,),
+        out_hbm=(1,),
+        aliases={pairs + 7: 1},
+        scratch=[wind_scratch[0], pltpu.VMEM(ends.shape, bf16), sem((3,))],
     )
     return (new_screens, spots[None])
 

time: 39.9 us -> 39.8 us (level)
  starting transfers between devices: 18.7 us -> 14.6 us
  waiting for transfers between devices: 4.37 us -> 7.82 us
  Pallas kernels: 15.4 us -> 16.4 us
    ppermute x3 -> x0, starting transfers between devices: 4.45 us -> none  [per_device(): lax.ppermute(sums[k], 'layer', [(i, i ^ 2 * k) for i in range(n_layer)])]
    ppermute x2 -> x3, waiting for transfers between devices: 1.62 us -> 5.45 us  [turn(): lax.ppermute(value, 'layer', [(i, (i + step) % n_layer) for i in range(n_...]
    pallas_call x11 -> x10, Pallas kernels: 15.4 us -> 16.4 us  [call(): pl.pallas_call(kernel, out_shape=out_shape, in_specs=in_specs, out_specs=...]
    ppermute x3 -> x0, waiting for transfers between devices: 0.71 us -> none  [per_device(): lax.ppermute(sums[k], 'layer', [(i, i ^ 2 * k) for i in range(n_layer)])]
    ppermute x2 -> x3, starting transfers between devices: 4.78 us -> 5.14 us  [turn(): lax.ppermute(value, 'layer', [(i, (i + step) % n_layer) for i in range(n_...]
  transfers between devices with their start and end apart: 15 -> 13, of which waited for: 4 -> 3; matrix products, arithmetic and copies ran while one was open for 0% -> 0% of each run, Pallas kernels for 30% -> 29%
where the time goes in v7:
time: 39.8 us; the launch traced here: 39.6 us
  Pallas kernels  16.4 us (41%)
  starting transfers between devices  14.6 us (37%)
  waiting for transfers between devices  7.82 us (20%)
  between operations  0.74 us (2%)
    pallas_call x10, Pallas kernels, call(): pl.pallas_call(kernel, out_shape=out_shape, in_specs=in_specs, out_specs=...  16.4 us
    ppermute x6, starting transfers between devices, swap(): return lax.ppermute(value, 'dir', [(i, i ^ bits) for i in range(n_dir)])  5.51 us
    ppermute x3, waiting for transfers between devices, turn(): lax.ppermute(value, 'layer', [(i, (i + step) % n_layer) for i in range(n_...  5.45 us
    ppermute x3, starting transfers between devices, turn(): lax.ppermute(value, 'layer', [(i, (i + step) % n_layer) for i in range(n_...  5.14 us
    ppermute x4, starting transfers between devices, partner(): lax.ppermute(value, ('layer', 'dir'), [(i, i ^ n_dir ^ bits) for i in ran...  3.99 us
    ppermute x6, waiting for transfers between devices, swap(): return lax.ppermute(value, 'dir', [(i, i ^ bits) for i in range(n_dir)])  1.61 us
  transfers between devices with their start and end apart: 13, of which 3 were waited for; matrix products, arithmetic and copies ran while one was open for 0% of the time, Pallas kernels for 29%

profile of v7, /device:TPU:0, one launch (start us, length us, event | category | flops | bytes accessed | tf_op | source)
XLA Modules:
  0.0 39.6 jit_solution(17865586557910022199)
XLA Ops:
  0.6 1.3 %split.1 = (bf16[3,128,512]{2,1,0:T(8,128)(2,1)S(1)}, bf16[3,128,128]{2,1,0:T(8,128)(2,1)S(1)}, bf16[3,128,128]{2,1,0:T(8,128)(2,1)S(1)}, bf16[3,128,128]{2,1,0:T(8,128)(2,1)S(1)}, bf16[3,128,128]{2,1,0:T(8,128)(2,1)S(1)}) custom-call(bf16[3,128,512]{2,1,0:T(8,128)(2,1)} %screens.1), custom_call_target="tpu_custom_call" | custom-call | tf_op jit(solution)/shard_map/split/pallas_call | solution.py:42
  1.9 0.5 %collective-permute-start.2 = (bf16[3,128,512]{2,1,0:T(8,128)(2,1)S(1)}, bf16[3,128,512]{2,1,0:T(8,128)(2,1)S(1)}, u32[]{:S(2)}, u32[]{:S(2)}) collective-permute-start(bf16[3,128,512]{2,1,0:T(8,128)(2,1)S(1)} %get-tuple-element.70.own), channel_id=1, source_target_pairs={{0,1},{1,0},{2,3},{3,2},{4,5},{5,4},{6,7},{7,6},{8,9},{9,8},{10,11... | collective-permute-start | bytes 1179656 | tf_op jit(solution)/shard_map/ppermute | solution.py:475
  2.4 2.6 %collective-permute-start.1 = (bf16[3,128,128]{2,1,0:T(8,128)(2,1)S(1)}, bf16[3,128,128]{2,1,0:T(8,128)(2,1)S(1)}, u32[]{:S(2)}, u32[]{:S(2)}) collective-permute-start(bf16[3,128,128]{2,1,0:T(8,128)(2,1)S(1)} %get-tuple-element.59), channel_id=1, source_target_pairs={{0,3},{1,2},{2,1},{3,0},{4,7},{5,6},{6,5},{7,4},{8,11},{9,10},{10,... | collective-permute-start | bytes 294920 | tf_op jit(solution)/shard_map/ppermute | solution.py:475
  5.0 0.0 collective-permute-start
  5.1 1.4 %collective-permute-start.4 = (bf16[3,128,128]{2,1,0:T(8,128)(2,1)S(1)}, bf16[3,128,128]{2,1,0:T(8,128)(2,1)S(1)}, u32[]{:S(2)}, u32[]{:S(2)}) collective-permute-start(bf16[3,128,128]{2,1,0:T(8,128)(2,1)S(1)} %get-tuple-element.82), channel_id=1, source_target_pairs={{0,3},{1,2},{2,1},{3,0},{4,7},{5,6},{6,5},{7,4},{8,11},{9,10},{10,... | collective-permute-start | bytes 294920 | tf_op jit(solution)/shard_map/ppermute | solution.py:475
  6.4 0.6 %collective-permute-start.3 = (bf16[3,128,128]{2,1,0:T(8,128)(2,1)S(1)}, bf16[3,128,128]{2,1,0:T(8,128)(2,1)S(1)}, u32[]{:S(2)}, u32[]{:S(2)}) collective-permute-start(bf16[3,128,128]{2,1,0:T(8,128)(2,1)S(1)} %get-tuple-element.81.refs_3_), channel_id=1, source_target_pairs={{0,2},{1,3},{2,0},{3,1},{4,6},{5,7},{6,4},{7,5},{8,10},{9,11},{10,... | collective-permute-start | bytes 294920 | tf_op jit(solution)/shard_map/ppermute | solution.py:475
  7.1 2.0 %weights.1 = (bf16[2,3,256,512]{3,2,1,0:T(8,128)(2,1)S(1)}, s32[8,1280]{1,0:T(8,128)S(1)}, s32[8,1280]{1,0:T(8,128)S(1)}, f32[8,1280]{1,0:T(8,128)S(1)}, f32[8,1280]{1,0:T(8,128)S(1)}) custom-call(s32[2,3]{1,0:T(2,128)} %bitcast.4, s32[3,2,4]{2,1,0:T(2,128)} %bitcast.8, s32[3,2,4]{2,1,0:T(2,128)} %bitcast.9), custom_call_target="tpu_custom_call" | custom-call | tf_op jit(solution)/shard_map/weights/pallas_call | solution.py:42
  9.1 0.0 collective-permute-done.1.diagonal.refs_2_.diagonal0
  9.1 1.6 %collective-permute-done.across.refs_1_ = bf16[3,128,128]{2,1,0:T(8,128)(2,1)S(1)} collective-permute-done((bf16[3,128,128]{2,1,0:T(8,128)(2,1)S(1)}, bf16[3,128,128]{2,1,0:T(8,128)(2,1)S(1)}, u32[]{:S(2)}, u32[]{:S(2)}) %collective-permute-start) | collective-permute-done | bytes 98336 | tf_op jit(solution)/shard_map/ppermute | solution.py:475
  10.7 0.0 collective-permute-done.2.near.refs_6_
  10.7 0.6 %rows_first.1 = (bf16[3,128,128]{2,1,0:T(8,128)(2,1)S(1)}, bf16[3,128,128]{2,1,0:T(8,128)(2,1)S(1)}, bf16[3,128,128]{2,1,0:T(8,128)(2,1)S(1)}, bf16[3,128,128]{2,1,0:T(8,128)(2,1)S(1)}) custom-call(bf16[2,3,256,512]{3,2,1,0:T(8,128)(2,1)S(1)} %get-tuple-element.69.rows_ref, bf16[3,128,128]{2,1,0:T(8,128)(2,1)S(1)} %get-tuple-element.58.keep.refs_0_, ...), custom_call_target="tpu_custom_call" | custom-call | tf_op jit(solution)/shard_map/rows_first/pallas_call | solution.py:42
  11.3 2.1 %collective-permute-start.5 = (bf16[3,128,128]{2,1,0:T(8,128)(2,1)S(1)}, bf16[3,128,128]{2,1,0:T(8,128)(2,1)S(1)}, u32[]{:S(2)}, u32[]{:S(2)}) collective-permute-start(bf16[3,128,128]{2,1,0:T(8,128)(2,1)S(1)} %get-tuple-element.85), channel_id=1, source_target_pairs={{0,4},{1,5},{2,6},{3,7},{4,0},{5,1},{6,2},{7,3},{8,12},{9,13},{10,... | collective-permute-start | bytes 294920 | tf_op jit(solution)/shard_map/ppermute | solution.py:479
  13.4 0.0 collective-permute-start.6
  13.4 1.5 %columns.1.refs_4_.mine_ref = bf16[3,512,1280]{2,1,0:T(8,128)(2,1)S(1)} custom-call(s32[8,1280]{1,0:T(8,128)S(1)} %get-tuple-element.74.refs_0_, s32[8,1280]{1,0:T(8,128)S(1)} %get-tuple-element.75.refs_1_, f32[8,1280]{1,0:T(8,128)S(1)} %get-tuple-element.76.refs_2_, f32[8,1280]{1,0:T(8,128)S(1)} %get-tuple-element.77.refs_3_), custom_call_target="tpu_custom_call" | custom-call | tf_op jit(solution)/shard_map/columns/pallas_call | solution.py:42
  14.9 0.0 collective-permute-done.4.refs_5_.diagonal1
  14.9 0.0 collective-permute-done.3.refs_4_
  14.9 1.5 %rows_later.1 = (bf16[3,128,128]{2,1,0:T(8,128)(2,1)S(1)}, bf16[416,128]{1,0:T(8,128)(2,1)S(1)}, bf16[416,128]{1,0:T(8,128)(2,1)S(1)}, bf16[3,160,256]{2,1,0:T(8,128)(2,1)S(1)}) custom-call(s32[2,3]{1,0:T(2,128)} %bitcast.5, bf16[2,3,256,512]{3,2,1,0:T(8,128)(2,1)S(1)} %get-tuple-element.69.rows_ref, ...), custom_call_target="tpu_custom_call" | custom-call | tf_op jit(solution)/shard_map/rows_later/pallas_call | solution.py:42
  16.4 1.6 %collective-permute-start.8 = (bf16[416,128]{1,0:T(8,128)(2,1)S(1)}, bf16[416,128]{1,0:T(8,128)(2,1)S(1)}, u32[]{:S(2)}, u32[]{:S(2)}) collective-permute-start(bf16[416,128]{1,0:T(8,128)(2,1)S(1)} %get-tuple-element.97), channel_id=1, source_target_pairs={{0,4},{1,5},{2,6},{3,7},{4,0},{5,1},{6,2},{7,3},{8,12},{9,13},{10,... | collective-permute-start | bytes 319496 | tf_op jit(solution)/shard_map/ppermute | solution.py:479
  18.0 0.3 collective-permute-start.9
  18.3 0.3 collective-permute-start.7
  18.6 0.0 collective-permute-done.5.refs_7_
  18.6 2.1 %phase.1 = (f32[128,1280]{1,0:T(8,128)S(1)}, bf16[3,512,1280]{2,1,0:T(8,128)(2,1)S(1)}) custom-call(s32[8,1280]{1,0:T(8,128)S(1)} %get-tuple-element.74.refs_0_, s32[8,1280]{1,0:T(8,128)S(1)} %get-tuple-element.75.refs_1_, f32[8,1280]{1,0:T(8,128)S(1)} %get-tuple-element.76.refs_2_, f32[8,1280]{1,0:T(8,128)S(1)} %get-tuple-element.77.refs_3_, ...), custom_call_target="tpu_custom_call" | custom-call | flops 10000000000 | bytes 9076736 | tf_op jit(solution)/shard_map/phase/pallas_call | solution.py:42
  20.7 2.0 %optics.1 = (f32[32,1280]{1,0:T(8,128)S(1)}, bf16[256,512]{1,0:T(8,128)(2,1)S(1)}, bf16[256,512]{1,0:T(8,128)(2,1)S(1)}, bf16[128,192]{1,0:T(8,128)(2,1)S(1)}) custom-call(f32[32,1280]{1,0:T(8,128)} %refs_0_, f32[128,128]{1,0:T(8,128)} %constant.6.clone.refs_1_, f32[256,512]{1,0:T(8,128)} %constant.7.clone.refs_2_, f32[128,64]{1,0:T(8,128)} %constant.8.clone.refs_3_), custom_call_target="tpu_custom_call" | custom-call | flops 30000000 | bytes 1523712 | tf_op jit(solution)/shard_map/optics/pallas_call | solution.py:42
  22.7 0.8 %collective-permute-done.9.sibling_came = bf16[416,128]{1,0:T(8,128)(2,1)S(1)} collective-permute-done((bf16[416,128]{1,0:T(8,128)(2,1)S(1)}, bf16[416,128]{1,0:T(8,128)(2,1)S(1)}, u32[]{:S(2)}, u32[]{:S(2)}) %collective-permute-start.9) | collective-permute-done | bytes 106528 | tf_op jit(solution)/shard_map/ppermute | solution.py:479
  23.5 0.7 %last.1 = (bf16[32,1280]{1,0:T(8,128)(2,1)S(1)}, bf16[32,1408]{1,0:T(8,128)(2,1)S(1)}, bf16[32,1280]{1,0:T(8,128)(2,1)S(1)}, bf16[32,1408]{1,0:T(8,128)(2,1)S(1)}, bf16[64,128]{1,0:T(8,128)(2,1)S(1)}) custom-call(bf16[3,512,1280]{2,1,0:T(8,128)(2,1)S(1)} %columns.1.refs_4_.mine_ref, bf16[3,512,1280]{2,1,0:T(8,128)(2,1)S(1)} %get-tuple-element.87.cols_ref, ...), custom_call_target="tpu_custom_call" | custom-call | flops 300000000 | bytes 9338880 | tf_op jit(solution)/shard_map/last/pallas_call | solution.py:42
  24.2 2.1 %collective-permute-start.10 = (bf16[32,1408]{1,0:T(8,128)(2,1)S(1)}, bf16[32,1408]{1,0:T(8,128)(2,1)S(1)}, u32[]{:S(2)}, u32[]{:S(2)}) collective-permute-start(bf16[32,1408]{1,0:T(8,128)(2,1)S(1)} %get-tuple-element.100), channel_id=1, source_target_pairs={{0,8},{4,12},{8,16},{12,20},{16,24},{20,28},{24,0},{28,4},{1,9},{5... | collective-permute-start | bytes 270344 | tf_op jit(solution)/shard_map/ppermute | solution.py:482
  26.3 2.1 %collective-permute-start.12 = (bf16[32,1408]{1,0:T(8,128)(2,1)S(1)}, bf16[32,1408]{1,0:T(8,128)(2,1)S(1)}, u32[]{:S(2)}, u32[]{:S(2)}) collective-permute-start(bf16[32,1408]{1,0:T(8,128)(2,1)S(1)} %get-tuple-element.102), channel_id=1, source_target_pairs={{0,24},{4,28},{8,0},{12,4},{16,8},{20,12},{24,16},{28,20},{1,25},{... | collective-permute-start | bytes 270344 | tf_op jit(solution)/shard_map/ppermute | solution.py:482
  28.4 0.9 %collective-permute-start.11 = (bf16[32,1280]{1,0:T(8,128)(2,1)S(1)}, bf16[32,1280]{1,0:T(8,128)(2,1)S(1)}, u32[]{:S(2)}, u32[]{:S(2)}) collective-permute-start(bf16[32,1280]{1,0:T(8,128)(2,1)S(1)} %get-tuple-element.101), channel_id=1, source_target_pairs={{0,16},{4,20},{8,24},{12,28},{16,0},{20,4},{24,8},{28,12},{1,17},{... | collective-permute-start | bytes 245768 | tf_op jit(solution)/shard_map/ppermute | solution.py:482
  29.3 1.9 %shift.1 = (bf16[3,128,512]{2,1,0:T(8,128)(2,1)}, bf16[2,3,128,128]{3,2,1,0:T(8,128)(2,1)S(1)}) custom-call(s32[2,3]{1,0:T(2,128)} %bitcast.6, bf16[3,128,512]{2,1,0:T(8,128)(2,1)S(1)} %get-tuple-element.70.own, bf16[3,128,512]{2,1,0:T(8,128)(2,1)S(1)} %collective-permute-done.2.near.refs_6_, ...), custom_call_target="tpu_custom_call" | custom-call | flops 1000000 | bytes 1818648 | tf_op jit(solution)/shard_map/shift/pallas_call | solution.py:42
  31.2 5.4 %collective-permute-done.11.refs_2_ = bf16[32,1280]{1,0:T(8,128)(2,1)S(1)} collective-permute-done((bf16[32,1280]{1,0:T(8,128)(2,1)S(1)}, bf16[32,1280]{1,0:T(8,128)(2,1)S(1)}, u32[]{:S(2)}, u32[]{:S(2)}) %collective-permute-start.11) | collective-permute-done | bytes 81952 | tf_op jit(solution)/shard_map/ppermute | solution.py:482
  36.7 0.0 collective-permute-done.12.refs_3_
  36.7 2.9 %imaging.1 = (f32[64,2560]{1,0:T(8,128)}, bf16[3,128,512]{2,1,0:T(8,128)(2,1)}) custom-call(s32[2,3]{1,0:T(2,128)} %bitcast.7, bf16[32,1280]{1,0:T(8,128)(2,1)S(1)} %get-tuple-element.99.refs_0_, bf16[32,1408]{1,0:T(8,128)(2,1)S(1)} %collective-permute-done.10.refs_1_, ...), custom_call_target="tpu_custom_call", output_to_operand_aliasing={{1}: (11, {})} | custom-call | flops 400000000 | bytes 2736152 | tf_op jit(solution)/shard_map/imaging/pallas_call | solution.py:42
  (4 shorter events, 0.0 us)
Async XLA Ops:
  1.9 8.8 %collective-permute-start.2 = (bf16[3,128,512]{2,1,0:T(8,128)(2,1)S(1)}, bf16[3,128,512]{2,1,0:T(8,128)(2,1)S(1)}, u32[]{:S(2)}, u32[]{:S(2)}) collective-permute-start(bf16[3,128,512]{2,1,0:T(8,128)(2,1)S(1)} %get-tuple-element.70.own), channel_id=1, source_target_pairs={{0,1},{1,0},{2,3},{3,2},{4,5},{5,4},{6,7},{7,6},{8,9},{9,8},{10,11... | collective-permute-start | bytes 1179656 | tf_op jit(solution)/shard_map/ppermute | solution.py:475
  2.4 6.7 %collective-permute-start.1 = (bf16[3,128,128]{2,1,0:T(8,128)(2,1)S(1)}, bf16[3,128,128]{2,1,0:T(8,128)(2,1)S(1)}, u32[]{:S(2)}, u32[]{:S(2)}) collective-permute-start(bf16[3,128,128]{2,1,0:T(8,128)(2,1)S(1)} %get-tuple-element.59), channel_id=1, source_target_pairs={{0,3},{1,2},{2,1},{3,0},{4,7},{5,6},{6,5},{7,4},{8,11},{9,10},{10,... | collective-permute-start | bytes 294920 | tf_op jit(solution)/shard_map/ppermute | solution.py:475
  5.0 5.7 %collective-permute-start = (bf16[3,128,128]{2,1,0:T(8,128)(2,1)S(1)}, bf16[3,128,128]{2,1,0:T(8,128)(2,1)S(1)}, u32[]{:S(2)}, u32[]{:S(2)}) collective-permute-start(bf16[3,128,128]{2,1,0:T(8,128)(2,1)S(1)} %get-tuple-element.58.keep.refs_0_), channel_id=1, source_target_pairs={{0,2},{1,3},{2,0},{3,1},{4,6},{5,7},{6,4},{7,5},{8,10},{9,11},{10,... | collective-permute-start | bytes 294920 | tf_op jit(solution)/shard_map/ppermute | solution.py:475
  5.1 9.8 %collective-permute-start.4 = (bf16[3,128,128]{2,1,0:T(8,128)(2,1)S(1)}, bf16[3,128,128]{2,1,0:T(8,128)(2,1)S(1)}, u32[]{:S(2)}, u32[]{:S(2)}) collective-permute-start(bf16[3,128,128]{2,1,0:T(8,128)(2,1)S(1)} %get-tuple-element.82), channel_id=1, source_target_pairs={{0,3},{1,2},{2,1},{3,0},{4,7},{5,6},{6,5},{7,4},{8,11},{9,10},{10,... | collective-permute-start | bytes 294920 | tf_op jit(solution)/shard_map/ppermute | solution.py:475
  6.4 8.5 %collective-permute-start.3 = (bf16[3,128,128]{2,1,0:T(8,128)(2,1)S(1)}, bf16[3,128,128]{2,1,0:T(8,128)(2,1)S(1)}, u32[]{:S(2)}, u32[]{:S(2)}) collective-permute-start(bf16[3,128,128]{2,1,0:T(8,128)(2,1)S(1)} %get-tuple-element.81.refs_3_), channel_id=1, source_target_pairs={{0,2},{1,3},{2,0},{3,1},{4,6},{5,7},{6,4},{7,5},{8,10},{9,11},{10,... | collective-permute-start | bytes 294920 | tf_op jit(solution)/shard_map/ppermute | solution.py:475
  11.3 7.3 %collective-permute-start.5 = (bf16[3,128,128]{2,1,0:T(8,128)(2,1)S(1)}, bf16[3,128,128]{2,1,0:T(8,128)(2,1)S(1)}, u32[]{:S(2)}, u32[]{:S(2)}) collective-permute-start(bf16[3,128,128]{2,1,0:T(8,128)(2,1)S(1)} %get-tuple-element.85), channel_id=1, source_target_pairs={{0,4},{1,5},{2,6},{3,7},{4,0},{5,1},{6,2},{7,3},{8,12},{9,13},{10,... | collective-permute-start | bytes 294920 | tf_op jit(solution)/shard_map/ppermute | solution.py:479
  13.4 5.2 %collective-permute-start.6 = (bf16[3,128,128]{2,1,0:T(8,128)(2,1)S(1)}, bf16[3,128,128]{2,1,0:T(8,128)(2,1)S(1)}, u32[]{:S(2)}, u32[]{:S(2)}) collective-permute-start(bf16[3,128,128]{2,1,0:T(8,128)(2,1)S(1)} %get-tuple-element.86), channel_id=1, source_target_pairs={{0,5},{1,4},{2,7},{3,6},{4,1},{5,0},{6,3},{7,2},{8,13},{9,12},{10,... | collective-permute-start | bytes 294920 | tf_op jit(solution)/shard_map/ppermute | solution.py:479
  16.4 6.3 %collective-permute-start.8 = (bf16[416,128]{1,0:T(8,128)(2,1)S(1)}, bf16[416,128]{1,0:T(8,128)(2,1)S(1)}, u32[]{:S(2)}, u32[]{:S(2)}) collective-permute-start(bf16[416,128]{1,0:T(8,128)(2,1)S(1)} %get-tuple-element.97), channel_id=1, source_target_pairs={{0,4},{1,5},{2,6},{3,7},{4,0},{5,1},{6,2},{7,3},{8,12},{9,13},{10,... | collective-permute-start | bytes 319496 | tf_op jit(solution)/shard_map/ppermute | solution.py:479
  18.0 5.5 %collective-permute-start.9 = (bf16[416,128]{1,0:T(8,128)(2,1)S(1)}, bf16[416,128]{1,0:T(8,128)(2,1)S(1)}, u32[]{:S(2)}, u32[]{:S(2)}) collective-permute-start(bf16[416,128]{1,0:T(8,128)(2,1)S(1)} %get-tuple-element.98), channel_id=1, source_target_pairs={{0,5},{1,4},{2,7},{3,6},{4,1},{5,0},{6,3},{7,2},{8,13},{9,12},{10,... | collective-permute-start | bytes 319496 | tf_op jit(solution)/shard_map/ppermute | solution.py:479
  18.3 5.2 %collective-permute-start.7 = (bf16[3,160,256]{2,1,0:T(8,128)(2,1)S(1)}, bf16[3,160,256]{2,1,0:T(8,128)(2,1)S(1)}, u32[]{:S(2)}, u32[]{:S(2)}) collective-permute-start(bf16[3,160,256]{2,1,0:T(8,128)(2,1)S(1)} %get-tuple-element.96), channel_id=1, source_target_pairs={{0,1},{1,0},{2,3},{3,2},{4,5},{5,4},{6,7},{7,6},{8,9},{9,8},{10,11... | collective-permute-start | bytes 737288 | tf_op jit(solution)/shard_map/ppermute | solution.py:475
  24.2 12.5 %collective-permute-start.10 = (bf16[32,1408]{1,0:T(8,128)(2,1)S(1)}, bf16[32,1408]{1,0:T(8,128)(2,1)S(1)}, u32[]{:S(2)}, u32[]{:S(2)}) collective-permute-start(bf16[32,1408]{1,0:T(8,128)(2,1)S(1)} %get-tuple-element.100), channel_id=1, source_target_pairs={{0,8},{4,12},{8,16},{12,20},{16,24},{20,28},{24,0},{28,4},{1,9},{5... | collective-permute-start | bytes 270344 | tf_op jit(solution)/shard_map/ppermute | solution.py:482
  26.3 10.4 %collective-permute-start.12 = (bf16[32,1408]{1,0:T(8,128)(2,1)S(1)}, bf16[32,1408]{1,0:T(8,128)(2,1)S(1)}, u32[]{:S(2)}, u32[]{:S(2)}) collective-permute-start(bf16[32,1408]{1,0:T(8,128)(2,1)S(1)} %get-tuple-element.102), channel_id=1, source_target_pairs={{0,24},{4,28},{8,0},{12,4},{16,8},{20,12},{24,16},{28,20},{1,25},{... | collective-permute-start | bytes 270344 | tf_op jit(solution)/shard_map/ppermute | solution.py:482
  28.4 8.3 %collective-permute-start.11 = (bf16[32,1280]{1,0:T(8,128)(2,1)S(1)}, bf16[32,1280]{1,0:T(8,128)(2,1)S(1)}, u32[]{:S(2)}, u32[]{:S(2)}) collective-permute-start(bf16[32,1280]{1,0:T(8,128)(2,1)S(1)} %get-tuple-element.101), channel_id=1, source_target_pairs={{0,16},{4,20},{8,24},{12,28},{16,0},{20,4},{24,8},{28,12},{1,17},{... | collective-permute-start | bytes 245768 | tf_op jit(solution)/shard_map/ppermute | solution.py:482

commit v8 on v7

--- a/solution.py
+++ b/solution.py
@@ -23,14 +23,12 @@
     return pltpu.CompilerParams(vmem_limit_bytes=held + 8 * 1024 * 1024)
 
 
-def call(kernel, out_shape, operands, flops, name, in_hbm=(), out_hbm=(), aliases=None, scratch=(), brief=False):
+def call(kernel, out_shape, operands, flops, name, in_hbm=(), scratch=(), brief=False):
     def spec(k, array):
         scalars = array.dtype == jnp.int32 and array.size < LANES
         return HBM_SPEC if scalars or k in in_hbm else VMEM_SPEC
 
-    count = len(jax.tree.leaves(out_shape))
-    out_specs = [HBM_SPEC if k in out_hbm else VMEM_SPEC for k in range(count)]
-    out_specs = jax.tree.unflatten(jax.tree.structure(out_shape), out_specs)
+    out_specs = jax.tree.map(lambda _: VMEM_SPEC, out_shape)
     size = sum(array.size * array.dtype.itemsize for array in jax.tree.leaves((operands, out_shape)))
     if brief:
         flops = size = 0
@@ -45,7 +43,6 @@
         in_specs=in_specs,
         out_specs=out_specs,
         scratch_shapes=list(scratch),
-        input_output_aliases=aliases or {},
         compiler_params=params(operands, out_shape),
         cost_estimate=pl.CostEstimate(flops=flops, bytes_accessed=size, transcendentals=0),
         name=name,
@@ -100,9 +97,11 @@
         load.wait()
 
 
-def weights_kernel(geometry, wind_hbm, offsets_hbm, ratio_hbm, rows_out, base_out, upper_out, low_out, high_out, *scratch):
+def weights_kernel(geometry, wind_hbm, offsets_hbm, ratio_hbm, *refs):
     n_layer, rows_dev, screen_cols = geometry
-    wind, offsets, ratio, sems = scratch
+    sources, (rows_out, base_out, upper_out, low_out, high_out), refs = refs[:4], refs[4:9], refs[9:]
+    copies, (wind, offsets, ratio, sems) = refs[:4], refs[4:]
+    others = fetch(*[(source, copy, sems.at[3 + k]) for k, (source, copy) in enumerate(zip(sources, copies))])
     loads = fetch(
         (wind_hbm, wind, sems.at[0]),
         (offsets_hbm, offsets, sems.at[1]),
@@ -114,8 +113,7 @@
     column = lax.axis_index("layer")
     block = pupil_rows // n_layer
     row = lax.broadcasted_iota(jnp.int32, (half, LANES), 0)
-    pair = row // block + column // 2
-    pair = jnp.where(pair >= n_layer // 2, pair - n_layer // 2, pair)
+    pair = jnp.bitwise_xor(row // block, column // 2)
     parity = lax.rem(column, 2)
     inside = lax.rem(row, block) + pair * (2 * block)
     pixel_rows = stack(inside + parity * block, inside + (1 - parity) * block)
@@ -147,6 +145,8 @@
         values = spans(pixel, anchor, num, den, screen_cols)
         for out, value in zip((base_out, upper_out, low_out, high_out), values):
             out[:, at : at + LANES] = value
+    for load in others:
+        load.wait()
 
 
 def column_weights(base_ref, upper_ref, low_ref, high_ref, first, out):
@@ -219,7 +219,8 @@
 
 
 def later_rows_kernel(wind_hbm, rows_ref, *refs):
-    chunks, (near, sibling0), (mine, other, sibling_other, give, wind, sem) = refs[:6], refs[6:8], refs[8:]
+    chunks, (near, sibling0), outs, (wind, sem) = refs[:6], refs[6:8], refs[8:-2], refs[-2:]
+    mine, give, other, sibling_other = outs
     load = fetch((wind_hbm, wind, sem))[0]
     keep0, across0, diagonal0, keep, across, diagonal = chunks
     layers, half, width = mine.shape
@@ -272,30 +273,34 @@
 
 
 def last_kernel(mine_ref, cols_ref, phase, taken, came, sibling_came, *outs):
-    *outs, partner_strips = outs
+    *outs, strips = outs
     layers, _, width = taken.shape
     width = width // 2
-    size, pupil_cols = outs[0].shape
-    half = size * len(outs)
+    size, half, pairs = outs[0].shape[0], phase.shape[0], len(outs)
     parts, cuts = [], []
     for level in range(layers):
         cut = slice(level * half, (level + 1) * half)
         parts += [taken[level, :half], came[cut], sibling_came[cut]]
         cuts += [(mine_ref, level, 2 * width, 4 * width)]
         cuts += [(cols_ref, level, width, 2 * width), (cols_ref, level, 3 * width, 4 * width)]
-    for at in range(0, pupil_cols, 256):
+    for at in range(0, phase.shape[1], 256):
         total = (phase[:, at : at + 256] + project(parts, cuts, at)).astype(jnp.bfloat16)
         for k, out in enumerate(outs):
             out[:, at : at + 256] = total[k * size : (k + 1) * size]
     odd = lax.rem(lax.axis_index("dir"), 2) == 1
     here = get_strip(came, layers * half).astype(jnp.float32)
     there = get_strip(sibling_came, layers * half).astype(jnp.float32)
-    last = jnp.where(odd, here, there).astype(jnp.bfloat16)
-    first = jnp.where(odd, there, here).astype(jnp.bfloat16)
-    outs[1][:, pupil_cols:] = last
-    outs[-1][:, pupil_cols:] = first
-    partner_strips[:STRIP] = last
-    partner_strips[STRIP:] = first
+    last, first = jnp.where(odd, here, there), jnp.where(odd, there, here)
+    strips[:STRIP] = last.astype(jnp.bfloat16)
+    strips[STRIP:] = first.astype(jnp.bfloat16)
+    pair = lax.axis_index("layer") // 2
+    for step in strip_steps(pairs):
+        after = lax.rem(pair + 1, pairs) == jnp.bitwise_xor(pair, step)
+        outs[step][:, phase.shape[1] :] = jnp.where(after, last, first).astype(jnp.bfloat16)
+
+
+def strip_steps(pairs):
+    return [2**k - 1 for k in range(1, pairs.bit_length())]
 
 
 def shifted_rows(shift, odd, own, near, edges):
@@ -307,55 +312,39 @@
     return pltpu.roll(stack(before, own, after), shift, 0)[16 : 16 + rows]
 
 
-def shift_kernel(wind_hbm, own, near, diagonal0, diagonal1, taken, whole, ends, wind, sem, out):
+def shift_kernel(pairs, wind_hbm, own, near, diagonal0, diagonal1, taken, partner_strips, *refs):
+    messages, (out, wind, sem) = refs[:-3], refs[-3:]
     load = fetch((wind_hbm, wind, sem))[0]
     layers, rows, cols = own.shape
     odd = lax.rem(lax.axis_index("dir"), 2) == 1
     half = taken.shape[1] - 32
+    pair, second = lax.axis_index("layer") // 2, lax.rem(lax.axis_index("layer"), 2) == 1
+    before = jnp.bitwise_xor(pair, lax.rem(pair + pairs - 1, pairs))
+    after = jnp.bitwise_xor(pair, lax.rem(pair + 1, pairs))
+    left = partner_strips[:STRIP].astype(jnp.float32)
+    right = partner_strips[STRIP:].astype(jnp.float32)
+    for step, message in zip(strip_steps(pairs), messages):
+        strip = message[:, message.shape[1] - rows :].astype(jnp.float32)
+        left = jnp.where(jnp.logical_and(before == step, jnp.logical_not(second)), strip, left)
+        right = jnp.where(jnp.logical_and(after == step, second), strip, right)
+    strips = stack(left, right, jnp.zeros((LANES - 2 * STRIP, rows), jnp.float32)).T
+    lane = lax.broadcasted_iota(jnp.int32, (rows, LANES), 1)
     load.wait()
     for level in range(layers):
+        last = pltpu.roll(strips, LANES - WIND_MAX * (level + 1), 1)
+        first = pltpu.roll(strips, LANES - STRIP - WIND_MAX * level, 1)
+        extra = jnp.where(lane < WIND_MAX, first, last)
         chunks = [stack(part[level, :16], part[level, rows - 16 :]) for part in (diagonal0, diagonal1)]
         here = beside(*chunks).astype(jnp.float32)
         there = taken[level, half:].astype(jnp.float32)
         edges = beside(jnp.where(odd, there, here), jnp.where(odd, here, there))
         moved = shifted_rows(wind[0, level], odd, own[level], near[level], edges)
         shift = wind[1, level]
-        moved = pltpu.roll(moved, jnp.where(shift < 0, shift + cols, shift), 1).astype(jnp.bfloat16)
-        out[level] = moved
-        ends[0, level] = moved[:, :LANES]
-        ends[1, level] = moved[:, cols - LANES :]
-    copy = pltpu.make_async_copy(out, whole, sem)
-    copy.start()
-    copy.wait()
-
-
-def patch_ends(wind, ends, partner_strips, below, above, out):
-    _, layers, rows, _ = ends.shape
-    second = lax.rem(lax.axis_index("layer"), 2) == 1
-    at = below.shape[1] - rows
-    strips = stack(partner_strips[:STRIP], below[:, at:], partner_strips[STRIP:], above[:, at:])
-    strips = strips.astype(jnp.float32).T
-    lane = lax.broadcasted_iota(jnp.int32, (rows, LANES), 1)
-    left = jnp.where(second, 0, STRIP)
-    right = jnp.where(second, 3 * STRIP, 2 * STRIP)
-    for level in range(layers):
-        shift = wind[1, level]
-        at = WIND_MAX * (level + 1)
-        value = pltpu.roll(strips, lax.rem(2 * LANES - at - left + shift, LANES), 1)
-        out[0, level] = jnp.where(lane < shift, value, ends[0, level].astype(jnp.float32)).astype(jnp.bfloat16)
-        at = WIND_MAX * level
-        value = pltpu.roll(strips, lax.rem(2 * LANES - at - right + shift, LANES), 1)
-        kept = ends[1, level].astype(jnp.float32)
-        out[1, level] = jnp.where(lane >= LANES + shift, value, kept).astype(jnp.bfloat16)
-
-
-def optics_kernel(*refs):
-    sources, refs = refs[:4], refs[4:]
-    amp_out, high_out, low_out, lines_out, amplitude, ones, columns, lines, sems = refs
-    targets = amplitude, ones, columns, lines
-    loads = fetch(*[(source, target, sems.at[k]) for k, (source, target) in enumerate(zip(sources, targets))])
-    for load in loads:
-        load.wait()
+        shift = jnp.where(shift < 0, shift + cols + LANES, shift)
+        out[level] = pltpu.roll(beside(moved, extra), shift, 1)[:, :cols].astype(jnp.bfloat16)
+
+
+def optics_kernel(amplitude, ones, columns, lines, amp_out, high_out, low_out, lines_out):
     rows, pupil_cols = amplitude.shape
     for step in range(pupil_cols // LANES):
         cut = slice(step * LANES, (step + 1) * LANES)
@@ -391,10 +380,9 @@
     return high, low
 
 
-def imaging_kernel(count, wind_hbm, *refs):
-    parts, refs = refs[:count], refs[count:]
-    amp_ref, cols_high, cols_low, rows_table, ends, partner_strips, _, out, screens, wind, patched, sems = refs
-    load = fetch((wind_hbm, wind, sems.at[0]))[0]
+def imaging_kernel(count, *refs):
+    parts = refs[:count]
+    amp_ref, cols_high, cols_low, rows_table, out = refs[count:]
     rows, cols = amp_ref.shape
     tiles = cols // LANES
     phase = parts[0][:, :cols].astype(jnp.float32)
@@ -414,13 +402,6 @@
     )
     high, low = split(field)
     half = dot(high, cols_high[...]) + (dot(low, cols_high[...]) + dot(high, cols_low[...]))
-    load.wait()
-    patch_ends(wind, ends, partner_strips, parts[1], parts[-1], patched)
-    width = screens.shape[2]
-    copies = fetch(
-        (patched.at[0], screens.at[:, :, :LANES], sems.at[1]),
-        (patched.at[1], screens.at[:, :, width - LANES :], sems.at[2]),
-    )
     wide = 2 * LANES
     out_rows = 2 * rows
     for t in range(tiles):
@@ -430,8 +411,6 @@
         full = dot(rows_table[...], jnp.concatenate([high, low, high], axis=0))
         real, imag = full[:out_rows], full[out_rows:]
         out[:, t * wide : (t + 1) * wide] = real * real + imag * imag
-    for copy in copies:
-        copy.wait()
 
 
 def tables_of(rows):
@@ -497,17 +476,23 @@
     diagonal0 = swap(give0, 3)
     across1 = swap(keep1, 2)
     diagonal1 = swap(give1, 3)
-    near = swap(own, 1)
+    ones = np.kron(np.eye(LANES // SUB_PIX), np.ones((SUB_PIX, SUB_PIX))).astype(np.float32)
+    optics_in = (amplitude, jnp.asarray(ones), *[jnp.asarray(table) for table in tables_of(rows)])
+    copies = [shape(*array.shape, dtype=f32) for array in optics_in]
     row_weights, *tables = call(
         functools.partial(weights_kernel, (n_layer, rows_dev, cols_dev * n_layer)),
         [shape(2, layers, pupil_rows, 4 * rows_dev)]
-        + [shape(8, pupil_cols, dtype=dtype) for dtype in (jnp.int32, jnp.int32, f32, f32)],
-        (wind, offsets, ratio),
+        + [shape(8, pupil_cols, dtype=dtype) for dtype in (jnp.int32, jnp.int32, f32, f32)]
+        + copies,
+        (wind, offsets, ratio, *optics_in),
         0,
         "weights",
-        scratch=[smem(array.shape, jnp.int32) for array in (wind, offsets, ratio)] + [sem((3,))],
+        in_hbm=range(3, 7),
+        scratch=[smem(array.shape, jnp.int32) for array in (wind, offsets, ratio)] + [sem((7,))],
         brief=True,
     )
+    tables, optics_in = tables[:4], tables[4:]
+    near = swap(own, 1)
     tables = tuple(tables)
     across0, diagonal0, row_weights, tables = lax.optimization_barrier((across0, diagonal0, row_weights, tables))
 
@@ -529,9 +514,9 @@
     )
     cols, sibling0 = lax.optimization_barrier((cols, sibling0))
     message = shape(layers * half + STRIP * rows_dev // LANES, width)
-    mine1, other1, sibling_other1, give = call(
+    mine1, give, other1, sibling_other1 = call(
         later_rows_kernel,
-        [projected, message, message, shape(layers, half + 32, 2 * width)],
+        [projected, shape(layers, half + 32, 2 * width), message, message],
         (wind, row_weights, keep0, across0, diagonal0, keep1, across1, diagonal1, near, sibling0),
         0,
         "rows_later",
@@ -550,57 +535,45 @@
         "phase",
     )
 
-    ones = np.kron(np.eye(LANES // SUB_PIX), np.ones((SUB_PIX, SUB_PIX))).astype(np.float32)
-    columns, lines = tables_of(rows)
-    amplitude, phase = lax.optimization_barrier((amplitude, phase))
-    optics_in = (amplitude, jnp.asarray(ones), jnp.asarray(columns), jnp.asarray(lines))
+    steps = strip_steps(pairs)
+    *sums, strips = call(
+        last_kernel,
+        [shape(rows, pupil_cols + (rows_dev if k in steps else 0)) for k in range(pairs)] + [shape(2 * STRIP, rows_dev)],
+        (cols, others, phase, taken, came1, sibling_came1),
+        300_000_000,
+        "last",
+    )
+    received = list(sums)
+    for k in range(pairs - 1, 0, -1):
+        received[k] = lax.ppermute(sums[k], "layer", [(i, i ^ (2 * k)) for i in range(n_layer)])
+
+    optics_in, received[0] = lax.optimization_barrier((optics_in, received[0]))
     optics = call(
         optics_kernel,
         (
             shape(rows, pupil_cols, dtype=f32),
-            shape(*columns.shape),
-            shape(*columns.shape),
-            shape(lines.shape[0], 3 * lines.shape[1]),
+            shape(*optics_in[2].shape),
+            shape(*optics_in[2].shape),
+            shape(optics_in[3].shape[0], 3 * optics_in[3].shape[1]),
         ),
         optics_in,
         30_000_000,
         "optics",
-        in_hbm=range(4),
-        scratch=[pltpu.VMEM(array.shape, f32) for array in optics_in] + [sem((4,))],
-    )
-    phase, optics = lax.optimization_barrier((phase, optics))
-    extra = [rows_dev if k in (1, pairs - 1) else 0 for k in range(pairs)]
-    *sums, strips = call(
-        last_kernel,
-        [shape(rows, pupil_cols + more) for more in extra] + [shape(2 * STRIP, rows_dev)],
-        (cols, others, phase, taken, came1, sibling_came1),
-        300_000_000,
-        "last",
-    )
-    received = [sums[0]] + [None] * (pairs - 1)
-    for k in sorted(range(1, pairs), key=lambda k: -min(k, pairs - k)):
-        received[k] = turn(sums[k], 2 * k)
-
-    diagonal0, strips = lax.optimization_barrier((diagonal0, strips))
-    shifted, ends = call(
-        shift_kernel,
-        [shape(layers, rows_dev, cols_dev), shape(2, layers, rows_dev, LANES)],
-        (wind, own, near, diagonal0, diagonal1, taken),
+    )
+    new_screens = call(
+        functools.partial(shift_kernel, pairs),
+        shape(layers, rows_dev, cols_dev),
+        (wind, own, near, diagonal0, diagonal1, taken, strips, *[received[k] for k in steps]),
         1_000_000,
         "shift",
-        scratch=wind_scratch + [pltpu.VMEM(own.shape, bf16)],
-        out_hbm=(0,),
-    )
-    spots, new_screens = call(
+        scratch=wind_scratch,
+    )
+    spots = call(
         functools.partial(imaging_kernel, pairs),
-        [shape(2 * rows, 2 * pupil_cols, dtype=f32), shape(layers, rows_dev, cols_dev)],
-        (wind, *received, *optics, ends, strips, shifted),
+        shape(2 * rows, 2 * pupil_cols, dtype=f32),
+        (*received, *optics),
         400_000_000,
         "imaging",
-        in_hbm=(pairs + 7,),
-        out_hbm=(1,),
-        aliases={pairs + 7: 1},
-        scratch=[wind_scratch[0], pltpu.VMEM(ends.shape, bf16), sem((3,))],
     )
     return (new_screens, spots[None])
 

time: 39.8 us -> 38.9 us (0.977)
  Pallas kernels: 16.4 us -> 14.2 us
  waiting for transfers between devices: 7.82 us -> 9.54 us
  starting transfers between devices: 14.6 us -> 14.2 us
    pallas_call x10, Pallas kernels: 16.4 us -> 14.2 us  [call(): pl.pallas_call(kernel, out_shape=out_shape, in_specs=in_specs, out_specs=...]
    ppermute x4, waiting for transfers between devices: 0.77 us -> 2.74 us  [partner(): lax.ppermute(value, ('layer', 'dir'), [(i, i ^ n_dir ^ bits) for i in ran...]
    ppermute x3, starting transfers between devices: 5.14 us -> 4.71 us  [per_device(): lax.ppermute(sums[k], 'layer', [(i, i ^ 2 * k) for i in range(n_layer)])]
  transfers between devices with their start and end apart: 13 -> 13, of which waited for: 3 -> 5; matrix products, arithmetic and copies ran while one was open for 0% -> 0% of each run, Pallas kernels for 29% -> 27%
where the time goes in v8:
time: 38.9 us; the launch traced here: 38.7 us
  Pallas kernels  14.2 us (37%)
  starting transfers between devices  14.2 us (37%)
  waiting for transfers between devices  9.54 us (25%)
  between operations  0.74 us (2%)
    pallas_call x10, Pallas kernels, call(): pl.pallas_call(kernel, out_shape=out_shape, in_specs=in_specs, out_specs=...  14.2 us
    ppermute x6, starting transfers between devices, swap(): return lax.ppermute(value, 'dir', [(i, i ^ bits) for i in range(n_dir)])  5.51 us
    ppermute x3, waiting for transfers between devices, per_device(): lax.ppermute(sums[k], 'layer', [(i, i ^ 2 * k) for i in range(n_layer)])  5.36 us
    ppermute x3, starting transfers between devices, per_device(): lax.ppermute(sums[k], 'layer', [(i, i ^ 2 * k) for i in range(n_layer)])  4.71 us
    ppermute x4, starting transfers between devices, partner(): lax.ppermute(value, ('layer', 'dir'), [(i, i ^ n_dir ^ bits) for i in ran...  4 us
    ppermute x4, waiting for transfers between devices, partner(): lax.ppermute(value, ('layer', 'dir'), [(i, i ^ n_dir ^ bits) for i in ran...  2.74 us
    ppermute x6, waiting for transfers between devices, swap(): return lax.ppermute(value, 'dir', [(i, i ^ bits) for i in range(n_dir)])  1.43 us
  transfers between devices with their start and end apart: 13, of which 5 were waited for; matrix products, arithmetic and copies ran while one was open for 0% of the time, Pallas kernels for 27%

profile of v8, /device:TPU:0, one launch (start us, length us, event | category | flops | bytes accessed | tf_op | source)
XLA Modules:
  0.0 38.7 jit_solution(6400005388561694101)
XLA Ops:
  0.6 1.3 %split.1 = (bf16[3,128,512]{2,1,0:T(8,128)(2,1)S(1)}, bf16[3,128,128]{2,1,0:T(8,128)(2,1)S(1)}, bf16[3,128,128]{2,1,0:T(8,128)(2,1)S(1)}, bf16[3,128,128]{2,1,0:T(8,128)(2,1)S(1)}, bf16[3,128,128]{2,1,0:T(8,128)(2,1)S(1)}) custom-call(bf16[3,128,512]{2,1,0:T(8,128)(2,1)} %screens.1), custom_call_target="tpu_custom_call" | custom-call | tf_op jit(solution)/shard_map/split/pallas_call | solution.py:40
  1.9 0.5 %collective-permute-start = (bf16[3,128,512]{2,1,0:T(8,128)(2,1)S(1)}, bf16[3,128,512]{2,1,0:T(8,128)(2,1)S(1)}, u32[]{:S(2)}, u32[]{:S(2)}) collective-permute-start(bf16[3,128,512]{2,1,0:T(8,128)(2,1)S(1)} %get-tuple-element.54.own), channel_id=1, source_target_pairs={{0,1},{1,0},{2,3},{3,2},{4,5},{5,4},{6,7},{7,6},{8,9},{9,8},{10,11... | collective-permute-start | bytes 1179656 | tf_op jit(solution)/shard_map/ppermute | solution.py:454
  2.4 2.6 %collective-permute-start.2 = (bf16[3,128,128]{2,1,0:T(8,128)(2,1)S(1)}, bf16[3,128,128]{2,1,0:T(8,128)(2,1)S(1)}, u32[]{:S(2)}, u32[]{:S(2)}) collective-permute-start(bf16[3,128,128]{2,1,0:T(8,128)(2,1)S(1)} %get-tuple-element.56), channel_id=1, source_target_pairs={{0,3},{1,2},{2,1},{3,0},{4,7},{5,6},{6,5},{7,4},{8,11},{9,10},{10,... | collective-permute-start | bytes 294920 | tf_op jit(solution)/shard_map/ppermute | solution.py:454
  5.0 0.0 collective-permute-start.1
  5.1 1.4 %collective-permute-start.3 = (bf16[3,128,128]{2,1,0:T(8,128)(2,1)S(1)}, bf16[3,128,128]{2,1,0:T(8,128)(2,1)S(1)}, u32[]{:S(2)}, u32[]{:S(2)}) collective-permute-start(bf16[3,128,128]{2,1,0:T(8,128)(2,1)S(1)} %get-tuple-element.63), channel_id=1, source_target_pairs={{0,3},{1,2},{2,1},{3,0},{4,7},{5,6},{6,5},{7,4},{8,11},{9,10},{10,... | collective-permute-start | bytes 294920 | tf_op jit(solution)/shard_map/ppermute | solution.py:454
  6.4 0.6 %collective-permute-start.4 = (bf16[3,128,128]{2,1,0:T(8,128)(2,1)S(1)}, bf16[3,128,128]{2,1,0:T(8,128)(2,1)S(1)}, u32[]{:S(2)}, u32[]{:S(2)}) collective-permute-start(bf16[3,128,128]{2,1,0:T(8,128)(2,1)S(1)} %get-tuple-element.66.refs_3_), channel_id=1, source_target_pairs={{0,2},{1,3},{2,0},{3,1},{4,6},{5,7},{6,4},{7,5},{8,10},{9,11},{10,... | collective-permute-start | bytes 294920 | tf_op jit(solution)/shard_map/ppermute | solution.py:454
  7.1 2.2 %weights.1 = (bf16[2,3,256,512]{3,2,1,0:T(8,128)(2,1)S(1)}, s32[8,1280]{1,0:T(8,128)S(1)}, s32[8,1280]{1,0:T(8,128)S(1)}, f32[8,1280]{1,0:T(8,128)S(1)}, f32[8,1...) custom-call(s32[2,3]{1,0:T(2,128)} %bitcast.5, ...), custom_call_target="tpu_custom_call" | custom-call | tf_op jit(solution)/shard_map/weights/pallas_call | solution.py:40
  9.3 0.0 collective-permute-done.2.diagonal.refs_2_.diagonal0
  9.3 1.4 %collective-permute-done.1.across.refs_1_ = bf16[3,128,128]{2,1,0:T(8,128)(2,1)S(1)} collective-permute-done((bf16[3,128,128]{2,1,0:T(8,128)(2,1)S(1)}, bf16[3,128,128]{2,1,0:T(8,128)(2,1)S(1)}, u32[]{:S(2)}, u32[]{:S(2)}) %collective-permute-start.1) | collective-permute-done | bytes 98336 | tf_op jit(solution)/shard_map/ppermute | solution.py:454
  10.7 0.0 collective-permute-done.near.refs_6_
  10.7 0.6 %rows_first.1 = (bf16[3,128,128]{2,1,0:T(8,128)(2,1)S(1)}, bf16[3,128,128]{2,1,0:T(8,128)(2,1)S(1)}, bf16[3,128,128]{2,1,0:T(8,128)(2,1)S(1)}, bf16[3,128,128]{2,1,0:T(8,128)(2,1)S(1)}) custom-call(bf16[2,3,256,512]{3,2,1,0:T(8,128)(2,1)S(1)} %get-tuple-element.64.rows_ref, bf16[3,128,128]{2,1,0:T(8,128)(2,1)S(1)} %get-tuple-element.55.keep.refs_0_, ...), custom_call_target="tpu_custom_call" | custom-call | tf_op jit(solution)/shard_map/rows_first/pallas_call | solution.py:40
  11.3 2.1 %collective-permute-start.6 = (bf16[3,128,128]{2,1,0:T(8,128)(2,1)S(1)}, bf16[3,128,128]{2,1,0:T(8,128)(2,1)S(1)}, u32[]{:S(2)}, u32[]{:S(2)}) collective-permute-start(bf16[3,128,128]{2,1,0:T(8,128)(2,1)S(1)} %get-tuple-element.82), channel_id=1, source_target_pairs={{0,4},{1,5},{2,6},{3,7},{4,0},{5,1},{6,2},{7,3},{8,12},{9,13},{10,... | collective-permute-start | bytes 294920 | tf_op jit(solution)/shard_map/ppermute | solution.py:458
  13.4 1.5 %columns.1.refs_4_.mine_ref = bf16[3,512,1280]{2,1,0:T(8,128)(2,1)S(1)} custom-call(s32[8,1280]{1,0:T(8,128)S(1)} %get-tuple-element.72.refs_0_, s32[8,1280]{1,0:T(8,128)S(1)} %get-tuple-element.73.refs_1_, f32[8,1280]{1,0:T(8,128)S(1)} %get-tuple-element.74.refs_2_, f32[8,1280]{1,0:T(8,128)S(1)} %get-tuple-element.75.refs_3_), custom_call_target="tpu_custom_call" | custom-call | tf_op jit(solution)/shard_map/columns/pallas_call | solution.py:40
  14.9 0.0 collective-permute-done.3.refs_5_.diagonal1
  14.9 1.5 %rows_later.1 = (bf16[3,128,128]{2,1,0:T(8,128)(2,1)S(1)}, bf16[3,160,256]{2,1,0:T(8,128)(2,1)S(1)}, bf16[416,128]{1,0:T(8,128)(2,1)S(1)}, bf16[416,128]{1,0:T(8,128)(2,1)S(1)}) custom-call(s32[2,3]{1,0:T(2,128)} %bitcast.6, bf16[2,3,256,512]{3,2,1,0:T(8,128)(2,1)S(1)} %get-tuple-element.64.rows_ref, ...), custom_call_target="tpu_custom_call" | custom-call | tf_op jit(solution)/shard_map/rows_later/pallas_call | solution.py:40
  16.4 1.6 %collective-permute-start.8 = (bf16[416,128]{1,0:T(8,128)(2,1)S(1)}, bf16[416,128]{1,0:T(8,128)(2,1)S(1)}, u32[]{:S(2)}, u32[]{:S(2)}) collective-permute-start(bf16[416,128]{1,0:T(8,128)(2,1)S(1)} %get-tuple-element.86), channel_id=1, source_target_pairs={{0,4},{1,5},{2,6},{3,7},{4,0},{5,1},{6,2},{7,3},{8,12},{9,13},{10,... | collective-permute-start | bytes 319496 | tf_op jit(solution)/shard_map/ppermute | solution.py:458
  18.0 0.3 collective-permute-start.9
  18.3 0.3 collective-permute-start.5
  18.6 0.0 collective-permute-done.6.refs_7_
  18.6 0.0 collective-permute-done.7.refs_8_
  18.6 2.1 %phase.1 = (f32[128,1280]{1,0:T(8,128)S(1)}, bf16[3,512,1280]{2,1,0:T(8,128)(2,1)S(1)}) custom-call(s32[8,1280]{1,0:T(8,128)S(1)} %get-tuple-element.72.refs_0_, s32[8,1280]{1,0:T(8,128)S(1)} %get-tuple-element.73.refs_1_, f32[8,1280]{1,0:T(8,128)S(1)} %get-tuple-element.74.refs_2_, f32[8,1280]{1,0:T(8,128)S(1)} %get-tuple-element.75.refs_3_, ...), custom_call_target="tpu_custom_call" | custom-call | flops 10000000000 | bytes 9076736 | tf_op jit(solution)/shard_map/phase/pallas_call | solution.py:40
  20.7 1.5 %collective-permute-done.8.came = bf16[416,128]{1,0:T(8,128)(2,1)S(1)} collective-permute-done((bf16[416,128]{1,0:T(8,128)(2,1)S(1)}, bf16[416,128]{1,0:T(8,128)(2,1)S(1)}, u32[]{:S(2)}, u32[]{:S(2)}) %collective-permute-start.8) | collective-permute-done | bytes 106528 | tf_op jit(solution)/shard_map/ppermute | solution.py:458
  22.2 1.3 %collective-permute-done.9.sibling_came = bf16[416,128]{1,0:T(8,128)(2,1)S(1)} collective-permute-done((bf16[416,128]{1,0:T(8,128)(2,1)S(1)}, bf16[416,128]{1,0:T(8,128)(2,1)S(1)}, u32[]{:S(2)}, u32[]{:S(2)}) %collective-permute-start.9) | collective-permute-done | bytes 106528 | tf_op jit(solution)/shard_map/ppermute | solution.py:458
  23.5 0.7 %last.1 = (bf16[32,1280]{1,0:T(8,128)(2,1)S(1)}, bf16[32,1408]{1,0:T(8,128)(2,1)S(1)}, bf16[32,1280]{1,0:T(8,128)(2,1)S(1)}, bf16[32,1408]{1,0:T(8,128)(2,1)S(1)}, bf16[64,128]{1,0:T(8,128)(2,1)S(1)}) custom-call(bf16[3,512,1280]{2,1,0:T(8,128)(2,1)S(1)} %columns.1.refs_4_.mine_ref, bf16[3,512,1280]{2,1,0:T(8,128)(2,1)S(1)} %get-tuple-element.84.cols_ref, ...), custom_call_target="tpu_custom_call" | custom-call | flops 300000000 | bytes 9338880 | tf_op jit(solution)/shard_map/last/pallas_call | solution.py:40
  24.2 2.1 %collective-permute-start.10 = (bf16[32,1408]{1,0:T(8,128)(2,1)S(1)}, bf16[32,1408]{1,0:T(8,128)(2,1)S(1)}, u32[]{:S(2)}, u32[]{:S(2)}) collective-permute-start(bf16[32,1408]{1,0:T(8,128)(2,1)S(1)} %get-tuple-element.89), channel_id=1, source_target_pairs={{0,8},{4,12},{8,0},{12,4},{16,24},{20,28},{24,16},{28,20},{1,9},{5... | collective-permute-start | bytes 270344 | tf_op jit(solution)/shard_map/ppermute | solution.py:548
  26.3 2.5 %collective-permute-start.11 = (bf16[32,1408]{1,0:T(8,128)(2,1)S(1)}, bf16[32,1408]{1,0:T(8,128)(2,1)S(1)}, u32[]{:S(2)}, u32[]{:S(2)}) collective-permute-start(bf16[32,1408]{1,0:T(8,128)(2,1)S(1)} %get-tuple-element.90), channel_id=1, source_target_pairs={{0,24},{4,28},{8,16},{12,20},{16,8},{20,12},{24,0},{28,4},{1,25},{... | collective-permute-start | bytes 270344 | tf_op jit(solution)/shard_map/ppermute | solution.py:548
  28.8 0.1 collective-permute-start.12
  28.9 0.7 %optics.1 = (f32[32,1280]{1,0:T(8,128)S(1)}, bf16[256,512]{1,0:T(8,128)(2,1)S(1)}, bf16[256,512]{1,0:T(8,128)(2,1)S(1)}, bf16[128,192]{1,0:T(8,128)(2,1)S(1)}) custom-call(f32[32,1280]{1,0:T(8,128)S(1)} %get-tuple-element.98.amplitude, f32[128,128]{1,0:T(8,128)S(1)} %get-tuple-element.99.ones, f32[256,512]{1,0:T(8,128)S(1)} %get-tuple-element.100.columns, ...), custom_call_target="tpu_custom_call" | custom-call | flops 30000000 | bytes 1523712 | tf_op jit(solution)/shard_map/optics/pallas_call | solution.py:40
  29.6 4.7 %collective-permute-done.11.refs_1_.refs_3_ = bf16[32,1408]{1,0:T(8,128)(2,1)S(1)} collective-permute-done((bf16[32,1408]{1,0:T(8,128)(2,1)S(1)}, bf16[32,1408]{1,0:T(8,128)(2,1)S(1)}, u32[]{:S(2)}, u32[]{:S(2)}) %collective-permute-start.11) | collective-permute-done | bytes 90144 | tf_op jit(solution)/shard_map/ppermute | solution.py:548
  34.3 2.0 %shift.1 = bf16[3,128,512]{2,1,0:T(8,128)(2,1)} custom-call(s32[2,3]{1,0:T(2,128)} %bitcast.7, bf16[3,128,512]{2,1,0:T(8,128)(2,1)S(1)} %get-tuple-element.54.own, bf16[3,128,512]{2,1,0:T(8,128)(2,1)S(1)} %collective-permute-done.near.refs_6_, bf16[3,128,128]{2,1,0:T(8,128)(2,1)S(1)} %collective-permute-done.2.diagonal.refs_2_.diagonal0, ...), custom_call_target="tpu_custom_call" | custom-call | flops 1000000 | bytes 1818648 | tf_op jit(solution)/shard_map/shift/pallas_call | solution.py:40
  36.3 0.7 %collective-permute-done.12.refs_2_ = bf16[32,1280]{1,0:T(8,128)(2,1)S(1)} collective-permute-done((bf16[32,1280]{1,0:T(8,128)(2,1)S(1)}, bf16[32,1280]{1,0:T(8,128)(2,1)S(1)}, u32[]{:S(2)}, u32[]{:S(2)}) %collective-permute-start.12) | collective-permute-done | bytes 81952 | tf_op jit(solution)/shard_map/ppermute | solution.py:548
  37.0 1.7 %imaging.1 = f32[64,2560]{1,0:T(8,128)} custom-call(bf16[32,1280]{1,0:T(8,128)(2,1)S(1)} %get-tuple-element.96.refs_0_, bf16[32,1408]{1,0:T(8,128)(2,1)S(1)} %collective-permute-done.10.refs_0_.refs_1_, bf16[32,1280]{1,0:T(8,128)(2,1)S(1)} %collective-permute-done.12.refs_2_, bf16[32,1408]{1,0:T(8,128)(2,1)S(1)} %collective-permute-done.11.refs_1_.refs_3_, ...), custom_call_target="tpu_custom_call" | custom-call | flops 400000000 | bytes 1736704 | tf_op jit(solution)/shard_map/imaging/pallas_call | solution.py:40
  (4 shorter events, 0.0 us)
Async XLA Ops:
  1.9 8.8 %collective-permute-start = (bf16[3,128,512]{2,1,0:T(8,128)(2,1)S(1)}, bf16[3,128,512]{2,1,0:T(8,128)(2,1)S(1)}, u32[]{:S(2)}, u32[]{:S(2)}) collective-permute-start(bf16[3,128,512]{2,1,0:T(8,128)(2,1)S(1)} %get-tuple-element.54.own), channel_id=1, source_target_pairs={{0,1},{1,0},{2,3},{3,2},{4,5},{5,4},{6,7},{7,6},{8,9},{9,8},{10,11... | collective-permute-start | bytes 1179656 | tf_op jit(solution)/shard_map/ppermute | solution.py:454
  2.4 6.9 %collective-permute-start.2 = (bf16[3,128,128]{2,1,0:T(8,128)(2,1)S(1)}, bf16[3,128,128]{2,1,0:T(8,128)(2,1)S(1)}, u32[]{:S(2)}, u32[]{:S(2)}) collective-permute-start(bf16[3,128,128]{2,1,0:T(8,128)(2,1)S(1)} %get-tuple-element.56), channel_id=1, source_target_pairs={{0,3},{1,2},{2,1},{3,0},{4,7},{5,6},{6,5},{7,4},{8,11},{9,10},{10,... | collective-permute-start | bytes 294920 | tf_op jit(solution)/shard_map/ppermute | solution.py:454
  5.0 5.7 %collective-permute-start.1 = (bf16[3,128,128]{2,1,0:T(8,128)(2,1)S(1)}, bf16[3,128,128]{2,1,0:T(8,128)(2,1)S(1)}, u32[]{:S(2)}, u32[]{:S(2)}) collective-permute-start(bf16[3,128,128]{2,1,0:T(8,128)(2,1)S(1)} %get-tuple-element.55.keep.refs_0_), channel_id=1, source_target_pairs={{0,2},{1,3},{2,0},{3,1},{4,6},{5,7},{6,4},{7,5},{8,10},{9,11},{10,... | collective-permute-start | bytes 294920 | tf_op jit(solution)/shard_map/ppermute | solution.py:454
  5.1 9.8 %collective-permute-start.3 = (bf16[3,128,128]{2,1,0:T(8,128)(2,1)S(1)}, bf16[3,128,128]{2,1,0:T(8,128)(2,1)S(1)}, u32[]{:S(2)}, u32[]{:S(2)}) collective-permute-start(bf16[3,128,128]{2,1,0:T(8,128)(2,1)S(1)} %get-tuple-element.63), channel_id=1, source_target_pairs={{0,3},{1,2},{2,1},{3,0},{4,7},{5,6},{6,5},{7,4},{8,11},{9,10},{10,... | collective-permute-start | bytes 294920 | tf_op jit(solution)/shard_map/ppermute | solution.py:454
  6.4 8.5 %collective-permute-start.4 = (bf16[3,128,128]{2,1,0:T(8,128)(2,1)S(1)}, bf16[3,128,128]{2,1,0:T(8,128)(2,1)S(1)}, u32[]{:S(2)}, u32[]{:S(2)}) collective-permute-start(bf16[3,128,128]{2,1,0:T(8,128)(2,1)S(1)} %get-tuple-element.66.refs_3_), channel_id=1, source_target_pairs={{0,2},{1,3},{2,0},{3,1},{4,6},{5,7},{6,4},{7,5},{8,10},{9,11},{10,... | collective-permute-start | bytes 294920 | tf_op jit(solution)/shard_map/ppermute | solution.py:454
  11.3 7.3 %collective-permute-start.6 = (bf16[3,128,128]{2,1,0:T(8,128)(2,1)S(1)}, bf16[3,128,128]{2,1,0:T(8,128)(2,1)S(1)}, u32[]{:S(2)}, u32[]{:S(2)}) collective-permute-start(bf16[3,128,128]{2,1,0:T(8,128)(2,1)S(1)} %get-tuple-element.82), channel_id=1, source_target_pairs={{0,4},{1,5},{2,6},{3,7},{4,0},{5,1},{6,2},{7,3},{8,12},{9,13},{10,... | collective-permute-start | bytes 294920 | tf_op jit(solution)/shard_map/ppermute | solution.py:458
  13.4 5.2 %collective-permute-start.7 = (bf16[3,128,128]{2,1,0:T(8,128)(2,1)S(1)}, bf16[3,128,128]{2,1,0:T(8,128)(2,1)S(1)}, u32[]{:S(2)}, u32[]{:S(2)}) collective-permute-start(bf16[3,128,128]{2,1,0:T(8,128)(2,1)S(1)} %get-tuple-element.83), channel_id=1, source_target_pairs={{0,5},{1,4},{2,7},{3,6},{4,1},{5,0},{6,3},{7,2},{8,13},{9,12},{10,... | collective-permute-start | bytes 294920 | tf_op jit(solution)/shard_map/ppermute | solution.py:458
  16.4 5.8 %collective-permute-start.8 = (bf16[416,128]{1,0:T(8,128)(2,1)S(1)}, bf16[416,128]{1,0:T(8,128)(2,1)S(1)}, u32[]{:S(2)}, u32[]{:S(2)}) collective-permute-start(bf16[416,128]{1,0:T(8,128)(2,1)S(1)} %get-tuple-element.86), channel_id=1, source_target_pairs={{0,4},{1,5},{2,6},{3,7},{4,0},{5,1},{6,2},{7,3},{8,12},{9,13},{10,... | collective-permute-start | bytes 319496 | tf_op jit(solution)/shard_map/ppermute | solution.py:458
  18.0 5.5 %collective-permute-start.9 = (bf16[416,128]{1,0:T(8,128)(2,1)S(1)}, bf16[416,128]{1,0:T(8,128)(2,1)S(1)}, u32[]{:S(2)}, u32[]{:S(2)}) collective-permute-start(bf16[416,128]{1,0:T(8,128)(2,1)S(1)} %get-tuple-element.87), channel_id=1, source_target_pairs={{0,5},{1,4},{2,7},{3,6},{4,1},{5,0},{6,3},{7,2},{8,13},{9,12},{10,... | collective-permute-start | bytes 319496 | tf_op jit(solution)/shard_map/ppermute | solution.py:458
  18.3 5.2 %collective-permute-start.5 = (bf16[3,160,256]{2,1,0:T(8,128)(2,1)S(1)}, bf16[3,160,256]{2,1,0:T(8,128)(2,1)S(1)}, u32[]{:S(2)}, u32[]{:S(2)}) collective-permute-start(bf16[3,160,256]{2,1,0:T(8,128)(2,1)S(1)} %get-tuple-element.78), channel_id=1, source_target_pairs={{0,1},{1,0},{2,3},{3,2},{4,5},{5,4},{6,7},{7,6},{8,9},{9,8},{10,11... | collective-permute-start | bytes 737288 | tf_op jit(solution)/shard_map/ppermute | solution.py:454
  24.2 5.4 %collective-permute-start.10 = (bf16[32,1408]{1,0:T(8,128)(2,1)S(1)}, bf16[32,1408]{1,0:T(8,128)(2,1)S(1)}, u32[]{:S(2)}, u32[]{:S(2)}) collective-permute-start(bf16[32,1408]{1,0:T(8,128)(2,1)S(1)} %get-tuple-element.89), channel_id=1, source_target_pairs={{0,8},{4,12},{8,0},{12,4},{16,24},{20,28},{24,16},{28,20},{1,9},{5... | collective-permute-start | bytes 270344 | tf_op jit(solution)/shard_map/ppermute | solution.py:548
  26.3 8.0 %collective-permute-start.11 = (bf16[32,1408]{1,0:T(8,128)(2,1)S(1)}, bf16[32,1408]{1,0:T(8,128)(2,1)S(1)}, u32[]{:S(2)}, u32[]{:S(2)}) collective-permute-start(bf16[32,1408]{1,0:T(8,128)(2,1)S(1)} %get-tuple-element.90), channel_id=1, source_target_pairs={{0,24},{4,28},{8,16},{12,20},{16,8},{20,12},{24,0},{28,4},{1,25},{... | collective-permute-start | bytes 270344 | tf_op jit(solution)/shard_map/ppermute | solution.py:548
  28.8 8.2 %collective-permute-start.12 = (bf16[32,1280]{1,0:T(8,128)(2,1)S(1)}, bf16[32,1280]{1,0:T(8,128)(2,1)S(1)}, u32[]{:S(2)}, u32[]{:S(2)}) collective-permute-start(bf16[32,1280]{1,0:T(8,128)(2,1)S(1)} %get-tuple-element.97), channel_id=1, source_target_pairs={{0,16},{4,20},{8,24},{12,28},{16,0},{20,4},{24,8},{28,12},{1,17},{... | collective-permute-start | bytes 245768 | tf_op jit(solution)/shard_map/ppermute | solution.py:548

commit v9 on v8

--- a/solution.py
+++ b/solution.py
@@ -84,7 +84,7 @@
 
 
 def split_kernel(screens, *refs):
-    own, outs, sems = refs[0], refs[1:-1], refs[-1]
+    outs, sems = refs[:-1], refs[-1]
     width = outs[0].shape[2]
     core = lax.rem(lax.axis_index("dir"), 2)
     pairs = []
@@ -92,15 +92,14 @@
         half = core if k < 2 else 1 - core
         start = pl.multiple_of((2 * half + k % 2) * width, LANES)
         pairs.append((screens.at[:, :, pl.ds(start, width)], out, sems.at[k]))
-    pairs.append((screens, own, sems.at[len(outs)]))
     for load in fetch(*pairs):
         load.wait()
 
 
 def weights_kernel(geometry, wind_hbm, offsets_hbm, ratio_hbm, *refs):
     n_layer, rows_dev, screen_cols = geometry
-    sources, (rows_out, base_out, upper_out, low_out, high_out), refs = refs[:4], refs[4:9], refs[9:]
-    copies, (wind, offsets, ratio, sems) = refs[:4], refs[4:]
+    sources, (rows_out, base_out, upper_out, low_out, high_out), refs = refs[:5], refs[5:10], refs[10:]
+    copies, (wind, offsets, ratio, sems) = refs[:5], refs[5:]
     others = fetch(*[(source, copy, sems.at[3 + k]) for k, (source, copy) in enumerate(zip(sources, copies))])
     loads = fetch(
         (wind_hbm, wind, sems.at[0]),
@@ -178,19 +177,16 @@
     column_weights(*tables, lax.axis_index("layer") * out.shape[1], out)
 
 
-def project_rows(chunk, rows_ref, keep, near, across, diagonal, level):
-    width = keep.shape[2]
-    core = lax.rem(lax.axis_index("dir"), 2)
-    start = pl.multiple_of((2 * core + chunk) * width, LANES)
-    screen = stack(keep[level], near[level, :, pl.ds(start, width)], across[level], diagonal[level])
+def project_rows(rows_ref, keep, near, across, diagonal, level):
+    screen = stack(keep[level], near[level], across[level], diagonal[level])
     rows = stack(rows_ref[0, level], rows_ref[1, level])
     return dot(rows, screen).astype(jnp.bfloat16)
 
 
-def first_rows_kernel(rows_ref, keep, near, across, diagonal, mine, sibling, other, sibling_other):
+def first_rows_kernel(rows_ref, across, diagonal, near, keep, mine, sibling, other, sibling_other):
     layers, half, _ = mine.shape
     for level in range(layers):
-        part = project_rows(0, rows_ref, keep, near, across, diagonal, level)
+        part = project_rows(rows_ref, keep, near, across, diagonal, level)
         for k, out in enumerate((mine, other, sibling, sibling_other)):
             out[level] = part[k * half : (k + 1) * half]
 
@@ -201,8 +197,8 @@
     lane = lax.broadcasted_iota(jnp.int32, (rows, LANES), 1)
     strip = jnp.zeros((rows, LANES), jnp.float32)
     for level in range(len(own)):
-        edges = stack(far[level][:16], far[level][rows - 16 :])
-        moved = shifted_rows(wind[0, level], odd, own[level], near[level], edges)
+        edges = [stack(block[level][:16], block[level][rows - 16 :]) for block in (near, far)]
+        moved = shifted_rows(wind[0, level], odd, own[level], *edges)
         at = WIND_MAX * level
         moved = pltpu.roll(moved, at + WIND_MAX * core, 1)
         strip = jnp.where((lane >= at) & (lane < at + WIND_MAX), moved, strip)
@@ -219,25 +215,24 @@
 
 
 def later_rows_kernel(wind_hbm, rows_ref, *refs):
-    chunks, (near, sibling0), outs, (wind, sem) = refs[:6], refs[6:8], refs[8:-2], refs[-2:]
+    chunks, sibling0, outs, (wind, sem) = refs[:8], refs[8], refs[9:-2], refs[-2:]
     mine, give, other, sibling_other = outs
     load = fetch((wind_hbm, wind, sem))[0]
-    keep0, across0, diagonal0, keep, across, diagonal = chunks
+    across, diagonal, near, keep, across0, diagonal0, near0, keep0 = chunks
     layers, half, width = mine.shape
-    rows, cols = near.shape[1:]
-    for level in range(layers):
-        part = project_rows(1, rows_ref, keep, near, across, diagonal, level)
+    rows = near.shape[1]
+    for level in range(layers):
+        part = project_rows(rows_ref, keep, near, across, diagonal, level)
         mine[level] = part[:half]
         other[level * half : (level + 1) * half] = part[half : 2 * half]
         sibling_other[level * half : (level + 1) * half] = part[3 * half :]
         give[level, :half, :width] = sibling0[level]
         give[level, :half, width:] = part[2 * half : 3 * half]
-        for k, block in enumerate((across0, across)):
+        for k, blocks in enumerate(((across0, keep0), (across, keep))):
             cut = slice(k * width, (k + 1) * width)
-            give[level, half : half + 16, cut] = block[level, :16]
-            give[level, half + 16 :, cut] = block[level, rows - 16 :]
+            edges = [block[level, at : at + 16] for block in blocks for at in (0, rows - 16)]
+            give[level, half:, cut] = stack(*edges)
     core = lax.rem(lax.axis_index("dir"), 2)
-    start = pl.multiple_of(core * (cols - LANES), LANES)
 
     def outer(first, second):
         return [
@@ -246,7 +241,7 @@
         ]
 
     own, far, sibling_far = outer(keep0, keep), outer(diagonal0, diagonal), outer(across0, across)
-    beyond = [near[level, :, pl.ds(start, LANES)] for level in range(layers)]
+    beyond = outer(near0, near)
     load.wait()
     put_strip(other, layers * half, outer_strip(wind, core == 1, own, beyond, far))
     put_strip(sibling_other, layers * half, outer_strip(wind, core == 0, beyond, own, sibling_far))
@@ -273,10 +268,10 @@
 
 
 def last_kernel(mine_ref, cols_ref, phase, taken, came, sibling_came, *outs):
-    *outs, strips = outs
+    *outs, strips, passed = outs
     layers, _, width = taken.shape
     width = width // 2
-    size, half, pairs = outs[0].shape[0], phase.shape[0], len(outs)
+    size, half = outs[0].shape[0], phase.shape[0]
     parts, cuts = [], []
     for level in range(layers):
         cut = slice(level * half, (level + 1) * half)
@@ -293,40 +288,28 @@
     last, first = jnp.where(odd, here, there), jnp.where(odd, there, here)
     strips[:STRIP] = last.astype(jnp.bfloat16)
     strips[STRIP:] = first.astype(jnp.bfloat16)
-    pair = lax.axis_index("layer") // 2
-    for step in strip_steps(pairs):
-        after = lax.rem(pair + 1, pairs) == jnp.bitwise_xor(pair, step)
-        outs[step][:, phase.shape[1] :] = jnp.where(after, last, first).astype(jnp.bfloat16)
-
-
-def strip_steps(pairs):
-    return [2**k - 1 for k in range(1, pairs.bit_length())]
-
-
-def shifted_rows(shift, odd, own, near, edges):
-    own, near, edges = [block.astype(jnp.float32) for block in (own, near, edges)]
+    second = lax.rem(lax.axis_index("layer"), 2) == 1
+    passed[...] = jnp.where(second, first, last).astype(jnp.bfloat16)
+
+
+def shifted_rows(shift, odd, own, near, far):
+    own, near, far = [block.astype(jnp.float32) for block in (own, near, far)]
     rows = own.shape[0]
-    before = jnp.where(odd, near[rows - 16 :], edges[16:])
-    after = jnp.where(odd, edges[:16], near[:16])
+    before = jnp.where(odd, near[16:], far[16:])
+    after = jnp.where(odd, far[:16], near[:16])
     shift = jnp.where(shift < 0, shift + rows + 32, shift)
     return pltpu.roll(stack(before, own, after), shift, 0)[16 : 16 + rows]
 
 
-def shift_kernel(pairs, wind_hbm, own, near, diagonal0, diagonal1, taken, partner_strips, *refs):
-    messages, (out, wind, sem) = refs[:-3], refs[-3:]
+def shift_kernel(wind_hbm, own, near0, near1, diagonal0, diagonal1, taken, partner_strips, came, out, wind, sem):
     load = fetch((wind_hbm, wind, sem))[0]
     layers, rows, cols = own.shape
     odd = lax.rem(lax.axis_index("dir"), 2) == 1
-    half = taken.shape[1] - 32
-    pair, second = lax.axis_index("layer") // 2, lax.rem(lax.axis_index("layer"), 2) == 1
-    before = jnp.bitwise_xor(pair, lax.rem(pair + pairs - 1, pairs))
-    after = jnp.bitwise_xor(pair, lax.rem(pair + 1, pairs))
-    left = partner_strips[:STRIP].astype(jnp.float32)
-    right = partner_strips[STRIP:].astype(jnp.float32)
-    for step, message in zip(strip_steps(pairs), messages):
-        strip = message[:, message.shape[1] - rows :].astype(jnp.float32)
-        left = jnp.where(jnp.logical_and(before == step, jnp.logical_not(second)), strip, left)
-        right = jnp.where(jnp.logical_and(after == step, second), strip, right)
+    half = taken.shape[1] - 64
+    second = lax.rem(lax.axis_index("layer"), 2) == 1
+    other = came[...].astype(jnp.float32)
+    left = jnp.where(second, partner_strips[:STRIP].astype(jnp.float32), other)
+    right = jnp.where(second, other, partner_strips[STRIP:].astype(jnp.float32))
     strips = stack(left, right, jnp.zeros((LANES - 2 * STRIP, rows), jnp.float32)).T
     lane = lax.broadcasted_iota(jnp.int32, (rows, LANES), 1)
     load.wait()
@@ -334,11 +317,13 @@
         last = pltpu.roll(strips, LANES - WIND_MAX * (level + 1), 1)
         first = pltpu.roll(strips, LANES - STRIP - WIND_MAX * level, 1)
         extra = jnp.where(lane < WIND_MAX, first, last)
-        chunks = [stack(part[level, :16], part[level, rows - 16 :]) for part in (diagonal0, diagonal1)]
-        here = beside(*chunks).astype(jnp.float32)
-        there = taken[level, half:].astype(jnp.float32)
-        edges = beside(jnp.where(odd, there, here), jnp.where(odd, here, there))
-        moved = shifted_rows(wind[0, level], odd, own[level], near[level], edges)
+        pair = []
+        for at, parts in ((half, (diagonal0, diagonal1)), (half + 32, (near0, near1))):
+            here = beside(*[stack(part[level, :16], part[level, rows - 16 :]) for part in parts])
+            here, there = here.astype(jnp.float32), taken[level, at : at + 32].astype(jnp.float32)
+            pair.append(beside(jnp.where(odd, there, here), jnp.where(odd, here, there)))
+        far, near = pair
+        moved = shifted_rows(wind[0, level], odd, own[level], near, far)
         shift = wind[1, level]
         shift = jnp.where(shift < 0, shift + cols + LANES, shift)
         out[level] = pltpu.roll(beside(moved, extra), shift, 1)[:, :cols].astype(jnp.bfloat16)
@@ -462,37 +447,39 @@
 
     width = cols_dev // 4
     chunk = shape(layers, rows_dev, width)
-    own, keep0, keep1, give0, give1 = call(
+    keep0, keep1, give0, give1 = call(
         split_kernel,
-        [shape(*screens.shape)] + [chunk] * 4,
+        [chunk] * 4,
         (screens,),
         0,
         "split",
         in_hbm=(0,),
-        scratch=[sem((5,))],
+        scratch=[sem((4,))],
         brief=True,
     )
     across0 = swap(keep0, 2)
     diagonal0 = swap(give0, 3)
+    near0 = swap(give0, 1)
     across1 = swap(keep1, 2)
     diagonal1 = swap(give1, 3)
     ones = np.kron(np.eye(LANES // SUB_PIX), np.ones((SUB_PIX, SUB_PIX))).astype(np.float32)
     optics_in = (amplitude, jnp.asarray(ones), *[jnp.asarray(table) for table in tables_of(rows)])
-    copies = [shape(*array.shape, dtype=f32) for array in optics_in]
+    copies = [shape(*array.shape, dtype=array.dtype) for array in (screens, *optics_in)]
     row_weights, *tables = call(
         functools.partial(weights_kernel, (n_layer, rows_dev, cols_dev * n_layer)),
         [shape(2, layers, pupil_rows, 4 * rows_dev)]
         + [shape(8, pupil_cols, dtype=dtype) for dtype in (jnp.int32, jnp.int32, f32, f32)]
         + copies,
-        (wind, offsets, ratio, *optics_in),
+        (wind, offsets, ratio, screens, *optics_in),
         0,
         "weights",
-        in_hbm=range(3, 7),
-        scratch=[smem(array.shape, jnp.int32) for array in (wind, offsets, ratio)] + [sem((7,))],
+        in_hbm=range(3, 8),
+        scratch=[smem(array.shape, jnp.int32) for array in (wind, offsets, ratio)] + [sem((8,))],
         brief=True,
     )
-    tables, optics_in = tables[:4], tables[4:]
-    near = swap(own, 1)
+    tables, own, optics_in = tables[:4], tables[4], tables[5:]
+    give1, own = lax.optimization_barrier((give1, own))
+    near1 = swap(give1, 1)
     tables = tuple(tables)
     across0, diagonal0, row_weights, tables = lax.optimization_barrier((across0, diagonal0, row_weights, tables))
 
@@ -500,7 +487,7 @@
     mine0, sibling0, other0, sibling_other0 = call(
         first_rows_kernel,
         [projected] * 4,
-        (row_weights, keep0, near, across0, diagonal0),
+        (row_weights, across0, diagonal0, near0, keep0),
         0,
         "rows_first",
         brief=True,
@@ -516,8 +503,8 @@
     message = shape(layers * half + STRIP * rows_dev // LANES, width)
     mine1, give, other1, sibling_other1 = call(
         later_rows_kernel,
-        [projected, shape(layers, half + 32, 2 * width), message, message],
-        (wind, row_weights, keep0, across0, diagonal0, keep1, across1, diagonal1, near, sibling0),
+        [projected, shape(layers, half + 64, 2 * width), message, message],
+        (wind, row_weights, across1, diagonal1, near1, keep1, across0, diagonal0, near0, keep0, sibling0),
         0,
         "rows_later",
         scratch=wind_scratch,
@@ -535,17 +522,19 @@
         "phase",
     )
 
-    steps = strip_steps(pairs)
-    *sums, strips = call(
+    *sums, strips, passed = call(
         last_kernel,
-        [shape(rows, pupil_cols + (rows_dev if k in steps else 0)) for k in range(pairs)] + [shape(2 * STRIP, rows_dev)],
+        [shape(rows, pupil_cols)] * pairs + [shape(2 * STRIP, rows_dev), shape(STRIP, rows_dev)],
         (cols, others, phase, taken, came1, sibling_came1),
         300_000_000,
         "last",
     )
-    received = list(sums)
-    for k in range(pairs - 1, 0, -1):
-        received[k] = lax.ppermute(sums[k], "layer", [(i, i ^ (2 * k)) for i in range(n_layer)])
+    order = sorted(range(1, pairs), key=lambda k: (-(k & (pairs // 2)), k))
+    received = [sums[0]] + [
+        lax.ppermute(sums[k], "layer", [(i, i ^ (2 * k)) for i in range(n_layer)]) for k in order
+    ]
+    steps = [(i, (i - 2 if i % 2 else i + 2) % n_layer) for i in range(n_layer)]
+    came = lax.ppermute(passed, "layer", steps)
 
     optics_in, received[0] = lax.optimization_barrier((optics_in, received[0]))
     optics = call(
@@ -560,10 +549,11 @@
         30_000_000,
         "optics",
     )
+    came, received[1] = lax.optimization_barrier((came, received[1]))
     new_screens = call(
-        functools.partial(shift_kernel, pairs),
+        shift_kernel,
         shape(layers, rows_dev, cols_dev),
-        (wind, own, near, diagonal0, diagonal1, taken, strips, *[received[k] for k in steps]),
+        (wind, own, near0, near1, diagonal0, diagonal1, taken, strips, came),
         1_000_000,
         "shift",
         scratch=wind_scratch,

time: 38.9 us -> 38.5 us (0.990)
  waiting for transfers between devices: 9.54 us -> 7.75 us
  starting transfers between devices: 14.2 us -> 15.8 us
    ppermute x3, waiting for transfers between devices: 5.36 us -> 0.01 us  [per_device(): lax.ppermute(sums[k], 'layer', [(i, i ^ 2 * k) for i in range(n_layer)])]
    ppermute x0 -> x1, waiting for transfers between devices: none -> 4.18 us  [per_device(): came = lax.ppermute(passed, 'layer', steps)]
    ppermute x0 -> x1, starting transfers between devices: none -> 1.8 us  [per_device(): came = lax.ppermute(passed, 'layer', steps)]
    ppermute x6 -> x7, waiting for transfers between devices: 1.43 us -> 0.59 us  [swap(): return lax.ppermute(value, 'dir', [(i, i ^ bits) for i in range(n_dir)])]
    ppermute x3, starting transfers between devices: 4.71 us -> 4.16 us  [per_device(): lax.ppermute(sums[k], 'layer', [(i, i ^ 2 * k) for i in range(n_layer)])]
    ppermute x6 -> x7, starting transfers between devices: 5.51 us -> 5.48 us  [swap(): return lax.ppermute(value, 'dir', [(i, i ^ bits) for i in range(n_dir)])]
  transfers between devices with their start and end apart: 13 -> 15, of which waited for: 5 -> 4; matrix products, arithmetic and copies ran while one was open for 0% -> 0% of each run, Pallas kernels for 27% -> 28%
where the time goes in v9:
time: 38.5 us; the launch traced here: 38.3 us
  starting transfers between devices  15.8 us (41%)
  Pallas kernels  14 us (36%)
  waiting for transfers between devices  7.75 us (20%)
  between operations  0.77 us (2%)
    pallas_call x10, Pallas kernels, call(): pl.pallas_call(kernel, out_shape=out_shape, in_specs=in_specs, out_specs=...  14 us
    ppermute x7, starting transfers between devices, swap(): return lax.ppermute(value, 'dir', [(i, i ^ bits) for i in range(n_dir)])  5.48 us
    ppermute x4, starting transfers between devices, partner(): lax.ppermute(value, ('layer', 'dir'), [(i, i ^ n_dir ^ bits) for i in ran...  4.32 us
    ppermute x1, waiting for transfers between devices, per_device(): came = lax.ppermute(passed, 'layer', steps)  4.18 us
    ppermute x3, starting transfers between devices, per_device(): lax.ppermute(sums[k], 'layer', [(i, i ^ 2 * k) for i in range(n_layer)])  4.16 us
    ppermute x4, waiting for transfers between devices, partner(): lax.ppermute(value, ('layer', 'dir'), [(i, i ^ n_dir ^ bits) for i in ran...  2.98 us
    ppermute x1, starting transfers between devices, per_device(): came = lax.ppermute(passed, 'layer', steps)  1.8 us
  transfers between devices with their start and end apart: 15, of which 4 were waited for; matrix products, arithmetic and copies ran while one was open for 0% of the time, Pallas kernels for 28%

profile of v9, /device:TPU:0, one launch (start us, length us, event | category | flops | bytes accessed | tf_op | source)
XLA Modules:
  0.0 38.3 jit_solution(3137535892250122348)
XLA Ops:
  0.6 1.1 %split.1 = (bf16[3,128,128]{2,1,0:T(8,128)(2,1)S(1)}, bf16[3,128,128]{2,1,0:T(8,128)(2,1)S(1)}, bf16[3,128,128]{2,1,0:T(8,128)(2,1)S(1)}, bf16[3,128,128]{2,1,0:T(8,128)(2,1)S(1)}) custom-call(bf16[3,128,512]{2,1,0:T(8,128)(2,1)} %refs_0_.1), custom_call_target="tpu_custom_call" | custom-call | tf_op jit(solution)/shard_map/split/pallas_call | solution.py:40
  1.7 2.4 %collective-permute-start.3 = (bf16[3,128,128]{2,1,0:T(8,128)(2,1)S(1)}, bf16[3,128,128]{2,1,0:T(8,128)(2,1)S(1)}, u32[]{:S(2)}, u32[]{:S(2)}) collective-permute-start(bf16[3,128,128]{2,1,0:T(8,128)(2,1)S(1)} %get-tuple-element.62), channel_id=1, source_target_pairs={{0,3},{1,2},{2,1},{3,0},{4,7},{5,6},{6,5},{7,4},{8,11},{9,10},{10,... | collective-permute-start | bytes 294920 | tf_op jit(solution)/shard_map/ppermute | solution.py:439
  4.2 0.6 %collective-permute-start.2 = (bf16[3,128,128]{2,1,0:T(8,128)(2,1)S(1)}, bf16[3,128,128]{2,1,0:T(8,128)(2,1)S(1)}, u32[]{:S(2)}, u32[]{:S(2)}) collective-permute-start(bf16[3,128,128]{2,1,0:T(8,128)(2,1)S(1)} %get-tuple-element.64.keep.refs_7_), channel_id=1, source_target_pairs={{0,2},{1,3},{2,0},{3,1},{4,6},{5,7},{6,4},{7,5},{8,10},{9,11},{10,... | collective-permute-start | bytes 294920 | tf_op jit(solution)/shard_map/ppermute | solution.py:439
  4.8 0.0 collective-permute-start
  4.8 1.5 %collective-permute-start.4 = (bf16[3,128,128]{2,1,0:T(8,128)(2,1)S(1)}, bf16[3,128,128]{2,1,0:T(8,128)(2,1)S(1)}, u32[]{:S(2)}, u32[]{:S(2)}) collective-permute-start(bf16[3,128,128]{2,1,0:T(8,128)(2,1)S(1)} %get-tuple-element.63), channel_id=1, source_target_pairs={{0,3},{1,2},{2,1},{3,0},{4,7},{5,6},{6,5},{7,4},{8,11},{9,10},{10,... | collective-permute-start | bytes 294920 | tf_op jit(solution)/shard_map/ppermute | solution.py:439
  6.3 0.6 %collective-permute-start.5 = (bf16[3,128,128]{2,1,0:T(8,128)(2,1)S(1)}, bf16[3,128,128]{2,1,0:T(8,128)(2,1)S(1)}, u32[]{:S(2)}, u32[]{:S(2)}) collective-permute-start(bf16[3,128,128]{2,1,0:T(8,128)(2,1)S(1)} %get-tuple-element.72.refs_3_), channel_id=1, source_target_pairs={{0,2},{1,3},{2,0},{3,1},{4,6},{5,7},{6,4},{7,5},{8,10},{9,11},{10,... | collective-permute-start | bytes 294920 | tf_op jit(solution)/shard_map/ppermute | solution.py:439
  7.0 2.2 %weights.1 = (bf16[2,3,256,512]{3,2,1,0:T(8,128)(2,1)S(1)}, s32[8,1280]{1,0:T(8,128)S(1)}, s32[8,1280]{1,0:T(8,128)S(1)}, f32[8,1280]{1,0:T(8,128)S(1)}, f32[8,1...) custom-call(s32[2,3]{1,0:T(2,128)} %bitcast.5, ...), custom_call_target="tpu_custom_call" | custom-call | tf_op jit(solution)/shard_map/weights/pallas_call | solution.py:40
  9.2 0.0 collective-permute-done.3.diagonal.refs_5_.diagonal0
  9.2 0.1 collective-permute-start.1
  9.3 0.6 %collective-permute-done.2.across.refs_4_ = bf16[3,128,128]{2,1,0:T(8,128)(2,1)S(1)} collective-permute-done((bf16[3,128,128]{2,1,0:T(8,128)(2,1)S(1)}, bf16[3,128,128]{2,1,0:T(8,128)(2,1)S(1)}, u32[]{:S(2)}, u32[]{:S(2)}) %collective-permute-start.2) | collective-permute-done | bytes 98336 | tf_op jit(solution)/shard_map/ppermute | solution.py:439
  9.8 0.6 %rows_first.1 = (bf16[3,128,128]{2,1,0:T(8,128)(2,1)S(1)}, bf16[3,128,128]{2,1,0:T(8,128)(2,1)S(1)}, bf16[3,128,128]{2,1,0:T(8,128)(2,1)S(1)}, bf16[3,128,128]{2,1,0:T(8,128)(2,1)S(1)}) custom-call(bf16[2,3,256,512]{3,2,1,0:T(8,128)(2,1)S(1)} %get-tuple-element.71.rows_ref, bf16[3,128,128]{2,1,0:T(8,128)(2,1)S(1)} %collective-permute-done.2.across.refs_4_, ...), custom_call_target="tpu_custom_call" | custom-call | tf_op jit(solution)/shard_map/rows_first/pallas_call | solution.py:40
  10.4 2.2 %collective-permute-start.7 = (bf16[3,128,128]{2,1,0:T(8,128)(2,1)S(1)}, bf16[3,128,128]{2,1,0:T(8,128)(2,1)S(1)}, u32[]{:S(2)}, u32[]{:S(2)}) collective-permute-start(bf16[3,128,128]{2,1,0:T(8,128)(2,1)S(1)} %get-tuple-element.89), channel_id=1, source_target_pairs={{0,4},{1,5},{2,6},{3,7},{4,0},{5,1},{6,2},{7,3},{8,12},{9,13},{10,... | collective-permute-start | bytes 294920 | tf_op jit(solution)/shard_map/ppermute | solution.py:443
  12.7 1.5 %columns.1.refs_4_.mine_ref = bf16[3,512,1280]{2,1,0:T(8,128)(2,1)S(1)} custom-call(s32[8,1280]{1,0:T(8,128)S(1)} %get-tuple-element.79.refs_0_, s32[8,1280]{1,0:T(8,128)S(1)} %get-tuple-element.80.refs_1_, f32[8,1280]{1,0:T(8,128)S(1)} %get-tuple-element.81.refs_2_, f32[8,1280]{1,0:T(8,128)S(1)} %get-tuple-element.82.refs_3_), custom_call_target="tpu_custom_call" | custom-call | tf_op jit(solution)/shard_map/columns/pallas_call | solution.py:40
  14.1 0.0 collective-permute-done.4.refs_1_.diagonal1
  14.1 0.0 collective-permute-done.1.refs_2_.near1
  14.2 1.5 %rows_later.1 = (bf16[3,128,128]{2,1,0:T(8,128)(2,1)S(1)}, bf16[3,192,256]{2,1,0:T(8,128)(2,1)S(1)}, bf16[416,128]{1,0:T(8,128)(2,1)S(1)}, bf16[416,128]{1,0:T(8,128)(2,1)S(1)}) custom-call(s32[2,3]{1,0:T(2,128)} %bitcast.6, bf16[2,3,256,512]{3,2,1,0:T(8,128)(2,1)S(1)} %get-tuple-element.71.rows_ref, ...), custom_call_target="tpu_custom_call" | custom-call | tf_op jit(solution)/shard_map/rows_later/pallas_call | solution.py:40
  15.6 2.1 %collective-permute-start.9 = (bf16[416,128]{1,0:T(8,128)(2,1)S(1)}, bf16[416,128]{1,0:T(8,128)(2,1)S(1)}, u32[]{:S(2)}, u32[]{:S(2)}) collective-permute-start(bf16[416,128]{1,0:T(8,128)(2,1)S(1)} %get-tuple-element.93), channel_id=1, source_target_pairs={{0,4},{1,5},{2,6},{3,7},{4,0},{5,1},{6,2},{7,3},{8,12},{9,13},{10,... | collective-permute-start | bytes 319496 | tf_op jit(solution)/shard_map/ppermute | solution.py:443
  17.7 0.2 collective-permute-start.6
  17.9 2.1 %phase.1 = (f32[128,1280]{1,0:T(8,128)S(1)}, bf16[3,512,1280]{2,1,0:T(8,128)(2,1)S(1)}) custom-call(s32[8,1280]{1,0:T(8,128)S(1)} %get-tuple-element.79.refs_0_, s32[8,1280]{1,0:T(8,128)S(1)} %get-tuple-element.80.refs_1_, f32[8,1280]{1,0:T(8,128)S(1)} %get-tuple-element.81.refs_2_, f32[8,1280]{1,0:T(8,128)S(1)} %get-tuple-element.82.refs_3_, ...), custom_call_target="tpu_custom_call" | custom-call | flops 10000000000 | bytes 9076736 | tf_op jit(solution)/shard_map/phase/pallas_call | solution.py:40
  20.1 1.1 %collective-permute-done.9.came = bf16[416,128]{1,0:T(8,128)(2,1)S(1)} collective-permute-done((bf16[416,128]{1,0:T(8,128)(2,1)S(1)}, bf16[416,128]{1,0:T(8,128)(2,1)S(1)}, u32[]{:S(2)}, u32[]{:S(2)}) %collective-permute-start.9) | collective-permute-done | bytes 106528 | tf_op jit(solution)/shard_map/ppermute | solution.py:443
  21.2 1.9 %collective-permute-done.10.sibling_came = bf16[416,128]{1,0:T(8,128)(2,1)S(1)} collective-permute-done((bf16[416,128]{1,0:T(8,128)(2,1)S(1)}, bf16[416,128]{1,0:T(8,128)(2,1)S(1)}, u32[]{:S(2)}, u32[]{:S(2)}) %collective-permute-start.10) | collective-permute-done | bytes 106528 | tf_op jit(solution)/shard_map/ppermute | solution.py:443
  23.0 0.7 %last.1 = (bf16[32,1280]{1,0:T(8,128)(2,1)S(1)}, bf16[32,1280]{1,0:T(8,128)(2,1)S(1)}, bf16[32,1280]{1,0:T(8,128)(2,1)S(1)}, bf16[32,1280]{1,0:T(8,128)(2,1)S(1)...) custom-call(bf16[3,512,1280]{2,1,0:T(8,128)(2,1)S(1)} %columns.1.refs_4_.mine_ref, ...), custom_call_target="tpu_custom_call" | custom-call | flops 300000000 | bytes 9379840 | tf_op jit(solution)/shard_map/last/pallas_call | solution.py:40
  23.8 2.6 %collective-permute-start.12 = (bf16[32,1280]{1,0:T(8,128)(2,1)S(1)}, bf16[32,1280]{1,0:T(8,128)(2,1)S(1)}, u32[]{:S(2)}, u32[]{:S(2)}) collective-permute-start(bf16[32,1280]{1,0:T(8,128)(2,1)S(1)} %get-tuple-element.97), channel_id=1, source_target_pairs={{0,16},{4,20},{8,24},{12,28},{16,0},{20,4},{24,8},{28,12},{1,17},{... | collective-permute-start | bytes 245768 | tf_op jit(solution)/shard_map/ppermute | solution.py:534
  26.3 1.3 %collective-permute-start.13 = (bf16[32,1280]{1,0:T(8,128)(2,1)S(1)}, bf16[32,1280]{1,0:T(8,128)(2,1)S(1)}, u32[]{:S(2)}, u32[]{:S(2)}) collective-permute-start(bf16[32,1280]{1,0:T(8,128)(2,1)S(1)} %get-tuple-element.106), channel_id=1, source_target_pairs={{0,24},{4,28},{8,16},{12,20},{16,8},{20,12},{24,0},{28,4},{1,25},{... | collective-permute-start | bytes 245768 | tf_op jit(solution)/shard_map/ppermute | solution.py:534
  27.7 0.2 collective-permute-start.14
  27.9 1.8 %collective-permute-start.11 = (bf16[32,128]{1,0:T(8,128)(2,1)S(1)}, bf16[32,128]{1,0:T(8,128)(2,1)S(1)}, u32[]{:S(2)}, u32[]{:S(2)}) collective-permute-start(bf16[32,128]{1,0:T(8,128)(2,1)S(1)} %get-tuple-element.96), channel_id=1, source_target_pairs={{0,8},{4,28},{8,16},{12,4},{16,24},{20,12},{24,0},{28,20},{1,9},{5... | collective-permute-start | bytes 24584 | tf_op jit(solution)/shard_map/ppermute | solution.py:537
  29.7 0.7 %optics.1 = (f32[32,1280]{1,0:T(8,128)S(1)}, bf16[256,512]{1,0:T(8,128)(2,1)S(1)}, bf16[256,512]{1,0:T(8,128)(2,1)S(1)}, bf16[128,192]{1,0:T(8,128)(2,1)S(1)}) custom-call(f32[32,1280]{1,0:T(8,128)S(1)} %get-tuple-element.108.amplitude, f32[128,128]{1,0:T(8,128)S(1)} %get-tuple-element.109.ones, f32[256,512]{1,0:T(8,128)S(1)} %get-tuple-element.110.columns, ...), custom_call_target="tpu_custom_call" | custom-call | flops 30000000 | bytes 1523712 | tf_op jit(solution)/shard_map/optics/pallas_call | solution.py:40
  30.4 4.2 %collective-permute-done.11.came = bf16[32,128]{1,0:T(8,128)(2,1)S(1)} collective-permute-done((bf16[32,128]{1,0:T(8,128)(2,1)S(1)}, bf16[32,128]{1,0:T(8,128)(2,1)S(1)}, u32[]{:S(2)}, u32[]{:S(2)}) %collective-permute-start.11) | collective-permute-done | bytes 8224 | tf_op jit(solution)/shard_map/ppermute | solution.py:537
  34.6 0.0 collective-permute-done.12.refs_1_
  34.6 2.0 %shift.1 = bf16[3,128,512]{2,1,0:T(8,128)(2,1)} custom-call(s32[2,3]{1,0:T(2,128)} %bitcast.7, bf16[3,128,512]{2,1,0:T(8,128)(2,1)S(1)} %get-tuple-element.61.own, bf16[3,128,128]{2,1,0:T(8,128)(2,1)S(1)} %collective-permute-done.near.refs_6_.near0, bf16[3,128,128]{2,1,0:T(8,128)(2,1)S(1)} %collective-permute-done.1.refs_2_.near1, ...), custom_call_target="tpu_custom_call" | custom-call | flops 1000000 | bytes 1499160 | tf_op jit(solution)/shard_map/shift/pallas_call | solution.py:40
  36.6 0.0 collective-permute-done.13.refs_2_
  36.6 1.7 %imaging.1 = f32[64,2560]{1,0:T(8,128)} custom-call(bf16[32,1280]{1,0:T(8,128)(2,1)S(1)} %get-tuple-element.104.refs_0_, bf16[32,1280]{1,0:T(8,128)(2,1)S(1)} %collective-permute-done.12.refs_1_, bf16[32,1280]{1,0:T(8,128)(2,1)S(1)} %collective-permute-done.13.refs_2_, bf16[32,1280]{1,0:T(8,128)(2,1)S(1)} %collective-permute-done.14.refs_3_, ...), custom_call_target="tpu_custom_call" | custom-call | flops 400000000 | bytes 1720320 | tf_op jit(solution)/shard_map/imaging/pallas_call | solution.py:40
  (8 shorter events, 0.0 us)
Async XLA Ops:
  1.7 7.5 %collective-permute-start.3 = (bf16[3,128,128]{2,1,0:T(8,128)(2,1)S(1)}, bf16[3,128,128]{2,1,0:T(8,128)(2,1)S(1)}, u32[]{:S(2)}, u32[]{:S(2)}) collective-permute-start(bf16[3,128,128]{2,1,0:T(8,128)(2,1)S(1)} %get-tuple-element.62), channel_id=1, source_target_pairs={{0,3},{1,2},{2,1},{3,0},{4,7},{5,6},{6,5},{7,4},{8,11},{9,10},{10,... | collective-permute-start | bytes 294920 | tf_op jit(solution)/shard_map/ppermute | solution.py:439
  4.2 5.7 %collective-permute-start.2 = (bf16[3,128,128]{2,1,0:T(8,128)(2,1)S(1)}, bf16[3,128,128]{2,1,0:T(8,128)(2,1)S(1)}, u32[]{:S(2)}, u32[]{:S(2)}) collective-permute-start(bf16[3,128,128]{2,1,0:T(8,128)(2,1)S(1)} %get-tuple-element.64.keep.refs_7_), channel_id=1, source_target_pairs={{0,2},{1,3},{2,0},{3,1},{4,6},{5,7},{6,4},{7,5},{8,10},{9,11},{10,... | collective-permute-start | bytes 294920 | tf_op jit(solution)/shard_map/ppermute | solution.py:439
  4.8 5.0 %collective-permute-start = (bf16[3,128,128]{2,1,0:T(8,128)(2,1)S(1)}, bf16[3,128,128]{2,1,0:T(8,128)(2,1)S(1)}, u32[]{:S(2)}, u32[]{:S(2)}) collective-permute-start(bf16[3,128,128]{2,1,0:T(8,128)(2,1)S(1)} %get-tuple-element.62), channel_id=1, source_target_pairs={{0,1},{1,0},{2,3},{3,2},{4,5},{5,4},{6,7},{7,6},{8,9},{9,8},{10,11... | collective-permute-start | bytes 294920 | tf_op jit(solution)/shard_map/ppermute | solution.py:439
  4.8 9.3 %collective-permute-start.4 = (bf16[3,128,128]{2,1,0:T(8,128)(2,1)S(1)}, bf16[3,128,128]{2,1,0:T(8,128)(2,1)S(1)}, u32[]{:S(2)}, u32[]{:S(2)}) collective-permute-start(bf16[3,128,128]{2,1,0:T(8,128)(2,1)S(1)} %get-tuple-element.63), channel_id=1, source_target_pairs={{0,3},{1,2},{2,1},{3,0},{4,7},{5,6},{6,5},{7,4},{8,11},{9,10},{10,... | collective-permute-start | bytes 294920 | tf_op jit(solution)/shard_map/ppermute | solution.py:439
  6.3 7.8 %collective-permute-start.5 = (bf16[3,128,128]{2,1,0:T(8,128)(2,1)S(1)}, bf16[3,128,128]{2,1,0:T(8,128)(2,1)S(1)}, u32[]{:S(2)}, u32[]{:S(2)}) collective-permute-start(bf16[3,128,128]{2,1,0:T(8,128)(2,1)S(1)} %get-tuple-element.72.refs_3_), channel_id=1, source_target_pairs={{0,2},{1,3},{2,0},{3,1},{4,6},{5,7},{6,4},{7,5},{8,10},{9,11},{10,... | collective-permute-start | bytes 294920 | tf_op jit(solution)/shard_map/ppermute | solution.py:439
  9.2 5.0 %collective-permute-start.1 = (bf16[3,128,128]{2,1,0:T(8,128)(2,1)S(1)}, bf16[3,128,128]{2,1,0:T(8,128)(2,1)S(1)}, u32[]{:S(2)}, u32[]{:S(2)}) collective-permute-start(bf16[3,128,128]{2,1,0:T(8,128)(2,1)S(1)} %get-tuple-element.63), channel_id=1, source_target_pairs={{0,1},{1,0},{2,3},{3,2},{4,5},{5,4},{6,7},{7,6},{8,9},{9,8},{10,11... | collective-permute-start | bytes 294920 | tf_op jit(solution)/shard_map/ppermute | solution.py:439
  10.4 7.5 %collective-permute-start.7 = (bf16[3,128,128]{2,1,0:T(8,128)(2,1)S(1)}, bf16[3,128,128]{2,1,0:T(8,128)(2,1)S(1)}, u32[]{:S(2)}, u32[]{:S(2)}) collective-permute-start(bf16[3,128,128]{2,1,0:T(8,128)(2,1)S(1)} %get-tuple-element.89), channel_id=1, source_target_pairs={{0,4},{1,5},{2,6},{3,7},{4,0},{5,1},{6,2},{7,3},{8,12},{9,13},{10,... | collective-permute-start | bytes 294920 | tf_op jit(solution)/shard_map/ppermute | solution.py:443
  12.7 5.3 %collective-permute-start.8 = (bf16[3,128,128]{2,1,0:T(8,128)(2,1)S(1)}, bf16[3,128,128]{2,1,0:T(8,128)(2,1)S(1)}, u32[]{:S(2)}, u32[]{:S(2)}) collective-permute-start(bf16[3,128,128]{2,1,0:T(8,128)(2,1)S(1)} %get-tuple-element.90), channel_id=1, source_target_pairs={{0,5},{1,4},{2,7},{3,6},{4,1},{5,0},{6,3},{7,2},{8,13},{9,12},{10,... | collective-permute-start | bytes 294920 | tf_op jit(solution)/shard_map/ppermute | solution.py:443
  15.6 5.5 %collective-permute-start.9 = (bf16[416,128]{1,0:T(8,128)(2,1)S(1)}, bf16[416,128]{1,0:T(8,128)(2,1)S(1)}, u32[]{:S(2)}, u32[]{:S(2)}) collective-permute-start(bf16[416,128]{1,0:T(8,128)(2,1)S(1)} %get-tuple-element.93), channel_id=1, source_target_pairs={{0,4},{1,5},{2,6},{3,7},{4,0},{5,1},{6,2},{7,3},{8,12},{9,13},{10,... | collective-permute-start | bytes 319496 | tf_op jit(solution)/shard_map/ppermute | solution.py:443
  17.7 5.3 %collective-permute-start.10 = (bf16[416,128]{1,0:T(8,128)(2,1)S(1)}, bf16[416,128]{1,0:T(8,128)(2,1)S(1)}, u32[]{:S(2)}, u32[]{:S(2)}) collective-permute-start(bf16[416,128]{1,0:T(8,128)(2,1)S(1)} %get-tuple-element.94), channel_id=1, source_target_pairs={{0,5},{1,4},{2,7},{3,6},{4,1},{5,0},{6,3},{7,2},{8,13},{9,12},{10,... | collective-permute-start | bytes 319496 | tf_op jit(solution)/shard_map/ppermute | solution.py:443
  17.7 5.3 %collective-permute-start.6 = (bf16[3,192,256]{2,1,0:T(8,128)(2,1)S(1)}, bf16[3,192,256]{2,1,0:T(8,128)(2,1)S(1)}, u32[]{:S(2)}, u32[]{:S(2)}) collective-permute-start(bf16[3,192,256]{2,1,0:T(8,128)(2,1)S(1)} %get-tuple-element.85), channel_id=1, source_target_pairs={{0,1},{1,0},{2,3},{3,2},{4,5},{5,4},{6,7},{7,6},{8,9},{9,8},{10,11... | collective-permute-start | bytes 884744 | tf_op jit(solution)/shard_map/ppermute | solution.py:439
  23.8 10.8 %collective-permute-start.12 = (bf16[32,1280]{1,0:T(8,128)(2,1)S(1)}, bf16[32,1280]{1,0:T(8,128)(2,1)S(1)}, u32[]{:S(2)}, u32[]{:S(2)}) collective-permute-start(bf16[32,1280]{1,0:T(8,128)(2,1)S(1)} %get-tuple-element.97), channel_id=1, source_target_pairs={{0,16},{4,20},{8,24},{12,28},{16,0},{20,4},{24,8},{28,12},{1,17},{... | collective-permute-start | bytes 245768 | tf_op jit(solution)/shard_map/ppermute | solution.py:534
  26.3 10.3 %collective-permute-start.13 = (bf16[32,1280]{1,0:T(8,128)(2,1)S(1)}, bf16[32,1280]{1,0:T(8,128)(2,1)S(1)}, u32[]{:S(2)}, u32[]{:S(2)}) collective-permute-start(bf16[32,1280]{1,0:T(8,128)(2,1)S(1)} %get-tuple-element.106), channel_id=1, source_target_pairs={{0,24},{4,28},{8,16},{12,20},{16,8},{20,12},{24,0},{28,4},{1,25},{... | collective-permute-start | bytes 245768 | tf_op jit(solution)/shard_map/ppermute | solution.py:534
  27.7 8.9 %collective-permute-start.14 = (bf16[32,1280]{1,0:T(8,128)(2,1)S(1)}, bf16[32,1280]{1,0:T(8,128)(2,1)S(1)}, u32[]{:S(2)}, u32[]{:S(2)}) collective-permute-start(bf16[32,1280]{1,0:T(8,128)(2,1)S(1)} %get-tuple-element.107), channel_id=1, source_target_pairs={{0,8},{4,12},{8,0},{12,4},{16,24},{20,28},{24,16},{28,20},{1,9},{5... | collective-permute-start | bytes 245768 | tf_op jit(solution)/shard_map/ppermute | solution.py:534
  27.9 6.6 %collective-permute-start.11 = (bf16[32,128]{1,0:T(8,128)(2,1)S(1)}, bf16[32,128]{1,0:T(8,128)(2,1)S(1)}, u32[]{:S(2)}, u32[]{:S(2)}) collective-permute-start(bf16[32,128]{1,0:T(8,128)(2,1)S(1)} %get-tuple-element.96), channel_id=1, source_target_pairs={{0,8},{4,28},{8,16},{12,4},{16,24},{20,12},{24,0},{28,20},{1,9},{5... | collective-permute-start | bytes 24584 | tf_op jit(solution)/shard_map/ppermute | solution.py:537

commit v10 on v9

--- a/solution.py
+++ b/solution.py
@@ -83,6 +83,10 @@
     return base, upper, 1.0 - fraction, fraction
 
 
+def chunk_start(half, chunk):
+    return 3 * half + chunk * (1 - 2 * half)
+
+
 def split_kernel(screens, *refs):
     outs, sems = refs[:-1], refs[-1]
     width = outs[0].shape[2]
@@ -90,7 +94,7 @@
     pairs = []
     for k, out in enumerate(outs):
         half = core if k < 2 else 1 - core
-        start = pl.multiple_of((2 * half + k % 2) * width, LANES)
+        start = pl.multiple_of(chunk_start(half, k % 2) * width, LANES)
         pairs.append((screens.at[:, :, pl.ds(start, width)], out, sems.at[k]))
     for load in fetch(*pairs):
         load.wait()
@@ -150,31 +154,44 @@
 
 def column_weights(base_ref, upper_ref, low_ref, high_ref, first, out):
     layers, cols_dev, pupil_cols = out.shape
-    half = cols_dev // 2
+    width = cols_dev // 4
     core = lax.rem(lax.axis_index("dir"), 2)
-    sub = lax.broadcasted_iota(jnp.int32, (half, LANES), 0).reshape(half // 8, 8, LANES)
+    sub = lax.broadcasted_iota(jnp.int32, (width, LANES), 0).astype(jnp.float32).astype(jnp.bfloat16)
+    zero = jnp.zeros((width, LANES), jnp.bfloat16)
     for level in range(layers):
 
         def tile(step, carry):
             start = pl.multiple_of(step * LANES, LANES)
             cut = (slice(level, level + 1), pl.ds(start, LANES))
-            base, upper, low, high = [
-                jnp.broadcast_to(ref[cut], (8, LANES)) for ref in (base_ref, upper_ref, low_ref, high_ref)
+            base, upper = base_ref[cut], upper_ref[cut]
+            low, high = [
+                jnp.broadcast_to(ref[cut].astype(jnp.bfloat16), (width, LANES)) for ref in (low_ref, high_ref)
             ]
-            for side in range(2):
-                shift = first + jnp.bitwise_xor(core, side) * half
-                weight = jnp.where(sub == (base - shift)[None], low[None], 0.0)
-                weight = jnp.where(sub == (upper - shift)[None], high[None], weight)
-                weight = weight.reshape(half, LANES).astype(jnp.bfloat16)
-                out[level, side * half : (side + 1) * half, pl.ds(start, LANES)] = weight
+            for k in range(4):
+                shift = first + chunk_start(jnp.bitwise_xor(core, k // 2), k % 2) * width
+                base_at, upper_at = [
+                    jnp.broadcast_to(
+                        jnp.clip(value - shift, -1, width).astype(jnp.float32).astype(jnp.bfloat16), (width, LANES)
+                    )
+                    for value in (base, upper)
+                ]
+                weight = jnp.where(sub == base_at, low, zero)
+                weight = jnp.where(sub == upper_at, high, weight)
+                out[level, k * width : (k + 1) * width, pl.ds(start, LANES)] = weight
             return carry
 
         lax.fori_loop(0, pupil_cols // LANES, tile, 0)
 
 
-def columns_kernel(*refs):
-    tables, out = refs[:4], refs[-1]
+def columns_kernel(wind_hbm, *refs):
+    tables, blocks, (out, strip, sibling_strip, wind, sem) = refs[:4], refs[4:8], refs[8:]
+    load = fetch((wind_hbm, wind, sem))[0]
     column_weights(*tables, lax.axis_index("layer") * out.shape[1], out)
+    across, diagonal, near, keep = blocks
+    core = lax.rem(lax.axis_index("dir"), 2)
+    load.wait()
+    strip[...] = outer_strip(wind, core == 1, keep, near, diagonal)
+    sibling_strip[...] = outer_strip(wind, core == 0, near, keep, across)
 
 
 def project_rows(rows_ref, keep, near, across, diagonal, level):
@@ -192,12 +209,12 @@
 
 
 def outer_strip(wind, odd, own, near, far):
-    rows = own[0].shape[0]
+    layers, rows, _ = own.shape
     core = lax.rem(lax.axis_index("dir"), 2)
     lane = lax.broadcasted_iota(jnp.int32, (rows, LANES), 1)
     strip = jnp.zeros((rows, LANES), jnp.float32)
-    for level in range(len(own)):
-        edges = [stack(block[level][:16], block[level][rows - 16 :]) for block in (near, far)]
+    for level in range(layers):
+        edges = [stack(block[level, :16], block[level, rows - 16 :]) for block in (near, far)]
         moved = shifted_rows(wind[0, level], odd, own[level], *edges)
         at = WIND_MAX * level
         moved = pltpu.roll(moved, at + WIND_MAX * core, 1)
@@ -214,37 +231,29 @@
     return beside(*[ref[start : start + STRIP, :] for start in range(at, ref.shape[0], STRIP)])
 
 
-def later_rows_kernel(wind_hbm, rows_ref, *refs):
-    chunks, sibling0, outs, (wind, sem) = refs[:8], refs[8], refs[9:-2], refs[-2:]
-    mine, give, other, sibling_other = outs
-    load = fetch((wind_hbm, wind, sem))[0]
+def later_rows_kernel(rows_ref, *refs):
+    chunks, refs = refs[:8], refs[8:]
+    sibling0, strip, sibling_strip, mine, give, far, sibling_far, rest, sibling_rest = refs
     across, diagonal, near, keep, across0, diagonal0, near0, keep0 = chunks
     layers, half, width = mine.shape
     rows = near.shape[1]
+    size = (far.shape[0] - STRIP * rows // LANES) // layers
+    start = half - size
     for level in range(layers):
         part = project_rows(rows_ref, keep, near, across, diagonal, level)
         mine[level] = part[:half]
-        other[level * half : (level + 1) * half] = part[half : 2 * half]
-        sibling_other[level * half : (level + 1) * half] = part[3 * half :]
+        for k, out, remainder in ((1, far, rest), (3, sibling_far, sibling_rest)):
+            piece = part[k * half : (k + 1) * half]
+            out[level * size : (level + 1) * size] = piece[start:]
+            remainder[level * start : (level + 1) * start] = piece[:start]
         give[level, :half, :width] = sibling0[level]
         give[level, :half, width:] = part[2 * half : 3 * half]
         for k, blocks in enumerate(((across0, keep0), (across, keep))):
             cut = slice(k * width, (k + 1) * width)
             edges = [block[level, at : at + 16] for block in blocks for at in (0, rows - 16)]
             give[level, half:, cut] = stack(*edges)
-    core = lax.rem(lax.axis_index("dir"), 2)
-
-    def outer(first, second):
-        return [
-            jnp.where(core == 1, second[level].astype(jnp.float32), first[level].astype(jnp.float32))
-            for level in range(layers)
-        ]
-
-    own, far, sibling_far = outer(keep0, keep), outer(diagonal0, diagonal), outer(across0, across)
-    beyond = outer(near0, near)
-    load.wait()
-    put_strip(other, layers * half, outer_strip(wind, core == 1, own, beyond, far))
-    put_strip(sibling_other, layers * half, outer_strip(wind, core == 0, beyond, own, sibling_far))
+    put_strip(far, layers * size, strip)
+    put_strip(sibling_far, layers * size, sibling_strip)
 
 
 def project(parts, cols_refs, at):
@@ -267,29 +276,54 @@
         phase[:, at : at + 256] = project(parts, cuts, at)
 
 
-def last_kernel(mine_ref, cols_ref, phase, taken, came, sibling_came, *outs):
-    *outs, strips, passed = outs
+def sum_up(start, mine_ref, cols_ref, phase, taken, came, sibling_came, outs):
     layers, _, width = taken.shape
     width = width // 2
-    size, half = outs[0].shape[0], phase.shape[0]
+    block = outs[0].shape[0]
+    size = block * len(outs)
+    rows = slice(start, start + size)
     parts, cuts = [], []
     for level in range(layers):
-        cut = slice(level * half, (level + 1) * half)
-        parts += [taken[level, :half], came[cut], sibling_came[cut]]
+        cut = slice(level * size, (level + 1) * size)
+        parts += [taken[level, rows], came[cut], sibling_came[cut]]
         cuts += [(mine_ref, level, 2 * width, 4 * width)]
         cuts += [(cols_ref, level, width, 2 * width), (cols_ref, level, 3 * width, 4 * width)]
-    for at in range(0, phase.shape[1], 256):
-        total = (phase[:, at : at + 256] + project(parts, cuts, at)).astype(jnp.bfloat16)
+    pupil_cols = phase.shape[1]
+    for at in range(0, pupil_cols, 256):
+        total = (phase[rows, at : at + 256] + project(parts, cuts, at)).astype(jnp.bfloat16)
         for k, out in enumerate(outs):
-            out[:, at : at + 256] = total[k * size : (k + 1) * size]
+            out[:, at : at + 256] = total[k * block : (k + 1) * block]
+
+
+def strip_steps(pairs):
+    return [2**k - 1 for k in range(1, pairs.bit_length())]
+
+
+def add_strip(pairs, step, strips, out):
+    pair = lax.axis_index("layer") // 2
+    after = lax.rem(pair + 1, pairs) == jnp.bitwise_xor(pair, step)
+    at = out.shape[1] - strips.shape[1]
+    last, first = strips[:STRIP].astype(jnp.float32), strips[STRIP:].astype(jnp.float32)
+    out[:, at:] = jnp.where(after, last, first).astype(jnp.bfloat16)
+
+
+def far_kernel(mine_ref, cols_ref, phase, taken, came, sibling_came, out, strips):
+    half, size = phase.shape[0], out.shape[0]
+    sum_up(half - size, mine_ref, cols_ref, phase, taken, came, sibling_came, [out])
+    layers = taken.shape[0]
     odd = lax.rem(lax.axis_index("dir"), 2) == 1
-    here = get_strip(came, layers * half).astype(jnp.float32)
-    there = get_strip(sibling_came, layers * half).astype(jnp.float32)
-    last, first = jnp.where(odd, here, there), jnp.where(odd, there, here)
-    strips[:STRIP] = last.astype(jnp.bfloat16)
-    strips[STRIP:] = first.astype(jnp.bfloat16)
-    second = lax.rem(lax.axis_index("layer"), 2) == 1
-    passed[...] = jnp.where(second, first, last).astype(jnp.bfloat16)
+    here = get_strip(came, layers * size).astype(jnp.float32)
+    there = get_strip(sibling_came, layers * size).astype(jnp.float32)
+    strips[:STRIP] = jnp.where(odd, here, there).astype(jnp.bfloat16)
+    strips[STRIP:] = jnp.where(odd, there, here).astype(jnp.bfloat16)
+    add_strip(half // size, half // size - 1, strips, out)
+
+
+def rest_kernel(mine_ref, cols_ref, phase, taken, came, sibling_came, strips, *outs):
+    sum_up(0, mine_ref, cols_ref, phase, taken, came, sibling_came, outs)
+    pairs = len(outs) + 1
+    for step in strip_steps(pairs)[:-1]:
+        add_strip(pairs, step, strips, outs[step])
 
 
 def shifted_rows(shift, odd, own, near, far):
@@ -301,15 +335,22 @@
     return pltpu.roll(stack(before, own, after), shift, 0)[16 : 16 + rows]
 
 
-def shift_kernel(wind_hbm, own, near0, near1, diagonal0, diagonal1, taken, partner_strips, came, out, wind, sem):
+def shift_kernel(wind_hbm, own, near0, near1, diagonal0, diagonal1, taken, partner_strips, *refs):
+    messages, (out, wind, sem) = refs[:-3], refs[-3:]
     load = fetch((wind_hbm, wind, sem))[0]
     layers, rows, cols = own.shape
     odd = lax.rem(lax.axis_index("dir"), 2) == 1
     half = taken.shape[1] - 64
-    second = lax.rem(lax.axis_index("layer"), 2) == 1
-    other = came[...].astype(jnp.float32)
-    left = jnp.where(second, partner_strips[:STRIP].astype(jnp.float32), other)
-    right = jnp.where(second, other, partner_strips[STRIP:].astype(jnp.float32))
+    pairs = 2 ** len(messages)
+    pair, second = lax.axis_index("layer") // 2, lax.rem(lax.axis_index("layer"), 2) == 1
+    before = jnp.bitwise_xor(pair, lax.rem(pair + pairs - 1, pairs))
+    after = jnp.bitwise_xor(pair, lax.rem(pair + 1, pairs))
+    left = partner_strips[:STRIP].astype(jnp.float32)
+    right = partner_strips[STRIP:].astype(jnp.float32)
+    for step, message in zip(strip_steps(pairs), messages):
+        strip = message[:, message.shape[1] - rows :].astype(jnp.float32)
+        left = jnp.where(jnp.logical_and(before == step, jnp.logical_not(second)), strip, left)
+        right = jnp.where(jnp.logical_and(after == step, second), strip, right)
     strips = stack(left, right, jnp.zeros((LANES - 2 * STRIP, rows), jnp.float32)).T
     lane = lax.broadcasted_iota(jnp.int32, (rows, LANES), 1)
     load.wait()
@@ -319,9 +360,11 @@
         extra = jnp.where(lane < WIND_MAX, first, last)
         pair = []
         for at, parts in ((half, (diagonal0, diagonal1)), (half + 32, (near0, near1))):
-            here = beside(*[stack(part[level, :16], part[level, rows - 16 :]) for part in parts])
-            here, there = here.astype(jnp.float32), taken[level, at : at + 32].astype(jnp.float32)
-            pair.append(beside(jnp.where(odd, there, here), jnp.where(odd, here, there)))
+            here = [stack(part[level, :16], part[level, rows - 16 :]).astype(jnp.float32) for part in parts]
+            there = taken[level, at : at + 32].astype(jnp.float32)
+            width = there.shape[1] // 2
+            quarters = [*here, there[:, width:], there[:, :width]]
+            pair.append(beside(*[jnp.where(odd, quarters[3 - k], quarters[k]) for k in range(4)]))
         far, near = pair
         moved = shifted_rows(wind[0, level], odd, own[level], near, far)
         shift = wind[1, level]
@@ -496,24 +539,28 @@
     sibling_came0 = partner(sibling_other0, 1)
 
     tables, mine0 = lax.optimization_barrier((tables, mine0))
-    cols = call(
-        columns_kernel, shape(layers, cols_dev, pupil_cols), tables, 0, "columns", brief=True
-    )
-    cols, sibling0 = lax.optimization_barrier((cols, sibling0))
-    message = shape(layers * half + STRIP * rows_dev // LANES, width)
-    mine1, give, other1, sibling_other1 = call(
+    cols, strip, sibling_strip = call(
+        columns_kernel,
+        [shape(layers, cols_dev, pupil_cols), shape(STRIP, rows_dev), shape(STRIP, rows_dev)],
+        (wind, *tables, across0, diagonal0, near0, keep0),
+        0,
+        "columns",
+        scratch=wind_scratch,
+        brief=True,
+    )
+    message = shape(layers * rows + STRIP * rows_dev // LANES, width)
+    remainder = shape(layers * (half - rows), width)
+    mine1, give, far1, sibling_far1, rest1, sibling_rest1 = call(
         later_rows_kernel,
-        [projected, shape(layers, half + 64, 2 * width), message, message],
-        (wind, row_weights, across1, diagonal1, near1, keep1, across0, diagonal0, near0, keep0, sibling0),
+        [projected, shape(layers, half + 64, 2 * width), message, message, remainder, remainder],
+        (row_weights, across1, diagonal1, near1, keep1, across0, diagonal0, near0, keep0, sibling0, strip, sibling_strip),
         0,
         "rows_later",
-        scratch=wind_scratch,
         brief=True,
     )
-    came1 = partner(other1)
-    sibling_came1 = partner(sibling_other1, 1)
+    far1, sibling_far1 = partner(far1), partner(sibling_far1, 1)
+    rest1, sibling_rest1 = partner(rest1), partner(sibling_rest1, 1)
     taken = swap(give, 1)
-
     phase, others = call(
         phase_kernel,
         (shape(half, pupil_cols, dtype=f32), shape(layers, cols_dev, pupil_cols)),
@@ -522,19 +569,25 @@
         "phase",
     )
 
-    *sums, strips, passed = call(
-        last_kernel,
-        [shape(rows, pupil_cols)] * pairs + [shape(2 * STRIP, rows_dev), shape(STRIP, rows_dev)],
-        (cols, others, phase, taken, came1, sibling_came1),
+    steps = strip_steps(pairs)
+    sums = [shape(rows, pupil_cols + (rows_dev if k in steps else 0)) for k in range(pairs)]
+    far_sum, strips = call(
+        far_kernel,
+        [sums[-1], shape(2 * STRIP, rows_dev)],
+        (cols, others, phase, taken, far1, sibling_far1),
         300_000_000,
-        "last",
-    )
-    order = sorted(range(1, pairs), key=lambda k: (-(k & (pairs // 2)), k))
-    received = [sums[0]] + [
-        lax.ppermute(sums[k], "layer", [(i, i ^ (2 * k)) for i in range(n_layer)]) for k in order
-    ]
-    steps = [(i, (i - 2 if i % 2 else i + 2) % n_layer) for i in range(n_layer)]
-    came = lax.ppermute(passed, "layer", steps)
+        "far",
+    )
+    rest_sums = call(
+        rest_kernel,
+        sums[:-1],
+        (cols, others, phase, taken, rest1, sibling_rest1, strips),
+        300_000_000,
+        "rest",
+    )
+    received = [*rest_sums, far_sum]
+    for k in range(1, pairs):
+        received[k] = lax.ppermute(received[k], "layer", [(i, i ^ (2 * k)) for i in range(n_layer)])
 
     optics_in, received[0] = lax.optimization_barrier((optics_in, received[0]))
     optics = call(
@@ -549,11 +602,10 @@
         30_000_000,
         "optics",
     )
-    came, received[1] = lax.optimization_barrier((came, received[1]))
     new_screens = call(
         shift_kernel,
         shape(layers, rows_dev, cols_dev),
-        (wind, own, near0, near1, diagonal0, diagonal1, taken, strips, came),
+        (wind, own, near0, near1, diagonal0, diagonal1, taken, strips, *[received[k] for k in steps]),
         1_000_000,
         "shift",
         scratch=wind_scratch,

time: 38.5 us -> 38.6 us (level)
    ppermute x4 -> x6, starting transfers between devices: 4.32 us -> 6.04 us  [partner(): lax.ppermute(value, ('layer', 'dir'), [(i, i ^ n_dir ^ bits) for i in ran...]
    ppermute x4 -> x3, starting transfers between devices: 5.95 us -> 4.23 us  [per_device(): lax.ppermute(received[k], 'layer', [(i, i ^ 2 * k) for i in range(n_layer)])]
    ppermute x4 -> x3, waiting for transfers between devices: 4.18 us -> 5.34 us  [per_device(): lax.ppermute(received[k], 'layer', [(i, i ^ 2 * k) for i in range(n_layer)])]
    ppermute x4 -> x6, waiting for transfers between devices: 2.98 us -> 1.92 us  [partner(): lax.ppermute(value, ('layer', 'dir'), [(i, i ^ n_dir ^ bits) for i in ran...]
    pallas_call x10 -> x11, Pallas kernels: 14 us -> 13.8 us  [call(): pl.pallas_call(kernel, out_shape=out_shape, in_specs=in_specs, out_specs=...]
  transfers between devices with their start and end apart: 15 -> 16, of which waited for: 4 -> 5; matrix products, arithmetic and copies ran while one was open for 0% -> 0% of each run, Pallas kernels for 28% -> 27%
where the time goes in v10:
time: 38.6 us; the launch traced here: 38.4 us
  starting transfers between devices  16 us (41%)
  Pallas kernels  13.8 us (36%)
  waiting for transfers between devices  7.85 us (20%)
  between operations  0.78 us (2%)
    pallas_call x11, Pallas kernels, call(): pl.pallas_call(kernel, out_shape=out_shape, in_specs=in_specs, out_specs=...  13.8 us
    ppermute x6, starting transfers between devices, partner(): lax.ppermute(value, ('layer', 'dir'), [(i, i ^ n_dir ^ bits) for i in ran...  6.04 us
    ppermute x7, starting transfers between devices, swap(): return lax.ppermute(value, 'dir', [(i, i ^ bits) for i in range(n_dir)])  5.69 us
    ppermute x3, waiting for transfers between devices, per_device(): lax.ppermute(received[k], 'layer', [(i, i ^ 2 * k) for i in range(n_layer)])  5.34 us
    ppermute x3, starting transfers between devices, per_device(): lax.ppermute(received[k], 'layer', [(i, i ^ 2 * k) for i in range(n_layer)])  4.23 us
    ppermute x6, waiting for transfers between devices, partner(): lax.ppermute(value, ('layer', 'dir'), [(i, i ^ n_dir ^ bits) for i in ran...  1.92 us
  transfers between devices with their start and end apart: 16, of which 5 were waited for; matrix products, arithmetic and copies ran while one was open for 0% of the time, Pallas kernels for 27%

profile of v10, /device:TPU:0, one launch (start us, length us, event | category | flops | bytes accessed | tf_op | source)
XLA Modules:
  0.0 38.4 jit_solution(6142319216937176755)
XLA Ops:
  0.6 1.1 %split.1 = (bf16[3,128,128]{2,1,0:T(8,128)(2,1)S(1)}, bf16[3,128,128]{2,1,0:T(8,128)(2,1)S(1)}, bf16[3,128,128]{2,1,0:T(8,128)(2,1)S(1)}, bf16[3,128,128]{2,1,0:T(8,128)(2,1)S(1)}) custom-call(bf16[3,128,512]{2,1,0:T(8,128)(2,1)} %refs_0_.1), custom_call_target="tpu_custom_call" | custom-call | tf_op jit(solution)/shard_map/split/pallas_call | solution.py:40
  1.7 2.4 %collective-permute-start.3 = (bf16[3,128,128]{2,1,0:T(8,128)(2,1)S(1)}, bf16[3,128,128]{2,1,0:T(8,128)(2,1)S(1)}, u32[]{:S(2)}, u32[]{:S(2)}) collective-permute-start(bf16[3,128,128]{2,1,0:T(8,128)(2,1)S(1)} %get-tuple-element.62), channel_id=1, source_target_pairs={{0,3},{1,2},{2,1},{3,0},{4,7},{5,6},{6,5},{7,4},{8,11},{9,10},{10,... | collective-permute-start | bytes 294920 | tf_op jit(solution)/shard_map/ppermute | solution.py:482
  4.2 0.6 %collective-permute-start.2 = (bf16[3,128,128]{2,1,0:T(8,128)(2,1)S(1)}, bf16[3,128,128]{2,1,0:T(8,128)(2,1)S(1)}, u32[]{:S(2)}, u32[]{:S(2)}) collective-permute-start(bf16[3,128,128]{2,1,0:T(8,128)(2,1)S(1)} %get-tuple-element.64.keep.refs_7_), channel_id=1, source_target_pairs={{0,2},{1,3},{2,0},{3,1},{4,6},{5,7},{6,4},{7,5},{8,10},{9,11},{10,... | collective-permute-start | bytes 294920 | tf_op jit(solution)/shard_map/ppermute | solution.py:482
  4.8 0.0 collective-permute-start
  4.9 1.5 %collective-permute-start.4 = (bf16[3,128,128]{2,1,0:T(8,128)(2,1)S(1)}, bf16[3,128,128]{2,1,0:T(8,128)(2,1)S(1)}, u32[]{:S(2)}, u32[]{:S(2)}) collective-permute-start(bf16[3,128,128]{2,1,0:T(8,128)(2,1)S(1)} %get-tuple-element.63), channel_id=1, source_target_pairs={{0,3},{1,2},{2,1},{3,0},{4,7},{5,6},{6,5},{7,4},{8,11},{9,10},{10,... | collective-permute-start | bytes 294920 | tf_op jit(solution)/shard_map/ppermute | solution.py:482
  6.3 0.6 %collective-permute-start.5 = (bf16[3,128,128]{2,1,0:T(8,128)(2,1)S(1)}, bf16[3,128,128]{2,1,0:T(8,128)(2,1)S(1)}, u32[]{:S(2)}, u32[]{:S(2)}) collective-permute-start(bf16[3,128,128]{2,1,0:T(8,128)(2,1)S(1)} %get-tuple-element.72.refs_3_), channel_id=1, source_target_pairs={{0,2},{1,3},{2,0},{3,1},{4,6},{5,7},{6,4},{7,5},{8,10},{9,11},{10,... | collective-permute-start | bytes 294920 | tf_op jit(solution)/shard_map/ppermute | solution.py:482
  7.0 2.2 %weights.1 = (bf16[2,3,256,512]{3,2,1,0:T(8,128)(2,1)S(1)}, s32[8,1280]{1,0:T(8,128)S(1)}, s32[8,1280]{1,0:T(8,128)S(1)}, f32[8,1280]{1,0:T(8,128)S(1)}, f32[8,1...) custom-call(s32[2,3]{1,0:T(2,128)} %bitcast.5, ...), custom_call_target="tpu_custom_call" | custom-call | tf_op jit(solution)/shard_map/weights/pallas_call | solution.py:40
  9.2 0.0 collective-permute-done.3.diagonal.refs_5_.diagonal0
  9.2 0.1 collective-permute-start.1
  9.3 0.6 %collective-permute-done.2.across.refs_4_ = bf16[3,128,128]{2,1,0:T(8,128)(2,1)S(1)} collective-permute-done((bf16[3,128,128]{2,1,0:T(8,128)(2,1)S(1)}, bf16[3,128,128]{2,1,0:T(8,128)(2,1)S(1)}, u32[]{:S(2)}, u32[]{:S(2)}) %collective-permute-start.2) | collective-permute-done | bytes 98336 | tf_op jit(solution)/shard_map/ppermute | solution.py:482
  9.8 0.6 %rows_first.1 = (bf16[3,128,128]{2,1,0:T(8,128)(2,1)S(1)}, bf16[3,128,128]{2,1,0:T(8,128)(2,1)S(1)}, bf16[3,128,128]{2,1,0:T(8,128)(2,1)S(1)}, bf16[3,128,128]{2,1,0:T(8,128)(2,1)S(1)}) custom-call(bf16[2,3,256,512]{3,2,1,0:T(8,128)(2,1)S(1)} %get-tuple-element.71.rows_ref, bf16[3,128,128]{2,1,0:T(8,128)(2,1)S(1)} %collective-permute-done.2.across.refs_4_, ...), custom_call_target="tpu_custom_call" | custom-call | tf_op jit(solution)/shard_map/rows_first/pallas_call | solution.py:40
  10.4 2.2 %collective-permute-start.7 = (bf16[3,128,128]{2,1,0:T(8,128)(2,1)S(1)}, bf16[3,128,128]{2,1,0:T(8,128)(2,1)S(1)}, u32[]{:S(2)}, u32[]{:S(2)}) collective-permute-start(bf16[3,128,128]{2,1,0:T(8,128)(2,1)S(1)} %get-tuple-element.90), channel_id=1, source_target_pairs={{0,4},{1,5},{2,6},{3,7},{4,0},{5,1},{6,2},{7,3},{8,12},{9,13},{10,... | collective-permute-start | bytes 294920 | tf_op jit(solution)/shard_map/ppermute | solution.py:486
  12.7 1.5 %columns.1 = (bf16[3,512,1280]{2,1,0:T(8,128)(2,1)S(1)}, bf16[32,128]{1,0:T(8,128)(2,1)S(1)}, bf16[32,128]{1,0:T(8,128)(2,1)S(1)}) custom-call(s32[2,3]{1,0:T(2,128)} %bitcast.6, s32[8,1280]{1,0:T(8,128)S(1)} %get-tuple-element.80.refs_0_, s32[8,1280]{1,0:T(8,128)S(1)} %get-tuple-element.81.refs_1_, f32[8,1280]{1,0:T(8,128)S(1)} %get-tuple-element.82.refs_2_, ...), custom_call_target="tpu_custom_call" | custom-call | tf_op jit(solution)/shard_map/columns/pallas_call | solution.py:40
  14.2 0.0 collective-permute-done.1.refs_2_.near1
  14.2 0.6 %rows_later.1 = (bf16[3,128,128]{2,1,0:T(8,128)(2,1)S(1)}, bf16[3,192,256]{2,1,0:T(8,128)(2,1)S(1)}, bf16[128,128]{1,0:T(8,128)(2,1)S(1)}, bf16[128,128]{1,0:T(8...) custom-call(bf16[2,3,256,512]{3,2,1,0:T(8,128)(2,1)S(1)} %get-tuple-element.71.rows_ref, ...), custom_call_target="tpu_custom_call" | custom-call | tf_op jit(solution)/shard_map/rows_later/pallas_call | solution.py:40
  14.8 2.0 %collective-permute-start.9 = (bf16[128,128]{1,0:T(8,128)(2,1)S(1)}, bf16[128,128]{1,0:T(8,128)(2,1)S(1)}, u32[]{:S(2)}, u32[]{:S(2)}) collective-permute-start(bf16[128,128]{1,0:T(8,128)(2,1)S(1)} %get-tuple-element.94), channel_id=1, source_target_pairs={{0,4},{1,5},{2,6},{3,7},{4,0},{5,1},{6,2},{7,3},{8,12},{9,13},{10,... | collective-permute-start | bytes 98312 | tf_op jit(solution)/shard_map/ppermute | solution.py:486
  16.8 1.5 %collective-permute-start.11 = (bf16[288,128]{1,0:T(8,128)(2,1)S(1)}, bf16[288,128]{1,0:T(8,128)(2,1)S(1)}, u32[]{:S(2)}, u32[]{:S(2)}) collective-permute-start(bf16[288,128]{1,0:T(8,128)(2,1)S(1)} %get-tuple-element.97), channel_id=1, source_target_pairs={{0,4},{1,5},{2,6},{3,7},{4,0},{5,1},{6,2},{7,3},{8,12},{9,13},{10,... | collective-permute-start | bytes 221192 | tf_op jit(solution)/shard_map/ppermute | solution.py:486
  18.4 0.3 collective-permute-start.12
  18.6 0.4 %collective-permute-start.6 = (bf16[3,192,256]{2,1,0:T(8,128)(2,1)S(1)}, bf16[3,192,256]{2,1,0:T(8,128)(2,1)S(1)}, u32[]{:S(2)}, u32[]{:S(2)}) collective-permute-start(bf16[3,192,256]{2,1,0:T(8,128)(2,1)S(1)} %get-tuple-element.86), channel_id=1, source_target_pairs={{0,1},{1,0},{2,3},{3,2},{4,5},{5,4},{6,7},{7,6},{8,9},{9,8},{10,11... | collective-permute-start | bytes 884744 | tf_op jit(solution)/shard_map/ppermute | solution.py:482
  19.0 1.9 %phase.1 = (f32[128,1280]{1,0:T(8,128)S(1)}, bf16[3,512,1280]{2,1,0:T(8,128)(2,1)S(1)}) custom-call(s32[8,1280]{1,0:T(8,128)S(1)} %get-tuple-element.80.refs_0_, s32[8,1280]{1,0:T(8,128)S(1)} %get-tuple-element.81.refs_1_, f32[8,1280]{1,0:T(8,128)S(1)} %get-tuple-element.82.refs_2_, f32[8,1280]{1,0:T(8,128)S(1)} %get-tuple-element.83.refs_3_, ...), custom_call_target="tpu_custom_call" | custom-call | flops 10000000000 | bytes 9076736 | tf_op jit(solution)/shard_map/phase/pallas_call | solution.py:40
  20.9 0.8 %far.1 = (bf16[32,1408]{1,0:T(8,128)(2,1)S(1)}, bf16[64,128]{1,0:T(8,128)(2,1)S(1)}) custom-call(bf16[3,512,1280]{2,1,0:T(8,128)(2,1)S(1)} %get-tuple-element.87.refs_4_.mine_ref, bf16[3,512,1280]{2,1,0:T(8,128)(2,1)S(1)} %get-tuple-element.92.cols_ref, f32[128,1280]{1,0:T(8,128)S(1)} %get-tuple-element.93.phase, ...), custom_call_target="tpu_custom_call" | custom-call | flops 300000000 | bytes 8986624 | tf_op jit(solution)/shard_map/far/pallas_call | solution.py:40
  21.7 0.5 %collective-permute-done.11.came = bf16[288,128]{1,0:T(8,128)(2,1)S(1)} collective-permute-done((bf16[288,128]{1,0:T(8,128)(2,1)S(1)}, bf16[288,128]{1,0:T(8,128)(2,1)S(1)}, u32[]{:S(2)}, u32[]{:S(2)}) %collective-permute-start.11) | collective-permute-done | bytes 73760 | tf_op jit(solution)/shard_map/ppermute | solution.py:486
  22.2 1.4 %collective-permute-done.12.sibling_came = bf16[288,128]{1,0:T(8,128)(2,1)S(1)} collective-permute-done((bf16[288,128]{1,0:T(8,128)(2,1)S(1)}, bf16[288,128]{1,0:T(8,128)(2,1)S(1)}, u32[]{:S(2)}, u32[]{:S(2)}) %collective-permute-start.12) | collective-permute-done | bytes 73760 | tf_op jit(solution)/shard_map/ppermute | solution.py:486
  23.6 0.8 %rest.1 = (bf16[32,1280]{1,0:T(8,128)(2,1)S(1)}, bf16[32,1408]{1,0:T(8,128)(2,1)S(1)}, bf16[32,1280]{1,0:T(8,128)(2,1)S(1)}) custom-call(bf16[3,512,1280]{2,1,0:T(8,128)(2,1)S(1)} %get-tuple-element.87.refs_4_.mine_ref, bf16[3,512,1280]{2,1,0:T(8,128)(2,1)S(1)} %get-tuple-element.92.cols_ref, f32[128,1280]{1,0:T(8,128)S(1)} %get-tuple-element.93.phase, ...), custom_call_target="tpu_custom_call" | custom-call | flops 300000000 | bytes 9232384 | tf_op jit(solution)/shard_map/rest/pallas_call | solution.py:40
  24.4 1.6 %collective-permute-start.13 = (bf16[32,1408]{1,0:T(8,128)(2,1)S(1)}, bf16[32,1408]{1,0:T(8,128)(2,1)S(1)}, u32[]{:S(2)}, u32[]{:S(2)}) collective-permute-start(bf16[32,1408]{1,0:T(8,128)(2,1)S(1)} %get-tuple-element.99), channel_id=1, source_target_pairs={{0,8},{4,12},{8,0},{12,4},{16,24},{20,28},{24,16},{28,20},{1,9},{5... | collective-permute-start | bytes 270344 | tf_op jit(solution)/shard_map/ppermute | solution.py:590
  26.0 2.5 %collective-permute-start.14 = (bf16[32,1408]{1,0:T(8,128)(2,1)S(1)}, bf16[32,1408]{1,0:T(8,128)(2,1)S(1)}, u32[]{:S(2)}, u32[]{:S(2)}) collective-permute-start(bf16[32,1408]{1,0:T(8,128)(2,1)S(1)} %get-tuple-element.100), channel_id=1, source_target_pairs={{0,24},{4,28},{8,16},{12,20},{16,8},{20,12},{24,0},{28,4},{1,25},{... | collective-permute-start | bytes 270344 | tf_op jit(solution)/shard_map/ppermute | solution.py:590
  28.5 0.1 collective-permute-start.15
  28.6 0.7 %optics.1 = (f32[32,1280]{1,0:T(8,128)S(1)}, bf16[256,512]{1,0:T(8,128)(2,1)S(1)}, bf16[256,512]{1,0:T(8,128)(2,1)S(1)}, bf16[128,192]{1,0:T(8,128)(2,1)S(1)}) custom-call(f32[32,1280]{1,0:T(8,128)S(1)} %get-tuple-element.108.amplitude, f32[128,128]{1,0:T(8,128)S(1)} %get-tuple-element.109.ones, f32[256,512]{1,0:T(8,128)S(1)} %get-tuple-element.110.columns, ...), custom_call_target="tpu_custom_call" | custom-call | flops 30000000 | bytes 1523712 | tf_op jit(solution)/shard_map/optics/pallas_call | solution.py:40
  29.3 4.7 %collective-permute-done.14.refs_1_.refs_3_ = bf16[32,1408]{1,0:T(8,128)(2,1)S(1)} collective-permute-done((bf16[32,1408]{1,0:T(8,128)(2,1)S(1)}, bf16[32,1408]{1,0:T(8,128)(2,1)S(1)}, u32[]{:S(2)}, u32[]{:S(2)}) %collective-permute-start.14) | collective-permute-done | bytes 90144 | tf_op jit(solution)/shard_map/ppermute | solution.py:590
  34.0 2.0 %shift.1 = bf16[3,128,512]{2,1,0:T(8,128)(2,1)} custom-call(s32[2,3]{1,0:T(2,128)} %bitcast.7, bf16[3,128,512]{2,1,0:T(8,128)(2,1)S(1)} %get-tuple-element.61.own, bf16[3,128,128]{2,1,0:T(8,128)(2,1)S(1)} %collective-permute-done.near.refs_6_.near0, bf16[3,128,128]{2,1,0:T(8,128)(2,1)S(1)} %collective-permute-done.1.refs_2_.near1, ...), custom_call_target="tpu_custom_call" | custom-call | flops 1000000 | bytes 1671192 | tf_op jit(solution)/shard_map/shift/pallas_call | solution.py:40
  36.0 0.7 %collective-permute-done.15.refs_2_ = bf16[32,1280]{1,0:T(8,128)(2,1)S(1)} collective-permute-done((bf16[32,1280]{1,0:T(8,128)(2,1)S(1)}, bf16[32,1280]{1,0:T(8,128)(2,1)S(1)}, u32[]{:S(2)}, u32[]{:S(2)}) %collective-permute-start.15) | collective-permute-done | bytes 81952 | tf_op jit(solution)/shard_map/ppermute | solution.py:590
  36.7 1.7 %imaging.1 = f32[64,2560]{1,0:T(8,128)} custom-call(bf16[32,1280]{1,0:T(8,128)(2,1)S(1)} %get-tuple-element.106.refs_0_, bf16[32,1408]{1,0:T(8,128)(2,1)S(1)} %collective-permute-done.13.refs_0_.refs_1_, bf16[32,1280]{1,0:T(8,128)(2,1)S(1)} %collective-permute-done.15.refs_2_, bf16[32,1408]{1,0:T(8,128)(2,1)S(1)} %collective-permute-done.14.refs_1_.refs_3_, ...), custom_call_target="tpu_custom_call" | custom-call | flops 400000000 | bytes 1736704 | tf_op jit(solution)/shard_map/imaging/pallas_call | solution.py:40
  (11 shorter events, 0.0 us)
Async XLA Ops:
  1.7 7.5 %collective-permute-start.3 = (bf16[3,128,128]{2,1,0:T(8,128)(2,1)S(1)}, bf16[3,128,128]{2,1,0:T(8,128)(2,1)S(1)}, u32[]{:S(2)}, u32[]{:S(2)}) collective-permute-start(bf16[3,128,128]{2,1,0:T(8,128)(2,1)S(1)} %get-tuple-element.62), channel_id=1, source_target_pairs={{0,3},{1,2},{2,1},{3,0},{4,7},{5,6},{6,5},{7,4},{8,11},{9,10},{10,... | collective-permute-start | bytes 294920 | tf_op jit(solution)/shard_map/ppermute | solution.py:482
  4.2 5.7 %collective-permute-start.2 = (bf16[3,128,128]{2,1,0:T(8,128)(2,1)S(1)}, bf16[3,128,128]{2,1,0:T(8,128)(2,1)S(1)}, u32[]{:S(2)}, u32[]{:S(2)}) collective-permute-start(bf16[3,128,128]{2,1,0:T(8,128)(2,1)S(1)} %get-tuple-element.64.keep.refs_7_), channel_id=1, source_target_pairs={{0,2},{1,3},{2,0},{3,1},{4,6},{5,7},{6,4},{7,5},{8,10},{9,11},{10,... | collective-permute-start | bytes 294920 | tf_op jit(solution)/shard_map/ppermute | solution.py:482
  4.8 5.0 %collective-permute-start = (bf16[3,128,128]{2,1,0:T(8,128)(2,1)S(1)}, bf16[3,128,128]{2,1,0:T(8,128)(2,1)S(1)}, u32[]{:S(2)}, u32[]{:S(2)}) collective-permute-start(bf16[3,128,128]{2,1,0:T(8,128)(2,1)S(1)} %get-tuple-element.62), channel_id=1, source_target_pairs={{0,1},{1,0},{2,3},{3,2},{4,5},{5,4},{6,7},{7,6},{8,9},{9,8},{10,11... | collective-permute-start | bytes 294920 | tf_op jit(solution)/shard_map/ppermute | solution.py:482
  4.9 9.3 %collective-permute-start.4 = (bf16[3,128,128]{2,1,0:T(8,128)(2,1)S(1)}, bf16[3,128,128]{2,1,0:T(8,128)(2,1)S(1)}, u32[]{:S(2)}, u32[]{:S(2)}) collective-permute-start(bf16[3,128,128]{2,1,0:T(8,128)(2,1)S(1)} %get-tuple-element.63), channel_id=1, source_target_pairs={{0,3},{1,2},{2,1},{3,0},{4,7},{5,6},{6,5},{7,4},{8,11},{9,10},{10,... | collective-permute-start | bytes 294920 | tf_op jit(solution)/shard_map/ppermute | solution.py:482
  6.3 7.9 %collective-permute-start.5 = (bf16[3,128,128]{2,1,0:T(8,128)(2,1)S(1)}, bf16[3,128,128]{2,1,0:T(8,128)(2,1)S(1)}, u32[]{:S(2)}, u32[]{:S(2)}) collective-permute-start(bf16[3,128,128]{2,1,0:T(8,128)(2,1)S(1)} %get-tuple-element.72.refs_3_), channel_id=1, source_target_pairs={{0,2},{1,3},{2,0},{3,1},{4,6},{5,7},{6,4},{7,5},{8,10},{9,11},{10,... | collective-permute-start | bytes 294920 | tf_op jit(solution)/shard_map/ppermute | solution.py:482
  9.2 5.0 %collective-permute-start.1 = (bf16[3,128,128]{2,1,0:T(8,128)(2,1)S(1)}, bf16[3,128,128]{2,1,0:T(8,128)(2,1)S(1)}, u32[]{:S(2)}, u32[]{:S(2)}) collective-permute-start(bf16[3,128,128]{2,1,0:T(8,128)(2,1)S(1)} %get-tuple-element.63), channel_id=1, source_target_pairs={{0,1},{1,0},{2,3},{3,2},{4,5},{5,4},{6,7},{7,6},{8,9},{9,8},{10,11... | collective-permute-start | bytes 294920 | tf_op jit(solution)/shard_map/ppermute | solution.py:482
  10.4 7.9 %collective-permute-start.7 = (bf16[3,128,128]{2,1,0:T(8,128)(2,1)S(1)}, bf16[3,128,128]{2,1,0:T(8,128)(2,1)S(1)}, u32[]{:S(2)}, u32[]{:S(2)}) collective-permute-start(bf16[3,128,128]{2,1,0:T(8,128)(2,1)S(1)} %get-tuple-element.90), channel_id=1, source_target_pairs={{0,4},{1,5},{2,6},{3,7},{4,0},{5,1},{6,2},{7,3},{8,12},{9,13},{10,... | collective-permute-start | bytes 294920 | tf_op jit(solution)/shard_map/ppermute | solution.py:486
  12.7 6.0 %collective-permute-start.8 = (bf16[3,128,128]{2,1,0:T(8,128)(2,1)S(1)}, bf16[3,128,128]{2,1,0:T(8,128)(2,1)S(1)}, u32[]{:S(2)}, u32[]{:S(2)}) collective-permute-start(bf16[3,128,128]{2,1,0:T(8,128)(2,1)S(1)} %get-tuple-element.91), channel_id=1, source_target_pairs={{0,5},{1,4},{2,7},{3,6},{4,1},{5,0},{6,3},{7,2},{8,13},{9,12},{10,... | collective-permute-start | bytes 294920 | tf_op jit(solution)/shard_map/ppermute | solution.py:486
  14.8 6.1 %collective-permute-start.9 = (bf16[128,128]{1,0:T(8,128)(2,1)S(1)}, bf16[128,128]{1,0:T(8,128)(2,1)S(1)}, u32[]{:S(2)}, u32[]{:S(2)}) collective-permute-start(bf16[128,128]{1,0:T(8,128)(2,1)S(1)} %get-tuple-element.94), channel_id=1, source_target_pairs={{0,4},{1,5},{2,6},{3,7},{4,0},{5,1},{6,2},{7,3},{8,12},{9,13},{10,... | collective-permute-start | bytes 98312 | tf_op jit(solution)/shard_map/ppermute | solution.py:486
  16.8 4.1 %collective-permute-start.10 = (bf16[128,128]{1,0:T(8,128)(2,1)S(1)}, bf16[128,128]{1,0:T(8,128)(2,1)S(1)}, u32[]{:S(2)}, u32[]{:S(2)}) collective-permute-start(bf16[128,128]{1,0:T(8,128)(2,1)S(1)} %get-tuple-element.95), channel_id=1, source_target_pairs={{0,5},{1,4},{2,7},{3,6},{4,1},{5,0},{6,3},{7,2},{8,13},{9,12},{10,... | collective-permute-start | bytes 98312 | tf_op jit(solution)/shard_map/ppermute | solution.py:486
  16.8 5.3 %collective-permute-start.11 = (bf16[288,128]{1,0:T(8,128)(2,1)S(1)}, bf16[288,128]{1,0:T(8,128)(2,1)S(1)}, u32[]{:S(2)}, u32[]{:S(2)}) collective-permute-start(bf16[288,128]{1,0:T(8,128)(2,1)S(1)} %get-tuple-element.97), channel_id=1, source_target_pairs={{0,4},{1,5},{2,6},{3,7},{4,0},{5,1},{6,2},{7,3},{8,12},{9,13},{10,... | collective-permute-start | bytes 221192 | tf_op jit(solution)/shard_map/ppermute | solution.py:486
  18.4 5.3 %collective-permute-start.12 = (bf16[288,128]{1,0:T(8,128)(2,1)S(1)}, bf16[288,128]{1,0:T(8,128)(2,1)S(1)}, u32[]{:S(2)}, u32[]{:S(2)}) collective-permute-start(bf16[288,128]{1,0:T(8,128)(2,1)S(1)} %get-tuple-element.98), channel_id=1, source_target_pairs={{0,5},{1,4},{2,7},{3,6},{4,1},{5,0},{6,3},{7,2},{8,13},{9,12},{10,... | collective-permute-start | bytes 221192 | tf_op jit(solution)/shard_map/ppermute | solution.py:486
  18.6 2.3 %collective-permute-start.6 = (bf16[3,192,256]{2,1,0:T(8,128)(2,1)S(1)}, bf16[3,192,256]{2,1,0:T(8,128)(2,1)S(1)}, u32[]{:S(2)}, u32[]{:S(2)}) collective-permute-start(bf16[3,192,256]{2,1,0:T(8,128)(2,1)S(1)} %get-tuple-element.86), channel_id=1, source_target_pairs={{0,1},{1,0},{2,3},{3,2},{4,5},{5,4},{6,7},{7,6},{8,9},{9,8},{10,11... | collective-permute-start | bytes 884744 | tf_op jit(solution)/shard_map/ppermute | solution.py:482
  24.4 4.9 %collective-permute-start.13 = (bf16[32,1408]{1,0:T(8,128)(2,1)S(1)}, bf16[32,1408]{1,0:T(8,128)(2,1)S(1)}, u32[]{:S(2)}, u32[]{:S(2)}) collective-permute-start(bf16[32,1408]{1,0:T(8,128)(2,1)S(1)} %get-tuple-element.99), channel_id=1, source_target_pairs={{0,8},{4,12},{8,0},{12,4},{16,24},{20,28},{24,16},{28,20},{1,9},{5... | collective-permute-start | bytes 270344 | tf_op jit(solution)/shard_map/ppermute | solution.py:590
  26.0 8.0 %collective-permute-start.14 = (bf16[32,1408]{1,0:T(8,128)(2,1)S(1)}, bf16[32,1408]{1,0:T(8,128)(2,1)S(1)}, u32[]{:S(2)}, u32[]{:S(2)}) collective-permute-start(bf16[32,1408]{1,0:T(8,128)(2,1)S(1)} %get-tuple-element.100), channel_id=1, source_target_pairs={{0,24},{4,28},{8,16},{12,20},{16,8},{20,12},{24,0},{28,4},{1,25},{... | collective-permute-start | bytes 270344 | tf_op jit(solution)/shard_map/ppermute | solution.py:590
  28.5 8.2 %collective-permute-start.15 = (bf16[32,1280]{1,0:T(8,128)(2,1)S(1)}, bf16[32,1280]{1,0:T(8,128)(2,1)S(1)}, u32[]{:S(2)}, u32[]{:S(2)}) collective-permute-start(bf16[32,1280]{1,0:T(8,128)(2,1)S(1)} %get-tuple-element.107), channel_id=1, source_target_pairs={{0,16},{4,20},{8,24},{12,28},{16,0},{20,4},{24,8},{28,12},{1,17},{... | collective-permute-start | bytes 245768 | tf_op jit(solution)/shard_map/ppermute | solution.py:590

commit v11 on v10

--- a/solution.py
+++ b/solution.py
@@ -582,14 +582,15 @@
         rest_kernel,
         sums[:-1],
         (cols, others, phase, taken, rest1, sibling_rest1, strips),
-        300_000_000,
+        0,
         "rest",
+        brief=True,
     )
     received = [*rest_sums, far_sum]
     for k in range(1, pairs):
         received[k] = lax.ppermute(received[k], "layer", [(i, i ^ (2 * k)) for i in range(n_layer)])
 
-    optics_in, received[0] = lax.optimization_barrier((optics_in, received[0]))
+    optics_in, received[-1] = lax.optimization_barrier((optics_in, received[-1]))
     optics = call(
         optics_kernel,
         (
@@ -599,16 +600,19 @@
             shape(optics_in[3].shape[0], 3 * optics_in[3].shape[1]),
         ),
         optics_in,
-        30_000_000,
+        0,
         "optics",
-    )
+        brief=True,
+    )
+    received[1], optics = lax.optimization_barrier((received[1], optics))
     new_screens = call(
         shift_kernel,
         shape(layers, rows_dev, cols_dev),
         (wind, own, near0, near1, diagonal0, diagonal1, taken, strips, *[received[k] for k in steps]),
-        1_000_000,
+        0,
         "shift",
         scratch=wind_scratch,
+        brief=True,
     )
     spots = call(
         functools.partial(imaging_kernel, pairs),

time: 38.6 us -> 35.9 us (0.930)
  waiting for transfers between devices: 7.85 us -> 3.3 us
  starting transfers between devices: 16 us -> 17.9 us
    ppermute x3, waiting for transfers between devices: 5.34 us -> 2.7 us  [per_device(): lax.ppermute(received[k], 'layer', [(i, i ^ 2 * k) for i in range(n_layer)])]
    ppermute x6, waiting for transfers between devices: 1.92 us -> 0.02 us  [partner(): lax.ppermute(value, ('layer', 'dir'), [(i, i ^ n_dir ^ bits) for i in ran...]
    ppermute x3, starting transfers between devices: 4.23 us -> 6.13 us  [per_device(): lax.ppermute(received[k], 'layer', [(i, i ^ 2 * k) for i in range(n_layer)])]
  transfers between devices with their start and end apart: 16 -> 16, of which waited for: 5 -> 2; matrix products, arithmetic and copies ran while one was open for 0% -> 0% of each run, Pallas kernels for 27% -> 31%
where the time goes in v11:
time: 35.9 us; the launch traced here: 35.7 us
  starting transfers between devices  17.9 us (50%)
  Pallas kernels  13.8 us (38%)
  waiting for transfers between devices  3.3 us (9%)
  between operations  0.78 us (2%)
    pallas_call x11, Pallas kernels, call(): pl.pallas_call(kernel, out_shape=out_shape, in_specs=in_specs, out_specs=...  13.8 us
    ppermute x3, starting transfers between devices, per_device(): lax.ppermute(received[k], 'layer', [(i, i ^ 2 * k) for i in range(n_layer)])  6.13 us
    ppermute x6, starting transfers between devices, partner(): lax.ppermute(value, ('layer', 'dir'), [(i, i ^ n_dir ^ bits) for i in ran...  6.04 us
    ppermute x7, starting transfers between devices, swap(): return lax.ppermute(value, 'dir', [(i, i ^ bits) for i in range(n_dir)])  5.69 us
    ppermute x3, waiting for transfers between devices, per_device(): lax.ppermute(received[k], 'layer', [(i, i ^ 2 * k) for i in range(n_layer)])  2.7 us
  transfers between devices with their start and end apart: 16, of which 2 were waited for; matrix products, arithmetic and copies ran while one was open for 0% of the time, Pallas kernels for 31%

profile of v11, /device:TPU:0, one launch (start us, length us, event | category | flops | bytes accessed | tf_op | source)
XLA Modules:
  0.0 35.7 jit_solution(5672146529822365879)
XLA Ops:
  0.6 1.1 %split.1 = (bf16[3,128,128]{2,1,0:T(8,128)(2,1)S(1)}, bf16[3,128,128]{2,1,0:T(8,128)(2,1)S(1)}, bf16[3,128,128]{2,1,0:T(8,128)(2,1)S(1)}, bf16[3,128,128]{2,1,0:T(8,128)(2,1)S(1)}) custom-call(bf16[3,128,512]{2,1,0:T(8,128)(2,1)} %refs_0_.1), custom_call_target="tpu_custom_call" | custom-call | tf_op jit(solution)/shard_map/split/pallas_call | solution.py:40
  1.7 2.4 %collective-permute-start.3 = (bf16[3,128,128]{2,1,0:T(8,128)(2,1)S(1)}, bf16[3,128,128]{2,1,0:T(8,128)(2,1)S(1)}, u32[]{:S(2)}, u32[]{:S(2)}) collective-permute-start(bf16[3,128,128]{2,1,0:T(8,128)(2,1)S(1)} %get-tuple-element.67), channel_id=1, source_target_pairs={{0,3},{1,2},{2,1},{3,0},{4,7},{5,6},{6,5},{7,4},{8,11},{9,10},{10,... | collective-permute-start | bytes 294920 | tf_op jit(solution)/shard_map/ppermute | solution.py:482
  4.2 0.6 %collective-permute-start.2 = (bf16[3,128,128]{2,1,0:T(8,128)(2,1)S(1)}, bf16[3,128,128]{2,1,0:T(8,128)(2,1)S(1)}, u32[]{:S(2)}, u32[]{:S(2)}) collective-permute-start(bf16[3,128,128]{2,1,0:T(8,128)(2,1)S(1)} %get-tuple-element.69.keep.refs_7_), channel_id=1, source_target_pairs={{0,2},{1,3},{2,0},{3,1},{4,6},{5,7},{6,4},{7,5},{8,10},{9,11},{10,... | collective-permute-start | bytes 294920 | tf_op jit(solution)/shard_map/ppermute | solution.py:482
  4.8 0.0 collective-permute-start
  4.9 1.5 %collective-permute-start.4 = (bf16[3,128,128]{2,1,0:T(8,128)(2,1)S(1)}, bf16[3,128,128]{2,1,0:T(8,128)(2,1)S(1)}, u32[]{:S(2)}, u32[]{:S(2)}) collective-permute-start(bf16[3,128,128]{2,1,0:T(8,128)(2,1)S(1)} %get-tuple-element.68), channel_id=1, source_target_pairs={{0,3},{1,2},{2,1},{3,0},{4,7},{5,6},{6,5},{7,4},{8,11},{9,10},{10,... | collective-permute-start | bytes 294920 | tf_op jit(solution)/shard_map/ppermute | solution.py:482
  6.3 0.6 %collective-permute-start.5 = (bf16[3,128,128]{2,1,0:T(8,128)(2,1)S(1)}, bf16[3,128,128]{2,1,0:T(8,128)(2,1)S(1)}, u32[]{:S(2)}, u32[]{:S(2)}) collective-permute-start(bf16[3,128,128]{2,1,0:T(8,128)(2,1)S(1)} %get-tuple-element.77.refs_3_), channel_id=1, source_target_pairs={{0,2},{1,3},{2,0},{3,1},{4,6},{5,7},{6,4},{7,5},{8,10},{9,11},{10,... | collective-permute-start | bytes 294920 | tf_op jit(solution)/shard_map/ppermute | solution.py:482
  7.0 2.2 %weights.1 = (bf16[2,3,256,512]{3,2,1,0:T(8,128)(2,1)S(1)}, s32[8,1280]{1,0:T(8,128)S(1)}, s32[8,1280]{1,0:T(8,128)S(1)}, f32[8,1280]{1,0:T(8,128)S(1)}, f32[8,1...) custom-call(s32[2,3]{1,0:T(2,128)} %bitcast.5, ...), custom_call_target="tpu_custom_call" | custom-call | tf_op jit(solution)/shard_map/weights/pallas_call | solution.py:40
  9.2 0.1 collective-permute-start.1
  9.3 0.6 %collective-permute-done.2.across.refs_4_ = bf16[3,128,128]{2,1,0:T(8,128)(2,1)S(1)} collective-permute-done((bf16[3,128,128]{2,1,0:T(8,128)(2,1)S(1)}, bf16[3,128,128]{2,1,0:T(8,128)(2,1)S(1)}, u32[]{:S(2)}, u32[]{:S(2)}) %collective-permute-start.2) | collective-permute-done | bytes 98336 | tf_op jit(solution)/shard_map/ppermute | solution.py:482
  9.8 0.0 collective-permute-done.near.refs_6_.near0
  9.8 0.6 %rows_first.1 = (bf16[3,128,128]{2,1,0:T(8,128)(2,1)S(1)}, bf16[3,128,128]{2,1,0:T(8,128)(2,1)S(1)}, bf16[3,128,128]{2,1,0:T(8,128)(2,1)S(1)}, bf16[3,128,128]{2,1,0:T(8,128)(2,1)S(1)}) custom-call(bf16[2,3,256,512]{3,2,1,0:T(8,128)(2,1)S(1)} %get-tuple-element.76.rows_ref, bf16[3,128,128]{2,1,0:T(8,128)(2,1)S(1)} %collective-permute-done.2.across.refs_4_, ...), custom_call_target="tpu_custom_call" | custom-call | tf_op jit(solution)/shard_map/rows_first/pallas_call | solution.py:40
  10.4 2.2 %collective-permute-start.7 = (bf16[3,128,128]{2,1,0:T(8,128)(2,1)S(1)}, bf16[3,128,128]{2,1,0:T(8,128)(2,1)S(1)}, u32[]{:S(2)}, u32[]{:S(2)}) collective-permute-start(bf16[3,128,128]{2,1,0:T(8,128)(2,1)S(1)} %get-tuple-element.95), channel_id=1, source_target_pairs={{0,4},{1,5},{2,6},{3,7},{4,0},{5,1},{6,2},{7,3},{8,12},{9,13},{10,... | collective-permute-start | bytes 294920 | tf_op jit(solution)/shard_map/ppermute | solution.py:486
  12.7 0.0 collective-permute-start.8
  12.7 1.5 %columns.1 = (bf16[3,512,1280]{2,1,0:T(8,128)(2,1)S(1)}, bf16[32,128]{1,0:T(8,128)(2,1)S(1)}, bf16[32,128]{1,0:T(8,128)(2,1)S(1)}) custom-call(s32[2,3]{1,0:T(2,128)} %bitcast.6, s32[8,1280]{1,0:T(8,128)S(1)} %get-tuple-element.85.refs_0_, s32[8,1280]{1,0:T(8,128)S(1)} %get-tuple-element.86.refs_1_, f32[8,1280]{1,0:T(8,128)S(1)} %get-tuple-element.87.refs_2_, ...), custom_call_target="tpu_custom_call" | custom-call | tf_op jit(solution)/shard_map/columns/pallas_call | solution.py:40
  14.2 0.0 collective-permute-done.4.refs_1_.diagonal1
  14.2 0.0 collective-permute-done.5.refs_0_
  14.2 0.6 %rows_later.1 = (bf16[3,128,128]{2,1,0:T(8,128)(2,1)S(1)}, bf16[3,192,256]{2,1,0:T(8,128)(2,1)S(1)}, bf16[128,128]{1,0:T(8,128)(2,1)S(1)}, bf16[128,128]{1,0:T(8...) custom-call(bf16[2,3,256,512]{3,2,1,0:T(8,128)(2,1)S(1)} %get-tuple-element.76.rows_ref, ...), custom_call_target="tpu_custom_call" | custom-call | tf_op jit(solution)/shard_map/rows_later/pallas_call | solution.py:40
  14.8 2.0 %collective-permute-start.9 = (bf16[128,128]{1,0:T(8,128)(2,1)S(1)}, bf16[128,128]{1,0:T(8,128)(2,1)S(1)}, u32[]{:S(2)}, u32[]{:S(2)}) collective-permute-start(bf16[128,128]{1,0:T(8,128)(2,1)S(1)} %get-tuple-element.99), channel_id=1, source_target_pairs={{0,4},{1,5},{2,6},{3,7},{4,0},{5,1},{6,2},{7,3},{8,12},{9,13},{10,... | collective-permute-start | bytes 98312 | tf_op jit(solution)/shard_map/ppermute | solution.py:486
  16.8 0.0 collective-permute-start.10
  16.8 1.5 %collective-permute-start.11 = (bf16[288,128]{1,0:T(8,128)(2,1)S(1)}, bf16[288,128]{1,0:T(8,128)(2,1)S(1)}, u32[]{:S(2)}, u32[]{:S(2)}) collective-permute-start(bf16[288,128]{1,0:T(8,128)(2,1)S(1)} %get-tuple-element.102), channel_id=1, source_target_pairs={{0,4},{1,5},{2,6},{3,7},{4,0},{5,1},{6,2},{7,3},{8,12},{9,13},{10,... | collective-permute-start | bytes 221192 | tf_op jit(solution)/shard_map/ppermute | solution.py:486
  18.4 0.3 collective-permute-start.12
  18.6 0.4 %collective-permute-start.6 = (bf16[3,192,256]{2,1,0:T(8,128)(2,1)S(1)}, bf16[3,192,256]{2,1,0:T(8,128)(2,1)S(1)}, u32[]{:S(2)}, u32[]{:S(2)}) collective-permute-start(bf16[3,192,256]{2,1,0:T(8,128)(2,1)S(1)} %get-tuple-element.91), channel_id=1, source_target_pairs={{0,1},{1,0},{2,3},{3,2},{4,5},{5,4},{6,7},{7,6},{8,9},{9,8},{10,11... | collective-permute-start | bytes 884744 | tf_op jit(solution)/shard_map/ppermute | solution.py:482
  19.0 1.9 %phase.1 = (f32[128,1280]{1,0:T(8,128)S(1)}, bf16[3,512,1280]{2,1,0:T(8,128)(2,1)S(1)}) custom-call(s32[8,1280]{1,0:T(8,128)S(1)} %get-tuple-element.85.refs_0_, s32[8,1280]{1,0:T(8,128)S(1)} %get-tuple-element.86.refs_1_, f32[8,1280]{1,0:T(8,128)S(1)} %get-tuple-element.87.refs_2_, f32[8,1280]{1,0:T(8,128)S(1)} %get-tuple-element.88.refs_3_, ...), custom_call_target="tpu_custom_call" | custom-call | flops 10000000000 | bytes 9076736 | tf_op jit(solution)/shard_map/phase/pallas_call | solution.py:40
  20.9 0.8 %far.1 = (bf16[32,1408]{1,0:T(8,128)(2,1)S(1)}, bf16[64,128]{1,0:T(8,128)(2,1)S(1)}) custom-call(bf16[3,512,1280]{2,1,0:T(8,128)(2,1)S(1)} %get-tuple-element.92.refs_4_.mine_ref, bf16[3,512,1280]{2,1,0:T(8,128)(2,1)S(1)} %get-tuple-element.97.cols_ref, f32[128,1280]{1,0:T(8,128)S(1)} %get-tuple-element.98.phase, ...), custom_call_target="tpu_custom_call" | custom-call | flops 300000000 | bytes 8986624 | tf_op jit(solution)/shard_map/far/pallas_call | solution.py:40
  21.7 3.7 %collective-permute-start.14 = (bf16[32,1408]{1,0:T(8,128)(2,1)S(1)}, bf16[32,1408]{1,0:T(8,128)(2,1)S(1)}, u32[]{:S(2)}, u32[]{:S(2)}) collective-permute-start(bf16[32,1408]{1,0:T(8,128)(2,1)S(1)} %get-tuple-element.109), channel_id=1, source_target_pairs={{0,24},{4,28},{8,16},{12,20},{16,8},{20,12},{24,0},{28,4},{1,25},{... | collective-permute-start | bytes 270344 | tf_op jit(solution)/shard_map/ppermute | solution.py:591
  25.4 0.8 %rest.1 = (bf16[32,1280]{1,0:T(8,128)(2,1)S(1)}, bf16[32,1408]{1,0:T(8,128)(2,1)S(1)}, bf16[32,1280]{1,0:T(8,128)(2,1)S(1)}) custom-call(bf16[3,512,1280]{2,1,0:T(8,128)(2,1)S(1)} %get-tuple-element.92.refs_4_.mine_ref, bf16[3,512,1280]{2,1,0:T(8,128)(2,1)S(1)} %get-tuple-element.97.cols_ref, f32[128,1280]{1,0:T(8,128)S(1)} %get-tuple-element.98.phase, ...), custom_call_target="tpu_custom_call" | custom-call | tf_op jit(solution)/shard_map/rest/pallas_call | solution.py:40
  26.2 0.1 collective-permute-start.13
  26.3 2.4 %collective-permute-start.15 = (bf16[32,1280]{1,0:T(8,128)(2,1)S(1)}, bf16[32,1280]{1,0:T(8,128)(2,1)S(1)}, u32[]{:S(2)}, u32[]{:S(2)}) collective-permute-start(bf16[32,1280]{1,0:T(8,128)(2,1)S(1)} %get-tuple-element.121), channel_id=1, source_target_pairs={{0,16},{4,20},{8,24},{12,28},{16,0},{20,4},{24,8},{28,12},{1,17},{... | collective-permute-start | bytes 245768 | tf_op jit(solution)/shard_map/ppermute | solution.py:591
  28.6 0.7 %optics.1 = (f32[32,1280]{1,0:T(8,128)S(1)}, bf16[256,512]{1,0:T(8,128)(2,1)S(1)}, bf16[256,512]{1,0:T(8,128)(2,1)S(1)}, bf16[128,192]{1,0:T(8,128)(2,1)S(1)}) custom-call(f32[32,1280]{1,0:T(8,128)S(1)} %get-tuple-element.110.amplitude, f32[128,128]{1,0:T(8,128)S(1)} %get-tuple-element.111.ones, f32[256,512]{1,0:T(8,128)S(1)} %get-tuple-element.112.columns, ...), custom_call_target="tpu_custom_call" | custom-call | tf_op jit(solution)/shard_map/optics/pallas_call | solution.py:40
  29.3 2.7 %collective-permute-done.13.refs_0_.refs_1_ = bf16[32,1408]{1,0:T(8,128)(2,1)S(1)} collective-permute-done((bf16[32,1408]{1,0:T(8,128)(2,1)S(1)}, bf16[32,1408]{1,0:T(8,128)(2,1)S(1)}, u32[]{:S(2)}, u32[]{:S(2)}) %collective-permute-start.13) | collective-permute-done | bytes 90144 | tf_op jit(solution)/shard_map/ppermute | solution.py:591
  32.0 2.0 %shift.1 = bf16[3,128,512]{2,1,0:T(8,128)(2,1)} custom-call(s32[2,3]{1,0:T(2,128)} %bitcast.7, bf16[3,128,512]{2,1,0:T(8,128)(2,1)S(1)} %get-tuple-element.66.own, bf16[3,128,128]{2,1,0:T(8,128)(2,1)S(1)} %collective-permute-done.near.refs_6_.near0, bf16[3,128,128]{2,1,0:T(8,128)(2,1)S(1)} %collective-permute-done.1.refs_2_.near1, ...), custom_call_target="tpu_custom_call" | custom-call | tf_op jit(solution)/shard_map/shift/pallas_call | solution.py:40
  34.0 1.7 %imaging.1 = f32[64,2560]{1,0:T(8,128)} custom-call(bf16[32,1280]{1,0:T(8,128)(2,1)S(1)} %get-tuple-element.120.refs_0_, bf16[32,1408]{1,0:T(8,128)(2,1)S(1)} %collective-permute-done.13.refs_0_.refs_1_, bf16[32,1280]{1,0:T(8,128)(2,1)S(1)} %collective-permute-done.15.refs_2_, bf16[32,1408]{1,0:T(8,128)(2,1)S(1)} %collective-permute-done.14.refs_1_.refs_3_, ...), custom_call_target="tpu_custom_call" | custom-call | flops 400000000 | bytes 1736704 | tf_op jit(solution)/shard_map/imaging/pallas_call | solution.py:40
  (11 shorter events, 0.0 us)
Async XLA Ops:
  1.7 7.5 %collective-permute-start.3 = (bf16[3,128,128]{2,1,0:T(8,128)(2,1)S(1)}, bf16[3,128,128]{2,1,0:T(8,128)(2,1)S(1)}, u32[]{:S(2)}, u32[]{:S(2)}) collective-permute-start(bf16[3,128,128]{2,1,0:T(8,128)(2,1)S(1)} %get-tuple-element.67), channel_id=1, source_target_pairs={{0,3},{1,2},{2,1},{3,0},{4,7},{5,6},{6,5},{7,4},{8,11},{9,10},{10,... | collective-permute-start | bytes 294920 | tf_op jit(solution)/shard_map/ppermute | solution.py:482
  4.2 5.7 %collective-permute-start.2 = (bf16[3,128,128]{2,1,0:T(8,128)(2,1)S(1)}, bf16[3,128,128]{2,1,0:T(8,128)(2,1)S(1)}, u32[]{:S(2)}, u32[]{:S(2)}) collective-permute-start(bf16[3,128,128]{2,1,0:T(8,128)(2,1)S(1)} %get-tuple-element.69.keep.refs_7_), channel_id=1, source_target_pairs={{0,2},{1,3},{2,0},{3,1},{4,6},{5,7},{6,4},{7,5},{8,10},{9,11},{10,... | collective-permute-start | bytes 294920 | tf_op jit(solution)/shard_map/ppermute | solution.py:482
  4.8 5.0 %collective-permute-start = (bf16[3,128,128]{2,1,0:T(8,128)(2,1)S(1)}, bf16[3,128,128]{2,1,0:T(8,128)(2,1)S(1)}, u32[]{:S(2)}, u32[]{:S(2)}) collective-permute-start(bf16[3,128,128]{2,1,0:T(8,128)(2,1)S(1)} %get-tuple-element.67), channel_id=1, source_target_pairs={{0,1},{1,0},{2,3},{3,2},{4,5},{5,4},{6,7},{7,6},{8,9},{9,8},{10,11... | collective-permute-start | bytes 294920 | tf_op jit(solution)/shard_map/ppermute | solution.py:482
  4.9 9.3 %collective-permute-start.4 = (bf16[3,128,128]{2,1,0:T(8,128)(2,1)S(1)}, bf16[3,128,128]{2,1,0:T(8,128)(2,1)S(1)}, u32[]{:S(2)}, u32[]{:S(2)}) collective-permute-start(bf16[3,128,128]{2,1,0:T(8,128)(2,1)S(1)} %get-tuple-element.68), channel_id=1, source_target_pairs={{0,3},{1,2},{2,1},{3,0},{4,7},{5,6},{6,5},{7,4},{8,11},{9,10},{10,... | collective-permute-start | bytes 294920 | tf_op jit(solution)/shard_map/ppermute | solution.py:482
  6.3 7.9 %collective-permute-start.5 = (bf16[3,128,128]{2,1,0:T(8,128)(2,1)S(1)}, bf16[3,128,128]{2,1,0:T(8,128)(2,1)S(1)}, u32[]{:S(2)}, u32[]{:S(2)}) collective-permute-start(bf16[3,128,128]{2,1,0:T(8,128)(2,1)S(1)} %get-tuple-element.77.refs_3_), channel_id=1, source_target_pairs={{0,2},{1,3},{2,0},{3,1},{4,6},{5,7},{6,4},{7,5},{8,10},{9,11},{10,... | collective-permute-start | bytes 294920 | tf_op jit(solution)/shard_map/ppermute | solution.py:482
  9.2 5.0 %collective-permute-start.1 = (bf16[3,128,128]{2,1,0:T(8,128)(2,1)S(1)}, bf16[3,128,128]{2,1,0:T(8,128)(2,1)S(1)}, u32[]{:S(2)}, u32[]{:S(2)}) collective-permute-start(bf16[3,128,128]{2,1,0:T(8,128)(2,1)S(1)} %get-tuple-element.68), channel_id=1, source_target_pairs={{0,1},{1,0},{2,3},{3,2},{4,5},{5,4},{6,7},{7,6},{8,9},{9,8},{10,11... | collective-permute-start | bytes 294920 | tf_op jit(solution)/shard_map/ppermute | solution.py:482
  10.4 7.9 %collective-permute-start.7 = (bf16[3,128,128]{2,1,0:T(8,128)(2,1)S(1)}, bf16[3,128,128]{2,1,0:T(8,128)(2,1)S(1)}, u32[]{:S(2)}, u32[]{:S(2)}) collective-permute-start(bf16[3,128,128]{2,1,0:T(8,128)(2,1)S(1)} %get-tuple-element.95), channel_id=1, source_target_pairs={{0,4},{1,5},{2,6},{3,7},{4,0},{5,1},{6,2},{7,3},{8,12},{9,13},{10,... | collective-permute-start | bytes 294920 | tf_op jit(solution)/shard_map/ppermute | solution.py:486
  12.7 6.0 %collective-permute-start.8 = (bf16[3,128,128]{2,1,0:T(8,128)(2,1)S(1)}, bf16[3,128,128]{2,1,0:T(8,128)(2,1)S(1)}, u32[]{:S(2)}, u32[]{:S(2)}) collective-permute-start(bf16[3,128,128]{2,1,0:T(8,128)(2,1)S(1)} %get-tuple-element.96), channel_id=1, source_target_pairs={{0,5},{1,4},{2,7},{3,6},{4,1},{5,0},{6,3},{7,2},{8,13},{9,12},{10,... | collective-permute-start | bytes 294920 | tf_op jit(solution)/shard_map/ppermute | solution.py:486
  14.8 6.1 %collective-permute-start.9 = (bf16[128,128]{1,0:T(8,128)(2,1)S(1)}, bf16[128,128]{1,0:T(8,128)(2,1)S(1)}, u32[]{:S(2)}, u32[]{:S(2)}) collective-permute-start(bf16[128,128]{1,0:T(8,128)(2,1)S(1)} %get-tuple-element.99), channel_id=1, source_target_pairs={{0,4},{1,5},{2,6},{3,7},{4,0},{5,1},{6,2},{7,3},{8,12},{9,13},{10,... | collective-permute-start | bytes 98312 | tf_op jit(solution)/shard_map/ppermute | solution.py:486
  16.8 4.1 %collective-permute-start.10 = (bf16[128,128]{1,0:T(8,128)(2,1)S(1)}, bf16[128,128]{1,0:T(8,128)(2,1)S(1)}, u32[]{:S(2)}, u32[]{:S(2)}) collective-permute-start(bf16[128,128]{1,0:T(8,128)(2,1)S(1)} %get-tuple-element.100), channel_id=1, source_target_pairs={{0,5},{1,4},{2,7},{3,6},{4,1},{5,0},{6,3},{7,2},{8,13},{9,12},{10,... | collective-permute-start | bytes 98312 | tf_op jit(solution)/shard_map/ppermute | solution.py:486
  16.8 8.6 %collective-permute-start.11 = (bf16[288,128]{1,0:T(8,128)(2,1)S(1)}, bf16[288,128]{1,0:T(8,128)(2,1)S(1)}, u32[]{:S(2)}, u32[]{:S(2)}) collective-permute-start(bf16[288,128]{1,0:T(8,128)(2,1)S(1)} %get-tuple-element.102), channel_id=1, source_target_pairs={{0,4},{1,5},{2,6},{3,7},{4,0},{5,1},{6,2},{7,3},{8,12},{9,13},{10,... | collective-permute-start | bytes 221192 | tf_op jit(solution)/shard_map/ppermute | solution.py:486
  18.4 7.0 %collective-permute-start.12 = (bf16[288,128]{1,0:T(8,128)(2,1)S(1)}, bf16[288,128]{1,0:T(8,128)(2,1)S(1)}, u32[]{:S(2)}, u32[]{:S(2)}) collective-permute-start(bf16[288,128]{1,0:T(8,128)(2,1)S(1)} %get-tuple-element.103), channel_id=1, source_target_pairs={{0,5},{1,4},{2,7},{3,6},{4,1},{5,0},{6,3},{7,2},{8,13},{9,12},{10,... | collective-permute-start | bytes 221192 | tf_op jit(solution)/shard_map/ppermute | solution.py:486
  18.6 2.3 %collective-permute-start.6 = (bf16[3,192,256]{2,1,0:T(8,128)(2,1)S(1)}, bf16[3,192,256]{2,1,0:T(8,128)(2,1)S(1)}, u32[]{:S(2)}, u32[]{:S(2)}) collective-permute-start(bf16[3,192,256]{2,1,0:T(8,128)(2,1)S(1)} %get-tuple-element.91), channel_id=1, source_target_pairs={{0,1},{1,0},{2,3},{3,2},{4,5},{5,4},{6,7},{7,6},{8,9},{9,8},{10,11... | collective-permute-start | bytes 884744 | tf_op jit(solution)/shard_map/ppermute | solution.py:482
  21.7 6.9 %collective-permute-start.14 = (bf16[32,1408]{1,0:T(8,128)(2,1)S(1)}, bf16[32,1408]{1,0:T(8,128)(2,1)S(1)}, u32[]{:S(2)}, u32[]{:S(2)}) collective-permute-start(bf16[32,1408]{1,0:T(8,128)(2,1)S(1)} %get-tuple-element.109), channel_id=1, source_target_pairs={{0,24},{4,28},{8,16},{12,20},{16,8},{20,12},{24,0},{28,4},{1,25},{... | collective-permute-start | bytes 270344 | tf_op jit(solution)/shard_map/ppermute | solution.py:591
  26.2 5.8 %collective-permute-start.13 = (bf16[32,1408]{1,0:T(8,128)(2,1)S(1)}, bf16[32,1408]{1,0:T(8,128)(2,1)S(1)}, u32[]{:S(2)}, u32[]{:S(2)}) collective-permute-start(bf16[32,1408]{1,0:T(8,128)(2,1)S(1)} %get-tuple-element.104), channel_id=1, source_target_pairs={{0,8},{4,12},{8,0},{12,4},{16,24},{20,28},{24,16},{28,20},{1,9},{5... | collective-permute-start | bytes 270344 | tf_op jit(solution)/shard_map/ppermute | solution.py:591
  26.3 7.8 %collective-permute-start.15 = (bf16[32,1280]{1,0:T(8,128)(2,1)S(1)}, bf16[32,1280]{1,0:T(8,128)(2,1)S(1)}, u32[]{:S(2)}, u32[]{:S(2)}) collective-permute-start(bf16[32,1280]{1,0:T(8,128)(2,1)S(1)} %get-tuple-element.121), channel_id=1, source_target_pairs={{0,16},{4,20},{8,24},{12,28},{16,0},{20,4},{24,8},{28,12},{1,17},{... | collective-permute-start | bytes 245768 | tf_op jit(solution)/shard_map/ppermute | solution.py:591

commit v12 on v11

--- a/solution.py
+++ b/solution.py
@@ -116,7 +116,10 @@
     column = lax.axis_index("layer")
     block = pupil_rows // n_layer
     row = lax.broadcasted_iota(jnp.int32, (half, LANES), 0)
-    pair = jnp.bitwise_xor(row // block, column // 2)
+    step = row // block
+    for at, value in enumerate(send_order(n_layer // 2)):
+        step = jnp.where(row // block == at, value, step)
+    pair = jnp.bitwise_xor(step, column // 2)
     parity = lax.rem(column, 2)
     inside = lax.rem(row, block) + pair * (2 * block)
     pixel_rows = stack(inside + parity * block, inside + (1 - parity) * block)
@@ -239,6 +242,10 @@
     rows = near.shape[1]
     size = (far.shape[0] - STRIP * rows // LANES) // layers
     start = half - size
+    for out in (rest, sibling_rest):
+        left = out.shape[0] - layers * start
+        if left:
+            out[layers * start :] = jnp.zeros((left, width), jnp.bfloat16)
     for level in range(layers):
         part = project_rows(rows_ref, keep, near, across, diagonal, level)
         mine[level] = part[:half]
@@ -299,6 +306,11 @@
     return [2**k - 1 for k in range(1, pairs.bit_length())]
 
 
+def send_order(pairs):
+    steps = strip_steps(pairs)
+    return [k for k in range(pairs) if k not in steps] + steps
+
+
 def add_strip(pairs, step, strips, out):
     pair = lax.axis_index("layer") // 2
     after = lax.rem(pair + 1, pairs) == jnp.bitwise_xor(pair, step)
@@ -307,23 +319,24 @@
     out[:, at:] = jnp.where(after, last, first).astype(jnp.bfloat16)
 
 
-def far_kernel(mine_ref, cols_ref, phase, taken, came, sibling_came, out, strips):
-    half, size = phase.shape[0], out.shape[0]
-    sum_up(half - size, mine_ref, cols_ref, phase, taken, came, sibling_came, [out])
+def far_kernel(mine_ref, cols_ref, phase, taken, came, sibling_came, *outs):
+    *outs, strips = outs
+    half = phase.shape[0]
+    size = outs[0].shape[0] * len(outs)
+    sum_up(half - size, mine_ref, cols_ref, phase, taken, came, sibling_came, outs)
     layers = taken.shape[0]
     odd = lax.rem(lax.axis_index("dir"), 2) == 1
     here = get_strip(came, layers * size).astype(jnp.float32)
     there = get_strip(sibling_came, layers * size).astype(jnp.float32)
     strips[:STRIP] = jnp.where(odd, here, there).astype(jnp.bfloat16)
     strips[STRIP:] = jnp.where(odd, there, here).astype(jnp.bfloat16)
-    add_strip(half // size, half // size - 1, strips, out)
-
-
-def rest_kernel(mine_ref, cols_ref, phase, taken, came, sibling_came, strips, *outs):
+    pairs = half // outs[0].shape[0]
+    for out, step in zip(outs, strip_steps(pairs)):
+        add_strip(pairs, step, strips, out)
+
+
+def rest_kernel(mine_ref, cols_ref, phase, taken, came, sibling_came, *outs):
     sum_up(0, mine_ref, cols_ref, phase, taken, came, sibling_came, outs)
-    pairs = len(outs) + 1
-    for step in strip_steps(pairs)[:-1]:
-        add_strip(pairs, step, strips, outs[step])
 
 
 def shifted_rows(shift, odd, own, near, far):
@@ -548,8 +561,10 @@
         scratch=wind_scratch,
         brief=True,
     )
-    message = shape(layers * rows + STRIP * rows_dev // LANES, width)
-    remainder = shape(layers * (half - rows), width)
+    steps = strip_steps(pairs)
+    far = len(steps) * rows
+    message = shape(layers * far + STRIP * rows_dev // LANES, width)
+    remainder = shape(max(layers * (half - far), message.shape[0] + 16), width)
     mine1, give, far1, sibling_far1, rest1, sibling_rest1 = call(
         later_rows_kernel,
         [projected, shape(layers, half + 64, 2 * width), message, message, remainder, remainder],
@@ -569,26 +584,25 @@
         "phase",
     )
 
-    steps = strip_steps(pairs)
-    sums = [shape(rows, pupil_cols + (rows_dev if k in steps else 0)) for k in range(pairs)]
-    far_sum, strips = call(
+    *far_sums, strips = call(
         far_kernel,
-        [sums[-1], shape(2 * STRIP, rows_dev)],
+        [shape(rows, pupil_cols + rows_dev)] * len(steps) + [shape(2 * STRIP, rows_dev)],
         (cols, others, phase, taken, far1, sibling_far1),
         300_000_000,
         "far",
     )
     rest_sums = call(
         rest_kernel,
-        sums[:-1],
-        (cols, others, phase, taken, rest1, sibling_rest1, strips),
+        [shape(rows, pupil_cols)] * (pairs - len(steps)),
+        (cols, others, phase, taken, rest1, sibling_rest1),
         0,
         "rest",
         brief=True,
     )
-    received = [*rest_sums, far_sum]
+    received = dict(zip(send_order(pairs), [*rest_sums, *far_sums]))
     for k in range(1, pairs):
         received[k] = lax.ppermute(received[k], "layer", [(i, i ^ (2 * k)) for i in range(n_layer)])
+    received = [received[k] for k in range(pairs)]
 
     optics_in, received[-1] = lax.optimization_barrier((optics_in, received[-1]))
     optics = call(

time: 35.9 us -> 35.6 us (level)
  starting transfers between devices: 17.9 us -> 16.2 us
  waiting for transfers between devices: 3.3 us -> 4.57 us
    ppermute x3, starting transfers between devices: 6.13 us -> 4.51 us  [per_device(): lax.ppermute(received[k], 'layer', [(i, i ^ 2 * k) for i in range(n_layer)])]
    ppermute x3, waiting for transfers between devices: 2.7 us -> 3.91 us  [per_device(): lax.ppermute(received[k], 'layer', [(i, i ^ 2 * k) for i in range(n_layer)])]
  transfers between devices with their start and end apart: 16 -> 16, of which waited for: 2 -> 4; matrix products, arithmetic and copies ran while one was open for 0% -> 0% of each run, Pallas kernels for 31% -> 31%
where the time goes in v12:
time: 35.6 us; the launch traced here: 35.5 us
  starting transfers between devices  16.2 us (46%)
  Pallas kernels  13.9 us (39%)
  waiting for transfers between devices  4.57 us (13%)
  between operations  0.76 us (2%)
    pallas_call x11, Pallas kernels, call(): pl.pallas_call(kernel, out_shape=out_shape, in_specs=in_specs, out_specs=...  13.9 us
    ppermute x6, starting transfers between devices, partner(): lax.ppermute(value, ('layer', 'dir'), [(i, i ^ n_dir ^ bits) for i in ran...  6.03 us
    ppermute x7, starting transfers between devices, swap(): return lax.ppermute(value, 'dir', [(i, i ^ bits) for i in range(n_dir)])  5.69 us
    ppermute x3, starting transfers between devices, per_device(): lax.ppermute(received[k], 'layer', [(i, i ^ 2 * k) for i in range(n_layer)])  4.51 us
    ppermute x3, waiting for transfers between devices, per_device(): lax.ppermute(received[k], 'layer', [(i, i ^ 2 * k) for i in range(n_layer)])  3.91 us
  transfers between devices with their start and end apart: 16, of which 4 were waited for; matrix products, arithmetic and copies ran while one was open for 0% of the time, Pallas kernels for 31%

profile of v12, /device:TPU:0, one launch (start us, length us, event | category | flops | bytes accessed | tf_op | source)
XLA Modules:
  0.0 35.5 jit_solution(11567116689523414089)
XLA Ops:
  0.6 1.1 %split.1 = (bf16[3,128,128]{2,1,0:T(8,128)(2,1)S(1)}, bf16[3,128,128]{2,1,0:T(8,128)(2,1)S(1)}, bf16[3,128,128]{2,1,0:T(8,128)(2,1)S(1)}, bf16[3,128,128]{2,1,0:T(8,128)(2,1)S(1)}) custom-call(bf16[3,128,512]{2,1,0:T(8,128)(2,1)} %refs_0_.1), custom_call_target="tpu_custom_call" | custom-call | tf_op jit(solution)/shard_map/split/pallas_call | solution.py:40
  1.7 2.4 %collective-permute-start.3 = (bf16[3,128,128]{2,1,0:T(8,128)(2,1)S(1)}, bf16[3,128,128]{2,1,0:T(8,128)(2,1)S(1)}, u32[]{:S(2)}, u32[]{:S(2)}) collective-permute-start(bf16[3,128,128]{2,1,0:T(8,128)(2,1)S(1)} %get-tuple-element.67), channel_id=1, source_target_pairs={{0,3},{1,2},{2,1},{3,0},{4,7},{5,6},{6,5},{7,4},{8,11},{9,10},{10,... | collective-permute-start | bytes 294920 | tf_op jit(solution)/shard_map/ppermute | solution.py:495
  4.2 0.6 %collective-permute-start.2 = (bf16[3,128,128]{2,1,0:T(8,128)(2,1)S(1)}, bf16[3,128,128]{2,1,0:T(8,128)(2,1)S(1)}, u32[]{:S(2)}, u32[]{:S(2)}) collective-permute-start(bf16[3,128,128]{2,1,0:T(8,128)(2,1)S(1)} %get-tuple-element.69.keep.refs_7_), channel_id=1, source_target_pairs={{0,2},{1,3},{2,0},{3,1},{4,6},{5,7},{6,4},{7,5},{8,10},{9,11},{10,... | collective-permute-start | bytes 294920 | tf_op jit(solution)/shard_map/ppermute | solution.py:495
  4.8 0.0 collective-permute-start
  4.9 1.5 %collective-permute-start.4 = (bf16[3,128,128]{2,1,0:T(8,128)(2,1)S(1)}, bf16[3,128,128]{2,1,0:T(8,128)(2,1)S(1)}, u32[]{:S(2)}, u32[]{:S(2)}) collective-permute-start(bf16[3,128,128]{2,1,0:T(8,128)(2,1)S(1)} %get-tuple-element.68), channel_id=1, source_target_pairs={{0,3},{1,2},{2,1},{3,0},{4,7},{5,6},{6,5},{7,4},{8,11},{9,10},{10,... | collective-permute-start | bytes 294920 | tf_op jit(solution)/shard_map/ppermute | solution.py:495
  6.3 0.6 %collective-permute-start.5 = (bf16[3,128,128]{2,1,0:T(8,128)(2,1)S(1)}, bf16[3,128,128]{2,1,0:T(8,128)(2,1)S(1)}, u32[]{:S(2)}, u32[]{:S(2)}) collective-permute-start(bf16[3,128,128]{2,1,0:T(8,128)(2,1)S(1)} %get-tuple-element.77.refs_3_), channel_id=1, source_target_pairs={{0,2},{1,3},{2,0},{3,1},{4,6},{5,7},{6,4},{7,5},{8,10},{9,11},{10,... | collective-permute-start | bytes 294920 | tf_op jit(solution)/shard_map/ppermute | solution.py:495
  7.0 2.2 %weights.1 = (bf16[2,3,256,512]{3,2,1,0:T(8,128)(2,1)S(1)}, s32[8,1280]{1,0:T(8,128)S(1)}, s32[8,1280]{1,0:T(8,128)S(1)}, f32[8,1280]{1,0:T(8,128)S(1)}, f32[8,1...) custom-call(s32[2,3]{1,0:T(2,128)} %bitcast.5, ...), custom_call_target="tpu_custom_call" | custom-call | tf_op jit(solution)/shard_map/weights/pallas_call | solution.py:40
  9.2 0.0 collective-permute-done.3.diagonal.refs_5_.diagonal0
  9.2 0.1 collective-permute-start.1
  9.3 0.6 %collective-permute-done.2.across.refs_4_ = bf16[3,128,128]{2,1,0:T(8,128)(2,1)S(1)} collective-permute-done((bf16[3,128,128]{2,1,0:T(8,128)(2,1)S(1)}, bf16[3,128,128]{2,1,0:T(8,128)(2,1)S(1)}, u32[]{:S(2)}, u32[]{:S(2)}) %collective-permute-start.2) | collective-permute-done | bytes 98336 | tf_op jit(solution)/shard_map/ppermute | solution.py:495
  9.8 0.0 collective-permute-done.near.refs_6_.near0
  9.8 0.6 %rows_first.1 = (bf16[3,128,128]{2,1,0:T(8,128)(2,1)S(1)}, bf16[3,128,128]{2,1,0:T(8,128)(2,1)S(1)}, bf16[3,128,128]{2,1,0:T(8,128)(2,1)S(1)}, bf16[3,128,128]{2,1,0:T(8,128)(2,1)S(1)}) custom-call(bf16[2,3,256,512]{3,2,1,0:T(8,128)(2,1)S(1)} %get-tuple-element.76.rows_ref, bf16[3,128,128]{2,1,0:T(8,128)(2,1)S(1)} %collective-permute-done.2.across.refs_4_, ...), custom_call_target="tpu_custom_call" | custom-call | tf_op jit(solution)/shard_map/rows_first/pallas_call | solution.py:40
  10.4 2.2 %collective-permute-start.7 = (bf16[3,128,128]{2,1,0:T(8,128)(2,1)S(1)}, bf16[3,128,128]{2,1,0:T(8,128)(2,1)S(1)}, u32[]{:S(2)}, u32[]{:S(2)}) collective-permute-start(bf16[3,128,128]{2,1,0:T(8,128)(2,1)S(1)} %get-tuple-element.95), channel_id=1, source_target_pairs={{0,4},{1,5},{2,6},{3,7},{4,0},{5,1},{6,2},{7,3},{8,12},{9,13},{10,... | collective-permute-start | bytes 294920 | tf_op jit(solution)/shard_map/ppermute | solution.py:499
  12.7 0.0 collective-permute-start.8
  12.7 1.5 %columns.1 = (bf16[3,512,1280]{2,1,0:T(8,128)(2,1)S(1)}, bf16[32,128]{1,0:T(8,128)(2,1)S(1)}, bf16[32,128]{1,0:T(8,128)(2,1)S(1)}) custom-call(s32[2,3]{1,0:T(2,128)} %bitcast.6, s32[8,1280]{1,0:T(8,128)S(1)} %get-tuple-element.85.refs_0_, s32[8,1280]{1,0:T(8,128)S(1)} %get-tuple-element.86.refs_1_, f32[8,1280]{1,0:T(8,128)S(1)} %get-tuple-element.87.refs_2_, ...), custom_call_target="tpu_custom_call" | custom-call | tf_op jit(solution)/shard_map/columns/pallas_call | solution.py:40
  14.2 0.0 collective-permute-done.4.refs_1_.diagonal1
  14.2 0.6 %rows_later.1 = (bf16[3,128,128]{2,1,0:T(8,128)(2,1)S(1)}, bf16[3,192,256]{2,1,0:T(8,128)(2,1)S(1)}, bf16[224,128]{1,0:T(8,128)(2,1)S(1)}, bf16[224,128]{1,0:T(8...) custom-call(bf16[2,3,256,512]{3,2,1,0:T(8,128)(2,1)S(1)} %get-tuple-element.76.rows_ref, ...), custom_call_target="tpu_custom_call" | custom-call | tf_op jit(solution)/shard_map/rows_later/pallas_call | solution.py:40
  14.8 2.0 %collective-permute-start.9 = (bf16[224,128]{1,0:T(8,128)(2,1)S(1)}, bf16[224,128]{1,0:T(8,128)(2,1)S(1)}, u32[]{:S(2)}, u32[]{:S(2)}) collective-permute-start(bf16[224,128]{1,0:T(8,128)(2,1)S(1)} %get-tuple-element.99), channel_id=1, source_target_pairs={{0,4},{1,5},{2,6},{3,7},{4,0},{5,1},{6,2},{7,3},{8,12},{9,13},{10,... | collective-permute-start | bytes 172040 | tf_op jit(solution)/shard_map/ppermute | solution.py:499
  16.8 1.5 %collective-permute-start.13 = (bf16[240,128]{1,0:T(8,128)(2,1)S(1)}, bf16[240,128]{1,0:T(8,128)(2,1)S(1)}, u32[]{:S(2)}, u32[]{:S(2)}) collective-permute-start(bf16[240,128]{1,0:T(8,128)(2,1)S(1)} %get-tuple-element.118), channel_id=1, source_target_pairs={{0,4},{1,5},{2,6},{3,7},{4,0},{5,1},{6,2},{7,3},{8,12},{9,13},{10,... | collective-permute-start | bytes 184328 | tf_op jit(solution)/shard_map/ppermute | solution.py:499
  18.4 0.3 collective-permute-start.14
  18.6 0.4 %collective-permute-start.6 = (bf16[3,192,256]{2,1,0:T(8,128)(2,1)S(1)}, bf16[3,192,256]{2,1,0:T(8,128)(2,1)S(1)}, u32[]{:S(2)}, u32[]{:S(2)}) collective-permute-start(bf16[3,192,256]{2,1,0:T(8,128)(2,1)S(1)} %get-tuple-element.91), channel_id=1, source_target_pairs={{0,1},{1,0},{2,3},{3,2},{4,5},{5,4},{6,7},{7,6},{8,9},{9,8},{10,11... | collective-permute-start | bytes 884744 | tf_op jit(solution)/shard_map/ppermute | solution.py:495
  19.0 1.9 %phase.1 = (f32[128,1280]{1,0:T(8,128)S(1)}, bf16[3,512,1280]{2,1,0:T(8,128)(2,1)S(1)}) custom-call(s32[8,1280]{1,0:T(8,128)S(1)} %get-tuple-element.85.refs_0_, s32[8,1280]{1,0:T(8,128)S(1)} %get-tuple-element.86.refs_1_, f32[8,1280]{1,0:T(8,128)S(1)} %get-tuple-element.87.refs_2_, f32[8,1280]{1,0:T(8,128)S(1)} %get-tuple-element.88.refs_3_, ...), custom_call_target="tpu_custom_call" | custom-call | flops 10000000000 | bytes 9076736 | tf_op jit(solution)/shard_map/phase/pallas_call | solution.py:40
  20.9 0.1 collective-permute-done.10.sibling_came
  21.0 0.8 %far.1 = (bf16[32,1408]{1,0:T(8,128)(2,1)S(1)}, bf16[32,1408]{1,0:T(8,128)(2,1)S(1)}, bf16[64,128]{1,0:T(8,128)(2,1)S(1)}) custom-call(bf16[3,512,1280]{2,1,0:T(8,128)(2,1)S(1)} %get-tuple-element.92.refs_4_.mine_ref, bf16[3,512,1280]{2,1,0:T(8,128)(2,1)S(1)} %get-tuple-element.97.cols_ref, f32[128,1280]{1,0:T(8,128)S(1)} %get-tuple-element.98.phase, ...), custom_call_target="tpu_custom_call" | custom-call | flops 300000000 | bytes 9125888 | tf_op jit(solution)/shard_map/far/pallas_call | solution.py:40
  21.8 3.7 %collective-permute-start.12 = (bf16[32,1408]{1,0:T(8,128)(2,1)S(1)}, bf16[32,1408]{1,0:T(8,128)(2,1)S(1)}, u32[]{:S(2)}, u32[]{:S(2)}) collective-permute-start(bf16[32,1408]{1,0:T(8,128)(2,1)S(1)} %get-tuple-element.107), channel_id=1, source_target_pairs={{0,24},{4,28},{8,16},{12,20},{16,8},{20,12},{24,0},{28,4},{1,25},{... | collective-permute-start | bytes 270344 | tf_op jit(solution)/shard_map/ppermute | solution.py:604
  25.5 0.8 %rest.1 = (bf16[32,1280]{1,0:T(8,128)(2,1)S(1)}, bf16[32,1280]{1,0:T(8,128)(2,1)S(1)}) custom-call(bf16[3,512,1280]{2,1,0:T(8,128)(2,1)S(1)} %get-tuple-element.92.refs_4_.mine_ref, bf16[3,512,1280]{2,1,0:T(8,128)(2,1)S(1)} %get-tuple-element.97.cols_ref, f32[128,1280]{1,0:T(8,128)S(1)} %get-tuple-element.98.phase, ...), custom_call_target="tpu_custom_call" | custom-call | tf_op jit(solution)/shard_map/rest/pallas_call | solution.py:40
  26.3 0.8 %collective-permute-start.15 = (bf16[32,1280]{1,0:T(8,128)(2,1)S(1)}, bf16[32,1280]{1,0:T(8,128)(2,1)S(1)}, u32[]{:S(2)}, u32[]{:S(2)}) collective-permute-start(bf16[32,1280]{1,0:T(8,128)(2,1)S(1)} %get-tuple-element.121), channel_id=1, source_target_pairs={{0,16},{4,20},{8,24},{12,28},{16,0},{20,4},{24,8},{28,12},{1,17},{... | collective-permute-start | bytes 245768 | tf_op jit(solution)/shard_map/ppermute | solution.py:604
  27.1 2.0 %collective-permute-done.12.refs_1_.refs_3_ = bf16[32,1408]{1,0:T(8,128)(2,1)S(1)} collective-permute-done((bf16[32,1408]{1,0:T(8,128)(2,1)S(1)}, bf16[32,1408]{1,0:T(8,128)(2,1)S(1)}, u32[]{:S(2)}, u32[]{:S(2)}) %collective-permute-start.12) | collective-permute-done | bytes 90144 | tf_op jit(solution)/shard_map/ppermute | solution.py:604
  29.1 0.7 %optics.1 = (f32[32,1280]{1,0:T(8,128)S(1)}, bf16[256,512]{1,0:T(8,128)(2,1)S(1)}, bf16[256,512]{1,0:T(8,128)(2,1)S(1)}, bf16[128,192]{1,0:T(8,128)(2,1)S(1)}) custom-call(f32[32,1280]{1,0:T(8,128)S(1)} %get-tuple-element.108.amplitude, f32[128,128]{1,0:T(8,128)S(1)} %get-tuple-element.109.ones, f32[256,512]{1,0:T(8,128)S(1)} %get-tuple-element.110.columns, ...), custom_call_target="tpu_custom_call" | custom-call | tf_op jit(solution)/shard_map/optics/pallas_call | solution.py:40
  29.8 1.9 %collective-permute-done.11.refs_0_.refs_1_ = bf16[32,1408]{1,0:T(8,128)(2,1)S(1)} collective-permute-done((bf16[32,1408]{1,0:T(8,128)(2,1)S(1)}, bf16[32,1408]{1,0:T(8,128)(2,1)S(1)}, u32[]{:S(2)}, u32[]{:S(2)}) %collective-permute-start.11) | collective-permute-done | bytes 90144 | tf_op jit(solution)/shard_map/ppermute | solution.py:604
  31.7 2.0 %shift.1 = bf16[3,128,512]{2,1,0:T(8,128)(2,1)} custom-call(s32[2,3]{1,0:T(2,128)} %bitcast.7, bf16[3,128,512]{2,1,0:T(8,128)(2,1)S(1)} %get-tuple-element.66.own, bf16[3,128,128]{2,1,0:T(8,128)(2,1)S(1)} %collective-permute-done.near.refs_6_.near0, bf16[3,128,128]{2,1,0:T(8,128)(2,1)S(1)} %collective-permute-done.1.refs_2_.near1, ...), custom_call_target="tpu_custom_call" | custom-call | tf_op jit(solution)/shard_map/shift/pallas_call | solution.py:40
  33.7 1.7 %imaging.1 = f32[64,2560]{1,0:T(8,128)} custom-call(bf16[32,1280]{1,0:T(8,128)(2,1)S(1)} %get-tuple-element.120.refs_0_, bf16[32,1408]{1,0:T(8,128)(2,1)S(1)} %collective-permute-done.11.refs_0_.refs_1_, bf16[32,1280]{1,0:T(8,128)(2,1)S(1)} %collective-permute-done.15.refs_2_, bf16[32,1408]{1,0:T(8,128)(2,1)S(1)} %collective-permute-done.12.refs_1_.refs_3_, ...), custom_call_target="tpu_custom_call" | custom-call | flops 400000000 | bytes 1736704 | tf_op jit(solution)/shard_map/imaging/pallas_call | solution.py:40
  (11 shorter events, 0.0 us)
Async XLA Ops:
  1.7 7.5 %collective-permute-start.3 = (bf16[3,128,128]{2,1,0:T(8,128)(2,1)S(1)}, bf16[3,128,128]{2,1,0:T(8,128)(2,1)S(1)}, u32[]{:S(2)}, u32[]{:S(2)}) collective-permute-start(bf16[3,128,128]{2,1,0:T(8,128)(2,1)S(1)} %get-tuple-element.67), channel_id=1, source_target_pairs={{0,3},{1,2},{2,1},{3,0},{4,7},{5,6},{6,5},{7,4},{8,11},{9,10},{10,... | collective-permute-start | bytes 294920 | tf_op jit(solution)/shard_map/ppermute | solution.py:495
  4.2 5.7 %collective-permute-start.2 = (bf16[3,128,128]{2,1,0:T(8,128)(2,1)S(1)}, bf16[3,128,128]{2,1,0:T(8,128)(2,1)S(1)}, u32[]{:S(2)}, u32[]{:S(2)}) collective-permute-start(bf16[3,128,128]{2,1,0:T(8,128)(2,1)S(1)} %get-tuple-element.69.keep.refs_7_), channel_id=1, source_target_pairs={{0,2},{1,3},{2,0},{3,1},{4,6},{5,7},{6,4},{7,5},{8,10},{9,11},{10,... | collective-permute-start | bytes 294920 | tf_op jit(solution)/shard_map/ppermute | solution.py:495
  4.8 5.0 %collective-permute-start = (bf16[3,128,128]{2,1,0:T(8,128)(2,1)S(1)}, bf16[3,128,128]{2,1,0:T(8,128)(2,1)S(1)}, u32[]{:S(2)}, u32[]{:S(2)}) collective-permute-start(bf16[3,128,128]{2,1,0:T(8,128)(2,1)S(1)} %get-tuple-element.67), channel_id=1, source_target_pairs={{0,1},{1,0},{2,3},{3,2},{4,5},{5,4},{6,7},{7,6},{8,9},{9,8},{10,11... | collective-permute-start | bytes 294920 | tf_op jit(solution)/shard_map/ppermute | solution.py:495
  4.9 9.3 %collective-permute-start.4 = (bf16[3,128,128]{2,1,0:T(8,128)(2,1)S(1)}, bf16[3,128,128]{2,1,0:T(8,128)(2,1)S(1)}, u32[]{:S(2)}, u32[]{:S(2)}) collective-permute-start(bf16[3,128,128]{2,1,0:T(8,128)(2,1)S(1)} %get-tuple-element.68), channel_id=1, source_target_pairs={{0,3},{1,2},{2,1},{3,0},{4,7},{5,6},{6,5},{7,4},{8,11},{9,10},{10,... | collective-permute-start | bytes 294920 | tf_op jit(solution)/shard_map/ppermute | solution.py:495
  6.3 7.9 %collective-permute-start.5 = (bf16[3,128,128]{2,1,0:T(8,128)(2,1)S(1)}, bf16[3,128,128]{2,1,0:T(8,128)(2,1)S(1)}, u32[]{:S(2)}, u32[]{:S(2)}) collective-permute-start(bf16[3,128,128]{2,1,0:T(8,128)(2,1)S(1)} %get-tuple-element.77.refs_3_), channel_id=1, source_target_pairs={{0,2},{1,3},{2,0},{3,1},{4,6},{5,7},{6,4},{7,5},{8,10},{9,11},{10,... | collective-permute-start | bytes 294920 | tf_op jit(solution)/shard_map/ppermute | solution.py:495
  9.2 5.0 %collective-permute-start.1 = (bf16[3,128,128]{2,1,0:T(8,128)(2,1)S(1)}, bf16[3,128,128]{2,1,0:T(8,128)(2,1)S(1)}, u32[]{:S(2)}, u32[]{:S(2)}) collective-permute-start(bf16[3,128,128]{2,1,0:T(8,128)(2,1)S(1)} %get-tuple-element.68), channel_id=1, source_target_pairs={{0,1},{1,0},{2,3},{3,2},{4,5},{5,4},{6,7},{7,6},{8,9},{9,8},{10,11... | collective-permute-start | bytes 294920 | tf_op jit(solution)/shard_map/ppermute | solution.py:495
  10.4 7.9 %collective-permute-start.7 = (bf16[3,128,128]{2,1,0:T(8,128)(2,1)S(1)}, bf16[3,128,128]{2,1,0:T(8,128)(2,1)S(1)}, u32[]{:S(2)}, u32[]{:S(2)}) collective-permute-start(bf16[3,128,128]{2,1,0:T(8,128)(2,1)S(1)} %get-tuple-element.95), channel_id=1, source_target_pairs={{0,4},{1,5},{2,6},{3,7},{4,0},{5,1},{6,2},{7,3},{8,12},{9,13},{10,... | collective-permute-start | bytes 294920 | tf_op jit(solution)/shard_map/ppermute | solution.py:499
  12.7 6.0 %collective-permute-start.8 = (bf16[3,128,128]{2,1,0:T(8,128)(2,1)S(1)}, bf16[3,128,128]{2,1,0:T(8,128)(2,1)S(1)}, u32[]{:S(2)}, u32[]{:S(2)}) collective-permute-start(bf16[3,128,128]{2,1,0:T(8,128)(2,1)S(1)} %get-tuple-element.96), channel_id=1, source_target_pairs={{0,5},{1,4},{2,7},{3,6},{4,1},{5,0},{6,3},{7,2},{8,13},{9,12},{10,... | collective-permute-start | bytes 294920 | tf_op jit(solution)/shard_map/ppermute | solution.py:499
  14.8 6.1 %collective-permute-start.9 = (bf16[224,128]{1,0:T(8,128)(2,1)S(1)}, bf16[224,128]{1,0:T(8,128)(2,1)S(1)}, u32[]{:S(2)}, u32[]{:S(2)}) collective-permute-start(bf16[224,128]{1,0:T(8,128)(2,1)S(1)} %get-tuple-element.99), channel_id=1, source_target_pairs={{0,4},{1,5},{2,6},{3,7},{4,0},{5,1},{6,2},{7,3},{8,12},{9,13},{10,... | collective-permute-start | bytes 172040 | tf_op jit(solution)/shard_map/ppermute | solution.py:499
  16.8 4.1 %collective-permute-start.10 = (bf16[224,128]{1,0:T(8,128)(2,1)S(1)}, bf16[224,128]{1,0:T(8,128)(2,1)S(1)}, u32[]{:S(2)}, u32[]{:S(2)}) collective-permute-start(bf16[224,128]{1,0:T(8,128)(2,1)S(1)} %get-tuple-element.100), channel_id=1, source_target_pairs={{0,5},{1,4},{2,7},{3,6},{4,1},{5,0},{6,3},{7,2},{8,13},{9,12},{10,... | collective-permute-start | bytes 172040 | tf_op jit(solution)/shard_map/ppermute | solution.py:499
  16.8 8.6 %collective-permute-start.13 = (bf16[240,128]{1,0:T(8,128)(2,1)S(1)}, bf16[240,128]{1,0:T(8,128)(2,1)S(1)}, u32[]{:S(2)}, u32[]{:S(2)}) collective-permute-start(bf16[240,128]{1,0:T(8,128)(2,1)S(1)} %get-tuple-element.118), channel_id=1, source_target_pairs={{0,4},{1,5},{2,6},{3,7},{4,0},{5,1},{6,2},{7,3},{8,12},{9,13},{10,... | collective-permute-start | bytes 184328 | tf_op jit(solution)/shard_map/ppermute | solution.py:499
  18.4 7.1 %collective-permute-start.14 = (bf16[240,128]{1,0:T(8,128)(2,1)S(1)}, bf16[240,128]{1,0:T(8,128)(2,1)S(1)}, u32[]{:S(2)}, u32[]{:S(2)}) collective-permute-start(bf16[240,128]{1,0:T(8,128)(2,1)S(1)} %get-tuple-element.119), channel_id=1, source_target_pairs={{0,5},{1,4},{2,7},{3,6},{4,1},{5,0},{6,3},{7,2},{8,13},{9,12},{10,... | collective-permute-start | bytes 184328 | tf_op jit(solution)/shard_map/ppermute | solution.py:499
  18.6 2.4 %collective-permute-start.6 = (bf16[3,192,256]{2,1,0:T(8,128)(2,1)S(1)}, bf16[3,192,256]{2,1,0:T(8,128)(2,1)S(1)}, u32[]{:S(2)}, u32[]{:S(2)}) collective-permute-start(bf16[3,192,256]{2,1,0:T(8,128)(2,1)S(1)} %get-tuple-element.91), channel_id=1, source_target_pairs={{0,1},{1,0},{2,3},{3,2},{4,5},{5,4},{6,7},{7,6},{8,9},{9,8},{10,11... | collective-permute-start | bytes 884744 | tf_op jit(solution)/shard_map/ppermute | solution.py:495
  21.8 7.3 %collective-permute-start.12 = (bf16[32,1408]{1,0:T(8,128)(2,1)S(1)}, bf16[32,1408]{1,0:T(8,128)(2,1)S(1)}, u32[]{:S(2)}, u32[]{:S(2)}) collective-permute-start(bf16[32,1408]{1,0:T(8,128)(2,1)S(1)} %get-tuple-element.107), channel_id=1, source_target_pairs={{0,24},{4,28},{8,16},{12,20},{16,8},{20,12},{24,0},{28,4},{1,25},{... | collective-permute-start | bytes 270344 | tf_op jit(solution)/shard_map/ppermute | solution.py:604
  25.5 6.2 %collective-permute-start.11 = (bf16[32,1408]{1,0:T(8,128)(2,1)S(1)}, bf16[32,1408]{1,0:T(8,128)(2,1)S(1)}, u32[]{:S(2)}, u32[]{:S(2)}) collective-permute-start(bf16[32,1408]{1,0:T(8,128)(2,1)S(1)} %get-tuple-element.102), channel_id=1, source_target_pairs={{0,8},{4,12},{8,0},{12,4},{16,24},{20,28},{24,16},{28,20},{1,9},{5... | collective-permute-start | bytes 270344 | tf_op jit(solution)/shard_map/ppermute | solution.py:604
  26.3 7.5 %collective-permute-start.15 = (bf16[32,1280]{1,0:T(8,128)(2,1)S(1)}, bf16[32,1280]{1,0:T(8,128)(2,1)S(1)}, u32[]{:S(2)}, u32[]{:S(2)}) collective-permute-start(bf16[32,1280]{1,0:T(8,128)(2,1)S(1)} %get-tuple-element.121), channel_id=1, source_target_pairs={{0,16},{4,20},{8,24},{12,28},{16,0},{20,4},{24,8},{28,12},{1,17},{... | collective-permute-start | bytes 245768 | tf_op jit(solution)/shard_map/ppermute | solution.py:604

commit v13 on v12

--- a/solution.py
+++ b/solution.py
@@ -23,12 +23,14 @@
     return pltpu.CompilerParams(vmem_limit_bytes=held + 8 * 1024 * 1024)
 
 
-def call(kernel, out_shape, operands, flops, name, in_hbm=(), scratch=(), brief=False):
+def call(kernel, out_shape, operands, flops, name, in_hbm=(), out_hbm=(), scratch=(), brief=False):
     def spec(k, array):
-        scalars = array.dtype == jnp.int32 and array.size < LANES
-        return HBM_SPEC if scalars or k in in_hbm else VMEM_SPEC
-
-    out_specs = jax.tree.map(lambda _: VMEM_SPEC, out_shape)
+        return HBM_SPEC if k in in_hbm else VMEM_SPEC
+
+    if out_hbm:
+        out_specs = [HBM_SPEC if k in out_hbm else VMEM_SPEC for k in range(len(out_shape))]
+    else:
+        out_specs = jax.tree.map(lambda _: VMEM_SPEC, out_shape)
     size = sum(array.size * array.dtype.itemsize for array in jax.tree.leaves((operands, out_shape)))
     if brief:
         flops = size = 0
@@ -103,8 +105,9 @@
 def weights_kernel(geometry, wind_hbm, offsets_hbm, ratio_hbm, *refs):
     n_layer, rows_dev, screen_cols = geometry
     sources, (rows_out, base_out, upper_out, low_out, high_out), refs = refs[:5], refs[5:10], refs[10:]
-    copies, (wind, offsets, ratio, sems) = refs[:5], refs[5:]
-    others = fetch(*[(source, copy, sems.at[3 + k]) for k, (source, copy) in enumerate(zip(sources, copies))])
+    copies, (wind_copy, wind, offsets, ratio, sems) = refs[:5], refs[5:]
+    pairs = [*zip(sources, copies), (wind_hbm, wind_copy)]
+    others = fetch(*[(source, copy, sems.at[3 + k]) for k, (source, copy) in enumerate(pairs)])
     loads = fetch(
         (wind_hbm, wind, sems.at[0]),
         (offsets_hbm, offsets, sems.at[1]),
@@ -186,9 +189,9 @@
         lax.fori_loop(0, pupil_cols // LANES, tile, 0)
 
 
-def columns_kernel(wind_hbm, *refs):
+def columns_kernel(wind_held, *refs):
     tables, blocks, (out, strip, sibling_strip, wind, sem) = refs[:4], refs[4:8], refs[8:]
-    load = fetch((wind_hbm, wind, sem))[0]
+    load = fetch((wind_held, wind, sem))[0]
     column_weights(*tables, lax.axis_index("layer") * out.shape[1], out)
     across, diagonal, near, keep = blocks
     core = lax.rem(lax.axis_index("dir"), 2)
@@ -348,9 +351,9 @@
     return pltpu.roll(stack(before, own, after), shift, 0)[16 : 16 + rows]
 
 
-def shift_kernel(wind_hbm, own, near0, near1, diagonal0, diagonal1, taken, partner_strips, *refs):
+def shift_kernel(wind_held, own, near0, near1, diagonal0, diagonal1, taken, partner_strips, *refs):
     messages, (out, wind, sem) = refs[:-3], refs[-3:]
-    load = fetch((wind_hbm, wind, sem))[0]
+    load = fetch((wind_held, wind, sem))[0]
     layers, rows, cols = own.shape
     odd = lax.rem(lax.axis_index("dir"), 2) == 1
     half = taken.shape[1] - 64
@@ -385,7 +388,7 @@
         out[level] = pltpu.roll(beside(moved, extra), shift, 1)[:, :cols].astype(jnp.bfloat16)
 
 
-def optics_kernel(amplitude, ones, columns, lines, amp_out, high_out, low_out, lines_out):
+def optics_kernel(amplitude, ones, columns, lines, amp_out, columns_out, lines_out):
     rows, pupil_cols = amplitude.shape
     for step in range(pupil_cols // LANES):
         cut = slice(step * LANES, (step + 1) * LANES)
@@ -394,9 +397,8 @@
         energy = jnp.broadcast_to(energy[:, None], (rows // SUB_PIX, SUB_PIX, LANES)).reshape(rows, LANES)
         total = jnp.dot(energy, ones[...], precision=lax.Precision.HIGHEST, preferred_element_type=jnp.float32)
         amp_out[:, cut] = amp * lax.rsqrt(total)
-    high_out[...], low_out[...] = split(columns[...])
-    high, low = split(lines[...])
-    lines_out[...] = jnp.concatenate([high, high, low], axis=1)
+    columns_out[...] = columns[...].astype(jnp.bfloat16)
+    lines_out[...] = lines[...].astype(jnp.bfloat16)
 
 
 def sin_cos(phase):
@@ -415,15 +417,9 @@
     return sine * rest * sign, cosine * sign
 
 
-def split(value):
-    high = value.astype(jnp.bfloat16)
-    low = (value - high.astype(jnp.float32)).astype(jnp.bfloat16)
-    return high, low
-
-
 def imaging_kernel(count, *refs):
-    parts = refs[:count]
-    amp_ref, cols_high, cols_low, rows_table, out = refs[count:]
+    parts, (amp_ref, columns, lines, shifted, spots, screens, out, sems) = refs[:count], refs[count:]
+    copies = fetch((shifted, screens, sems.at[0]))
     rows, cols = amp_ref.shape
     tiles = cols // LANES
     phase = parts[0][:, :cols].astype(jnp.float32)
@@ -431,27 +427,22 @@
         phase = phase + part[:, :cols].astype(jnp.float32)
     sine, cosine = sin_cos(phase)
     amp = amp_ref[...]
-    real, imag = amp * cosine, amp * sine
-    field = jnp.concatenate(
-        [
-            jnp.concatenate(
-                [real[:, t * LANES : (t + 1) * LANES], imag[:, t * LANES : (t + 1) * LANES]], axis=1
-            )
-            for t in range(tiles)
-        ],
-        axis=0,
-    )
-    high, low = split(field)
-    half = dot(high, cols_high[...]) + (dot(low, cols_high[...]) + dot(high, cols_low[...]))
+    real, imag = (amp * cosine).astype(jnp.bfloat16), (amp * sine).astype(jnp.bfloat16)
+    cuts = [slice(t * LANES, (t + 1) * LANES) for t in range(tiles)]
+    field = stack(*[beside(real[:, cut], imag[:, cut]) for cut in cuts])
+    half = dot(field, columns[...]).astype(jnp.bfloat16)
     wide = 2 * LANES
     out_rows = 2 * rows
     for t in range(tiles):
         mine = half[t * rows : (t + 1) * rows]
-        mine = jnp.concatenate([mine[:, :wide], mine[:, wide:]], axis=0)
-        high, low = split(mine)
-        full = dot(rows_table[...], jnp.concatenate([high, low, high], axis=0))
+        full = dot(lines[...], stack(mine[:, :wide], mine[:, wide:]))
         real, imag = full[:out_rows], full[out_rows:]
         out[:, t * wide : (t + 1) * wide] = real * real + imag * imag
+        if t % 2:
+            cut = slice((t - 1) * wide, (t + 1) * wide)
+            copies += fetch((out.at[:, cut], spots.at[:, cut], sems.at[1 + t // 2]))
+    for copy in copies:
+        copy.wait()
 
 
 def tables_of(rows):
@@ -520,7 +511,7 @@
     diagonal1 = swap(give1, 3)
     ones = np.kron(np.eye(LANES // SUB_PIX), np.ones((SUB_PIX, SUB_PIX))).astype(np.float32)
     optics_in = (amplitude, jnp.asarray(ones), *[jnp.asarray(table) for table in tables_of(rows)])
-    copies = [shape(*array.shape, dtype=array.dtype) for array in (screens, *optics_in)]
+    copies = [shape(*array.shape, dtype=array.dtype) for array in (screens, *optics_in, wind)]
     row_weights, *tables = call(
         functools.partial(weights_kernel, (n_layer, rows_dev, cols_dev * n_layer)),
         [shape(2, layers, pupil_rows, 4 * rows_dev)]
@@ -529,11 +520,11 @@
         (wind, offsets, ratio, screens, *optics_in),
         0,
         "weights",
-        in_hbm=range(3, 8),
-        scratch=[smem(array.shape, jnp.int32) for array in (wind, offsets, ratio)] + [sem((8,))],
-        brief=True,
-    )
-    tables, own, optics_in = tables[:4], tables[4], tables[5:]
+        in_hbm=range(8),
+        scratch=[smem(array.shape, jnp.int32) for array in (wind, offsets, ratio)] + [sem((9,))],
+        brief=True,
+    )
+    tables, own, optics_in, wind = tables[:4], tables[4], tables[5:-1], tables[-1]
     give1, own = lax.optimization_barrier((give1, own))
     near1 = swap(give1, 1)
     tables = tuple(tables)
@@ -610,8 +601,7 @@
         (
             shape(rows, pupil_cols, dtype=f32),
             shape(*optics_in[2].shape),
-            shape(*optics_in[2].shape),
-            shape(optics_in[3].shape[0], 3 * optics_in[3].shape[1]),
+            shape(*optics_in[3].shape),
         ),
         optics_in,
         0,
@@ -619,7 +609,7 @@
         brief=True,
     )
     received[1], optics = lax.optimization_barrier((received[1], optics))
-    new_screens = call(
+    shifted = call(
         shift_kernel,
         shape(layers, rows_dev, cols_dev),
         (wind, own, near0, near1, diagonal0, diagonal1, taken, strips, *[received[k] for k in steps]),
@@ -628,12 +618,15 @@
         scratch=wind_scratch,
         brief=True,
     )
-    spots = call(
+    spots_shape = shape(2 * rows, 2 * pupil_cols, dtype=f32)
+    spots, new_screens = call(
         functools.partial(imaging_kernel, pairs),
-        shape(2 * rows, 2 * pupil_cols, dtype=f32),
-        (*received, *optics),
+        [spots_shape, shape(layers, rows_dev, cols_dev)],
+        (*received, *optics, shifted),
         400_000_000,
         "imaging",
+        out_hbm=(0, 1),
+        scratch=[pltpu.VMEM(spots_shape.shape, f32), sem((1 + pupil_cols // (2 * LANES),))],
     )
     return (new_screens, spots[None])
 

time: 35.6 us -> 34.9 us (0.980)
  Pallas kernels: 13.9 us -> 12.6 us
  waiting for transfers between devices: 4.57 us -> 5.12 us
    pallas_call x11, Pallas kernels: 13.9 us -> 12.6 us  [call(): pl.pallas_call(kernel, out_shape=out_shape, in_specs=in_specs, out_specs=...]
    ppermute x3, waiting for transfers between devices: 3.91 us -> 4.54 us  [per_device(): lax.ppermute(received[k], 'layer', [(i, i ^ 2 * k) for i in range(n_layer)])]
  transfers between devices with their start and end apart: 16 -> 16, of which waited for: 4 -> 4; matrix products, arithmetic and copies ran while one was open for 0% -> 0% of each run, Pallas kernels for 31% -> 29%
where the time goes in v13:
time: 34.9 us; the launch traced here: 34.7 us
  starting transfers between devices  16.2 us (46%)
  Pallas kernels  12.6 us (36%)
  waiting for transfers between devices  5.12 us (15%)
  between operations  0.75 us (2%)
    pallas_call x11, Pallas kernels, call(): pl.pallas_call(kernel, out_shape=out_shape, in_specs=in_specs, out_specs=...  12.6 us
    ppermute x6, starting transfers between devices, partner(): lax.ppermute(value, ('layer', 'dir'), [(i, i ^ n_dir ^ bits) for i in ran...  5.99 us
    ppermute x7, starting transfers between devices, swap(): return lax.ppermute(value, 'dir', [(i, i ^ bits) for i in range(n_dir)])  5.73 us
    ppermute x3, waiting for transfers between devices, per_device(): lax.ppermute(received[k], 'layer', [(i, i ^ 2 * k) for i in range(n_layer)])  4.54 us
    ppermute x3, starting transfers between devices, per_device(): lax.ppermute(received[k], 'layer', [(i, i ^ 2 * k) for i in range(n_layer)])  4.51 us
  transfers between devices with their start and end apart: 16, of which 4 were waited for; matrix products, arithmetic and copies ran while one was open for 0% of the time, Pallas kernels for 29%

profile of v13, /device:TPU:0, one launch (start us, length us, event | category | flops | bytes accessed | tf_op | source)
XLA Modules:
  0.0 34.7 jit_solution(14979821803343324873)
XLA Ops:
  0.6 1.1 %split.1 = (bf16[3,128,128]{2,1,0:T(8,128)(2,1)S(1)}, bf16[3,128,128]{2,1,0:T(8,128)(2,1)S(1)}, bf16[3,128,128]{2,1,0:T(8,128)(2,1)S(1)}, bf16[3,128,128]{2,1,0:T(8,128)(2,1)S(1)}) custom-call(bf16[3,128,512]{2,1,0:T(8,128)(2,1)} %screens.1), custom_call_target="tpu_custom_call" | custom-call | tf_op jit(solution)/shard_map/split/pallas_call | solution.py:42
  1.7 2.4 %collective-permute-start.1 = (bf16[3,128,128]{2,1,0:T(8,128)(2,1)S(1)}, bf16[3,128,128]{2,1,0:T(8,128)(2,1)S(1)}, u32[]{:S(2)}, u32[]{:S(2)}) collective-permute-start(bf16[3,128,128]{2,1,0:T(8,128)(2,1)S(1)} %get-tuple-element.67), channel_id=1, source_target_pairs={{0,3},{1,2},{2,1},{3,0},{4,7},{5,6},{6,5},{7,4},{8,11},{9,10},{10,... | collective-permute-start | bytes 294920 | tf_op jit(solution)/shard_map/ppermute | solution.py:486
  4.2 0.6 %collective-permute-start = (bf16[3,128,128]{2,1,0:T(8,128)(2,1)S(1)}, bf16[3,128,128]{2,1,0:T(8,128)(2,1)S(1)}, u32[]{:S(2)}, u32[]{:S(2)}) collective-permute-start(bf16[3,128,128]{2,1,0:T(8,128)(2,1)S(1)} %get-tuple-element.66.keep.refs_7_), channel_id=1, source_target_pairs={{0,2},{1,3},{2,0},{3,1},{4,6},{5,7},{6,4},{7,5},{8,10},{9,11},{10,... | collective-permute-start | bytes 294920 | tf_op jit(solution)/shard_map/ppermute | solution.py:486
  4.8 0.0 collective-permute-start.2
  4.9 1.7 %collective-permute-start.3 = (bf16[3,128,128]{2,1,0:T(8,128)(2,1)S(1)}, bf16[3,128,128]{2,1,0:T(8,128)(2,1)S(1)}, u32[]{:S(2)}, u32[]{:S(2)}) collective-permute-start(bf16[3,128,128]{2,1,0:T(8,128)(2,1)S(1)} %get-tuple-element.87.refs_3_), channel_id=1, source_target_pairs={{0,2},{1,3},{2,0},{3,1},{4,6},{5,7},{6,4},{7,5},{8,10},{9,11},{10,... | collective-permute-start | bytes 294920 | tf_op jit(solution)/shard_map/ppermute | solution.py:486
  6.6 0.1 collective-permute-start.4
  6.7 2.2 %weights.1 = (bf16[2,3,256,512]{3,2,1,0:T(8,128)(2,1)S(1)}, s32[8,1280]{1,0:T(8,128)S(1)}, s32[8,1280]{1,0:T(8,128)S(1)}, f32[8,1280]{1,0:T(8,128)S(1)}, f32[8,1...) custom-call(s32[2,3]{1,0:T(2,128)} %bitcast.6, ...), custom_call_target="tpu_custom_call" | custom-call | tf_op jit(solution)/shard_map/weights/pallas_call | solution.py:42
  8.9 0.0 collective-permute-done.1.diagonal.refs_5_.diagonal0
  8.9 0.4 %collective-permute-start.5 = (bf16[3,128,128]{2,1,0:T(8,128)(2,1)S(1)}, bf16[3,128,128]{2,1,0:T(8,128)(2,1)S(1)}, u32[]{:S(2)}, u32[]{:S(2)}) collective-permute-start(bf16[3,128,128]{2,1,0:T(8,128)(2,1)S(1)} %get-tuple-element.90), channel_id=1, source_target_pairs={{0,1},{1,0},{2,3},{3,2},{4,5},{5,4},{6,7},{7,6},{8,9},{9,8},{10,11... | collective-permute-start | bytes 294920 | tf_op jit(solution)/shard_map/ppermute | solution.py:486
  9.3 0.5 %collective-permute-done.across.refs_4_ = bf16[3,128,128]{2,1,0:T(8,128)(2,1)S(1)} collective-permute-done((bf16[3,128,128]{2,1,0:T(8,128)(2,1)S(1)}, bf16[3,128,128]{2,1,0:T(8,128)(2,1)S(1)}, u32[]{:S(2)}, u32[]{:S(2)}) %collective-permute-start) | collective-permute-done | bytes 98336 | tf_op jit(solution)/shard_map/ppermute | solution.py:486
  9.8 0.0 collective-permute-done.2.near.refs_6_.near0
  9.8 0.6 %rows_first.1 = (bf16[3,128,128]{2,1,0:T(8,128)(2,1)S(1)}, bf16[3,128,128]{2,1,0:T(8,128)(2,1)S(1)}, bf16[3,128,128]{2,1,0:T(8,128)(2,1)S(1)}, bf16[3,128,128]{2,1,0:T(8,128)(2,1)S(1)}) custom-call(bf16[2,3,256,512]{3,2,1,0:T(8,128)(2,1)S(1)} %get-tuple-element.77.rows_ref, bf16[3,128,128]{2,1,0:T(8,128)(2,1)S(1)} %collective-permute-done.across.refs_4_, ...), custom_call_target="tpu_custom_call" | custom-call | tf_op jit(solution)/shard_map/rows_first/pallas_call | solution.py:42
  10.4 2.2 %collective-permute-start.6 = (bf16[3,128,128]{2,1,0:T(8,128)(2,1)S(1)}, bf16[3,128,128]{2,1,0:T(8,128)(2,1)S(1)}, u32[]{:S(2)}, u32[]{:S(2)}) collective-permute-start(bf16[3,128,128]{2,1,0:T(8,128)(2,1)S(1)} %get-tuple-element.95), channel_id=1, source_target_pairs={{0,4},{1,5},{2,6},{3,7},{4,0},{5,1},{6,2},{7,3},{8,12},{9,13},{10,... | collective-permute-start | bytes 294920 | tf_op jit(solution)/shard_map/ppermute | solution.py:490
  12.7 0.0 collective-permute-start.7
  12.7 1.5 %columns.1 = (bf16[3,512,1280]{2,1,0:T(8,128)(2,1)S(1)}, bf16[32,128]{1,0:T(8,128)(2,1)S(1)}, bf16[32,128]{1,0:T(8,128)(2,1)S(1)}) custom-call(s32[2,3]{1,0:T(2,128)S(1)} %get-tuple-element.65.wind_held, s32[8,1280]{1,0:T(8,128)S(1)} %get-tuple-element.81.refs_0_, s32[8,1280]{1,0:T(8,128)S(1)} %get-tuple-element.82.refs_1_, ...), custom_call_target="tpu_custom_call" | custom-call | tf_op jit(solution)/shard_map/columns/pallas_call | solution.py:42
  14.2 0.6 %rows_later.1 = (bf16[3,128,128]{2,1,0:T(8,128)(2,1)S(1)}, bf16[3,192,256]{2,1,0:T(8,128)(2,1)S(1)}, bf16[224,128]{1,0:T(8,128)(2,1)S(1)}, bf16[224,128]{1,0:T(8...) custom-call(bf16[2,3,256,512]{3,2,1,0:T(8,128)(2,1)S(1)} %get-tuple-element.77.rows_ref, ...), custom_call_target="tpu_custom_call" | custom-call | tf_op jit(solution)/shard_map/rows_later/pallas_call | solution.py:42
  14.8 2.0 %collective-permute-start.11 = (bf16[224,128]{1,0:T(8,128)(2,1)S(1)}, bf16[224,128]{1,0:T(8,128)(2,1)S(1)}, u32[]{:S(2)}, u32[]{:S(2)}) collective-permute-start(bf16[224,128]{1,0:T(8,128)(2,1)S(1)} %get-tuple-element.103), channel_id=1, source_target_pairs={{0,4},{1,5},{2,6},{3,7},{4,0},{5,1},{6,2},{7,3},{8,12},{9,13},{10,... | collective-permute-start | bytes 172040 | tf_op jit(solution)/shard_map/ppermute | solution.py:490
  16.8 1.6 %collective-permute-start.9 = (bf16[240,128]{1,0:T(8,128)(2,1)S(1)}, bf16[240,128]{1,0:T(8,128)(2,1)S(1)}, u32[]{:S(2)}, u32[]{:S(2)}) collective-permute-start(bf16[240,128]{1,0:T(8,128)(2,1)S(1)} %get-tuple-element.100), channel_id=1, source_target_pairs={{0,4},{1,5},{2,6},{3,7},{4,0},{5,1},{6,2},{7,3},{8,12},{9,13},{10,... | collective-permute-start | bytes 184328 | tf_op jit(solution)/shard_map/ppermute | solution.py:490
  18.4 0.2 collective-permute-start.10
  18.6 0.4 %collective-permute-start.8 = (bf16[3,192,256]{2,1,0:T(8,128)(2,1)S(1)}, bf16[3,192,256]{2,1,0:T(8,128)(2,1)S(1)}, u32[]{:S(2)}, u32[]{:S(2)}) collective-permute-start(bf16[3,192,256]{2,1,0:T(8,128)(2,1)S(1)} %get-tuple-element.99), channel_id=1, source_target_pairs={{0,1},{1,0},{2,3},{3,2},{4,5},{5,4},{6,7},{7,6},{8,9},{9,8},{10,11... | collective-permute-start | bytes 884744 | tf_op jit(solution)/shard_map/ppermute | solution.py:486
  19.0 1.9 %phase.1 = (f32[128,1280]{1,0:T(8,128)S(1)}, bf16[3,512,1280]{2,1,0:T(8,128)(2,1)S(1)}) custom-call(s32[8,1280]{1,0:T(8,128)S(1)} %get-tuple-element.81.refs_0_, s32[8,1280]{1,0:T(8,128)S(1)} %get-tuple-element.82.refs_1_, f32[8,1280]{1,0:T(8,128)S(1)} %get-tuple-element.83.refs_2_, f32[8,1280]{1,0:T(8,128)S(1)} %get-tuple-element.84.refs_3_, ...), custom_call_target="tpu_custom_call" | custom-call | flops 10000000000 | bytes 9076736 | tf_op jit(solution)/shard_map/phase/pallas_call | solution.py:42
  20.9 0.0 collective-permute-done.12.sibling_came
  20.9 0.8 %far.1 = (bf16[32,1408]{1,0:T(8,128)(2,1)S(1)}, bf16[32,1408]{1,0:T(8,128)(2,1)S(1)}, bf16[64,128]{1,0:T(8,128)(2,1)S(1)}) custom-call(bf16[3,512,1280]{2,1,0:T(8,128)(2,1)S(1)} %get-tuple-element.85.refs_4_.mine_ref, bf16[3,512,1280]{2,1,0:T(8,128)(2,1)S(1)} %get-tuple-element.97.cols_ref, f32[128,1280]{1,0:T(8,128)S(1)} %get-tuple-element.98.phase, ...), custom_call_target="tpu_custom_call" | custom-call | flops 300000000 | bytes 9125888 | tf_op jit(solution)/shard_map/far/pallas_call | solution.py:42
  21.7 3.7 %collective-permute-start.14 = (bf16[32,1408]{1,0:T(8,128)(2,1)S(1)}, bf16[32,1408]{1,0:T(8,128)(2,1)S(1)}, u32[]{:S(2)}, u32[]{:S(2)}) collective-permute-start(bf16[32,1408]{1,0:T(8,128)(2,1)S(1)} %get-tuple-element.110), channel_id=1, source_target_pairs={{0,24},{4,28},{8,16},{12,20},{16,8},{20,12},{24,0},{28,4},{1,25},{... | collective-permute-start | bytes 270344 | tf_op jit(solution)/shard_map/ppermute | solution.py:595
  25.4 0.8 %rest.1 = (bf16[32,1280]{1,0:T(8,128)(2,1)S(1)}, bf16[32,1280]{1,0:T(8,128)(2,1)S(1)}) custom-call(bf16[3,512,1280]{2,1,0:T(8,128)(2,1)S(1)} %get-tuple-element.85.refs_4_.mine_ref, bf16[3,512,1280]{2,1,0:T(8,128)(2,1)S(1)} %get-tuple-element.97.cols_ref, f32[128,1280]{1,0:T(8,128)S(1)} %get-tuple-element.98.phase, ...), custom_call_target="tpu_custom_call" | custom-call | tf_op jit(solution)/shard_map/rest/pallas_call | solution.py:42
  26.2 0.8 %collective-permute-start.15 = (bf16[32,1280]{1,0:T(8,128)(2,1)S(1)}, bf16[32,1280]{1,0:T(8,128)(2,1)S(1)}, u32[]{:S(2)}, u32[]{:S(2)}) collective-permute-start(bf16[32,1280]{1,0:T(8,128)(2,1)S(1)} %get-tuple-element.119), channel_id=1, source_target_pairs={{0,16},{4,20},{8,24},{12,28},{16,0},{20,4},{24,8},{28,12},{1,17},{... | collective-permute-start | bytes 245768 | tf_op jit(solution)/shard_map/ppermute | solution.py:595
  27.0 2.0 %collective-permute-done.14.refs_1_.refs_3_ = bf16[32,1408]{1,0:T(8,128)(2,1)S(1)} collective-permute-done((bf16[32,1408]{1,0:T(8,128)(2,1)S(1)}, bf16[32,1408]{1,0:T(8,128)(2,1)S(1)}, u32[]{:S(2)}, u32[]{:S(2)}) %collective-permute-start.14) | collective-permute-done | bytes 90144 | tf_op jit(solution)/shard_map/ppermute | solution.py:595
  29.0 0.6 %optics.1 = (f32[32,1280]{1,0:T(8,128)S(1)}, bf16[256,512]{1,0:T(8,128)(2,1)S(1)}, bf16[128,64]{1,0:T(8,128)(2,1)S(1)}) custom-call(f32[32,1280]{1,0:T(8,128)S(1)} %get-tuple-element.111.amplitude, f32[128,128]{1,0:T(8,128)S(1)} %get-tuple-element.112.ones, f32[256,512]{1,0:T(8,128)S(1)} %get-tuple-element.113.columns, f32[128,64]{1,0:T(8,128)S(1)} %get-tuple-element.114.lines), custom_call_target="tpu_custom_call" | custom-call | tf_op jit(solution)/shard_map/optics/pallas_call | solution.py:42
  29.7 2.0 %collective-permute-done.13.refs_0_.refs_1_ = bf16[32,1408]{1,0:T(8,128)(2,1)S(1)} collective-permute-done((bf16[32,1408]{1,0:T(8,128)(2,1)S(1)}, bf16[32,1408]{1,0:T(8,128)(2,1)S(1)}, u32[]{:S(2)}, u32[]{:S(2)}) %collective-permute-start.13) | collective-permute-done | bytes 90144 | tf_op jit(solution)/shard_map/ppermute | solution.py:595
  31.7 1.1 %shift.1.refs_7_ = bf16[3,128,512]{2,1,0:T(8,128)(2,1)S(1)} custom-call(s32[2,3]{1,0:T(2,128)S(1)} %get-tuple-element.65.wind_held, bf16[3,128,512]{2,1,0:T(8,128)(2,1)S(1)} %get-tuple-element.124.own, bf16[3,128,128]{2,1,0:T(8,128)(2,1)S(1)} %collective-permute-done.2.near.refs_6_.near0, bf16[3,128,128]{2,1,0:T(8,128)(2,1)S(1)} %collective-permute-done.5.refs_2_.near1, ...), custom_call_target="tpu_custom_call" | custom-call | tf_op jit(solution)/shard_map/shift/pallas_call | solution.py:42
  32.8 0.5 %collective-permute-done.15.refs_2_ = bf16[32,1280]{1,0:T(8,128)(2,1)S(1)} collective-permute-done((bf16[32,1280]{1,0:T(8,128)(2,1)S(1)}, bf16[32,1280]{1,0:T(8,128)(2,1)S(1)}, u32[]{:S(2)}, u32[]{:S(2)}) %collective-permute-start.15) | collective-permute-done | bytes 81952 | tf_op jit(solution)/shard_map/ppermute | solution.py:595
  33.4 1.3 %imaging.1 = (f32[64,2560]{1,0:T(8,128)}, bf16[3,128,512]{2,1,0:T(8,128)(2,1)}) custom-call(bf16[32,1280]{1,0:T(8,128)(2,1)S(1)} %get-tuple-element.102.refs_0_, bf16[32,1408]{1,0:T(8,128)(2,1)S(1)} %collective-permute-done.13.refs_0_.refs_1_, bf16[32,1280]{1,0:T(8,128)(2,1)S(1)} %collective-permute-done.15.refs_2_, ...), custom_call_target="tpu_custom_call" | custom-call | flops 400000000 | bytes 2228224 | tf_op jit(solution)/shard_map/imaging/pallas_call | solution.py:42
  (11 shorter events, 0.0 us)
Async XLA Ops:
  1.7 7.2 %collective-permute-start.1 = (bf16[3,128,128]{2,1,0:T(8,128)(2,1)S(1)}, bf16[3,128,128]{2,1,0:T(8,128)(2,1)S(1)}, u32[]{:S(2)}, u32[]{:S(2)}) collective-permute-start(bf16[3,128,128]{2,1,0:T(8,128)(2,1)S(1)} %get-tuple-element.67), channel_id=1, source_target_pairs={{0,3},{1,2},{2,1},{3,0},{4,7},{5,6},{6,5},{7,4},{8,11},{9,10},{10,... | collective-permute-start | bytes 294920 | tf_op jit(solution)/shard_map/ppermute | solution.py:486
  4.2 5.7 %collective-permute-start = (bf16[3,128,128]{2,1,0:T(8,128)(2,1)S(1)}, bf16[3,128,128]{2,1,0:T(8,128)(2,1)S(1)}, u32[]{:S(2)}, u32[]{:S(2)}) collective-permute-start(bf16[3,128,128]{2,1,0:T(8,128)(2,1)S(1)} %get-tuple-element.66.keep.refs_7_), channel_id=1, source_target_pairs={{0,2},{1,3},{2,0},{3,1},{4,6},{5,7},{6,4},{7,5},{8,10},{9,11},{10,... | collective-permute-start | bytes 294920 | tf_op jit(solution)/shard_map/ppermute | solution.py:486
  4.8 5.0 %collective-permute-start.2 = (bf16[3,128,128]{2,1,0:T(8,128)(2,1)S(1)}, bf16[3,128,128]{2,1,0:T(8,128)(2,1)S(1)}, u32[]{:S(2)}, u32[]{:S(2)}) collective-permute-start(bf16[3,128,128]{2,1,0:T(8,128)(2,1)S(1)} %get-tuple-element.67), channel_id=1, source_target_pairs={{0,1},{1,0},{2,3},{3,2},{4,5},{5,4},{6,7},{7,6},{8,9},{9,8},{10,11... | collective-permute-start | bytes 294920 | tf_op jit(solution)/shard_map/ppermute | solution.py:486
  4.9 9.3 %collective-permute-start.3 = (bf16[3,128,128]{2,1,0:T(8,128)(2,1)S(1)}, bf16[3,128,128]{2,1,0:T(8,128)(2,1)S(1)}, u32[]{:S(2)}, u32[]{:S(2)}) collective-permute-start(bf16[3,128,128]{2,1,0:T(8,128)(2,1)S(1)} %get-tuple-element.87.refs_3_), channel_id=1, source_target_pairs={{0,2},{1,3},{2,0},{3,1},{4,6},{5,7},{6,4},{7,5},{8,10},{9,11},{10,... | collective-permute-start | bytes 294920 | tf_op jit(solution)/shard_map/ppermute | solution.py:486
  6.6 7.6 %collective-permute-start.4 = (bf16[3,128,128]{2,1,0:T(8,128)(2,1)S(1)}, bf16[3,128,128]{2,1,0:T(8,128)(2,1)S(1)}, u32[]{:S(2)}, u32[]{:S(2)}) collective-permute-start(bf16[3,128,128]{2,1,0:T(8,128)(2,1)S(1)} %get-tuple-element.90), channel_id=1, source_target_pairs={{0,3},{1,2},{2,1},{3,0},{4,7},{5,6},{6,5},{7,4},{8,11},{9,10},{10,... | collective-permute-start | bytes 294920 | tf_op jit(solution)/shard_map/ppermute | solution.py:486
  8.9 5.3 %collective-permute-start.5 = (bf16[3,128,128]{2,1,0:T(8,128)(2,1)S(1)}, bf16[3,128,128]{2,1,0:T(8,128)(2,1)S(1)}, u32[]{:S(2)}, u32[]{:S(2)}) collective-permute-start(bf16[3,128,128]{2,1,0:T(8,128)(2,1)S(1)} %get-tuple-element.90), channel_id=1, source_target_pairs={{0,1},{1,0},{2,3},{3,2},{4,5},{5,4},{6,7},{7,6},{8,9},{9,8},{10,11... | collective-permute-start | bytes 294920 | tf_op jit(solution)/shard_map/ppermute | solution.py:486
  10.4 7.9 %collective-permute-start.6 = (bf16[3,128,128]{2,1,0:T(8,128)(2,1)S(1)}, bf16[3,128,128]{2,1,0:T(8,128)(2,1)S(1)}, u32[]{:S(2)}, u32[]{:S(2)}) collective-permute-start(bf16[3,128,128]{2,1,0:T(8,128)(2,1)S(1)} %get-tuple-element.95), channel_id=1, source_target_pairs={{0,4},{1,5},{2,6},{3,7},{4,0},{5,1},{6,2},{7,3},{8,12},{9,13},{10,... | collective-permute-start | bytes 294920 | tf_op jit(solution)/shard_map/ppermute | solution.py:490
  12.7 5.9 %collective-permute-start.7 = (bf16[3,128,128]{2,1,0:T(8,128)(2,1)S(1)}, bf16[3,128,128]{2,1,0:T(8,128)(2,1)S(1)}, u32[]{:S(2)}, u32[]{:S(2)}) collective-permute-start(bf16[3,128,128]{2,1,0:T(8,128)(2,1)S(1)} %get-tuple-element.96), channel_id=1, source_target_pairs={{0,5},{1,4},{2,7},{3,6},{4,1},{5,0},{6,3},{7,2},{8,13},{9,12},{10,... | collective-permute-start | bytes 294920 | tf_op jit(solution)/shard_map/ppermute | solution.py:490
  14.8 6.1 %collective-permute-start.11 = (bf16[224,128]{1,0:T(8,128)(2,1)S(1)}, bf16[224,128]{1,0:T(8,128)(2,1)S(1)}, u32[]{:S(2)}, u32[]{:S(2)}) collective-permute-start(bf16[224,128]{1,0:T(8,128)(2,1)S(1)} %get-tuple-element.103), channel_id=1, source_target_pairs={{0,4},{1,5},{2,6},{3,7},{4,0},{5,1},{6,2},{7,3},{8,12},{9,13},{10,... | collective-permute-start | bytes 172040 | tf_op jit(solution)/shard_map/ppermute | solution.py:490
  16.8 4.1 %collective-permute-start.12 = (bf16[224,128]{1,0:T(8,128)(2,1)S(1)}, bf16[224,128]{1,0:T(8,128)(2,1)S(1)}, u32[]{:S(2)}, u32[]{:S(2)}) collective-permute-start(bf16[224,128]{1,0:T(8,128)(2,1)S(1)} %get-tuple-element.104), channel_id=1, source_target_pairs={{0,5},{1,4},{2,7},{3,6},{4,1},{5,0},{6,3},{7,2},{8,13},{9,12},{10,... | collective-permute-start | bytes 172040 | tf_op jit(solution)/shard_map/ppermute | solution.py:490
  16.8 8.6 %collective-permute-start.9 = (bf16[240,128]{1,0:T(8,128)(2,1)S(1)}, bf16[240,128]{1,0:T(8,128)(2,1)S(1)}, u32[]{:S(2)}, u32[]{:S(2)}) collective-permute-start(bf16[240,128]{1,0:T(8,128)(2,1)S(1)} %get-tuple-element.100), channel_id=1, source_target_pairs={{0,4},{1,5},{2,6},{3,7},{4,0},{5,1},{6,2},{7,3},{8,12},{9,13},{10,... | collective-permute-start | bytes 184328 | tf_op jit(solution)/shard_map/ppermute | solution.py:490
  18.4 7.0 %collective-permute-start.10 = (bf16[240,128]{1,0:T(8,128)(2,1)S(1)}, bf16[240,128]{1,0:T(8,128)(2,1)S(1)}, u32[]{:S(2)}, u32[]{:S(2)}) collective-permute-start(bf16[240,128]{1,0:T(8,128)(2,1)S(1)} %get-tuple-element.101), channel_id=1, source_target_pairs={{0,5},{1,4},{2,7},{3,6},{4,1},{5,0},{6,3},{7,2},{8,13},{9,12},{10,... | collective-permute-start | bytes 184328 | tf_op jit(solution)/shard_map/ppermute | solution.py:490
  18.6 2.3 %collective-permute-start.8 = (bf16[3,192,256]{2,1,0:T(8,128)(2,1)S(1)}, bf16[3,192,256]{2,1,0:T(8,128)(2,1)S(1)}, u32[]{:S(2)}, u32[]{:S(2)}) collective-permute-start(bf16[3,192,256]{2,1,0:T(8,128)(2,1)S(1)} %get-tuple-element.99), channel_id=1, source_target_pairs={{0,1},{1,0},{2,3},{3,2},{4,5},{5,4},{6,7},{7,6},{8,9},{9,8},{10,11... | collective-permute-start | bytes 884744 | tf_op jit(solution)/shard_map/ppermute | solution.py:486
  21.7 7.3 %collective-permute-start.14 = (bf16[32,1408]{1,0:T(8,128)(2,1)S(1)}, bf16[32,1408]{1,0:T(8,128)(2,1)S(1)}, u32[]{:S(2)}, u32[]{:S(2)}) collective-permute-start(bf16[32,1408]{1,0:T(8,128)(2,1)S(1)} %get-tuple-element.110), channel_id=1, source_target_pairs={{0,24},{4,28},{8,16},{12,20},{16,8},{20,12},{24,0},{28,4},{1,25},{... | collective-permute-start | bytes 270344 | tf_op jit(solution)/shard_map/ppermute | solution.py:595
  25.4 6.3 %collective-permute-start.13 = (bf16[32,1408]{1,0:T(8,128)(2,1)S(1)}, bf16[32,1408]{1,0:T(8,128)(2,1)S(1)}, u32[]{:S(2)}, u32[]{:S(2)}) collective-permute-start(bf16[32,1408]{1,0:T(8,128)(2,1)S(1)} %get-tuple-element.105), channel_id=1, source_target_pairs={{0,8},{4,12},{8,0},{12,4},{16,24},{20,28},{24,16},{28,20},{1,9},{5... | collective-permute-start | bytes 270344 | tf_op jit(solution)/shard_map/ppermute | solution.py:595
  26.2 7.2 %collective-permute-start.15 = (bf16[32,1280]{1,0:T(8,128)(2,1)S(1)}, bf16[32,1280]{1,0:T(8,128)(2,1)S(1)}, u32[]{:S(2)}, u32[]{:S(2)}) collective-permute-start(bf16[32,1280]{1,0:T(8,128)(2,1)S(1)} %get-tuple-element.119), channel_id=1, source_target_pairs={{0,16},{4,20},{8,24},{12,28},{16,0},{20,4},{24,8},{28,12},{1,17},{... | collective-permute-start | bytes 245768 | tf_op jit(solution)/shard_map/ppermute | solution.py:595

commit v14 on v13

--- a/solution.py
+++ b/solution.py
@@ -104,8 +104,9 @@
 
 def weights_kernel(geometry, wind_hbm, offsets_hbm, ratio_hbm, *refs):
     n_layer, rows_dev, screen_cols = geometry
-    sources, (rows_out, base_out, upper_out, low_out, high_out), refs = refs[:5], refs[5:10], refs[10:]
-    copies, (wind_copy, wind, offsets, ratio, sems) = refs[:5], refs[5:]
+    sources, (rows_out, mine_out, other_out), refs = refs[:5], refs[5:8], refs[8:]
+    copies, (wind_copy, wind, offsets, ratio, *tables, sems) = refs[:5], refs[5:]
+    pupil_cols = mine_out.shape[2]
     pairs = [*zip(sources, copies), (wind_hbm, wind_copy)]
     others = fetch(*[(source, copy, sems.at[3 + k]) for k, (source, copy) in enumerate(pairs)])
     loads = fetch(
@@ -149,11 +150,13 @@
         anchor = jnp.where(sub == level, start, anchor)
         num = jnp.where(sub == level, ratio[level, 0, direction], num)
         den = jnp.where(sub == level, ratio[level, 1, direction], den)
-    for at in range(0, base_out.shape[1], LANES):
+    for at in range(0, pupil_cols, LANES):
         pixel = lax.broadcasted_iota(jnp.int32, (8, LANES), 1) + at
         values = spans(pixel, anchor, num, den, screen_cols)
-        for out, value in zip((base_out, upper_out, low_out, high_out), values):
-            out[:, at : at + LANES] = value
+        for table, value in zip(tables, values):
+            table[:, at : at + LANES] = value
+    for out, block in ((mine_out, column), (other_out, jnp.bitwise_xor(column, 1))):
+        column_weights(*tables, block * out.shape[1], out)
     for load in others:
         load.wait()
 
@@ -189,15 +192,35 @@
         lax.fori_loop(0, pupil_cols // LANES, tile, 0)
 
 
-def columns_kernel(wind_held, *refs):
-    tables, blocks, (out, strip, sibling_strip, wind, sem) = refs[:4], refs[4:8], refs[8:]
+def strips_kernel(wind_held, across, diagonal, near, keep, strip, sibling_strip, wind, sem):
     load = fetch((wind_held, wind, sem))[0]
-    column_weights(*tables, lax.axis_index("layer") * out.shape[1], out)
-    across, diagonal, near, keep = blocks
+    layers, rows, _ = keep.shape
     core = lax.rem(lax.axis_index("dir"), 2)
+    odd = core == 1
+    lane = lax.broadcasted_iota(jnp.int32, (rows + 32, LANES), 1)
+
+    def wide(own, near, far, odd, level):
+        own, near, far = [block[level].astype(jnp.float32) for block in (own, near, far)]
+        before = jnp.where(odd, near[rows - 16 :], far[rows - 16 :])
+        return stack(before, own, jnp.where(odd, far[:16], near[:16]))
+
+    packed = jnp.zeros((rows + 32, LANES), jnp.float32)
+    for level in range(layers):
+        blocks = (keep, near, diagonal, odd), (near, keep, across, core == 0)
+        for at, block in zip((WIND_MAX * level, STRIP + WIND_MAX * level), blocks):
+            block = pltpu.roll(wide(*block, level), at + WIND_MAX * core, 1)
+            packed = jnp.where((lane >= at) & (lane < at + WIND_MAX), block, packed)
     load.wait()
-    strip[...] = outer_strip(wind, core == 1, keep, near, diagonal)
-    sibling_strip[...] = outer_strip(wind, core == 0, near, keep, across)
+    strips = jnp.zeros((rows, LANES), jnp.float32)
+    for level in range(layers):
+        shift = wind[0, level]
+        shift = jnp.where(shift < 0, shift + rows + 32, shift)
+        moved = pltpu.roll(packed, shift, 0)[16 : 16 + rows]
+        mine = lax.rem(lane[:rows], STRIP)
+        strips = jnp.where((mine >= WIND_MAX * level) & (mine < WIND_MAX * (level + 1)), moved, strips)
+    strips = strips.T.astype(jnp.bfloat16)
+    strip[...] = strips[:STRIP]
+    sibling_strip[...] = strips[STRIP : 2 * STRIP]
 
 
 def project_rows(rows_ref, keep, near, across, diagonal, level):
@@ -212,20 +235,6 @@
         part = project_rows(rows_ref, keep, near, across, diagonal, level)
         for k, out in enumerate((mine, other, sibling, sibling_other)):
             out[level] = part[k * half : (k + 1) * half]
-
-
-def outer_strip(wind, odd, own, near, far):
-    layers, rows, _ = own.shape
-    core = lax.rem(lax.axis_index("dir"), 2)
-    lane = lax.broadcasted_iota(jnp.int32, (rows, LANES), 1)
-    strip = jnp.zeros((rows, LANES), jnp.float32)
-    for level in range(layers):
-        edges = [stack(block[level, :16], block[level, rows - 16 :]) for block in (near, far)]
-        moved = shifted_rows(wind[0, level], odd, own[level], *edges)
-        at = WIND_MAX * level
-        moved = pltpu.roll(moved, at + WIND_MAX * core, 1)
-        strip = jnp.where((lane >= at) & (lane < at + WIND_MAX), moved, strip)
-    return strip.T[:STRIP].astype(jnp.bfloat16)
 
 
 def put_strip(out, at, strip):
@@ -271,17 +280,13 @@
     return dot(beside(*parts), cols)
 
 
-def phase_kernel(*refs):
-    tables, refs = refs[:4], refs[4:]
-    cols_ref, mine0, mine1, came, sibling_came, phase, cols_out = refs
-    first = jnp.bitwise_xor(lax.axis_index("layer"), 1) * cols_out.shape[1]
-    column_weights(*tables, first, cols_out)
+def phase_kernel(mine_ref, other_ref, mine0, mine1, came, sibling_came, phase):
     layers, _, width = mine0.shape
     parts, cuts = [], []
     for level in range(layers):
         parts += [mine0[level], mine1[level], came[level], sibling_came[level]]
-        cuts += [(cols_ref, level, 0, 2 * width)]
-        cuts += [(cols_out, level, 0, width), (cols_out, level, 2 * width, 3 * width)]
+        cuts += [(mine_ref, level, 0, 2 * width)]
+        cuts += [(other_ref, level, 0, width), (other_ref, level, 2 * width, 3 * width)]
     for at in range(0, phase.shape[1], 256):
         phase[:, at : at + 256] = project(parts, cuts, at)
 
@@ -512,23 +517,22 @@
     ones = np.kron(np.eye(LANES // SUB_PIX), np.ones((SUB_PIX, SUB_PIX))).astype(np.float32)
     optics_in = (amplitude, jnp.asarray(ones), *[jnp.asarray(table) for table in tables_of(rows)])
     copies = [shape(*array.shape, dtype=array.dtype) for array in (screens, *optics_in, wind)]
-    row_weights, *tables = call(
+    row_weights, cols, others, *loaded = call(
         functools.partial(weights_kernel, (n_layer, rows_dev, cols_dev * n_layer)),
-        [shape(2, layers, pupil_rows, 4 * rows_dev)]
-        + [shape(8, pupil_cols, dtype=dtype) for dtype in (jnp.int32, jnp.int32, f32, f32)]
-        + copies,
+        [shape(2, layers, pupil_rows, 4 * rows_dev)] + [shape(layers, cols_dev, pupil_cols)] * 2 + copies,
         (wind, offsets, ratio, screens, *optics_in),
         0,
         "weights",
         in_hbm=range(8),
-        scratch=[smem(array.shape, jnp.int32) for array in (wind, offsets, ratio)] + [sem((9,))],
-        brief=True,
-    )
-    tables, own, optics_in, wind = tables[:4], tables[4], tables[5:-1], tables[-1]
+        scratch=[smem(array.shape, jnp.int32) for array in (wind, offsets, ratio)]
+        + [pltpu.VMEM((8, pupil_cols), dtype) for dtype in (jnp.int32, jnp.int32, f32, f32)]
+        + [sem((9,))],
+        brief=True,
+    )
+    own, *optics_in, wind = loaded
     give1, own = lax.optimization_barrier((give1, own))
     near1 = swap(give1, 1)
-    tables = tuple(tables)
-    across0, diagonal0, row_weights, tables = lax.optimization_barrier((across0, diagonal0, row_weights, tables))
+    across0, diagonal0, row_weights, cols = lax.optimization_barrier((across0, diagonal0, row_weights, cols))
 
     projected = shape(layers, half, width)
     mine0, sibling0, other0, sibling_other0 = call(
@@ -542,13 +546,13 @@
     came0 = partner(other0)
     sibling_came0 = partner(sibling_other0, 1)
 
-    tables, mine0 = lax.optimization_barrier((tables, mine0))
-    cols, strip, sibling_strip = call(
-        columns_kernel,
-        [shape(layers, cols_dev, pupil_cols), shape(STRIP, rows_dev), shape(STRIP, rows_dev)],
-        (wind, *tables, across0, diagonal0, near0, keep0),
-        0,
-        "columns",
+    wind, mine0 = lax.optimization_barrier((wind, mine0))
+    strip, sibling_strip = call(
+        strips_kernel,
+        [shape(STRIP, rows_dev)] * 2,
+        (wind, across0, diagonal0, near0, keep0),
+        0,
+        "strips",
         scratch=wind_scratch,
         brief=True,
     )
@@ -567,10 +571,10 @@
     far1, sibling_far1 = partner(far1), partner(sibling_far1, 1)
     rest1, sibling_rest1 = partner(rest1), partner(sibling_rest1, 1)
     taken = swap(give, 1)
-    phase, others = call(
+    phase = call(
         phase_kernel,
-        (shape(half, pupil_cols, dtype=f32), shape(layers, cols_dev, pupil_cols)),
-        (*tables, cols, mine0, mine1, came0, sibling_came0),
+        shape(half, pupil_cols, dtype=f32),
+        (cols, others, mine0, mine1, came0, sibling_came0),
         10_000_000_000,
         "phase",
     )

time: 34.9 us -> 35.7 us (1.023)
  waiting for transfers between devices: 5.12 us -> 5.79 us
  Pallas kernels: 12.6 us -> 13 us
    ppermute x6, waiting for transfers between devices: 0.04 us -> 1.28 us  [partner(): lax.ppermute(value, ('layer', 'dir'), [(i, i ^ n_dir ^ bits) for i in ran...]
    ppermute x6, starting transfers between devices: 5.99 us -> 5.42 us  [partner(): lax.ppermute(value, ('layer', 'dir'), [(i, i ^ n_dir ^ bits) for i in ran...]
    ppermute x7, waiting for transfers between devices: 0.55 us -> 0.02 us  [swap(): return lax.ppermute(value, 'dir', [(i, i ^ bits) for i in range(n_dir)])]
    pallas_call x11, Pallas kernels: 12.6 us -> 13 us  [call(): pl.pallas_call(kernel, out_shape=out_shape, in_specs=in_specs, out_specs=...]
  transfers between devices with their start and end apart: 16 -> 16, of which waited for: 4 -> 6; matrix products, arithmetic and copies ran while one was open for 0% -> 0% of each run, Pallas kernels for 29% -> 30%
where the time goes in v14:
time: 35.7 us; the launch traced here: 35.5 us
  starting transfers between devices  15.9 us (45%)
  Pallas kernels  13 us (36%)
  waiting for transfers between devices  5.79 us (16%)
  between operations  0.74 us (2%)
    pallas_call x11, Pallas kernels, call(): pl.pallas_call(kernel, out_shape=out_shape, in_specs=in_specs, out_specs=...  13 us
    ppermute x7, starting transfers between devices, swap(): return lax.ppermute(value, 'dir', [(i, i ^ bits) for i in range(n_dir)])  5.98 us
    ppermute x6, starting transfers between devices, partner(): lax.ppermute(value, ('layer', 'dir'), [(i, i ^ n_dir ^ bits) for i in ran...  5.42 us
    ppermute x3, starting transfers between devices, per_device(): lax.ppermute(received[k], 'layer', [(i, i ^ 2 * k) for i in range(n_layer)])  4.51 us
    ppermute x3, waiting for transfers between devices, per_device(): lax.ppermute(received[k], 'layer', [(i, i ^ 2 * k) for i in range(n_layer)])  4.49 us
    ppermute x6, waiting for transfers between devices, partner(): lax.ppermute(value, ('layer', 'dir'), [(i, i ^ n_dir ^ bits) for i in ran...  1.28 us
  transfers between devices with their start and end apart: 16, of which 6 were waited for; matrix products, arithmetic and copies ran while one was open for 0% of the time, Pallas kernels for 30%

profile of v14, /device:TPU:0, one launch (start us, length us, event | category | flops | bytes accessed | tf_op | source)
XLA Modules:
  0.0 35.5 jit_solution(10877694357074307760)
XLA Ops:
  0.6 1.1 %split.1 = (bf16[3,128,128]{2,1,0:T(8,128)(2,1)S(1)}, bf16[3,128,128]{2,1,0:T(8,128)(2,1)S(1)}, bf16[3,128,128]{2,1,0:T(8,128)(2,1)S(1)}, bf16[3,128,128]{2,1,0:T(8,128)(2,1)S(1)}) custom-call(bf16[3,128,512]{2,1,0:T(8,128)(2,1)} %refs_0_.1), custom_call_target="tpu_custom_call" | custom-call | tf_op jit(solution)/shard_map/split/pallas_call | solution.py:42
  1.7 2.4 %collective-permute-start.1 = (bf16[3,128,128]{2,1,0:T(8,128)(2,1)S(1)}, bf16[3,128,128]{2,1,0:T(8,128)(2,1)S(1)}, u32[]{:S(2)}, u32[]{:S(2)}) collective-permute-start(bf16[3,128,128]{2,1,0:T(8,128)(2,1)S(1)} %get-tuple-element.55), channel_id=1, source_target_pairs={{0,3},{1,2},{2,1},{3,0},{4,7},{5,6},{6,5},{7,4},{8,11},{9,10},{10,... | collective-permute-start | bytes 294920 | tf_op jit(solution)/shard_map/ppermute | solution.py:491
  4.2 0.6 %collective-permute-start = (bf16[3,128,128]{2,1,0:T(8,128)(2,1)S(1)}, bf16[3,128,128]{2,1,0:T(8,128)(2,1)S(1)}, u32[]{:S(2)}, u32[]{:S(2)}) collective-permute-start(bf16[3,128,128]{2,1,0:T(8,128)(2,1)S(1)} %get-tuple-element.54.keep.refs_7_), channel_id=1, source_target_pairs={{0,2},{1,3},{2,0},{3,1},{4,6},{5,7},{6,4},{7,5},{8,10},{9,11},{10,... | collective-permute-start | bytes 294920 | tf_op jit(solution)/shard_map/ppermute | solution.py:491
  4.8 0.0 collective-permute-start.2
  4.9 1.7 %collective-permute-start.3 = (bf16[3,128,128]{2,1,0:T(8,128)(2,1)S(1)}, bf16[3,128,128]{2,1,0:T(8,128)(2,1)S(1)}, u32[]{:S(2)}, u32[]{:S(2)}) collective-permute-start(bf16[3,128,128]{2,1,0:T(8,128)(2,1)S(1)} %get-tuple-element.66.refs_3_), channel_id=1, source_target_pairs={{0,2},{1,3},{2,0},{3,1},{4,6},{5,7},{6,4},{7,5},{8,10},{9,11},{10,... | collective-permute-start | bytes 294920 | tf_op jit(solution)/shard_map/ppermute | solution.py:491
  6.6 0.1 collective-permute-start.4
  6.7 4.6 %weights.1 = (bf16[2,3,256,512]{3,2,1,0:T(8,128)(2,1)S(1)}, bf16[3,512,1280]{2,1,0:T(8,128)(2,1)S(1)}, bf16[3,512,1280]{2,1,0:T(8,128)(2,1)S(1)}, bf16[3,128,512...) custom-call(s32[2,3]{1,0:T(2,128)} %bitcast.6, ...), custom_call_target="tpu_custom_call" | custom-call | tf_op jit(solution)/shard_map/weights/pallas_call | solution.py:42
  11.3 0.4 %collective-permute-start.5 = (bf16[3,128,128]{2,1,0:T(8,128)(2,1)S(1)}, bf16[3,128,128]{2,1,0:T(8,128)(2,1)S(1)}, u32[]{:S(2)}, u32[]{:S(2)}) collective-permute-start(bf16[3,128,128]{2,1,0:T(8,128)(2,1)S(1)} %get-tuple-element.69), channel_id=1, source_target_pairs={{0,1},{1,0},{2,3},{3,2},{4,5},{5,4},{6,7},{7,6},{8,9},{9,8},{10,11... | collective-permute-start | bytes 294920 | tf_op jit(solution)/shard_map/ppermute | solution.py:491
  11.7 0.6 %rows_first.1 = (bf16[3,128,128]{2,1,0:T(8,128)(2,1)S(1)}, bf16[3,128,128]{2,1,0:T(8,128)(2,1)S(1)}, bf16[3,128,128]{2,1,0:T(8,128)(2,1)S(1)}, bf16[3,128,128]{2,1,0:T(8,128)(2,1)S(1)}) custom-call(bf16[2,3,256,512]{3,2,1,0:T(8,128)(2,1)S(1)} %get-tuple-element.61.rows_ref, bf16[3,128,128]{2,1,0:T(8,128)(2,1)S(1)} %collective-permute-done.across.refs_4_, ...), custom_call_target="tpu_custom_call" | custom-call | tf_op jit(solution)/shard_map/rows_first/pallas_call | solution.py:42
  12.3 1.8 %collective-permute-start.6 = (bf16[3,128,128]{2,1,0:T(8,128)(2,1)S(1)}, bf16[3,128,128]{2,1,0:T(8,128)(2,1)S(1)}, u32[]{:S(2)}, u32[]{:S(2)}) collective-permute-start(bf16[3,128,128]{2,1,0:T(8,128)(2,1)S(1)} %get-tuple-element.75), channel_id=1, source_target_pairs={{0,4},{1,5},{2,6},{3,7},{4,0},{5,1},{6,2},{7,3},{8,12},{9,13},{10,... | collective-permute-start | bytes 294920 | tf_op jit(solution)/shard_map/ppermute | solution.py:495
  14.1 0.0 collective-permute-start.7
  14.1 0.7 %strips.1 = (bf16[32,128]{1,0:T(8,128)(2,1)S(1)}, bf16[32,128]{1,0:T(8,128)(2,1)S(1)}) custom-call(s32[2,3]{1,0:T(2,128)S(1)} %get-tuple-element.71.wind_held, bf16[3,128,128]{2,1,0:T(8,128)(2,1)S(1)} %collective-permute-done.across.refs_4_, bf16[3,128,128]{2,1,0:T(8,128)(2,1)S(1)} %collective-permute-done.1.diagonal.refs_5_.diagonal0, ...), custom_call_target="tpu_custom_call" | custom-call | tf_op jit(solution)/shard_map/strips/pallas_call | solution.py:42
  14.9 0.6 %rows_later.1 = (bf16[3,128,128]{2,1,0:T(8,128)(2,1)S(1)}, bf16[3,192,256]{2,1,0:T(8,128)(2,1)S(1)}, bf16[224,128]{1,0:T(8,128)(2,1)S(1)}, bf16[224,128]{1,0:T(8...) custom-call(bf16[2,3,256,512]{3,2,1,0:T(8,128)(2,1)S(1)} %get-tuple-element.61.rows_ref, ...), custom_call_target="tpu_custom_call" | custom-call | tf_op jit(solution)/shard_map/rows_later/pallas_call | solution.py:42
  15.5 1.4 %collective-permute-start.11 = (bf16[224,128]{1,0:T(8,128)(2,1)S(1)}, bf16[224,128]{1,0:T(8,128)(2,1)S(1)}, u32[]{:S(2)}, u32[]{:S(2)}) collective-permute-start(bf16[224,128]{1,0:T(8,128)(2,1)S(1)} %get-tuple-element.81), channel_id=1, source_target_pairs={{0,4},{1,5},{2,6},{3,7},{4,0},{5,1},{6,2},{7,3},{8,12},{9,13},{10,... | collective-permute-start | bytes 172040 | tf_op jit(solution)/shard_map/ppermute | solution.py:495
  16.9 0.4 %collective-permute-start.12 = (bf16[224,128]{1,0:T(8,128)(2,1)S(1)}, bf16[224,128]{1,0:T(8,128)(2,1)S(1)}, u32[]{:S(2)}, u32[]{:S(2)}) collective-permute-start(bf16[224,128]{1,0:T(8,128)(2,1)S(1)} %get-tuple-element.82), channel_id=1, source_target_pairs={{0,5},{1,4},{2,7},{3,6},{4,1},{5,0},{6,3},{7,2},{8,13},{9,12},{10,... | collective-permute-start | bytes 172040 | tf_op jit(solution)/shard_map/ppermute | solution.py:495
  17.4 1.7 %collective-permute-start.9 = (bf16[240,128]{1,0:T(8,128)(2,1)S(1)}, bf16[240,128]{1,0:T(8,128)(2,1)S(1)}, u32[]{:S(2)}, u32[]{:S(2)}) collective-permute-start(bf16[240,128]{1,0:T(8,128)(2,1)S(1)} %get-tuple-element.78), channel_id=1, source_target_pairs={{0,4},{1,5},{2,6},{3,7},{4,0},{5,1},{6,2},{7,3},{8,12},{9,13},{10,... | collective-permute-start | bytes 184328 | tf_op jit(solution)/shard_map/ppermute | solution.py:495
  19.0 0.0 collective-permute-start.10
  19.1 0.2 collective-permute-done.7.sibling_came
  19.2 0.7 %collective-permute-start.8 = (bf16[3,192,256]{2,1,0:T(8,128)(2,1)S(1)}, bf16[3,192,256]{2,1,0:T(8,128)(2,1)S(1)}, u32[]{:S(2)}, u32[]{:S(2)}) collective-permute-start(bf16[3,192,256]{2,1,0:T(8,128)(2,1)S(1)} %get-tuple-element.77), channel_id=1, source_target_pairs={{0,1},{1,0},{2,3},{3,2},{4,5},{5,4},{6,7},{7,6},{8,9},{9,8},{10,11... | collective-permute-start | bytes 884744 | tf_op jit(solution)/shard_map/ppermute | solution.py:491
  19.9 0.7 %phase.1 = f32[128,1280]{1,0:T(8,128)S(1)} custom-call(bf16[3,512,1280]{2,1,0:T(8,128)(2,1)S(1)} %get-tuple-element.58.mine_ref, bf16[3,512,1280]{2,1,0:T(8,128)(2,1)S(1)} %get-tuple-element.59.other_ref.cols_ref, bf16[3,128,128]{2,1,0:T(8,128)(2,1)S(1)} %get-tuple-element.65.mine0, bf16[3,128,128]{2,1,0:T(8,128)(2,1)S(1)} %get-tuple-element.74.mine1, ...), custom_call_target="tpu_custom_call" | custom-call | flops 10000000000 | bytes 8912896 | tf_op jit(solution)/shard_map/phase/pallas_call | solution.py:42
  20.6 0.1 collective-permute-done.11.came
  20.7 1.0 %collective-permute-done.12.sibling_came = bf16[224,128]{1,0:T(8,128)(2,1)S(1)} collective-permute-done((bf16[224,128]{1,0:T(8,128)(2,1)S(1)}, bf16[224,128]{1,0:T(8,128)(2,1)S(1)}, u32[]{:S(2)}, u32[]{:S(2)}) %collective-permute-start.12) | collective-permute-done | bytes 57376 | tf_op jit(solution)/shard_map/ppermute | solution.py:495
  21.7 0.8 %far.1 = (bf16[32,1408]{1,0:T(8,128)(2,1)S(1)}, bf16[32,1408]{1,0:T(8,128)(2,1)S(1)}, bf16[64,128]{1,0:T(8,128)(2,1)S(1)}) custom-call(bf16[3,512,1280]{2,1,0:T(8,128)(2,1)S(1)} %get-tuple-element.58.mine_ref, bf16[3,512,1280]{2,1,0:T(8,128)(2,1)S(1)} %get-tuple-element.59.other_ref.cols_ref, f32[128,1280]{1,0:T(8,128)S(1)} %phase.1, ...), custom_call_target="tpu_custom_call" | custom-call | flops 300000000 | bytes 9125888 | tf_op jit(solution)/shard_map/far/pallas_call | solution.py:42
  22.5 3.6 %collective-permute-start.14 = (bf16[32,1408]{1,0:T(8,128)(2,1)S(1)}, bf16[32,1408]{1,0:T(8,128)(2,1)S(1)}, u32[]{:S(2)}, u32[]{:S(2)}) collective-permute-start(bf16[32,1408]{1,0:T(8,128)(2,1)S(1)} %get-tuple-element.88), channel_id=1, source_target_pairs={{0,24},{4,28},{8,16},{12,20},{16,8},{20,12},{24,0},{28,4},{1,25},{... | collective-permute-start | bytes 270344 | tf_op jit(solution)/shard_map/ppermute | solution.py:599
  26.2 0.8 %rest.1 = (bf16[32,1280]{1,0:T(8,128)(2,1)S(1)}, bf16[32,1280]{1,0:T(8,128)(2,1)S(1)}) custom-call(bf16[3,512,1280]{2,1,0:T(8,128)(2,1)S(1)} %get-tuple-element.58.mine_ref, bf16[3,512,1280]{2,1,0:T(8,128)(2,1)S(1)} %get-tuple-element.59.other_ref.cols_ref, f32[128,1280]{1,0:T(8,128)S(1)} %phase.1, bf16[3,192,256]{2,1,0:T(8,128)(2,1)S(1)} %collective-permute-done.8.taken, ...), custom_call_target="tpu_custom_call" | custom-call | tf_op jit(solution)/shard_map/rest/pallas_call | solution.py:42
  27.0 0.9 %collective-permute-start.15 = (bf16[32,1280]{1,0:T(8,128)(2,1)S(1)}, bf16[32,1280]{1,0:T(8,128)(2,1)S(1)}, u32[]{:S(2)}, u32[]{:S(2)}) collective-permute-start(bf16[32,1280]{1,0:T(8,128)(2,1)S(1)} %get-tuple-element.97), channel_id=1, source_target_pairs={{0,16},{4,20},{8,24},{12,28},{16,0},{20,4},{24,8},{28,12},{1,17},{... | collective-permute-start | bytes 245768 | tf_op jit(solution)/shard_map/ppermute | solution.py:599
  27.9 2.0 %collective-permute-done.14.refs_1_.refs_3_ = bf16[32,1408]{1,0:T(8,128)(2,1)S(1)} collective-permute-done((bf16[32,1408]{1,0:T(8,128)(2,1)S(1)}, bf16[32,1408]{1,0:T(8,128)(2,1)S(1)}, u32[]{:S(2)}, u32[]{:S(2)}) %collective-permute-start.14) | collective-permute-done | bytes 90144 | tf_op jit(solution)/shard_map/ppermute | solution.py:599
  29.9 0.6 %optics.1 = (f32[32,1280]{1,0:T(8,128)S(1)}, bf16[256,512]{1,0:T(8,128)(2,1)S(1)}, bf16[128,64]{1,0:T(8,128)(2,1)S(1)}) custom-call(f32[32,1280]{1,0:T(8,128)S(1)} %get-tuple-element.89.amplitude, f32[128,128]{1,0:T(8,128)S(1)} %get-tuple-element.90.ones, f32[256,512]{1,0:T(8,128)S(1)} %get-tuple-element.91.columns, f32[128,64]{1,0:T(8,128)S(1)} %get-tuple-element.92.lines), custom_call_target="tpu_custom_call" | custom-call | tf_op jit(solution)/shard_map/optics/pallas_call | solution.py:42
  30.5 1.9 %collective-permute-done.13.refs_0_.refs_1_ = bf16[32,1408]{1,0:T(8,128)(2,1)S(1)} collective-permute-done((bf16[32,1408]{1,0:T(8,128)(2,1)S(1)}, bf16[32,1408]{1,0:T(8,128)(2,1)S(1)}, u32[]{:S(2)}, u32[]{:S(2)}) %collective-permute-start.13) | collective-permute-done | bytes 90144 | tf_op jit(solution)/shard_map/ppermute | solution.py:599
  32.4 1.1 %shift.1.refs_7_ = bf16[3,128,512]{2,1,0:T(8,128)(2,1)S(1)} custom-call(s32[2,3]{1,0:T(2,128)S(1)} %get-tuple-element.71.wind_held, bf16[3,128,512]{2,1,0:T(8,128)(2,1)S(1)} %get-tuple-element.102.own, bf16[3,128,128]{2,1,0:T(8,128)(2,1)S(1)} %collective-permute-done.2.near.refs_6_.near0, bf16[3,128,128]{2,1,0:T(8,128)(2,1)S(1)} %collective-permute-done.5.refs_2_.near1, ...), custom_call_target="tpu_custom_call" | custom-call | tf_op jit(solution)/shard_map/shift/pallas_call | solution.py:42
  33.6 0.6 %collective-permute-done.15.refs_2_ = bf16[32,1280]{1,0:T(8,128)(2,1)S(1)} collective-permute-done((bf16[32,1280]{1,0:T(8,128)(2,1)S(1)}, bf16[32,1280]{1,0:T(8,128)(2,1)S(1)}, u32[]{:S(2)}, u32[]{:S(2)}) %collective-permute-start.15) | collective-permute-done | bytes 81952 | tf_op jit(solution)/shard_map/ppermute | solution.py:599
  34.2 1.3 %imaging.1 = (f32[64,2560]{1,0:T(8,128)}, bf16[3,128,512]{2,1,0:T(8,128)(2,1)}) custom-call(bf16[32,1280]{1,0:T(8,128)(2,1)S(1)} %get-tuple-element.80.refs_0_, bf16[32,1408]{1,0:T(8,128)(2,1)S(1)} %collective-permute-done.13.refs_0_.refs_1_, bf16[32,1280]{1,0:T(8,128)(2,1)S(1)} %collective-permute-done.15.refs_2_, ...), custom_call_target="tpu_custom_call" | custom-call | flops 400000000 | bytes 2228224 | tf_op jit(solution)/shard_map/imaging/pallas_call | solution.py:42
  (11 shorter events, 0.0 us)
Async XLA Ops:
  1.7 9.6 %collective-permute-start.1 = (bf16[3,128,128]{2,1,0:T(8,128)(2,1)S(1)}, bf16[3,128,128]{2,1,0:T(8,128)(2,1)S(1)}, u32[]{:S(2)}, u32[]{:S(2)}) collective-permute-start(bf16[3,128,128]{2,1,0:T(8,128)(2,1)S(1)} %get-tuple-element.55), channel_id=1, source_target_pairs={{0,3},{1,2},{2,1},{3,0},{4,7},{5,6},{6,5},{7,4},{8,11},{9,10},{10,... | collective-permute-start | bytes 294920 | tf_op jit(solution)/shard_map/ppermute | solution.py:491
  4.2 7.5 %collective-permute-start = (bf16[3,128,128]{2,1,0:T(8,128)(2,1)S(1)}, bf16[3,128,128]{2,1,0:T(8,128)(2,1)S(1)}, u32[]{:S(2)}, u32[]{:S(2)}) collective-permute-start(bf16[3,128,128]{2,1,0:T(8,128)(2,1)S(1)} %get-tuple-element.54.keep.refs_7_), channel_id=1, source_target_pairs={{0,2},{1,3},{2,0},{3,1},{4,6},{5,7},{6,4},{7,5},{8,10},{9,11},{10,... | collective-permute-start | bytes 294920 | tf_op jit(solution)/shard_map/ppermute | solution.py:491
  4.8 6.9 %collective-permute-start.2 = (bf16[3,128,128]{2,1,0:T(8,128)(2,1)S(1)}, bf16[3,128,128]{2,1,0:T(8,128)(2,1)S(1)}, u32[]{:S(2)}, u32[]{:S(2)}) collective-permute-start(bf16[3,128,128]{2,1,0:T(8,128)(2,1)S(1)} %get-tuple-element.55), channel_id=1, source_target_pairs={{0,1},{1,0},{2,3},{3,2},{4,5},{5,4},{6,7},{7,6},{8,9},{9,8},{10,11... | collective-permute-start | bytes 294920 | tf_op jit(solution)/shard_map/ppermute | solution.py:491
  4.9 10.0 %collective-permute-start.3 = (bf16[3,128,128]{2,1,0:T(8,128)(2,1)S(1)}, bf16[3,128,128]{2,1,0:T(8,128)(2,1)S(1)}, u32[]{:S(2)}, u32[]{:S(2)}) collective-permute-start(bf16[3,128,128]{2,1,0:T(8,128)(2,1)S(1)} %get-tuple-element.66.refs_3_), channel_id=1, source_target_pairs={{0,2},{1,3},{2,0},{3,1},{4,6},{5,7},{6,4},{7,5},{8,10},{9,11},{10,... | collective-permute-start | bytes 294920 | tf_op jit(solution)/shard_map/ppermute | solution.py:491
  6.6 8.3 %collective-permute-start.4 = (bf16[3,128,128]{2,1,0:T(8,128)(2,1)S(1)}, bf16[3,128,128]{2,1,0:T(8,128)(2,1)S(1)}, u32[]{:S(2)}, u32[]{:S(2)}) collective-permute-start(bf16[3,128,128]{2,1,0:T(8,128)(2,1)S(1)} %get-tuple-element.69), channel_id=1, source_target_pairs={{0,3},{1,2},{2,1},{3,0},{4,7},{5,6},{6,5},{7,4},{8,11},{9,10},{10,... | collective-permute-start | bytes 294920 | tf_op jit(solution)/shard_map/ppermute | solution.py:491
  11.3 3.6 %collective-permute-start.5 = (bf16[3,128,128]{2,1,0:T(8,128)(2,1)S(1)}, bf16[3,128,128]{2,1,0:T(8,128)(2,1)S(1)}, u32[]{:S(2)}, u32[]{:S(2)}) collective-permute-start(bf16[3,128,128]{2,1,0:T(8,128)(2,1)S(1)} %get-tuple-element.69), channel_id=1, source_target_pairs={{0,1},{1,0},{2,3},{3,2},{4,5},{5,4},{6,7},{7,6},{8,9},{9,8},{10,11... | collective-permute-start | bytes 294920 | tf_op jit(solution)/shard_map/ppermute | solution.py:491
  12.3 6.7 %collective-permute-start.6 = (bf16[3,128,128]{2,1,0:T(8,128)(2,1)S(1)}, bf16[3,128,128]{2,1,0:T(8,128)(2,1)S(1)}, u32[]{:S(2)}, u32[]{:S(2)}) collective-permute-start(bf16[3,128,128]{2,1,0:T(8,128)(2,1)S(1)} %get-tuple-element.75), channel_id=1, source_target_pairs={{0,4},{1,5},{2,6},{3,7},{4,0},{5,1},{6,2},{7,3},{8,12},{9,13},{10,... | collective-permute-start | bytes 294920 | tf_op jit(solution)/shard_map/ppermute | solution.py:495
  14.1 5.1 %collective-permute-start.7 = (bf16[3,128,128]{2,1,0:T(8,128)(2,1)S(1)}, bf16[3,128,128]{2,1,0:T(8,128)(2,1)S(1)}, u32[]{:S(2)}, u32[]{:S(2)}) collective-permute-start(bf16[3,128,128]{2,1,0:T(8,128)(2,1)S(1)} %get-tuple-element.76), channel_id=1, source_target_pairs={{0,5},{1,4},{2,7},{3,6},{4,1},{5,0},{6,3},{7,2},{8,13},{9,12},{10,... | collective-permute-start | bytes 294920 | tf_op jit(solution)/shard_map/ppermute | solution.py:495
  15.5 5.2 %collective-permute-start.11 = (bf16[224,128]{1,0:T(8,128)(2,1)S(1)}, bf16[224,128]{1,0:T(8,128)(2,1)S(1)}, u32[]{:S(2)}, u32[]{:S(2)}) collective-permute-start(bf16[224,128]{1,0:T(8,128)(2,1)S(1)} %get-tuple-element.81), channel_id=1, source_target_pairs={{0,4},{1,5},{2,6},{3,7},{4,0},{5,1},{6,2},{7,3},{8,12},{9,13},{10,... | collective-permute-start | bytes 172040 | tf_op jit(solution)/shard_map/ppermute | solution.py:495
  16.9 4.8 %collective-permute-start.12 = (bf16[224,128]{1,0:T(8,128)(2,1)S(1)}, bf16[224,128]{1,0:T(8,128)(2,1)S(1)}, u32[]{:S(2)}, u32[]{:S(2)}) collective-permute-start(bf16[224,128]{1,0:T(8,128)(2,1)S(1)} %get-tuple-element.82), channel_id=1, source_target_pairs={{0,5},{1,4},{2,7},{3,6},{4,1},{5,0},{6,3},{7,2},{8,13},{9,12},{10,... | collective-permute-start | bytes 172040 | tf_op jit(solution)/shard_map/ppermute | solution.py:495
  17.4 8.8 %collective-permute-start.9 = (bf16[240,128]{1,0:T(8,128)(2,1)S(1)}, bf16[240,128]{1,0:T(8,128)(2,1)S(1)}, u32[]{:S(2)}, u32[]{:S(2)}) collective-permute-start(bf16[240,128]{1,0:T(8,128)(2,1)S(1)} %get-tuple-element.78), channel_id=1, source_target_pairs={{0,4},{1,5},{2,6},{3,7},{4,0},{5,1},{6,2},{7,3},{8,12},{9,13},{10,... | collective-permute-start | bytes 184328 | tf_op jit(solution)/shard_map/ppermute | solution.py:495
  19.0 7.1 %collective-permute-start.10 = (bf16[240,128]{1,0:T(8,128)(2,1)S(1)}, bf16[240,128]{1,0:T(8,128)(2,1)S(1)}, u32[]{:S(2)}, u32[]{:S(2)}) collective-permute-start(bf16[240,128]{1,0:T(8,128)(2,1)S(1)} %get-tuple-element.79), channel_id=1, source_target_pairs={{0,5},{1,4},{2,7},{3,6},{4,1},{5,0},{6,3},{7,2},{8,13},{9,12},{10,... | collective-permute-start | bytes 184328 | tf_op jit(solution)/shard_map/ppermute | solution.py:495
  19.2 2.5 %collective-permute-start.8 = (bf16[3,192,256]{2,1,0:T(8,128)(2,1)S(1)}, bf16[3,192,256]{2,1,0:T(8,128)(2,1)S(1)}, u32[]{:S(2)}, u32[]{:S(2)}) collective-permute-start(bf16[3,192,256]{2,1,0:T(8,128)(2,1)S(1)} %get-tuple-element.77), channel_id=1, source_target_pairs={{0,1},{1,0},{2,3},{3,2},{4,5},{5,4},{6,7},{7,6},{8,9},{9,8},{10,11... | collective-permute-start | bytes 884744 | tf_op jit(solution)/shard_map/ppermute | solution.py:491
  22.5 7.4 %collective-permute-start.14 = (bf16[32,1408]{1,0:T(8,128)(2,1)S(1)}, bf16[32,1408]{1,0:T(8,128)(2,1)S(1)}, u32[]{:S(2)}, u32[]{:S(2)}) collective-permute-start(bf16[32,1408]{1,0:T(8,128)(2,1)S(1)} %get-tuple-element.88), channel_id=1, source_target_pairs={{0,24},{4,28},{8,16},{12,20},{16,8},{20,12},{24,0},{28,4},{1,25},{... | collective-permute-start | bytes 270344 | tf_op jit(solution)/shard_map/ppermute | solution.py:599
  26.2 6.3 %collective-permute-start.13 = (bf16[32,1408]{1,0:T(8,128)(2,1)S(1)}, bf16[32,1408]{1,0:T(8,128)(2,1)S(1)}, u32[]{:S(2)}, u32[]{:S(2)}) collective-permute-start(bf16[32,1408]{1,0:T(8,128)(2,1)S(1)} %get-tuple-element.83), channel_id=1, source_target_pairs={{0,8},{4,12},{8,0},{12,4},{16,24},{20,28},{24,16},{28,20},{1,9},{5... | collective-permute-start | bytes 270344 | tf_op jit(solution)/shard_map/ppermute | solution.py:599
  27.0 7.2 %collective-permute-start.15 = (bf16[32,1280]{1,0:T(8,128)(2,1)S(1)}, bf16[32,1280]{1,0:T(8,128)(2,1)S(1)}, u32[]{:S(2)}, u32[]{:S(2)}) collective-permute-start(bf16[32,1280]{1,0:T(8,128)(2,1)S(1)} %get-tuple-element.97), channel_id=1, source_target_pairs={{0,16},{4,20},{8,24},{12,28},{16,0},{20,4},{24,8},{28,12},{1,17},{... | collective-permute-start | bytes 245768 | tf_op jit(solution)/shard_map/ppermute | solution.py:599

commit v15 on v14

--- a/solution.py
+++ b/solution.py
@@ -104,9 +104,9 @@
 
 def weights_kernel(geometry, wind_hbm, offsets_hbm, ratio_hbm, *refs):
     n_layer, rows_dev, screen_cols = geometry
-    sources, (rows_out, mine_out, other_out), refs = refs[:5], refs[5:8], refs[8:]
-    copies, (wind_copy, wind, offsets, ratio, *tables, sems) = refs[:5], refs[5:]
-    pupil_cols = mine_out.shape[2]
+    sources, (rows_out, cols_out, *tables), refs = refs[:5], refs[5:11], refs[11:]
+    copies, (wind_copy, wind, offsets, ratio, sems) = refs[:5], refs[5:]
+    pupil_cols = cols_out.shape[2]
     pairs = [*zip(sources, copies), (wind_hbm, wind_copy)]
     others = fetch(*[(source, copy, sems.at[3 + k]) for k, (source, copy) in enumerate(pairs)])
     loads = fetch(
@@ -155,8 +155,7 @@
         values = spans(pixel, anchor, num, den, screen_cols)
         for table, value in zip(tables, values):
             table[:, at : at + LANES] = value
-    for out, block in ((mine_out, column), (other_out, jnp.bitwise_xor(column, 1))):
-        column_weights(*tables, block * out.shape[1], out)
+    column_weights(*tables, column * cols_out.shape[1], cols_out)
     for load in others:
         load.wait()
 
@@ -192,8 +191,10 @@
         lax.fori_loop(0, pupil_cols // LANES, tile, 0)
 
 
-def strips_kernel(wind_held, across, diagonal, near, keep, strip, sibling_strip, wind, sem):
+def strips_kernel(wind_held, *refs):
+    tables, (across, diagonal, near, keep, cols_out, strip, sibling_strip, wind, sem) = refs[:4], refs[4:]
     load = fetch((wind_held, wind, sem))[0]
+    column_weights(*tables, jnp.bitwise_xor(lax.axis_index("layer"), 1) * cols_out.shape[1], cols_out)
     layers, rows, _ = keep.shape
     core = lax.rem(lax.axis_index("dir"), 2)
     odd = core == 1
@@ -517,19 +518,20 @@
     ones = np.kron(np.eye(LANES // SUB_PIX), np.ones((SUB_PIX, SUB_PIX))).astype(np.float32)
     optics_in = (amplitude, jnp.asarray(ones), *[jnp.asarray(table) for table in tables_of(rows)])
     copies = [shape(*array.shape, dtype=array.dtype) for array in (screens, *optics_in, wind)]
-    row_weights, cols, others, *loaded = call(
+    row_weights, cols, *loaded = call(
         functools.partial(weights_kernel, (n_layer, rows_dev, cols_dev * n_layer)),
-        [shape(2, layers, pupil_rows, 4 * rows_dev)] + [shape(layers, cols_dev, pupil_cols)] * 2 + copies,
+        [shape(2, layers, pupil_rows, 4 * rows_dev), shape(layers, cols_dev, pupil_cols)]
+        + [shape(8, pupil_cols, dtype=dtype) for dtype in (jnp.int32, jnp.int32, f32, f32)]
+        + copies,
         (wind, offsets, ratio, screens, *optics_in),
         0,
         "weights",
         in_hbm=range(8),
         scratch=[smem(array.shape, jnp.int32) for array in (wind, offsets, ratio)]
-        + [pltpu.VMEM((8, pupil_cols), dtype) for dtype in (jnp.int32, jnp.int32, f32, f32)]
         + [sem((9,))],
         brief=True,
     )
-    own, *optics_in, wind = loaded
+    tables, (own, *optics_in, wind) = loaded[:4], loaded[4:]
     give1, own = lax.optimization_barrier((give1, own))
     near1 = swap(give1, 1)
     across0, diagonal0, row_weights, cols = lax.optimization_barrier((across0, diagonal0, row_weights, cols))
@@ -547,10 +549,10 @@
     sibling_came0 = partner(sibling_other0, 1)
 
     wind, mine0 = lax.optimization_barrier((wind, mine0))
-    strip, sibling_strip = call(
+    others, strip, sibling_strip = call(
         strips_kernel,
-        [shape(STRIP, rows_dev)] * 2,
-        (wind, across0, diagonal0, near0, keep0),
+        [shape(layers, cols_dev, pupil_cols)] + [shape(STRIP, rows_dev)] * 2,
+        (wind, *tables, across0, diagonal0, near0, keep0),
         0,
         "strips",
         scratch=wind_scratch,
@@ -569,7 +571,6 @@
         brief=True,
     )
     far1, sibling_far1 = partner(far1), partner(sibling_far1, 1)
-    rest1, sibling_rest1 = partner(rest1), partner(sibling_rest1, 1)
     taken = swap(give, 1)
     phase = call(
         phase_kernel,
@@ -579,6 +580,8 @@
         "phase",
     )
 
+    rest1, sibling_rest1, phase = lax.optimization_barrier((rest1, sibling_rest1, phase))
+    rest1, sibling_rest1 = partner(rest1), partner(sibling_rest1, 1)
     *far_sums, strips = call(
         far_kernel,
         [shape(rows, pupil_cols + rows_dev)] * len(steps) + [shape(2 * STRIP, rows_dev)],

time: 35.7 us -> 34.7 us (0.972)
  waiting for transfers between devices: 5.79 us -> 5.08 us
  Pallas kernels: 13 us -> 12.6 us
    ppermute x3, starting transfers between devices: 4.51 us -> 5.14 us  [per_device(): lax.ppermute(received[k], 'layer', [(i, i ^ 2 * k) for i in range(n_layer)])]
    ppermute x3, waiting for transfers between devices: 4.49 us -> 3.9 us  [per_device(): lax.ppermute(received[k], 'layer', [(i, i ^ 2 * k) for i in range(n_layer)])]
    pallas_call x11, Pallas kernels: 13 us -> 12.6 us  [call(): pl.pallas_call(kernel, out_shape=out_shape, in_specs=in_specs, out_specs=...]
  transfers between devices with their start and end apart: 16 -> 16, of which waited for: 6 -> 5; matrix products, arithmetic and copies ran while one was open for 0% -> 0% of each run, Pallas kernels for 30% -> 30%
where the time goes in v15:
time: 34.7 us; the launch traced here: 34.5 us
  starting transfers between devices  16.1 us (46%)
  Pallas kernels  12.6 us (36%)
  waiting for transfers between devices  5.08 us (15%)
  between operations  0.74 us (2%)
    pallas_call x11, Pallas kernels, call(): pl.pallas_call(kernel, out_shape=out_shape, in_specs=in_specs, out_specs=...  12.6 us
    ppermute x7, starting transfers between devices, swap(): return lax.ppermute(value, 'dir', [(i, i ^ bits) for i in range(n_dir)])  5.67 us
    ppermute x6, starting transfers between devices, partner(): lax.ppermute(value, ('layer', 'dir'), [(i, i ^ n_dir ^ bits) for i in ran...  5.25 us
    ppermute x3, starting transfers between devices, per_device(): lax.ppermute(received[k], 'layer', [(i, i ^ 2 * k) for i in range(n_layer)])  5.14 us
    ppermute x3, waiting for transfers between devices, per_device(): lax.ppermute(received[k], 'layer', [(i, i ^ 2 * k) for i in range(n_layer)])  3.9 us
    ppermute x6, waiting for transfers between devices, partner(): lax.ppermute(value, ('layer', 'dir'), [(i, i ^ n_dir ^ bits) for i in ran...  1.16 us
  transfers between devices with their start and end apart: 16, of which 5 were waited for; matrix products, arithmetic and copies ran while one was open for 0% of the time, Pallas kernels for 30%

profile of v15, /device:TPU:0, one launch (start us, length us, event | category | flops | bytes accessed | tf_op | source)
XLA Modules:
  0.0 34.5 jit_solution(1104925022574643207)
XLA Ops:
  0.6 1.1 %split.1 = (bf16[3,128,128]{2,1,0:T(8,128)(2,1)S(1)}, bf16[3,128,128]{2,1,0:T(8,128)(2,1)S(1)}, bf16[3,128,128]{2,1,0:T(8,128)(2,1)S(1)}, bf16[3,128,128]{2,1,0:T(8,128)(2,1)S(1)}) custom-call(bf16[3,128,512]{2,1,0:T(8,128)(2,1)} %refs_0_.1), custom_call_target="tpu_custom_call" | custom-call | tf_op jit(solution)/shard_map/split/pallas_call | solution.py:42
  1.7 2.4 %collective-permute-start.1 = (bf16[3,128,128]{2,1,0:T(8,128)(2,1)S(1)}, bf16[3,128,128]{2,1,0:T(8,128)(2,1)S(1)}, u32[]{:S(2)}, u32[]{:S(2)}) collective-permute-start(bf16[3,128,128]{2,1,0:T(8,128)(2,1)S(1)} %get-tuple-element.62), channel_id=1, source_target_pairs={{0,3},{1,2},{2,1},{3,0},{4,7},{5,6},{6,5},{7,4},{8,11},{9,10},{10,... | collective-permute-start | bytes 294920 | tf_op jit(solution)/shard_map/ppermute | solution.py:492
  4.2 0.6 %collective-permute-start = (bf16[3,128,128]{2,1,0:T(8,128)(2,1)S(1)}, bf16[3,128,128]{2,1,0:T(8,128)(2,1)S(1)}, u32[]{:S(2)}, u32[]{:S(2)}) collective-permute-start(bf16[3,128,128]{2,1,0:T(8,128)(2,1)S(1)} %get-tuple-element.61.keep.refs_7_), channel_id=1, source_target_pairs={{0,2},{1,3},{2,0},{3,1},{4,6},{5,7},{6,4},{7,5},{8,10},{9,11},{10,... | collective-permute-start | bytes 294920 | tf_op jit(solution)/shard_map/ppermute | solution.py:492
  4.8 0.0 collective-permute-start.2
  4.9 1.7 %collective-permute-start.3 = (bf16[3,128,128]{2,1,0:T(8,128)(2,1)S(1)}, bf16[3,128,128]{2,1,0:T(8,128)(2,1)S(1)}, u32[]{:S(2)}, u32[]{:S(2)}) collective-permute-start(bf16[3,128,128]{2,1,0:T(8,128)(2,1)S(1)} %get-tuple-element.77.refs_3_), channel_id=1, source_target_pairs={{0,2},{1,3},{2,0},{3,1},{4,6},{5,7},{6,4},{7,5},{8,10},{9,11},{10,... | collective-permute-start | bytes 294920 | tf_op jit(solution)/shard_map/ppermute | solution.py:492
  6.6 0.1 collective-permute-start.4
  6.7 3.5 %weights.1 = (bf16[2,3,256,512]{3,2,1,0:T(8,128)(2,1)S(1)}, bf16[3,512,1280]{2,1,0:T(8,128)(2,1)S(1)}, s32[8,1280]{1,0:T(8,128)S(1)}, s32[8,1280]{1,0:T(8,128)S(...) custom-call(s32[2,3]{1,0:T(2,128)} %bitcast.6, ...), custom_call_target="tpu_custom_call" | custom-call | tf_op jit(solution)/shard_map/weights/pallas_call | solution.py:42
  10.1 0.0 collective-permute-done.1.diagonal.refs_5_.diagonal0
  10.1 0.4 %collective-permute-start.5 = (bf16[3,128,128]{2,1,0:T(8,128)(2,1)S(1)}, bf16[3,128,128]{2,1,0:T(8,128)(2,1)S(1)}, u32[]{:S(2)}, u32[]{:S(2)}) collective-permute-start(bf16[3,128,128]{2,1,0:T(8,128)(2,1)S(1)} %get-tuple-element.80), channel_id=1, source_target_pairs={{0,1},{1,0},{2,3},{3,2},{4,5},{5,4},{6,7},{7,6},{8,9},{9,8},{10,11... | collective-permute-start | bytes 294920 | tf_op jit(solution)/shard_map/ppermute | solution.py:492
  10.5 0.0 collective-permute-done.across.refs_4_
  10.5 0.6 %rows_first.1 = (bf16[3,128,128]{2,1,0:T(8,128)(2,1)S(1)}, bf16[3,128,128]{2,1,0:T(8,128)(2,1)S(1)}, bf16[3,128,128]{2,1,0:T(8,128)(2,1)S(1)}, bf16[3,128,128]{2,1,0:T(8,128)(2,1)S(1)}) custom-call(bf16[2,3,256,512]{3,2,1,0:T(8,128)(2,1)S(1)} %get-tuple-element.67.rows_ref, bf16[3,128,128]{2,1,0:T(8,128)(2,1)S(1)} %collective-permute-done.across.refs_4_, ...), custom_call_target="tpu_custom_call" | custom-call | tf_op jit(solution)/shard_map/rows_first/pallas_call | solution.py:42
  11.1 1.8 %collective-permute-start.6 = (bf16[3,128,128]{2,1,0:T(8,128)(2,1)S(1)}, bf16[3,128,128]{2,1,0:T(8,128)(2,1)S(1)}, u32[]{:S(2)}, u32[]{:S(2)}) collective-permute-start(bf16[3,128,128]{2,1,0:T(8,128)(2,1)S(1)} %get-tuple-element.88), channel_id=1, source_target_pairs={{0,4},{1,5},{2,6},{3,7},{4,0},{5,1},{6,2},{7,3},{8,12},{9,13},{10,... | collective-permute-start | bytes 294920 | tf_op jit(solution)/shard_map/ppermute | solution.py:496
  13.0 1.5 %strips.1 = (bf16[3,512,1280]{2,1,0:T(8,128)(2,1)S(1)}, bf16[32,128]{1,0:T(8,128)(2,1)S(1)}, bf16[32,128]{1,0:T(8,128)(2,1)S(1)}) custom-call(s32[2,3]{1,0:T(2,128)S(1)} %get-tuple-element.71.wind_held, s32[8,1280]{1,0:T(8,128)S(1)} %get-tuple-element.72.refs_0_, s32[8,1280]{1,0:T(8,128)S(1)} %get-tuple-element.73.refs_1_, ...), custom_call_target="tpu_custom_call" | custom-call | tf_op jit(solution)/shard_map/strips/pallas_call | solution.py:42
  14.5 0.6 %rows_later.1 = (bf16[3,128,128]{2,1,0:T(8,128)(2,1)S(1)}, bf16[3,192,256]{2,1,0:T(8,128)(2,1)S(1)}, bf16[224,128]{1,0:T(8,128)(2,1)S(1)}, bf16[224,128]{1,0:T(8...) custom-call(bf16[2,3,256,512]{3,2,1,0:T(8,128)(2,1)S(1)} %get-tuple-element.67.rows_ref, ...), custom_call_target="tpu_custom_call" | custom-call | tf_op jit(solution)/shard_map/rows_later/pallas_call | solution.py:42
  15.1 1.7 %collective-permute-start.11 = (bf16[224,128]{1,0:T(8,128)(2,1)S(1)}, bf16[224,128]{1,0:T(8,128)(2,1)S(1)}, u32[]{:S(2)}, u32[]{:S(2)}) collective-permute-start(bf16[224,128]{1,0:T(8,128)(2,1)S(1)} %get-tuple-element.95), channel_id=1, source_target_pairs={{0,4},{1,5},{2,6},{3,7},{4,0},{5,1},{6,2},{7,3},{8,12},{9,13},{10,... | collective-permute-start | bytes 172040 | tf_op jit(solution)/shard_map/ppermute | solution.py:496
  16.8 0.2 collective-permute-start.12
  17.0 0.3 collective-permute-start.8
  17.3 0.8 %collective-permute-done.7.sibling_came = bf16[3,128,128]{2,1,0:T(8,128)(2,1)S(1)} collective-permute-done((bf16[3,128,128]{2,1,0:T(8,128)(2,1)S(1)}, bf16[3,128,128]{2,1,0:T(8,128)(2,1)S(1)}, u32[]{:S(2)}, u32[]{:S(2)}) %collective-permute-start.7) | collective-permute-done | bytes 98336 | tf_op jit(solution)/shard_map/ppermute | solution.py:496
  18.1 0.7 %phase.1 = f32[128,1280]{1,0:T(8,128)S(1)} custom-call(bf16[3,512,1280]{2,1,0:T(8,128)(2,1)S(1)} %get-tuple-element.65.mine_ref, bf16[3,512,1280]{2,1,0:T(8,128)(2,1)S(1)} %get-tuple-element.76.other_ref.cols_ref, bf16[3,128,128]{2,1,0:T(8,128)(2,1)S(1)} %get-tuple-element.86.mine0, bf16[3,128,128]{2,1,0:T(8,128)(2,1)S(1)} %get-tuple-element.87.mine1, ...), custom_call_target="tpu_custom_call" | custom-call | flops 10000000000 | bytes 8912896 | tf_op jit(solution)/shard_map/phase/pallas_call | solution.py:42
  18.8 0.9 %collective-permute-start.9 = (bf16[240,128]{1,0:T(8,128)(2,1)S(1)}, bf16[240,128]{1,0:T(8,128)(2,1)S(1)}, u32[]{:S(2)}, u32[]{:S(2)}) collective-permute-start(bf16[240,128]{1,0:T(8,128)(2,1)S(1)} %get-tuple-element.92), channel_id=1, source_target_pairs={{0,4},{1,5},{2,6},{3,7},{4,0},{5,1},{6,2},{7,3},{8,12},{9,13},{10,... | collective-permute-start | bytes 184328 | tf_op jit(solution)/shard_map/ppermute | solution.py:496
  19.7 0.6 %collective-permute-start.10 = (bf16[240,128]{1,0:T(8,128)(2,1)S(1)}, bf16[240,128]{1,0:T(8,128)(2,1)S(1)}, u32[]{:S(2)}, u32[]{:S(2)}) collective-permute-start(bf16[240,128]{1,0:T(8,128)(2,1)S(1)} %get-tuple-element.93), channel_id=1, source_target_pairs={{0,5},{1,4},{2,7},{3,6},{4,1},{5,0},{6,3},{7,2},{8,13},{9,12},{10,... | collective-permute-start | bytes 184328 | tf_op jit(solution)/shard_map/ppermute | solution.py:496
  20.3 0.4 %collective-permute-done.12.sibling_came = bf16[224,128]{1,0:T(8,128)(2,1)S(1)} collective-permute-done((bf16[224,128]{1,0:T(8,128)(2,1)S(1)}, bf16[224,128]{1,0:T(8,128)(2,1)S(1)}, u32[]{:S(2)}, u32[]{:S(2)}) %collective-permute-start.12) | collective-permute-done | bytes 57376 | tf_op jit(solution)/shard_map/ppermute | solution.py:496
  20.7 0.8 %far.1 = (bf16[32,1408]{1,0:T(8,128)(2,1)S(1)}, bf16[32,1408]{1,0:T(8,128)(2,1)S(1)}, bf16[64,128]{1,0:T(8,128)(2,1)S(1)}) custom-call(bf16[3,512,1280]{2,1,0:T(8,128)(2,1)S(1)} %get-tuple-element.65.mine_ref, bf16[3,512,1280]{2,1,0:T(8,128)(2,1)S(1)} %get-tuple-element.76.other_ref.cols_ref, f32[128,1280]{1,0:T(8,128)S(1)} %phase.1, ...), custom_call_target="tpu_custom_call" | custom-call | flops 300000000 | bytes 9125888 | tf_op jit(solution)/shard_map/far/pallas_call | solution.py:42
  21.5 3.7 %collective-permute-start.14 = (bf16[32,1408]{1,0:T(8,128)(2,1)S(1)}, bf16[32,1408]{1,0:T(8,128)(2,1)S(1)}, u32[]{:S(2)}, u32[]{:S(2)}) collective-permute-start(bf16[32,1408]{1,0:T(8,128)(2,1)S(1)} %get-tuple-element.102), channel_id=1, source_target_pairs={{0,24},{4,28},{8,16},{12,20},{16,8},{20,12},{24,0},{28,4},{1,25},{... | collective-permute-start | bytes 270344 | tf_op jit(solution)/shard_map/ppermute | solution.py:602
  25.2 0.8 %rest.1 = (bf16[32,1280]{1,0:T(8,128)(2,1)S(1)}, bf16[32,1280]{1,0:T(8,128)(2,1)S(1)}) custom-call(bf16[3,512,1280]{2,1,0:T(8,128)(2,1)S(1)} %get-tuple-element.65.mine_ref, bf16[3,512,1280]{2,1,0:T(8,128)(2,1)S(1)} %get-tuple-element.76.other_ref.cols_ref, f32[128,1280]{1,0:T(8,128)S(1)} %phase.1, bf16[3,192,256]{2,1,0:T(8,128)(2,1)S(1)} %collective-permute-done.8.taken, ...), custom_call_target="tpu_custom_call" | custom-call | tf_op jit(solution)/shard_map/rest/pallas_call | solution.py:42
  26.0 1.5 %collective-permute-start.15 = (bf16[32,1280]{1,0:T(8,128)(2,1)S(1)}, bf16[32,1280]{1,0:T(8,128)(2,1)S(1)}, u32[]{:S(2)}, u32[]{:S(2)}) collective-permute-start(bf16[32,1280]{1,0:T(8,128)(2,1)S(1)} %get-tuple-element.111), channel_id=1, source_target_pairs={{0,16},{4,20},{8,24},{12,28},{16,0},{20,4},{24,8},{28,12},{1,17},{... | collective-permute-start | bytes 245768 | tf_op jit(solution)/shard_map/ppermute | solution.py:602
  27.5 1.4 %collective-permute-done.14.refs_1_.refs_3_ = bf16[32,1408]{1,0:T(8,128)(2,1)S(1)} collective-permute-done((bf16[32,1408]{1,0:T(8,128)(2,1)S(1)}, bf16[32,1408]{1,0:T(8,128)(2,1)S(1)}, u32[]{:S(2)}, u32[]{:S(2)}) %collective-permute-start.14) | collective-permute-done | bytes 90144 | tf_op jit(solution)/shard_map/ppermute | solution.py:602
  28.8 0.6 %optics.1 = (f32[32,1280]{1,0:T(8,128)S(1)}, bf16[256,512]{1,0:T(8,128)(2,1)S(1)}, bf16[128,64]{1,0:T(8,128)(2,1)S(1)}) custom-call(f32[32,1280]{1,0:T(8,128)S(1)} %get-tuple-element.103.amplitude, f32[128,128]{1,0:T(8,128)S(1)} %get-tuple-element.104.ones, f32[256,512]{1,0:T(8,128)S(1)} %get-tuple-element.105.columns, f32[128,64]{1,0:T(8,128)S(1)} %get-tuple-element.106.lines), custom_call_target="tpu_custom_call" | custom-call | tf_op jit(solution)/shard_map/optics/pallas_call | solution.py:42
  29.5 2.0 %collective-permute-done.13.refs_0_.refs_1_ = bf16[32,1408]{1,0:T(8,128)(2,1)S(1)} collective-permute-done((bf16[32,1408]{1,0:T(8,128)(2,1)S(1)}, bf16[32,1408]{1,0:T(8,128)(2,1)S(1)}, u32[]{:S(2)}, u32[]{:S(2)}) %collective-permute-start.13) | collective-permute-done | bytes 90144 | tf_op jit(solution)/shard_map/ppermute | solution.py:602
  31.4 1.1 %shift.1.refs_7_ = bf16[3,128,512]{2,1,0:T(8,128)(2,1)S(1)} custom-call(s32[2,3]{1,0:T(2,128)S(1)} %get-tuple-element.71.wind_held, bf16[3,128,512]{2,1,0:T(8,128)(2,1)S(1)} %get-tuple-element.116.own, bf16[3,128,128]{2,1,0:T(8,128)(2,1)S(1)} %collective-permute-done.2.near.refs_6_.near0, bf16[3,128,128]{2,1,0:T(8,128)(2,1)S(1)} %collective-permute-done.5.refs_2_.near1, ...), custom_call_target="tpu_custom_call" | custom-call | tf_op jit(solution)/shard_map/shift/pallas_call | solution.py:42
  32.6 0.6 %collective-permute-done.15.refs_2_ = bf16[32,1280]{1,0:T(8,128)(2,1)S(1)} collective-permute-done((bf16[32,1280]{1,0:T(8,128)(2,1)S(1)}, bf16[32,1280]{1,0:T(8,128)(2,1)S(1)}, u32[]{:S(2)}, u32[]{:S(2)}) %collective-permute-start.15) | collective-permute-done | bytes 81952 | tf_op jit(solution)/shard_map/ppermute | solution.py:602
  33.2 1.3 %imaging.1 = (f32[64,2560]{1,0:T(8,128)}, bf16[3,128,512]{2,1,0:T(8,128)(2,1)}) custom-call(bf16[32,1280]{1,0:T(8,128)(2,1)S(1)} %get-tuple-element.94.refs_0_, bf16[32,1408]{1,0:T(8,128)(2,1)S(1)} %collective-permute-done.13.refs_0_.refs_1_, bf16[32,1280]{1,0:T(8,128)(2,1)S(1)} %collective-permute-done.15.refs_2_, ...), custom_call_target="tpu_custom_call" | custom-call | flops 400000000 | bytes 2228224 | tf_op jit(solution)/shard_map/imaging/pallas_call | solution.py:42
  (11 shorter events, 0.0 us)
Async XLA Ops:
  1.7 8.4 %collective-permute-start.1 = (bf16[3,128,128]{2,1,0:T(8,128)(2,1)S(1)}, bf16[3,128,128]{2,1,0:T(8,128)(2,1)S(1)}, u32[]{:S(2)}, u32[]{:S(2)}) collective-permute-start(bf16[3,128,128]{2,1,0:T(8,128)(2,1)S(1)} %get-tuple-element.62), channel_id=1, source_target_pairs={{0,3},{1,2},{2,1},{3,0},{4,7},{5,6},{6,5},{7,4},{8,11},{9,10},{10,... | collective-permute-start | bytes 294920 | tf_op jit(solution)/shard_map/ppermute | solution.py:492
  4.2 6.4 %collective-permute-start = (bf16[3,128,128]{2,1,0:T(8,128)(2,1)S(1)}, bf16[3,128,128]{2,1,0:T(8,128)(2,1)S(1)}, u32[]{:S(2)}, u32[]{:S(2)}) collective-permute-start(bf16[3,128,128]{2,1,0:T(8,128)(2,1)S(1)} %get-tuple-element.61.keep.refs_7_), channel_id=1, source_target_pairs={{0,2},{1,3},{2,0},{3,1},{4,6},{5,7},{6,4},{7,5},{8,10},{9,11},{10,... | collective-permute-start | bytes 294920 | tf_op jit(solution)/shard_map/ppermute | solution.py:492
  4.8 5.7 %collective-permute-start.2 = (bf16[3,128,128]{2,1,0:T(8,128)(2,1)S(1)}, bf16[3,128,128]{2,1,0:T(8,128)(2,1)S(1)}, u32[]{:S(2)}, u32[]{:S(2)}) collective-permute-start(bf16[3,128,128]{2,1,0:T(8,128)(2,1)S(1)} %get-tuple-element.62), channel_id=1, source_target_pairs={{0,1},{1,0},{2,3},{3,2},{4,5},{5,4},{6,7},{7,6},{8,9},{9,8},{10,11... | collective-permute-start | bytes 294920 | tf_op jit(solution)/shard_map/ppermute | solution.py:492
  4.9 9.6 %collective-permute-start.3 = (bf16[3,128,128]{2,1,0:T(8,128)(2,1)S(1)}, bf16[3,128,128]{2,1,0:T(8,128)(2,1)S(1)}, u32[]{:S(2)}, u32[]{:S(2)}) collective-permute-start(bf16[3,128,128]{2,1,0:T(8,128)(2,1)S(1)} %get-tuple-element.77.refs_3_), channel_id=1, source_target_pairs={{0,2},{1,3},{2,0},{3,1},{4,6},{5,7},{6,4},{7,5},{8,10},{9,11},{10,... | collective-permute-start | bytes 294920 | tf_op jit(solution)/shard_map/ppermute | solution.py:492
  6.6 7.9 %collective-permute-start.4 = (bf16[3,128,128]{2,1,0:T(8,128)(2,1)S(1)}, bf16[3,128,128]{2,1,0:T(8,128)(2,1)S(1)}, u32[]{:S(2)}, u32[]{:S(2)}) collective-permute-start(bf16[3,128,128]{2,1,0:T(8,128)(2,1)S(1)} %get-tuple-element.80), channel_id=1, source_target_pairs={{0,3},{1,2},{2,1},{3,0},{4,7},{5,6},{6,5},{7,4},{8,11},{9,10},{10,... | collective-permute-start | bytes 294920 | tf_op jit(solution)/shard_map/ppermute | solution.py:492
  10.1 4.3 %collective-permute-start.5 = (bf16[3,128,128]{2,1,0:T(8,128)(2,1)S(1)}, bf16[3,128,128]{2,1,0:T(8,128)(2,1)S(1)}, u32[]{:S(2)}, u32[]{:S(2)}) collective-permute-start(bf16[3,128,128]{2,1,0:T(8,128)(2,1)S(1)} %get-tuple-element.80), channel_id=1, source_target_pairs={{0,1},{1,0},{2,3},{3,2},{4,5},{5,4},{6,7},{7,6},{8,9},{9,8},{10,11... | collective-permute-start | bytes 294920 | tf_op jit(solution)/shard_map/ppermute | solution.py:492
  11.1 6.2 %collective-permute-start.6 = (bf16[3,128,128]{2,1,0:T(8,128)(2,1)S(1)}, bf16[3,128,128]{2,1,0:T(8,128)(2,1)S(1)}, u32[]{:S(2)}, u32[]{:S(2)}) collective-permute-start(bf16[3,128,128]{2,1,0:T(8,128)(2,1)S(1)} %get-tuple-element.88), channel_id=1, source_target_pairs={{0,4},{1,5},{2,6},{3,7},{4,0},{5,1},{6,2},{7,3},{8,12},{9,13},{10,... | collective-permute-start | bytes 294920 | tf_op jit(solution)/shard_map/ppermute | solution.py:496
  13.0 5.1 %collective-permute-start.7 = (bf16[3,128,128]{2,1,0:T(8,128)(2,1)S(1)}, bf16[3,128,128]{2,1,0:T(8,128)(2,1)S(1)}, u32[]{:S(2)}, u32[]{:S(2)}) collective-permute-start(bf16[3,128,128]{2,1,0:T(8,128)(2,1)S(1)} %get-tuple-element.89), channel_id=1, source_target_pairs={{0,5},{1,4},{2,7},{3,6},{4,1},{5,0},{6,3},{7,2},{8,13},{9,12},{10,... | collective-permute-start | bytes 294920 | tf_op jit(solution)/shard_map/ppermute | solution.py:496
  15.1 5.2 %collective-permute-start.11 = (bf16[224,128]{1,0:T(8,128)(2,1)S(1)}, bf16[224,128]{1,0:T(8,128)(2,1)S(1)}, u32[]{:S(2)}, u32[]{:S(2)}) collective-permute-start(bf16[224,128]{1,0:T(8,128)(2,1)S(1)} %get-tuple-element.95), channel_id=1, source_target_pairs={{0,4},{1,5},{2,6},{3,7},{4,0},{5,1},{6,2},{7,3},{8,12},{9,13},{10,... | collective-permute-start | bytes 172040 | tf_op jit(solution)/shard_map/ppermute | solution.py:496
  16.8 3.9 %collective-permute-start.12 = (bf16[224,128]{1,0:T(8,128)(2,1)S(1)}, bf16[224,128]{1,0:T(8,128)(2,1)S(1)}, u32[]{:S(2)}, u32[]{:S(2)}) collective-permute-start(bf16[224,128]{1,0:T(8,128)(2,1)S(1)} %get-tuple-element.96), channel_id=1, source_target_pairs={{0,5},{1,4},{2,7},{3,6},{4,1},{5,0},{6,3},{7,2},{8,13},{9,12},{10,... | collective-permute-start | bytes 172040 | tf_op jit(solution)/shard_map/ppermute | solution.py:496
  17.0 3.7 %collective-permute-start.8 = (bf16[3,192,256]{2,1,0:T(8,128)(2,1)S(1)}, bf16[3,192,256]{2,1,0:T(8,128)(2,1)S(1)}, u32[]{:S(2)}, u32[]{:S(2)}) collective-permute-start(bf16[3,192,256]{2,1,0:T(8,128)(2,1)S(1)} %get-tuple-element.91), channel_id=1, source_target_pairs={{0,1},{1,0},{2,3},{3,2},{4,5},{5,4},{6,7},{7,6},{8,9},{9,8},{10,11... | collective-permute-start | bytes 884744 | tf_op jit(solution)/shard_map/ppermute | solution.py:492
  18.8 6.4 %collective-permute-start.9 = (bf16[240,128]{1,0:T(8,128)(2,1)S(1)}, bf16[240,128]{1,0:T(8,128)(2,1)S(1)}, u32[]{:S(2)}, u32[]{:S(2)}) collective-permute-start(bf16[240,128]{1,0:T(8,128)(2,1)S(1)} %get-tuple-element.92), channel_id=1, source_target_pairs={{0,4},{1,5},{2,6},{3,7},{4,0},{5,1},{6,2},{7,3},{8,12},{9,13},{10,... | collective-permute-start | bytes 184328 | tf_op jit(solution)/shard_map/ppermute | solution.py:496
  19.7 5.5 %collective-permute-start.10 = (bf16[240,128]{1,0:T(8,128)(2,1)S(1)}, bf16[240,128]{1,0:T(8,128)(2,1)S(1)}, u32[]{:S(2)}, u32[]{:S(2)}) collective-permute-start(bf16[240,128]{1,0:T(8,128)(2,1)S(1)} %get-tuple-element.93), channel_id=1, source_target_pairs={{0,5},{1,4},{2,7},{3,6},{4,1},{5,0},{6,3},{7,2},{8,13},{9,12},{10,... | collective-permute-start | bytes 184328 | tf_op jit(solution)/shard_map/ppermute | solution.py:496
  21.5 7.3 %collective-permute-start.14 = (bf16[32,1408]{1,0:T(8,128)(2,1)S(1)}, bf16[32,1408]{1,0:T(8,128)(2,1)S(1)}, u32[]{:S(2)}, u32[]{:S(2)}) collective-permute-start(bf16[32,1408]{1,0:T(8,128)(2,1)S(1)} %get-tuple-element.102), channel_id=1, source_target_pairs={{0,24},{4,28},{8,16},{12,20},{16,8},{20,12},{24,0},{28,4},{1,25},{... | collective-permute-start | bytes 270344 | tf_op jit(solution)/shard_map/ppermute | solution.py:602
  25.2 6.3 %collective-permute-start.13 = (bf16[32,1408]{1,0:T(8,128)(2,1)S(1)}, bf16[32,1408]{1,0:T(8,128)(2,1)S(1)}, u32[]{:S(2)}, u32[]{:S(2)}) collective-permute-start(bf16[32,1408]{1,0:T(8,128)(2,1)S(1)} %get-tuple-element.97), channel_id=1, source_target_pairs={{0,8},{4,12},{8,0},{12,4},{16,24},{20,28},{24,16},{28,20},{1,9},{5... | collective-permute-start | bytes 270344 | tf_op jit(solution)/shard_map/ppermute | solution.py:602
  26.0 7.2 %collective-permute-start.15 = (bf16[32,1280]{1,0:T(8,128)(2,1)S(1)}, bf16[32,1280]{1,0:T(8,128)(2,1)S(1)}, u32[]{:S(2)}, u32[]{:S(2)}) collective-permute-start(bf16[32,1280]{1,0:T(8,128)(2,1)S(1)} %get-tuple-element.111), channel_id=1, source_target_pairs={{0,16},{4,20},{8,24},{12,28},{16,0},{20,4},{24,8},{28,12},{1,17},{... | collective-permute-start | bytes 245768 | tf_op jit(solution)/shard_map/ppermute | solution.py:602

commit v16 on v15

--- a/solution.py
+++ b/solution.py
@@ -255,10 +255,6 @@
     rows = near.shape[1]
     size = (far.shape[0] - STRIP * rows // LANES) // layers
     start = half - size
-    for out in (rest, sibling_rest):
-        left = out.shape[0] - layers * start
-        if left:
-            out[layers * start :] = jnp.zeros((left, width), jnp.bfloat16)
     for level in range(layers):
         part = project_rows(rows_ref, keep, near, across, diagonal, level)
         mine[level] = part[:half]
@@ -561,7 +557,7 @@
     steps = strip_steps(pairs)
     far = len(steps) * rows
     message = shape(layers * far + STRIP * rows_dev // LANES, width)
-    remainder = shape(max(layers * (half - far), message.shape[0] + 16), width)
+    remainder = shape(layers * (half - far), width)
     mine1, give, far1, sibling_far1, rest1, sibling_rest1 = call(
         later_rows_kernel,
         [projected, shape(layers, half + 64, 2 * width), message, message, remainder, remainder],

time: 34.7 us -> 34.6 us (level)
  starting transfers between devices: 16.1 us -> 15.7 us
  waiting for transfers between devices: 5.08 us -> 5.43 us
    ppermute x3, starting transfers between devices: 5.14 us -> 4.75 us  [per_device(): lax.ppermute(received[k], 'layer', [(i, i ^ 2 * k) for i in range(n_layer)])]
    ppermute x3, waiting for transfers between devices: 3.9 us -> 4.28 us  [per_device(): lax.ppermute(received[k], 'layer', [(i, i ^ 2 * k) for i in range(n_layer)])]
where the time goes in v16:
time: 34.6 us; the launch traced here: 34.5 us
  starting transfers between devices  15.7 us (45%)
  Pallas kernels  12.6 us (36%)
  waiting for transfers between devices  5.43 us (16%)
  between operations  0.74 us (2%)
    pallas_call x11, Pallas kernels, call(): pl.pallas_call(kernel, out_shape=out_shape, in_specs=in_specs, out_specs=...  12.6 us
    ppermute x7, starting transfers between devices, swap(): return lax.ppermute(value, 'dir', [(i, i ^ bits) for i in range(n_dir)])  5.67 us
    ppermute x6, starting transfers between devices, partner(): lax.ppermute(value, ('layer', 'dir'), [(i, i ^ n_dir ^ bits) for i in ran...  5.25 us
    ppermute x3, starting transfers between devices, per_device(): lax.ppermute(received[k], 'layer', [(i, i ^ 2 * k) for i in range(n_layer)])  4.75 us
    ppermute x3, waiting for transfers between devices, per_device(): lax.ppermute(received[k], 'layer', [(i, i ^ 2 * k) for i in range(n_layer)])  4.28 us
    ppermute x6, waiting for transfers between devices, partner(): lax.ppermute(value, ('layer', 'dir'), [(i, i ^ n_dir ^ bits) for i in ran...  1.13 us
  transfers between devices with their start and end apart: 16, of which 5 were waited for; matrix products, arithmetic and copies ran while one was open for 0% of the time, Pallas kernels for 30%

profile of v16, /device:TPU:0, one launch (start us, length us, event | category | flops | bytes accessed | tf_op | source)
XLA Modules:
  0.0 34.5 jit_solution(12302944547342269318)
XLA Ops:
  0.6 1.1 %split.1 = (bf16[3,128,128]{2,1,0:T(8,128)(2,1)S(1)}, bf16[3,128,128]{2,1,0:T(8,128)(2,1)S(1)}, bf16[3,128,128]{2,1,0:T(8,128)(2,1)S(1)}, bf16[3,128,128]{2,1,0:T(8,128)(2,1)S(1)}) custom-call(bf16[3,128,512]{2,1,0:T(8,128)(2,1)} %refs_0_.1), custom_call_target="tpu_custom_call" | custom-call | tf_op jit(solution)/shard_map/split/pallas_call | solution.py:42
  1.7 2.4 %collective-permute-start.1 = (bf16[3,128,128]{2,1,0:T(8,128)(2,1)S(1)}, bf16[3,128,128]{2,1,0:T(8,128)(2,1)S(1)}, u32[]{:S(2)}, u32[]{:S(2)}) collective-permute-start(bf16[3,128,128]{2,1,0:T(8,128)(2,1)S(1)} %get-tuple-element.62), channel_id=1, source_target_pairs={{0,3},{1,2},{2,1},{3,0},{4,7},{5,6},{6,5},{7,4},{8,11},{9,10},{10,... | collective-permute-start | bytes 294920 | tf_op jit(solution)/shard_map/ppermute | solution.py:488
  4.2 0.6 %collective-permute-start = (bf16[3,128,128]{2,1,0:T(8,128)(2,1)S(1)}, bf16[3,128,128]{2,1,0:T(8,128)(2,1)S(1)}, u32[]{:S(2)}, u32[]{:S(2)}) collective-permute-start(bf16[3,128,128]{2,1,0:T(8,128)(2,1)S(1)} %get-tuple-element.61.keep.refs_7_), channel_id=1, source_target_pairs={{0,2},{1,3},{2,0},{3,1},{4,6},{5,7},{6,4},{7,5},{8,10},{9,11},{10,... | collective-permute-start | bytes 294920 | tf_op jit(solution)/shard_map/ppermute | solution.py:488
  4.8 0.0 collective-permute-start.2
  4.9 1.7 %collective-permute-start.3 = (bf16[3,128,128]{2,1,0:T(8,128)(2,1)S(1)}, bf16[3,128,128]{2,1,0:T(8,128)(2,1)S(1)}, u32[]{:S(2)}, u32[]{:S(2)}) collective-permute-start(bf16[3,128,128]{2,1,0:T(8,128)(2,1)S(1)} %get-tuple-element.77.refs_3_), channel_id=1, source_target_pairs={{0,2},{1,3},{2,0},{3,1},{4,6},{5,7},{6,4},{7,5},{8,10},{9,11},{10,... | collective-permute-start | bytes 294920 | tf_op jit(solution)/shard_map/ppermute | solution.py:488
  6.6 0.1 collective-permute-start.4
  6.7 3.5 %weights.1 = (bf16[2,3,256,512]{3,2,1,0:T(8,128)(2,1)S(1)}, bf16[3,512,1280]{2,1,0:T(8,128)(2,1)S(1)}, s32[8,1280]{1,0:T(8,128)S(1)}, s32[8,1280]{1,0:T(8,128)S(...) custom-call(s32[2,3]{1,0:T(2,128)} %bitcast.6, ...), custom_call_target="tpu_custom_call" | custom-call | tf_op jit(solution)/shard_map/weights/pallas_call | solution.py:42
  10.1 0.0 collective-permute-done.1.diagonal.refs_5_.diagonal0
  10.1 0.4 %collective-permute-start.5 = (bf16[3,128,128]{2,1,0:T(8,128)(2,1)S(1)}, bf16[3,128,128]{2,1,0:T(8,128)(2,1)S(1)}, u32[]{:S(2)}, u32[]{:S(2)}) collective-permute-start(bf16[3,128,128]{2,1,0:T(8,128)(2,1)S(1)} %get-tuple-element.80), channel_id=1, source_target_pairs={{0,1},{1,0},{2,3},{3,2},{4,5},{5,4},{6,7},{7,6},{8,9},{9,8},{10,11... | collective-permute-start | bytes 294920 | tf_op jit(solution)/shard_map/ppermute | solution.py:488
  10.5 0.6 %rows_first.1 = (bf16[3,128,128]{2,1,0:T(8,128)(2,1)S(1)}, bf16[3,128,128]{2,1,0:T(8,128)(2,1)S(1)}, bf16[3,128,128]{2,1,0:T(8,128)(2,1)S(1)}, bf16[3,128,128]{2,1,0:T(8,128)(2,1)S(1)}) custom-call(bf16[2,3,256,512]{3,2,1,0:T(8,128)(2,1)S(1)} %get-tuple-element.67.rows_ref, bf16[3,128,128]{2,1,0:T(8,128)(2,1)S(1)} %collective-permute-done.across.refs_4_, ...), custom_call_target="tpu_custom_call" | custom-call | tf_op jit(solution)/shard_map/rows_first/pallas_call | solution.py:42
  11.1 1.8 %collective-permute-start.6 = (bf16[3,128,128]{2,1,0:T(8,128)(2,1)S(1)}, bf16[3,128,128]{2,1,0:T(8,128)(2,1)S(1)}, u32[]{:S(2)}, u32[]{:S(2)}) collective-permute-start(bf16[3,128,128]{2,1,0:T(8,128)(2,1)S(1)} %get-tuple-element.88), channel_id=1, source_target_pairs={{0,4},{1,5},{2,6},{3,7},{4,0},{5,1},{6,2},{7,3},{8,12},{9,13},{10,... | collective-permute-start | bytes 294920 | tf_op jit(solution)/shard_map/ppermute | solution.py:492
  13.0 1.5 %strips.1 = (bf16[3,512,1280]{2,1,0:T(8,128)(2,1)S(1)}, bf16[32,128]{1,0:T(8,128)(2,1)S(1)}, bf16[32,128]{1,0:T(8,128)(2,1)S(1)}) custom-call(s32[2,3]{1,0:T(2,128)S(1)} %get-tuple-element.71.wind_held, s32[8,1280]{1,0:T(8,128)S(1)} %get-tuple-element.72.refs_0_, s32[8,1280]{1,0:T(8,128)S(1)} %get-tuple-element.73.refs_1_, ...), custom_call_target="tpu_custom_call" | custom-call | tf_op jit(solution)/shard_map/strips/pallas_call | solution.py:42
  14.5 0.0 collective-permute-done.3.refs_0_
  14.5 0.6 %rows_later.1 = (bf16[3,128,128]{2,1,0:T(8,128)(2,1)S(1)}, bf16[3,192,256]{2,1,0:T(8,128)(2,1)S(1)}, bf16[224,128]{1,0:T(8,128)(2,1)S(1)}, bf16[224,128]{1,0:T(8...) custom-call(bf16[2,3,256,512]{3,2,1,0:T(8,128)(2,1)S(1)} %get-tuple-element.67.rows_ref, ...), custom_call_target="tpu_custom_call" | custom-call | tf_op jit(solution)/shard_map/rows_later/pallas_call | solution.py:42
  15.1 1.7 %collective-permute-start.11 = (bf16[224,128]{1,0:T(8,128)(2,1)S(1)}, bf16[224,128]{1,0:T(8,128)(2,1)S(1)}, u32[]{:S(2)}, u32[]{:S(2)}) collective-permute-start(bf16[224,128]{1,0:T(8,128)(2,1)S(1)} %get-tuple-element.95), channel_id=1, source_target_pairs={{0,4},{1,5},{2,6},{3,7},{4,0},{5,1},{6,2},{7,3},{8,12},{9,13},{10,... | collective-permute-start | bytes 172040 | tf_op jit(solution)/shard_map/ppermute | solution.py:492
  16.8 0.2 collective-permute-start.12
  17.0 0.3 collective-permute-start.8
  17.3 0.8 %collective-permute-done.7.sibling_came = bf16[3,128,128]{2,1,0:T(8,128)(2,1)S(1)} collective-permute-done((bf16[3,128,128]{2,1,0:T(8,128)(2,1)S(1)}, bf16[3,128,128]{2,1,0:T(8,128)(2,1)S(1)}, u32[]{:S(2)}, u32[]{:S(2)}) %collective-permute-start.7) | collective-permute-done | bytes 98336 | tf_op jit(solution)/shard_map/ppermute | solution.py:492
  18.1 0.7 %phase.1 = f32[128,1280]{1,0:T(8,128)S(1)} custom-call(bf16[3,512,1280]{2,1,0:T(8,128)(2,1)S(1)} %get-tuple-element.65.mine_ref, bf16[3,512,1280]{2,1,0:T(8,128)(2,1)S(1)} %get-tuple-element.76.other_ref.cols_ref, bf16[3,128,128]{2,1,0:T(8,128)(2,1)S(1)} %get-tuple-element.86.mine0, bf16[3,128,128]{2,1,0:T(8,128)(2,1)S(1)} %get-tuple-element.87.mine1, ...), custom_call_target="tpu_custom_call" | custom-call | flops 10000000000 | bytes 8912896 | tf_op jit(solution)/shard_map/phase/pallas_call | solution.py:42
  18.8 0.9 %collective-permute-start.9 = (bf16[192,128]{1,0:T(8,128)(2,1)S(1)}, bf16[192,128]{1,0:T(8,128)(2,1)S(1)}, u32[]{:S(2)}, u32[]{:S(2)}) collective-permute-start(bf16[192,128]{1,0:T(8,128)(2,1)S(1)} %get-tuple-element.92), channel_id=1, source_target_pairs={{0,4},{1,5},{2,6},{3,7},{4,0},{5,1},{6,2},{7,3},{8,12},{9,13},{10,... | collective-permute-start | bytes 147464 | tf_op jit(solution)/shard_map/ppermute | solution.py:492
  19.7 0.6 %collective-permute-start.10 = (bf16[192,128]{1,0:T(8,128)(2,1)S(1)}, bf16[192,128]{1,0:T(8,128)(2,1)S(1)}, u32[]{:S(2)}, u32[]{:S(2)}) collective-permute-start(bf16[192,128]{1,0:T(8,128)(2,1)S(1)} %get-tuple-element.93), channel_id=1, source_target_pairs={{0,5},{1,4},{2,7},{3,6},{4,1},{5,0},{6,3},{7,2},{8,13},{9,12},{10,... | collective-permute-start | bytes 147464 | tf_op jit(solution)/shard_map/ppermute | solution.py:492
  20.3 0.3 collective-permute-done.12.sibling_came
  20.7 0.8 %far.1 = (bf16[32,1408]{1,0:T(8,128)(2,1)S(1)}, bf16[32,1408]{1,0:T(8,128)(2,1)S(1)}, bf16[64,128]{1,0:T(8,128)(2,1)S(1)}) custom-call(bf16[3,512,1280]{2,1,0:T(8,128)(2,1)S(1)} %get-tuple-element.65.mine_ref, bf16[3,512,1280]{2,1,0:T(8,128)(2,1)S(1)} %get-tuple-element.76.other_ref.cols_ref, f32[128,1280]{1,0:T(8,128)S(1)} %phase.1, ...), custom_call_target="tpu_custom_call" | custom-call | flops 300000000 | bytes 9125888 | tf_op jit(solution)/shard_map/far/pallas_call | solution.py:42
  21.5 3.7 %collective-permute-start.14 = (bf16[32,1408]{1,0:T(8,128)(2,1)S(1)}, bf16[32,1408]{1,0:T(8,128)(2,1)S(1)}, u32[]{:S(2)}, u32[]{:S(2)}) collective-permute-start(bf16[32,1408]{1,0:T(8,128)(2,1)S(1)} %get-tuple-element.102), channel_id=1, source_target_pairs={{0,24},{4,28},{8,16},{12,20},{16,8},{20,12},{24,0},{28,4},{1,25},{... | collective-permute-start | bytes 270344 | tf_op jit(solution)/shard_map/ppermute | solution.py:598
  25.2 0.8 %rest.1 = (bf16[32,1280]{1,0:T(8,128)(2,1)S(1)}, bf16[32,1280]{1,0:T(8,128)(2,1)S(1)}) custom-call(bf16[3,512,1280]{2,1,0:T(8,128)(2,1)S(1)} %get-tuple-element.65.mine_ref, bf16[3,512,1280]{2,1,0:T(8,128)(2,1)S(1)} %get-tuple-element.76.other_ref.cols_ref, f32[128,1280]{1,0:T(8,128)S(1)} %phase.1, bf16[3,192,256]{2,1,0:T(8,128)(2,1)S(1)} %collective-permute-done.8.taken, ...), custom_call_target="tpu_custom_call" | custom-call | tf_op jit(solution)/shard_map/rest/pallas_call | solution.py:42
  26.0 1.1 %collective-permute-start.15 = (bf16[32,1280]{1,0:T(8,128)(2,1)S(1)}, bf16[32,1280]{1,0:T(8,128)(2,1)S(1)}, u32[]{:S(2)}, u32[]{:S(2)}) collective-permute-start(bf16[32,1280]{1,0:T(8,128)(2,1)S(1)} %get-tuple-element.111), channel_id=1, source_target_pairs={{0,16},{4,20},{8,24},{12,28},{16,0},{20,4},{24,8},{28,12},{1,17},{... | collective-permute-start | bytes 245768 | tf_op jit(solution)/shard_map/ppermute | solution.py:598
  27.1 1.8 %collective-permute-done.14.refs_1_.refs_3_ = bf16[32,1408]{1,0:T(8,128)(2,1)S(1)} collective-permute-done((bf16[32,1408]{1,0:T(8,128)(2,1)S(1)}, bf16[32,1408]{1,0:T(8,128)(2,1)S(1)}, u32[]{:S(2)}, u32[]{:S(2)}) %collective-permute-start.14) | collective-permute-done | bytes 90144 | tf_op jit(solution)/shard_map/ppermute | solution.py:598
  28.9 0.6 %optics.1 = (f32[32,1280]{1,0:T(8,128)S(1)}, bf16[256,512]{1,0:T(8,128)(2,1)S(1)}, bf16[128,64]{1,0:T(8,128)(2,1)S(1)}) custom-call(f32[32,1280]{1,0:T(8,128)S(1)} %get-tuple-element.103.amplitude, f32[128,128]{1,0:T(8,128)S(1)} %get-tuple-element.104.ones, f32[256,512]{1,0:T(8,128)S(1)} %get-tuple-element.105.columns, f32[128,64]{1,0:T(8,128)S(1)} %get-tuple-element.106.lines), custom_call_target="tpu_custom_call" | custom-call | tf_op jit(solution)/shard_map/optics/pallas_call | solution.py:42
  29.5 2.0 %collective-permute-done.13.refs_0_.refs_1_ = bf16[32,1408]{1,0:T(8,128)(2,1)S(1)} collective-permute-done((bf16[32,1408]{1,0:T(8,128)(2,1)S(1)}, bf16[32,1408]{1,0:T(8,128)(2,1)S(1)}, u32[]{:S(2)}, u32[]{:S(2)}) %collective-permute-start.13) | collective-permute-done | bytes 90144 | tf_op jit(solution)/shard_map/ppermute | solution.py:598
  31.5 1.1 %shift.1.refs_7_ = bf16[3,128,512]{2,1,0:T(8,128)(2,1)S(1)} custom-call(s32[2,3]{1,0:T(2,128)S(1)} %get-tuple-element.71.wind_held, bf16[3,128,512]{2,1,0:T(8,128)(2,1)S(1)} %get-tuple-element.116.own, bf16[3,128,128]{2,1,0:T(8,128)(2,1)S(1)} %collective-permute-done.2.near.refs_6_.near0, bf16[3,128,128]{2,1,0:T(8,128)(2,1)S(1)} %collective-permute-done.5.refs_2_.near1, ...), custom_call_target="tpu_custom_call" | custom-call | tf_op jit(solution)/shard_map/shift/pallas_call | solution.py:42
  32.6 0.5 %collective-permute-done.15.refs_2_ = bf16[32,1280]{1,0:T(8,128)(2,1)S(1)} collective-permute-done((bf16[32,1280]{1,0:T(8,128)(2,1)S(1)}, bf16[32,1280]{1,0:T(8,128)(2,1)S(1)}, u32[]{:S(2)}, u32[]{:S(2)}) %collective-permute-start.15) | collective-permute-done | bytes 81952 | tf_op jit(solution)/shard_map/ppermute | solution.py:598
  33.1 1.3 %imaging.1 = (f32[64,2560]{1,0:T(8,128)}, bf16[3,128,512]{2,1,0:T(8,128)(2,1)}) custom-call(bf16[32,1280]{1,0:T(8,128)(2,1)S(1)} %get-tuple-element.94.refs_0_, bf16[32,1408]{1,0:T(8,128)(2,1)S(1)} %collective-permute-done.13.refs_0_.refs_1_, bf16[32,1280]{1,0:T(8,128)(2,1)S(1)} %collective-permute-done.15.refs_2_, ...), custom_call_target="tpu_custom_call" | custom-call | flops 400000000 | bytes 2228224 | tf_op jit(solution)/shard_map/imaging/pallas_call | solution.py:42
  (11 shorter events, 0.0 us)
Async XLA Ops:
  1.7 8.4 %collective-permute-start.1 = (bf16[3,128,128]{2,1,0:T(8,128)(2,1)S(1)}, bf16[3,128,128]{2,1,0:T(8,128)(2,1)S(1)}, u32[]{:S(2)}, u32[]{:S(2)}) collective-permute-start(bf16[3,128,128]{2,1,0:T(8,128)(2,1)S(1)} %get-tuple-element.62), channel_id=1, source_target_pairs={{0,3},{1,2},{2,1},{3,0},{4,7},{5,6},{6,5},{7,4},{8,11},{9,10},{10,... | collective-permute-start | bytes 294920 | tf_op jit(solution)/shard_map/ppermute | solution.py:488
  4.2 6.4 %collective-permute-start = (bf16[3,128,128]{2,1,0:T(8,128)(2,1)S(1)}, bf16[3,128,128]{2,1,0:T(8,128)(2,1)S(1)}, u32[]{:S(2)}, u32[]{:S(2)}) collective-permute-start(bf16[3,128,128]{2,1,0:T(8,128)(2,1)S(1)} %get-tuple-element.61.keep.refs_7_), channel_id=1, source_target_pairs={{0,2},{1,3},{2,0},{3,1},{4,6},{5,7},{6,4},{7,5},{8,10},{9,11},{10,... | collective-permute-start | bytes 294920 | tf_op jit(solution)/shard_map/ppermute | solution.py:488
  4.8 5.7 %collective-permute-start.2 = (bf16[3,128,128]{2,1,0:T(8,128)(2,1)S(1)}, bf16[3,128,128]{2,1,0:T(8,128)(2,1)S(1)}, u32[]{:S(2)}, u32[]{:S(2)}) collective-permute-start(bf16[3,128,128]{2,1,0:T(8,128)(2,1)S(1)} %get-tuple-element.62), channel_id=1, source_target_pairs={{0,1},{1,0},{2,3},{3,2},{4,5},{5,4},{6,7},{7,6},{8,9},{9,8},{10,11... | collective-permute-start | bytes 294920 | tf_op jit(solution)/shard_map/ppermute | solution.py:488
  4.9 9.6 %collective-permute-start.3 = (bf16[3,128,128]{2,1,0:T(8,128)(2,1)S(1)}, bf16[3,128,128]{2,1,0:T(8,128)(2,1)S(1)}, u32[]{:S(2)}, u32[]{:S(2)}) collective-permute-start(bf16[3,128,128]{2,1,0:T(8,128)(2,1)S(1)} %get-tuple-element.77.refs_3_), channel_id=1, source_target_pairs={{0,2},{1,3},{2,0},{3,1},{4,6},{5,7},{6,4},{7,5},{8,10},{9,11},{10,... | collective-permute-start | bytes 294920 | tf_op jit(solution)/shard_map/ppermute | solution.py:488
  6.6 7.9 %collective-permute-start.4 = (bf16[3,128,128]{2,1,0:T(8,128)(2,1)S(1)}, bf16[3,128,128]{2,1,0:T(8,128)(2,1)S(1)}, u32[]{:S(2)}, u32[]{:S(2)}) collective-permute-start(bf16[3,128,128]{2,1,0:T(8,128)(2,1)S(1)} %get-tuple-element.80), channel_id=1, source_target_pairs={{0,3},{1,2},{2,1},{3,0},{4,7},{5,6},{6,5},{7,4},{8,11},{9,10},{10,... | collective-permute-start | bytes 294920 | tf_op jit(solution)/shard_map/ppermute | solution.py:488
  10.1 4.3 %collective-permute-start.5 = (bf16[3,128,128]{2,1,0:T(8,128)(2,1)S(1)}, bf16[3,128,128]{2,1,0:T(8,128)(2,1)S(1)}, u32[]{:S(2)}, u32[]{:S(2)}) collective-permute-start(bf16[3,128,128]{2,1,0:T(8,128)(2,1)S(1)} %get-tuple-element.80), channel_id=1, source_target_pairs={{0,1},{1,0},{2,3},{3,2},{4,5},{5,4},{6,7},{7,6},{8,9},{9,8},{10,11... | collective-permute-start | bytes 294920 | tf_op jit(solution)/shard_map/ppermute | solution.py:488
  11.1 6.2 %collective-permute-start.6 = (bf16[3,128,128]{2,1,0:T(8,128)(2,1)S(1)}, bf16[3,128,128]{2,1,0:T(8,128)(2,1)S(1)}, u32[]{:S(2)}, u32[]{:S(2)}) collective-permute-start(bf16[3,128,128]{2,1,0:T(8,128)(2,1)S(1)} %get-tuple-element.88), channel_id=1, source_target_pairs={{0,4},{1,5},{2,6},{3,7},{4,0},{5,1},{6,2},{7,3},{8,12},{9,13},{10,... | collective-permute-start | bytes 294920 | tf_op jit(solution)/shard_map/ppermute | solution.py:492
  13.0 5.1 %collective-permute-start.7 = (bf16[3,128,128]{2,1,0:T(8,128)(2,1)S(1)}, bf16[3,128,128]{2,1,0:T(8,128)(2,1)S(1)}, u32[]{:S(2)}, u32[]{:S(2)}) collective-permute-start(bf16[3,128,128]{2,1,0:T(8,128)(2,1)S(1)} %get-tuple-element.89), channel_id=1, source_target_pairs={{0,5},{1,4},{2,7},{3,6},{4,1},{5,0},{6,3},{7,2},{8,13},{9,12},{10,... | collective-permute-start | bytes 294920 | tf_op jit(solution)/shard_map/ppermute | solution.py:492
  15.1 5.3 %collective-permute-start.11 = (bf16[224,128]{1,0:T(8,128)(2,1)S(1)}, bf16[224,128]{1,0:T(8,128)(2,1)S(1)}, u32[]{:S(2)}, u32[]{:S(2)}) collective-permute-start(bf16[224,128]{1,0:T(8,128)(2,1)S(1)} %get-tuple-element.95), channel_id=1, source_target_pairs={{0,4},{1,5},{2,6},{3,7},{4,0},{5,1},{6,2},{7,3},{8,12},{9,13},{10,... | collective-permute-start | bytes 172040 | tf_op jit(solution)/shard_map/ppermute | solution.py:492
  16.8 3.9 %collective-permute-start.12 = (bf16[224,128]{1,0:T(8,128)(2,1)S(1)}, bf16[224,128]{1,0:T(8,128)(2,1)S(1)}, u32[]{:S(2)}, u32[]{:S(2)}) collective-permute-start(bf16[224,128]{1,0:T(8,128)(2,1)S(1)} %get-tuple-element.96), channel_id=1, source_target_pairs={{0,5},{1,4},{2,7},{3,6},{4,1},{5,0},{6,3},{7,2},{8,13},{9,12},{10,... | collective-permute-start | bytes 172040 | tf_op jit(solution)/shard_map/ppermute | solution.py:492
  17.0 3.7 %collective-permute-start.8 = (bf16[3,192,256]{2,1,0:T(8,128)(2,1)S(1)}, bf16[3,192,256]{2,1,0:T(8,128)(2,1)S(1)}, u32[]{:S(2)}, u32[]{:S(2)}) collective-permute-start(bf16[3,192,256]{2,1,0:T(8,128)(2,1)S(1)} %get-tuple-element.91), channel_id=1, source_target_pairs={{0,1},{1,0},{2,3},{3,2},{4,5},{5,4},{6,7},{7,6},{8,9},{9,8},{10,11... | collective-permute-start | bytes 884744 | tf_op jit(solution)/shard_map/ppermute | solution.py:488
  18.8 6.4 %collective-permute-start.9 = (bf16[192,128]{1,0:T(8,128)(2,1)S(1)}, bf16[192,128]{1,0:T(8,128)(2,1)S(1)}, u32[]{:S(2)}, u32[]{:S(2)}) collective-permute-start(bf16[192,128]{1,0:T(8,128)(2,1)S(1)} %get-tuple-element.92), channel_id=1, source_target_pairs={{0,4},{1,5},{2,6},{3,7},{4,0},{5,1},{6,2},{7,3},{8,12},{9,13},{10,... | collective-permute-start | bytes 147464 | tf_op jit(solution)/shard_map/ppermute | solution.py:492
  19.7 5.5 %collective-permute-start.10 = (bf16[192,128]{1,0:T(8,128)(2,1)S(1)}, bf16[192,128]{1,0:T(8,128)(2,1)S(1)}, u32[]{:S(2)}, u32[]{:S(2)}) collective-permute-start(bf16[192,128]{1,0:T(8,128)(2,1)S(1)} %get-tuple-element.93), channel_id=1, source_target_pairs={{0,5},{1,4},{2,7},{3,6},{4,1},{5,0},{6,3},{7,2},{8,13},{9,12},{10,... | collective-permute-start | bytes 147464 | tf_op jit(solution)/shard_map/ppermute | solution.py:492
  21.5 7.3 %collective-permute-start.14 = (bf16[32,1408]{1,0:T(8,128)(2,1)S(1)}, bf16[32,1408]{1,0:T(8,128)(2,1)S(1)}, u32[]{:S(2)}, u32[]{:S(2)}) collective-permute-start(bf16[32,1408]{1,0:T(8,128)(2,1)S(1)} %get-tuple-element.102), channel_id=1, source_target_pairs={{0,24},{4,28},{8,16},{12,20},{16,8},{20,12},{24,0},{28,4},{1,25},{... | collective-permute-start | bytes 270344 | tf_op jit(solution)/shard_map/ppermute | solution.py:598
  25.2 6.3 %collective-permute-start.13 = (bf16[32,1408]{1,0:T(8,128)(2,1)S(1)}, bf16[32,1408]{1,0:T(8,128)(2,1)S(1)}, u32[]{:S(2)}, u32[]{:S(2)}) collective-permute-start(bf16[32,1408]{1,0:T(8,128)(2,1)S(1)} %get-tuple-element.97), channel_id=1, source_target_pairs={{0,8},{4,12},{8,0},{12,4},{16,24},{20,28},{24,16},{28,20},{1,9},{5... | collective-permute-start | bytes 270344 | tf_op jit(solution)/shard_map/ppermute | solution.py:598
  26.0 7.2 %collective-permute-start.15 = (bf16[32,1280]{1,0:T(8,128)(2,1)S(1)}, bf16[32,1280]{1,0:T(8,128)(2,1)S(1)}, u32[]{:S(2)}, u32[]{:S(2)}) collective-permute-start(bf16[32,1280]{1,0:T(8,128)(2,1)S(1)} %get-tuple-element.111), channel_id=1, source_target_pairs={{0,16},{4,20},{8,24},{12,28},{16,0},{20,4},{24,8},{28,12},{1,17},{... | collective-permute-start | bytes 245768 | tf_op jit(solution)/shard_map/ppermute | solution.py:598

commit v17 on v16

--- a/solution.py
+++ b/solution.py
@@ -598,7 +598,7 @@
         received[k] = lax.ppermute(received[k], "layer", [(i, i ^ (2 * k)) for i in range(n_layer)])
     received = [received[k] for k in range(pairs)]
 
-    optics_in, received[-1] = lax.optimization_barrier((optics_in, received[-1]))
+    optics_in, received[1] = lax.optimization_barrier((optics_in, received[1]))
     optics = call(
         optics_kernel,
         (
@@ -611,7 +611,7 @@
         "optics",
         brief=True,
     )
-    received[1], optics = lax.optimization_barrier((received[1], optics))
+    received[-1], optics = lax.optimization_barrier((received[-1], optics))
     shifted = call(
         shift_kernel,
         shape(layers, rows_dev, cols_dev),

time: 34.6 us -> 35.4 us (1.023)
  waiting for transfers between devices: 5.43 us -> 6.21 us
    ppermute x3, waiting for transfers between devices: 4.28 us -> 5.06 us  [per_device(): lax.ppermute(received[k], 'layer', [(i, i ^ 2 * k) for i in range(n_layer)])]
  transfers between devices with their start and end apart: 16 -> 16, of which waited for: 5 -> 4; matrix products, arithmetic and copies ran while one was open for 0% -> 0% of each run, Pallas kernels for 30% -> 29%
where the time goes in v17:
time: 35.4 us; the launch traced here: 35.3 us
  starting transfers between devices  15.7 us (44%)
  Pallas kernels  12.6 us (36%)
  waiting for transfers between devices  6.21 us (18%)
  between operations  0.74 us (2%)
    pallas_call x11, Pallas kernels, call(): pl.pallas_call(kernel, out_shape=out_shape, in_specs=in_specs, out_specs=...  12.6 us
    ppermute x7, starting transfers between devices, swap(): return lax.ppermute(value, 'dir', [(i, i ^ bits) for i in range(n_dir)])  5.67 us
    ppermute x6, starting transfers between devices, partner(): lax.ppermute(value, ('layer', 'dir'), [(i, i ^ n_dir ^ bits) for i in ran...  5.25 us
    ppermute x3, waiting for transfers between devices, per_device(): lax.ppermute(received[k], 'layer', [(i, i ^ 2 * k) for i in range(n_layer)])  5.06 us
    ppermute x3, starting transfers between devices, per_device(): lax.ppermute(received[k], 'layer', [(i, i ^ 2 * k) for i in range(n_layer)])  4.76 us
    ppermute x6, waiting for transfers between devices, partner(): lax.ppermute(value, ('layer', 'dir'), [(i, i ^ n_dir ^ bits) for i in ran...  1.13 us
  transfers between devices with their start and end apart: 16, of which 4 were waited for; matrix products, arithmetic and copies ran while one was open for 0% of the time, Pallas kernels for 29%

profile of v17, /device:TPU:0, one launch (start us, length us, event | category | flops | bytes accessed | tf_op | source)
XLA Modules:
  0.0 35.3 jit_solution(16786993018620693945)
XLA Ops:
  0.6 1.1 %split.1 = (bf16[3,128,128]{2,1,0:T(8,128)(2,1)S(1)}, bf16[3,128,128]{2,1,0:T(8,128)(2,1)S(1)}, bf16[3,128,128]{2,1,0:T(8,128)(2,1)S(1)}, bf16[3,128,128]{2,1,0:T(8,128)(2,1)S(1)}) custom-call(bf16[3,128,512]{2,1,0:T(8,128)(2,1)} %refs_0_.1), custom_call_target="tpu_custom_call" | custom-call | tf_op jit(solution)/shard_map/split/pallas_call | solution.py:42
  1.7 2.4 %collective-permute-start.1 = (bf16[3,128,128]{2,1,0:T(8,128)(2,1)S(1)}, bf16[3,128,128]{2,1,0:T(8,128)(2,1)S(1)}, u32[]{:S(2)}, u32[]{:S(2)}) collective-permute-start(bf16[3,128,128]{2,1,0:T(8,128)(2,1)S(1)} %get-tuple-element.62), channel_id=1, source_target_pairs={{0,3},{1,2},{2,1},{3,0},{4,7},{5,6},{6,5},{7,4},{8,11},{9,10},{10,... | collective-permute-start | bytes 294920 | tf_op jit(solution)/shard_map/ppermute | solution.py:488
  4.2 0.6 %collective-permute-start = (bf16[3,128,128]{2,1,0:T(8,128)(2,1)S(1)}, bf16[3,128,128]{2,1,0:T(8,128)(2,1)S(1)}, u32[]{:S(2)}, u32[]{:S(2)}) collective-permute-start(bf16[3,128,128]{2,1,0:T(8,128)(2,1)S(1)} %get-tuple-element.61.keep.refs_7_), channel_id=1, source_target_pairs={{0,2},{1,3},{2,0},{3,1},{4,6},{5,7},{6,4},{7,5},{8,10},{9,11},{10,... | collective-permute-start | bytes 294920 | tf_op jit(solution)/shard_map/ppermute | solution.py:488
  4.8 0.0 collective-permute-start.2
  4.9 1.7 %collective-permute-start.3 = (bf16[3,128,128]{2,1,0:T(8,128)(2,1)S(1)}, bf16[3,128,128]{2,1,0:T(8,128)(2,1)S(1)}, u32[]{:S(2)}, u32[]{:S(2)}) collective-permute-start(bf16[3,128,128]{2,1,0:T(8,128)(2,1)S(1)} %get-tuple-element.77.refs_3_), channel_id=1, source_target_pairs={{0,2},{1,3},{2,0},{3,1},{4,6},{5,7},{6,4},{7,5},{8,10},{9,11},{10,... | collective-permute-start | bytes 294920 | tf_op jit(solution)/shard_map/ppermute | solution.py:488
  6.6 0.1 collective-permute-start.4
  6.7 3.5 %weights.1 = (bf16[2,3,256,512]{3,2,1,0:T(8,128)(2,1)S(1)}, bf16[3,512,1280]{2,1,0:T(8,128)(2,1)S(1)}, s32[8,1280]{1,0:T(8,128)S(1)}, s32[8,1280]{1,0:T(8,128)S(...) custom-call(s32[2,3]{1,0:T(2,128)} %bitcast.6, ...), custom_call_target="tpu_custom_call" | custom-call | tf_op jit(solution)/shard_map/weights/pallas_call | solution.py:42
  10.1 0.0 collective-permute-done.1.diagonal.refs_5_.diagonal0
  10.1 0.4 %collective-permute-start.5 = (bf16[3,128,128]{2,1,0:T(8,128)(2,1)S(1)}, bf16[3,128,128]{2,1,0:T(8,128)(2,1)S(1)}, u32[]{:S(2)}, u32[]{:S(2)}) collective-permute-start(bf16[3,128,128]{2,1,0:T(8,128)(2,1)S(1)} %get-tuple-element.80), channel_id=1, source_target_pairs={{0,1},{1,0},{2,3},{3,2},{4,5},{5,4},{6,7},{7,6},{8,9},{9,8},{10,11... | collective-permute-start | bytes 294920 | tf_op jit(solution)/shard_map/ppermute | solution.py:488
  10.5 0.0 collective-permute-done.across.refs_4_
  10.5 0.6 %rows_first.1 = (bf16[3,128,128]{2,1,0:T(8,128)(2,1)S(1)}, bf16[3,128,128]{2,1,0:T(8,128)(2,1)S(1)}, bf16[3,128,128]{2,1,0:T(8,128)(2,1)S(1)}, bf16[3,128,128]{2,1,0:T(8,128)(2,1)S(1)}) custom-call(bf16[2,3,256,512]{3,2,1,0:T(8,128)(2,1)S(1)} %get-tuple-element.67.rows_ref, bf16[3,128,128]{2,1,0:T(8,128)(2,1)S(1)} %collective-permute-done.across.refs_4_, ...), custom_call_target="tpu_custom_call" | custom-call | tf_op jit(solution)/shard_map/rows_first/pallas_call | solution.py:42
  11.1 1.8 %collective-permute-start.6 = (bf16[3,128,128]{2,1,0:T(8,128)(2,1)S(1)}, bf16[3,128,128]{2,1,0:T(8,128)(2,1)S(1)}, u32[]{:S(2)}, u32[]{:S(2)}) collective-permute-start(bf16[3,128,128]{2,1,0:T(8,128)(2,1)S(1)} %get-tuple-element.88), channel_id=1, source_target_pairs={{0,4},{1,5},{2,6},{3,7},{4,0},{5,1},{6,2},{7,3},{8,12},{9,13},{10,... | collective-permute-start | bytes 294920 | tf_op jit(solution)/shard_map/ppermute | solution.py:492
  13.0 1.5 %strips.1 = (bf16[3,512,1280]{2,1,0:T(8,128)(2,1)S(1)}, bf16[32,128]{1,0:T(8,128)(2,1)S(1)}, bf16[32,128]{1,0:T(8,128)(2,1)S(1)}) custom-call(s32[2,3]{1,0:T(2,128)S(1)} %get-tuple-element.71.wind_held, s32[8,1280]{1,0:T(8,128)S(1)} %get-tuple-element.72.refs_0_, s32[8,1280]{1,0:T(8,128)S(1)} %get-tuple-element.73.refs_1_, ...), custom_call_target="tpu_custom_call" | custom-call | tf_op jit(solution)/shard_map/strips/pallas_call | solution.py:42
  14.5 0.6 %rows_later.1 = (bf16[3,128,128]{2,1,0:T(8,128)(2,1)S(1)}, bf16[3,192,256]{2,1,0:T(8,128)(2,1)S(1)}, bf16[224,128]{1,0:T(8,128)(2,1)S(1)}, bf16[224,128]{1,0:T(8...) custom-call(bf16[2,3,256,512]{3,2,1,0:T(8,128)(2,1)S(1)} %get-tuple-element.67.rows_ref, ...), custom_call_target="tpu_custom_call" | custom-call | tf_op jit(solution)/shard_map/rows_later/pallas_call | solution.py:42
  15.1 1.7 %collective-permute-start.11 = (bf16[224,128]{1,0:T(8,128)(2,1)S(1)}, bf16[224,128]{1,0:T(8,128)(2,1)S(1)}, u32[]{:S(2)}, u32[]{:S(2)}) collective-permute-start(bf16[224,128]{1,0:T(8,128)(2,1)S(1)} %get-tuple-element.99), channel_id=1, source_target_pairs={{0,4},{1,5},{2,6},{3,7},{4,0},{5,1},{6,2},{7,3},{8,12},{9,13},{10,... | collective-permute-start | bytes 172040 | tf_op jit(solution)/shard_map/ppermute | solution.py:492
  16.8 0.2 collective-permute-start.12
  17.0 0.3 collective-permute-start.8
  17.3 0.8 %collective-permute-done.7.sibling_came = bf16[3,128,128]{2,1,0:T(8,128)(2,1)S(1)} collective-permute-done((bf16[3,128,128]{2,1,0:T(8,128)(2,1)S(1)}, bf16[3,128,128]{2,1,0:T(8,128)(2,1)S(1)}, u32[]{:S(2)}, u32[]{:S(2)}) %collective-permute-start.7) | collective-permute-done | bytes 98336 | tf_op jit(solution)/shard_map/ppermute | solution.py:492
  18.1 0.7 %phase.1 = f32[128,1280]{1,0:T(8,128)S(1)} custom-call(bf16[3,512,1280]{2,1,0:T(8,128)(2,1)S(1)} %get-tuple-element.65.mine_ref, bf16[3,512,1280]{2,1,0:T(8,128)(2,1)S(1)} %get-tuple-element.76.other_ref.cols_ref, bf16[3,128,128]{2,1,0:T(8,128)(2,1)S(1)} %get-tuple-element.86.mine0, bf16[3,128,128]{2,1,0:T(8,128)(2,1)S(1)} %get-tuple-element.87.mine1, ...), custom_call_target="tpu_custom_call" | custom-call | flops 10000000000 | bytes 8912896 | tf_op jit(solution)/shard_map/phase/pallas_call | solution.py:42
  18.8 0.9 %collective-permute-start.9 = (bf16[192,128]{1,0:T(8,128)(2,1)S(1)}, bf16[192,128]{1,0:T(8,128)(2,1)S(1)}, u32[]{:S(2)}, u32[]{:S(2)}) collective-permute-start(bf16[192,128]{1,0:T(8,128)(2,1)S(1)} %get-tuple-element.92), channel_id=1, source_target_pairs={{0,4},{1,5},{2,6},{3,7},{4,0},{5,1},{6,2},{7,3},{8,12},{9,13},{10,... | collective-permute-start | bytes 147464 | tf_op jit(solution)/shard_map/ppermute | solution.py:492
  19.7 0.6 %collective-permute-start.10 = (bf16[192,128]{1,0:T(8,128)(2,1)S(1)}, bf16[192,128]{1,0:T(8,128)(2,1)S(1)}, u32[]{:S(2)}, u32[]{:S(2)}) collective-permute-start(bf16[192,128]{1,0:T(8,128)(2,1)S(1)} %get-tuple-element.93), channel_id=1, source_target_pairs={{0,5},{1,4},{2,7},{3,6},{4,1},{5,0},{6,3},{7,2},{8,13},{9,12},{10,... | collective-permute-start | bytes 147464 | tf_op jit(solution)/shard_map/ppermute | solution.py:492
  20.3 0.3 collective-permute-done.12.sibling_came
  20.7 0.8 %far.1 = (bf16[32,1408]{1,0:T(8,128)(2,1)S(1)}, bf16[32,1408]{1,0:T(8,128)(2,1)S(1)}, bf16[64,128]{1,0:T(8,128)(2,1)S(1)}) custom-call(bf16[3,512,1280]{2,1,0:T(8,128)(2,1)S(1)} %get-tuple-element.65.mine_ref, bf16[3,512,1280]{2,1,0:T(8,128)(2,1)S(1)} %get-tuple-element.76.other_ref.cols_ref, f32[128,1280]{1,0:T(8,128)S(1)} %phase.1, ...), custom_call_target="tpu_custom_call" | custom-call | flops 300000000 | bytes 9125888 | tf_op jit(solution)/shard_map/far/pallas_call | solution.py:42
  21.5 1.6 %collective-permute-start.13 = (bf16[32,1408]{1,0:T(8,128)(2,1)S(1)}, bf16[32,1408]{1,0:T(8,128)(2,1)S(1)}, u32[]{:S(2)}, u32[]{:S(2)}) collective-permute-start(bf16[32,1408]{1,0:T(8,128)(2,1)S(1)} %get-tuple-element.101), channel_id=1, source_target_pairs={{0,8},{4,12},{8,0},{12,4},{16,24},{20,28},{24,16},{28,20},{1,9},{5... | collective-permute-start | bytes 270344 | tf_op jit(solution)/shard_map/ppermute | solution.py:598
  23.1 2.5 %collective-permute-start.15 = (bf16[32,1408]{1,0:T(8,128)(2,1)S(1)}, bf16[32,1408]{1,0:T(8,128)(2,1)S(1)}, u32[]{:S(2)}, u32[]{:S(2)}) collective-permute-start(bf16[32,1408]{1,0:T(8,128)(2,1)S(1)} %get-tuple-element.104), channel_id=1, source_target_pairs={{0,24},{4,28},{8,16},{12,20},{16,8},{20,12},{24,0},{28,4},{1,25},{... | collective-permute-start | bytes 270344 | tf_op jit(solution)/shard_map/ppermute | solution.py:598
  25.6 0.8 %rest.1 = (bf16[32,1280]{1,0:T(8,128)(2,1)S(1)}, bf16[32,1280]{1,0:T(8,128)(2,1)S(1)}) custom-call(bf16[3,512,1280]{2,1,0:T(8,128)(2,1)S(1)} %get-tuple-element.65.mine_ref, bf16[3,512,1280]{2,1,0:T(8,128)(2,1)S(1)} %get-tuple-element.76.other_ref.cols_ref, f32[128,1280]{1,0:T(8,128)S(1)} %phase.1, bf16[3,192,256]{2,1,0:T(8,128)(2,1)S(1)} %collective-permute-done.8.taken, ...), custom_call_target="tpu_custom_call" | custom-call | tf_op jit(solution)/shard_map/rest/pallas_call | solution.py:42
  26.4 0.6 %collective-permute-start.14 = (bf16[32,1280]{1,0:T(8,128)(2,1)S(1)}, bf16[32,1280]{1,0:T(8,128)(2,1)S(1)}, u32[]{:S(2)}, u32[]{:S(2)}) collective-permute-start(bf16[32,1280]{1,0:T(8,128)(2,1)S(1)} %get-tuple-element.103), channel_id=1, source_target_pairs={{0,16},{4,20},{8,24},{12,28},{16,0},{20,4},{24,8},{28,12},{1,17},{... | collective-permute-start | bytes 245768 | tf_op jit(solution)/shard_map/ppermute | solution.py:598
  27.1 0.6 %optics.1 = (f32[32,1280]{1,0:T(8,128)S(1)}, bf16[256,512]{1,0:T(8,128)(2,1)S(1)}, bf16[128,64]{1,0:T(8,128)(2,1)S(1)}) custom-call(f32[32,1280]{1,0:T(8,128)S(1)} %get-tuple-element.105.amplitude, f32[128,128]{1,0:T(8,128)S(1)} %get-tuple-element.106.ones, f32[256,512]{1,0:T(8,128)S(1)} %get-tuple-element.107.columns, f32[128,64]{1,0:T(8,128)S(1)} %get-tuple-element.108.lines), custom_call_target="tpu_custom_call" | custom-call | tf_op jit(solution)/shard_map/optics/pallas_call | solution.py:42
  27.7 3.2 %collective-permute-done.15.refs_1_.refs_3_ = bf16[32,1408]{1,0:T(8,128)(2,1)S(1)} collective-permute-done((bf16[32,1408]{1,0:T(8,128)(2,1)S(1)}, bf16[32,1408]{1,0:T(8,128)(2,1)S(1)}, u32[]{:S(2)}, u32[]{:S(2)}) %collective-permute-start.15) | collective-permute-done | bytes 90144 | tf_op jit(solution)/shard_map/ppermute | solution.py:598
  30.9 1.1 %shift.1.refs_7_ = bf16[3,128,512]{2,1,0:T(8,128)(2,1)S(1)} custom-call(s32[2,3]{1,0:T(2,128)S(1)} %get-tuple-element.71.wind_held, bf16[3,128,512]{2,1,0:T(8,128)(2,1)S(1)} %get-tuple-element.116.own, bf16[3,128,128]{2,1,0:T(8,128)(2,1)S(1)} %collective-permute-done.2.near.refs_6_.near0, bf16[3,128,128]{2,1,0:T(8,128)(2,1)S(1)} %collective-permute-done.5.refs_2_.near1, ...), custom_call_target="tpu_custom_call" | custom-call | tf_op jit(solution)/shard_map/shift/pallas_call | solution.py:42
  32.0 1.9 %collective-permute-done.14.refs_2_ = bf16[32,1280]{1,0:T(8,128)(2,1)S(1)} collective-permute-done((bf16[32,1280]{1,0:T(8,128)(2,1)S(1)}, bf16[32,1280]{1,0:T(8,128)(2,1)S(1)}, u32[]{:S(2)}, u32[]{:S(2)}) %collective-permute-start.14) | collective-permute-done | bytes 81952 | tf_op jit(solution)/shard_map/ppermute | solution.py:598
  33.9 1.3 %imaging.1 = (f32[64,2560]{1,0:T(8,128)}, bf16[3,128,512]{2,1,0:T(8,128)(2,1)}) custom-call(bf16[32,1280]{1,0:T(8,128)(2,1)S(1)} %get-tuple-element.94.refs_0_, bf16[32,1408]{1,0:T(8,128)(2,1)S(1)} %collective-permute-done.13.refs_0_.refs_1_, bf16[32,1280]{1,0:T(8,128)(2,1)S(1)} %collective-permute-done.14.refs_2_, ...), custom_call_target="tpu_custom_call" | custom-call | flops 400000000 | bytes 2228224 | tf_op jit(solution)/shard_map/imaging/pallas_call | solution.py:42
  (11 shorter events, 0.0 us)
Async XLA Ops:
  1.7 8.4 %collective-permute-start.1 = (bf16[3,128,128]{2,1,0:T(8,128)(2,1)S(1)}, bf16[3,128,128]{2,1,0:T(8,128)(2,1)S(1)}, u32[]{:S(2)}, u32[]{:S(2)}) collective-permute-start(bf16[3,128,128]{2,1,0:T(8,128)(2,1)S(1)} %get-tuple-element.62), channel_id=1, source_target_pairs={{0,3},{1,2},{2,1},{3,0},{4,7},{5,6},{6,5},{7,4},{8,11},{9,10},{10,... | collective-permute-start | bytes 294920 | tf_op jit(solution)/shard_map/ppermute | solution.py:488
  4.2 6.4 %collective-permute-start = (bf16[3,128,128]{2,1,0:T(8,128)(2,1)S(1)}, bf16[3,128,128]{2,1,0:T(8,128)(2,1)S(1)}, u32[]{:S(2)}, u32[]{:S(2)}) collective-permute-start(bf16[3,128,128]{2,1,0:T(8,128)(2,1)S(1)} %get-tuple-element.61.keep.refs_7_), channel_id=1, source_target_pairs={{0,2},{1,3},{2,0},{3,1},{4,6},{5,7},{6,4},{7,5},{8,10},{9,11},{10,... | collective-permute-start | bytes 294920 | tf_op jit(solution)/shard_map/ppermute | solution.py:488
  4.8 5.7 %collective-permute-start.2 = (bf16[3,128,128]{2,1,0:T(8,128)(2,1)S(1)}, bf16[3,128,128]{2,1,0:T(8,128)(2,1)S(1)}, u32[]{:S(2)}, u32[]{:S(2)}) collective-permute-start(bf16[3,128,128]{2,1,0:T(8,128)(2,1)S(1)} %get-tuple-element.62), channel_id=1, source_target_pairs={{0,1},{1,0},{2,3},{3,2},{4,5},{5,4},{6,7},{7,6},{8,9},{9,8},{10,11... | collective-permute-start | bytes 294920 | tf_op jit(solution)/shard_map/ppermute | solution.py:488
  4.9 9.6 %collective-permute-start.3 = (bf16[3,128,128]{2,1,0:T(8,128)(2,1)S(1)}, bf16[3,128,128]{2,1,0:T(8,128)(2,1)S(1)}, u32[]{:S(2)}, u32[]{:S(2)}) collective-permute-start(bf16[3,128,128]{2,1,0:T(8,128)(2,1)S(1)} %get-tuple-element.77.refs_3_), channel_id=1, source_target_pairs={{0,2},{1,3},{2,0},{3,1},{4,6},{5,7},{6,4},{7,5},{8,10},{9,11},{10,... | collective-permute-start | bytes 294920 | tf_op jit(solution)/shard_map/ppermute | solution.py:488
  6.6 7.9 %collective-permute-start.4 = (bf16[3,128,128]{2,1,0:T(8,128)(2,1)S(1)}, bf16[3,128,128]{2,1,0:T(8,128)(2,1)S(1)}, u32[]{:S(2)}, u32[]{:S(2)}) collective-permute-start(bf16[3,128,128]{2,1,0:T(8,128)(2,1)S(1)} %get-tuple-element.80), channel_id=1, source_target_pairs={{0,3},{1,2},{2,1},{3,0},{4,7},{5,6},{6,5},{7,4},{8,11},{9,10},{10,... | collective-permute-start | bytes 294920 | tf_op jit(solution)/shard_map/ppermute | solution.py:488
  10.1 4.3 %collective-permute-start.5 = (bf16[3,128,128]{2,1,0:T(8,128)(2,1)S(1)}, bf16[3,128,128]{2,1,0:T(8,128)(2,1)S(1)}, u32[]{:S(2)}, u32[]{:S(2)}) collective-permute-start(bf16[3,128,128]{2,1,0:T(8,128)(2,1)S(1)} %get-tuple-element.80), channel_id=1, source_target_pairs={{0,1},{1,0},{2,3},{3,2},{4,5},{5,4},{6,7},{7,6},{8,9},{9,8},{10,11... | collective-permute-start | bytes 294920 | tf_op jit(solution)/shard_map/ppermute | solution.py:488
  11.1 6.2 %collective-permute-start.6 = (bf16[3,128,128]{2,1,0:T(8,128)(2,1)S(1)}, bf16[3,128,128]{2,1,0:T(8,128)(2,1)S(1)}, u32[]{:S(2)}, u32[]{:S(2)}) collective-permute-start(bf16[3,128,128]{2,1,0:T(8,128)(2,1)S(1)} %get-tuple-element.88), channel_id=1, source_target_pairs={{0,4},{1,5},{2,6},{3,7},{4,0},{5,1},{6,2},{7,3},{8,12},{9,13},{10,... | collective-permute-start | bytes 294920 | tf_op jit(solution)/shard_map/ppermute | solution.py:492
  13.0 5.1 %collective-permute-start.7 = (bf16[3,128,128]{2,1,0:T(8,128)(2,1)S(1)}, bf16[3,128,128]{2,1,0:T(8,128)(2,1)S(1)}, u32[]{:S(2)}, u32[]{:S(2)}) collective-permute-start(bf16[3,128,128]{2,1,0:T(8,128)(2,1)S(1)} %get-tuple-element.89), channel_id=1, source_target_pairs={{0,5},{1,4},{2,7},{3,6},{4,1},{5,0},{6,3},{7,2},{8,13},{9,12},{10,... | collective-permute-start | bytes 294920 | tf_op jit(solution)/shard_map/ppermute | solution.py:492
  15.1 5.3 %collective-permute-start.11 = (bf16[224,128]{1,0:T(8,128)(2,1)S(1)}, bf16[224,128]{1,0:T(8,128)(2,1)S(1)}, u32[]{:S(2)}, u32[]{:S(2)}) collective-permute-start(bf16[224,128]{1,0:T(8,128)(2,1)S(1)} %get-tuple-element.99), channel_id=1, source_target_pairs={{0,4},{1,5},{2,6},{3,7},{4,0},{5,1},{6,2},{7,3},{8,12},{9,13},{10,... | collective-permute-start | bytes 172040 | tf_op jit(solution)/shard_map/ppermute | solution.py:492
  16.8 3.9 %collective-permute-start.12 = (bf16[224,128]{1,0:T(8,128)(2,1)S(1)}, bf16[224,128]{1,0:T(8,128)(2,1)S(1)}, u32[]{:S(2)}, u32[]{:S(2)}) collective-permute-start(bf16[224,128]{1,0:T(8,128)(2,1)S(1)} %get-tuple-element.100), channel_id=1, source_target_pairs={{0,5},{1,4},{2,7},{3,6},{4,1},{5,0},{6,3},{7,2},{8,13},{9,12},{10,... | collective-permute-start | bytes 172040 | tf_op jit(solution)/shard_map/ppermute | solution.py:492
  17.0 3.7 %collective-permute-start.8 = (bf16[3,192,256]{2,1,0:T(8,128)(2,1)S(1)}, bf16[3,192,256]{2,1,0:T(8,128)(2,1)S(1)}, u32[]{:S(2)}, u32[]{:S(2)}) collective-permute-start(bf16[3,192,256]{2,1,0:T(8,128)(2,1)S(1)} %get-tuple-element.91), channel_id=1, source_target_pairs={{0,1},{1,0},{2,3},{3,2},{4,5},{5,4},{6,7},{7,6},{8,9},{9,8},{10,11... | collective-permute-start | bytes 884744 | tf_op jit(solution)/shard_map/ppermute | solution.py:488
  18.8 6.8 %collective-permute-start.9 = (bf16[192,128]{1,0:T(8,128)(2,1)S(1)}, bf16[192,128]{1,0:T(8,128)(2,1)S(1)}, u32[]{:S(2)}, u32[]{:S(2)}) collective-permute-start(bf16[192,128]{1,0:T(8,128)(2,1)S(1)} %get-tuple-element.92), channel_id=1, source_target_pairs={{0,4},{1,5},{2,6},{3,7},{4,0},{5,1},{6,2},{7,3},{8,12},{9,13},{10,... | collective-permute-start | bytes 147464 | tf_op jit(solution)/shard_map/ppermute | solution.py:492
  19.7 5.9 %collective-permute-start.10 = (bf16[192,128]{1,0:T(8,128)(2,1)S(1)}, bf16[192,128]{1,0:T(8,128)(2,1)S(1)}, u32[]{:S(2)}, u32[]{:S(2)}) collective-permute-start(bf16[192,128]{1,0:T(8,128)(2,1)S(1)} %get-tuple-element.93), channel_id=1, source_target_pairs={{0,5},{1,4},{2,7},{3,6},{4,1},{5,0},{6,3},{7,2},{8,13},{9,12},{10,... | collective-permute-start | bytes 147464 | tf_op jit(solution)/shard_map/ppermute | solution.py:492
  21.5 5.6 %collective-permute-start.13 = (bf16[32,1408]{1,0:T(8,128)(2,1)S(1)}, bf16[32,1408]{1,0:T(8,128)(2,1)S(1)}, u32[]{:S(2)}, u32[]{:S(2)}) collective-permute-start(bf16[32,1408]{1,0:T(8,128)(2,1)S(1)} %get-tuple-element.101), channel_id=1, source_target_pairs={{0,8},{4,12},{8,0},{12,4},{16,24},{20,28},{24,16},{28,20},{1,9},{5... | collective-permute-start | bytes 270344 | tf_op jit(solution)/shard_map/ppermute | solution.py:598
  23.1 7.7 %collective-permute-start.15 = (bf16[32,1408]{1,0:T(8,128)(2,1)S(1)}, bf16[32,1408]{1,0:T(8,128)(2,1)S(1)}, u32[]{:S(2)}, u32[]{:S(2)}) collective-permute-start(bf16[32,1408]{1,0:T(8,128)(2,1)S(1)} %get-tuple-element.104), channel_id=1, source_target_pairs={{0,24},{4,28},{8,16},{12,20},{16,8},{20,12},{24,0},{28,4},{1,25},{... | collective-permute-start | bytes 270344 | tf_op jit(solution)/shard_map/ppermute | solution.py:598
  26.4 7.5 %collective-permute-start.14 = (bf16[32,1280]{1,0:T(8,128)(2,1)S(1)}, bf16[32,1280]{1,0:T(8,128)(2,1)S(1)}, u32[]{:S(2)}, u32[]{:S(2)}) collective-permute-start(bf16[32,1280]{1,0:T(8,128)(2,1)S(1)} %get-tuple-element.103), channel_id=1, source_target_pairs={{0,16},{4,20},{8,24},{12,28},{16,0},{20,4},{24,8},{28,12},{1,17},{... | collective-permute-start | bytes 245768 | tf_op jit(solution)/shard_map/ppermute | solution.py:598

commit v18 on v16

--- a/solution.py
+++ b/solution.py
@@ -90,7 +90,7 @@
 
 
 def split_kernel(screens, *refs):
-    outs, sems = refs[:-1], refs[-1]
+    ints, outs, held, sems = refs[:3], refs[3:7], refs[7:10], refs[-1]
     width = outs[0].shape[2]
     core = lax.rem(lax.axis_index("dir"), 2)
     pairs = []
@@ -98,22 +98,23 @@
         half = core if k < 2 else 1 - core
         start = pl.multiple_of(chunk_start(half, k % 2) * width, LANES)
         pairs.append((screens.at[:, :, pl.ds(start, width)], out, sems.at[k]))
+    pairs += [(source, copy, sems.at[4 + k]) for k, (source, copy) in enumerate(zip(ints, held))]
     for load in fetch(*pairs):
         load.wait()
 
 
-def weights_kernel(geometry, wind_hbm, offsets_hbm, ratio_hbm, *refs):
+def weights_kernel(geometry, wind_held, offsets_held, ratio_held, *refs):
     n_layer, rows_dev, screen_cols = geometry
     sources, (rows_out, cols_out, *tables), refs = refs[:5], refs[5:11], refs[11:]
-    copies, (wind_copy, wind, offsets, ratio, sems) = refs[:5], refs[5:]
+    copies, (wind, offsets, ratio, sems) = refs[:5], refs[5:]
     pupil_cols = cols_out.shape[2]
-    pairs = [*zip(sources, copies), (wind_hbm, wind_copy)]
+    loads = fetch(
+        (wind_held, wind, sems.at[0]),
+        (offsets_held, offsets, sems.at[1]),
+        (ratio_held, ratio, sems.at[2]),
+    )
+    pairs = [*zip(sources, copies)]
     others = fetch(*[(source, copy, sems.at[3 + k]) for k, (source, copy) in enumerate(pairs)])
-    loads = fetch(
-        (wind_hbm, wind, sems.at[0]),
-        (offsets_hbm, offsets, sems.at[1]),
-        (ratio_hbm, ratio, sems.at[2]),
-    )
     _, layers, pupil_rows, screen_rows = rows_out.shape
     half = pupil_rows // 2
     direction = lax.axis_index("dir")
@@ -288,17 +289,25 @@
         phase[:, at : at + 256] = project(parts, cuts, at)
 
 
-def sum_up(start, mine_ref, cols_ref, phase, taken, came, sibling_came, outs):
-    layers, _, width = taken.shape
-    width = width // 2
+def taken_kernel(mine_ref, phase, taken, out):
+    half, pupil_cols = phase.shape
+    layers, cols_dev, _ = mine_ref.shape
+    parts = [taken[level, :half] for level in range(layers)]
+    cuts = [(mine_ref, level, cols_dev // 2, cols_dev) for level in range(layers)]
+    for at in range(0, pupil_cols, 256):
+        out[:, at : at + 256] = phase[:, at : at + 256] + project(parts, cuts, at)
+
+
+def sum_up(start, cols_ref, phase, came, sibling_came, outs):
+    layers, cols_dev, _ = cols_ref.shape
+    width = cols_dev // 4
     block = outs[0].shape[0]
     size = block * len(outs)
     rows = slice(start, start + size)
     parts, cuts = [], []
     for level in range(layers):
         cut = slice(level * size, (level + 1) * size)
-        parts += [taken[level, rows], came[cut], sibling_came[cut]]
-        cuts += [(mine_ref, level, 2 * width, 4 * width)]
+        parts += [came[cut], sibling_came[cut]]
         cuts += [(cols_ref, level, width, 2 * width), (cols_ref, level, 3 * width, 4 * width)]
     pupil_cols = phase.shape[1]
     for at in range(0, pupil_cols, 256):
@@ -324,12 +333,12 @@
     out[:, at:] = jnp.where(after, last, first).astype(jnp.bfloat16)
 
 
-def far_kernel(mine_ref, cols_ref, phase, taken, came, sibling_came, *outs):
+def far_kernel(cols_ref, phase, came, sibling_came, *outs):
     *outs, strips = outs
     half = phase.shape[0]
     size = outs[0].shape[0] * len(outs)
-    sum_up(half - size, mine_ref, cols_ref, phase, taken, came, sibling_came, outs)
-    layers = taken.shape[0]
+    sum_up(half - size, cols_ref, phase, came, sibling_came, outs)
+    layers = cols_ref.shape[0]
     odd = lax.rem(lax.axis_index("dir"), 2) == 1
     here = get_strip(came, layers * size).astype(jnp.float32)
     there = get_strip(sibling_came, layers * size).astype(jnp.float32)
@@ -340,8 +349,8 @@
         add_strip(pairs, step, strips, out)
 
 
-def rest_kernel(mine_ref, cols_ref, phase, taken, came, sibling_came, *outs):
-    sum_up(0, mine_ref, cols_ref, phase, taken, came, sibling_came, outs)
+def rest_kernel(cols_ref, phase, came, sibling_came, *outs):
+    sum_up(0, cols_ref, phase, came, sibling_came, outs)
 
 
 def shifted_rows(shift, odd, own, near, far):
@@ -496,14 +505,15 @@
 
     width = cols_dev // 4
     chunk = shape(layers, rows_dev, width)
-    keep0, keep1, give0, give1 = call(
+    ints = (wind, offsets, ratio)
+    keep0, keep1, give0, give1, *ints = call(
         split_kernel,
-        [chunk] * 4,
-        (screens,),
+        [chunk] * 4 + [shape(*array.shape, dtype=jnp.int32) for array in ints],
+        (screens, *ints),
         0,
         "split",
-        in_hbm=(0,),
-        scratch=[sem((4,))],
+        in_hbm=range(4),
+        scratch=[sem((7,))],
         brief=True,
     )
     across0 = swap(keep0, 2)
@@ -513,21 +523,22 @@
     diagonal1 = swap(give1, 3)
     ones = np.kron(np.eye(LANES // SUB_PIX), np.ones((SUB_PIX, SUB_PIX))).astype(np.float32)
     optics_in = (amplitude, jnp.asarray(ones), *[jnp.asarray(table) for table in tables_of(rows)])
-    copies = [shape(*array.shape, dtype=array.dtype) for array in (screens, *optics_in, wind)]
+    copies = [shape(*array.shape, dtype=array.dtype) for array in (screens, *optics_in)]
     row_weights, cols, *loaded = call(
         functools.partial(weights_kernel, (n_layer, rows_dev, cols_dev * n_layer)),
         [shape(2, layers, pupil_rows, 4 * rows_dev), shape(layers, cols_dev, pupil_cols)]
         + [shape(8, pupil_cols, dtype=dtype) for dtype in (jnp.int32, jnp.int32, f32, f32)]
         + copies,
-        (wind, offsets, ratio, screens, *optics_in),
+        (*ints, screens, *optics_in),
         0,
         "weights",
-        in_hbm=range(8),
+        in_hbm=range(3, 8),
         scratch=[smem(array.shape, jnp.int32) for array in (wind, offsets, ratio)]
-        + [sem((9,))],
-        brief=True,
-    )
-    tables, (own, *optics_in, wind) = loaded[:4], loaded[4:]
+        + [sem((8,))],
+        brief=True,
+    )
+    tables, (own, *optics_in) = loaded[:4], loaded[4:]
+    wind = ints[0]
     give1, own = lax.optimization_barrier((give1, own))
     near1 = swap(give1, 1)
     across0, diagonal0, row_weights, cols = lax.optimization_barrier((across0, diagonal0, row_weights, cols))
@@ -578,17 +589,25 @@
 
     rest1, sibling_rest1, phase = lax.optimization_barrier((rest1, sibling_rest1, phase))
     rest1, sibling_rest1 = partner(rest1), partner(sibling_rest1, 1)
+    phase = call(
+        taken_kernel,
+        shape(half, pupil_cols, dtype=f32),
+        (cols, phase, taken),
+        0,
+        "taken",
+        brief=True,
+    )
     *far_sums, strips = call(
         far_kernel,
         [shape(rows, pupil_cols + rows_dev)] * len(steps) + [shape(2 * STRIP, rows_dev)],
-        (cols, others, phase, taken, far1, sibling_far1),
+        (others, phase, far1, sibling_far1),
         300_000_000,
         "far",
     )
     rest_sums = call(
         rest_kernel,
         [shape(rows, pupil_cols)] * (pairs - len(steps)),
-        (cols, others, phase, taken, rest1, sibling_rest1),
+        (others, phase, rest1, sibling_rest1),
         0,
         "rest",
         brief=True,

time: 34.6 us -> 34.2 us (0.988)
  Pallas kernels: 12.6 us -> 12.1 us
    pallas_call x11 -> x12, Pallas kernels: 12.6 us -> 12.1 us  [call(): pl.pallas_call(kernel, out_shape=out_shape, in_specs=in_specs, out_specs=...]
  transfers between devices with their start and end apart: 16 -> 16, of which waited for: 5 -> 5; matrix products, arithmetic and copies ran while one was open for 0% -> 0% of each run, Pallas kernels for 30% -> 28%
where the time goes in v18:
time: 34.2 us; the launch traced here: 34.1 us
  starting transfers between devices  15.7 us (46%)
  Pallas kernels  12.1 us (35%)
  waiting for transfers between devices  5.52 us (16%)
  between operations  0.77 us (2%)
    pallas_call x12, Pallas kernels, call(): pl.pallas_call(kernel, out_shape=out_shape, in_specs=in_specs, out_specs=...  12.1 us
    ppermute x7, starting transfers between devices, swap(): return lax.ppermute(value, 'dir', [(i, i ^ bits) for i in range(n_dir)])  5.55 us
    ppermute x6, starting transfers between devices, partner(): lax.ppermute(value, ('layer', 'dir'), [(i, i ^ n_dir ^ bits) for i in ran...  5.38 us
    ppermute x3, starting transfers between devices, per_device(): lax.ppermute(received[k], 'layer', [(i, i ^ 2 * k) for i in range(n_layer)])  4.76 us
    ppermute x3, waiting for transfers between devices, per_device(): lax.ppermute(received[k], 'layer', [(i, i ^ 2 * k) for i in range(n_layer)])  4.28 us
    ppermute x6, waiting for transfers between devices, partner(): lax.ppermute(value, ('layer', 'dir'), [(i, i ^ n_dir ^ bits) for i in ran...  1.22 us
  transfers between devices with their start and end apart: 16, of which 5 were waited for; matrix products, arithmetic and copies ran while one was open for 0% of the time, Pallas kernels for 28%

profile of v18, /device:TPU:0, one launch (start us, length us, event | category | flops | bytes accessed | tf_op | source)
XLA Modules:
  0.0 34.1 jit_solution(5987542423562774784)
XLA Ops:
  0.6 1.1 %split.1 = (bf16[3,128,128]{2,1,0:T(8,128)(2,1)S(1)}, bf16[3,128,128]{2,1,0:T(8,128)(2,1)S(1)}, bf16[3,128,128]{2,1,0:T(8,128)(2,1)S(1)}, bf16[3,128,128]{2,1,0:...) custom-call(bf16[3,128,512]{2,1,0:T(8,128)(2,1)} %refs_0_.1, ...), custom_call_target="tpu_custom_call" | custom-call | tf_op jit(solution)/shard_map/split/pallas_call | solution.py:42
  1.8 2.4 %collective-permute-start.1 = (bf16[3,128,128]{2,1,0:T(8,128)(2,1)S(1)}, bf16[3,128,128]{2,1,0:T(8,128)(2,1)S(1)}, u32[]{:S(2)}, u32[]{:S(2)}) collective-permute-start(bf16[3,128,128]{2,1,0:T(8,128)(2,1)S(1)} %get-tuple-element.65), channel_id=1, source_target_pairs={{0,3},{1,2},{2,1},{3,0},{4,7},{5,6},{6,5},{7,4},{8,11},{9,10},{10,... | collective-permute-start | bytes 294920 | tf_op jit(solution)/shard_map/ppermute | solution.py:497
  4.2 0.6 %collective-permute-start = (bf16[3,128,128]{2,1,0:T(8,128)(2,1)S(1)}, bf16[3,128,128]{2,1,0:T(8,128)(2,1)S(1)}, u32[]{:S(2)}, u32[]{:S(2)}) collective-permute-start(bf16[3,128,128]{2,1,0:T(8,128)(2,1)S(1)} %get-tuple-element.64.keep.refs_7_), channel_id=1, source_target_pairs={{0,2},{1,3},{2,0},{3,1},{4,6},{5,7},{6,4},{7,5},{8,10},{9,11},{10,... | collective-permute-start | bytes 294920 | tf_op jit(solution)/shard_map/ppermute | solution.py:497
  4.8 0.0 collective-permute-start.2
  4.9 1.7 %collective-permute-start.3 = (bf16[3,128,128]{2,1,0:T(8,128)(2,1)S(1)}, bf16[3,128,128]{2,1,0:T(8,128)(2,1)S(1)}, u32[]{:S(2)}, u32[]{:S(2)}) collective-permute-start(bf16[3,128,128]{2,1,0:T(8,128)(2,1)S(1)} %get-tuple-element.81.refs_3_), channel_id=1, source_target_pairs={{0,2},{1,3},{2,0},{3,1},{4,6},{5,7},{6,4},{7,5},{8,10},{9,11},{10,... | collective-permute-start | bytes 294920 | tf_op jit(solution)/shard_map/ppermute | solution.py:497
  6.6 0.1 collective-permute-start.4
  6.7 3.2 %weights.1 = (bf16[2,3,256,512]{3,2,1,0:T(8,128)(2,1)S(1)}, bf16[3,512,1280]{2,1,0:T(8,128)(2,1)S(1)}, s32[8,1280]{1,0:T(8,128)S(1)}, s32[8,1280]{1,0:T(8,128)S(...) custom-call(s32[2,3]{1,0:T(2,128)S(1)} %get-tuple-element.74.wind_he, ...), custom_call_target="tpu_custom_call" | custom-call | tf_op jit(solution)/shard_map/weights/pallas_call | solution.py:42
  9.9 0.0 collective-permute-done.1.diagonal.refs_5_.diagonal0
  9.9 0.4 %collective-permute-start.5 = (bf16[3,128,128]{2,1,0:T(8,128)(2,1)S(1)}, bf16[3,128,128]{2,1,0:T(8,128)(2,1)S(1)}, u32[]{:S(2)}, u32[]{:S(2)}) collective-permute-start(bf16[3,128,128]{2,1,0:T(8,128)(2,1)S(1)} %get-tuple-element.84), channel_id=1, source_target_pairs={{0,1},{1,0},{2,3},{3,2},{4,5},{5,4},{6,7},{7,6},{8,9},{9,8},{10,11... | collective-permute-start | bytes 294920 | tf_op jit(solution)/shard_map/ppermute | solution.py:497
  10.3 0.6 %rows_first.1 = (bf16[3,128,128]{2,1,0:T(8,128)(2,1)S(1)}, bf16[3,128,128]{2,1,0:T(8,128)(2,1)S(1)}, bf16[3,128,128]{2,1,0:T(8,128)(2,1)S(1)}, bf16[3,128,128]{2,1,0:T(8,128)(2,1)S(1)}) custom-call(bf16[2,3,256,512]{3,2,1,0:T(8,128)(2,1)S(1)} %get-tuple-element.70.rows_ref, bf16[3,128,128]{2,1,0:T(8,128)(2,1)S(1)} %collective-permute-done.across.refs_4_, ...), custom_call_target="tpu_custom_call" | custom-call | tf_op jit(solution)/shard_map/rows_first/pallas_call | solution.py:42
  10.9 1.8 %collective-permute-start.6 = (bf16[3,128,128]{2,1,0:T(8,128)(2,1)S(1)}, bf16[3,128,128]{2,1,0:T(8,128)(2,1)S(1)}, u32[]{:S(2)}, u32[]{:S(2)}) collective-permute-start(bf16[3,128,128]{2,1,0:T(8,128)(2,1)S(1)} %get-tuple-element.92), channel_id=1, source_target_pairs={{0,4},{1,5},{2,6},{3,7},{4,0},{5,1},{6,2},{7,3},{8,12},{9,13},{10,... | collective-permute-start | bytes 294920 | tf_op jit(solution)/shard_map/ppermute | solution.py:501
  12.7 0.0 collective-permute-start.7
  12.7 1.5 %strips.1 = (bf16[3,512,1280]{2,1,0:T(8,128)(2,1)S(1)}, bf16[32,128]{1,0:T(8,128)(2,1)S(1)}, bf16[32,128]{1,0:T(8,128)(2,1)S(1)}) custom-call(s32[2,3]{1,0:T(2,128)S(1)} %get-tuple-element.74.wind_held, s32[8,1280]{1,0:T(8,128)S(1)} %get-tuple-element.75.refs_0_, s32[8,1280]{1,0:T(8,128)S(1)} %get-tuple-element.76.refs_1_, ...), custom_call_target="tpu_custom_call" | custom-call | tf_op jit(solution)/shard_map/strips/pallas_call | solution.py:42
  14.2 0.6 %rows_later.1 = (bf16[3,128,128]{2,1,0:T(8,128)(2,1)S(1)}, bf16[3,192,256]{2,1,0:T(8,128)(2,1)S(1)}, bf16[224,128]{1,0:T(8,128)(2,1)S(1)}, bf16[224,128]{1,0:T(8...) custom-call(bf16[2,3,256,512]{3,2,1,0:T(8,128)(2,1)S(1)} %get-tuple-element.70.rows_ref, ...), custom_call_target="tpu_custom_call" | custom-call | tf_op jit(solution)/shard_map/rows_later/pallas_call | solution.py:42
  14.8 2.0 %collective-permute-start.11 = (bf16[224,128]{1,0:T(8,128)(2,1)S(1)}, bf16[224,128]{1,0:T(8,128)(2,1)S(1)}, u32[]{:S(2)}, u32[]{:S(2)}) collective-permute-start(bf16[224,128]{1,0:T(8,128)(2,1)S(1)} %get-tuple-element.99), channel_id=1, source_target_pairs={{0,4},{1,5},{2,6},{3,7},{4,0},{5,1},{6,2},{7,3},{8,12},{9,13},{10,... | collective-permute-start | bytes 172040 | tf_op jit(solution)/shard_map/ppermute | solution.py:501
  16.8 0.2 collective-permute-start.8
  17.0 0.8 %collective-permute-done.7.sibling_came = bf16[3,128,128]{2,1,0:T(8,128)(2,1)S(1)} collective-permute-done((bf16[3,128,128]{2,1,0:T(8,128)(2,1)S(1)}, bf16[3,128,128]{2,1,0:T(8,128)(2,1)S(1)}, u32[]{:S(2)}, u32[]{:S(2)}) %collective-permute-start.7) | collective-permute-done | bytes 98336 | tf_op jit(solution)/shard_map/ppermute | solution.py:501
  17.8 0.7 %phase.1 = f32[128,1280]{1,0:T(8,128)S(1)} custom-call(bf16[3,512,1280]{2,1,0:T(8,128)(2,1)S(1)} %get-tuple-element.80.mine_ref, bf16[3,512,1280]{2,1,0:T(8,128)(2,1)S(1)} %get-tuple-element.79.other_ref.cols_ref, bf16[3,128,128]{2,1,0:T(8,128)(2,1)S(1)} %get-tuple-element.90.mine0, bf16[3,128,128]{2,1,0:T(8,128)(2,1)S(1)} %get-tuple-element.91.mine1, ...), custom_call_target="tpu_custom_call" | custom-call | flops 10000000000 | bytes 8912896 | tf_op jit(solution)/shard_map/phase/pallas_call | solution.py:42
  18.5 1.2 %collective-permute-start.9 = (bf16[192,128]{1,0:T(8,128)(2,1)S(1)}, bf16[192,128]{1,0:T(8,128)(2,1)S(1)}, u32[]{:S(2)}, u32[]{:S(2)}) collective-permute-start(bf16[192,128]{1,0:T(8,128)(2,1)S(1)} %get-tuple-element.96), channel_id=1, source_target_pairs={{0,4},{1,5},{2,6},{3,7},{4,0},{5,1},{6,2},{7,3},{8,12},{9,13},{10,... | collective-permute-start | bytes 147464 | tf_op jit(solution)/shard_map/ppermute | solution.py:501
  19.8 0.3 collective-permute-start.10
  20.1 0.4 %taken.1.phase = f32[128,1280]{1,0:T(8,128)S(1)} custom-call(bf16[3,512,1280]{2,1,0:T(8,128)(2,1)S(1)} %get-tuple-element.80.mine_ref, f32[128,1280]{1,0:T(8,128)S(1)} %phase.1, bf16[3,192,256]{2,1,0:T(8,128)(2,1)S(1)} %collective-permute-done.8.taken), custom_call_target="tpu_custom_call" | custom-call | tf_op jit(solution)/shard_map/taken/pallas_call | solution.py:42
  20.5 0.4 %collective-permute-done.12.sibling_came = bf16[224,128]{1,0:T(8,128)(2,1)S(1)} collective-permute-done((bf16[224,128]{1,0:T(8,128)(2,1)S(1)}, bf16[224,128]{1,0:T(8,128)(2,1)S(1)}, u32[]{:S(2)}, u32[]{:S(2)}) %collective-permute-start.12) | collective-permute-done | bytes 57376 | tf_op jit(solution)/shard_map/ppermute | solution.py:501
  20.9 0.5 %far.1 = (bf16[32,1408]{1,0:T(8,128)(2,1)S(1)}, bf16[32,1408]{1,0:T(8,128)(2,1)S(1)}, bf16[64,128]{1,0:T(8,128)(2,1)S(1)}) custom-call(bf16[3,512,1280]{2,1,0:T(8,128)(2,1)S(1)} %get-tuple-element.79.other_ref.cols_ref, f32[128,1280]{1,0:T(8,128)S(1)} %taken.1.phase, bf16[224,128]{1,0:T(8,128)(2,1)S(1)} %collective-permute-done.11.came, ...), custom_call_target="tpu_custom_call" | custom-call | flops 300000000 | bytes 4898816 | tf_op jit(solution)/shard_map/far/pallas_call | solution.py:42
  21.4 3.7 %collective-permute-start.14 = (bf16[32,1408]{1,0:T(8,128)(2,1)S(1)}, bf16[32,1408]{1,0:T(8,128)(2,1)S(1)}, u32[]{:S(2)}, u32[]{:S(2)}) collective-permute-start(bf16[32,1408]{1,0:T(8,128)(2,1)S(1)} %get-tuple-element.106), channel_id=1, source_target_pairs={{0,24},{4,28},{8,16},{12,20},{16,8},{20,12},{24,0},{28,4},{1,25},{... | collective-permute-start | bytes 270344 | tf_op jit(solution)/shard_map/ppermute | solution.py:617
  25.1 0.5 %rest.1 = (bf16[32,1280]{1,0:T(8,128)(2,1)S(1)}, bf16[32,1280]{1,0:T(8,128)(2,1)S(1)}) custom-call(bf16[3,512,1280]{2,1,0:T(8,128)(2,1)S(1)} %get-tuple-element.79.other_ref.cols_ref, f32[128,1280]{1,0:T(8,128)S(1)} %taken.1.phase, bf16[192,128]{1,0:T(8,128)(2,1)S(1)} %collective-permute-done.9.came, bf16[192,128]{1,0:T(8,128)(2,1)S(1)} %collective-permute-done.10.sibling_came), custom_call_target="tpu_custom_call" | custom-call | tf_op jit(solution)/shard_map/rest/pallas_call | solution.py:42
  25.6 1.1 %collective-permute-start.15 = (bf16[32,1280]{1,0:T(8,128)(2,1)S(1)}, bf16[32,1280]{1,0:T(8,128)(2,1)S(1)}, u32[]{:S(2)}, u32[]{:S(2)}) collective-permute-start(bf16[32,1280]{1,0:T(8,128)(2,1)S(1)} %get-tuple-element.115), channel_id=1, source_target_pairs={{0,16},{4,20},{8,24},{12,28},{16,0},{20,4},{24,8},{28,12},{1,17},{... | collective-permute-start | bytes 245768 | tf_op jit(solution)/shard_map/ppermute | solution.py:617
  26.7 2.1 %collective-permute-done.14.refs_1_.refs_3_ = bf16[32,1408]{1,0:T(8,128)(2,1)S(1)} collective-permute-done((bf16[32,1408]{1,0:T(8,128)(2,1)S(1)}, bf16[32,1408]{1,0:T(8,128)(2,1)S(1)}, u32[]{:S(2)}, u32[]{:S(2)}) %collective-permute-start.14) | collective-permute-done | bytes 90144 | tf_op jit(solution)/shard_map/ppermute | solution.py:617
  28.8 0.6 %optics.1 = (f32[32,1280]{1,0:T(8,128)S(1)}, bf16[256,512]{1,0:T(8,128)(2,1)S(1)}, bf16[128,64]{1,0:T(8,128)(2,1)S(1)}) custom-call(f32[32,1280]{1,0:T(8,128)S(1)} %get-tuple-element.107.amplitude, f32[128,128]{1,0:T(8,128)S(1)} %get-tuple-element.108.ones, f32[256,512]{1,0:T(8,128)S(1)} %get-tuple-element.109.columns, f32[128,64]{1,0:T(8,128)S(1)} %get-tuple-element.110.lines), custom_call_target="tpu_custom_call" | custom-call | tf_op jit(solution)/shard_map/optics/pallas_call | solution.py:42
  29.4 1.8 %collective-permute-done.13.refs_0_.refs_1_ = bf16[32,1408]{1,0:T(8,128)(2,1)S(1)} collective-permute-done((bf16[32,1408]{1,0:T(8,128)(2,1)S(1)}, bf16[32,1408]{1,0:T(8,128)(2,1)S(1)}, u32[]{:S(2)}, u32[]{:S(2)}) %collective-permute-start.13) | collective-permute-done | bytes 90144 | tf_op jit(solution)/shard_map/ppermute | solution.py:617
  31.2 1.1 %shift.1.refs_7_ = bf16[3,128,512]{2,1,0:T(8,128)(2,1)S(1)} custom-call(s32[2,3]{1,0:T(2,128)S(1)} %get-tuple-element.74.wind_held, bf16[3,128,512]{2,1,0:T(8,128)(2,1)S(1)} %get-tuple-element.120.own, bf16[3,128,128]{2,1,0:T(8,128)(2,1)S(1)} %collective-permute-done.2.near.refs_6_.near0, bf16[3,128,128]{2,1,0:T(8,128)(2,1)S(1)} %collective-permute-done.5.refs_2_.near1, ...), custom_call_target="tpu_custom_call" | custom-call | tf_op jit(solution)/shard_map/shift/pallas_call | solution.py:42
  32.4 0.3 collective-permute-done.15.refs_2_
  32.7 1.3 %imaging.1 = (f32[64,2560]{1,0:T(8,128)}, bf16[3,128,512]{2,1,0:T(8,128)(2,1)}) custom-call(bf16[32,1280]{1,0:T(8,128)(2,1)S(1)} %get-tuple-element.98.refs_0_, bf16[32,1408]{1,0:T(8,128)(2,1)S(1)} %collective-permute-done.13.refs_0_.refs_1_, bf16[32,1280]{1,0:T(8,128)(2,1)S(1)} %collective-permute-done.15.refs_2_, ...), custom_call_target="tpu_custom_call" | custom-call | flops 400000000 | bytes 2228224 | tf_op jit(solution)/shard_map/imaging/pallas_call | solution.py:42
  (12 shorter events, 0.0 us)
Async XLA Ops:
  1.8 8.1 %collective-permute-start.1 = (bf16[3,128,128]{2,1,0:T(8,128)(2,1)S(1)}, bf16[3,128,128]{2,1,0:T(8,128)(2,1)S(1)}, u32[]{:S(2)}, u32[]{:S(2)}) collective-permute-start(bf16[3,128,128]{2,1,0:T(8,128)(2,1)S(1)} %get-tuple-element.65), channel_id=1, source_target_pairs={{0,3},{1,2},{2,1},{3,0},{4,7},{5,6},{6,5},{7,4},{8,11},{9,10},{10,... | collective-permute-start | bytes 294920 | tf_op jit(solution)/shard_map/ppermute | solution.py:497
  4.2 6.1 %collective-permute-start = (bf16[3,128,128]{2,1,0:T(8,128)(2,1)S(1)}, bf16[3,128,128]{2,1,0:T(8,128)(2,1)S(1)}, u32[]{:S(2)}, u32[]{:S(2)}) collective-permute-start(bf16[3,128,128]{2,1,0:T(8,128)(2,1)S(1)} %get-tuple-element.64.keep.refs_7_), channel_id=1, source_target_pairs={{0,2},{1,3},{2,0},{3,1},{4,6},{5,7},{6,4},{7,5},{8,10},{9,11},{10,... | collective-permute-start | bytes 294920 | tf_op jit(solution)/shard_map/ppermute | solution.py:497
  4.8 5.4 %collective-permute-start.2 = (bf16[3,128,128]{2,1,0:T(8,128)(2,1)S(1)}, bf16[3,128,128]{2,1,0:T(8,128)(2,1)S(1)}, u32[]{:S(2)}, u32[]{:S(2)}) collective-permute-start(bf16[3,128,128]{2,1,0:T(8,128)(2,1)S(1)} %get-tuple-element.65), channel_id=1, source_target_pairs={{0,1},{1,0},{2,3},{3,2},{4,5},{5,4},{6,7},{7,6},{8,9},{9,8},{10,11... | collective-permute-start | bytes 294920 | tf_op jit(solution)/shard_map/ppermute | solution.py:497
  4.9 9.3 %collective-permute-start.3 = (bf16[3,128,128]{2,1,0:T(8,128)(2,1)S(1)}, bf16[3,128,128]{2,1,0:T(8,128)(2,1)S(1)}, u32[]{:S(2)}, u32[]{:S(2)}) collective-permute-start(bf16[3,128,128]{2,1,0:T(8,128)(2,1)S(1)} %get-tuple-element.81.refs_3_), channel_id=1, source_target_pairs={{0,2},{1,3},{2,0},{3,1},{4,6},{5,7},{6,4},{7,5},{8,10},{9,11},{10,... | collective-permute-start | bytes 294920 | tf_op jit(solution)/shard_map/ppermute | solution.py:497
  6.6 7.6 %collective-permute-start.4 = (bf16[3,128,128]{2,1,0:T(8,128)(2,1)S(1)}, bf16[3,128,128]{2,1,0:T(8,128)(2,1)S(1)}, u32[]{:S(2)}, u32[]{:S(2)}) collective-permute-start(bf16[3,128,128]{2,1,0:T(8,128)(2,1)S(1)} %get-tuple-element.84), channel_id=1, source_target_pairs={{0,3},{1,2},{2,1},{3,0},{4,7},{5,6},{6,5},{7,4},{8,11},{9,10},{10,... | collective-permute-start | bytes 294920 | tf_op jit(solution)/shard_map/ppermute | solution.py:497
  9.9 4.3 %collective-permute-start.5 = (bf16[3,128,128]{2,1,0:T(8,128)(2,1)S(1)}, bf16[3,128,128]{2,1,0:T(8,128)(2,1)S(1)}, u32[]{:S(2)}, u32[]{:S(2)}) collective-permute-start(bf16[3,128,128]{2,1,0:T(8,128)(2,1)S(1)} %get-tuple-element.84), channel_id=1, source_target_pairs={{0,1},{1,0},{2,3},{3,2},{4,5},{5,4},{6,7},{7,6},{8,9},{9,8},{10,11... | collective-permute-start | bytes 294920 | tf_op jit(solution)/shard_map/ppermute | solution.py:497
  10.9 6.2 %collective-permute-start.6 = (bf16[3,128,128]{2,1,0:T(8,128)(2,1)S(1)}, bf16[3,128,128]{2,1,0:T(8,128)(2,1)S(1)}, u32[]{:S(2)}, u32[]{:S(2)}) collective-permute-start(bf16[3,128,128]{2,1,0:T(8,128)(2,1)S(1)} %get-tuple-element.92), channel_id=1, source_target_pairs={{0,4},{1,5},{2,6},{3,7},{4,0},{5,1},{6,2},{7,3},{8,12},{9,13},{10,... | collective-permute-start | bytes 294920 | tf_op jit(solution)/shard_map/ppermute | solution.py:501
  12.7 5.1 %collective-permute-start.7 = (bf16[3,128,128]{2,1,0:T(8,128)(2,1)S(1)}, bf16[3,128,128]{2,1,0:T(8,128)(2,1)S(1)}, u32[]{:S(2)}, u32[]{:S(2)}) collective-permute-start(bf16[3,128,128]{2,1,0:T(8,128)(2,1)S(1)} %get-tuple-element.93), channel_id=1, source_target_pairs={{0,5},{1,4},{2,7},{3,6},{4,1},{5,0},{6,3},{7,2},{8,13},{9,12},{10,... | collective-permute-start | bytes 294920 | tf_op jit(solution)/shard_map/ppermute | solution.py:501
  14.8 5.7 %collective-permute-start.11 = (bf16[224,128]{1,0:T(8,128)(2,1)S(1)}, bf16[224,128]{1,0:T(8,128)(2,1)S(1)}, u32[]{:S(2)}, u32[]{:S(2)}) collective-permute-start(bf16[224,128]{1,0:T(8,128)(2,1)S(1)} %get-tuple-element.99), channel_id=1, source_target_pairs={{0,4},{1,5},{2,6},{3,7},{4,0},{5,1},{6,2},{7,3},{8,12},{9,13},{10,... | collective-permute-start | bytes 172040 | tf_op jit(solution)/shard_map/ppermute | solution.py:501
  16.8 4.1 %collective-permute-start.12 = (bf16[224,128]{1,0:T(8,128)(2,1)S(1)}, bf16[224,128]{1,0:T(8,128)(2,1)S(1)}, u32[]{:S(2)}, u32[]{:S(2)}) collective-permute-start(bf16[224,128]{1,0:T(8,128)(2,1)S(1)} %get-tuple-element.100), channel_id=1, source_target_pairs={{0,5},{1,4},{2,7},{3,6},{4,1},{5,0},{6,3},{7,2},{8,13},{9,12},{10,... | collective-permute-start | bytes 172040 | tf_op jit(solution)/shard_map/ppermute | solution.py:501
  16.8 3.2 %collective-permute-start.8 = (bf16[3,192,256]{2,1,0:T(8,128)(2,1)S(1)}, bf16[3,192,256]{2,1,0:T(8,128)(2,1)S(1)}, u32[]{:S(2)}, u32[]{:S(2)}) collective-permute-start(bf16[3,192,256]{2,1,0:T(8,128)(2,1)S(1)} %get-tuple-element.95), channel_id=1, source_target_pairs={{0,1},{1,0},{2,3},{3,2},{4,5},{5,4},{6,7},{7,6},{8,9},{9,8},{10,11... | collective-permute-start | bytes 884744 | tf_op jit(solution)/shard_map/ppermute | solution.py:497
  18.5 6.6 %collective-permute-start.9 = (bf16[192,128]{1,0:T(8,128)(2,1)S(1)}, bf16[192,128]{1,0:T(8,128)(2,1)S(1)}, u32[]{:S(2)}, u32[]{:S(2)}) collective-permute-start(bf16[192,128]{1,0:T(8,128)(2,1)S(1)} %get-tuple-element.96), channel_id=1, source_target_pairs={{0,4},{1,5},{2,6},{3,7},{4,0},{5,1},{6,2},{7,3},{8,12},{9,13},{10,... | collective-permute-start | bytes 147464 | tf_op jit(solution)/shard_map/ppermute | solution.py:501
  19.8 5.3 %collective-permute-start.10 = (bf16[192,128]{1,0:T(8,128)(2,1)S(1)}, bf16[192,128]{1,0:T(8,128)(2,1)S(1)}, u32[]{:S(2)}, u32[]{:S(2)}) collective-permute-start(bf16[192,128]{1,0:T(8,128)(2,1)S(1)} %get-tuple-element.97), channel_id=1, source_target_pairs={{0,5},{1,4},{2,7},{3,6},{4,1},{5,0},{6,3},{7,2},{8,13},{9,12},{10,... | collective-permute-start | bytes 147464 | tf_op jit(solution)/shard_map/ppermute | solution.py:501
  21.4 7.4 %collective-permute-start.14 = (bf16[32,1408]{1,0:T(8,128)(2,1)S(1)}, bf16[32,1408]{1,0:T(8,128)(2,1)S(1)}, u32[]{:S(2)}, u32[]{:S(2)}) collective-permute-start(bf16[32,1408]{1,0:T(8,128)(2,1)S(1)} %get-tuple-element.106), channel_id=1, source_target_pairs={{0,24},{4,28},{8,16},{12,20},{16,8},{20,12},{24,0},{28,4},{1,25},{... | collective-permute-start | bytes 270344 | tf_op jit(solution)/shard_map/ppermute | solution.py:617
  25.1 6.2 %collective-permute-start.13 = (bf16[32,1408]{1,0:T(8,128)(2,1)S(1)}, bf16[32,1408]{1,0:T(8,128)(2,1)S(1)}, u32[]{:S(2)}, u32[]{:S(2)}) collective-permute-start(bf16[32,1408]{1,0:T(8,128)(2,1)S(1)} %get-tuple-element.101), channel_id=1, source_target_pairs={{0,8},{4,12},{8,0},{12,4},{16,24},{20,28},{24,16},{28,20},{1,9},{5... | collective-permute-start | bytes 270344 | tf_op jit(solution)/shard_map/ppermute | solution.py:617
  25.6 7.2 %collective-permute-start.15 = (bf16[32,1280]{1,0:T(8,128)(2,1)S(1)}, bf16[32,1280]{1,0:T(8,128)(2,1)S(1)}, u32[]{:S(2)}, u32[]{:S(2)}) collective-permute-start(bf16[32,1280]{1,0:T(8,128)(2,1)S(1)} %get-tuple-element.115), channel_id=1, source_target_pairs={{0,16},{4,20},{8,24},{12,28},{16,0},{20,4},{24,8},{28,12},{1,17},{... | collective-permute-start | bytes 245768 | tf_op jit(solution)/shard_map/ppermute | solution.py:617

commit v19 on v18

--- a/solution.py
+++ b/solution.py
@@ -124,7 +124,8 @@
     step = row // block
     for at, value in enumerate(send_order(n_layer // 2)):
         step = jnp.where(row // block == at, value, step)
-    pair = jnp.bitwise_xor(step, column // 2)
+    pair = step + column // 2
+    pair = jnp.where(pair >= n_layer // 2, pair - n_layer // 2, pair)
     parity = lax.rem(column, 2)
     inside = lax.rem(row, block) + pair * (2 * block)
     pixel_rows = stack(inside + parity * block, inside + (1 - parity) * block)
@@ -316,21 +317,8 @@
             out[:, at : at + 256] = total[k * block : (k + 1) * block]
 
 
-def strip_steps(pairs):
-    return [2**k - 1 for k in range(1, pairs.bit_length())]
-
-
 def send_order(pairs):
-    steps = strip_steps(pairs)
-    return [k for k in range(pairs) if k not in steps] + steps
-
-
-def add_strip(pairs, step, strips, out):
-    pair = lax.axis_index("layer") // 2
-    after = lax.rem(pair + 1, pairs) == jnp.bitwise_xor(pair, step)
-    at = out.shape[1] - strips.shape[1]
-    last, first = strips[:STRIP].astype(jnp.float32), strips[STRIP:].astype(jnp.float32)
-    out[:, at:] = jnp.where(after, last, first).astype(jnp.bfloat16)
+    return [0, *range(2, pairs - 1), 1, pairs - 1]
 
 
 def far_kernel(cols_ref, phase, came, sibling_came, *outs):
@@ -342,11 +330,11 @@
     odd = lax.rem(lax.axis_index("dir"), 2) == 1
     here = get_strip(came, layers * size).astype(jnp.float32)
     there = get_strip(sibling_came, layers * size).astype(jnp.float32)
-    strips[:STRIP] = jnp.where(odd, here, there).astype(jnp.bfloat16)
-    strips[STRIP:] = jnp.where(odd, there, here).astype(jnp.bfloat16)
-    pairs = half // outs[0].shape[0]
-    for out, step in zip(outs, strip_steps(pairs)):
-        add_strip(pairs, step, strips, out)
+    last = jnp.where(odd, here, there).astype(jnp.bfloat16)
+    first = jnp.where(odd, there, here).astype(jnp.bfloat16)
+    strips[:STRIP], strips[STRIP:] = last, first
+    for out, strip in zip(outs, (last, first)):
+        out[:, phase.shape[1] :] = strip
 
 
 def rest_kernel(cols_ref, phase, came, sibling_came, *outs):
@@ -362,22 +350,15 @@
     return pltpu.roll(stack(before, own, after), shift, 0)[16 : 16 + rows]
 
 
-def shift_kernel(wind_held, own, near0, near1, diagonal0, diagonal1, taken, partner_strips, *refs):
-    messages, (out, wind, sem) = refs[:-3], refs[-3:]
+def shift_kernel(wind_held, own, near0, near1, diagonal0, diagonal1, taken, partner_strips, before, after, out, wind, sem):
     load = fetch((wind_held, wind, sem))[0]
     layers, rows, cols = own.shape
     odd = lax.rem(lax.axis_index("dir"), 2) == 1
     half = taken.shape[1] - 64
-    pairs = 2 ** len(messages)
-    pair, second = lax.axis_index("layer") // 2, lax.rem(lax.axis_index("layer"), 2) == 1
-    before = jnp.bitwise_xor(pair, lax.rem(pair + pairs - 1, pairs))
-    after = jnp.bitwise_xor(pair, lax.rem(pair + 1, pairs))
-    left = partner_strips[:STRIP].astype(jnp.float32)
-    right = partner_strips[STRIP:].astype(jnp.float32)
-    for step, message in zip(strip_steps(pairs), messages):
-        strip = message[:, message.shape[1] - rows :].astype(jnp.float32)
-        left = jnp.where(jnp.logical_and(before == step, jnp.logical_not(second)), strip, left)
-        right = jnp.where(jnp.logical_and(after == step, second), strip, right)
+    second = lax.rem(lax.axis_index("layer"), 2) == 1
+    at = before.shape[1] - rows
+    left = jnp.where(second, partner_strips[:STRIP].astype(jnp.float32), before[:, at:].astype(jnp.float32))
+    right = jnp.where(second, after[:, at:].astype(jnp.float32), partner_strips[STRIP:].astype(jnp.float32))
     strips = stack(left, right, jnp.zeros((LANES - 2 * STRIP, rows), jnp.float32)).T
     lane = lax.broadcasted_iota(jnp.int32, (rows, LANES), 1)
     load.wait()
@@ -565,8 +546,7 @@
         scratch=wind_scratch,
         brief=True,
     )
-    steps = strip_steps(pairs)
-    far = len(steps) * rows
+    far = 2 * rows
     message = shape(layers * far + STRIP * rows_dev // LANES, width)
     remainder = shape(layers * (half - far), width)
     mine1, give, far1, sibling_far1, rest1, sibling_rest1 = call(
@@ -599,14 +579,14 @@
     )
     *far_sums, strips = call(
         far_kernel,
-        [shape(rows, pupil_cols + rows_dev)] * len(steps) + [shape(2 * STRIP, rows_dev)],
+        [shape(rows, pupil_cols + rows_dev)] * 2 + [shape(2 * STRIP, rows_dev)],
         (others, phase, far1, sibling_far1),
         300_000_000,
         "far",
     )
     rest_sums = call(
         rest_kernel,
-        [shape(rows, pupil_cols)] * (pairs - len(steps)),
+        [shape(rows, pupil_cols)] * (pairs - 2),
         (others, phase, rest1, sibling_rest1),
         0,
         "rest",
@@ -614,10 +594,10 @@
     )
     received = dict(zip(send_order(pairs), [*rest_sums, *far_sums]))
     for k in range(1, pairs):
-        received[k] = lax.ppermute(received[k], "layer", [(i, i ^ (2 * k)) for i in range(n_layer)])
+        received[k] = turn(received[k], 2 * k)
     received = [received[k] for k in range(pairs)]
 
-    optics_in, received[-1] = lax.optimization_barrier((optics_in, received[-1]))
+    optics_in, received[1] = lax.optimization_barrier((optics_in, received[1]))
     optics = call(
         optics_kernel,
         (
@@ -630,11 +610,11 @@
         "optics",
         brief=True,
     )
-    received[1], optics = lax.optimization_barrier((received[1], optics))
+    received[-1], optics = lax.optimization_barrier((received[-1], optics))
     shifted = call(
         shift_kernel,
         shape(layers, rows_dev, cols_dev),
-        (wind, own, near0, near1, diagonal0, diagonal1, taken, strips, *[received[k] for k in steps]),
+        (wind, own, near0, near1, diagonal0, diagonal1, taken, strips, received[1], received[-1]),
         0,
         "shift",
         scratch=wind_scratch,

time: 34.2 us -> 35 us (1.023)
  waiting for transfers between devices: 5.52 us -> 6.3 us
    ppermute x3, waiting for transfers between devices: 4.28 us -> 5.06 us  [turn(): lax.ppermute(value, 'layer', [(i, (i + step) % n_layer) for i in range(n_...]
where the time goes in v19:
time: 35 us; the launch traced here: 34.8 us
  starting transfers between devices  15.7 us (45%)
  Pallas kernels  12.1 us (35%)
  waiting for transfers between devices  6.3 us (18%)
  between operations  0.76 us (2%)
    pallas_call x12, Pallas kernels, call(): pl.pallas_call(kernel, out_shape=out_shape, in_specs=in_specs, out_specs=...  12.1 us
    ppermute x7, starting transfers between devices, swap(): return lax.ppermute(value, 'dir', [(i, i ^ bits) for i in range(n_dir)])  5.55 us
    ppermute x6, starting transfers between devices, partner(): lax.ppermute(value, ('layer', 'dir'), [(i, i ^ n_dir ^ bits) for i in ran...  5.38 us
    ppermute x3, waiting for transfers between devices, turn(): lax.ppermute(value, 'layer', [(i, (i + step) % n_layer) for i in range(n_...  5.06 us
    ppermute x3, starting transfers between devices, turn(): lax.ppermute(value, 'layer', [(i, (i + step) % n_layer) for i in range(n_...  4.76 us
    ppermute x6, waiting for transfers between devices, partner(): lax.ppermute(value, ('layer', 'dir'), [(i, i ^ n_dir ^ bits) for i in ran...  1.22 us
  transfers between devices with their start and end apart: 16, of which 5 were waited for; matrix products, arithmetic and copies ran while one was open for 0% of the time, Pallas kernels for 28%

profile of v19, /device:TPU:0, one launch (start us, length us, event | category | flops | bytes accessed | tf_op | source)
XLA Modules:
  0.0 34.8 jit_solution(16316601601046130634)
XLA Ops:
  0.6 1.1 %split.1 = (bf16[3,128,128]{2,1,0:T(8,128)(2,1)S(1)}, bf16[3,128,128]{2,1,0:T(8,128)(2,1)S(1)}, bf16[3,128,128]{2,1,0:T(8,128)(2,1)S(1)}, bf16[3,128,128]{2,1,0:...) custom-call(bf16[3,128,512]{2,1,0:T(8,128)(2,1)} %refs_0_.1, ...), custom_call_target="tpu_custom_call" | custom-call | tf_op jit(solution)/shard_map/split/pallas_call | solution.py:42
  1.8 2.4 %collective-permute-start.1 = (bf16[3,128,128]{2,1,0:T(8,128)(2,1)S(1)}, bf16[3,128,128]{2,1,0:T(8,128)(2,1)S(1)}, u32[]{:S(2)}, u32[]{:S(2)}) collective-permute-start(bf16[3,128,128]{2,1,0:T(8,128)(2,1)S(1)} %get-tuple-element.65), channel_id=1, source_target_pairs={{0,3},{1,2},{2,1},{3,0},{4,7},{5,6},{6,5},{7,4},{8,11},{9,10},{10,... | collective-permute-start | bytes 294920 | tf_op jit(solution)/shard_map/ppermute | solution.py:478
  4.2 0.6 %collective-permute-start = (bf16[3,128,128]{2,1,0:T(8,128)(2,1)S(1)}, bf16[3,128,128]{2,1,0:T(8,128)(2,1)S(1)}, u32[]{:S(2)}, u32[]{:S(2)}) collective-permute-start(bf16[3,128,128]{2,1,0:T(8,128)(2,1)S(1)} %get-tuple-element.64.keep.refs_7_), channel_id=1, source_target_pairs={{0,2},{1,3},{2,0},{3,1},{4,6},{5,7},{6,4},{7,5},{8,10},{9,11},{10,... | collective-permute-start | bytes 294920 | tf_op jit(solution)/shard_map/ppermute | solution.py:478
  4.8 0.0 collective-permute-start.2
  4.9 1.7 %collective-permute-start.3 = (bf16[3,128,128]{2,1,0:T(8,128)(2,1)S(1)}, bf16[3,128,128]{2,1,0:T(8,128)(2,1)S(1)}, u32[]{:S(2)}, u32[]{:S(2)}) collective-permute-start(bf16[3,128,128]{2,1,0:T(8,128)(2,1)S(1)} %get-tuple-element.81.refs_3_), channel_id=1, source_target_pairs={{0,2},{1,3},{2,0},{3,1},{4,6},{5,7},{6,4},{7,5},{8,10},{9,11},{10,... | collective-permute-start | bytes 294920 | tf_op jit(solution)/shard_map/ppermute | solution.py:478
  6.6 0.1 collective-permute-start.4
  6.7 3.2 %weights.1 = (bf16[2,3,256,512]{3,2,1,0:T(8,128)(2,1)S(1)}, bf16[3,512,1280]{2,1,0:T(8,128)(2,1)S(1)}, s32[8,1280]{1,0:T(8,128)S(1)}, s32[8,1280]{1,0:T(8,128)S(...) custom-call(s32[2,3]{1,0:T(2,128)S(1)} %get-tuple-element.74.wind_he, ...), custom_call_target="tpu_custom_call" | custom-call | tf_op jit(solution)/shard_map/weights/pallas_call | solution.py:42
  9.9 0.4 %collective-permute-start.5 = (bf16[3,128,128]{2,1,0:T(8,128)(2,1)S(1)}, bf16[3,128,128]{2,1,0:T(8,128)(2,1)S(1)}, u32[]{:S(2)}, u32[]{:S(2)}) collective-permute-start(bf16[3,128,128]{2,1,0:T(8,128)(2,1)S(1)} %get-tuple-element.84), channel_id=1, source_target_pairs={{0,1},{1,0},{2,3},{3,2},{4,5},{5,4},{6,7},{7,6},{8,9},{9,8},{10,11... | collective-permute-start | bytes 294920 | tf_op jit(solution)/shard_map/ppermute | solution.py:478
  10.3 0.0 collective-permute-done.2.near.refs_6_.near0
  10.3 0.6 %rows_first.1 = (bf16[3,128,128]{2,1,0:T(8,128)(2,1)S(1)}, bf16[3,128,128]{2,1,0:T(8,128)(2,1)S(1)}, bf16[3,128,128]{2,1,0:T(8,128)(2,1)S(1)}, bf16[3,128,128]{2,1,0:T(8,128)(2,1)S(1)}) custom-call(bf16[2,3,256,512]{3,2,1,0:T(8,128)(2,1)S(1)} %get-tuple-element.70.rows_ref, bf16[3,128,128]{2,1,0:T(8,128)(2,1)S(1)} %collective-permute-done.across.refs_4_, ...), custom_call_target="tpu_custom_call" | custom-call | tf_op jit(solution)/shard_map/rows_first/pallas_call | solution.py:42
  10.9 1.8 %collective-permute-start.6 = (bf16[3,128,128]{2,1,0:T(8,128)(2,1)S(1)}, bf16[3,128,128]{2,1,0:T(8,128)(2,1)S(1)}, u32[]{:S(2)}, u32[]{:S(2)}) collective-permute-start(bf16[3,128,128]{2,1,0:T(8,128)(2,1)S(1)} %get-tuple-element.92), channel_id=1, source_target_pairs={{0,4},{1,5},{2,6},{3,7},{4,0},{5,1},{6,2},{7,3},{8,12},{9,13},{10,... | collective-permute-start | bytes 294920 | tf_op jit(solution)/shard_map/ppermute | solution.py:482
  12.7 1.5 %strips.1 = (bf16[3,512,1280]{2,1,0:T(8,128)(2,1)S(1)}, bf16[32,128]{1,0:T(8,128)(2,1)S(1)}, bf16[32,128]{1,0:T(8,128)(2,1)S(1)}) custom-call(s32[2,3]{1,0:T(2,128)S(1)} %get-tuple-element.74.wind_held, s32[8,1280]{1,0:T(8,128)S(1)} %get-tuple-element.75.refs_0_, s32[8,1280]{1,0:T(8,128)S(1)} %get-tuple-element.76.refs_1_, ...), custom_call_target="tpu_custom_call" | custom-call | tf_op jit(solution)/shard_map/strips/pallas_call | solution.py:42
  14.2 0.6 %rows_later.1 = (bf16[3,128,128]{2,1,0:T(8,128)(2,1)S(1)}, bf16[3,192,256]{2,1,0:T(8,128)(2,1)S(1)}, bf16[224,128]{1,0:T(8,128)(2,1)S(1)}, bf16[224,128]{1,0:T(8...) custom-call(bf16[2,3,256,512]{3,2,1,0:T(8,128)(2,1)S(1)} %get-tuple-element.70.rows_ref, ...), custom_call_target="tpu_custom_call" | custom-call | tf_op jit(solution)/shard_map/rows_later/pallas_call | solution.py:42
  14.8 2.0 %collective-permute-start.11 = (bf16[224,128]{1,0:T(8,128)(2,1)S(1)}, bf16[224,128]{1,0:T(8,128)(2,1)S(1)}, u32[]{:S(2)}, u32[]{:S(2)}) collective-permute-start(bf16[224,128]{1,0:T(8,128)(2,1)S(1)} %get-tuple-element.103), channel_id=1, source_target_pairs={{0,4},{1,5},{2,6},{3,7},{4,0},{5,1},{6,2},{7,3},{8,12},{9,13},{10,... | collective-permute-start | bytes 172040 | tf_op jit(solution)/shard_map/ppermute | solution.py:482
  16.8 0.2 collective-permute-start.8
  17.0 0.8 %collective-permute-done.7.sibling_came = bf16[3,128,128]{2,1,0:T(8,128)(2,1)S(1)} collective-permute-done((bf16[3,128,128]{2,1,0:T(8,128)(2,1)S(1)}, bf16[3,128,128]{2,1,0:T(8,128)(2,1)S(1)}, u32[]{:S(2)}, u32[]{:S(2)}) %collective-permute-start.7) | collective-permute-done | bytes 98336 | tf_op jit(solution)/shard_map/ppermute | solution.py:482
  17.8 0.7 %phase.1 = f32[128,1280]{1,0:T(8,128)S(1)} custom-call(bf16[3,512,1280]{2,1,0:T(8,128)(2,1)S(1)} %get-tuple-element.80.mine_ref, bf16[3,512,1280]{2,1,0:T(8,128)(2,1)S(1)} %get-tuple-element.79.other_ref.cols_ref, bf16[3,128,128]{2,1,0:T(8,128)(2,1)S(1)} %get-tuple-element.90.mine0, bf16[3,128,128]{2,1,0:T(8,128)(2,1)S(1)} %get-tuple-element.91.mine1, ...), custom_call_target="tpu_custom_call" | custom-call | flops 10000000000 | bytes 8912896 | tf_op jit(solution)/shard_map/phase/pallas_call | solution.py:42
  18.5 1.2 %collective-permute-start.9 = (bf16[192,128]{1,0:T(8,128)(2,1)S(1)}, bf16[192,128]{1,0:T(8,128)(2,1)S(1)}, u32[]{:S(2)}, u32[]{:S(2)}) collective-permute-start(bf16[192,128]{1,0:T(8,128)(2,1)S(1)} %get-tuple-element.96), channel_id=1, source_target_pairs={{0,4},{1,5},{2,6},{3,7},{4,0},{5,1},{6,2},{7,3},{8,12},{9,13},{10,... | collective-permute-start | bytes 147464 | tf_op jit(solution)/shard_map/ppermute | solution.py:482
  19.8 0.3 collective-permute-start.10
  20.1 0.4 %taken.1.phase = f32[128,1280]{1,0:T(8,128)S(1)} custom-call(bf16[3,512,1280]{2,1,0:T(8,128)(2,1)S(1)} %get-tuple-element.80.mine_ref, f32[128,1280]{1,0:T(8,128)S(1)} %phase.1, bf16[3,192,256]{2,1,0:T(8,128)(2,1)S(1)} %collective-permute-done.8.taken), custom_call_target="tpu_custom_call" | custom-call | tf_op jit(solution)/shard_map/taken/pallas_call | solution.py:42
  20.5 0.4 %collective-permute-done.12.sibling_came = bf16[224,128]{1,0:T(8,128)(2,1)S(1)} collective-permute-done((bf16[224,128]{1,0:T(8,128)(2,1)S(1)}, bf16[224,128]{1,0:T(8,128)(2,1)S(1)}, u32[]{:S(2)}, u32[]{:S(2)}) %collective-permute-start.12) | collective-permute-done | bytes 57376 | tf_op jit(solution)/shard_map/ppermute | solution.py:482
  20.9 0.5 %far.1 = (bf16[32,1408]{1,0:T(8,128)(2,1)S(1)}, bf16[32,1408]{1,0:T(8,128)(2,1)S(1)}, bf16[64,128]{1,0:T(8,128)(2,1)S(1)}) custom-call(bf16[3,512,1280]{2,1,0:T(8,128)(2,1)S(1)} %get-tuple-element.79.other_ref.cols_ref, f32[128,1280]{1,0:T(8,128)S(1)} %taken.1.phase, bf16[224,128]{1,0:T(8,128)(2,1)S(1)} %collective-permute-done.11.came, ...), custom_call_target="tpu_custom_call" | custom-call | flops 300000000 | bytes 4898816 | tf_op jit(solution)/shard_map/far/pallas_call | solution.py:42
  21.4 1.6 %collective-permute-start.13 = (bf16[32,1408]{1,0:T(8,128)(2,1)S(1)}, bf16[32,1408]{1,0:T(8,128)(2,1)S(1)}, u32[]{:S(2)}, u32[]{:S(2)}) collective-permute-start(bf16[32,1408]{1,0:T(8,128)(2,1)S(1)} %get-tuple-element.105), channel_id=1, source_target_pairs={{0,8},{4,12},{8,16},{12,20},{16,24},{20,28},{24,0},{28,4},{1,9},{5... | collective-permute-start | bytes 270344 | tf_op jit(solution)/shard_map/ppermute | solution.py:485
  23.0 2.2 %collective-permute-start.15 = (bf16[32,1408]{1,0:T(8,128)(2,1)S(1)}, bf16[32,1408]{1,0:T(8,128)(2,1)S(1)}, u32[]{:S(2)}, u32[]{:S(2)}) collective-permute-start(bf16[32,1408]{1,0:T(8,128)(2,1)S(1)} %get-tuple-element.108), channel_id=1, source_target_pairs={{0,24},{4,28},{8,0},{12,4},{16,8},{20,12},{24,16},{28,20},{1,25},{... | collective-permute-start | bytes 270344 | tf_op jit(solution)/shard_map/ppermute | solution.py:485
  25.3 0.5 %rest.1 = (bf16[32,1280]{1,0:T(8,128)(2,1)S(1)}, bf16[32,1280]{1,0:T(8,128)(2,1)S(1)}) custom-call(bf16[3,512,1280]{2,1,0:T(8,128)(2,1)S(1)} %get-tuple-element.79.other_ref.cols_ref, f32[128,1280]{1,0:T(8,128)S(1)} %taken.1.phase, bf16[192,128]{1,0:T(8,128)(2,1)S(1)} %collective-permute-done.9.came, bf16[192,128]{1,0:T(8,128)(2,1)S(1)} %collective-permute-done.10.sibling_came), custom_call_target="tpu_custom_call" | custom-call | tf_op jit(solution)/shard_map/rest/pallas_call | solution.py:42
  25.8 0.9 %collective-permute-start.14 = (bf16[32,1280]{1,0:T(8,128)(2,1)S(1)}, bf16[32,1280]{1,0:T(8,128)(2,1)S(1)}, u32[]{:S(2)}, u32[]{:S(2)}) collective-permute-start(bf16[32,1280]{1,0:T(8,128)(2,1)S(1)} %get-tuple-element.107), channel_id=1, source_target_pairs={{0,16},{4,20},{8,24},{12,28},{16,0},{20,4},{24,8},{28,12},{1,17},{... | collective-permute-start | bytes 245768 | tf_op jit(solution)/shard_map/ppermute | solution.py:485
  26.7 1.9 %collective-permute-done.13.before.refs_1_ = bf16[32,1408]{1,0:T(8,128)(2,1)S(1)} collective-permute-done((bf16[32,1408]{1,0:T(8,128)(2,1)S(1)}, bf16[32,1408]{1,0:T(8,128)(2,1)S(1)}, u32[]{:S(2)}, u32[]{:S(2)}) %collective-permute-start.13) | collective-permute-done | bytes 90144 | tf_op jit(solution)/shard_map/ppermute | solution.py:485
  28.6 0.6 %optics.1 = (f32[32,1280]{1,0:T(8,128)S(1)}, bf16[256,512]{1,0:T(8,128)(2,1)S(1)}, bf16[128,64]{1,0:T(8,128)(2,1)S(1)}) custom-call(f32[32,1280]{1,0:T(8,128)S(1)} %get-tuple-element.109.amplitude, f32[128,128]{1,0:T(8,128)S(1)} %get-tuple-element.110.ones, f32[256,512]{1,0:T(8,128)S(1)} %get-tuple-element.111.columns, f32[128,64]{1,0:T(8,128)S(1)} %get-tuple-element.112.lines), custom_call_target="tpu_custom_call" | custom-call | tf_op jit(solution)/shard_map/optics/pallas_call | solution.py:42
  29.2 0.2 collective-permute-done.15.after.refs_3_
  29.4 1.1 %shift.1.refs_7_ = bf16[3,128,512]{2,1,0:T(8,128)(2,1)S(1)} custom-call(s32[2,3]{1,0:T(2,128)S(1)} %get-tuple-element.74.wind_held, bf16[3,128,512]{2,1,0:T(8,128)(2,1)S(1)} %get-tuple-element.120.own, bf16[3,128,128]{2,1,0:T(8,128)(2,1)S(1)} %collective-permute-done.2.near.refs_6_.near0, bf16[3,128,128]{2,1,0:T(8,128)(2,1)S(1)} %collective-permute-done.5.refs_2_.near1, ...), custom_call_target="tpu_custom_call" | custom-call | tf_op jit(solution)/shard_map/shift/pallas_call | solution.py:42
  30.6 2.9 %collective-permute-done.14.refs_2_ = bf16[32,1280]{1,0:T(8,128)(2,1)S(1)} collective-permute-done((bf16[32,1280]{1,0:T(8,128)(2,1)S(1)}, bf16[32,1280]{1,0:T(8,128)(2,1)S(1)}, u32[]{:S(2)}, u32[]{:S(2)}) %collective-permute-start.14) | collective-permute-done | bytes 81952 | tf_op jit(solution)/shard_map/ppermute | solution.py:485
  33.5 1.3 %imaging.1 = (f32[64,2560]{1,0:T(8,128)}, bf16[3,128,512]{2,1,0:T(8,128)(2,1)}) custom-call(bf16[32,1280]{1,0:T(8,128)(2,1)S(1)} %get-tuple-element.98.refs_0_, bf16[32,1408]{1,0:T(8,128)(2,1)S(1)} %collective-permute-done.13.before.refs_1_, bf16[32,1280]{1,0:T(8,128)(2,1)S(1)} %collective-permute-done.14.refs_2_, ...), custom_call_target="tpu_custom_call" | custom-call | flops 400000000 | bytes 2228224 | tf_op jit(solution)/shard_map/imaging/pallas_call | solution.py:42
  (12 shorter events, 0.0 us)
Async XLA Ops:
  1.8 8.1 %collective-permute-start.1 = (bf16[3,128,128]{2,1,0:T(8,128)(2,1)S(1)}, bf16[3,128,128]{2,1,0:T(8,128)(2,1)S(1)}, u32[]{:S(2)}, u32[]{:S(2)}) collective-permute-start(bf16[3,128,128]{2,1,0:T(8,128)(2,1)S(1)} %get-tuple-element.65), channel_id=1, source_target_pairs={{0,3},{1,2},{2,1},{3,0},{4,7},{5,6},{6,5},{7,4},{8,11},{9,10},{10,... | collective-permute-start | bytes 294920 | tf_op jit(solution)/shard_map/ppermute | solution.py:478
  4.2 6.1 %collective-permute-start = (bf16[3,128,128]{2,1,0:T(8,128)(2,1)S(1)}, bf16[3,128,128]{2,1,0:T(8,128)(2,1)S(1)}, u32[]{:S(2)}, u32[]{:S(2)}) collective-permute-start(bf16[3,128,128]{2,1,0:T(8,128)(2,1)S(1)} %get-tuple-element.64.keep.refs_7_), channel_id=1, source_target_pairs={{0,2},{1,3},{2,0},{3,1},{4,6},{5,7},{6,4},{7,5},{8,10},{9,11},{10,... | collective-permute-start | bytes 294920 | tf_op jit(solution)/shard_map/ppermute | solution.py:478
  4.8 5.4 %collective-permute-start.2 = (bf16[3,128,128]{2,1,0:T(8,128)(2,1)S(1)}, bf16[3,128,128]{2,1,0:T(8,128)(2,1)S(1)}, u32[]{:S(2)}, u32[]{:S(2)}) collective-permute-start(bf16[3,128,128]{2,1,0:T(8,128)(2,1)S(1)} %get-tuple-element.65), channel_id=1, source_target_pairs={{0,1},{1,0},{2,3},{3,2},{4,5},{5,4},{6,7},{7,6},{8,9},{9,8},{10,11... | collective-permute-start | bytes 294920 | tf_op jit(solution)/shard_map/ppermute | solution.py:478
  4.9 9.3 %collective-permute-start.3 = (bf16[3,128,128]{2,1,0:T(8,128)(2,1)S(1)}, bf16[3,128,128]{2,1,0:T(8,128)(2,1)S(1)}, u32[]{:S(2)}, u32[]{:S(2)}) collective-permute-start(bf16[3,128,128]{2,1,0:T(8,128)(2,1)S(1)} %get-tuple-element.81.refs_3_), channel_id=1, source_target_pairs={{0,2},{1,3},{2,0},{3,1},{4,6},{5,7},{6,4},{7,5},{8,10},{9,11},{10,... | collective-permute-start | bytes 294920 | tf_op jit(solution)/shard_map/ppermute | solution.py:478
  6.6 7.6 %collective-permute-start.4 = (bf16[3,128,128]{2,1,0:T(8,128)(2,1)S(1)}, bf16[3,128,128]{2,1,0:T(8,128)(2,1)S(1)}, u32[]{:S(2)}, u32[]{:S(2)}) collective-permute-start(bf16[3,128,128]{2,1,0:T(8,128)(2,1)S(1)} %get-tuple-element.84), channel_id=1, source_target_pairs={{0,3},{1,2},{2,1},{3,0},{4,7},{5,6},{6,5},{7,4},{8,11},{9,10},{10,... | collective-permute-start | bytes 294920 | tf_op jit(solution)/shard_map/ppermute | solution.py:478
  9.9 4.3 %collective-permute-start.5 = (bf16[3,128,128]{2,1,0:T(8,128)(2,1)S(1)}, bf16[3,128,128]{2,1,0:T(8,128)(2,1)S(1)}, u32[]{:S(2)}, u32[]{:S(2)}) collective-permute-start(bf16[3,128,128]{2,1,0:T(8,128)(2,1)S(1)} %get-tuple-element.84), channel_id=1, source_target_pairs={{0,1},{1,0},{2,3},{3,2},{4,5},{5,4},{6,7},{7,6},{8,9},{9,8},{10,11... | collective-permute-start | bytes 294920 | tf_op jit(solution)/shard_map/ppermute | solution.py:478
  10.9 6.2 %collective-permute-start.6 = (bf16[3,128,128]{2,1,0:T(8,128)(2,1)S(1)}, bf16[3,128,128]{2,1,0:T(8,128)(2,1)S(1)}, u32[]{:S(2)}, u32[]{:S(2)}) collective-permute-start(bf16[3,128,128]{2,1,0:T(8,128)(2,1)S(1)} %get-tuple-element.92), channel_id=1, source_target_pairs={{0,4},{1,5},{2,6},{3,7},{4,0},{5,1},{6,2},{7,3},{8,12},{9,13},{10,... | collective-permute-start | bytes 294920 | tf_op jit(solution)/shard_map/ppermute | solution.py:482
  12.7 5.1 %collective-permute-start.7 = (bf16[3,128,128]{2,1,0:T(8,128)(2,1)S(1)}, bf16[3,128,128]{2,1,0:T(8,128)(2,1)S(1)}, u32[]{:S(2)}, u32[]{:S(2)}) collective-permute-start(bf16[3,128,128]{2,1,0:T(8,128)(2,1)S(1)} %get-tuple-element.93), channel_id=1, source_target_pairs={{0,5},{1,4},{2,7},{3,6},{4,1},{5,0},{6,3},{7,2},{8,13},{9,12},{10,... | collective-permute-start | bytes 294920 | tf_op jit(solution)/shard_map/ppermute | solution.py:482
  14.8 5.7 %collective-permute-start.11 = (bf16[224,128]{1,0:T(8,128)(2,1)S(1)}, bf16[224,128]{1,0:T(8,128)(2,1)S(1)}, u32[]{:S(2)}, u32[]{:S(2)}) collective-permute-start(bf16[224,128]{1,0:T(8,128)(2,1)S(1)} %get-tuple-element.103), channel_id=1, source_target_pairs={{0,4},{1,5},{2,6},{3,7},{4,0},{5,1},{6,2},{7,3},{8,12},{9,13},{10,... | collective-permute-start | bytes 172040 | tf_op jit(solution)/shard_map/ppermute | solution.py:482
  16.8 4.1 %collective-permute-start.12 = (bf16[224,128]{1,0:T(8,128)(2,1)S(1)}, bf16[224,128]{1,0:T(8,128)(2,1)S(1)}, u32[]{:S(2)}, u32[]{:S(2)}) collective-permute-start(bf16[224,128]{1,0:T(8,128)(2,1)S(1)} %get-tuple-element.104), channel_id=1, source_target_pairs={{0,5},{1,4},{2,7},{3,6},{4,1},{5,0},{6,3},{7,2},{8,13},{9,12},{10,... | collective-permute-start | bytes 172040 | tf_op jit(solution)/shard_map/ppermute | solution.py:482
  16.8 3.2 %collective-permute-start.8 = (bf16[3,192,256]{2,1,0:T(8,128)(2,1)S(1)}, bf16[3,192,256]{2,1,0:T(8,128)(2,1)S(1)}, u32[]{:S(2)}, u32[]{:S(2)}) collective-permute-start(bf16[3,192,256]{2,1,0:T(8,128)(2,1)S(1)} %get-tuple-element.95), channel_id=1, source_target_pairs={{0,1},{1,0},{2,3},{3,2},{4,5},{5,4},{6,7},{7,6},{8,9},{9,8},{10,11... | collective-permute-start | bytes 884744 | tf_op jit(solution)/shard_map/ppermute | solution.py:478
  18.5 6.8 %collective-permute-start.9 = (bf16[192,128]{1,0:T(8,128)(2,1)S(1)}, bf16[192,128]{1,0:T(8,128)(2,1)S(1)}, u32[]{:S(2)}, u32[]{:S(2)}) collective-permute-start(bf16[192,128]{1,0:T(8,128)(2,1)S(1)} %get-tuple-element.96), channel_id=1, source_target_pairs={{0,4},{1,5},{2,6},{3,7},{4,0},{5,1},{6,2},{7,3},{8,12},{9,13},{10,... | collective-permute-start | bytes 147464 | tf_op jit(solution)/shard_map/ppermute | solution.py:482
  19.8 5.5 %collective-permute-start.10 = (bf16[192,128]{1,0:T(8,128)(2,1)S(1)}, bf16[192,128]{1,0:T(8,128)(2,1)S(1)}, u32[]{:S(2)}, u32[]{:S(2)}) collective-permute-start(bf16[192,128]{1,0:T(8,128)(2,1)S(1)} %get-tuple-element.97), channel_id=1, source_target_pairs={{0,5},{1,4},{2,7},{3,6},{4,1},{5,0},{6,3},{7,2},{8,13},{9,12},{10,... | collective-permute-start | bytes 147464 | tf_op jit(solution)/shard_map/ppermute | solution.py:482
  21.4 7.2 %collective-permute-start.13 = (bf16[32,1408]{1,0:T(8,128)(2,1)S(1)}, bf16[32,1408]{1,0:T(8,128)(2,1)S(1)}, u32[]{:S(2)}, u32[]{:S(2)}) collective-permute-start(bf16[32,1408]{1,0:T(8,128)(2,1)S(1)} %get-tuple-element.105), channel_id=1, source_target_pairs={{0,8},{4,12},{8,16},{12,20},{16,24},{20,28},{24,0},{28,4},{1,9},{5... | collective-permute-start | bytes 270344 | tf_op jit(solution)/shard_map/ppermute | solution.py:485
  23.0 6.4 %collective-permute-start.15 = (bf16[32,1408]{1,0:T(8,128)(2,1)S(1)}, bf16[32,1408]{1,0:T(8,128)(2,1)S(1)}, u32[]{:S(2)}, u32[]{:S(2)}) collective-permute-start(bf16[32,1408]{1,0:T(8,128)(2,1)S(1)} %get-tuple-element.108), channel_id=1, source_target_pairs={{0,24},{4,28},{8,0},{12,4},{16,8},{20,12},{24,16},{28,20},{1,25},{... | collective-permute-start | bytes 270344 | tf_op jit(solution)/shard_map/ppermute | solution.py:485
  25.8 7.7 %collective-permute-start.14 = (bf16[32,1280]{1,0:T(8,128)(2,1)S(1)}, bf16[32,1280]{1,0:T(8,128)(2,1)S(1)}, u32[]{:S(2)}, u32[]{:S(2)}) collective-permute-start(bf16[32,1280]{1,0:T(8,128)(2,1)S(1)} %get-tuple-element.107), channel_id=1, source_target_pairs={{0,16},{4,20},{8,24},{12,28},{16,0},{20,4},{24,8},{28,12},{1,17},{... | collective-permute-start | bytes 245768 | tf_op jit(solution)/shard_map/ppermute | solution.py:485

commit v20 on v18

--- a/solution.py
+++ b/solution.py
@@ -193,8 +193,15 @@
 
 
 def strips_kernel(wind_held, *refs):
-    tables, (across, diagonal, near, keep, cols_out, strip, sibling_strip, wind, sem) = refs[:4], refs[4:]
+    tables, rows_ref, blocks, refs = refs[:4], refs[4], refs[5:9], refs[9:]
+    across, diagonal, near, keep = blocks
+    cols_out, mine, sibling, strip, sibling_strip, wind, sem = refs
     load = fetch((wind_held, wind, sem))[0]
+    half = mine.shape[1]
+    for level in range(mine.shape[0]):
+        part = project_rows(rows_ref, keep, near, across, diagonal, level, slice(0, half))
+        mine[level] = part[:half]
+        sibling[level] = part[half:]
     column_weights(*tables, jnp.bitwise_xor(lax.axis_index("layer"), 1) * cols_out.shape[1], cols_out)
     layers, rows, _ = keep.shape
     core = lax.rem(lax.axis_index("dir"), 2)
@@ -225,18 +232,18 @@
     sibling_strip[...] = strips[STRIP : 2 * STRIP]
 
 
-def project_rows(rows_ref, keep, near, across, diagonal, level):
+def project_rows(rows_ref, keep, near, across, diagonal, level, cut=slice(None)):
     screen = stack(keep[level], near[level], across[level], diagonal[level])
-    rows = stack(rows_ref[0, level], rows_ref[1, level])
+    rows = stack(rows_ref[0, level, cut], rows_ref[1, level, cut])
     return dot(rows, screen).astype(jnp.bfloat16)
 
 
-def first_rows_kernel(rows_ref, across, diagonal, near, keep, mine, sibling, other, sibling_other):
-    layers, half, _ = mine.shape
-    for level in range(layers):
-        part = project_rows(rows_ref, keep, near, across, diagonal, level)
-        for k, out in enumerate((mine, other, sibling, sibling_other)):
-            out[level] = part[k * half : (k + 1) * half]
+def first_rows_kernel(rows_ref, across, diagonal, near, keep, other, sibling_other):
+    layers, half, _ = other.shape
+    for level in range(layers):
+        part = project_rows(rows_ref, keep, near, across, diagonal, level, slice(half, 2 * half))
+        other[level] = part[:half]
+        sibling_other[level] = part[half:]
 
 
 def put_strip(out, at, strip):
@@ -544,22 +551,23 @@
     across0, diagonal0, row_weights, cols = lax.optimization_barrier((across0, diagonal0, row_weights, cols))
 
     projected = shape(layers, half, width)
-    mine0, sibling0, other0, sibling_other0 = call(
+    other0, sibling_other0 = call(
         first_rows_kernel,
-        [projected] * 4,
+        [projected] * 2,
         (row_weights, across0, diagonal0, near0, keep0),
         0,
         "rows_first",
         brief=True,
     )
-    came0 = partner(other0)
-    sibling_came0 = partner(sibling_other0, 1)
-
-    wind, mine0 = lax.optimization_barrier((wind, mine0))
-    others, strip, sibling_strip = call(
+    sends = other0, sibling_other0
+    came0 = partner(sends[0])
+    sibling_came0 = partner(sends[1], 1)
+
+    wind, other0 = lax.optimization_barrier((wind, other0))
+    others, mine0, sibling0, strip, sibling_strip = call(
         strips_kernel,
-        [shape(layers, cols_dev, pupil_cols)] + [shape(STRIP, rows_dev)] * 2,
-        (wind, *tables, across0, diagonal0, near0, keep0),
+        [shape(layers, cols_dev, pupil_cols)] + [projected] * 2 + [shape(STRIP, rows_dev)] * 2,
+        (wind, *tables, row_weights, across0, diagonal0, near0, keep0),
         0,
         "strips",
         scratch=wind_scratch,

time: 34.2 us -> 34.6 us (1.012)
  starting transfers between devices: 15.7 us -> 16.8 us
  waiting for transfers between devices: 5.52 us -> 4.67 us
    ppermute x3, starting transfers between devices: 4.76 us -> 5.46 us  [per_device(): lax.ppermute(received[k], 'layer', [(i, i ^ 2 * k) for i in range(n_layer)])]
    ppermute x6, waiting for transfers between devices: 1.22 us -> 0.73 us  [partner(): lax.ppermute(value, ('layer', 'dir'), [(i, i ^ n_dir ^ bits) for i in ran...]
    ppermute x3, waiting for transfers between devices: 4.28 us -> 3.92 us  [per_device(): lax.ppermute(received[k], 'layer', [(i, i ^ 2 * k) for i in range(n_layer)])]
  transfers between devices with their start and end apart: 16 -> 16, of which waited for: 5 -> 4; matrix products, arithmetic and copies ran while one was open for 0% -> 0% of each run, Pallas kernels for 28% -> 28%
where the time goes in v20:
time: 34.6 us; the launch traced here: 34.4 us
  starting transfers between devices  16.8 us (49%)
  Pallas kernels  12.2 us (35%)
  waiting for transfers between devices  4.67 us (13%)
  between operations  0.76 us (2%)
    pallas_call x12, Pallas kernels, call(): pl.pallas_call(kernel, out_shape=out_shape, in_specs=in_specs, out_specs=...  12.2 us
    ppermute x7, starting transfers between devices, swap(): return lax.ppermute(value, 'dir', [(i, i ^ bits) for i in range(n_dir)])  5.72 us
    ppermute x6, starting transfers between devices, partner(): lax.ppermute(value, ('layer', 'dir'), [(i, i ^ n_dir ^ bits) for i in ran...  5.62 us
    ppermute x3, starting transfers between devices, per_device(): lax.ppermute(received[k], 'layer', [(i, i ^ 2 * k) for i in range(n_layer)])  5.46 us
    ppermute x3, waiting for transfers between devices, per_device(): lax.ppermute(received[k], 'layer', [(i, i ^ 2 * k) for i in range(n_layer)])  3.92 us
    ppermute x6, waiting for transfers between devices, partner(): lax.ppermute(value, ('layer', 'dir'), [(i, i ^ n_dir ^ bits) for i in ran...  0.73 us
  transfers between devices with their start and end apart: 16, of which 4 were waited for; matrix products, arithmetic and copies ran while one was open for 0% of the time, Pallas kernels for 28%

profile of v20, /device:TPU:0, one launch (start us, length us, event | category | flops | bytes accessed | tf_op | source)
XLA Modules:
  0.0 34.4 jit_solution(17195783415494830695)
XLA Ops:
  0.6 1.1 %split.1 = (bf16[3,128,128]{2,1,0:T(8,128)(2,1)S(1)}, bf16[3,128,128]{2,1,0:T(8,128)(2,1)S(1)}, bf16[3,128,128]{2,1,0:T(8,128)(2,1)S(1)}, bf16[3,128,128]{2,1,0:...) custom-call(bf16[3,128,512]{2,1,0:T(8,128)(2,1)} %refs_0_.1, ...), custom_call_target="tpu_custom_call" | custom-call | tf_op jit(solution)/shard_map/split/pallas_call | solution.py:42
  1.8 2.4 %collective-permute-start.1 = (bf16[3,128,128]{2,1,0:T(8,128)(2,1)S(1)}, bf16[3,128,128]{2,1,0:T(8,128)(2,1)S(1)}, u32[]{:S(2)}, u32[]{:S(2)}) collective-permute-start(bf16[3,128,128]{2,1,0:T(8,128)(2,1)S(1)} %get-tuple-element.64), channel_id=1, source_target_pairs={{0,3},{1,2},{2,1},{3,0},{4,7},{5,6},{6,5},{7,4},{8,11},{9,10},{10,... | collective-permute-start | bytes 294920 | tf_op jit(solution)/shard_map/ppermute | solution.py:504
  4.2 0.6 %collective-permute-start = (bf16[3,128,128]{2,1,0:T(8,128)(2,1)S(1)}, bf16[3,128,128]{2,1,0:T(8,128)(2,1)S(1)}, u32[]{:S(2)}, u32[]{:S(2)}) collective-permute-start(bf16[3,128,128]{2,1,0:T(8,128)(2,1)S(1)} %get-tuple-element.63.keep.refs_8_.refs_7_), channel_id=1, source_target_pairs={{0,2},{1,3},{2,0},{3,1},{4,6},{5,7},{6,4},{7,5},{8,10},{9,11},{10,... | collective-permute-start | bytes 294920 | tf_op jit(solution)/shard_map/ppermute | solution.py:504
  4.8 0.0 collective-permute-start.2
  4.9 1.7 %collective-permute-start.3 = (bf16[3,128,128]{2,1,0:T(8,128)(2,1)S(1)}, bf16[3,128,128]{2,1,0:T(8,128)(2,1)S(1)}, u32[]{:S(2)}, u32[]{:S(2)}) collective-permute-start(bf16[3,128,128]{2,1,0:T(8,128)(2,1)S(1)} %get-tuple-element.80.refs_3_), channel_id=1, source_target_pairs={{0,2},{1,3},{2,0},{3,1},{4,6},{5,7},{6,4},{7,5},{8,10},{9,11},{10,... | collective-permute-start | bytes 294920 | tf_op jit(solution)/shard_map/ppermute | solution.py:504
  6.6 0.1 collective-permute-start.4
  6.7 3.2 %weights.1 = (bf16[2,3,256,512]{3,2,1,0:T(8,128)(2,1)S(1)}, bf16[3,512,1280]{2,1,0:T(8,128)(2,1)S(1)}, s32[8,1280]{1,0:T(8,128)S(1)}, s32[8,1280]{1,0:T(8,128)S(...) custom-call(s32[2,3]{1,0:T(2,128)S(1)} %get-tuple-element.73.wind_he, ...), custom_call_target="tpu_custom_call" | custom-call | tf_op jit(solution)/shard_map/weights/pallas_call | solution.py:42
  9.9 0.0 collective-permute-done.1.diagonal.refs_6_.refs_5_.diagonal0
  9.9 0.4 %collective-permute-start.5 = (bf16[3,128,128]{2,1,0:T(8,128)(2,1)S(1)}, bf16[3,128,128]{2,1,0:T(8,128)(2,1)S(1)}, u32[]{:S(2)}, u32[]{:S(2)}) collective-permute-start(bf16[3,128,128]{2,1,0:T(8,128)(2,1)S(1)} %get-tuple-element.83), channel_id=1, source_target_pairs={{0,1},{1,0},{2,3},{3,2},{4,5},{5,4},{6,7},{7,6},{8,9},{9,8},{10,11... | collective-permute-start | bytes 294920 | tf_op jit(solution)/shard_map/ppermute | solution.py:504
  10.3 0.0 collective-permute-done.across.refs_5_.refs_4_
  10.3 0.4 %rows_first.1 = (bf16[3,128,128]{2,1,0:T(8,128)(2,1)S(1)}, bf16[3,128,128]{2,1,0:T(8,128)(2,1)S(1)}) custom-call(bf16[2,3,256,512]{3,2,1,0:T(8,128)(2,1)S(1)} %get-tuple-element.69.rows_ref.refs_4_, bf16[3,128,128]{2,1,0:T(8,128)(2,1)S(1)} %collective-permute-done.across.refs_5_.refs_4_, ...), custom_call_target="tpu_custom_call" | custom-call | tf_op jit(solution)/shard_map/rows_first/pallas_call | solution.py:42
  10.6 1.5 %collective-permute-start.7 = (bf16[3,128,128]{2,1,0:T(8,128)(2,1)S(1)}, bf16[3,128,128]{2,1,0:T(8,128)(2,1)S(1)}, u32[]{:S(2)}, u32[]{:S(2)}) collective-permute-start(bf16[3,128,128]{2,1,0:T(8,128)(2,1)S(1)} %get-tuple-element.91), channel_id=1, source_target_pairs={{0,5},{1,4},{2,7},{3,6},{4,1},{5,0},{6,3},{7,2},{8,13},{9,12},{10,... | collective-permute-start | bytes 294920 | tf_op jit(solution)/shard_map/ppermute | solution.py:508
  12.1 0.4 %collective-permute-start.6 = (bf16[3,128,128]{2,1,0:T(8,128)(2,1)S(1)}, bf16[3,128,128]{2,1,0:T(8,128)(2,1)S(1)}, u32[]{:S(2)}, u32[]{:S(2)}) collective-permute-start(bf16[3,128,128]{2,1,0:T(8,128)(2,1)S(1)} %get-tuple-element.72), channel_id=1, source_target_pairs={{0,4},{1,5},{2,6},{3,7},{4,0},{5,1},{6,2},{7,3},{8,12},{9,13},{10,... | collective-permute-start | bytes 294920 | tf_op jit(solution)/shard_map/ppermute | solution.py:508
  12.5 1.8 %strips.1 = (bf16[3,512,1280]{2,1,0:T(8,128)(2,1)S(1)}, bf16[3,128,128]{2,1,0:T(8,128)(2,1)S(1)}, bf16[3,128,128]{2,1,0:T(8,128)(2,1)S(1)}, bf16[32,128]{1,0:T(8,128)(2,1)S(1)}, bf16[32,128]{1,0:T(8,128)(2,1)S(1)}) custom-call(s32[2,3]{1,0:T(2,128)S(1)} %get-tuple-element.73.wind_held, s32[8,1280]{1,0:T(8,128)S(1)} %get-tuple-element.74.refs_0_, ...), custom_call_target="tpu_custom_call" | custom-call | tf_op jit(solution)/shard_map/strips/pallas_call | solution.py:42
  14.4 0.6 %rows_later.1 = (bf16[3,128,128]{2,1,0:T(8,128)(2,1)S(1)}, bf16[3,192,256]{2,1,0:T(8,128)(2,1)S(1)}, bf16[224,128]{1,0:T(8,128)(2,1)S(1)}, bf16[224,128]{1,0:T(8...) custom-call(bf16[2,3,256,512]{3,2,1,0:T(8,128)(2,1)S(1)} %get-tuple-element.69.rows_ref.refs_4_, ...), custom_call_target="tpu_custom_call" | custom-call | tf_op jit(solution)/shard_map/rows_later/pallas_call | solution.py:42
  15.0 1.8 %collective-permute-start.11 = (bf16[224,128]{1,0:T(8,128)(2,1)S(1)}, bf16[224,128]{1,0:T(8,128)(2,1)S(1)}, u32[]{:S(2)}, u32[]{:S(2)}) collective-permute-start(bf16[224,128]{1,0:T(8,128)(2,1)S(1)} %get-tuple-element.97), channel_id=1, source_target_pairs={{0,4},{1,5},{2,6},{3,7},{4,0},{5,1},{6,2},{7,3},{8,12},{9,13},{10,... | collective-permute-start | bytes 172040 | tf_op jit(solution)/shard_map/ppermute | solution.py:508
  16.8 0.4 %collective-permute-start.8 = (bf16[3,192,256]{2,1,0:T(8,128)(2,1)S(1)}, bf16[3,192,256]{2,1,0:T(8,128)(2,1)S(1)}, u32[]{:S(2)}, u32[]{:S(2)}) collective-permute-start(bf16[3,192,256]{2,1,0:T(8,128)(2,1)S(1)} %get-tuple-element.93), channel_id=1, source_target_pairs={{0,1},{1,0},{2,3},{3,2},{4,5},{5,4},{6,7},{7,6},{8,9},{9,8},{10,11... | collective-permute-start | bytes 884744 | tf_op jit(solution)/shard_map/ppermute | solution.py:504
  17.2 0.7 %collective-permute-done.6.came = bf16[3,128,128]{2,1,0:T(8,128)(2,1)S(1)} collective-permute-done((bf16[3,128,128]{2,1,0:T(8,128)(2,1)S(1)}, bf16[3,128,128]{2,1,0:T(8,128)(2,1)S(1)}, u32[]{:S(2)}, u32[]{:S(2)}) %collective-permute-start.6) | collective-permute-done | bytes 98336 | tf_op jit(solution)/shard_map/ppermute | solution.py:508
  17.9 0.7 %phase.1 = f32[128,1280]{1,0:T(8,128)S(1)} custom-call(bf16[3,512,1280]{2,1,0:T(8,128)(2,1)S(1)} %get-tuple-element.79.mine_ref, bf16[3,512,1280]{2,1,0:T(8,128)(2,1)S(1)} %get-tuple-element.78.other_ref.cols_ref, bf16[3,128,128]{2,1,0:T(8,128)(2,1)S(1)} %get-tuple-element.89.mine0, bf16[3,128,128]{2,1,0:T(8,128)(2,1)S(1)} %get-tuple-element.90.mine1, ...), custom_call_target="tpu_custom_call" | custom-call | flops 10000000000 | bytes 8912896 | tf_op jit(solution)/shard_map/phase/pallas_call | solution.py:42
  18.6 1.9 %collective-permute-start.9 = (bf16[192,128]{1,0:T(8,128)(2,1)S(1)}, bf16[192,128]{1,0:T(8,128)(2,1)S(1)}, u32[]{:S(2)}, u32[]{:S(2)}) collective-permute-start(bf16[192,128]{1,0:T(8,128)(2,1)S(1)} %get-tuple-element.94), channel_id=1, source_target_pairs={{0,4},{1,5},{2,6},{3,7},{4,0},{5,1},{6,2},{7,3},{8,12},{9,13},{10,... | collective-permute-start | bytes 147464 | tf_op jit(solution)/shard_map/ppermute | solution.py:508
  20.5 0.4 %taken.1.phase = f32[128,1280]{1,0:T(8,128)S(1)} custom-call(bf16[3,512,1280]{2,1,0:T(8,128)(2,1)S(1)} %get-tuple-element.79.mine_ref, f32[128,1280]{1,0:T(8,128)S(1)} %phase.1, bf16[3,192,256]{2,1,0:T(8,128)(2,1)S(1)} %collective-permute-done.8.taken), custom_call_target="tpu_custom_call" | custom-call | tf_op jit(solution)/shard_map/taken/pallas_call | solution.py:42
  20.9 0.0 collective-permute-done.12.sibling_came
  21.0 0.5 %far.1 = (bf16[32,1408]{1,0:T(8,128)(2,1)S(1)}, bf16[32,1408]{1,0:T(8,128)(2,1)S(1)}, bf16[64,128]{1,0:T(8,128)(2,1)S(1)}) custom-call(bf16[3,512,1280]{2,1,0:T(8,128)(2,1)S(1)} %get-tuple-element.78.other_ref.cols_ref, f32[128,1280]{1,0:T(8,128)S(1)} %taken.1.phase, bf16[224,128]{1,0:T(8,128)(2,1)S(1)} %collective-permute-done.11.came, ...), custom_call_target="tpu_custom_call" | custom-call | flops 300000000 | bytes 4898816 | tf_op jit(solution)/shard_map/far/pallas_call | solution.py:42
  21.5 3.7 %collective-permute-start.14 = (bf16[32,1408]{1,0:T(8,128)(2,1)S(1)}, bf16[32,1408]{1,0:T(8,128)(2,1)S(1)}, u32[]{:S(2)}, u32[]{:S(2)}) collective-permute-start(bf16[32,1408]{1,0:T(8,128)(2,1)S(1)} %get-tuple-element.104), channel_id=1, source_target_pairs={{0,24},{4,28},{8,16},{12,20},{16,8},{20,12},{24,0},{28,4},{1,25},{... | collective-permute-start | bytes 270344 | tf_op jit(solution)/shard_map/ppermute | solution.py:625
  25.2 0.5 %rest.1 = (bf16[32,1280]{1,0:T(8,128)(2,1)S(1)}, bf16[32,1280]{1,0:T(8,128)(2,1)S(1)}) custom-call(bf16[3,512,1280]{2,1,0:T(8,128)(2,1)S(1)} %get-tuple-element.78.other_ref.cols_ref, f32[128,1280]{1,0:T(8,128)S(1)} %taken.1.phase, bf16[192,128]{1,0:T(8,128)(2,1)S(1)} %collective-permute-done.9.came, bf16[192,128]{1,0:T(8,128)(2,1)S(1)} %collective-permute-done.10.sibling_came), custom_call_target="tpu_custom_call" | custom-call | tf_op jit(solution)/shard_map/rest/pallas_call | solution.py:42
  25.7 1.7 %collective-permute-start.15 = (bf16[32,1280]{1,0:T(8,128)(2,1)S(1)}, bf16[32,1280]{1,0:T(8,128)(2,1)S(1)}, u32[]{:S(2)}, u32[]{:S(2)}) collective-permute-start(bf16[32,1280]{1,0:T(8,128)(2,1)S(1)} %get-tuple-element.113), channel_id=1, source_target_pairs={{0,16},{4,20},{8,24},{12,28},{16,0},{20,4},{24,8},{28,12},{1,17},{... | collective-permute-start | bytes 245768 | tf_op jit(solution)/shard_map/ppermute | solution.py:625
  27.4 1.5 %collective-permute-done.14.refs_1_.refs_3_ = bf16[32,1408]{1,0:T(8,128)(2,1)S(1)} collective-permute-done((bf16[32,1408]{1,0:T(8,128)(2,1)S(1)}, bf16[32,1408]{1,0:T(8,128)(2,1)S(1)}, u32[]{:S(2)}, u32[]{:S(2)}) %collective-permute-start.14) | collective-permute-done | bytes 90144 | tf_op jit(solution)/shard_map/ppermute | solution.py:625
  28.9 0.6 %optics.1 = (f32[32,1280]{1,0:T(8,128)S(1)}, bf16[256,512]{1,0:T(8,128)(2,1)S(1)}, bf16[128,64]{1,0:T(8,128)(2,1)S(1)}) custom-call(f32[32,1280]{1,0:T(8,128)S(1)} %get-tuple-element.105.amplitude, f32[128,128]{1,0:T(8,128)S(1)} %get-tuple-element.106.ones, f32[256,512]{1,0:T(8,128)S(1)} %get-tuple-element.107.columns, f32[128,64]{1,0:T(8,128)S(1)} %get-tuple-element.108.lines), custom_call_target="tpu_custom_call" | custom-call | tf_op jit(solution)/shard_map/optics/pallas_call | solution.py:42
  29.5 2.1 %collective-permute-done.13.refs_0_.refs_1_ = bf16[32,1408]{1,0:T(8,128)(2,1)S(1)} collective-permute-done((bf16[32,1408]{1,0:T(8,128)(2,1)S(1)}, bf16[32,1408]{1,0:T(8,128)(2,1)S(1)}, u32[]{:S(2)}, u32[]{:S(2)}) %collective-permute-start.13) | collective-permute-done | bytes 90144 | tf_op jit(solution)/shard_map/ppermute | solution.py:625
  31.6 1.1 %shift.1.refs_7_ = bf16[3,128,512]{2,1,0:T(8,128)(2,1)S(1)} custom-call(s32[2,3]{1,0:T(2,128)S(1)} %get-tuple-element.73.wind_held, bf16[3,128,512]{2,1,0:T(8,128)(2,1)S(1)} %get-tuple-element.118.own, bf16[3,128,128]{2,1,0:T(8,128)(2,1)S(1)} %collective-permute-done.2.near.refs_7_.refs_6_.near0, ...), custom_call_target="tpu_custom_call" | custom-call | tf_op jit(solution)/shard_map/shift/pallas_call | solution.py:42
  32.8 0.3 collective-permute-done.15.refs_2_
  33.1 1.3 %imaging.1 = (f32[64,2560]{1,0:T(8,128)}, bf16[3,128,512]{2,1,0:T(8,128)(2,1)}) custom-call(bf16[32,1280]{1,0:T(8,128)(2,1)S(1)} %get-tuple-element.96.refs_0_, bf16[32,1408]{1,0:T(8,128)(2,1)S(1)} %collective-permute-done.13.refs_0_.refs_1_, bf16[32,1280]{1,0:T(8,128)(2,1)S(1)} %collective-permute-done.15.refs_2_, ...), custom_call_target="tpu_custom_call" | custom-call | flops 400000000 | bytes 2228224 | tf_op jit(solution)/shard_map/imaging/pallas_call | solution.py:42
  (12 shorter events, 0.0 us)
Async XLA Ops:
  1.8 8.1 %collective-permute-start.1 = (bf16[3,128,128]{2,1,0:T(8,128)(2,1)S(1)}, bf16[3,128,128]{2,1,0:T(8,128)(2,1)S(1)}, u32[]{:S(2)}, u32[]{:S(2)}) collective-permute-start(bf16[3,128,128]{2,1,0:T(8,128)(2,1)S(1)} %get-tuple-element.64), channel_id=1, source_target_pairs={{0,3},{1,2},{2,1},{3,0},{4,7},{5,6},{6,5},{7,4},{8,11},{9,10},{10,... | collective-permute-start | bytes 294920 | tf_op jit(solution)/shard_map/ppermute | solution.py:504
  4.2 6.1 %collective-permute-start = (bf16[3,128,128]{2,1,0:T(8,128)(2,1)S(1)}, bf16[3,128,128]{2,1,0:T(8,128)(2,1)S(1)}, u32[]{:S(2)}, u32[]{:S(2)}) collective-permute-start(bf16[3,128,128]{2,1,0:T(8,128)(2,1)S(1)} %get-tuple-element.63.keep.refs_8_.refs_7_), channel_id=1, source_target_pairs={{0,2},{1,3},{2,0},{3,1},{4,6},{5,7},{6,4},{7,5},{8,10},{9,11},{10,... | collective-permute-start | bytes 294920 | tf_op jit(solution)/shard_map/ppermute | solution.py:504
  4.8 5.4 %collective-permute-start.2 = (bf16[3,128,128]{2,1,0:T(8,128)(2,1)S(1)}, bf16[3,128,128]{2,1,0:T(8,128)(2,1)S(1)}, u32[]{:S(2)}, u32[]{:S(2)}) collective-permute-start(bf16[3,128,128]{2,1,0:T(8,128)(2,1)S(1)} %get-tuple-element.64), channel_id=1, source_target_pairs={{0,1},{1,0},{2,3},{3,2},{4,5},{5,4},{6,7},{7,6},{8,9},{9,8},{10,11... | collective-permute-start | bytes 294920 | tf_op jit(solution)/shard_map/ppermute | solution.py:504
  4.9 9.5 %collective-permute-start.3 = (bf16[3,128,128]{2,1,0:T(8,128)(2,1)S(1)}, bf16[3,128,128]{2,1,0:T(8,128)(2,1)S(1)}, u32[]{:S(2)}, u32[]{:S(2)}) collective-permute-start(bf16[3,128,128]{2,1,0:T(8,128)(2,1)S(1)} %get-tuple-element.80.refs_3_), channel_id=1, source_target_pairs={{0,2},{1,3},{2,0},{3,1},{4,6},{5,7},{6,4},{7,5},{8,10},{9,11},{10,... | collective-permute-start | bytes 294920 | tf_op jit(solution)/shard_map/ppermute | solution.py:504
  6.6 7.8 %collective-permute-start.4 = (bf16[3,128,128]{2,1,0:T(8,128)(2,1)S(1)}, bf16[3,128,128]{2,1,0:T(8,128)(2,1)S(1)}, u32[]{:S(2)}, u32[]{:S(2)}) collective-permute-start(bf16[3,128,128]{2,1,0:T(8,128)(2,1)S(1)} %get-tuple-element.83), channel_id=1, source_target_pairs={{0,3},{1,2},{2,1},{3,0},{4,7},{5,6},{6,5},{7,4},{8,11},{9,10},{10,... | collective-permute-start | bytes 294920 | tf_op jit(solution)/shard_map/ppermute | solution.py:504
  9.9 4.5 %collective-permute-start.5 = (bf16[3,128,128]{2,1,0:T(8,128)(2,1)S(1)}, bf16[3,128,128]{2,1,0:T(8,128)(2,1)S(1)}, u32[]{:S(2)}, u32[]{:S(2)}) collective-permute-start(bf16[3,128,128]{2,1,0:T(8,128)(2,1)S(1)} %get-tuple-element.83), channel_id=1, source_target_pairs={{0,1},{1,0},{2,3},{3,2},{4,5},{5,4},{6,7},{7,6},{8,9},{9,8},{10,11... | collective-permute-start | bytes 294920 | tf_op jit(solution)/shard_map/ppermute | solution.py:504
  10.6 6.6 %collective-permute-start.7 = (bf16[3,128,128]{2,1,0:T(8,128)(2,1)S(1)}, bf16[3,128,128]{2,1,0:T(8,128)(2,1)S(1)}, u32[]{:S(2)}, u32[]{:S(2)}) collective-permute-start(bf16[3,128,128]{2,1,0:T(8,128)(2,1)S(1)} %get-tuple-element.91), channel_id=1, source_target_pairs={{0,5},{1,4},{2,7},{3,6},{4,1},{5,0},{6,3},{7,2},{8,13},{9,12},{10,... | collective-permute-start | bytes 294920 | tf_op jit(solution)/shard_map/ppermute | solution.py:508
  12.1 5.8 %collective-permute-start.6 = (bf16[3,128,128]{2,1,0:T(8,128)(2,1)S(1)}, bf16[3,128,128]{2,1,0:T(8,128)(2,1)S(1)}, u32[]{:S(2)}, u32[]{:S(2)}) collective-permute-start(bf16[3,128,128]{2,1,0:T(8,128)(2,1)S(1)} %get-tuple-element.72), channel_id=1, source_target_pairs={{0,4},{1,5},{2,6},{3,7},{4,0},{5,1},{6,2},{7,3},{8,12},{9,13},{10,... | collective-permute-start | bytes 294920 | tf_op jit(solution)/shard_map/ppermute | solution.py:508
  15.0 5.9 %collective-permute-start.11 = (bf16[224,128]{1,0:T(8,128)(2,1)S(1)}, bf16[224,128]{1,0:T(8,128)(2,1)S(1)}, u32[]{:S(2)}, u32[]{:S(2)}) collective-permute-start(bf16[224,128]{1,0:T(8,128)(2,1)S(1)} %get-tuple-element.97), channel_id=1, source_target_pairs={{0,4},{1,5},{2,6},{3,7},{4,0},{5,1},{6,2},{7,3},{8,12},{9,13},{10,... | collective-permute-start | bytes 172040 | tf_op jit(solution)/shard_map/ppermute | solution.py:508
  16.8 4.2 %collective-permute-start.12 = (bf16[224,128]{1,0:T(8,128)(2,1)S(1)}, bf16[224,128]{1,0:T(8,128)(2,1)S(1)}, u32[]{:S(2)}, u32[]{:S(2)}) collective-permute-start(bf16[224,128]{1,0:T(8,128)(2,1)S(1)} %get-tuple-element.98), channel_id=1, source_target_pairs={{0,5},{1,4},{2,7},{3,6},{4,1},{5,0},{6,3},{7,2},{8,13},{9,12},{10,... | collective-permute-start | bytes 172040 | tf_op jit(solution)/shard_map/ppermute | solution.py:508
  16.8 3.7 %collective-permute-start.8 = (bf16[3,192,256]{2,1,0:T(8,128)(2,1)S(1)}, bf16[3,192,256]{2,1,0:T(8,128)(2,1)S(1)}, u32[]{:S(2)}, u32[]{:S(2)}) collective-permute-start(bf16[3,192,256]{2,1,0:T(8,128)(2,1)S(1)} %get-tuple-element.93), channel_id=1, source_target_pairs={{0,1},{1,0},{2,3},{3,2},{4,5},{5,4},{6,7},{7,6},{8,9},{9,8},{10,11... | collective-permute-start | bytes 884744 | tf_op jit(solution)/shard_map/ppermute | solution.py:504
  18.6 6.6 %collective-permute-start.9 = (bf16[192,128]{1,0:T(8,128)(2,1)S(1)}, bf16[192,128]{1,0:T(8,128)(2,1)S(1)}, u32[]{:S(2)}, u32[]{:S(2)}) collective-permute-start(bf16[192,128]{1,0:T(8,128)(2,1)S(1)} %get-tuple-element.94), channel_id=1, source_target_pairs={{0,4},{1,5},{2,6},{3,7},{4,0},{5,1},{6,2},{7,3},{8,12},{9,13},{10,... | collective-permute-start | bytes 147464 | tf_op jit(solution)/shard_map/ppermute | solution.py:508
  20.5 4.7 %collective-permute-start.10 = (bf16[192,128]{1,0:T(8,128)(2,1)S(1)}, bf16[192,128]{1,0:T(8,128)(2,1)S(1)}, u32[]{:S(2)}, u32[]{:S(2)}) collective-permute-start(bf16[192,128]{1,0:T(8,128)(2,1)S(1)} %get-tuple-element.95), channel_id=1, source_target_pairs={{0,5},{1,4},{2,7},{3,6},{4,1},{5,0},{6,3},{7,2},{8,13},{9,12},{10,... | collective-permute-start | bytes 147464 | tf_op jit(solution)/shard_map/ppermute | solution.py:508
  21.5 7.4 %collective-permute-start.14 = (bf16[32,1408]{1,0:T(8,128)(2,1)S(1)}, bf16[32,1408]{1,0:T(8,128)(2,1)S(1)}, u32[]{:S(2)}, u32[]{:S(2)}) collective-permute-start(bf16[32,1408]{1,0:T(8,128)(2,1)S(1)} %get-tuple-element.104), channel_id=1, source_target_pairs={{0,24},{4,28},{8,16},{12,20},{16,8},{20,12},{24,0},{28,4},{1,25},{... | collective-permute-start | bytes 270344 | tf_op jit(solution)/shard_map/ppermute | solution.py:625
  25.2 6.5 %collective-permute-start.13 = (bf16[32,1408]{1,0:T(8,128)(2,1)S(1)}, bf16[32,1408]{1,0:T(8,128)(2,1)S(1)}, u32[]{:S(2)}, u32[]{:S(2)}) collective-permute-start(bf16[32,1408]{1,0:T(8,128)(2,1)S(1)} %get-tuple-element.99), channel_id=1, source_target_pairs={{0,8},{4,12},{8,0},{12,4},{16,24},{20,28},{24,16},{28,20},{1,9},{5... | collective-permute-start | bytes 270344 | tf_op jit(solution)/shard_map/ppermute | solution.py:625
  25.7 7.4 %collective-permute-start.15 = (bf16[32,1280]{1,0:T(8,128)(2,1)S(1)}, bf16[32,1280]{1,0:T(8,128)(2,1)S(1)}, u32[]{:S(2)}, u32[]{:S(2)}) collective-permute-start(bf16[32,1280]{1,0:T(8,128)(2,1)S(1)} %get-tuple-element.113), channel_id=1, source_target_pairs={{0,16},{4,20},{8,24},{12,28},{16,0},{20,4},{24,8},{28,12},{1,17},{... | collective-permute-start | bytes 245768 | tf_op jit(solution)/shard_map/ppermute | solution.py:625

commit v21 on v18

--- a/solution.py
+++ b/solution.py
@@ -519,8 +519,7 @@
     across0 = swap(keep0, 2)
     diagonal0 = swap(give0, 3)
     near0 = swap(give0, 1)
-    across1 = swap(keep1, 2)
-    diagonal1 = swap(give1, 3)
+    near1 = swap(give1, 1)
     ones = np.kron(np.eye(LANES // SUB_PIX), np.ones((SUB_PIX, SUB_PIX))).astype(np.float32)
     optics_in = (amplitude, jnp.asarray(ones), *[jnp.asarray(table) for table in tables_of(rows)])
     copies = [shape(*array.shape, dtype=array.dtype) for array in (screens, *optics_in)]
@@ -539,8 +538,9 @@
     )
     tables, (own, *optics_in) = loaded[:4], loaded[4:]
     wind = ints[0]
-    give1, own = lax.optimization_barrier((give1, own))
-    near1 = swap(give1, 1)
+    keep1, give1, own = lax.optimization_barrier((keep1, give1, own))
+    across1 = swap(keep1, 2)
+    diagonal1 = swap(give1, 3)
     across0, diagonal0, row_weights, cols = lax.optimization_barrier((across0, diagonal0, row_weights, cols))
 
     projected = shape(layers, half, width)

time: 34.2 us -> 35.1 us (1.026)
  waiting for transfers between devices: 5.52 us -> 6.07 us
  starting transfers between devices: 15.7 us -> 16.1 us
    ppermute x7, waiting for transfers between devices: 0.02 us -> 1.6 us  [swap(): return lax.ppermute(value, 'dir', [(i, i ^ bits) for i in range(n_dir)])]
    ppermute x6, waiting for transfers between devices: 1.22 us -> 0.55 us  [partner(): lax.ppermute(value, ('layer', 'dir'), [(i, i ^ n_dir ^ bits) for i in ran...]
    ppermute x7, starting transfers between devices: 5.55 us -> 5.95 us  [swap(): return lax.ppermute(value, 'dir', [(i, i ^ bits) for i in range(n_dir)])]
    ppermute x6, starting transfers between devices: 5.38 us -> 5.01 us  [partner(): lax.ppermute(value, ('layer', 'dir'), [(i, i ^ n_dir ^ bits) for i in ran...]
    ppermute x3, starting transfers between devices: 4.76 us -> 5.12 us  [per_device(): lax.ppermute(received[k], 'layer', [(i, i ^ 2 * k) for i in range(n_layer)])]
    ppermute x3, waiting for transfers between devices: 4.28 us -> 3.92 us  [per_device(): lax.ppermute(received[k], 'layer', [(i, i ^ 2 * k) for i in range(n_layer)])]
  transfers between devices with their start and end apart: 16 -> 16, of which waited for: 5 -> 5; matrix products, arithmetic and copies ran while one was open for 0% -> 0% of each run, Pallas kernels for 28% -> 27%
where the time goes in v21:
time: 35.1 us; the launch traced here: 35 us
  starting transfers between devices  16.1 us (46%)
  Pallas kernels  12.1 us (34%)
  waiting for transfers between devices  6.07 us (17%)
  between operations  0.75 us (2%)
    pallas_call x12, Pallas kernels, call(): pl.pallas_call(kernel, out_shape=out_shape, in_specs=in_specs, out_specs=...  12.1 us
    ppermute x7, starting transfers between devices, swap(): return lax.ppermute(value, 'dir', [(i, i ^ bits) for i in range(n_dir)])  5.95 us
    ppermute x3, starting transfers between devices, per_device(): lax.ppermute(received[k], 'layer', [(i, i ^ 2 * k) for i in range(n_layer)])  5.12 us
    ppermute x6, starting transfers between devices, partner(): lax.ppermute(value, ('layer', 'dir'), [(i, i ^ n_dir ^ bits) for i in ran...  5.01 us
    ppermute x3, waiting for transfers between devices, per_device(): lax.ppermute(received[k], 'layer', [(i, i ^ 2 * k) for i in range(n_layer)])  3.92 us
    ppermute x7, waiting for transfers between devices, swap(): return lax.ppermute(value, 'dir', [(i, i ^ bits) for i in range(n_dir)])  1.6 us
  transfers between devices with their start and end apart: 16, of which 5 were waited for; matrix products, arithmetic and copies ran while one was open for 0% of the time, Pallas kernels for 27%

profile of v21, /device:TPU:0, one launch (start us, length us, event | category | flops | bytes accessed | tf_op | source)
XLA Modules:
  0.0 35.0 jit_solution(14753788654311952138)
XLA Ops:
  0.6 1.1 %split.1 = (bf16[3,128,128]{2,1,0:T(8,128)(2,1)S(1)}, bf16[3,128,128]{2,1,0:T(8,128)(2,1)S(1)}, bf16[3,128,128]{2,1,0:T(8,128)(2,1)S(1)}, bf16[3,128,128]{2,1,0:...) custom-call(bf16[3,128,512]{2,1,0:T(8,128)(2,1)} %refs_0_.1, ...), custom_call_target="tpu_custom_call" | custom-call | tf_op jit(solution)/shard_map/split/pallas_call | solution.py:42
  1.8 2.4 %collective-permute-start.1 = (bf16[3,128,128]{2,1,0:T(8,128)(2,1)S(1)}, bf16[3,128,128]{2,1,0:T(8,128)(2,1)S(1)}, u32[]{:S(2)}, u32[]{:S(2)}) collective-permute-start(bf16[3,128,128]{2,1,0:T(8,128)(2,1)S(1)} %get-tuple-element.66), channel_id=1, source_target_pairs={{0,3},{1,2},{2,1},{3,0},{4,7},{5,6},{6,5},{7,4},{8,11},{9,10},{10,... | collective-permute-start | bytes 294920 | tf_op jit(solution)/shard_map/ppermute | solution.py:497
  4.2 0.6 %collective-permute-start = (bf16[3,128,128]{2,1,0:T(8,128)(2,1)S(1)}, bf16[3,128,128]{2,1,0:T(8,128)(2,1)S(1)}, u32[]{:S(2)}, u32[]{:S(2)}) collective-permute-start(bf16[3,128,128]{2,1,0:T(8,128)(2,1)S(1)} %get-tuple-element.65.keep.refs_7_), channel_id=1, source_target_pairs={{0,2},{1,3},{2,0},{3,1},{4,6},{5,7},{6,4},{7,5},{8,10},{9,11},{10,... | collective-permute-start | bytes 294920 | tf_op jit(solution)/shard_map/ppermute | solution.py:497
  4.8 0.0 collective-permute-start.2
  4.9 0.5 %collective-permute-start.5 = (bf16[3,128,128]{2,1,0:T(8,128)(2,1)S(1)}, bf16[3,128,128]{2,1,0:T(8,128)(2,1)S(1)}, u32[]{:S(2)}, u32[]{:S(2)}) collective-permute-start(bf16[3,128,128]{2,1,0:T(8,128)(2,1)S(1)} %get-tuple-element.86), channel_id=1, source_target_pairs={{0,1},{1,0},{2,3},{3,2},{4,5},{5,4},{6,7},{7,6},{8,9},{9,8},{10,11... | collective-permute-start | bytes 294920 | tf_op jit(solution)/shard_map/ppermute | solution.py:497
  5.4 3.2 %weights.1 = (bf16[2,3,256,512]{3,2,1,0:T(8,128)(2,1)S(1)}, bf16[3,512,1280]{2,1,0:T(8,128)(2,1)S(1)}, s32[8,1280]{1,0:T(8,128)S(1)}, s32[8,1280]{1,0:T(8,128)S(...) custom-call(s32[2,3]{1,0:T(2,128)S(1)} %get-tuple-element.75.wind_he, ...), custom_call_target="tpu_custom_call" | custom-call | tf_op jit(solution)/shard_map/weights/pallas_call | solution.py:42
  8.5 1.5 %collective-permute-start.4 = (bf16[3,128,128]{2,1,0:T(8,128)(2,1)S(1)}, bf16[3,128,128]{2,1,0:T(8,128)(2,1)S(1)}, u32[]{:S(2)}, u32[]{:S(2)}) collective-permute-start(bf16[3,128,128]{2,1,0:T(8,128)(2,1)S(1)} %get-tuple-element.86), channel_id=1, source_target_pairs={{0,3},{1,2},{2,1},{3,0},{4,7},{5,6},{6,5},{7,4},{8,11},{9,10},{10,... | collective-permute-start | bytes 294920 | tf_op jit(solution)/shard_map/ppermute | solution.py:497
  10.0 0.0 collective-permute-done.1.diagonal.refs_5_.diagonal0
  10.0 0.2 collective-permute-start.3
  10.3 0.0 collective-permute-done.across.refs_4_
  10.3 0.0 collective-permute-done.2.near.refs_6_.near0
  10.3 0.6 %rows_first.1 = (bf16[3,128,128]{2,1,0:T(8,128)(2,1)S(1)}, bf16[3,128,128]{2,1,0:T(8,128)(2,1)S(1)}, bf16[3,128,128]{2,1,0:T(8,128)(2,1)S(1)}, bf16[3,128,128]{2,1,0:T(8,128)(2,1)S(1)}) custom-call(bf16[2,3,256,512]{3,2,1,0:T(8,128)(2,1)S(1)} %get-tuple-element.71.rows_ref, bf16[3,128,128]{2,1,0:T(8,128)(2,1)S(1)} %collective-permute-done.across.refs_4_, ...), custom_call_target="tpu_custom_call" | custom-call | tf_op jit(solution)/shard_map/rows_first/pallas_call | solution.py:42
  10.8 1.8 %collective-permute-start.6 = (bf16[3,128,128]{2,1,0:T(8,128)(2,1)S(1)}, bf16[3,128,128]{2,1,0:T(8,128)(2,1)S(1)}, u32[]{:S(2)}, u32[]{:S(2)}) collective-permute-start(bf16[3,128,128]{2,1,0:T(8,128)(2,1)S(1)} %get-tuple-element.94), channel_id=1, source_target_pairs={{0,4},{1,5},{2,6},{3,7},{4,0},{5,1},{6,2},{7,3},{8,12},{9,13},{10,... | collective-permute-start | bytes 294920 | tf_op jit(solution)/shard_map/ppermute | solution.py:501
  12.7 1.5 %strips.1 = (bf16[3,512,1280]{2,1,0:T(8,128)(2,1)S(1)}, bf16[32,128]{1,0:T(8,128)(2,1)S(1)}, bf16[32,128]{1,0:T(8,128)(2,1)S(1)}) custom-call(s32[2,3]{1,0:T(2,128)S(1)} %get-tuple-element.75.wind_held, s32[8,1280]{1,0:T(8,128)S(1)} %get-tuple-element.76.refs_0_, s32[8,1280]{1,0:T(8,128)S(1)} %get-tuple-element.77.refs_1_, ...), custom_call_target="tpu_custom_call" | custom-call | tf_op jit(solution)/shard_map/strips/pallas_call | solution.py:42
  14.2 1.6 %collective-permute-done.3.refs_0_ = bf16[3,128,128]{2,1,0:T(8,128)(2,1)S(1)} collective-permute-done((bf16[3,128,128]{2,1,0:T(8,128)(2,1)S(1)}, bf16[3,128,128]{2,1,0:T(8,128)(2,1)S(1)}, u32[]{:S(2)}, u32[]{:S(2)}) %collective-permute-start.3) | collective-permute-done | bytes 98336 | tf_op jit(solution)/shard_map/ppermute | solution.py:497
  15.8 0.6 %rows_later.1 = (bf16[3,128,128]{2,1,0:T(8,128)(2,1)S(1)}, bf16[3,192,256]{2,1,0:T(8,128)(2,1)S(1)}, bf16[224,128]{1,0:T(8,128)(2,1)S(1)}, bf16[224,128]{1,0:T(8...) custom-call(bf16[2,3,256,512]{3,2,1,0:T(8,128)(2,1)S(1)} %get-tuple-element.71.rows_ref, ...), custom_call_target="tpu_custom_call" | custom-call | tf_op jit(solution)/shard_map/rows_later/pallas_call | solution.py:42
  16.4 1.6 %collective-permute-start.11 = (bf16[224,128]{1,0:T(8,128)(2,1)S(1)}, bf16[224,128]{1,0:T(8,128)(2,1)S(1)}, u32[]{:S(2)}, u32[]{:S(2)}) collective-permute-start(bf16[224,128]{1,0:T(8,128)(2,1)S(1)} %get-tuple-element.101), channel_id=1, source_target_pairs={{0,4},{1,5},{2,6},{3,7},{4,0},{5,1},{6,2},{7,3},{8,12},{9,13},{10,... | collective-permute-start | bytes 172040 | tf_op jit(solution)/shard_map/ppermute | solution.py:501
  18.0 0.6 %collective-permute-start.8 = (bf16[3,192,256]{2,1,0:T(8,128)(2,1)S(1)}, bf16[3,192,256]{2,1,0:T(8,128)(2,1)S(1)}, u32[]{:S(2)}, u32[]{:S(2)}) collective-permute-start(bf16[3,192,256]{2,1,0:T(8,128)(2,1)S(1)} %get-tuple-element.97), channel_id=1, source_target_pairs={{0,1},{1,0},{2,3},{3,2},{4,5},{5,4},{6,7},{7,6},{8,9},{9,8},{10,11... | collective-permute-start | bytes 884744 | tf_op jit(solution)/shard_map/ppermute | solution.py:497
  18.6 0.7 %phase.1 = f32[128,1280]{1,0:T(8,128)S(1)} custom-call(bf16[3,512,1280]{2,1,0:T(8,128)(2,1)S(1)} %get-tuple-element.81.mine_ref, bf16[3,512,1280]{2,1,0:T(8,128)(2,1)S(1)} %get-tuple-element.80.other_ref.cols_ref, bf16[3,128,128]{2,1,0:T(8,128)(2,1)S(1)} %get-tuple-element.92.mine0, bf16[3,128,128]{2,1,0:T(8,128)(2,1)S(1)} %get-tuple-element.93.mine1, ...), custom_call_target="tpu_custom_call" | custom-call | flops 10000000000 | bytes 8912896 | tf_op jit(solution)/shard_map/phase/pallas_call | solution.py:42
  19.3 1.6 %collective-permute-start.9 = (bf16[192,128]{1,0:T(8,128)(2,1)S(1)}, bf16[192,128]{1,0:T(8,128)(2,1)S(1)}, u32[]{:S(2)}, u32[]{:S(2)}) collective-permute-start(bf16[192,128]{1,0:T(8,128)(2,1)S(1)} %get-tuple-element.98), channel_id=1, source_target_pairs={{0,4},{1,5},{2,6},{3,7},{4,0},{5,1},{6,2},{7,3},{8,12},{9,13},{10,... | collective-permute-start | bytes 147464 | tf_op jit(solution)/shard_map/ppermute | solution.py:501
  20.9 0.4 %taken.1.phase = f32[128,1280]{1,0:T(8,128)S(1)} custom-call(bf16[3,512,1280]{2,1,0:T(8,128)(2,1)S(1)} %get-tuple-element.81.mine_ref, f32[128,1280]{1,0:T(8,128)S(1)} %phase.1, bf16[3,192,256]{2,1,0:T(8,128)(2,1)S(1)} %collective-permute-done.8.taken), custom_call_target="tpu_custom_call" | custom-call | tf_op jit(solution)/shard_map/taken/pallas_call | solution.py:42
  21.3 0.5 %collective-permute-done.12.sibling_came = bf16[224,128]{1,0:T(8,128)(2,1)S(1)} collective-permute-done((bf16[224,128]{1,0:T(8,128)(2,1)S(1)}, bf16[224,128]{1,0:T(8,128)(2,1)S(1)}, u32[]{:S(2)}, u32[]{:S(2)}) %collective-permute-start.12) | collective-permute-done | bytes 57376 | tf_op jit(solution)/shard_map/ppermute | solution.py:501
  21.8 0.5 %far.1 = (bf16[32,1408]{1,0:T(8,128)(2,1)S(1)}, bf16[32,1408]{1,0:T(8,128)(2,1)S(1)}, bf16[64,128]{1,0:T(8,128)(2,1)S(1)}) custom-call(bf16[3,512,1280]{2,1,0:T(8,128)(2,1)S(1)} %get-tuple-element.80.other_ref.cols_ref, f32[128,1280]{1,0:T(8,128)S(1)} %taken.1.phase, bf16[224,128]{1,0:T(8,128)(2,1)S(1)} %collective-permute-done.11.came, ...), custom_call_target="tpu_custom_call" | custom-call | flops 300000000 | bytes 4898816 | tf_op jit(solution)/shard_map/far/pallas_call | solution.py:42
  22.3 3.7 %collective-permute-start.14 = (bf16[32,1408]{1,0:T(8,128)(2,1)S(1)}, bf16[32,1408]{1,0:T(8,128)(2,1)S(1)}, u32[]{:S(2)}, u32[]{:S(2)}) collective-permute-start(bf16[32,1408]{1,0:T(8,128)(2,1)S(1)} %get-tuple-element.108), channel_id=1, source_target_pairs={{0,24},{4,28},{8,16},{12,20},{16,8},{20,12},{24,0},{28,4},{1,25},{... | collective-permute-start | bytes 270344 | tf_op jit(solution)/shard_map/ppermute | solution.py:617
  26.0 0.5 %rest.1 = (bf16[32,1280]{1,0:T(8,128)(2,1)S(1)}, bf16[32,1280]{1,0:T(8,128)(2,1)S(1)}) custom-call(bf16[3,512,1280]{2,1,0:T(8,128)(2,1)S(1)} %get-tuple-element.80.other_ref.cols_ref, f32[128,1280]{1,0:T(8,128)S(1)} %taken.1.phase, bf16[192,128]{1,0:T(8,128)(2,1)S(1)} %collective-permute-done.9.came, bf16[192,128]{1,0:T(8,128)(2,1)S(1)} %collective-permute-done.10.sibling_came), custom_call_target="tpu_custom_call" | custom-call | tf_op jit(solution)/shard_map/rest/pallas_call | solution.py:42
  26.5 1.4 %collective-permute-start.15 = (bf16[32,1280]{1,0:T(8,128)(2,1)S(1)}, bf16[32,1280]{1,0:T(8,128)(2,1)S(1)}, u32[]{:S(2)}, u32[]{:S(2)}) collective-permute-start(bf16[32,1280]{1,0:T(8,128)(2,1)S(1)} %get-tuple-element.117), channel_id=1, source_target_pairs={{0,16},{4,20},{8,24},{12,28},{16,0},{20,4},{24,8},{28,12},{1,17},{... | collective-permute-start | bytes 245768 | tf_op jit(solution)/shard_map/ppermute | solution.py:617
  27.9 1.8 %collective-permute-done.14.refs_1_.refs_3_ = bf16[32,1408]{1,0:T(8,128)(2,1)S(1)} collective-permute-done((bf16[32,1408]{1,0:T(8,128)(2,1)S(1)}, bf16[32,1408]{1,0:T(8,128)(2,1)S(1)}, u32[]{:S(2)}, u32[]{:S(2)}) %collective-permute-start.14) | collective-permute-done | bytes 90144 | tf_op jit(solution)/shard_map/ppermute | solution.py:617
  29.7 0.6 %optics.1 = (f32[32,1280]{1,0:T(8,128)S(1)}, bf16[256,512]{1,0:T(8,128)(2,1)S(1)}, bf16[128,64]{1,0:T(8,128)(2,1)S(1)}) custom-call(f32[32,1280]{1,0:T(8,128)S(1)} %get-tuple-element.109.amplitude, f32[128,128]{1,0:T(8,128)S(1)} %get-tuple-element.110.ones, f32[256,512]{1,0:T(8,128)S(1)} %get-tuple-element.111.columns, f32[128,64]{1,0:T(8,128)S(1)} %get-tuple-element.112.lines), custom_call_target="tpu_custom_call" | custom-call | tf_op jit(solution)/shard_map/optics/pallas_call | solution.py:42
  30.3 1.7 %collective-permute-done.13.refs_0_.refs_1_ = bf16[32,1408]{1,0:T(8,128)(2,1)S(1)} collective-permute-done((bf16[32,1408]{1,0:T(8,128)(2,1)S(1)}, bf16[32,1408]{1,0:T(8,128)(2,1)S(1)}, u32[]{:S(2)}, u32[]{:S(2)}) %collective-permute-start.13) | collective-permute-done | bytes 90144 | tf_op jit(solution)/shard_map/ppermute | solution.py:617
  32.0 1.1 %shift.1.refs_7_ = bf16[3,128,512]{2,1,0:T(8,128)(2,1)S(1)} custom-call(s32[2,3]{1,0:T(2,128)S(1)} %get-tuple-element.75.wind_held, bf16[3,128,512]{2,1,0:T(8,128)(2,1)S(1)} %get-tuple-element.122.own, bf16[3,128,128]{2,1,0:T(8,128)(2,1)S(1)} %collective-permute-done.2.near.refs_6_.near0, bf16[3,128,128]{2,1,0:T(8,128)(2,1)S(1)} %collective-permute-done.5.refs_2_.near1, ...), custom_call_target="tpu_custom_call" | custom-call | tf_op jit(solution)/shard_map/shift/pallas_call | solution.py:42
  33.1 0.5 %collective-permute-done.15.refs_2_ = bf16[32,1280]{1,0:T(8,128)(2,1)S(1)} collective-permute-done((bf16[32,1280]{1,0:T(8,128)(2,1)S(1)}, bf16[32,1280]{1,0:T(8,128)(2,1)S(1)}, u32[]{:S(2)}, u32[]{:S(2)}) %collective-permute-start.15) | collective-permute-done | bytes 81952 | tf_op jit(solution)/shard_map/ppermute | solution.py:617
  33.6 1.3 %imaging.1 = (f32[64,2560]{1,0:T(8,128)}, bf16[3,128,512]{2,1,0:T(8,128)(2,1)}) custom-call(bf16[32,1280]{1,0:T(8,128)(2,1)S(1)} %get-tuple-element.100.refs_0_, bf16[32,1408]{1,0:T(8,128)(2,1)S(1)} %collective-permute-done.13.refs_0_.refs_1_, bf16[32,1280]{1,0:T(8,128)(2,1)S(1)} %collective-permute-done.15.refs_2_, ...), custom_call_target="tpu_custom_call" | custom-call | flops 400000000 | bytes 2228224 | tf_op jit(solution)/shard_map/imaging/pallas_call | solution.py:42
  (12 shorter events, 0.0 us)
Async XLA Ops:
  1.8 8.2 %collective-permute-start.1 = (bf16[3,128,128]{2,1,0:T(8,128)(2,1)S(1)}, bf16[3,128,128]{2,1,0:T(8,128)(2,1)S(1)}, u32[]{:S(2)}, u32[]{:S(2)}) collective-permute-start(bf16[3,128,128]{2,1,0:T(8,128)(2,1)S(1)} %get-tuple-element.66), channel_id=1, source_target_pairs={{0,3},{1,2},{2,1},{3,0},{4,7},{5,6},{6,5},{7,4},{8,11},{9,10},{10,... | collective-permute-start | bytes 294920 | tf_op jit(solution)/shard_map/ppermute | solution.py:497
  4.2 6.1 %collective-permute-start = (bf16[3,128,128]{2,1,0:T(8,128)(2,1)S(1)}, bf16[3,128,128]{2,1,0:T(8,128)(2,1)S(1)}, u32[]{:S(2)}, u32[]{:S(2)}) collective-permute-start(bf16[3,128,128]{2,1,0:T(8,128)(2,1)S(1)} %get-tuple-element.65.keep.refs_7_), channel_id=1, source_target_pairs={{0,2},{1,3},{2,0},{3,1},{4,6},{5,7},{6,4},{7,5},{8,10},{9,11},{10,... | collective-permute-start | bytes 294920 | tf_op jit(solution)/shard_map/ppermute | solution.py:497
  4.8 5.4 %collective-permute-start.2 = (bf16[3,128,128]{2,1,0:T(8,128)(2,1)S(1)}, bf16[3,128,128]{2,1,0:T(8,128)(2,1)S(1)}, u32[]{:S(2)}, u32[]{:S(2)}) collective-permute-start(bf16[3,128,128]{2,1,0:T(8,128)(2,1)S(1)} %get-tuple-element.66), channel_id=1, source_target_pairs={{0,1},{1,0},{2,3},{3,2},{4,5},{5,4},{6,7},{7,6},{8,9},{9,8},{10,11... | collective-permute-start | bytes 294920 | tf_op jit(solution)/shard_map/ppermute | solution.py:497
  4.9 9.3 %collective-permute-start.5 = (bf16[3,128,128]{2,1,0:T(8,128)(2,1)S(1)}, bf16[3,128,128]{2,1,0:T(8,128)(2,1)S(1)}, u32[]{:S(2)}, u32[]{:S(2)}) collective-permute-start(bf16[3,128,128]{2,1,0:T(8,128)(2,1)S(1)} %get-tuple-element.86), channel_id=1, source_target_pairs={{0,1},{1,0},{2,3},{3,2},{4,5},{5,4},{6,7},{7,6},{8,9},{9,8},{10,11... | collective-permute-start | bytes 294920 | tf_op jit(solution)/shard_map/ppermute | solution.py:497
  8.5 5.7 %collective-permute-start.4 = (bf16[3,128,128]{2,1,0:T(8,128)(2,1)S(1)}, bf16[3,128,128]{2,1,0:T(8,128)(2,1)S(1)}, u32[]{:S(2)}, u32[]{:S(2)}) collective-permute-start(bf16[3,128,128]{2,1,0:T(8,128)(2,1)S(1)} %get-tuple-element.86), channel_id=1, source_target_pairs={{0,3},{1,2},{2,1},{3,0},{4,7},{5,6},{6,5},{7,4},{8,11},{9,10},{10,... | collective-permute-start | bytes 294920 | tf_op jit(solution)/shard_map/ppermute | solution.py:497
  10.0 5.8 %collective-permute-start.3 = (bf16[3,128,128]{2,1,0:T(8,128)(2,1)S(1)}, bf16[3,128,128]{2,1,0:T(8,128)(2,1)S(1)}, u32[]{:S(2)}, u32[]{:S(2)}) collective-permute-start(bf16[3,128,128]{2,1,0:T(8,128)(2,1)S(1)} %get-tuple-element.85.refs_3_), channel_id=1, source_target_pairs={{0,2},{1,3},{2,0},{3,1},{4,6},{5,7},{6,4},{7,5},{8,10},{9,11},{10,... | collective-permute-start | bytes 294920 | tf_op jit(solution)/shard_map/ppermute | solution.py:497
  10.8 7.7 %collective-permute-start.6 = (bf16[3,128,128]{2,1,0:T(8,128)(2,1)S(1)}, bf16[3,128,128]{2,1,0:T(8,128)(2,1)S(1)}, u32[]{:S(2)}, u32[]{:S(2)}) collective-permute-start(bf16[3,128,128]{2,1,0:T(8,128)(2,1)S(1)} %get-tuple-element.94), channel_id=1, source_target_pairs={{0,4},{1,5},{2,6},{3,7},{4,0},{5,1},{6,2},{7,3},{8,12},{9,13},{10,... | collective-permute-start | bytes 294920 | tf_op jit(solution)/shard_map/ppermute | solution.py:501
  12.7 5.9 %collective-permute-start.7 = (bf16[3,128,128]{2,1,0:T(8,128)(2,1)S(1)}, bf16[3,128,128]{2,1,0:T(8,128)(2,1)S(1)}, u32[]{:S(2)}, u32[]{:S(2)}) collective-permute-start(bf16[3,128,128]{2,1,0:T(8,128)(2,1)S(1)} %get-tuple-element.95), channel_id=1, source_target_pairs={{0,5},{1,4},{2,7},{3,6},{4,1},{5,0},{6,3},{7,2},{8,13},{9,12},{10,... | collective-permute-start | bytes 294920 | tf_op jit(solution)/shard_map/ppermute | solution.py:501
  16.4 4.9 %collective-permute-start.11 = (bf16[224,128]{1,0:T(8,128)(2,1)S(1)}, bf16[224,128]{1,0:T(8,128)(2,1)S(1)}, u32[]{:S(2)}, u32[]{:S(2)}) collective-permute-start(bf16[224,128]{1,0:T(8,128)(2,1)S(1)} %get-tuple-element.101), channel_id=1, source_target_pairs={{0,4},{1,5},{2,6},{3,7},{4,0},{5,1},{6,2},{7,3},{8,12},{9,13},{10,... | collective-permute-start | bytes 172040 | tf_op jit(solution)/shard_map/ppermute | solution.py:501
  18.0 3.9 %collective-permute-start.12 = (bf16[224,128]{1,0:T(8,128)(2,1)S(1)}, bf16[224,128]{1,0:T(8,128)(2,1)S(1)}, u32[]{:S(2)}, u32[]{:S(2)}) collective-permute-start(bf16[224,128]{1,0:T(8,128)(2,1)S(1)} %get-tuple-element.102), channel_id=1, source_target_pairs={{0,5},{1,4},{2,7},{3,6},{4,1},{5,0},{6,3},{7,2},{8,13},{9,12},{10,... | collective-permute-start | bytes 172040 | tf_op jit(solution)/shard_map/ppermute | solution.py:501
  18.0 2.9 %collective-permute-start.8 = (bf16[3,192,256]{2,1,0:T(8,128)(2,1)S(1)}, bf16[3,192,256]{2,1,0:T(8,128)(2,1)S(1)}, u32[]{:S(2)}, u32[]{:S(2)}) collective-permute-start(bf16[3,192,256]{2,1,0:T(8,128)(2,1)S(1)} %get-tuple-element.97), channel_id=1, source_target_pairs={{0,1},{1,0},{2,3},{3,2},{4,5},{5,4},{6,7},{7,6},{8,9},{9,8},{10,11... | collective-permute-start | bytes 884744 | tf_op jit(solution)/shard_map/ppermute | solution.py:497
  19.3 6.7 %collective-permute-start.9 = (bf16[192,128]{1,0:T(8,128)(2,1)S(1)}, bf16[192,128]{1,0:T(8,128)(2,1)S(1)}, u32[]{:S(2)}, u32[]{:S(2)}) collective-permute-start(bf16[192,128]{1,0:T(8,128)(2,1)S(1)} %get-tuple-element.98), channel_id=1, source_target_pairs={{0,4},{1,5},{2,6},{3,7},{4,0},{5,1},{6,2},{7,3},{8,12},{9,13},{10,... | collective-permute-start | bytes 147464 | tf_op jit(solution)/shard_map/ppermute | solution.py:501
  20.9 5.1 %collective-permute-start.10 = (bf16[192,128]{1,0:T(8,128)(2,1)S(1)}, bf16[192,128]{1,0:T(8,128)(2,1)S(1)}, u32[]{:S(2)}, u32[]{:S(2)}) collective-permute-start(bf16[192,128]{1,0:T(8,128)(2,1)S(1)} %get-tuple-element.99), channel_id=1, source_target_pairs={{0,5},{1,4},{2,7},{3,6},{4,1},{5,0},{6,3},{7,2},{8,13},{9,12},{10,... | collective-permute-start | bytes 147464 | tf_op jit(solution)/shard_map/ppermute | solution.py:501
  22.3 7.4 %collective-permute-start.14 = (bf16[32,1408]{1,0:T(8,128)(2,1)S(1)}, bf16[32,1408]{1,0:T(8,128)(2,1)S(1)}, u32[]{:S(2)}, u32[]{:S(2)}) collective-permute-start(bf16[32,1408]{1,0:T(8,128)(2,1)S(1)} %get-tuple-element.108), channel_id=1, source_target_pairs={{0,24},{4,28},{8,16},{12,20},{16,8},{20,12},{24,0},{28,4},{1,25},{... | collective-permute-start | bytes 270344 | tf_op jit(solution)/shard_map/ppermute | solution.py:617
  26.0 6.0 %collective-permute-start.13 = (bf16[32,1408]{1,0:T(8,128)(2,1)S(1)}, bf16[32,1408]{1,0:T(8,128)(2,1)S(1)}, u32[]{:S(2)}, u32[]{:S(2)}) collective-permute-start(bf16[32,1408]{1,0:T(8,128)(2,1)S(1)} %get-tuple-element.103), channel_id=1, source_target_pairs={{0,8},{4,12},{8,0},{12,4},{16,24},{20,28},{24,16},{28,20},{1,9},{5... | collective-permute-start | bytes 270344 | tf_op jit(solution)/shard_map/ppermute | solution.py:617
  26.5 7.2 %collective-permute-start.15 = (bf16[32,1280]{1,0:T(8,128)(2,1)S(1)}, bf16[32,1280]{1,0:T(8,128)(2,1)S(1)}, u32[]{:S(2)}, u32[]{:S(2)}) collective-permute-start(bf16[32,1280]{1,0:T(8,128)(2,1)S(1)} %get-tuple-element.117), channel_id=1, source_target_pairs={{0,16},{4,20},{8,24},{12,28},{16,0},{20,4},{24,8},{28,12},{1,17},{... | collective-permute-start | bytes 245768 | tf_op jit(solution)/shard_map/ppermute | solution.py:617

commit v22 on v21

--- a/solution.py
+++ b/solution.py
@@ -520,6 +520,7 @@
     diagonal0 = swap(give0, 3)
     near0 = swap(give0, 1)
     near1 = swap(give1, 1)
+    diagonal1 = swap(give1, 3)
     ones = np.kron(np.eye(LANES // SUB_PIX), np.ones((SUB_PIX, SUB_PIX))).astype(np.float32)
     optics_in = (amplitude, jnp.asarray(ones), *[jnp.asarray(table) for table in tables_of(rows)])
     copies = [shape(*array.shape, dtype=array.dtype) for array in (screens, *optics_in)]
@@ -538,9 +539,8 @@
     )
     tables, (own, *optics_in) = loaded[:4], loaded[4:]
     wind = ints[0]
-    keep1, give1, own = lax.optimization_barrier((keep1, give1, own))
+    keep1, own = lax.optimization_barrier((keep1, own))
     across1 = swap(keep1, 2)
-    diagonal1 = swap(give1, 3)
     across0, diagonal0, row_weights, cols = lax.optimization_barrier((across0, diagonal0, row_weights, cols))
 
     projected = shape(layers, half, width)

time: 35.1 us -> 34.4 us (0.980)
  starting transfers between devices: 16.1 us -> 15.7 us
  waiting for transfers between devices: 6.07 us -> 5.68 us
    ppermute x7, waiting for transfers between devices: 1.6 us -> 0.6 us  [swap(): return lax.ppermute(value, 'dir', [(i, i ^ bits) for i in range(n_dir)])]
  transfers between devices with their start and end apart: 16 -> 16, of which waited for: 5 -> 6; matrix products, arithmetic and copies ran while one was open for 0% -> 0% of each run, Pallas kernels for 27% -> 28%
where the time goes in v22:
time: 34.4 us; the launch traced here: 34.2 us
  starting transfers between devices  15.7 us (46%)
  Pallas kernels  12.1 us (35%)
  waiting for transfers between devices  5.68 us (17%)
  between operations  0.76 us (2%)
    pallas_call x12, Pallas kernels, call(): pl.pallas_call(kernel, out_shape=out_shape, in_specs=in_specs, out_specs=...  12.1 us
    ppermute x7, starting transfers between devices, swap(): return lax.ppermute(value, 'dir', [(i, i ^ bits) for i in range(n_dir)])  5.95 us
    ppermute x6, starting transfers between devices, partner(): lax.ppermute(value, ('layer', 'dir'), [(i, i ^ n_dir ^ bits) for i in ran...  4.96 us
    ppermute x3, starting transfers between devices, per_device(): lax.ppermute(received[k], 'layer', [(i, i ^ 2 * k) for i in range(n_layer)])  4.82 us
    ppermute x3, waiting for transfers between devices, per_device(): lax.ppermute(received[k], 'layer', [(i, i ^ 2 * k) for i in range(n_layer)])  4.2 us
    ppermute x6, waiting for transfers between devices, partner(): lax.ppermute(value, ('layer', 'dir'), [(i, i ^ n_dir ^ bits) for i in ran...  0.88 us
  transfers between devices with their start and end apart: 16, of which 6 were waited for; matrix products, arithmetic and copies ran while one was open for 0% of the time, Pallas kernels for 28%

profile of v22, /device:TPU:0, one launch (start us, length us, event | category | flops | bytes accessed | tf_op | source)
XLA Modules:
  0.0 34.2 jit_solution(17997941533946853844)
XLA Ops:
  0.6 1.1 %split.1 = (bf16[3,128,128]{2,1,0:T(8,128)(2,1)S(1)}, bf16[3,128,128]{2,1,0:T(8,128)(2,1)S(1)}, bf16[3,128,128]{2,1,0:T(8,128)(2,1)S(1)}, bf16[3,128,128]{2,1,0:...) custom-call(bf16[3,128,512]{2,1,0:T(8,128)(2,1)} %refs_0_.1, ...), custom_call_target="tpu_custom_call" | custom-call | tf_op jit(solution)/shard_map/split/pallas_call | solution.py:42
  1.8 2.4 %collective-permute-start.1 = (bf16[3,128,128]{2,1,0:T(8,128)(2,1)S(1)}, bf16[3,128,128]{2,1,0:T(8,128)(2,1)S(1)}, u32[]{:S(2)}, u32[]{:S(2)}) collective-permute-start(bf16[3,128,128]{2,1,0:T(8,128)(2,1)S(1)} %get-tuple-element.65), channel_id=1, source_target_pairs={{0,3},{1,2},{2,1},{3,0},{4,7},{5,6},{6,5},{7,4},{8,11},{9,10},{10,... | collective-permute-start | bytes 294920 | tf_op jit(solution)/shard_map/ppermute | solution.py:497
  4.2 0.6 %collective-permute-start = (bf16[3,128,128]{2,1,0:T(8,128)(2,1)S(1)}, bf16[3,128,128]{2,1,0:T(8,128)(2,1)S(1)}, u32[]{:S(2)}, u32[]{:S(2)}) collective-permute-start(bf16[3,128,128]{2,1,0:T(8,128)(2,1)S(1)} %get-tuple-element.64.keep.refs_7_), channel_id=1, source_target_pairs={{0,2},{1,3},{2,0},{3,1},{4,6},{5,7},{6,4},{7,5},{8,10},{9,11},{10,... | collective-permute-start | bytes 294920 | tf_op jit(solution)/shard_map/ppermute | solution.py:497
  4.8 0.0 collective-permute-start.2
  4.9 0.5 %collective-permute-start.5 = (bf16[3,128,128]{2,1,0:T(8,128)(2,1)S(1)}, bf16[3,128,128]{2,1,0:T(8,128)(2,1)S(1)}, u32[]{:S(2)}, u32[]{:S(2)}) collective-permute-start(bf16[3,128,128]{2,1,0:T(8,128)(2,1)S(1)} %get-tuple-element.84), channel_id=1, source_target_pairs={{0,1},{1,0},{2,3},{3,2},{4,5},{5,4},{6,7},{7,6},{8,9},{9,8},{10,11... | collective-permute-start | bytes 294920 | tf_op jit(solution)/shard_map/ppermute | solution.py:497
  5.4 1.4 %collective-permute-start.4 = (bf16[3,128,128]{2,1,0:T(8,128)(2,1)S(1)}, bf16[3,128,128]{2,1,0:T(8,128)(2,1)S(1)}, u32[]{:S(2)}, u32[]{:S(2)}) collective-permute-start(bf16[3,128,128]{2,1,0:T(8,128)(2,1)S(1)} %get-tuple-element.84), channel_id=1, source_target_pairs={{0,3},{1,2},{2,1},{3,0},{4,7},{5,6},{6,5},{7,4},{8,11},{9,10},{10,... | collective-permute-start | bytes 294920 | tf_op jit(solution)/shard_map/ppermute | solution.py:497
  6.8 3.2 %weights.1 = (bf16[2,3,256,512]{3,2,1,0:T(8,128)(2,1)S(1)}, bf16[3,512,1280]{2,1,0:T(8,128)(2,1)S(1)}, s32[8,1280]{1,0:T(8,128)S(1)}, s32[8,1280]{1,0:T(8,128)S(...) custom-call(s32[2,3]{1,0:T(2,128)S(1)} %get-tuple-element.74.wind_he, ...), custom_call_target="tpu_custom_call" | custom-call | tf_op jit(solution)/shard_map/weights/pallas_call | solution.py:42
  9.9 0.0 collective-permute-done.1.diagonal.refs_5_.diagonal0
  10.0 0.3 collective-permute-start.3
  10.3 0.6 %rows_first.1 = (bf16[3,128,128]{2,1,0:T(8,128)(2,1)S(1)}, bf16[3,128,128]{2,1,0:T(8,128)(2,1)S(1)}, bf16[3,128,128]{2,1,0:T(8,128)(2,1)S(1)}, bf16[3,128,128]{2,1,0:T(8,128)(2,1)S(1)}) custom-call(bf16[2,3,256,512]{3,2,1,0:T(8,128)(2,1)S(1)} %get-tuple-element.70.rows_ref, bf16[3,128,128]{2,1,0:T(8,128)(2,1)S(1)} %collective-permute-done.across.refs_4_, ...), custom_call_target="tpu_custom_call" | custom-call | tf_op jit(solution)/shard_map/rows_first/pallas_call | solution.py:42
  10.9 1.8 %collective-permute-start.6 = (bf16[3,128,128]{2,1,0:T(8,128)(2,1)S(1)}, bf16[3,128,128]{2,1,0:T(8,128)(2,1)S(1)}, u32[]{:S(2)}, u32[]{:S(2)}) collective-permute-start(bf16[3,128,128]{2,1,0:T(8,128)(2,1)S(1)} %get-tuple-element.92), channel_id=1, source_target_pairs={{0,4},{1,5},{2,6},{3,7},{4,0},{5,1},{6,2},{7,3},{8,12},{9,13},{10,... | collective-permute-start | bytes 294920 | tf_op jit(solution)/shard_map/ppermute | solution.py:501
  12.7 1.5 %strips.1 = (bf16[3,512,1280]{2,1,0:T(8,128)(2,1)S(1)}, bf16[32,128]{1,0:T(8,128)(2,1)S(1)}, bf16[32,128]{1,0:T(8,128)(2,1)S(1)}) custom-call(s32[2,3]{1,0:T(2,128)S(1)} %get-tuple-element.74.wind_held, s32[8,1280]{1,0:T(8,128)S(1)} %get-tuple-element.75.refs_0_, s32[8,1280]{1,0:T(8,128)S(1)} %get-tuple-element.76.refs_1_, ...), custom_call_target="tpu_custom_call" | custom-call | tf_op jit(solution)/shard_map/strips/pallas_call | solution.py:42
  14.2 0.6 %collective-permute-done.3.refs_0_ = bf16[3,128,128]{2,1,0:T(8,128)(2,1)S(1)} collective-permute-done((bf16[3,128,128]{2,1,0:T(8,128)(2,1)S(1)}, bf16[3,128,128]{2,1,0:T(8,128)(2,1)S(1)}, u32[]{:S(2)}, u32[]{:S(2)}) %collective-permute-start.3) | collective-permute-done | bytes 98336 | tf_op jit(solution)/shard_map/ppermute | solution.py:497
  14.8 0.6 %rows_later.1 = (bf16[3,128,128]{2,1,0:T(8,128)(2,1)S(1)}, bf16[3,192,256]{2,1,0:T(8,128)(2,1)S(1)}, bf16[224,128]{1,0:T(8,128)(2,1)S(1)}, bf16[224,128]{1,0:T(8...) custom-call(bf16[2,3,256,512]{3,2,1,0:T(8,128)(2,1)S(1)} %get-tuple-element.70.rows_ref, ...), custom_call_target="tpu_custom_call" | custom-call | tf_op jit(solution)/shard_map/rows_later/pallas_call | solution.py:42
  15.4 1.6 %collective-permute-start.11 = (bf16[224,128]{1,0:T(8,128)(2,1)S(1)}, bf16[224,128]{1,0:T(8,128)(2,1)S(1)}, u32[]{:S(2)}, u32[]{:S(2)}) collective-permute-start(bf16[224,128]{1,0:T(8,128)(2,1)S(1)} %get-tuple-element.99), channel_id=1, source_target_pairs={{0,4},{1,5},{2,6},{3,7},{4,0},{5,1},{6,2},{7,3},{8,12},{9,13},{10,... | collective-permute-start | bytes 172040 | tf_op jit(solution)/shard_map/ppermute | solution.py:501
  17.0 0.6 %collective-permute-start.8 = (bf16[3,192,256]{2,1,0:T(8,128)(2,1)S(1)}, bf16[3,192,256]{2,1,0:T(8,128)(2,1)S(1)}, u32[]{:S(2)}, u32[]{:S(2)}) collective-permute-start(bf16[3,192,256]{2,1,0:T(8,128)(2,1)S(1)} %get-tuple-element.95), channel_id=1, source_target_pairs={{0,1},{1,0},{2,3},{3,2},{4,5},{5,4},{6,7},{7,6},{8,9},{9,8},{10,11... | collective-permute-start | bytes 884744 | tf_op jit(solution)/shard_map/ppermute | solution.py:497
  17.6 0.2 collective-permute-done.7.sibling_came
  17.8 0.7 %phase.1 = f32[128,1280]{1,0:T(8,128)S(1)} custom-call(bf16[3,512,1280]{2,1,0:T(8,128)(2,1)S(1)} %get-tuple-element.80.mine_ref, bf16[3,512,1280]{2,1,0:T(8,128)(2,1)S(1)} %get-tuple-element.79.other_ref.cols_ref, bf16[3,128,128]{2,1,0:T(8,128)(2,1)S(1)} %get-tuple-element.90.mine0, bf16[3,128,128]{2,1,0:T(8,128)(2,1)S(1)} %get-tuple-element.91.mine1, ...), custom_call_target="tpu_custom_call" | custom-call | flops 10000000000 | bytes 8912896 | tf_op jit(solution)/shard_map/phase/pallas_call | solution.py:42
  18.5 1.4 %collective-permute-start.9 = (bf16[192,128]{1,0:T(8,128)(2,1)S(1)}, bf16[192,128]{1,0:T(8,128)(2,1)S(1)}, u32[]{:S(2)}, u32[]{:S(2)}) collective-permute-start(bf16[192,128]{1,0:T(8,128)(2,1)S(1)} %get-tuple-element.96), channel_id=1, source_target_pairs={{0,4},{1,5},{2,6},{3,7},{4,0},{5,1},{6,2},{7,3},{8,12},{9,13},{10,... | collective-permute-start | bytes 147464 | tf_op jit(solution)/shard_map/ppermute | solution.py:501
  19.9 0.2 collective-permute-start.10
  20.0 0.4 %taken.1.phase = f32[128,1280]{1,0:T(8,128)S(1)} custom-call(bf16[3,512,1280]{2,1,0:T(8,128)(2,1)S(1)} %get-tuple-element.80.mine_ref, f32[128,1280]{1,0:T(8,128)S(1)} %phase.1, bf16[3,192,256]{2,1,0:T(8,128)(2,1)S(1)} %collective-permute-done.8.taken), custom_call_target="tpu_custom_call" | custom-call | tf_op jit(solution)/shard_map/taken/pallas_call | solution.py:42
  20.5 0.7 %collective-permute-done.12.sibling_came = bf16[224,128]{1,0:T(8,128)(2,1)S(1)} collective-permute-done((bf16[224,128]{1,0:T(8,128)(2,1)S(1)}, bf16[224,128]{1,0:T(8,128)(2,1)S(1)}, u32[]{:S(2)}, u32[]{:S(2)}) %collective-permute-start.12) | collective-permute-done | bytes 57376 | tf_op jit(solution)/shard_map/ppermute | solution.py:501
  21.1 0.5 %far.1 = (bf16[32,1408]{1,0:T(8,128)(2,1)S(1)}, bf16[32,1408]{1,0:T(8,128)(2,1)S(1)}, bf16[64,128]{1,0:T(8,128)(2,1)S(1)}) custom-call(bf16[3,512,1280]{2,1,0:T(8,128)(2,1)S(1)} %get-tuple-element.79.other_ref.cols_ref, f32[128,1280]{1,0:T(8,128)S(1)} %taken.1.phase, bf16[224,128]{1,0:T(8,128)(2,1)S(1)} %collective-permute-done.11.came, ...), custom_call_target="tpu_custom_call" | custom-call | flops 300000000 | bytes 4898816 | tf_op jit(solution)/shard_map/far/pallas_call | solution.py:42
  21.6 3.7 %collective-permute-start.14 = (bf16[32,1408]{1,0:T(8,128)(2,1)S(1)}, bf16[32,1408]{1,0:T(8,128)(2,1)S(1)}, u32[]{:S(2)}, u32[]{:S(2)}) collective-permute-start(bf16[32,1408]{1,0:T(8,128)(2,1)S(1)} %get-tuple-element.106), channel_id=1, source_target_pairs={{0,24},{4,28},{8,16},{12,20},{16,8},{20,12},{24,0},{28,4},{1,25},{... | collective-permute-start | bytes 270344 | tf_op jit(solution)/shard_map/ppermute | solution.py:617
  25.3 0.5 %rest.1 = (bf16[32,1280]{1,0:T(8,128)(2,1)S(1)}, bf16[32,1280]{1,0:T(8,128)(2,1)S(1)}) custom-call(bf16[3,512,1280]{2,1,0:T(8,128)(2,1)S(1)} %get-tuple-element.79.other_ref.cols_ref, f32[128,1280]{1,0:T(8,128)S(1)} %taken.1.phase, bf16[192,128]{1,0:T(8,128)(2,1)S(1)} %collective-permute-done.9.came, bf16[192,128]{1,0:T(8,128)(2,1)S(1)} %collective-permute-done.10.sibling_came), custom_call_target="tpu_custom_call" | custom-call | tf_op jit(solution)/shard_map/rest/pallas_call | solution.py:42
  25.8 1.2 %collective-permute-start.15 = (bf16[32,1280]{1,0:T(8,128)(2,1)S(1)}, bf16[32,1280]{1,0:T(8,128)(2,1)S(1)}, u32[]{:S(2)}, u32[]{:S(2)}) collective-permute-start(bf16[32,1280]{1,0:T(8,128)(2,1)S(1)} %get-tuple-element.115), channel_id=1, source_target_pairs={{0,16},{4,20},{8,24},{12,28},{16,0},{20,4},{24,8},{28,12},{1,17},{... | collective-permute-start | bytes 245768 | tf_op jit(solution)/shard_map/ppermute | solution.py:617
  26.9 2.1 %collective-permute-done.14.refs_1_.refs_3_ = bf16[32,1408]{1,0:T(8,128)(2,1)S(1)} collective-permute-done((bf16[32,1408]{1,0:T(8,128)(2,1)S(1)}, bf16[32,1408]{1,0:T(8,128)(2,1)S(1)}, u32[]{:S(2)}, u32[]{:S(2)}) %collective-permute-start.14) | collective-permute-done | bytes 90144 | tf_op jit(solution)/shard_map/ppermute | solution.py:617
  29.0 0.6 %optics.1 = (f32[32,1280]{1,0:T(8,128)S(1)}, bf16[256,512]{1,0:T(8,128)(2,1)S(1)}, bf16[128,64]{1,0:T(8,128)(2,1)S(1)}) custom-call(f32[32,1280]{1,0:T(8,128)S(1)} %get-tuple-element.107.amplitude, f32[128,128]{1,0:T(8,128)S(1)} %get-tuple-element.108.ones, f32[256,512]{1,0:T(8,128)S(1)} %get-tuple-element.109.columns, f32[128,64]{1,0:T(8,128)S(1)} %get-tuple-element.110.lines), custom_call_target="tpu_custom_call" | custom-call | tf_op jit(solution)/shard_map/optics/pallas_call | solution.py:42
  29.6 1.6 %collective-permute-done.13.refs_0_.refs_1_ = bf16[32,1408]{1,0:T(8,128)(2,1)S(1)} collective-permute-done((bf16[32,1408]{1,0:T(8,128)(2,1)S(1)}, bf16[32,1408]{1,0:T(8,128)(2,1)S(1)}, u32[]{:S(2)}, u32[]{:S(2)}) %collective-permute-start.13) | collective-permute-done | bytes 90144 | tf_op jit(solution)/shard_map/ppermute | solution.py:617
  31.2 1.1 %shift.1.refs_7_ = bf16[3,128,512]{2,1,0:T(8,128)(2,1)S(1)} custom-call(s32[2,3]{1,0:T(2,128)S(1)} %get-tuple-element.74.wind_held, bf16[3,128,512]{2,1,0:T(8,128)(2,1)S(1)} %get-tuple-element.120.own, bf16[3,128,128]{2,1,0:T(8,128)(2,1)S(1)} %collective-permute-done.2.near.refs_6_.near0, bf16[3,128,128]{2,1,0:T(8,128)(2,1)S(1)} %collective-permute-done.5.refs_2_.near1, ...), custom_call_target="tpu_custom_call" | custom-call | tf_op jit(solution)/shard_map/shift/pallas_call | solution.py:42
  32.4 0.5 %collective-permute-done.15.refs_2_ = bf16[32,1280]{1,0:T(8,128)(2,1)S(1)} collective-permute-done((bf16[32,1280]{1,0:T(8,128)(2,1)S(1)}, bf16[32,1280]{1,0:T(8,128)(2,1)S(1)}, u32[]{:S(2)}, u32[]{:S(2)}) %collective-permute-start.15) | collective-permute-done | bytes 81952 | tf_op jit(solution)/shard_map/ppermute | solution.py:617
  32.9 1.3 %imaging.1 = (f32[64,2560]{1,0:T(8,128)}, bf16[3,128,512]{2,1,0:T(8,128)(2,1)}) custom-call(bf16[32,1280]{1,0:T(8,128)(2,1)S(1)} %get-tuple-element.98.refs_0_, bf16[32,1408]{1,0:T(8,128)(2,1)S(1)} %collective-permute-done.13.refs_0_.refs_1_, bf16[32,1280]{1,0:T(8,128)(2,1)S(1)} %collective-permute-done.15.refs_2_, ...), custom_call_target="tpu_custom_call" | custom-call | flops 400000000 | bytes 2228224 | tf_op jit(solution)/shard_map/imaging/pallas_call | solution.py:42
  (12 shorter events, 0.0 us)
Async XLA Ops:
  1.8 8.2 %collective-permute-start.1 = (bf16[3,128,128]{2,1,0:T(8,128)(2,1)S(1)}, bf16[3,128,128]{2,1,0:T(8,128)(2,1)S(1)}, u32[]{:S(2)}, u32[]{:S(2)}) collective-permute-start(bf16[3,128,128]{2,1,0:T(8,128)(2,1)S(1)} %get-tuple-element.65), channel_id=1, source_target_pairs={{0,3},{1,2},{2,1},{3,0},{4,7},{5,6},{6,5},{7,4},{8,11},{9,10},{10,... | collective-permute-start | bytes 294920 | tf_op jit(solution)/shard_map/ppermute | solution.py:497
  4.2 6.1 %collective-permute-start = (bf16[3,128,128]{2,1,0:T(8,128)(2,1)S(1)}, bf16[3,128,128]{2,1,0:T(8,128)(2,1)S(1)}, u32[]{:S(2)}, u32[]{:S(2)}) collective-permute-start(bf16[3,128,128]{2,1,0:T(8,128)(2,1)S(1)} %get-tuple-element.64.keep.refs_7_), channel_id=1, source_target_pairs={{0,2},{1,3},{2,0},{3,1},{4,6},{5,7},{6,4},{7,5},{8,10},{9,11},{10,... | collective-permute-start | bytes 294920 | tf_op jit(solution)/shard_map/ppermute | solution.py:497
  4.8 5.4 %collective-permute-start.2 = (bf16[3,128,128]{2,1,0:T(8,128)(2,1)S(1)}, bf16[3,128,128]{2,1,0:T(8,128)(2,1)S(1)}, u32[]{:S(2)}, u32[]{:S(2)}) collective-permute-start(bf16[3,128,128]{2,1,0:T(8,128)(2,1)S(1)} %get-tuple-element.65), channel_id=1, source_target_pairs={{0,1},{1,0},{2,3},{3,2},{4,5},{5,4},{6,7},{7,6},{8,9},{9,8},{10,11... | collective-permute-start | bytes 294920 | tf_op jit(solution)/shard_map/ppermute | solution.py:497
  4.9 9.3 %collective-permute-start.5 = (bf16[3,128,128]{2,1,0:T(8,128)(2,1)S(1)}, bf16[3,128,128]{2,1,0:T(8,128)(2,1)S(1)}, u32[]{:S(2)}, u32[]{:S(2)}) collective-permute-start(bf16[3,128,128]{2,1,0:T(8,128)(2,1)S(1)} %get-tuple-element.84), channel_id=1, source_target_pairs={{0,1},{1,0},{2,3},{3,2},{4,5},{5,4},{6,7},{7,6},{8,9},{9,8},{10,11... | collective-permute-start | bytes 294920 | tf_op jit(solution)/shard_map/ppermute | solution.py:497
  5.4 8.8 %collective-permute-start.4 = (bf16[3,128,128]{2,1,0:T(8,128)(2,1)S(1)}, bf16[3,128,128]{2,1,0:T(8,128)(2,1)S(1)}, u32[]{:S(2)}, u32[]{:S(2)}) collective-permute-start(bf16[3,128,128]{2,1,0:T(8,128)(2,1)S(1)} %get-tuple-element.84), channel_id=1, source_target_pairs={{0,3},{1,2},{2,1},{3,0},{4,7},{5,6},{6,5},{7,4},{8,11},{9,10},{10,... | collective-permute-start | bytes 294920 | tf_op jit(solution)/shard_map/ppermute | solution.py:497
  10.0 4.8 %collective-permute-start.3 = (bf16[3,128,128]{2,1,0:T(8,128)(2,1)S(1)}, bf16[3,128,128]{2,1,0:T(8,128)(2,1)S(1)}, u32[]{:S(2)}, u32[]{:S(2)}) collective-permute-start(bf16[3,128,128]{2,1,0:T(8,128)(2,1)S(1)} %get-tuple-element.83.refs_3_), channel_id=1, source_target_pairs={{0,2},{1,3},{2,0},{3,1},{4,6},{5,7},{6,4},{7,5},{8,10},{9,11},{10,... | collective-permute-start | bytes 294920 | tf_op jit(solution)/shard_map/ppermute | solution.py:497
  10.9 6.7 %collective-permute-start.6 = (bf16[3,128,128]{2,1,0:T(8,128)(2,1)S(1)}, bf16[3,128,128]{2,1,0:T(8,128)(2,1)S(1)}, u32[]{:S(2)}, u32[]{:S(2)}) collective-permute-start(bf16[3,128,128]{2,1,0:T(8,128)(2,1)S(1)} %get-tuple-element.92), channel_id=1, source_target_pairs={{0,4},{1,5},{2,6},{3,7},{4,0},{5,1},{6,2},{7,3},{8,12},{9,13},{10,... | collective-permute-start | bytes 294920 | tf_op jit(solution)/shard_map/ppermute | solution.py:501
  12.7 5.1 %collective-permute-start.7 = (bf16[3,128,128]{2,1,0:T(8,128)(2,1)S(1)}, bf16[3,128,128]{2,1,0:T(8,128)(2,1)S(1)}, u32[]{:S(2)}, u32[]{:S(2)}) collective-permute-start(bf16[3,128,128]{2,1,0:T(8,128)(2,1)S(1)} %get-tuple-element.93), channel_id=1, source_target_pairs={{0,5},{1,4},{2,7},{3,6},{4,1},{5,0},{6,3},{7,2},{8,13},{9,12},{10,... | collective-permute-start | bytes 294920 | tf_op jit(solution)/shard_map/ppermute | solution.py:501
  15.4 5.1 %collective-permute-start.11 = (bf16[224,128]{1,0:T(8,128)(2,1)S(1)}, bf16[224,128]{1,0:T(8,128)(2,1)S(1)}, u32[]{:S(2)}, u32[]{:S(2)}) collective-permute-start(bf16[224,128]{1,0:T(8,128)(2,1)S(1)} %get-tuple-element.99), channel_id=1, source_target_pairs={{0,4},{1,5},{2,6},{3,7},{4,0},{5,1},{6,2},{7,3},{8,12},{9,13},{10,... | collective-permute-start | bytes 172040 | tf_op jit(solution)/shard_map/ppermute | solution.py:501
  17.0 4.2 %collective-permute-start.12 = (bf16[224,128]{1,0:T(8,128)(2,1)S(1)}, bf16[224,128]{1,0:T(8,128)(2,1)S(1)}, u32[]{:S(2)}, u32[]{:S(2)}) collective-permute-start(bf16[224,128]{1,0:T(8,128)(2,1)S(1)} %get-tuple-element.100), channel_id=1, source_target_pairs={{0,5},{1,4},{2,7},{3,6},{4,1},{5,0},{6,3},{7,2},{8,13},{9,12},{10,... | collective-permute-start | bytes 172040 | tf_op jit(solution)/shard_map/ppermute | solution.py:501
  17.0 3.1 %collective-permute-start.8 = (bf16[3,192,256]{2,1,0:T(8,128)(2,1)S(1)}, bf16[3,192,256]{2,1,0:T(8,128)(2,1)S(1)}, u32[]{:S(2)}, u32[]{:S(2)}) collective-permute-start(bf16[3,192,256]{2,1,0:T(8,128)(2,1)S(1)} %get-tuple-element.95), channel_id=1, source_target_pairs={{0,1},{1,0},{2,3},{3,2},{4,5},{5,4},{6,7},{7,6},{8,9},{9,8},{10,11... | collective-permute-start | bytes 884744 | tf_op jit(solution)/shard_map/ppermute | solution.py:497
  18.5 6.8 %collective-permute-start.9 = (bf16[192,128]{1,0:T(8,128)(2,1)S(1)}, bf16[192,128]{1,0:T(8,128)(2,1)S(1)}, u32[]{:S(2)}, u32[]{:S(2)}) collective-permute-start(bf16[192,128]{1,0:T(8,128)(2,1)S(1)} %get-tuple-element.96), channel_id=1, source_target_pairs={{0,4},{1,5},{2,6},{3,7},{4,0},{5,1},{6,2},{7,3},{8,12},{9,13},{10,... | collective-permute-start | bytes 147464 | tf_op jit(solution)/shard_map/ppermute | solution.py:501
  19.9 5.4 %collective-permute-start.10 = (bf16[192,128]{1,0:T(8,128)(2,1)S(1)}, bf16[192,128]{1,0:T(8,128)(2,1)S(1)}, u32[]{:S(2)}, u32[]{:S(2)}) collective-permute-start(bf16[192,128]{1,0:T(8,128)(2,1)S(1)} %get-tuple-element.97), channel_id=1, source_target_pairs={{0,5},{1,4},{2,7},{3,6},{4,1},{5,0},{6,3},{7,2},{8,13},{9,12},{10,... | collective-permute-start | bytes 147464 | tf_op jit(solution)/shard_map/ppermute | solution.py:501
  21.6 7.4 %collective-permute-start.14 = (bf16[32,1408]{1,0:T(8,128)(2,1)S(1)}, bf16[32,1408]{1,0:T(8,128)(2,1)S(1)}, u32[]{:S(2)}, u32[]{:S(2)}) collective-permute-start(bf16[32,1408]{1,0:T(8,128)(2,1)S(1)} %get-tuple-element.106), channel_id=1, source_target_pairs={{0,24},{4,28},{8,16},{12,20},{16,8},{20,12},{24,0},{28,4},{1,25},{... | collective-permute-start | bytes 270344 | tf_op jit(solution)/shard_map/ppermute | solution.py:617
  25.3 5.9 %collective-permute-start.13 = (bf16[32,1408]{1,0:T(8,128)(2,1)S(1)}, bf16[32,1408]{1,0:T(8,128)(2,1)S(1)}, u32[]{:S(2)}, u32[]{:S(2)}) collective-permute-start(bf16[32,1408]{1,0:T(8,128)(2,1)S(1)} %get-tuple-element.101), channel_id=1, source_target_pairs={{0,8},{4,12},{8,0},{12,4},{16,24},{20,28},{24,16},{28,20},{1,9},{5... | collective-permute-start | bytes 270344 | tf_op jit(solution)/shard_map/ppermute | solution.py:617
  25.8 7.1 %collective-permute-start.15 = (bf16[32,1280]{1,0:T(8,128)(2,1)S(1)}, bf16[32,1280]{1,0:T(8,128)(2,1)S(1)}, u32[]{:S(2)}, u32[]{:S(2)}) collective-permute-start(bf16[32,1280]{1,0:T(8,128)(2,1)S(1)} %get-tuple-element.115), channel_id=1, source_target_pairs={{0,16},{4,20},{8,24},{12,28},{16,0},{20,4},{24,8},{28,12},{1,17},{... | collective-permute-start | bytes 245768 | tf_op jit(solution)/shard_map/ppermute | solution.py:617

commit v23 on v22

--- a/solution.py
+++ b/solution.py
@@ -439,19 +439,19 @@
     sine, cosine = sin_cos(phase)
     amp = amp_ref[...]
     real, imag = (amp * cosine).astype(jnp.bfloat16), (amp * sine).astype(jnp.bfloat16)
-    cuts = [slice(t * LANES, (t + 1) * LANES) for t in range(tiles)]
-    field = stack(*[beside(real[:, cut], imag[:, cut]) for cut in cuts])
-    half = dot(field, columns[...]).astype(jnp.bfloat16)
-    wide = 2 * LANES
-    out_rows = 2 * rows
-    for t in range(tiles):
-        mine = half[t * rows : (t + 1) * rows]
-        full = dot(lines[...], stack(mine[:, :wide], mine[:, wide:]))
-        real, imag = full[:out_rows], full[out_rows:]
-        out[:, t * wide : (t + 1) * wide] = real * real + imag * imag
-        if t % 2:
-            cut = slice((t - 1) * wide, (t + 1) * wide)
-            copies += fetch((out.at[:, cut], spots.at[:, cut], sems.at[1 + t // 2]))
+    lined = dot(lines[...], stack(real, imag)).astype(jnp.bfloat16)
+    out_rows, wide, group = 2 * rows, 2 * LANES, tiles // 2
+    for part in range(2):
+        cuts = [slice(t * LANES, (t + 1) * LANES) for t in range(part * group, (part + 1) * group)]
+        field = stack(*[beside(lined[:out_rows, cut], lined[out_rows:, cut]) for cut in cuts])
+        full = dot(field, columns[...])
+        for k in range(group):
+            mine = full[k * out_rows : (k + 1) * out_rows]
+            real, imag = mine[:, :wide], mine[:, wide:]
+            at = (part * group + k) * wide
+            out[:, at : at + wide] = real * real + imag * imag
+        cut = slice(part * group * wide, (part + 1) * group * wide)
+        copies += fetch((out.at[:, cut], spots.at[:, cut], sems.at[1 + part]))
     for copy in copies:
         copy.wait()
 
@@ -648,7 +648,7 @@
         400_000_000,
         "imaging",
         out_hbm=(0, 1),
-        scratch=[pltpu.VMEM(spots_shape.shape, f32), sem((1 + pupil_cols // (2 * LANES),))],
+        scratch=[pltpu.VMEM(spots_shape.shape, f32), sem((3,))],
     )
     return (new_screens, spots[None])
 

time: 34.4 us -> 34.5 us (level)
  no operation moved by 1% of the time
where the time goes in v23:
time: 34.5 us; the launch traced here: 34.3 us
  starting transfers between devices  15.7 us (46%)
  Pallas kernels  12.1 us (35%)
  waiting for transfers between devices  5.68 us (16%)
  between operations  0.76 us (2%)
    pallas_call x12, Pallas kernels, call(): pl.pallas_call(kernel, out_shape=out_shape, in_specs=in_specs, out_specs=...  12.1 us
    ppermute x7, starting transfers between devices, swap(): return lax.ppermute(value, 'dir', [(i, i ^ bits) for i in range(n_dir)])  5.95 us
    ppermute x6, starting transfers between devices, partner(): lax.ppermute(value, ('layer', 'dir'), [(i, i ^ n_dir ^ bits) for i in ran...  4.96 us
    ppermute x3, starting transfers between devices, per_device(): lax.ppermute(received[k], 'layer', [(i, i ^ 2 * k) for i in range(n_layer)])  4.82 us
    ppermute x3, waiting for transfers between devices, per_device(): lax.ppermute(received[k], 'layer', [(i, i ^ 2 * k) for i in range(n_layer)])  4.2 us
    ppermute x6, waiting for transfers between devices, partner(): lax.ppermute(value, ('layer', 'dir'), [(i, i ^ n_dir ^ bits) for i in ran...  0.88 us
  transfers between devices with their start and end apart: 16, of which 6 were waited for; matrix products, arithmetic and copies ran while one was open for 0% of the time, Pallas kernels for 28%

profile of v23, /device:TPU:0, one launch (start us, length us, event | category | flops | bytes accessed | tf_op | source)
XLA Modules:
  0.0 34.3 jit_solution(18060940847846752738)
XLA Ops:
  0.6 1.1 %split.1 = (bf16[3,128,128]{2,1,0:T(8,128)(2,1)S(1)}, bf16[3,128,128]{2,1,0:T(8,128)(2,1)S(1)}, bf16[3,128,128]{2,1,0:T(8,128)(2,1)S(1)}, bf16[3,128,128]{2,1,0:...) custom-call(bf16[3,128,512]{2,1,0:T(8,128)(2,1)} %refs_0_.1, ...), custom_call_target="tpu_custom_call" | custom-call | tf_op jit(solution)/shard_map/split/pallas_call | solution.py:42
  1.8 2.4 %collective-permute-start.1 = (bf16[3,128,128]{2,1,0:T(8,128)(2,1)S(1)}, bf16[3,128,128]{2,1,0:T(8,128)(2,1)S(1)}, u32[]{:S(2)}, u32[]{:S(2)}) collective-permute-start(bf16[3,128,128]{2,1,0:T(8,128)(2,1)S(1)} %get-tuple-element.65), channel_id=1, source_target_pairs={{0,3},{1,2},{2,1},{3,0},{4,7},{5,6},{6,5},{7,4},{8,11},{9,10},{10,... | collective-permute-start | bytes 294920 | tf_op jit(solution)/shard_map/ppermute | solution.py:497
  4.2 0.6 %collective-permute-start = (bf16[3,128,128]{2,1,0:T(8,128)(2,1)S(1)}, bf16[3,128,128]{2,1,0:T(8,128)(2,1)S(1)}, u32[]{:S(2)}, u32[]{:S(2)}) collective-permute-start(bf16[3,128,128]{2,1,0:T(8,128)(2,1)S(1)} %get-tuple-element.64.keep.refs_7_), channel_id=1, source_target_pairs={{0,2},{1,3},{2,0},{3,1},{4,6},{5,7},{6,4},{7,5},{8,10},{9,11},{10,... | collective-permute-start | bytes 294920 | tf_op jit(solution)/shard_map/ppermute | solution.py:497
  4.8 0.0 collective-permute-start.2
  4.9 0.5 %collective-permute-start.5 = (bf16[3,128,128]{2,1,0:T(8,128)(2,1)S(1)}, bf16[3,128,128]{2,1,0:T(8,128)(2,1)S(1)}, u32[]{:S(2)}, u32[]{:S(2)}) collective-permute-start(bf16[3,128,128]{2,1,0:T(8,128)(2,1)S(1)} %get-tuple-element.84), channel_id=1, source_target_pairs={{0,1},{1,0},{2,3},{3,2},{4,5},{5,4},{6,7},{7,6},{8,9},{9,8},{10,11... | collective-permute-start | bytes 294920 | tf_op jit(solution)/shard_map/ppermute | solution.py:497
  5.4 1.4 %collective-permute-start.4 = (bf16[3,128,128]{2,1,0:T(8,128)(2,1)S(1)}, bf16[3,128,128]{2,1,0:T(8,128)(2,1)S(1)}, u32[]{:S(2)}, u32[]{:S(2)}) collective-permute-start(bf16[3,128,128]{2,1,0:T(8,128)(2,1)S(1)} %get-tuple-element.84), channel_id=1, source_target_pairs={{0,3},{1,2},{2,1},{3,0},{4,7},{5,6},{6,5},{7,4},{8,11},{9,10},{10,... | collective-permute-start | bytes 294920 | tf_op jit(solution)/shard_map/ppermute | solution.py:497
  6.8 3.2 %weights.1 = (bf16[2,3,256,512]{3,2,1,0:T(8,128)(2,1)S(1)}, bf16[3,512,1280]{2,1,0:T(8,128)(2,1)S(1)}, s32[8,1280]{1,0:T(8,128)S(1)}, s32[8,1280]{1,0:T(8,128)S(...) custom-call(s32[2,3]{1,0:T(2,128)S(1)} %get-tuple-element.74.wind_he, ...), custom_call_target="tpu_custom_call" | custom-call | tf_op jit(solution)/shard_map/weights/pallas_call | solution.py:42
  10.0 0.3 collective-permute-start.3
  10.3 0.0 collective-permute-done.across.refs_4_
  10.3 0.6 %rows_first.1 = (bf16[3,128,128]{2,1,0:T(8,128)(2,1)S(1)}, bf16[3,128,128]{2,1,0:T(8,128)(2,1)S(1)}, bf16[3,128,128]{2,1,0:T(8,128)(2,1)S(1)}, bf16[3,128,128]{2,1,0:T(8,128)(2,1)S(1)}) custom-call(bf16[2,3,256,512]{3,2,1,0:T(8,128)(2,1)S(1)} %get-tuple-element.70.rows_ref, bf16[3,128,128]{2,1,0:T(8,128)(2,1)S(1)} %collective-permute-done.across.refs_4_, ...), custom_call_target="tpu_custom_call" | custom-call | tf_op jit(solution)/shard_map/rows_first/pallas_call | solution.py:42
  10.9 1.8 %collective-permute-start.6 = (bf16[3,128,128]{2,1,0:T(8,128)(2,1)S(1)}, bf16[3,128,128]{2,1,0:T(8,128)(2,1)S(1)}, u32[]{:S(2)}, u32[]{:S(2)}) collective-permute-start(bf16[3,128,128]{2,1,0:T(8,128)(2,1)S(1)} %get-tuple-element.92), channel_id=1, source_target_pairs={{0,4},{1,5},{2,6},{3,7},{4,0},{5,1},{6,2},{7,3},{8,12},{9,13},{10,... | collective-permute-start | bytes 294920 | tf_op jit(solution)/shard_map/ppermute | solution.py:501
  12.7 1.5 %strips.1 = (bf16[3,512,1280]{2,1,0:T(8,128)(2,1)S(1)}, bf16[32,128]{1,0:T(8,128)(2,1)S(1)}, bf16[32,128]{1,0:T(8,128)(2,1)S(1)}) custom-call(s32[2,3]{1,0:T(2,128)S(1)} %get-tuple-element.74.wind_held, s32[8,1280]{1,0:T(8,128)S(1)} %get-tuple-element.75.refs_0_, s32[8,1280]{1,0:T(8,128)S(1)} %get-tuple-element.76.refs_1_, ...), custom_call_target="tpu_custom_call" | custom-call | tf_op jit(solution)/shard_map/strips/pallas_call | solution.py:42
  14.2 0.6 %collective-permute-done.3.refs_0_ = bf16[3,128,128]{2,1,0:T(8,128)(2,1)S(1)} collective-permute-done((bf16[3,128,128]{2,1,0:T(8,128)(2,1)S(1)}, bf16[3,128,128]{2,1,0:T(8,128)(2,1)S(1)}, u32[]{:S(2)}, u32[]{:S(2)}) %collective-permute-start.3) | collective-permute-done | bytes 98336 | tf_op jit(solution)/shard_map/ppermute | solution.py:497
  14.8 0.6 %rows_later.1 = (bf16[3,128,128]{2,1,0:T(8,128)(2,1)S(1)}, bf16[3,192,256]{2,1,0:T(8,128)(2,1)S(1)}, bf16[224,128]{1,0:T(8,128)(2,1)S(1)}, bf16[224,128]{1,0:T(8...) custom-call(bf16[2,3,256,512]{3,2,1,0:T(8,128)(2,1)S(1)} %get-tuple-element.70.rows_ref, ...), custom_call_target="tpu_custom_call" | custom-call | tf_op jit(solution)/shard_map/rows_later/pallas_call | solution.py:42
  15.4 1.6 %collective-permute-start.11 = (bf16[224,128]{1,0:T(8,128)(2,1)S(1)}, bf16[224,128]{1,0:T(8,128)(2,1)S(1)}, u32[]{:S(2)}, u32[]{:S(2)}) collective-permute-start(bf16[224,128]{1,0:T(8,128)(2,1)S(1)} %get-tuple-element.99), channel_id=1, source_target_pairs={{0,4},{1,5},{2,6},{3,7},{4,0},{5,1},{6,2},{7,3},{8,12},{9,13},{10,... | collective-permute-start | bytes 172040 | tf_op jit(solution)/shard_map/ppermute | solution.py:501
  17.0 0.6 %collective-permute-start.8 = (bf16[3,192,256]{2,1,0:T(8,128)(2,1)S(1)}, bf16[3,192,256]{2,1,0:T(8,128)(2,1)S(1)}, u32[]{:S(2)}, u32[]{:S(2)}) collective-permute-start(bf16[3,192,256]{2,1,0:T(8,128)(2,1)S(1)} %get-tuple-element.95), channel_id=1, source_target_pairs={{0,1},{1,0},{2,3},{3,2},{4,5},{5,4},{6,7},{7,6},{8,9},{9,8},{10,11... | collective-permute-start | bytes 884744 | tf_op jit(solution)/shard_map/ppermute | solution.py:497
  17.6 0.2 collective-permute-done.7.sibling_came
  17.8 0.7 %phase.1 = f32[128,1280]{1,0:T(8,128)S(1)} custom-call(bf16[3,512,1280]{2,1,0:T(8,128)(2,1)S(1)} %get-tuple-element.80.mine_ref, bf16[3,512,1280]{2,1,0:T(8,128)(2,1)S(1)} %get-tuple-element.79.other_ref.cols_ref, bf16[3,128,128]{2,1,0:T(8,128)(2,1)S(1)} %get-tuple-element.90.mine0, bf16[3,128,128]{2,1,0:T(8,128)(2,1)S(1)} %get-tuple-element.91.mine1, ...), custom_call_target="tpu_custom_call" | custom-call | flops 10000000000 | bytes 8912896 | tf_op jit(solution)/shard_map/phase/pallas_call | solution.py:42
  18.5 1.4 %collective-permute-start.9 = (bf16[192,128]{1,0:T(8,128)(2,1)S(1)}, bf16[192,128]{1,0:T(8,128)(2,1)S(1)}, u32[]{:S(2)}, u32[]{:S(2)}) collective-permute-start(bf16[192,128]{1,0:T(8,128)(2,1)S(1)} %get-tuple-element.96), channel_id=1, source_target_pairs={{0,4},{1,5},{2,6},{3,7},{4,0},{5,1},{6,2},{7,3},{8,12},{9,13},{10,... | collective-permute-start | bytes 147464 | tf_op jit(solution)/shard_map/ppermute | solution.py:501
  19.9 0.2 collective-permute-start.10
  20.0 0.4 %taken.1.phase = f32[128,1280]{1,0:T(8,128)S(1)} custom-call(bf16[3,512,1280]{2,1,0:T(8,128)(2,1)S(1)} %get-tuple-element.80.mine_ref, f32[128,1280]{1,0:T(8,128)S(1)} %phase.1, bf16[3,192,256]{2,1,0:T(8,128)(2,1)S(1)} %collective-permute-done.8.taken), custom_call_target="tpu_custom_call" | custom-call | tf_op jit(solution)/shard_map/taken/pallas_call | solution.py:42
  20.5 0.7 %collective-permute-done.12.sibling_came = bf16[224,128]{1,0:T(8,128)(2,1)S(1)} collective-permute-done((bf16[224,128]{1,0:T(8,128)(2,1)S(1)}, bf16[224,128]{1,0:T(8,128)(2,1)S(1)}, u32[]{:S(2)}, u32[]{:S(2)}) %collective-permute-start.12) | collective-permute-done | bytes 57376 | tf_op jit(solution)/shard_map/ppermute | solution.py:501
  21.1 0.5 %far.1 = (bf16[32,1408]{1,0:T(8,128)(2,1)S(1)}, bf16[32,1408]{1,0:T(8,128)(2,1)S(1)}, bf16[64,128]{1,0:T(8,128)(2,1)S(1)}) custom-call(bf16[3,512,1280]{2,1,0:T(8,128)(2,1)S(1)} %get-tuple-element.79.other_ref.cols_ref, f32[128,1280]{1,0:T(8,128)S(1)} %taken.1.phase, bf16[224,128]{1,0:T(8,128)(2,1)S(1)} %collective-permute-done.11.came, ...), custom_call_target="tpu_custom_call" | custom-call | flops 300000000 | bytes 4898816 | tf_op jit(solution)/shard_map/far/pallas_call | solution.py:42
  21.6 3.7 %collective-permute-start.14 = (bf16[32,1408]{1,0:T(8,128)(2,1)S(1)}, bf16[32,1408]{1,0:T(8,128)(2,1)S(1)}, u32[]{:S(2)}, u32[]{:S(2)}) collective-permute-start(bf16[32,1408]{1,0:T(8,128)(2,1)S(1)} %get-tuple-element.106), channel_id=1, source_target_pairs={{0,24},{4,28},{8,16},{12,20},{16,8},{20,12},{24,0},{28,4},{1,25},{... | collective-permute-start | bytes 270344 | tf_op jit(solution)/shard_map/ppermute | solution.py:617
  25.3 0.5 %rest.1 = (bf16[32,1280]{1,0:T(8,128)(2,1)S(1)}, bf16[32,1280]{1,0:T(8,128)(2,1)S(1)}) custom-call(bf16[3,512,1280]{2,1,0:T(8,128)(2,1)S(1)} %get-tuple-element.79.other_ref.cols_ref, f32[128,1280]{1,0:T(8,128)S(1)} %taken.1.phase, bf16[192,128]{1,0:T(8,128)(2,1)S(1)} %collective-permute-done.9.came, bf16[192,128]{1,0:T(8,128)(2,1)S(1)} %collective-permute-done.10.sibling_came), custom_call_target="tpu_custom_call" | custom-call | tf_op jit(solution)/shard_map/rest/pallas_call | solution.py:42
  25.8 1.2 %collective-permute-start.15 = (bf16[32,1280]{1,0:T(8,128)(2,1)S(1)}, bf16[32,1280]{1,0:T(8,128)(2,1)S(1)}, u32[]{:S(2)}, u32[]{:S(2)}) collective-permute-start(bf16[32,1280]{1,0:T(8,128)(2,1)S(1)} %get-tuple-element.115), channel_id=1, source_target_pairs={{0,16},{4,20},{8,24},{12,28},{16,0},{20,4},{24,8},{28,12},{1,17},{... | collective-permute-start | bytes 245768 | tf_op jit(solution)/shard_map/ppermute | solution.py:617
  26.9 2.1 %collective-permute-done.14.refs_1_.refs_3_ = bf16[32,1408]{1,0:T(8,128)(2,1)S(1)} collective-permute-done((bf16[32,1408]{1,0:T(8,128)(2,1)S(1)}, bf16[32,1408]{1,0:T(8,128)(2,1)S(1)}, u32[]{:S(2)}, u32[]{:S(2)}) %collective-permute-start.14) | collective-permute-done | bytes 90144 | tf_op jit(solution)/shard_map/ppermute | solution.py:617
  29.0 0.6 %optics.1 = (f32[32,1280]{1,0:T(8,128)S(1)}, bf16[256,512]{1,0:T(8,128)(2,1)S(1)}, bf16[128,64]{1,0:T(8,128)(2,1)S(1)}) custom-call(f32[32,1280]{1,0:T(8,128)S(1)} %get-tuple-element.107.amplitude, f32[128,128]{1,0:T(8,128)S(1)} %get-tuple-element.108.ones, f32[256,512]{1,0:T(8,128)S(1)} %get-tuple-element.109.columns, f32[128,64]{1,0:T(8,128)S(1)} %get-tuple-element.110.lines), custom_call_target="tpu_custom_call" | custom-call | tf_op jit(solution)/shard_map/optics/pallas_call | solution.py:42
  29.6 1.6 %collective-permute-done.13.refs_0_.refs_1_ = bf16[32,1408]{1,0:T(8,128)(2,1)S(1)} collective-permute-done((bf16[32,1408]{1,0:T(8,128)(2,1)S(1)}, bf16[32,1408]{1,0:T(8,128)(2,1)S(1)}, u32[]{:S(2)}, u32[]{:S(2)}) %collective-permute-start.13) | collective-permute-done | bytes 90144 | tf_op jit(solution)/shard_map/ppermute | solution.py:617
  31.2 1.1 %shift.1.refs_7_ = bf16[3,128,512]{2,1,0:T(8,128)(2,1)S(1)} custom-call(s32[2,3]{1,0:T(2,128)S(1)} %get-tuple-element.74.wind_held, bf16[3,128,512]{2,1,0:T(8,128)(2,1)S(1)} %get-tuple-element.120.own, bf16[3,128,128]{2,1,0:T(8,128)(2,1)S(1)} %collective-permute-done.2.near.refs_6_.near0, bf16[3,128,128]{2,1,0:T(8,128)(2,1)S(1)} %collective-permute-done.5.refs_2_.near1, ...), custom_call_target="tpu_custom_call" | custom-call | tf_op jit(solution)/shard_map/shift/pallas_call | solution.py:42
  32.4 0.5 %collective-permute-done.15.refs_2_ = bf16[32,1280]{1,0:T(8,128)(2,1)S(1)} collective-permute-done((bf16[32,1280]{1,0:T(8,128)(2,1)S(1)}, bf16[32,1280]{1,0:T(8,128)(2,1)S(1)}, u32[]{:S(2)}, u32[]{:S(2)}) %collective-permute-start.15) | collective-permute-done | bytes 81952 | tf_op jit(solution)/shard_map/ppermute | solution.py:617
  32.9 1.4 %imaging.1 = (f32[64,2560]{1,0:T(8,128)}, bf16[3,128,512]{2,1,0:T(8,128)(2,1)}) custom-call(bf16[32,1280]{1,0:T(8,128)(2,1)S(1)} %get-tuple-element.98.refs_0_, bf16[32,1408]{1,0:T(8,128)(2,1)S(1)} %collective-permute-done.13.refs_0_.refs_1_, bf16[32,1280]{1,0:T(8,128)(2,1)S(1)} %collective-permute-done.15.refs_2_, ...), custom_call_target="tpu_custom_call" | custom-call | flops 400000000 | bytes 2228224 | tf_op jit(solution)/shard_map/imaging/pallas_call | solution.py:42
  (12 shorter events, 0.0 us)
Async XLA Ops:
  1.8 8.2 %collective-permute-start.1 = (bf16[3,128,128]{2,1,0:T(8,128)(2,1)S(1)}, bf16[3,128,128]{2,1,0:T(8,128)(2,1)S(1)}, u32[]{:S(2)}, u32[]{:S(2)}) collective-permute-start(bf16[3,128,128]{2,1,0:T(8,128)(2,1)S(1)} %get-tuple-element.65), channel_id=1, source_target_pairs={{0,3},{1,2},{2,1},{3,0},{4,7},{5,6},{6,5},{7,4},{8,11},{9,10},{10,... | collective-permute-start | bytes 294920 | tf_op jit(solution)/shard_map/ppermute | solution.py:497
  4.2 6.1 %collective-permute-start = (bf16[3,128,128]{2,1,0:T(8,128)(2,1)S(1)}, bf16[3,128,128]{2,1,0:T(8,128)(2,1)S(1)}, u32[]{:S(2)}, u32[]{:S(2)}) collective-permute-start(bf16[3,128,128]{2,1,0:T(8,128)(2,1)S(1)} %get-tuple-element.64.keep.refs_7_), channel_id=1, source_target_pairs={{0,2},{1,3},{2,0},{3,1},{4,6},{5,7},{6,4},{7,5},{8,10},{9,11},{10,... | collective-permute-start | bytes 294920 | tf_op jit(solution)/shard_map/ppermute | solution.py:497
  4.8 5.4 %collective-permute-start.2 = (bf16[3,128,128]{2,1,0:T(8,128)(2,1)S(1)}, bf16[3,128,128]{2,1,0:T(8,128)(2,1)S(1)}, u32[]{:S(2)}, u32[]{:S(2)}) collective-permute-start(bf16[3,128,128]{2,1,0:T(8,128)(2,1)S(1)} %get-tuple-element.65), channel_id=1, source_target_pairs={{0,1},{1,0},{2,3},{3,2},{4,5},{5,4},{6,7},{7,6},{8,9},{9,8},{10,11... | collective-permute-start | bytes 294920 | tf_op jit(solution)/shard_map/ppermute | solution.py:497
  4.9 9.3 %collective-permute-start.5 = (bf16[3,128,128]{2,1,0:T(8,128)(2,1)S(1)}, bf16[3,128,128]{2,1,0:T(8,128)(2,1)S(1)}, u32[]{:S(2)}, u32[]{:S(2)}) collective-permute-start(bf16[3,128,128]{2,1,0:T(8,128)(2,1)S(1)} %get-tuple-element.84), channel_id=1, source_target_pairs={{0,1},{1,0},{2,3},{3,2},{4,5},{5,4},{6,7},{7,6},{8,9},{9,8},{10,11... | collective-permute-start | bytes 294920 | tf_op jit(solution)/shard_map/ppermute | solution.py:497
  5.4 8.8 %collective-permute-start.4 = (bf16[3,128,128]{2,1,0:T(8,128)(2,1)S(1)}, bf16[3,128,128]{2,1,0:T(8,128)(2,1)S(1)}, u32[]{:S(2)}, u32[]{:S(2)}) collective-permute-start(bf16[3,128,128]{2,1,0:T(8,128)(2,1)S(1)} %get-tuple-element.84), channel_id=1, source_target_pairs={{0,3},{1,2},{2,1},{3,0},{4,7},{5,6},{6,5},{7,4},{8,11},{9,10},{10,... | collective-permute-start | bytes 294920 | tf_op jit(solution)/shard_map/ppermute | solution.py:497
  10.0 4.8 %collective-permute-start.3 = (bf16[3,128,128]{2,1,0:T(8,128)(2,1)S(1)}, bf16[3,128,128]{2,1,0:T(8,128)(2,1)S(1)}, u32[]{:S(2)}, u32[]{:S(2)}) collective-permute-start(bf16[3,128,128]{2,1,0:T(8,128)(2,1)S(1)} %get-tuple-element.83.refs_3_), channel_id=1, source_target_pairs={{0,2},{1,3},{2,0},{3,1},{4,6},{5,7},{6,4},{7,5},{8,10},{9,11},{10,... | collective-permute-start | bytes 294920 | tf_op jit(solution)/shard_map/ppermute | solution.py:497
  10.9 6.7 %collective-permute-start.6 = (bf16[3,128,128]{2,1,0:T(8,128)(2,1)S(1)}, bf16[3,128,128]{2,1,0:T(8,128)(2,1)S(1)}, u32[]{:S(2)}, u32[]{:S(2)}) collective-permute-start(bf16[3,128,128]{2,1,0:T(8,128)(2,1)S(1)} %get-tuple-element.92), channel_id=1, source_target_pairs={{0,4},{1,5},{2,6},{3,7},{4,0},{5,1},{6,2},{7,3},{8,12},{9,13},{10,... | collective-permute-start | bytes 294920 | tf_op jit(solution)/shard_map/ppermute | solution.py:501
  12.7 5.1 %collective-permute-start.7 = (bf16[3,128,128]{2,1,0:T(8,128)(2,1)S(1)}, bf16[3,128,128]{2,1,0:T(8,128)(2,1)S(1)}, u32[]{:S(2)}, u32[]{:S(2)}) collective-permute-start(bf16[3,128,128]{2,1,0:T(8,128)(2,1)S(1)} %get-tuple-element.93), channel_id=1, source_target_pairs={{0,5},{1,4},{2,7},{3,6},{4,1},{5,0},{6,3},{7,2},{8,13},{9,12},{10,... | collective-permute-start | bytes 294920 | tf_op jit(solution)/shard_map/ppermute | solution.py:501
  15.4 5.1 %collective-permute-start.11 = (bf16[224,128]{1,0:T(8,128)(2,1)S(1)}, bf16[224,128]{1,0:T(8,128)(2,1)S(1)}, u32[]{:S(2)}, u32[]{:S(2)}) collective-permute-start(bf16[224,128]{1,0:T(8,128)(2,1)S(1)} %get-tuple-element.99), channel_id=1, source_target_pairs={{0,4},{1,5},{2,6},{3,7},{4,0},{5,1},{6,2},{7,3},{8,12},{9,13},{10,... | collective-permute-start | bytes 172040 | tf_op jit(solution)/shard_map/ppermute | solution.py:501
  17.0 4.2 %collective-permute-start.12 = (bf16[224,128]{1,0:T(8,128)(2,1)S(1)}, bf16[224,128]{1,0:T(8,128)(2,1)S(1)}, u32[]{:S(2)}, u32[]{:S(2)}) collective-permute-start(bf16[224,128]{1,0:T(8,128)(2,1)S(1)} %get-tuple-element.100), channel_id=1, source_target_pairs={{0,5},{1,4},{2,7},{3,6},{4,1},{5,0},{6,3},{7,2},{8,13},{9,12},{10,... | collective-permute-start | bytes 172040 | tf_op jit(solution)/shard_map/ppermute | solution.py:501
  17.0 3.1 %collective-permute-start.8 = (bf16[3,192,256]{2,1,0:T(8,128)(2,1)S(1)}, bf16[3,192,256]{2,1,0:T(8,128)(2,1)S(1)}, u32[]{:S(2)}, u32[]{:S(2)}) collective-permute-start(bf16[3,192,256]{2,1,0:T(8,128)(2,1)S(1)} %get-tuple-element.95), channel_id=1, source_target_pairs={{0,1},{1,0},{2,3},{3,2},{4,5},{5,4},{6,7},{7,6},{8,9},{9,8},{10,11... | collective-permute-start | bytes 884744 | tf_op jit(solution)/shard_map/ppermute | solution.py:497
  18.5 6.8 %collective-permute-start.9 = (bf16[192,128]{1,0:T(8,128)(2,1)S(1)}, bf16[192,128]{1,0:T(8,128)(2,1)S(1)}, u32[]{:S(2)}, u32[]{:S(2)}) collective-permute-start(bf16[192,128]{1,0:T(8,128)(2,1)S(1)} %get-tuple-element.96), channel_id=1, source_target_pairs={{0,4},{1,5},{2,6},{3,7},{4,0},{5,1},{6,2},{7,3},{8,12},{9,13},{10,... | collective-permute-start | bytes 147464 | tf_op jit(solution)/shard_map/ppermute | solution.py:501
  19.9 5.4 %collective-permute-start.10 = (bf16[192,128]{1,0:T(8,128)(2,1)S(1)}, bf16[192,128]{1,0:T(8,128)(2,1)S(1)}, u32[]{:S(2)}, u32[]{:S(2)}) collective-permute-start(bf16[192,128]{1,0:T(8,128)(2,1)S(1)} %get-tuple-element.97), channel_id=1, source_target_pairs={{0,5},{1,4},{2,7},{3,6},{4,1},{5,0},{6,3},{7,2},{8,13},{9,12},{10,... | collective-permute-start | bytes 147464 | tf_op jit(solution)/shard_map/ppermute | solution.py:501
  21.6 7.4 %collective-permute-start.14 = (bf16[32,1408]{1,0:T(8,128)(2,1)S(1)}, bf16[32,1408]{1,0:T(8,128)(2,1)S(1)}, u32[]{:S(2)}, u32[]{:S(2)}) collective-permute-start(bf16[32,1408]{1,0:T(8,128)(2,1)S(1)} %get-tuple-element.106), channel_id=1, source_target_pairs={{0,24},{4,28},{8,16},{12,20},{16,8},{20,12},{24,0},{28,4},{1,25},{... | collective-permute-start | bytes 270344 | tf_op jit(solution)/shard_map/ppermute | solution.py:617
  25.3 5.9 %collective-permute-start.13 = (bf16[32,1408]{1,0:T(8,128)(2,1)S(1)}, bf16[32,1408]{1,0:T(8,128)(2,1)S(1)}, u32[]{:S(2)}, u32[]{:S(2)}) collective-permute-start(bf16[32,1408]{1,0:T(8,128)(2,1)S(1)} %get-tuple-element.101), channel_id=1, source_target_pairs={{0,8},{4,12},{8,0},{12,4},{16,24},{20,28},{24,16},{28,20},{1,9},{5... | collective-permute-start | bytes 270344 | tf_op jit(solution)/shard_map/ppermute | solution.py:617
  25.8 7.1 %collective-permute-start.15 = (bf16[32,1280]{1,0:T(8,128)(2,1)S(1)}, bf16[32,1280]{1,0:T(8,128)(2,1)S(1)}, u32[]{:S(2)}, u32[]{:S(2)}) collective-permute-start(bf16[32,1280]{1,0:T(8,128)(2,1)S(1)} %get-tuple-element.115), channel_id=1, source_target_pairs={{0,16},{4,20},{8,24},{12,28},{16,0},{20,4},{24,8},{28,12},{1,17},{... | collective-permute-start | bytes 245768 | tf_op jit(solution)/shard_map/ppermute | solution.py:617

commit v24 on v18

--- a/solution.py
+++ b/solution.py
@@ -345,12 +345,15 @@
     strips[:STRIP] = jnp.where(odd, here, there).astype(jnp.bfloat16)
     strips[STRIP:] = jnp.where(odd, there, here).astype(jnp.bfloat16)
     pairs = half // outs[0].shape[0]
-    for out, step in zip(outs, strip_steps(pairs)):
-        add_strip(pairs, step, strips, out)
-
-
-def rest_kernel(cols_ref, phase, came, sibling_came, *outs):
+    add_strip(pairs, strip_steps(pairs)[-1], strips, outs[0])
+
+
+def rest_kernel(cols_ref, phase, came, sibling_came, strips, *outs):
     sum_up(0, cols_ref, phase, came, sibling_came, outs)
+    pairs = len(outs) + 1
+    for out, step in zip(outs, send_order(pairs)):
+        if step in strip_steps(pairs):
+            add_strip(pairs, step, strips, out)
 
 
 def shifted_rows(shift, odd, own, near, far):
@@ -566,7 +569,7 @@
         brief=True,
     )
     steps = strip_steps(pairs)
-    far = len(steps) * rows
+    far = rows
     message = shape(layers * far + STRIP * rows_dev // LANES, width)
     remainder = shape(layers * (half - far), width)
     mine1, give, far1, sibling_far1, rest1, sibling_rest1 = call(
@@ -578,6 +581,7 @@
         brief=True,
     )
     far1, sibling_far1 = partner(far1), partner(sibling_far1, 1)
+    rest1, sibling_rest1 = partner(rest1), partner(sibling_rest1, 1)
     taken = swap(give, 1)
     phase = call(
         phase_kernel,
@@ -587,8 +591,6 @@
         "phase",
     )
 
-    rest1, sibling_rest1, phase = lax.optimization_barrier((rest1, sibling_rest1, phase))
-    rest1, sibling_rest1 = partner(rest1), partner(sibling_rest1, 1)
     phase = call(
         taken_kernel,
         shape(half, pupil_cols, dtype=f32),
@@ -599,15 +601,15 @@
     )
     *far_sums, strips = call(
         far_kernel,
-        [shape(rows, pupil_cols + rows_dev)] * len(steps) + [shape(2 * STRIP, rows_dev)],
+        [shape(rows, pupil_cols + rows_dev), shape(2 * STRIP, rows_dev)],
         (others, phase, far1, sibling_far1),
         300_000_000,
         "far",
     )
     rest_sums = call(
         rest_kernel,
-        [shape(rows, pupil_cols)] * (pairs - len(steps)),
-        (others, phase, rest1, sibling_rest1),
+        [shape(rows, pupil_cols + (rows_dev if k in steps else 0)) for k in send_order(pairs)[:-1]],
+        (others, phase, rest1, sibling_rest1, strips),
         0,
         "rest",
         brief=True,

time: 34.2 us -> 34.3 us (level)
  starting transfers between devices: 15.7 us -> 18 us
  waiting for transfers between devices: 5.52 us -> 3.27 us
    ppermute x3, starting transfers between devices: 4.76 us -> 6.65 us  [per_device(): lax.ppermute(received[k], 'layer', [(i, i ^ 2 * k) for i in range(n_layer)])]
    ppermute x3, waiting for transfers between devices: 4.28 us -> 2.71 us  [per_device(): lax.ppermute(received[k], 'layer', [(i, i ^ 2 * k) for i in range(n_layer)])]
    ppermute x6, waiting for transfers between devices: 1.22 us -> 0.02 us  [partner(): lax.ppermute(value, ('layer', 'dir'), [(i, i ^ n_dir ^ bits) for i in ran...]
    ppermute x7, waiting for transfers between devices: 0.02 us -> 0.54 us  [swap(): return lax.ppermute(value, 'dir', [(i, i ^ bits) for i in range(n_dir)])]
  transfers between devices with their start and end apart: 16 -> 16, of which waited for: 5 -> 2; matrix products, arithmetic and copies ran while one was open for 0% -> 0% of each run, Pallas kernels for 28% -> 28%
where the time goes in v24:
time: 34.3 us; the launch traced here: 34.1 us
  starting transfers between devices  18 us (52%)
  Pallas kernels  12.1 us (35%)
  waiting for transfers between devices  3.27 us (10%)
  between operations  0.78 us (2%)
    pallas_call x12, Pallas kernels, call(): pl.pallas_call(kernel, out_shape=out_shape, in_specs=in_specs, out_specs=...  12.1 us
    ppermute x3, starting transfers between devices, per_device(): lax.ppermute(received[k], 'layer', [(i, i ^ 2 * k) for i in range(n_layer)])  6.65 us
    ppermute x7, starting transfers between devices, swap(): return lax.ppermute(value, 'dir', [(i, i ^ bits) for i in range(n_dir)])  5.73 us
    ppermute x6, starting transfers between devices, partner(): lax.ppermute(value, ('layer', 'dir'), [(i, i ^ n_dir ^ bits) for i in ran...  5.62 us
    ppermute x3, waiting for transfers between devices, per_device(): lax.ppermute(received[k], 'layer', [(i, i ^ 2 * k) for i in range(n_layer)])  2.71 us
  transfers between devices with their start and end apart: 16, of which 2 were waited for; matrix products, arithmetic and copies ran while one was open for 0% of the time, Pallas kernels for 28%

profile of v24, /device:TPU:0, one launch (start us, length us, event | category | flops | bytes accessed | tf_op | source)
XLA Modules:
  0.0 34.1 jit_solution(17197193698631641036)
XLA Ops:
  0.6 1.1 %split.1 = (bf16[3,128,128]{2,1,0:T(8,128)(2,1)S(1)}, bf16[3,128,128]{2,1,0:T(8,128)(2,1)S(1)}, bf16[3,128,128]{2,1,0:T(8,128)(2,1)S(1)}, bf16[3,128,128]{2,1,0:...) custom-call(bf16[3,128,512]{2,1,0:T(8,128)(2,1)} %refs_0_.1, ...), custom_call_target="tpu_custom_call" | custom-call | tf_op jit(solution)/shard_map/split/pallas_call | solution.py:42
  1.8 2.4 %collective-permute-start.1 = (bf16[3,128,128]{2,1,0:T(8,128)(2,1)S(1)}, bf16[3,128,128]{2,1,0:T(8,128)(2,1)S(1)}, u32[]{:S(2)}, u32[]{:S(2)}) collective-permute-start(bf16[3,128,128]{2,1,0:T(8,128)(2,1)S(1)} %get-tuple-element.62), channel_id=1, source_target_pairs={{0,3},{1,2},{2,1},{3,0},{4,7},{5,6},{6,5},{7,4},{8,11},{9,10},{10,... | collective-permute-start | bytes 294920 | tf_op jit(solution)/shard_map/ppermute | solution.py:500
  4.2 0.6 %collective-permute-start = (bf16[3,128,128]{2,1,0:T(8,128)(2,1)S(1)}, bf16[3,128,128]{2,1,0:T(8,128)(2,1)S(1)}, u32[]{:S(2)}, u32[]{:S(2)}) collective-permute-start(bf16[3,128,128]{2,1,0:T(8,128)(2,1)S(1)} %get-tuple-element.61.keep.refs_7_), channel_id=1, source_target_pairs={{0,2},{1,3},{2,0},{3,1},{4,6},{5,7},{6,4},{7,5},{8,10},{9,11},{10,... | collective-permute-start | bytes 294920 | tf_op jit(solution)/shard_map/ppermute | solution.py:500
  4.8 0.0 collective-permute-start.2
  4.9 1.7 %collective-permute-start.3 = (bf16[3,128,128]{2,1,0:T(8,128)(2,1)S(1)}, bf16[3,128,128]{2,1,0:T(8,128)(2,1)S(1)}, u32[]{:S(2)}, u32[]{:S(2)}) collective-permute-start(bf16[3,128,128]{2,1,0:T(8,128)(2,1)S(1)} %get-tuple-element.79.refs_3_), channel_id=1, source_target_pairs={{0,2},{1,3},{2,0},{3,1},{4,6},{5,7},{6,4},{7,5},{8,10},{9,11},{10,... | collective-permute-start | bytes 294920 | tf_op jit(solution)/shard_map/ppermute | solution.py:500
  6.6 0.1 collective-permute-start.4
  6.7 3.2 %weights.1 = (bf16[2,3,256,512]{3,2,1,0:T(8,128)(2,1)S(1)}, bf16[3,512,1280]{2,1,0:T(8,128)(2,1)S(1)}, s32[8,1280]{1,0:T(8,128)S(1)}, s32[8,1280]{1,0:T(8,128)S(...) custom-call(s32[2,3]{1,0:T(2,128)S(1)} %get-tuple-element.71.wind_he, ...), custom_call_target="tpu_custom_call" | custom-call | tf_op jit(solution)/shard_map/weights/pallas_call | solution.py:42
  9.9 0.4 %collective-permute-start.5 = (bf16[3,128,128]{2,1,0:T(8,128)(2,1)S(1)}, bf16[3,128,128]{2,1,0:T(8,128)(2,1)S(1)}, u32[]{:S(2)}, u32[]{:S(2)}) collective-permute-start(bf16[3,128,128]{2,1,0:T(8,128)(2,1)S(1)} %get-tuple-element.82), channel_id=1, source_target_pairs={{0,1},{1,0},{2,3},{3,2},{4,5},{5,4},{6,7},{7,6},{8,9},{9,8},{10,11... | collective-permute-start | bytes 294920 | tf_op jit(solution)/shard_map/ppermute | solution.py:500
  10.3 0.0 collective-permute-done.across.refs_4_
  10.3 0.0 collective-permute-done.2.near.refs_6_.near0
  10.3 0.6 %rows_first.1 = (bf16[3,128,128]{2,1,0:T(8,128)(2,1)S(1)}, bf16[3,128,128]{2,1,0:T(8,128)(2,1)S(1)}, bf16[3,128,128]{2,1,0:T(8,128)(2,1)S(1)}, bf16[3,128,128]{2,1,0:T(8,128)(2,1)S(1)}) custom-call(bf16[2,3,256,512]{3,2,1,0:T(8,128)(2,1)S(1)} %get-tuple-element.67.rows_ref, bf16[3,128,128]{2,1,0:T(8,128)(2,1)S(1)} %collective-permute-done.across.refs_4_, ...), custom_call_target="tpu_custom_call" | custom-call | tf_op jit(solution)/shard_map/rows_first/pallas_call | solution.py:42
  10.9 1.8 %collective-permute-start.6 = (bf16[3,128,128]{2,1,0:T(8,128)(2,1)S(1)}, bf16[3,128,128]{2,1,0:T(8,128)(2,1)S(1)}, u32[]{:S(2)}, u32[]{:S(2)}) collective-permute-start(bf16[3,128,128]{2,1,0:T(8,128)(2,1)S(1)} %get-tuple-element.87), channel_id=1, source_target_pairs={{0,4},{1,5},{2,6},{3,7},{4,0},{5,1},{6,2},{7,3},{8,12},{9,13},{10,... | collective-permute-start | bytes 294920 | tf_op jit(solution)/shard_map/ppermute | solution.py:504
  12.7 1.5 %strips.1 = (bf16[3,512,1280]{2,1,0:T(8,128)(2,1)S(1)}, bf16[32,128]{1,0:T(8,128)(2,1)S(1)}, bf16[32,128]{1,0:T(8,128)(2,1)S(1)}) custom-call(s32[2,3]{1,0:T(2,128)S(1)} %get-tuple-element.71.wind_held, s32[8,1280]{1,0:T(8,128)S(1)} %get-tuple-element.72.refs_0_, s32[8,1280]{1,0:T(8,128)S(1)} %get-tuple-element.73.refs_1_, ...), custom_call_target="tpu_custom_call" | custom-call | tf_op jit(solution)/shard_map/strips/pallas_call | solution.py:42
  14.2 0.0 collective-permute-done.3.refs_0_
  14.2 0.6 %rows_later.1 = (bf16[3,128,128]{2,1,0:T(8,128)(2,1)S(1)}, bf16[3,192,256]{2,1,0:T(8,128)(2,1)S(1)}, bf16[128,128]{1,0:T(8,128)(2,1)S(1)}, bf16[128,128]{1,0:T(8...) custom-call(bf16[2,3,256,512]{3,2,1,0:T(8,128)(2,1)S(1)} %get-tuple-element.67.rows_ref, ...), custom_call_target="tpu_custom_call" | custom-call | tf_op jit(solution)/shard_map/rows_later/pallas_call | solution.py:42
  14.8 2.0 %collective-permute-start.11 = (bf16[128,128]{1,0:T(8,128)(2,1)S(1)}, bf16[128,128]{1,0:T(8,128)(2,1)S(1)}, u32[]{:S(2)}, u32[]{:S(2)}) collective-permute-start(bf16[128,128]{1,0:T(8,128)(2,1)S(1)} %get-tuple-element.92), channel_id=1, source_target_pairs={{0,4},{1,5},{2,6},{3,7},{4,0},{5,1},{6,2},{7,3},{8,12},{9,13},{10,... | collective-permute-start | bytes 98312 | tf_op jit(solution)/shard_map/ppermute | solution.py:504
  16.8 0.0 collective-permute-start.12
  16.8 1.5 %collective-permute-start.9 = (bf16[288,128]{1,0:T(8,128)(2,1)S(1)}, bf16[288,128]{1,0:T(8,128)(2,1)S(1)}, u32[]{:S(2)}, u32[]{:S(2)}) collective-permute-start(bf16[288,128]{1,0:T(8,128)(2,1)S(1)} %get-tuple-element.90), channel_id=1, source_target_pairs={{0,4},{1,5},{2,6},{3,7},{4,0},{5,1},{6,2},{7,3},{8,12},{9,13},{10,... | collective-permute-start | bytes 221192 | tf_op jit(solution)/shard_map/ppermute | solution.py:504
  18.4 0.2 collective-permute-start.10
  18.6 0.4 %collective-permute-start.8 = (bf16[3,192,256]{2,1,0:T(8,128)(2,1)S(1)}, bf16[3,192,256]{2,1,0:T(8,128)(2,1)S(1)}, u32[]{:S(2)}, u32[]{:S(2)}) collective-permute-start(bf16[3,192,256]{2,1,0:T(8,128)(2,1)S(1)} %get-tuple-element.89), channel_id=1, source_target_pairs={{0,1},{1,0},{2,3},{3,2},{4,5},{5,4},{6,7},{7,6},{8,9},{9,8},{10,11... | collective-permute-start | bytes 884744 | tf_op jit(solution)/shard_map/ppermute | solution.py:500
  19.0 0.7 %phase.1 = f32[128,1280]{1,0:T(8,128)S(1)} custom-call(bf16[3,512,1280]{2,1,0:T(8,128)(2,1)S(1)} %get-tuple-element.77.mine_ref, bf16[3,512,1280]{2,1,0:T(8,128)(2,1)S(1)} %get-tuple-element.76.other_ref.cols_ref, bf16[3,128,128]{2,1,0:T(8,128)(2,1)S(1)} %get-tuple-element.78.mine0, bf16[3,128,128]{2,1,0:T(8,128)(2,1)S(1)} %get-tuple-element.86.mine1, ...), custom_call_target="tpu_custom_call" | custom-call | flops 10000000000 | bytes 8912896 | tf_op jit(solution)/shard_map/phase/pallas_call | solution.py:42
  19.7 0.5 %collective-permute-done.8.taken = bf16[3,192,256]{2,1,0:T(8,128)(2,1)S(1)} collective-permute-done((bf16[3,192,256]{2,1,0:T(8,128)(2,1)S(1)}, bf16[3,192,256]{2,1,0:T(8,128)(2,1)S(1)}, u32[]{:S(2)}, u32[]{:S(2)}) %collective-permute-start.8) | collective-permute-done | bytes 294944 | tf_op jit(solution)/shard_map/ppermute | solution.py:500
  20.2 0.4 %taken.1.phase = f32[128,1280]{1,0:T(8,128)S(1)} custom-call(bf16[3,512,1280]{2,1,0:T(8,128)(2,1)S(1)} %get-tuple-element.77.mine_ref, f32[128,1280]{1,0:T(8,128)S(1)} %phase.1, bf16[3,192,256]{2,1,0:T(8,128)(2,1)S(1)} %collective-permute-done.8.taken), custom_call_target="tpu_custom_call" | custom-call | tf_op jit(solution)/shard_map/taken/pallas_call | solution.py:42
  20.7 0.5 %far.1 = (bf16[32,1408]{1,0:T(8,128)(2,1)S(1)}, bf16[64,128]{1,0:T(8,128)(2,1)S(1)}) custom-call(bf16[3,512,1280]{2,1,0:T(8,128)(2,1)S(1)} %get-tuple-element.76.other_ref.cols_ref, f32[128,1280]{1,0:T(8,128)S(1)} %taken.1.phase, bf16[128,128]{1,0:T(8,128)(2,1)S(1)} %collective-permute-done.11.came, bf16[128,128]{1,0:T(8,128)(2,1)S(1)} %collective-permute-done.12.sibling_came), custom_call_target="tpu_custom_call" | custom-call | flops 300000000 | bytes 4759552 | tf_op jit(solution)/shard_map/far/pallas_call | solution.py:42
  21.1 3.8 %collective-permute-start.14 = (bf16[32,1408]{1,0:T(8,128)(2,1)S(1)}, bf16[32,1408]{1,0:T(8,128)(2,1)S(1)}, u32[]{:S(2)}, u32[]{:S(2)}) collective-permute-start(bf16[32,1408]{1,0:T(8,128)(2,1)S(1)} %get-tuple-element.101), channel_id=1, source_target_pairs={{0,24},{4,28},{8,16},{12,20},{16,8},{20,12},{24,0},{28,4},{1,25},{... | collective-permute-start | bytes 270344 | tf_op jit(solution)/shard_map/ppermute | solution.py:619
  24.9 0.5 %rest.1 = (bf16[32,1280]{1,0:T(8,128)(2,1)S(1)}, bf16[32,1280]{1,0:T(8,128)(2,1)S(1)}, bf16[32,1408]{1,0:T(8,128)(2,1)S(1)}) custom-call(bf16[3,512,1280]{2,1,0:T(8,128)(2,1)S(1)} %get-tuple-element.76.other_ref.cols_ref, f32[128,1280]{1,0:T(8,128)S(1)} %taken.1.phase, bf16[288,128]{1,0:T(8,128)(2,1)S(1)} %collective-permute-done.9.came, ...), custom_call_target="tpu_custom_call" | custom-call | tf_op jit(solution)/shard_map/rest/pallas_call | solution.py:42
  25.4 0.3 collective-permute-start.13
  25.7 2.6 %collective-permute-start.15 = (bf16[32,1280]{1,0:T(8,128)(2,1)S(1)}, bf16[32,1280]{1,0:T(8,128)(2,1)S(1)}, u32[]{:S(2)}, u32[]{:S(2)}) collective-permute-start(bf16[32,1280]{1,0:T(8,128)(2,1)S(1)} %get-tuple-element.110), channel_id=1, source_target_pairs={{0,16},{4,20},{8,24},{12,28},{16,0},{20,4},{24,8},{28,12},{1,17},{... | collective-permute-start | bytes 245768 | tf_op jit(solution)/shard_map/ppermute | solution.py:619
  28.3 0.6 %optics.1 = (f32[32,1280]{1,0:T(8,128)S(1)}, bf16[256,512]{1,0:T(8,128)(2,1)S(1)}, bf16[128,64]{1,0:T(8,128)(2,1)S(1)}) custom-call(f32[32,1280]{1,0:T(8,128)S(1)} %get-tuple-element.102.amplitude, f32[128,128]{1,0:T(8,128)S(1)} %get-tuple-element.103.ones, f32[256,512]{1,0:T(8,128)S(1)} %get-tuple-element.104.columns, f32[128,64]{1,0:T(8,128)S(1)} %get-tuple-element.105.lines), custom_call_target="tpu_custom_call" | custom-call | tf_op jit(solution)/shard_map/optics/pallas_call | solution.py:42
  28.9 2.7 %collective-permute-done.13.refs_0_.refs_1_ = bf16[32,1408]{1,0:T(8,128)(2,1)S(1)} collective-permute-done((bf16[32,1408]{1,0:T(8,128)(2,1)S(1)}, bf16[32,1408]{1,0:T(8,128)(2,1)S(1)}, u32[]{:S(2)}, u32[]{:S(2)}) %collective-permute-start.13) | collective-permute-done | bytes 90144 | tf_op jit(solution)/shard_map/ppermute | solution.py:619
  31.6 1.1 %shift.1.refs_7_ = bf16[3,128,512]{2,1,0:T(8,128)(2,1)S(1)} custom-call(s32[2,3]{1,0:T(2,128)S(1)} %get-tuple-element.71.wind_held, bf16[3,128,512]{2,1,0:T(8,128)(2,1)S(1)} %get-tuple-element.115.own, bf16[3,128,128]{2,1,0:T(8,128)(2,1)S(1)} %collective-permute-done.2.near.refs_6_.near0, bf16[3,128,128]{2,1,0:T(8,128)(2,1)S(1)} %collective-permute-done.5.refs_2_.near1, ...), custom_call_target="tpu_custom_call" | custom-call | tf_op jit(solution)/shard_map/shift/pallas_call | solution.py:42
  32.8 1.3 %imaging.1 = (f32[64,2560]{1,0:T(8,128)}, bf16[3,128,512]{2,1,0:T(8,128)(2,1)}) custom-call(bf16[32,1280]{1,0:T(8,128)(2,1)S(1)} %get-tuple-element.95.refs_0_, bf16[32,1408]{1,0:T(8,128)(2,1)S(1)} %collective-permute-done.13.refs_0_.refs_1_, bf16[32,1280]{1,0:T(8,128)(2,1)S(1)} %collective-permute-done.15.refs_2_, ...), custom_call_target="tpu_custom_call" | custom-call | flops 400000000 | bytes 2228224 | tf_op jit(solution)/shard_map/imaging/pallas_call | solution.py:42
  (12 shorter events, 0.0 us)
Async XLA Ops:
  1.8 8.1 %collective-permute-start.1 = (bf16[3,128,128]{2,1,0:T(8,128)(2,1)S(1)}, bf16[3,128,128]{2,1,0:T(8,128)(2,1)S(1)}, u32[]{:S(2)}, u32[]{:S(2)}) collective-permute-start(bf16[3,128,128]{2,1,0:T(8,128)(2,1)S(1)} %get-tuple-element.62), channel_id=1, source_target_pairs={{0,3},{1,2},{2,1},{3,0},{4,7},{5,6},{6,5},{7,4},{8,11},{9,10},{10,... | collective-permute-start | bytes 294920 | tf_op jit(solution)/shard_map/ppermute | solution.py:500
  4.2 6.1 %collective-permute-start = (bf16[3,128,128]{2,1,0:T(8,128)(2,1)S(1)}, bf16[3,128,128]{2,1,0:T(8,128)(2,1)S(1)}, u32[]{:S(2)}, u32[]{:S(2)}) collective-permute-start(bf16[3,128,128]{2,1,0:T(8,128)(2,1)S(1)} %get-tuple-element.61.keep.refs_7_), channel_id=1, source_target_pairs={{0,2},{1,3},{2,0},{3,1},{4,6},{5,7},{6,4},{7,5},{8,10},{9,11},{10,... | collective-permute-start | bytes 294920 | tf_op jit(solution)/shard_map/ppermute | solution.py:500
  4.8 5.4 %collective-permute-start.2 = (bf16[3,128,128]{2,1,0:T(8,128)(2,1)S(1)}, bf16[3,128,128]{2,1,0:T(8,128)(2,1)S(1)}, u32[]{:S(2)}, u32[]{:S(2)}) collective-permute-start(bf16[3,128,128]{2,1,0:T(8,128)(2,1)S(1)} %get-tuple-element.62), channel_id=1, source_target_pairs={{0,1},{1,0},{2,3},{3,2},{4,5},{5,4},{6,7},{7,6},{8,9},{9,8},{10,11... | collective-permute-start | bytes 294920 | tf_op jit(solution)/shard_map/ppermute | solution.py:500
  4.9 9.3 %collective-permute-start.3 = (bf16[3,128,128]{2,1,0:T(8,128)(2,1)S(1)}, bf16[3,128,128]{2,1,0:T(8,128)(2,1)S(1)}, u32[]{:S(2)}, u32[]{:S(2)}) collective-permute-start(bf16[3,128,128]{2,1,0:T(8,128)(2,1)S(1)} %get-tuple-element.79.refs_3_), channel_id=1, source_target_pairs={{0,2},{1,3},{2,0},{3,1},{4,6},{5,7},{6,4},{7,5},{8,10},{9,11},{10,... | collective-permute-start | bytes 294920 | tf_op jit(solution)/shard_map/ppermute | solution.py:500
  6.6 7.6 %collective-permute-start.4 = (bf16[3,128,128]{2,1,0:T(8,128)(2,1)S(1)}, bf16[3,128,128]{2,1,0:T(8,128)(2,1)S(1)}, u32[]{:S(2)}, u32[]{:S(2)}) collective-permute-start(bf16[3,128,128]{2,1,0:T(8,128)(2,1)S(1)} %get-tuple-element.82), channel_id=1, source_target_pairs={{0,3},{1,2},{2,1},{3,0},{4,7},{5,6},{6,5},{7,4},{8,11},{9,10},{10,... | collective-permute-start | bytes 294920 | tf_op jit(solution)/shard_map/ppermute | solution.py:500
  9.9 4.3 %collective-permute-start.5 = (bf16[3,128,128]{2,1,0:T(8,128)(2,1)S(1)}, bf16[3,128,128]{2,1,0:T(8,128)(2,1)S(1)}, u32[]{:S(2)}, u32[]{:S(2)}) collective-permute-start(bf16[3,128,128]{2,1,0:T(8,128)(2,1)S(1)} %get-tuple-element.82), channel_id=1, source_target_pairs={{0,1},{1,0},{2,3},{3,2},{4,5},{5,4},{6,7},{7,6},{8,9},{9,8},{10,11... | collective-permute-start | bytes 294920 | tf_op jit(solution)/shard_map/ppermute | solution.py:500
  10.9 7.5 %collective-permute-start.6 = (bf16[3,128,128]{2,1,0:T(8,128)(2,1)S(1)}, bf16[3,128,128]{2,1,0:T(8,128)(2,1)S(1)}, u32[]{:S(2)}, u32[]{:S(2)}) collective-permute-start(bf16[3,128,128]{2,1,0:T(8,128)(2,1)S(1)} %get-tuple-element.87), channel_id=1, source_target_pairs={{0,4},{1,5},{2,6},{3,7},{4,0},{5,1},{6,2},{7,3},{8,12},{9,13},{10,... | collective-permute-start | bytes 294920 | tf_op jit(solution)/shard_map/ppermute | solution.py:504
  12.7 5.9 %collective-permute-start.7 = (bf16[3,128,128]{2,1,0:T(8,128)(2,1)S(1)}, bf16[3,128,128]{2,1,0:T(8,128)(2,1)S(1)}, u32[]{:S(2)}, u32[]{:S(2)}) collective-permute-start(bf16[3,128,128]{2,1,0:T(8,128)(2,1)S(1)} %get-tuple-element.88), channel_id=1, source_target_pairs={{0,5},{1,4},{2,7},{3,6},{4,1},{5,0},{6,3},{7,2},{8,13},{9,12},{10,... | collective-permute-start | bytes 294920 | tf_op jit(solution)/shard_map/ppermute | solution.py:504
  14.8 5.8 %collective-permute-start.11 = (bf16[128,128]{1,0:T(8,128)(2,1)S(1)}, bf16[128,128]{1,0:T(8,128)(2,1)S(1)}, u32[]{:S(2)}, u32[]{:S(2)}) collective-permute-start(bf16[128,128]{1,0:T(8,128)(2,1)S(1)} %get-tuple-element.92), channel_id=1, source_target_pairs={{0,4},{1,5},{2,6},{3,7},{4,0},{5,1},{6,2},{7,3},{8,12},{9,13},{10,... | collective-permute-start | bytes 98312 | tf_op jit(solution)/shard_map/ppermute | solution.py:504
  16.8 3.8 %collective-permute-start.12 = (bf16[128,128]{1,0:T(8,128)(2,1)S(1)}, bf16[128,128]{1,0:T(8,128)(2,1)S(1)}, u32[]{:S(2)}, u32[]{:S(2)}) collective-permute-start(bf16[128,128]{1,0:T(8,128)(2,1)S(1)} %get-tuple-element.93), channel_id=1, source_target_pairs={{0,5},{1,4},{2,7},{3,6},{4,1},{5,0},{6,3},{7,2},{8,13},{9,12},{10,... | collective-permute-start | bytes 98312 | tf_op jit(solution)/shard_map/ppermute | solution.py:504
  16.8 8.1 %collective-permute-start.9 = (bf16[288,128]{1,0:T(8,128)(2,1)S(1)}, bf16[288,128]{1,0:T(8,128)(2,1)S(1)}, u32[]{:S(2)}, u32[]{:S(2)}) collective-permute-start(bf16[288,128]{1,0:T(8,128)(2,1)S(1)} %get-tuple-element.90), channel_id=1, source_target_pairs={{0,4},{1,5},{2,6},{3,7},{4,0},{5,1},{6,2},{7,3},{8,12},{9,13},{10,... | collective-permute-start | bytes 221192 | tf_op jit(solution)/shard_map/ppermute | solution.py:504
  18.4 6.6 %collective-permute-start.10 = (bf16[288,128]{1,0:T(8,128)(2,1)S(1)}, bf16[288,128]{1,0:T(8,128)(2,1)S(1)}, u32[]{:S(2)}, u32[]{:S(2)}) collective-permute-start(bf16[288,128]{1,0:T(8,128)(2,1)S(1)} %get-tuple-element.91), channel_id=1, source_target_pairs={{0,5},{1,4},{2,7},{3,6},{4,1},{5,0},{6,3},{7,2},{8,13},{9,12},{10,... | collective-permute-start | bytes 221192 | tf_op jit(solution)/shard_map/ppermute | solution.py:504
  18.6 1.6 %collective-permute-start.8 = (bf16[3,192,256]{2,1,0:T(8,128)(2,1)S(1)}, bf16[3,192,256]{2,1,0:T(8,128)(2,1)S(1)}, u32[]{:S(2)}, u32[]{:S(2)}) collective-permute-start(bf16[3,192,256]{2,1,0:T(8,128)(2,1)S(1)} %get-tuple-element.89), channel_id=1, source_target_pairs={{0,1},{1,0},{2,3},{3,2},{4,5},{5,4},{6,7},{7,6},{8,9},{9,8},{10,11... | collective-permute-start | bytes 884744 | tf_op jit(solution)/shard_map/ppermute | solution.py:500
  21.1 7.1 %collective-permute-start.14 = (bf16[32,1408]{1,0:T(8,128)(2,1)S(1)}, bf16[32,1408]{1,0:T(8,128)(2,1)S(1)}, u32[]{:S(2)}, u32[]{:S(2)}) collective-permute-start(bf16[32,1408]{1,0:T(8,128)(2,1)S(1)} %get-tuple-element.101), channel_id=1, source_target_pairs={{0,24},{4,28},{8,16},{12,20},{16,8},{20,12},{24,0},{28,4},{1,25},{... | collective-permute-start | bytes 270344 | tf_op jit(solution)/shard_map/ppermute | solution.py:619
  25.4 6.2 %collective-permute-start.13 = (bf16[32,1408]{1,0:T(8,128)(2,1)S(1)}, bf16[32,1408]{1,0:T(8,128)(2,1)S(1)}, u32[]{:S(2)}, u32[]{:S(2)}) collective-permute-start(bf16[32,1408]{1,0:T(8,128)(2,1)S(1)} %get-tuple-element.96), channel_id=1, source_target_pairs={{0,8},{4,12},{8,0},{12,4},{16,24},{20,28},{24,16},{28,20},{1,9},{5... | collective-permute-start | bytes 270344 | tf_op jit(solution)/shard_map/ppermute | solution.py:619
  25.7 7.1 %collective-permute-start.15 = (bf16[32,1280]{1,0:T(8,128)(2,1)S(1)}, bf16[32,1280]{1,0:T(8,128)(2,1)S(1)}, u32[]{:S(2)}, u32[]{:S(2)}) collective-permute-start(bf16[32,1280]{1,0:T(8,128)(2,1)S(1)} %get-tuple-element.110), channel_id=1, source_target_pairs={{0,16},{4,20},{8,24},{12,28},{16,0},{20,4},{24,8},{28,12},{1,17},{... | collective-permute-start | bytes 245768 | tf_op jit(solution)/shard_map/ppermute | solution.py:619

commit v25 on v24

--- a/solution.py
+++ b/solution.py
@@ -581,6 +581,7 @@
         brief=True,
     )
     far1, sibling_far1 = partner(far1), partner(sibling_far1, 1)
+    rest1, sibling_rest1, sibling_came0 = lax.optimization_barrier((rest1, sibling_rest1, sibling_came0))
     rest1, sibling_rest1 = partner(rest1), partner(sibling_rest1, 1)
     taken = swap(give, 1)
     phase = call(

time: 34.3 us -> 34.4 us (level)
  starting transfers between devices: 18 us -> 18.5 us
  waiting for transfers between devices: 3.27 us -> 2.88 us
    ppermute x6, starting transfers between devices: 5.62 us -> 6.18 us  [partner(): lax.ppermute(value, ('layer', 'dir'), [(i, i ^ n_dir ^ bits) for i in ran...]
    ppermute x7, waiting for transfers between devices: 0.54 us -> 0.02 us  [swap(): return lax.ppermute(value, 'dir', [(i, i ^ bits) for i in range(n_dir)])]
  transfers between devices with their start and end apart: 16 -> 16, of which waited for: 2 -> 3; matrix products, arithmetic and copies ran while one was open for 0% -> 0% of each run, Pallas kernels for 28% -> 28%
where the time goes in v25:
time: 34.4 us; the launch traced here: 34.2 us
  starting transfers between devices  18.5 us (54%)
  Pallas kernels  12.1 us (35%)
  waiting for transfers between devices  2.88 us (8%)
  between operations  0.78 us (2%)
    pallas_call x12, Pallas kernels, call(): pl.pallas_call(kernel, out_shape=out_shape, in_specs=in_specs, out_specs=...  12.1 us
    ppermute x3, starting transfers between devices, per_device(): lax.ppermute(received[k], 'layer', [(i, i ^ 2 * k) for i in range(n_layer)])  6.72 us
    ppermute x6, starting transfers between devices, partner(): lax.ppermute(value, ('layer', 'dir'), [(i, i ^ n_dir ^ bits) for i in ran...  6.18 us
    ppermute x7, starting transfers between devices, swap(): return lax.ppermute(value, 'dir', [(i, i ^ bits) for i in range(n_dir)])  5.6 us
    ppermute x3, waiting for transfers between devices, per_device(): lax.ppermute(received[k], 'layer', [(i, i ^ 2 * k) for i in range(n_layer)])  2.85 us
  transfers between devices with their start and end apart: 16, of which 3 were waited for; matrix products, arithmetic and copies ran while one was open for 0% of the time, Pallas kernels for 28%

profile of v25, /device:TPU:0, one launch (start us, length us, event | category | flops | bytes accessed | tf_op | source)
XLA Modules:
  0.0 34.2 jit_solution(12600202902388123552)
XLA Ops:
  0.6 1.1 %split.1 = (bf16[3,128,128]{2,1,0:T(8,128)(2,1)S(1)}, bf16[3,128,128]{2,1,0:T(8,128)(2,1)S(1)}, bf16[3,128,128]{2,1,0:T(8,128)(2,1)S(1)}, bf16[3,128,128]{2,1,0:...) custom-call(bf16[3,128,512]{2,1,0:T(8,128)(2,1)} %refs_0_.1, ...), custom_call_target="tpu_custom_call" | custom-call | tf_op jit(solution)/shard_map/split/pallas_call | solution.py:42
  1.8 2.4 %collective-permute-start.1 = (bf16[3,128,128]{2,1,0:T(8,128)(2,1)S(1)}, bf16[3,128,128]{2,1,0:T(8,128)(2,1)S(1)}, u32[]{:S(2)}, u32[]{:S(2)}) collective-permute-start(bf16[3,128,128]{2,1,0:T(8,128)(2,1)S(1)} %get-tuple-element.65), channel_id=1, source_target_pairs={{0,3},{1,2},{2,1},{3,0},{4,7},{5,6},{6,5},{7,4},{8,11},{9,10},{10,... | collective-permute-start | bytes 294920 | tf_op jit(solution)/shard_map/ppermute | solution.py:500
  4.2 0.6 %collective-permute-start = (bf16[3,128,128]{2,1,0:T(8,128)(2,1)S(1)}, bf16[3,128,128]{2,1,0:T(8,128)(2,1)S(1)}, u32[]{:S(2)}, u32[]{:S(2)}) collective-permute-start(bf16[3,128,128]{2,1,0:T(8,128)(2,1)S(1)} %get-tuple-element.64.keep.refs_7_), channel_id=1, source_target_pairs={{0,2},{1,3},{2,0},{3,1},{4,6},{5,7},{6,4},{7,5},{8,10},{9,11},{10,... | collective-permute-start | bytes 294920 | tf_op jit(solution)/shard_map/ppermute | solution.py:500
  4.8 0.0 collective-permute-start.2
  4.9 1.7 %collective-permute-start.3 = (bf16[3,128,128]{2,1,0:T(8,128)(2,1)S(1)}, bf16[3,128,128]{2,1,0:T(8,128)(2,1)S(1)}, u32[]{:S(2)}, u32[]{:S(2)}) collective-permute-start(bf16[3,128,128]{2,1,0:T(8,128)(2,1)S(1)} %get-tuple-element.82.refs_3_), channel_id=1, source_target_pairs={{0,2},{1,3},{2,0},{3,1},{4,6},{5,7},{6,4},{7,5},{8,10},{9,11},{10,... | collective-permute-start | bytes 294920 | tf_op jit(solution)/shard_map/ppermute | solution.py:500
  6.6 0.1 collective-permute-start.4
  6.7 3.2 %weights.1 = (bf16[2,3,256,512]{3,2,1,0:T(8,128)(2,1)S(1)}, bf16[3,512,1280]{2,1,0:T(8,128)(2,1)S(1)}, s32[8,1280]{1,0:T(8,128)S(1)}, s32[8,1280]{1,0:T(8,128)S(...) custom-call(s32[2,3]{1,0:T(2,128)S(1)} %get-tuple-element.74.wind_he, ...), custom_call_target="tpu_custom_call" | custom-call | tf_op jit(solution)/shard_map/weights/pallas_call | solution.py:42
  9.9 0.0 collective-permute-done.1.diagonal.refs_5_.diagonal0
  9.9 0.4 %collective-permute-start.5 = (bf16[3,128,128]{2,1,0:T(8,128)(2,1)S(1)}, bf16[3,128,128]{2,1,0:T(8,128)(2,1)S(1)}, u32[]{:S(2)}, u32[]{:S(2)}) collective-permute-start(bf16[3,128,128]{2,1,0:T(8,128)(2,1)S(1)} %get-tuple-element.85), channel_id=1, source_target_pairs={{0,1},{1,0},{2,3},{3,2},{4,5},{5,4},{6,7},{7,6},{8,9},{9,8},{10,11... | collective-permute-start | bytes 294920 | tf_op jit(solution)/shard_map/ppermute | solution.py:500
  10.3 0.0 collective-permute-done.across.refs_4_
  10.3 0.6 %rows_first.1 = (bf16[3,128,128]{2,1,0:T(8,128)(2,1)S(1)}, bf16[3,128,128]{2,1,0:T(8,128)(2,1)S(1)}, bf16[3,128,128]{2,1,0:T(8,128)(2,1)S(1)}, bf16[3,128,128]{2,1,0:T(8,128)(2,1)S(1)}) custom-call(bf16[2,3,256,512]{3,2,1,0:T(8,128)(2,1)S(1)} %get-tuple-element.70.rows_ref, bf16[3,128,128]{2,1,0:T(8,128)(2,1)S(1)} %collective-permute-done.across.refs_4_, ...), custom_call_target="tpu_custom_call" | custom-call | tf_op jit(solution)/shard_map/rows_first/pallas_call | solution.py:42
  10.9 1.5 %collective-permute-start.7 = (bf16[3,128,128]{2,1,0:T(8,128)(2,1)S(1)}, bf16[3,128,128]{2,1,0:T(8,128)(2,1)S(1)}, u32[]{:S(2)}, u32[]{:S(2)}) collective-permute-start(bf16[3,128,128]{2,1,0:T(8,128)(2,1)S(1)} %get-tuple-element.93), channel_id=1, source_target_pairs={{0,5},{1,4},{2,7},{3,6},{4,1},{5,0},{6,3},{7,2},{8,13},{9,12},{10,... | collective-permute-start | bytes 294920 | tf_op jit(solution)/shard_map/ppermute | solution.py:504
  12.3 0.4 %collective-permute-start.6 = (bf16[3,128,128]{2,1,0:T(8,128)(2,1)S(1)}, bf16[3,128,128]{2,1,0:T(8,128)(2,1)S(1)}, u32[]{:S(2)}, u32[]{:S(2)}) collective-permute-start(bf16[3,128,128]{2,1,0:T(8,128)(2,1)S(1)} %get-tuple-element.90), channel_id=1, source_target_pairs={{0,4},{1,5},{2,6},{3,7},{4,0},{5,1},{6,2},{7,3},{8,12},{9,13},{10,... | collective-permute-start | bytes 294920 | tf_op jit(solution)/shard_map/ppermute | solution.py:504
  12.8 1.5 %strips.1 = (bf16[3,512,1280]{2,1,0:T(8,128)(2,1)S(1)}, bf16[32,128]{1,0:T(8,128)(2,1)S(1)}, bf16[32,128]{1,0:T(8,128)(2,1)S(1)}) custom-call(s32[2,3]{1,0:T(2,128)S(1)} %get-tuple-element.74.wind_held, s32[8,1280]{1,0:T(8,128)S(1)} %get-tuple-element.75.refs_0_, s32[8,1280]{1,0:T(8,128)S(1)} %get-tuple-element.76.refs_1_, ...), custom_call_target="tpu_custom_call" | custom-call | tf_op jit(solution)/shard_map/strips/pallas_call | solution.py:42
  14.3 0.6 %rows_later.1 = (bf16[3,128,128]{2,1,0:T(8,128)(2,1)S(1)}, bf16[3,192,256]{2,1,0:T(8,128)(2,1)S(1)}, bf16[128,128]{1,0:T(8,128)(2,1)S(1)}, bf16[128,128]{1,0:T(8...) custom-call(bf16[2,3,256,512]{3,2,1,0:T(8,128)(2,1)S(1)} %get-tuple-element.70.rows_ref, ...), custom_call_target="tpu_custom_call" | custom-call | tf_op jit(solution)/shard_map/rows_later/pallas_call | solution.py:42
  14.9 1.9 %collective-permute-start.11 = (bf16[128,128]{1,0:T(8,128)(2,1)S(1)}, bf16[128,128]{1,0:T(8,128)(2,1)S(1)}, u32[]{:S(2)}, u32[]{:S(2)}) collective-permute-start(bf16[128,128]{1,0:T(8,128)(2,1)S(1)} %get-tuple-element.98), channel_id=1, source_target_pairs={{0,4},{1,5},{2,6},{3,7},{4,0},{5,1},{6,2},{7,3},{8,12},{9,13},{10,... | collective-permute-start | bytes 98312 | tf_op jit(solution)/shard_map/ppermute | solution.py:504
  16.8 0.3 collective-permute-start.8
  17.1 1.9 %collective-permute-start.9 = (bf16[288,128]{1,0:T(8,128)(2,1)S(1)}, bf16[288,128]{1,0:T(8,128)(2,1)S(1)}, u32[]{:S(2)}, u32[]{:S(2)}) collective-permute-start(bf16[288,128]{1,0:T(8,128)(2,1)S(1)} %get-tuple-element.96), channel_id=1, source_target_pairs={{0,4},{1,5},{2,6},{3,7},{4,0},{5,1},{6,2},{7,3},{8,12},{9,13},{10,... | collective-permute-start | bytes 221192 | tf_op jit(solution)/shard_map/ppermute | solution.py:504
  19.0 0.5 %collective-permute-start.10 = (bf16[288,128]{1,0:T(8,128)(2,1)S(1)}, bf16[288,128]{1,0:T(8,128)(2,1)S(1)}, u32[]{:S(2)}, u32[]{:S(2)}) collective-permute-start(bf16[288,128]{1,0:T(8,128)(2,1)S(1)} %get-tuple-element.97), channel_id=1, source_target_pairs={{0,5},{1,4},{2,7},{3,6},{4,1},{5,0},{6,3},{7,2},{8,13},{9,12},{10,... | collective-permute-start | bytes 221192 | tf_op jit(solution)/shard_map/ppermute | solution.py:504
  19.4 0.7 %phase.1 = f32[128,1280]{1,0:T(8,128)S(1)} custom-call(bf16[3,512,1280]{2,1,0:T(8,128)(2,1)S(1)} %get-tuple-element.80.mine_ref, bf16[3,512,1280]{2,1,0:T(8,128)(2,1)S(1)} %get-tuple-element.79.other_ref.cols_ref, bf16[3,128,128]{2,1,0:T(8,128)(2,1)S(1)} %get-tuple-element.81.mine0, bf16[3,128,128]{2,1,0:T(8,128)(2,1)S(1)} %get-tuple-element.89.mine1, ...), custom_call_target="tpu_custom_call" | custom-call | flops 10000000000 | bytes 8912896 | tf_op jit(solution)/shard_map/phase/pallas_call | solution.py:42
  20.1 0.4 %taken.1.phase = f32[128,1280]{1,0:T(8,128)S(1)} custom-call(bf16[3,512,1280]{2,1,0:T(8,128)(2,1)S(1)} %get-tuple-element.80.mine_ref, f32[128,1280]{1,0:T(8,128)S(1)} %phase.1, bf16[3,192,256]{2,1,0:T(8,128)(2,1)S(1)} %collective-permute-done.8.taken), custom_call_target="tpu_custom_call" | custom-call | tf_op jit(solution)/shard_map/taken/pallas_call | solution.py:42
  20.6 0.5 %far.1 = (bf16[32,1408]{1,0:T(8,128)(2,1)S(1)}, bf16[64,128]{1,0:T(8,128)(2,1)S(1)}) custom-call(bf16[3,512,1280]{2,1,0:T(8,128)(2,1)S(1)} %get-tuple-element.79.other_ref.cols_ref, f32[128,1280]{1,0:T(8,128)S(1)} %taken.1.phase, bf16[128,128]{1,0:T(8,128)(2,1)S(1)} %collective-permute-done.11.came, bf16[128,128]{1,0:T(8,128)(2,1)S(1)} %collective-permute-done.12.sibling_came), custom_call_target="tpu_custom_call" | custom-call | flops 300000000 | bytes 4759552 | tf_op jit(solution)/shard_map/far/pallas_call | solution.py:42
  21.1 3.6 %collective-permute-start.14 = (bf16[32,1408]{1,0:T(8,128)(2,1)S(1)}, bf16[32,1408]{1,0:T(8,128)(2,1)S(1)}, u32[]{:S(2)}, u32[]{:S(2)}) collective-permute-start(bf16[32,1408]{1,0:T(8,128)(2,1)S(1)} %get-tuple-element.107), channel_id=1, source_target_pairs={{0,24},{4,28},{8,16},{12,20},{16,8},{20,12},{24,0},{28,4},{1,25},{... | collective-permute-start | bytes 270344 | tf_op jit(solution)/shard_map/ppermute | solution.py:620
  24.7 0.5 %rest.1 = (bf16[32,1280]{1,0:T(8,128)(2,1)S(1)}, bf16[32,1280]{1,0:T(8,128)(2,1)S(1)}, bf16[32,1408]{1,0:T(8,128)(2,1)S(1)}) custom-call(bf16[3,512,1280]{2,1,0:T(8,128)(2,1)S(1)} %get-tuple-element.79.other_ref.cols_ref, f32[128,1280]{1,0:T(8,128)S(1)} %taken.1.phase, bf16[288,128]{1,0:T(8,128)(2,1)S(1)} %collective-permute-done.9.came, ...), custom_call_target="tpu_custom_call" | custom-call | tf_op jit(solution)/shard_map/rest/pallas_call | solution.py:42
  25.2 0.5 %collective-permute-start.13 = (bf16[32,1408]{1,0:T(8,128)(2,1)S(1)}, bf16[32,1408]{1,0:T(8,128)(2,1)S(1)}, u32[]{:S(2)}, u32[]{:S(2)}) collective-permute-start(bf16[32,1408]{1,0:T(8,128)(2,1)S(1)} %get-tuple-element.102), channel_id=1, source_target_pairs={{0,8},{4,12},{8,0},{12,4},{16,24},{20,28},{24,16},{28,20},{1,9},{5... | collective-permute-start | bytes 270344 | tf_op jit(solution)/shard_map/ppermute | solution.py:620
  25.7 2.6 %collective-permute-start.15 = (bf16[32,1280]{1,0:T(8,128)(2,1)S(1)}, bf16[32,1280]{1,0:T(8,128)(2,1)S(1)}, u32[]{:S(2)}, u32[]{:S(2)}) collective-permute-start(bf16[32,1280]{1,0:T(8,128)(2,1)S(1)} %get-tuple-element.116), channel_id=1, source_target_pairs={{0,16},{4,20},{8,24},{12,28},{16,0},{20,4},{24,8},{28,12},{1,17},{... | collective-permute-start | bytes 245768 | tf_op jit(solution)/shard_map/ppermute | solution.py:620
  28.3 0.1 collective-permute-done.14.refs_1_.refs_3_
  28.4 0.6 %optics.1 = (f32[32,1280]{1,0:T(8,128)S(1)}, bf16[256,512]{1,0:T(8,128)(2,1)S(1)}, bf16[128,64]{1,0:T(8,128)(2,1)S(1)}) custom-call(f32[32,1280]{1,0:T(8,128)S(1)} %get-tuple-element.108.amplitude, f32[128,128]{1,0:T(8,128)S(1)} %get-tuple-element.109.ones, f32[256,512]{1,0:T(8,128)S(1)} %get-tuple-element.110.columns, f32[128,64]{1,0:T(8,128)S(1)} %get-tuple-element.111.lines), custom_call_target="tpu_custom_call" | custom-call | tf_op jit(solution)/shard_map/optics/pallas_call | solution.py:42
  29.0 2.7 %collective-permute-done.13.refs_0_.refs_1_ = bf16[32,1408]{1,0:T(8,128)(2,1)S(1)} collective-permute-done((bf16[32,1408]{1,0:T(8,128)(2,1)S(1)}, bf16[32,1408]{1,0:T(8,128)(2,1)S(1)}, u32[]{:S(2)}, u32[]{:S(2)}) %collective-permute-start.13) | collective-permute-done | bytes 90144 | tf_op jit(solution)/shard_map/ppermute | solution.py:620
  31.7 1.1 %shift.1.refs_7_ = bf16[3,128,512]{2,1,0:T(8,128)(2,1)S(1)} custom-call(s32[2,3]{1,0:T(2,128)S(1)} %get-tuple-element.74.wind_held, bf16[3,128,512]{2,1,0:T(8,128)(2,1)S(1)} %get-tuple-element.121.own, bf16[3,128,128]{2,1,0:T(8,128)(2,1)S(1)} %collective-permute-done.2.near.refs_6_.near0, bf16[3,128,128]{2,1,0:T(8,128)(2,1)S(1)} %collective-permute-done.5.refs_2_.near1, ...), custom_call_target="tpu_custom_call" | custom-call | tf_op jit(solution)/shard_map/shift/pallas_call | solution.py:42
  32.8 0.1 collective-permute-done.15.refs_2_
  32.9 1.3 %imaging.1 = (f32[64,2560]{1,0:T(8,128)}, bf16[3,128,512]{2,1,0:T(8,128)(2,1)}) custom-call(bf16[32,1280]{1,0:T(8,128)(2,1)S(1)} %get-tuple-element.101.refs_0_, bf16[32,1408]{1,0:T(8,128)(2,1)S(1)} %collective-permute-done.13.refs_0_.refs_1_, bf16[32,1280]{1,0:T(8,128)(2,1)S(1)} %collective-permute-done.15.refs_2_, ...), custom_call_target="tpu_custom_call" | custom-call | flops 400000000 | bytes 2228224 | tf_op jit(solution)/shard_map/imaging/pallas_call | solution.py:42
  (12 shorter events, 0.0 us)
Async XLA Ops:
  1.8 8.1 %collective-permute-start.1 = (bf16[3,128,128]{2,1,0:T(8,128)(2,1)S(1)}, bf16[3,128,128]{2,1,0:T(8,128)(2,1)S(1)}, u32[]{:S(2)}, u32[]{:S(2)}) collective-permute-start(bf16[3,128,128]{2,1,0:T(8,128)(2,1)S(1)} %get-tuple-element.65), channel_id=1, source_target_pairs={{0,3},{1,2},{2,1},{3,0},{4,7},{5,6},{6,5},{7,4},{8,11},{9,10},{10,... | collective-permute-start | bytes 294920 | tf_op jit(solution)/shard_map/ppermute | solution.py:500
  4.2 6.1 %collective-permute-start = (bf16[3,128,128]{2,1,0:T(8,128)(2,1)S(1)}, bf16[3,128,128]{2,1,0:T(8,128)(2,1)S(1)}, u32[]{:S(2)}, u32[]{:S(2)}) collective-permute-start(bf16[3,128,128]{2,1,0:T(8,128)(2,1)S(1)} %get-tuple-element.64.keep.refs_7_), channel_id=1, source_target_pairs={{0,2},{1,3},{2,0},{3,1},{4,6},{5,7},{6,4},{7,5},{8,10},{9,11},{10,... | collective-permute-start | bytes 294920 | tf_op jit(solution)/shard_map/ppermute | solution.py:500
  4.8 5.4 %collective-permute-start.2 = (bf16[3,128,128]{2,1,0:T(8,128)(2,1)S(1)}, bf16[3,128,128]{2,1,0:T(8,128)(2,1)S(1)}, u32[]{:S(2)}, u32[]{:S(2)}) collective-permute-start(bf16[3,128,128]{2,1,0:T(8,128)(2,1)S(1)} %get-tuple-element.65), channel_id=1, source_target_pairs={{0,1},{1,0},{2,3},{3,2},{4,5},{5,4},{6,7},{7,6},{8,9},{9,8},{10,11... | collective-permute-start | bytes 294920 | tf_op jit(solution)/shard_map/ppermute | solution.py:500
  4.9 9.4 %collective-permute-start.3 = (bf16[3,128,128]{2,1,0:T(8,128)(2,1)S(1)}, bf16[3,128,128]{2,1,0:T(8,128)(2,1)S(1)}, u32[]{:S(2)}, u32[]{:S(2)}) collective-permute-start(bf16[3,128,128]{2,1,0:T(8,128)(2,1)S(1)} %get-tuple-element.82.refs_3_), channel_id=1, source_target_pairs={{0,2},{1,3},{2,0},{3,1},{4,6},{5,7},{6,4},{7,5},{8,10},{9,11},{10,... | collective-permute-start | bytes 294920 | tf_op jit(solution)/shard_map/ppermute | solution.py:500
  6.6 7.6 %collective-permute-start.4 = (bf16[3,128,128]{2,1,0:T(8,128)(2,1)S(1)}, bf16[3,128,128]{2,1,0:T(8,128)(2,1)S(1)}, u32[]{:S(2)}, u32[]{:S(2)}) collective-permute-start(bf16[3,128,128]{2,1,0:T(8,128)(2,1)S(1)} %get-tuple-element.85), channel_id=1, source_target_pairs={{0,3},{1,2},{2,1},{3,0},{4,7},{5,6},{6,5},{7,4},{8,11},{9,10},{10,... | collective-permute-start | bytes 294920 | tf_op jit(solution)/shard_map/ppermute | solution.py:500
  9.9 4.4 %collective-permute-start.5 = (bf16[3,128,128]{2,1,0:T(8,128)(2,1)S(1)}, bf16[3,128,128]{2,1,0:T(8,128)(2,1)S(1)}, u32[]{:S(2)}, u32[]{:S(2)}) collective-permute-start(bf16[3,128,128]{2,1,0:T(8,128)(2,1)S(1)} %get-tuple-element.85), channel_id=1, source_target_pairs={{0,1},{1,0},{2,3},{3,2},{4,5},{5,4},{6,7},{7,6},{8,9},{9,8},{10,11... | collective-permute-start | bytes 294920 | tf_op jit(solution)/shard_map/ppermute | solution.py:500
  10.9 6.2 %collective-permute-start.7 = (bf16[3,128,128]{2,1,0:T(8,128)(2,1)S(1)}, bf16[3,128,128]{2,1,0:T(8,128)(2,1)S(1)}, u32[]{:S(2)}, u32[]{:S(2)}) collective-permute-start(bf16[3,128,128]{2,1,0:T(8,128)(2,1)S(1)} %get-tuple-element.93), channel_id=1, source_target_pairs={{0,5},{1,4},{2,7},{3,6},{4,1},{5,0},{6,3},{7,2},{8,13},{9,12},{10,... | collective-permute-start | bytes 294920 | tf_op jit(solution)/shard_map/ppermute | solution.py:504
  12.3 6.6 %collective-permute-start.6 = (bf16[3,128,128]{2,1,0:T(8,128)(2,1)S(1)}, bf16[3,128,128]{2,1,0:T(8,128)(2,1)S(1)}, u32[]{:S(2)}, u32[]{:S(2)}) collective-permute-start(bf16[3,128,128]{2,1,0:T(8,128)(2,1)S(1)} %get-tuple-element.90), channel_id=1, source_target_pairs={{0,4},{1,5},{2,6},{3,7},{4,0},{5,1},{6,2},{7,3},{8,12},{9,13},{10,... | collective-permute-start | bytes 294920 | tf_op jit(solution)/shard_map/ppermute | solution.py:504
  14.9 5.7 %collective-permute-start.11 = (bf16[128,128]{1,0:T(8,128)(2,1)S(1)}, bf16[128,128]{1,0:T(8,128)(2,1)S(1)}, u32[]{:S(2)}, u32[]{:S(2)}) collective-permute-start(bf16[128,128]{1,0:T(8,128)(2,1)S(1)} %get-tuple-element.98), channel_id=1, source_target_pairs={{0,4},{1,5},{2,6},{3,7},{4,0},{5,1},{6,2},{7,3},{8,12},{9,13},{10,... | collective-permute-start | bytes 98312 | tf_op jit(solution)/shard_map/ppermute | solution.py:504
  16.8 3.8 %collective-permute-start.12 = (bf16[128,128]{1,0:T(8,128)(2,1)S(1)}, bf16[128,128]{1,0:T(8,128)(2,1)S(1)}, u32[]{:S(2)}, u32[]{:S(2)}) collective-permute-start(bf16[128,128]{1,0:T(8,128)(2,1)S(1)} %get-tuple-element.99), channel_id=1, source_target_pairs={{0,5},{1,4},{2,7},{3,6},{4,1},{5,0},{6,3},{7,2},{8,13},{9,12},{10,... | collective-permute-start | bytes 98312 | tf_op jit(solution)/shard_map/ppermute | solution.py:504
  16.8 3.3 %collective-permute-start.8 = (bf16[3,192,256]{2,1,0:T(8,128)(2,1)S(1)}, bf16[3,192,256]{2,1,0:T(8,128)(2,1)S(1)}, u32[]{:S(2)}, u32[]{:S(2)}) collective-permute-start(bf16[3,192,256]{2,1,0:T(8,128)(2,1)S(1)} %get-tuple-element.95), channel_id=1, source_target_pairs={{0,1},{1,0},{2,3},{3,2},{4,5},{5,4},{6,7},{7,6},{8,9},{9,8},{10,11... | collective-permute-start | bytes 884744 | tf_op jit(solution)/shard_map/ppermute | solution.py:500
  17.1 7.6 %collective-permute-start.9 = (bf16[288,128]{1,0:T(8,128)(2,1)S(1)}, bf16[288,128]{1,0:T(8,128)(2,1)S(1)}, u32[]{:S(2)}, u32[]{:S(2)}) collective-permute-start(bf16[288,128]{1,0:T(8,128)(2,1)S(1)} %get-tuple-element.96), channel_id=1, source_target_pairs={{0,4},{1,5},{2,6},{3,7},{4,0},{5,1},{6,2},{7,3},{8,12},{9,13},{10,... | collective-permute-start | bytes 221192 | tf_op jit(solution)/shard_map/ppermute | solution.py:504
  19.0 5.7 %collective-permute-start.10 = (bf16[288,128]{1,0:T(8,128)(2,1)S(1)}, bf16[288,128]{1,0:T(8,128)(2,1)S(1)}, u32[]{:S(2)}, u32[]{:S(2)}) collective-permute-start(bf16[288,128]{1,0:T(8,128)(2,1)S(1)} %get-tuple-element.97), channel_id=1, source_target_pairs={{0,5},{1,4},{2,7},{3,6},{4,1},{5,0},{6,3},{7,2},{8,13},{9,12},{10,... | collective-permute-start | bytes 221192 | tf_op jit(solution)/shard_map/ppermute | solution.py:504
  21.1 7.3 %collective-permute-start.14 = (bf16[32,1408]{1,0:T(8,128)(2,1)S(1)}, bf16[32,1408]{1,0:T(8,128)(2,1)S(1)}, u32[]{:S(2)}, u32[]{:S(2)}) collective-permute-start(bf16[32,1408]{1,0:T(8,128)(2,1)S(1)} %get-tuple-element.107), channel_id=1, source_target_pairs={{0,24},{4,28},{8,16},{12,20},{16,8},{20,12},{24,0},{28,4},{1,25},{... | collective-permute-start | bytes 270344 | tf_op jit(solution)/shard_map/ppermute | solution.py:620
  25.2 6.5 %collective-permute-start.13 = (bf16[32,1408]{1,0:T(8,128)(2,1)S(1)}, bf16[32,1408]{1,0:T(8,128)(2,1)S(1)}, u32[]{:S(2)}, u32[]{:S(2)}) collective-permute-start(bf16[32,1408]{1,0:T(8,128)(2,1)S(1)} %get-tuple-element.102), channel_id=1, source_target_pairs={{0,8},{4,12},{8,0},{12,4},{16,24},{20,28},{24,16},{28,20},{1,9},{5... | collective-permute-start | bytes 270344 | tf_op jit(solution)/shard_map/ppermute | solution.py:620
  25.7 7.2 %collective-permute-start.15 = (bf16[32,1280]{1,0:T(8,128)(2,1)S(1)}, bf16[32,1280]{1,0:T(8,128)(2,1)S(1)}, u32[]{:S(2)}, u32[]{:S(2)}) collective-permute-start(bf16[32,1280]{1,0:T(8,128)(2,1)S(1)} %get-tuple-element.116), channel_id=1, source_target_pairs={{0,16},{4,20},{8,24},{12,28},{16,0},{20,4},{24,8},{28,12},{1,17},{... | collective-permute-start | bytes 245768 | tf_op jit(solution)/shard_map/ppermute | solution.py:620
